TPU v7x, 32 devices: a whole 2x2x4 slice. The times are simulated.
32 devices in a mesh: fsdp: 4 (over y, x), ctx: 2 (over core), tp: 4 (over z).
Axes of the slice: x: 2, y: 2, z: 4, core: 2. Of those that a mesh axis runs over, the one named last changes fastest.
Arguments:
- inputs: bfloat16 [8, 196, 768], P('fsdp', 'ctx'), may hold values from -6 to 6
- norm1_gain: bfloat16 [768], P('fsdp'), may hold values from 0.25 to 1.75
- norm1_bias: bfloat16 [768], P('fsdp'), may hold values from -1.75 to 1.75
- qkv_weight: bfloat16 [768, 3, 768], P('fsdp', None, 'tp'), may hold values from -0.21875 to 0.21875
- qv_bias: bfloat16 [2, 12, 64], P(None, 'tp', 'fsdp'), may hold values from -3 to 3
- proj_weight: bfloat16 [768, 768], P('tp', 'fsdp'), may hold values from -0.875 to 0.875
- proj_bias: bfloat16 [768], P('fsdp'), may hold values from -3 to 3
- norm2_gain: bfloat16 [768], P('fsdp'), may hold values from 0.25 to 1.75
- norm2_bias: bfloat16 [768], P('fsdp'), may hold values from -1.75 to 1.75
- fc1_weight: bfloat16 [768, 3072], P('fsdp', 'tp'), may hold values from -0.21875 to 0.21875
- fc1_bias: bfloat16 [48, 64], P('tp', 'fsdp'), may hold values from -3 to 3
- fc2_weight: bfloat16 [3072, 768], P('tp', 'fsdp'), may hold values from -0.109375 to 0.109375
- fc2_bias: bfloat16 [768], P('fsdp'), may hold values from -3 to 3
- cotangent: bfloat16 [8, 196, 768], P('fsdp', 'ctx'), may hold values from -6 to 6
Outputs:
- output: bfloat16 [8, 196, 768], P('fsdp', 'ctx')
- input_grad: float32 [8, 196, 768], P('fsdp', 'ctx')
- norm1_gain_grad: float32 [768], P('fsdp')
- norm1_bias_grad: float32 [768], P('fsdp')
- qkv_weight_grad: float32 [768, 3, 768], P('fsdp', None, 'tp')
- qv_bias_grad: float32 [2, 12, 64], P(None, 'tp', 'fsdp')
- proj_weight_grad: float32 [768, 768], P('tp', 'fsdp')
- proj_bias_grad: float32 [768], P('fsdp')
- norm2_gain_grad: float32 [768], P('fsdp')
- norm2_bias_grad: float32 [768], P('fsdp')
- fc1_weight_grad: float32 [768, 3072], P('fsdp', 'tp')
- fc1_bias_grad: float32 [48, 64], P('tp', 'fsdp')
- fc2_weight_grad: float32 [3072, 768], P('tp', 'fsdp')
- fc2_bias_grad: float32 [768], P('fsdp')
All inputs are finite; a program needn't handle non-finite values.
Results may differ from a plain program's by a relative error of at most 0.02.
Values may be sent and summed in bfloat16 or wider, within the bound.
No kernel may reach another device: no remote copies, remote signals or barrier semaphores. Data moves between devices by JAX's collectives and lax.ppermute only.
A program may use at most 64 MiB of HBM per device.

v0:
```python
import jax
import jax.numpy as jnp
from jax import lax
from jax.sharding import PartitionSpec as P

HD = 64


EPSILON = 1e-06
QUERY_SCALE = 0.125


def exact_gelu(values):
    return jax.nn.gelu(values, approximate=False)


def norm_forward(values, norm_gain, norm_bias):
    average = jnp.mean(values, axis=-1, keepdims=True)
    centred = values - average
    variance = jnp.mean(centred * centred, axis=-1, keepdims=True)
    inverse = lax.rsqrt(variance + EPSILON)
    normal = centred * inverse
    return (normal * norm_gain + norm_bias, normal, inverse)


def norm_backward(grad_normed, normal, inverse, norm_gain):
    scaled = grad_normed * norm_gain
    mean_grad = jnp.mean(scaled, axis=-1, keepdims=True)
    mean_cross = jnp.mean(scaled * normal, axis=-1, keepdims=True)
    return inverse * (scaled - mean_grad - normal * mean_cross)


def split_weights(gathered):
    (
        gain_one,
        bias_one,
        w_qkv,
        qv_full,
        w_proj,
        proj_b,
        gain_two,
        bias_two,
        w_up,
        up_b,
        w_down,
        down_b,
    ) = gathered
    return (
        gain_one.astype(jnp.float32),
        bias_one.astype(jnp.float32),
        w_qkv,
        qv_full.astype(jnp.float32).reshape(2, -1),
        w_proj,
        proj_b.astype(jnp.float32),
        gain_two.astype(jnp.float32),
        bias_two.astype(jnp.float32),
        w_up,
        up_b.astype(jnp.float32).reshape(-1),
        w_down,
        down_b.astype(jnp.float32),
    )


def attention_inputs(stream, weights):
    normed_one, normal_one, inverse_one = norm_forward(stream, weights[0], weights[1])
    normed_low = normed_one.astype(jnp.bfloat16)
    projected = jnp.einsum(
        "rd,dce->rce", normed_low, weights[2], preferred_element_type=jnp.float32
    )
    query_low = ((projected[:, 0] + weights[3][0]) * QUERY_SCALE).astype(jnp.bfloat16)
    key_low = projected[:, 1].astype(jnp.bfloat16)
    value_low = (projected[:, 2] + weights[3][1]).astype(jnp.bfloat16)
    return (normed_low, normal_one, inverse_one, query_low, key_low, value_low)


def feed_inputs(middle, weights):
    normed_two, normal_two, inverse_two = norm_forward(middle, weights[6], weights[7])
    normed2_low = normed_two.astype(jnp.bfloat16)
    pre_act = jnp.dot(normed2_low, weights[8], preferred_element_type=jnp.float32) + weights[9]
    activated, gelu_pull = jax.vjp(exact_gelu, pre_act)
    return (normed2_low, normal_two, inverse_two, activated.astype(jnp.bfloat16), gelu_pull)


def frame_scores(query_low, key_all, local_heads, head_size):
    frame_count = key_all.shape[0]
    query_heads = query_low.reshape(frame_count, -1, local_heads, head_size)
    key_heads = key_all.reshape(frame_count, -1, local_heads, head_size)
    return jnp.einsum("fqhd,fkhd->fhqk", query_heads, key_heads, preferred_element_type=jnp.float32)


def local(
    inputs,
    norm1_gain,
    norm1_bias,
    qkv_weight,
    qv_bias,
    proj_weight,
    proj_bias,
    norm2_gain,
    norm2_bias,
    fc1_weight,
    fc1_bias,
    fc2_weight,
    fc2_bias,
    cotangent,
):
    frame_count, place_count, model_width = inputs.shape
    row_count = frame_count * place_count
    local_heads = qv_bias.shape[1]
    head_size = HD

    def partial_rows(left, product):
        return lax.psum(product(left).astype(jnp.bfloat16), "tp").astype(jnp.float32)

    gathered = (
        lax.all_gather(norm1_gain, "fsdp", axis=0, tiled=True),
        lax.all_gather(norm1_bias, "fsdp", axis=0, tiled=True),
        lax.all_gather(qkv_weight, "fsdp", axis=0, tiled=True),
        lax.all_gather(qv_bias, "fsdp", axis=2, tiled=True),
        lax.all_gather(proj_weight, "fsdp", axis=1, tiled=True),
        lax.all_gather(proj_bias, "fsdp", axis=0, tiled=True),
        lax.all_gather(norm2_gain, "fsdp", axis=0, tiled=True),
        lax.all_gather(norm2_bias, "fsdp", axis=0, tiled=True),
        lax.all_gather(fc1_weight, "fsdp", axis=0, tiled=True),
        lax.all_gather(fc1_bias, "fsdp", axis=1, tiled=True),
        lax.all_gather(fc2_weight, "fsdp", axis=1, tiled=True),
        lax.all_gather(fc2_bias, "fsdp", axis=0, tiled=True),
    )
    weights = split_weights(gathered)
    stream = inputs.astype(jnp.float32).reshape(row_count, model_width)
    normed_low, normal_one, inverse_one, query_low, key_low, value_low = attention_inputs(
        stream, weights
    )
    key_all, value_all = (
        lax.all_gather(key_low.reshape(frame_count, place_count, -1), "ctx", axis=1, tiled=True),
        lax.all_gather(value_low.reshape(frame_count, place_count, -1), "ctx", axis=1, tiled=True),
    )
    scores = frame_scores(query_low, key_all, local_heads, head_size)
    row_max = jnp.max(scores, axis=-1, keepdims=True)
    exponent = jnp.exp(scores - row_max)
    row_total = jnp.sum(exponent, axis=-1, keepdims=True)
    soft_probs = exponent / row_total
    log_total = row_max + jnp.log(row_total)
    value_heads = value_all.reshape(frame_count, -1, local_heads, head_size)
    attended = jnp.einsum(
        "fhqk,fkhd->fqhd",
        soft_probs.astype(jnp.bfloat16),
        value_heads,
        preferred_element_type=jnp.float32,
    )
    attended_low = attended.reshape(row_count, -1).astype(jnp.bfloat16)
    proj_now = weights[4]

    def project_attn(rows):
        return jnp.dot(rows, proj_now, preferred_element_type=jnp.float32)

    branch = partial_rows(attended_low, project_attn)
    middle = stream + branch + weights[5]
    normed2_low, normal_two, inverse_two, hidden_low, gelu_pull = feed_inputs(middle, weights)
    down_now = weights[10]

    def project_down(rows):
        return jnp.dot(rows, down_now, preferred_element_type=jnp.float32)

    branch_two = partial_rows(hidden_low, project_down)
    output_rows = (middle + branch_two + weights[11]).astype(jnp.bfloat16)
    gathered = (
        lax.all_gather(norm1_gain, "fsdp", axis=0, tiled=True),
        lax.all_gather(norm1_bias, "fsdp", axis=0, tiled=True),
        lax.all_gather(qkv_weight, "fsdp", axis=0, tiled=True),
        lax.all_gather(qv_bias, "fsdp", axis=2, tiled=True),
        lax.all_gather(proj_weight, "fsdp", axis=1, tiled=True),
        lax.all_gather(proj_bias, "fsdp", axis=0, tiled=True),
        lax.all_gather(norm2_gain, "fsdp", axis=0, tiled=True),
        lax.all_gather(norm2_bias, "fsdp", axis=0, tiled=True),
        lax.all_gather(fc1_weight, "fsdp", axis=0, tiled=True),
        lax.all_gather(fc1_bias, "fsdp", axis=1, tiled=True),
        lax.all_gather(fc2_weight, "fsdp", axis=1, tiled=True),
        lax.all_gather(fc2_bias, "fsdp", axis=0, tiled=True),
    )
    weights = split_weights(gathered)
    normed_low, normal_one, inverse_one, query_low, key_low, value_low = attention_inputs(
        stream, weights
    )
    key_all, value_all = (
        lax.all_gather(key_low.reshape(frame_count, place_count, -1), "ctx", axis=1, tiled=True),
        lax.all_gather(value_low.reshape(frame_count, place_count, -1), "ctx", axis=1, tiled=True),
    )
    value_heads = value_all.reshape(frame_count, -1, local_heads, head_size)
    normed2_low, normal_two, inverse_two, hidden_low, gelu_pull = feed_inputs(middle, weights)
    up_now = weights[8]
    qkv_now = weights[2]

    def back_up(rows):
        return jnp.einsum("rf,df->rd", rows, up_now, preferred_element_type=jnp.float32)

    def back_qkv(rows):
        return jnp.einsum("rce,dce->rd", rows, qkv_now, preferred_element_type=jnp.float32)

    grad_out = cotangent.astype(jnp.float32).reshape(row_count, model_width)
    grad_down_b = jnp.sum(grad_out, axis=0)
    grad_out_low = grad_out.astype(jnp.bfloat16)
    grad_w_down = jnp.einsum(
        "rf,rd->fd", hidden_low, grad_out_low, preferred_element_type=jnp.float32
    )
    grad_hidden = jnp.einsum(
        "rd,fd->rf", grad_out_low, weights[10], preferred_element_type=jnp.float32
    )
    grad_pre_low = gelu_pull(grad_hidden)[0].astype(jnp.bfloat16)
    grad_up_b = jnp.sum(grad_pre_low, axis=0, dtype=jnp.float32).reshape(fc1_bias.shape[0], -1)
    grad_w_up = jnp.einsum(
        "rd,rf->df", normed2_low, grad_pre_low, preferred_element_type=jnp.float32
    )
    grad_normed_two = partial_rows(grad_pre_low, back_up)
    grad_gain_two = jnp.sum(grad_normed_two * normal_two, axis=0)
    grad_bias_two = jnp.sum(grad_normed_two, axis=0)
    grad_middle = grad_out + norm_backward(grad_normed_two, normal_two, inverse_two, weights[6])
    grad_proj_b = jnp.sum(grad_middle, axis=0)
    grad_mid_low = grad_middle.astype(jnp.bfloat16)
    grad_w_proj = jnp.einsum(
        "re,rd->ed", attended_low, grad_mid_low, preferred_element_type=jnp.float32
    )
    grad_attended = jnp.einsum(
        "rd,ed->re", grad_mid_low, weights[4], preferred_element_type=jnp.float32
    ).astype(jnp.bfloat16)
    grad_att_heads = grad_attended.reshape(frame_count, place_count, local_heads, head_size)
    scores = frame_scores(query_low, key_all, local_heads, head_size)
    soft_probs = jnp.exp(scores - log_total)
    soft_low = soft_probs.astype(jnp.bfloat16)
    key_heads = key_all.reshape(frame_count, -1, local_heads, head_size)
    query_heads = query_low.reshape(frame_count, place_count, local_heads, head_size)
    grad_value_all = jnp.einsum(
        "fhqk,fqhd->fkhd", soft_low, grad_att_heads, preferred_element_type=jnp.float32
    )
    grad_soft = jnp.einsum(
        "fqhd,fkhd->fhqk", grad_att_heads, value_heads, preferred_element_type=jnp.float32
    )
    row_delta = jnp.sum(soft_probs * grad_soft, axis=-1, keepdims=True)
    grad_scores = (soft_probs * (grad_soft - row_delta)).astype(jnp.bfloat16)
    grad_query = jnp.einsum(
        "fhqk,fkhd->fqhd", grad_scores, key_heads, preferred_element_type=jnp.float32
    )
    grad_key_all = jnp.einsum(
        "fhqk,fqhd->fkhd", grad_scores, query_heads, preferred_element_type=jnp.float32
    )
    grad_key, grad_value = (
        lax.psum_scatter(
            grad_key_all.reshape(frame_count, -1, local_heads * head_size).astype(jnp.bfloat16),
            "ctx",
            scatter_dimension=1,
            tiled=True,
        ).astype(jnp.float32),
        lax.psum_scatter(
            grad_value_all.reshape(frame_count, -1, local_heads * head_size).astype(jnp.bfloat16),
            "ctx",
            scatter_dimension=1,
            tiled=True,
        ).astype(jnp.float32),
    )
    grad_query_low = grad_query.reshape(row_count, -1).astype(jnp.bfloat16) * QUERY_SCALE
    grad_projected = jnp.stack(
        (
            grad_query_low,
            grad_key.reshape(row_count, -1).astype(jnp.bfloat16),
            grad_value.reshape(row_count, -1).astype(jnp.bfloat16),
        ),
        axis=1,
    )
    grad_w_qkv = jnp.einsum(
        "rd,rce->dce", normed_low, grad_projected, preferred_element_type=jnp.float32
    )
    grad_qv = jnp.sum(grad_projected[:, 0::2], axis=0, dtype=jnp.float32).reshape(
        2, local_heads, head_size
    )
    grad_normed_one = partial_rows(grad_projected, back_qkv)
    grad_gain_one = jnp.sum(grad_normed_one * normal_one, axis=0)
    grad_bias_one = jnp.sum(grad_normed_one, axis=0)
    grad_input = grad_middle + norm_backward(grad_normed_one, normal_one, inverse_one, weights[0])
    shared = (
        lax.psum_scatter(
            grad_gain_one.astype(jnp.bfloat16), "fsdp", scatter_dimension=0, tiled=True
        ).astype(jnp.float32),
        lax.psum_scatter(
            grad_bias_one.astype(jnp.bfloat16), "fsdp", scatter_dimension=0, tiled=True
        ).astype(jnp.float32),
        lax.psum_scatter(
            grad_w_qkv.astype(jnp.bfloat16), "fsdp", scatter_dimension=0, tiled=True
        ).astype(jnp.float32),
        lax.psum_scatter(
            grad_qv.astype(jnp.bfloat16), "fsdp", scatter_dimension=2, tiled=True
        ).astype(jnp.float32),
        lax.psum_scatter(
            grad_w_proj.astype(jnp.bfloat16), "fsdp", scatter_dimension=1, tiled=True
        ).astype(jnp.float32),
        lax.psum_scatter(
            grad_proj_b.astype(jnp.bfloat16), "fsdp", scatter_dimension=0, tiled=True
        ).astype(jnp.float32),
        lax.psum_scatter(
            grad_gain_two.astype(jnp.bfloat16), "fsdp", scatter_dimension=0, tiled=True
        ).astype(jnp.float32),
        lax.psum_scatter(
            grad_bias_two.astype(jnp.bfloat16), "fsdp", scatter_dimension=0, tiled=True
        ).astype(jnp.float32),
        lax.psum_scatter(
            grad_w_up.astype(jnp.bfloat16), "fsdp", scatter_dimension=0, tiled=True
        ).astype(jnp.float32),
        lax.psum_scatter(
            grad_up_b.astype(jnp.bfloat16), "fsdp", scatter_dimension=1, tiled=True
        ).astype(jnp.float32),
        lax.psum_scatter(
            grad_w_down.astype(jnp.bfloat16), "fsdp", scatter_dimension=1, tiled=True
        ).astype(jnp.float32),
        lax.psum_scatter(
            grad_down_b.astype(jnp.bfloat16), "fsdp", scatter_dimension=0, tiled=True
        ).astype(jnp.float32),
    )
    final = (
        lax.psum(shared[0].astype(jnp.bfloat16), "ctx").astype(jnp.float32),
        lax.psum(shared[1].astype(jnp.bfloat16), "ctx").astype(jnp.float32),
        lax.psum(shared[2].astype(jnp.bfloat16), "ctx").astype(jnp.float32),
        lax.psum(shared[3].astype(jnp.bfloat16), "ctx").astype(jnp.float32),
        lax.psum(shared[4].astype(jnp.bfloat16), "ctx").astype(jnp.float32),
        lax.psum(shared[5].astype(jnp.bfloat16), "ctx").astype(jnp.float32),
        lax.psum(shared[6].astype(jnp.bfloat16), "ctx").astype(jnp.float32),
        lax.psum(shared[7].astype(jnp.bfloat16), "ctx").astype(jnp.float32),
        lax.psum(shared[8].astype(jnp.bfloat16), "ctx").astype(jnp.float32),
        lax.psum(shared[9].astype(jnp.bfloat16), "ctx").astype(jnp.float32),
        lax.psum(shared[10].astype(jnp.bfloat16), "ctx").astype(jnp.float32),
        lax.psum(shared[11].astype(jnp.bfloat16), "ctx").astype(jnp.float32),
    )
    return (
        output_rows.reshape(frame_count, place_count, model_width),
        grad_input.reshape(frame_count, place_count, model_width),
        final[0],
        final[1],
        final[2],
        final[3],
        final[4],
        final[5],
        final[6],
        final[7],
        final[8],
        final[9],
        final[10],
        final[11],
    )


def solution(mesh):
    return jax.shard_map(
        local,
        mesh=mesh,
        in_specs=(
            P("fsdp", "ctx", None),
            P("fsdp"),
            P("fsdp"),
            P("fsdp", None, "tp"),
            P(None, "tp", "fsdp"),
            P("tp", "fsdp"),
            P("fsdp"),
            P("fsdp"),
            P("fsdp"),
            P("fsdp", "tp"),
            P("tp", "fsdp"),
            P("tp", "fsdp"),
            P("fsdp"),
            P("fsdp", "ctx", None),
        ),
        out_specs=(
            P("fsdp", "ctx", None),
            P("fsdp", "ctx", None),
            P("fsdp"),
            P("fsdp"),
            P("fsdp", None, "tp"),
            P(None, "tp", "fsdp"),
            P("tp", "fsdp"),
            P("fsdp"),
            P("fsdp"),
            P("fsdp"),
            P("fsdp", "tp"),
            P("tp", "fsdp"),
            P("tp", "fsdp"),
            P("fsdp"),
        ),
        check_vma=False,
    )
```

profile of v0, /device:TPU:0, one launch (start us, length us, event | category | flops | bytes accessed | tf_op | source)
XLA Modules:
  0.0 344.8 jit_solution(9399627889849202559)
XLA Ops:
  8.1 1.0 copy.139
  9.1 1.3 convert_reduce_fusion
  10.5 0.6 multiply_reduce_fusion.2
  11.5 19.2 %all_gather.56 = bf16[768,3,192]{2,1,0:T(4,128)(2,1)S(1)} all-gather(bf16[192,3,192]{2,1,0:T(4,128)(2,1)S(1)} %copy.143), channel_id=1, replica_groups=mesh['fsdp'=4,'ctx'=2,'tp'=4] {'fsdp'}, dimensions={0}, use_global_device_ids=true | all-gather | bytes 1105920 | tf_op jit(solution)/shard_map/all_gather | solution.py:118
  30.7 0.9 copy.144
  31.6 0.6 fusion.52
  34.1 15.0 %all-reduce.18 = (bf16[768]{0:T(1024)(128)(2,1)S(1)}, bf16[768]{0:T(1024)(128)(2,1)S(1)}, bf16[768]{0:T(1024)(128)(2,1)S(1)}, bf16[768]{0:T(1024)(128)(2,1)S(1)}, bf16[768]{0:T(1024)(128)(2,1)S(1)}) all-reduce(bf16[768]{0:T(1024)(128)(2,1)S(1)} %dynamic-update-slice.1, ...), channel_id=1, replica_groups=mesh['fsdp'=4,'ctx'=2,'tp'=4] {'fsdp'}, use_global_device_ids=true, to_apply=%add.1 | all-reduce | flops 3840 | bytes 15360
  49.4 0.5 fusion.44
  50.7 8.1 %all_gather.57 = bf16[2,3,64]{1,0,2:T(2,128)(2,1)S(1)} all-gather(bf16[2,3,16]{1,0,2:T(2,128)(2,1)S(1)} %copy.145), channel_id=1, replica_groups=mesh['fsdp'=4,'ctx'=2,'tp'=4] {'fsdp'}, dimensions={2}, use_global_device_ids=true | all-gather | bytes 960 | tf_op jit(solution)/shard_map/all_gather | solution.py:119
  59.3 1.9 all_gather.58
  61.7 1.9 all_gather.59
  65.7 8.7 %all_gather.60 = bf16[192,768]{0,1:T(8,128)(2,1)S(1)} all-gather(bf16[192,192]{0,1:T(8,128)(2,1)S(1)} %copy.155), channel_id=1, replica_groups=mesh['fsdp'=4,'ctx'=2,'tp'=4] {'fsdp'}, dimensions={1}, use_global_device_ids=true | all-gather | bytes 368640 | tf_op jit(solution)/shard_map/all_gather | solution.py:120
  74.4 0.7 copy-done.1
  75.1 1.0 convolution_convert_fusion.5
  76.8 0.5 all-gather.5.cloned.1.call-update
  77.6 8.1 %all_gather.65 = bf16[12,64]{0,1:T(8,128)(2,1)S(1)} all-gather(bf16[12,16]{0,1:T(8,128)(2,1)S(1)} %copy.156), channel_id=1, replica_groups=mesh['fsdp'=4,'ctx'=2,'tp'=4] {'fsdp'}, dimensions={1}, use_global_device_ids=true | all-gather | bytes 1920 | tf_op jit(solution)/shard_map/all_gather | solution.py:125
  86.0 0.6 dynamic-slice.6
  87.2 25.1 %all-reduce.28.cloned.1.call-done = bf16[196,768]{1,0:T(8,128)(2,1)} async-done(((bf16[196,768]{1,0:T(8,128)(2,1)}), bf16[196,768]{1,0:T(8,128)(2,1)}) %all-reduce.28.cloned.1.call-update) | async-done | bytes 301072 | tf_op jit(solution)/shard_map/psum | solution.py:113
  112.3 1.1 fusion.49
  113.8 2.7 convolution_add_fusion
  116.4 19.3 %all-gather.5.cloned.1.call-done = bf16[768,768]{0,1:T(8,128)(2,1)} async-done(((bf16[768,192]{0,1:T(8,128)(2,1)}), bf16[768,768]{0,1:T(8,128)(2,1)}) %all-gather.5.cloned.1.call-update) | async-done | bytes 1179664 | tf_op jit(solution)/shard_map/all_gather | solution.py:126
  135.7 4.6 %fusion.45 = (bf16[768]{0:T(1024)(128)(2,1)}, bf16[196,768]{1,0:T(8,128)(2,1)S(1)}, f32[196,768]{1,0:T(8,128)}) fusion(f32[196,768]{1,0:T(8,128)} %convolution_add_fusion, bf16[196,768]{1,0:T(8,128)(2,1)S(1)} %reshape.215, bf16[768,768]{0,1:T(8,128)(2,1)} %all-gather.5.cloned.1.call-done), kind=kOutput, calls=%fused_computation.105 | convolution fusion | flops 242198784 | bytes 2987520 | tf_op jit(solution)/shard_map/rd,fd->rf/dot_general | solution.py:206
  140.3 1.3 convolution_convert_fusion.3
  141.8 1.4 multiply_convert_fusion.1
  143.5 1.3 convolution_convert_fusion.4
  144.8 32.7 %all-reduce.30.cloned.1.call-done = bf16[196,768]{1,0:T(8,128)(2,1)} async-done(((bf16[196,768]{1,0:T(8,128)(2,1)}), bf16[196,768]{1,0:T(8,128)(2,1)}) %all-reduce.30.cloned.1.call-update) | async-done | bytes 301072 | tf_op jit(solution)/shard_map/psum | solution.py:113
  177.5 2.0 fusion.14
  179.5 1.9 fusion.47
  181.4 1.0 convolution_convert_fusion.10
  182.4 1.6 reshape.217
  184.1 1.4 multiply_reduce_fusion
  186.3 1.0 convolution_convert_fusion.8
  187.4 1.0 convolution_convert_fusion.7
  188.9 0.9 copy.174
  189.9 17.5 %all-reduce.36.cloned.1.call-done = (bf16[2,196,192]{1,2,0:T(8,128)(2,1)}, bf16[2,196,192]{1,2,0:T(8,128)(2,1)}) async-done(((bf16[2,196,192]{1,2,0:T(8,128)(2,1)}, bf16[2,196,192]{1,2,0:T(8,128)(2,1)}), (bf16[2,196,192]{1,2,0:T(8,128)(2,1)}, bf16[2,196,192]{1,2,0:T(8,128)(2,1)})) %all-reduce.36.cloned.1.call-update) | async-done | bytes 301072
  207.5 1.0 constant_dynamic-slice_fusion.3
  208.7 1.0 constant_dynamic-slice_fusion.2
  210.0 1.2 fusion
  211.3 1.7 convolution_convert_fusion.1
  213.1 1.6 convolution_convert_fusion
  214.8 1.7 convolution_convert_fusion.2
  218.9 1.6 copy.175
  220.5 31.8 %all-reduce.32.cloned.1.call-done = (bf16[196,768]{1,0:T(8,128)(2,1)}, bf16[196,768]{1,0:T(8,128)(2,1)}) async-done(((bf16[196,768]{1,0:T(8,128)(2,1)}, bf16[196,768]{1,0:T(8,128)(2,1)}), (bf16[196,768]{1,0:T(8,128)(2,1)}, bf16[196,768]{1,0:T(8,128)(2,1)})) %all-reduce.32.cloned.1.call-update) | async-done | bytes 602128 | tf_op jit(solution)/shard_map/psum | solution.py:113
  252.3 1.1 reduce_sum.204
  253.4 1.4 fusion.19
  254.8 17.0 %all-reduce.17 = (bf16[2,3,64]{2,1,0:T(4,128)(2,1)S(1)}, bf16[768]{0:T(1024)(128)(2,1)S(1)}, bf16[768]{0:T(1024)(128)(2,1)S(1)}, bf16[768]{0:T(1024)(128)(2,1)S(...) all-reduce(bf16[2,3,64]{2,1,0:T(4,128)(2,1)S(1)} %convert_element_t, ...), channel_id=7, replica_groups=mesh['fsdp'=4,'ctx'=2,'tp'=4] {'fsdp'}, use_global_device_ids=true, to_apply=%region_26.0.clone | all-reduce | flops 6528 | bytes 26112
  271.9 0.9 copy.165
  272.9 8.2 %reduce-scatter.15.cloned.1.call-done = bf16[768,192]{0,1:T(8,128)(2,1)} async-done(((bf16[768,768]{0,1:T(8,128)(2,1)}), bf16[768,192]{0,1:T(8,128)(2,1)}) %reduce-scatter.15.cloned.1.call-update) | async-done | bytes 294928 | tf_op jit(solution)/shard_map/reduce_scatter | solution.py:310
  281.0 31.7 %reduce-scatter.11.cloned.1.call-done = bf16[192,3,192]{2,0,1:T(8,128)(2,1)} async-done(((bf16[768,3,192]{2,0,1:T(8,128)(2,1)}), bf16[192,3,192]{2,0,1:T(8,128)(2,1)}) %reduce-scatter.11.cloned.1.call-update) | async-done | bytes 221200 | tf_op jit(solution)/shard_map/reduce_scatter | solution.py:286
  313.2 1.1 copy.166
  314.9 2.5 all-reduce.19
  317.4 0.6 convert_element_type.305
  318.0 0.6 convert_element_type.306
  318.5 0.6 copy.167
  319.1 0.6 convert_element_type.314
  319.7 0.6 convert_element_type.316
  320.2 0.6 convert_element_type.317
  320.8 0.6 convert_element_type.321
  321.4 0.6 convert_element_type.324
  322.0 10.5 %all-reduce.34.cloned.1.call-done = (bf16[192,3,192]{2,0,1:T(8,128)(2,1)}, bf16[192,192]{1,0:T(8,128)(2,1)}, bf16[192,768]{1,0:T(8,128)(2,1)}, bf16[768,192]{0,1:T(8,128)(2,1)}) async-done(((bf16[192,3,192]{2,0,1:T(8,128)(2,1)}, bf16[192,192]{1,0:T(8,128)(2,1)}, bf16[192,768]{1,0:T(8,128)(2,1)}, bf16[768,192]{0,1:T(8,128)(2,1)}), (bf16[192,3,192]{2,0,1:T(8,128)(2,1)}, bf16[192,192]{1,0:T(8,128)(2,1)}, ...) | async-done | bytes 884752 | tf_op jit(solution)/shard_map/psum | solution.py:320
  332.5 1.9 convert_element_type.308
  334.4 1.6 convert_element_type.312
  336.0 0.9 convert_element_type.319
  336.8 0.9 convert_element_type.323
  (213 shorter events, 11.5 us)
Async XLA Ops:
  8.0 2.5 copy-start.9
  8.0 104.3 %all-reduce.28.cloned.1.call-start = ((), (), s32[]{:S(2)}) async-start(), calls=%async_computation.4 | async-start | bytes 614400 | tf_op jit(solution)/shard_map/psum | solution.py:113
  9.1 2.1 copy-start.24
  30.7 1.0 copy-start.42
  30.7 2.2 copy-start.44
  30.7 2.5 copy-start.45
  30.7 2.7 copy-start.46
  30.7 2.9 copy-start.47
  30.7 3.1 copy-start.48
  49.1 0.9 copy-start.26
  49.3 0.7 copy-start.30
  49.4 0.6 copy-start.32
  49.9 0.7 copy-start.43
  61.4 3.2 copy-start.20
  64.0 1.0 copy-start.10
  64.1 0.6 copy-start.36
  64.7 0.9 copy-start.25
  65.6 11.8 %copy-start.18 = (bf16[196,192]{0,1:T(8,128)(2,1)}, bf16[196,192]{0,1:T(8,128)(2,1)S(1)}, u32[]{:S(2)}) copy-start(bf16[196,192]{0,1:T(8,128)(2,1)S(1)} %convert_element_type.274) | copy-start | bytes 225796
  65.6 11.9 %copy-start.40 = (bf16[12,16]{1,0:T(8,128)(2,1)S(1)}, bf16[12,16]{1,0:T(8,128)(2,1)}, u32[]{:S(2)}) copy-start(bf16[12,16]{1,0:T(8,128)(2,1)} %param.24) | copy-start | bytes 1156
  65.7 20.1 %copy-start.14 = (bf16[2,98,768]{2,0,1:T(2,128)(2,1)S(1)}, bf16[2,98,768]{2,0,1:T(2,128)(2,1)}, u32[]{:S(2)}) copy-start(bf16[2,98,768]{2,0,1:T(2,128)(2,1)} %param.27) | copy-start | bytes 903172
  74.4 0.7 copy-start.1
  76.2 9.8 %copy-start.50 = (u32[32]{0:T(128)S(1)}, u32[32]{0:T(128)}, u32[]{:S(2)}) copy-start(u32[32]{0:T(128)} %constant.128) | copy-start | bytes 388
  76.2 37.5 %all-gather.3.cloned.1.call-start = ((), (), s32[]{:S(2)}) async-start(), calls=%async_computation.5 | async-start | bytes 1474560 | tf_op jit(solution)/shard_map/all_gather | solution.py:124
  76.8 58.9 %all-gather.5.cloned.1.call-start = ((), (), s32[]{:S(2)}) async-start(), calls=%async_computation.6 | async-start | bytes 1474560 | tf_op jit(solution)/shard_map/all_gather | solution.py:126
  77.4 100.1 %all-reduce.30.cloned.1.call-start = ((), (), s32[]{:S(2)}) async-start(), calls=%async_computation.7 | async-start | bytes 614400 | tf_op jit(solution)/shard_map/psum | solution.py:113
  85.8 28.0 %copy-start.28 = (f32[768]{0:T(1024)}, f32[768]{0:T(1024)S(1)}, u32[]{:S(2)}) copy-start(f32[768]{0:T(1024)S(1)} %convert_element_type.279) | copy-start | bytes 9220
  86.0 49.7 %copy-start.5 = (bf16[196,768]{1,0:T(8,128)(2,1)}, bf16[196,768]{1,0:T(8,128)(2,1)S(1)}, u32[]{:S(2)}) copy-start(bf16[196,768]{1,0:T(8,128)(2,1)S(1)} %reshape.215) | copy-start | bytes 903172
  113.7 2.7 copy-start.34
  135.7 4.6 %copy-start = (bf16[768,768]{1,0:T(8,128)(2,1)S(1)}, bf16[768,768]{1,0:T(8,128)(2,1)}, u32[]{:S(2)}) copy-start(bf16[768,768]{1,0:T(8,128)(2,1)} %all-gather.3.cloned.1.call-done) | copy-start | bytes 3538948
  140.3 3.0 copy-start.12
  141.6 65.9 %all-reduce.36.cloned.1.call-start = ((), (), s32[]{:S(2)}) async-start(), calls=%async_computation.14 | async-start | bytes 786432
  141.8 1.6 copy-start.16
  143.5 36.0 %copy-start.3 = (bf16[196,768]{1,0:T(8,128)(2,1)}, bf16[196,768]{1,0:T(8,128)(2,1)S(1)}, u32[]{:S(2)}) copy-start(bf16[196,768]{1,0:T(8,128)(2,1)S(1)} %multiply_convert_fusion.1) | copy-start | bytes 903172
  177.5 4.0 %copy-start.2 = (bf16[192,768]{0,1:T(8,128)(2,1)S(1)}, bf16[192,768]{0,1:T(8,128)(2,1)}, u32[]{:S(2)}) copy-start(bf16[192,768]{0,1:T(8,128)(2,1)} %copy-done.1) | copy-start | bytes 884740
  185.4 0.9 copy-start.11
  185.4 0.9 copy-start.37
  185.4 1.9 copy-start.17
  186.3 2.3 copy-start.19
  188.6 30.3 %reduce-scatter.17.cloned.1.call-start = ((), (), s32[]{:S(2)}) async-start(), calls=%async_computation.11 | async-start | bytes 491520
  189.9 62.5 %all-reduce.32.cloned.1.call-start = ((), (), s32[]{:S(2)}) async-start(), calls=%async_computation.12 | async-start | bytes 1228800 | tf_op jit(solution)/shard_map/psum | solution.py:113
  210.0 1.3 copy-start.13
  210.0 1.3 copy-start.29
  210.0 1.3 copy-start.35
  211.2 1.9 copy-start.4
  211.2 1.9 copy-start.6
  211.2 61.6 %reduce-scatter.13.cloned.1.call-start = ((), (), s32[]{:S(2)}) async-start(), calls=%async_computation.9 | async-start | bytes 1474560 | tf_op jit(solution)/shard_map/reduce_scatter | solution.py:304
  213.0 1.8 copy-start.27
  213.0 1.8 copy-start.31
  213.1 1.8 copy-start.33
  213.1 68.0 %reduce-scatter.15.cloned.1.call-start = ((), (), s32[]{:S(2)}) async-start(), calls=%async_computation.10 | async-start | bytes 1474560 | tf_op jit(solution)/shard_map/reduce_scatter | solution.py:310
  214.7 1.9 copy-start.15
  214.7 98.0 %reduce-scatter.11.cloned.1.call-start = ((), (), s32[]{:S(2)}) async-start(), calls=%async_computation.8 | async-start | bytes 1474560 | tf_op jit(solution)/shard_map/reduce_scatter | solution.py:286
  216.5 1.7 copy-start.49
  216.5 2.0 copy-start.41
  216.5 2.1 copy-start.7
  216.6 38.2 %copy-start.38 = (bf16[768]{0:T(1024)(128)(2,1)S(1)}, bf16[768]{0:T(1024)(128)(2,1)}, u32[]{:S(2)}) copy-start(bf16[768]{0:T(1024)(128)(2,1)} %get-tuple-element.98) | copy-start | bytes 4612
  216.6 38.2 %copy-start.39 = (bf16[768]{0:T(1024)(128)(2,1)S(1)}, bf16[768]{0:T(1024)(128)(2,1)}, u32[]{:S(2)}) copy-start(bf16[768]{0:T(1024)(128)(2,1)} %get-tuple-element.137) | copy-start | bytes 4612
  216.6 115.9 %all-reduce.34.cloned.1.call-start = ((), (), s32[]{:S(2)}) async-start(), calls=%async_computation.13 | async-start | bytes 1966080 | tf_op jit(solution)/shard_map/psum | solution.py:320
  252.3 19.4 %copy-start.21 = (bf16[196,768]{1,0:T(8,128)(2,1)S(1)}, bf16[196,768]{1,0:T(8,128)(2,1)}, u32[]{:S(2)}) copy-start(bf16[196,768]{1,0:T(8,128)(2,1)} %get-tuple-element.104) | copy-start | bytes 903172
  271.8 41.0 %copy-start.8 = (bf16[196,768]{1,0:T(8,128)(2,1)S(1)}, bf16[196,768]{1,0:T(8,128)(2,1)}, u32[]{:S(2)}) copy-start(bf16[196,768]{1,0:T(8,128)(2,1)} %get-tuple-element.105) | copy-start | bytes 903172
  332.5 3.5 %copy-start.23 = (bf16[192,768]{1,0:T(8,128)(2,1)S(1)}, bf16[192,768]{1,0:T(8,128)(2,1)}, u32[]{:S(2)}) copy-start(bf16[192,768]{1,0:T(8,128)(2,1)} %get-tuple-element.130) | copy-start | bytes 884740
  332.5 4.3 %copy-start.22 = (bf16[768,192]{0,1:T(8,128)(2,1)S(1)}, bf16[768,192]{0,1:T(8,128)(2,1)}, u32[]{:S(2)}) copy-start(bf16[768,192]{0,1:T(8,128)(2,1)} %get-tuple-element.131) | copy-start | bytes 884740
Sparse Core Ops, SparseCore 0:
  76.3 35.9 all-reduce.27
  141.7 35.7 all-reduce.29
  188.7 18.6 all-reduce.35
  211.3 40.9 all-reduce.31
  312.9 19.5 all-reduce.33
Sparse Core Ops, SparseCore 1:
  78.5 27.8 all-gather.2
  108.1 27.5 all-gather.4
  192.7 24.5 reduce-scatter.16
  220.5 28.5 reduce-scatter.12
  252.2 28.8 reduce-scatter.14
  284.2 28.5 reduce-scatter.10
where the time goes:
time: 346 us; the launch traced here: 345 us
  waiting for transfers between devices  178 us (51%)
  blocking collectives  82.4 us (24%)
  matrix products  23.1 us (7%)
  other arithmetic  21.5 us (6%)
  local copies, waits for them, and re-layouts  20.3 us (6%)
  between operations  18.8 us (5%)
    psum x3, waiting for transfers between devices, partial_rows(): lax.psum(product(left).astype(jnp.bfloat16), 'tp').astype(jnp.float32)  89.6 us
    unnamed x2, blocking collectives  32 us
    reduce_scatter x1, waiting for transfers between devices, local(): lax.psum_scatter(grad_w_qkv.astype(jnp.bfloat16), 'fsdp', scatter_dimensi...  31.7 us
    all_gather x1, waiting for transfers between devices, local(): lax.all_gather(fc2_weight, 'fsdp', axis=1, tiled=True)  19.3 us
    all_gather x1, blocking collectives, local(): lax.all_gather(qkv_weight, 'fsdp', axis=0, tiled=True)  19.2 us
    unnamed x13, waiting for transfers between devices  18.7 us
    unnamed x140, local copies, waits for them, and re-layouts  13.7 us
    psum x1, waiting for transfers between devices, local(): lax.psum(shared[2].astype(jnp.bfloat16), 'ctx').astype(jnp.float32)  10.5 us
  transfers between devices with their start and end apart: 11, of which 8 were waited for; matrix products, arithmetic and copies ran while one was open for 9% of the time, Pallas kernels for 0%

commit v1 on v0

v1 whole, which is shorter than its diff:
```python
import jax
import jax.numpy as jnp
from jax import lax
from jax.sharding import PartitionSpec as P

HD = 64
EPSILON = 1e-06
QUERY_SCALE = 0.125
F32 = jnp.float32
LOW = jnp.bfloat16


def dot(left, right, dims):
    return lax.dot_general(left, right, (dims, ((), ())), preferred_element_type=F32)


NN = ((1,), (0,))
NT = ((1,), (1,))
TN = ((0,), (0,))


def exact_gelu(values):
    return jax.nn.gelu(values, approximate=False)


def normalise(values):
    average = jnp.mean(values, axis=-1, keepdims=True)
    centred = values - average
    variance = jnp.mean(centred * centred, axis=-1, keepdims=True)
    inverse = lax.rsqrt(variance + EPSILON)
    return centred * inverse, inverse


def norm_backward(grad_normed, normal, inverse, norm_gain):
    scaled = grad_normed * norm_gain
    mean_grad = jnp.mean(scaled, axis=-1, keepdims=True)
    mean_cross = jnp.mean(scaled * normal, axis=-1, keepdims=True)
    return inverse * (scaled - mean_grad - normal * mean_cross)


def xor_pairs(size, step):
    return [(i, i ^ step) for i in range(size)]


def build(nf, nc, nt):
    def local(
        inputs,
        norm1_gain,
        norm1_bias,
        qkv_weight,
        qv_bias,
        proj_weight,
        proj_bias,
        norm2_gain,
        norm2_bias,
        fc1_weight,
        fc1_bias,
        fc2_weight,
        fc2_bias,
        cotangent,
    ):
        frames, half, width = inputs.shape
        shard = width // nf
        heads = qv_bias.shape[1]
        inner = heads * HD
        ff = fc1_weight.shape[1]
        pad = -half % 8
        padded = half + pad
        rows = 2 * padded
        block = -(-(rows // nt) // 8) * 8
        starts = [rows // nt * j // 8 * 8 for j in range(nt)]
        chunk = width // 8
        direct = nf == 4
        c = lax.axis_index("ctx")
        f = lax.axis_index("fsdp")
        t = lax.axis_index("tp")
        b = f if direct else 0
        start_of = jnp.asarray(starts, jnp.int32)

        def other_core(value):
            return lax.ppermute(value, "ctx", [(0, 1), (1, 0)])

        def to_tp(value, k):
            return lax.ppermute(value, "tp", xor_pairs(nt, k))

        def to_fsdp(value, k):
            return lax.ppermute(value, "fsdp", xor_pairs(nf, k))

        def pick(value, index, axis=0):
            return lax.dynamic_index_in_dim(value, index, axis, False)

        def frame(keep, received):
            zero = jnp.zeros((pad, width), keep.dtype)
            return jnp.concatenate([keep, zero, received, zero], 0)

        x_recv = other_core(pick(inputs, 1 - c))
        cot_recv = other_core(pick(cotangent, 1 - c))

        mark = (jnp.arange(nf) == f).astype(LOW)
        vectors = jnp.stack([norm1_gain, norm1_bias, proj_bias, norm2_gain, norm2_bias, fc2_bias])
        vectors = (vectors[:, None, :] * mark[None, :, None]).reshape(6, width)
        up_bias = (fc1_bias[:, None, :] * mark[None, :, None]).reshape(1, ff)
        qv_flat = (qv_bias[:, :, None, :] * mark[None, None, :, None]).reshape(1, 2 * inner)
        qv_flat = jnp.pad(qv_flat, ((0, 0), (0, width - 2 * inner)))
        small = jnp.concatenate([vectors, up_bias, qv_flat], 0)
        small = jnp.concatenate(
            [small[:, : 3 * inner], jnp.pad(small[:, 3 * inner :], ((0, 0), (0, 6 * inner - width)))], 0
        )

        qkv_rows = qkv_weight.reshape(shard, 3 * inner)
        if direct:
            half_qkv = lax.dynamic_slice_in_dim(qkv_rows, c * chunk, chunk, 0)
            sent = jnp.concatenate([half_qkv, small], 0)
            got = [to_fsdp(sent, k) for k in (1, 2, 3)]
            proj_half = lax.dynamic_slice_in_dim(proj_weight.T, c * chunk, chunk, 0)
            proj_parts = [proj_half] + [to_tp(proj_half, k) for k in range(1, nt)]
            shared = [other_core(g) for g in got]
            qkv_all = jnp.zeros((4, 2, chunk, 3 * inner), LOW)
            qkv_all = lax.dynamic_update_slice(qkv_all, qkv_rows.reshape(1, 2, chunk, 3 * inner), (f, 0, 0, 0))
            small_all = small.astype(F32)
            for k in (1, 2, 3):
                qkv_all = lax.dynamic_update_slice(qkv_all, got[k - 1][None, None, :chunk], (f ^ k, c, 0, 0))
                qkv_all = lax.dynamic_update_slice(qkv_all, shared[k - 1][None, None, :chunk], (f ^ k, 1 - c, 0, 0))
                small_all = small_all + got[k - 1][chunk:].astype(F32)
            rest = jnp.concatenate(
                [
                    lax.dynamic_slice_in_dim(fc1_weight, c * chunk, chunk, 0),
                    lax.dynamic_slice_in_dim(fc2_weight.T, c * chunk, chunk, 0),
                ]
                + proj_parts,
                1,
            )
            rest_got = [rest] + [to_fsdp(rest, k) for k in (1, 2, 3)]
            rest_shared = [other_core(g) for g in rest_got]
            rest_all = jnp.zeros((4, 2, chunk, rest.shape[1]), LOW)
            for k in range(4):
                rest_all = lax.dynamic_update_slice(rest_all, rest_got[k][None, None], (f ^ k, c, 0, 0))
                rest_all = lax.dynamic_update_slice(rest_all, rest_shared[k][None, None], (f ^ k, 1 - c, 0, 0))
        else:
            qkv_all = lax.all_gather(qkv_rows, "fsdp", axis=0, tiled=True)
            small_all = jnp.sum(lax.all_gather(small, "fsdp", axis=0).astype(F32), 0)
            proj_t = proj_weight.T
            proj_parts = [proj_t] + [to_tp(proj_t, k) for k in range(1, nt)]
            rest = jnp.concatenate([fc1_weight, fc2_weight.T] + proj_parts, 1)
            rest_all = lax.all_gather(rest, "fsdp", axis=0, tiled=True)
        qkv_all = qkv_all.reshape(width, 3 * inner)
        rest_all = rest_all.reshape(width, -1)
        small_all = jnp.concatenate([small_all[:8], small_all[8:, : width - 3 * inner]], 1)
        gain_one, bias_one, proj_b, gain_two, bias_two, down_b, up_b = [small_all[i : i + 1] for i in range(7)]
        query_b, value_b = small_all[7:8, :inner], small_all[7:8, inner : 2 * inner]
        w_up, w_down_t, w_proj_t = rest_all[:, :ff], rest_all[:, ff : 2 * ff], rest_all[:, 2 * ff :]

        stream = frame(pick(inputs, c), x_recv).astype(F32)
        normal_one, inverse_one = normalise(stream)
        normed_low = (normal_one * gain_one + bias_one).astype(LOW)
        projected = dot(normed_low, qkv_all, NN)
        query = ((projected[:, :inner] + query_b) * QUERY_SCALE).astype(LOW)
        key = projected[:, inner : 2 * inner].astype(LOW)
        value = (projected[:, 2 * inner :] + value_b).astype(LOW)
        valid = (jnp.arange(rows) % padded < half)[None]
        soft = []
        attended = []
        for h in range(heads):
            cut = slice(h * HD, (h + 1) * HD)
            scores = jnp.where(valid, dot(query[:, cut], key[:, cut], NT), -1e30)
            exponent = jnp.exp(scores - jnp.max(scores, -1, keepdims=True))
            soft.append(exponent / jnp.sum(exponent, -1, keepdims=True))
            attended.append(dot(soft[h].astype(LOW), value[:, cut], NN).astype(LOW))
        attended = jnp.concatenate(attended, 1)
        att = [attended] + [to_tp(attended, k) for k in range(1, nt)]

        grad_out_low = frame(pick(cotangent, c), cot_recv)
        grad_out = grad_out_low.astype(F32)
        branch = sum(dot(att[k], w_proj_t[:, k * inner : (k + 1) * inner], NT) for k in range(nt))
        middle = stream + branch + proj_b
        normal_two, inverse_two = normalise(middle)
        normed2_low = (normal_two * gain_two + bias_two).astype(LOW)
        pre_act = dot(normed2_low, w_up, NN) + up_b
        activated, gelu_pull = jax.vjp(exact_gelu, pre_act)
        hidden = activated.astype(LOW)
        grad_pre = gelu_pull(dot(grad_out_low, w_down_t, NN))[0].astype(LOW)
        grad_normed_two = dot(grad_pre, w_up, NT)
        part_middle = grad_out * (1.0 / nt) + norm_backward(grad_normed_two, normal_two, inverse_two, gain_two)
        part_low = part_middle.astype(LOW)
        part_att = dot(part_low, w_proj_t, NN)
        att_got = [to_tp(part_att[:, k * inner : (k + 1) * inner].astype(LOW), k) for k in range(1, nt)]

        out_part = dot(hidden, w_down_t, NT)

        def row_block(value, j):
            return lax.dynamic_slice_in_dim(value, pick(start_of, j), block, 0)

        out_got = [to_tp(row_block(out_part, t ^ k).astype(LOW), k) for k in range(1, nt)]
        out_sum = row_block(out_part, t) + row_block(middle, t) + down_b
        for g in out_got:
            out_sum = out_sum + g.astype(F32)
        out_own = out_sum.astype(LOW)

        def whole_rows(own):
            whole = jnp.zeros((rows, width), own.dtype)
            whole = lax.dynamic_update_slice(whole, own, (pick(start_of, t), 0))
            for k in range(1, nt):
                whole = lax.dynamic_update_slice(whole, to_tp(own, k), (pick(start_of, t ^ k), 0))
            theirs = other_core(whole[padded : padded + half])
            mine = whole[:half]
            return jnp.stack([jnp.where(c == 0, mine, theirs), jnp.where(c == 0, theirs, mine)])

        output = whole_rows(out_own)

        grad_rest = jnp.concatenate(
            [dot(normed2_low, grad_pre, TN), dot(grad_out_low, hidden, TN), dot(part_low, jnp.concatenate(att, 1), TN)], 1
        )

        def scatter(grad):
            if not direct:
                total = lax.psum(grad.astype(LOW), "ctx")
                total = lax.psum_scatter(total, "fsdp", scatter_dimension=0, tiled=True)
                return total.astype(F32)
            parts = grad.reshape(4, 2, chunk, grad.shape[1])
            keep, sent = pick(parts, c, 1), pick(parts, 1 - c, 1)
            total = keep + other_core(sent.astype(LOW)).astype(F32)
            own = pick(total, f)
            for k in (1, 2, 3):
                own = own + to_fsdp(pick(total, f ^ k).astype(LOW), k).astype(F32)
            return own

        def both_halves(own):
            if not direct:
                return own
            theirs = other_core(own.astype(LOW)).astype(F32)
            return jnp.concatenate([jnp.where(c == 0, own, theirs), jnp.where(c == 0, theirs, own)], 0)

        rest_own = scatter(grad_rest)
        proj_own = rest_own[:, 2 * ff : 2 * ff + inner]
        for k in range(1, nt):
            cut = rest_own[:, 2 * ff + k * inner : 2 * ff + (k + 1) * inner]
            proj_own = proj_own + to_tp(cut.astype(LOW), k).astype(F32)
        rest_final = both_halves(jnp.concatenate([rest_own[:, : 2 * ff], proj_own], 1))
        fc1_grad = rest_final[:, :ff]
        fc2_grad = rest_final[:, ff : 2 * ff].T
        proj_grad = rest_final[:, 2 * ff :].T

        grad_att = part_att[:, :inner]
        for g in att_got:
            grad_att = grad_att + g.astype(F32)
        grad_att = grad_att.astype(LOW)
        grads = [[], [], []]
        for h in range(heads):
            cut = slice(h * HD, (h + 1) * HD)
            grad_soft = dot(grad_att[:, cut], value[:, cut], NT)
            delta = jnp.sum(soft[h] * grad_soft, -1, keepdims=True)
            grad_scores = (soft[h] * (grad_soft - delta)).astype(LOW)
            grads[0].append(dot(grad_scores, key[:, cut], NN).astype(LOW) * QUERY_SCALE)
            grads[1].append(dot(grad_scores, query[:, cut], TN).astype(LOW))
            grads[2].append(dot(soft[h].astype(LOW), grad_att[:, cut], TN).astype(LOW))
        grad_qkv = jnp.concatenate(grads[0] + grads[1] + grads[2], 1)
        grad_normed_one = dot(grad_qkv, qkv_all, NT)
        part_input = part_middle + norm_backward(grad_normed_one, normal_one, inverse_one, gain_one)

        def total_rows(value):
            return jnp.sum(value, 0, keepdims=True)

        small_part = jnp.concatenate(
            [
                total_rows(grad_normed_one * normal_one),
                total_rows(grad_normed_one),
                total_rows(part_middle),
                total_rows(grad_normed_two * normal_two),
                total_rows(grad_normed_two),
                total_rows(grad_out) * (1.0 / nt),
                jnp.zeros((2, width), F32),
            ],
            0,
        )

        def input_block(k):
            return jnp.concatenate([row_block(part_input, t ^ k), small_part], 0)

        in_sum = input_block(0)
        for k in range(1, nt):
            in_sum = in_sum + to_tp(input_block(k).astype(LOW), k).astype(F32)
        input_grad = whole_rows(in_sum[:block].astype(LOW)).astype(F32)
        vector_sums = in_sum[block : block + 6].reshape(6, nf, shard)

        up_sum = jnp.sum(grad_pre.astype(F32), 0).reshape(-1, nf, fc1_bias.shape[1])
        both = grad_qkv.astype(F32)
        qv_sum = jnp.stack([jnp.sum(both[:, :inner], 0), jnp.sum(both[:, 2 * inner :], 0)])
        qv_sum = qv_sum.reshape(2 * heads, nf, qv_bias.shape[2])
        small_grads = jnp.concatenate(
            [
                vector_sums.transpose(1, 0, 2).reshape(nf, -1),
                up_sum.transpose(1, 0, 2).reshape(nf, -1),
                qv_sum.transpose(1, 0, 2).reshape(nf, -1),
            ],
            1,
        )
        if direct:
            own = pick(small_grads, f)
            for k in (1, 2, 3):
                own = own + to_fsdp(pick(small_grads, f ^ k).astype(LOW)[None], k)[0].astype(F32)
            own = own + other_core(own.astype(LOW)[None])[0].astype(F32)
        else:
            own = pick(lax.psum(small_grads, ("fsdp", "ctx")), f)
        vector_grads = own[: 6 * shard].reshape(6, shard)
        up_grad = own[6 * shard : 6 * shard + fc1_bias.size].reshape(fc1_bias.shape)
        qv_grad = own[6 * shard + fc1_bias.size :].reshape(qv_bias.shape)

        qkv_grad = both_halves(scatter(dot(normed_low, grad_qkv, TN))).reshape(qkv_weight.shape)
        return (
            output,
            input_grad,
            vector_grads[0],
            vector_grads[1],
            qkv_grad,
            qv_grad,
            proj_grad,
            vector_grads[2],
            vector_grads[3],
            vector_grads[4],
            fc1_grad,
            up_grad,
            fc2_grad,
            vector_grads[5],
        )

    return local


def solution(mesh):
    sizes = mesh.shape
    return jax.shard_map(
        build(sizes["fsdp"], sizes["ctx"], sizes["tp"]),
        mesh=mesh,
        in_specs=(
            P("fsdp", "ctx", None),
            P("fsdp"),
            P("fsdp"),
            P("fsdp", None, "tp"),
            P(None, "tp", "fsdp"),
            P("tp", "fsdp"),
            P("fsdp"),
            P("fsdp"),
            P("fsdp"),
            P("fsdp", "tp"),
            P("tp", "fsdp"),
            P("tp", "fsdp"),
            P("fsdp"),
            P("fsdp", "ctx", None),
        ),
        out_specs=(
            P("fsdp", "ctx", None),
            P("fsdp", "ctx", None),
            P("fsdp"),
            P("fsdp"),
            P("fsdp", None, "tp"),
            P(None, "tp", "fsdp"),
            P("tp", "fsdp"),
            P("fsdp"),
            P("fsdp"),
            P("fsdp"),
            P("fsdp", "tp"),
            P("tp", "fsdp"),
            P("tp", "fsdp"),
            P("fsdp"),
        ),
        check_vma=False,
    )
```

time: 346 us -> 204 us (0.59)
  waiting for transfers between devices: 178 us -> 51.4 us
  blocking collectives: 82.4 us -> 0 us
  starting transfers between devices: 0.64 us -> 58.4 us
  local copies, waits for them, and re-layouts: 20.3 us -> 48.6 us
  between operations: 18.8 us -> 9.86 us
  other arithmetic: 21.5 us -> 15 us
    psum x4 -> x0, waiting for transfers between devices: 100 us -> none  [the longest x3 89.6 us: partial_rows(): lax.psum(product(left).astype(jnp.bfloat16), 'tp').astype(jnp.float32)]
    ppermute x0 -> x55, starting transfers between devices: none -> 58.4 us  [the longest x24 35 us: to_tp(): return lax.ppermute(value, 'tp', xor_pairs(nt, k))]
    ppermute x0 -> x55, waiting for transfers between devices: none -> 51.4 us  [the longest x24 31.9 us: to_tp(): return lax.ppermute(value, 'tp', xor_pairs(nt, k))]
    all_gather x6 -> x0, blocking collectives: 48 us -> none  [the longest x1 19.2 us: local(): lax.all_gather(qkv_weight, 'fsdp', axis=0, tiled=True)]
    reduce_scatter x3 -> x0, waiting for transfers between devices: 39.9 us -> none  [the longest x1 31.7 us: local(): lax.psum_scatter(grad_w_qkv.astype(jnp.bfloat16), 'fsdp', scatter_dimensi...]
    unnamed x2 -> x0, blocking collectives: 32 us -> none
    all_gather x2 -> x0, waiting for transfers between devices: 19.3 us -> none  [the longest x1 19.3 us: local(): lax.all_gather(fc2_weight, 'fsdp', axis=1, tiled=True)]
    unnamed x13 -> x0, waiting for transfers between devices: 18.7 us -> none
  transfers between devices with their start and end apart: 11 -> 55, of which waited for: 8 -> 22; matrix products, arithmetic and copies ran while one was open for 9% -> 33% of each run, Pallas kernels for 0% -> 0%
where the time goes in v1:
time: 204 us
  starting transfers between devices  58.4 us (29%)
  waiting for transfers between devices  51.4 us (25%)
  local copies, waits for them, and re-layouts  48.6 us (24%)
  matrix products  20.2 us (10%)
  other arithmetic  15 us (7%)
  between operations  9.86 us (5%)
    ppermute x24, starting transfers between devices, to_tp(): return lax.ppermute(value, 'tp', xor_pairs(nt, k))  35 us
    ppermute x24, waiting for transfers between devices, to_tp(): return lax.ppermute(value, 'tp', xor_pairs(nt, k))  31.9 us
    ppermute x15, starting transfers between devices, to_fsdp(): return lax.ppermute(value, 'fsdp', xor_pairs(nf, k))  20.8 us
    dot_general x33, matrix products, dot(): lax.dot_general(left, right, (dims, ((), ())), preferred_element_type=F32)  20.2 us
    ppermute x15, waiting for transfers between devices, to_fsdp(): return lax.ppermute(value, 'fsdp', xor_pairs(nf, k))  15.1 us
    concatenate x1, local copies, waits for them, and re-layouts, local(): jnp.concatenate([dot(normed2_low, grad_pre, TN), dot(grad_out_low, hidden...  8.02 us
    unnamed x79, local copies, waits for them, and re-layouts  7.63 us
    ppermute x16, waiting for transfers between devices, other_core(): return lax.ppermute(value, 'ctx', [(0, 1), (1, 0)])  4.46 us
  transfers between devices with their start and end apart: 55, of which 22 were waited for; matrix products, arithmetic and copies ran while one was open for 33% of the time, Pallas kernels for 0%

profile of v1, /device:TPU:0, one launch (start us, length us, event | category | flops | bytes accessed | tf_op | source)
XLA Modules:
  0.0 203.5 jit_solution(14388706358390907754)
XLA Ops:
  6.8 1.2 copy.125
  8.3 4.0 %collective-permute-start.3 = (bf16[112,576]{1,0:T(8,128)(2,1)S(1)}, bf16[112,576]{1,0:T(8,128)(2,1)S(1)}, u32[]{:S(2)}, u32[]{:S(2)}) collective-permute-start(bf16[112,576]{1,0:T(8,128)(2,1)S(1)} %pad_maximum_fusion.10), channel_id=1, source_target_pairs={{0,24},{8,16},{16,8},{24,0},{1,25},{9,17},{17,9},{25,1},{2,26},{10... | collective-permute-start | bytes 387080 | tf_op jit(solution)/shard_map/ppermute | solution.py:87
  12.9 1.0 constant_dynamic-slice_fusion.7
  14.0 2.0 %collective-permute-start.7 = (bf16[96,192]{1,0:T(8,128)(2,1)S(1)}, bf16[96,192]{1,0:T(8,128)(2,1)S(1)}, u32[]{:S(2)}, u32[]{:S(2)}) collective-permute-start(bf16[96,192]{1,0:T(8,128)(2,1)S(1)} %bitcast.170), channel_id=1, source_target_pairs={{0,1},{1,0},{2,3},{3,2},{4,5},{5,4},{6,7},{7,6},{8,9},{9,8},{10,11... | collective-permute-start | bytes 110600 | tf_op jit(solution)/shard_map/ppermute | solution.py:84
  16.1 2.6 %collective-permute-start.8 = (bf16[96,192]{1,0:T(8,128)(2,1)S(1)}, bf16[96,192]{1,0:T(8,128)(2,1)S(1)}, u32[]{:S(2)}, u32[]{:S(2)}) collective-permute-start(bf16[96,192]{1,0:T(8,128)(2,1)S(1)} %bitcast.171), channel_id=1, source_target_pairs={{0,2},{1,3},{2,0},{3,1},{4,6},{5,7},{6,4},{7,5},{8,10},{9,11},{10,... | collective-permute-start | bytes 110600 | tf_op jit(solution)/shard_map/ppermute | solution.py:84
  18.7 1.2 copy.144
  20.2 1.0 broadcast_in_dim.122
  21.9 1.2 constant_dynamic-slice_fusion.6
  33.3 1.7 collective-permute-start.11
  35.0 1.5 collective-permute-start.13
  38.1 0.9 collective-permute-done.4
  42.9 1.7 fusion.161
  47.6 3.7 %collective-permute-done.17 = bf16[208,192]{0,1:T(8,128)(2,1)S(1)} collective-permute-done((bf16[208,192]{0,1:T(8,128)(2,1)S(1)}, bf16[208,192]{0,1:T(8,128)(2,1)S(1)}, u32[]{:S(2)}, u32[]{:S(2)}) %collective-permute-start.17) | collective-permute-done | bytes 79904 | tf_op jit(solution)/shard_map/ppermute | solution.py:84
  51.3 2.6 %collective-permute-start.18 = (bf16[208,192]{0,1:T(8,128)(2,1)S(1)}, bf16[208,192]{0,1:T(8,128)(2,1)S(1)}, u32[]{:S(2)}, u32[]{:S(2)}) collective-permute-start(bf16[208,192]{0,1:T(8,128)(2,1)S(1)} %pad_maximum_fusion.11), channel_id=1, source_target_pairs={{0,2},{1,3},{2,0},{3,1},{4,6},{5,7},{6,4},{7,5},{8,10},{9,11},{10,... | collective-permute-start | bytes 239624 | tf_op jit(solution)/shard_map/ppermute | solution.py:84
  53.9 4.7 %collective-permute-done.18 = bf16[208,192]{0,1:T(8,128)(2,1)S(1)} collective-permute-done((bf16[208,192]{0,1:T(8,128)(2,1)S(1)}, bf16[208,192]{0,1:T(8,128)(2,1)S(1)}, u32[]{:S(2)}, u32[]{:S(2)}) %collective-permute-start.18) | collective-permute-done | bytes 79904 | tf_op jit(solution)/shard_map/ppermute | solution.py:84
  58.6 3.5 %collective-permute-start.19 = (bf16[208,192]{0,1:T(8,128)(2,1)S(1)}, bf16[208,192]{0,1:T(8,128)(2,1)S(1)}, u32[]{:S(2)}, u32[]{:S(2)}) collective-permute-start(bf16[208,192]{0,1:T(8,128)(2,1)S(1)} %pad_maximum_fusion.11), channel_id=1, source_target_pairs={{0,3},{1,2},{2,1},{3,0},{4,7},{5,6},{6,5},{7,4},{8,11},{9,10},{10,... | collective-permute-start | bytes 239624 | tf_op jit(solution)/shard_map/ppermute | solution.py:84
  62.1 3.0 %collective-permute-done.19 = bf16[208,192]{0,1:T(8,128)(2,1)S(1)} collective-permute-done((bf16[208,192]{0,1:T(8,128)(2,1)S(1)}, bf16[208,192]{0,1:T(8,128)(2,1)S(1)}, u32[]{:S(2)}, u32[]{:S(2)}) %collective-permute-start.19) | collective-permute-done | bytes 79904 | tf_op jit(solution)/shard_map/ppermute | solution.py:84
  70.3 1.7 multiply_convert_fusion
  74.8 2.2 %fusion.145 = f32[768,768]{0,1:T(8,128)} fusion(bf16[208,768]{1,0:T(8,128)(2,1)S(1)} %get-tuple-element.188, f32[208,768]{1,0:T(8,128)S(1)} %get-tuple-element.175, f32[768]{0:T(1024)S(1)} %get-tuple-element.96, f32[768]{0:T(1024)S(1)} %get-tuple-element.97, f32[208]{0:T(256)S(1)} %add_rsqrt_fusion, f32[208]{0:T(256)S(1)} %broadcast_multiply_fusion.8), kind=kOutput, calls=%fused_computation.308 | convolution fusion | flops 246165504 | bytes 3325568 | tf_op jit(solution)/shard_map/dot_general | solution.py:14
  78.4 3.5 %collective-permute-start.22 = (bf16[56,768]{1,0:T(8,128)(2,1)}, bf16[56,768]{1,0:T(8,128)(2,1)}, u32[]{:S(2)}, u32[]{:S(2)}) collective-permute-start(bf16[56,768]{1,0:T(8,128)(2,1)} %get-tuple-element.130), channel_id=1, source_target_pairs={{0,3},{1,2},{2,1},{3,0},{4,7},{5,6},{6,5},{7,4},{8,11},{9,10},{10,... | collective-permute-start | bytes 258056 | tf_op jit(solution)/shard_map/ppermute | solution.py:84
  81.9 1.3 fusion.166
  84.4 2.5 %collective-permute-start.29 = (bf16[208,192]{1,0:T(8,128)(2,1)}, bf16[208,192]{1,0:T(8,128)(2,1)}, u32[]{:S(2)}, u32[]{:S(2)}) collective-permute-start(bf16[208,192]{1,0:T(8,128)(2,1)} %get-tuple-element.145), channel_id=1, source_target_pairs={{0,2},{1,3},{2,0},{3,1},{4,6},{5,7},{6,4},{7,5},{8,10},{9,11},{10,... | collective-permute-start | bytes 239624 | tf_op jit(solution)/shard_map/ppermute | solution.py:84
  86.9 1.5 collective-permute-start.28
  91.1 1.6 fusion.78
  92.7 1.4 fusion.146
  94.1 3.2 %pad_maximum_fusion = f32[768,2304]{0,1:T(8,128)} fusion(f32[768,768]{0,1:T(8,128)S(1)} %fusion.78, f32[768,768]{0,1:T(8,128)S(1)} %fusion.146, f32[768,768]{0,1:T(8,128)S(1)} %copy-done.2), kind=kLoop, calls=%fused_computation | loop fusion | flops 3538944 | bytes 14155776 | tf_op jit(solution)/shard_map/concatenate | solution.py:210
  97.3 8.0 %copy.137 = f32[768,2304]{1,0:T(8,128)} copy(f32[768,2304]{0,1:T(8,128)} %pad_maximum_fusion) | data formatting | bytes 14155776 | tf_op jit(solution)/shard_map/concatenate | solution.py:210
  105.4 3.6 %fusion = bf16[4,96,2304]{2,1,0:T(8,128)(2,1)} fusion(f32[4,2,96,2304]{3,2,1,0:T(8,128)} %bitcast.144, s32[]{:T(128)S(6)} %select_n.195), kind=kLoop, calls=%fused_computation.3 | loop fusion | bytes 3538948 | tf_op jit(solution)/shard_map/convert_element_type | solution.py:221
  109.6 1.2 fusion.68
  114.0 1.9 fusion.39
  116.4 1.4 concatenate.79
  117.8 2.9 %collective-permute-start.33 = (bf16[64,768]{1,0:T(8,128)(2,1)}, bf16[64,768]{1,0:T(8,128)(2,1)}, u32[]{:S(2)}, u32[]{:S(2)}) collective-permute-start(bf16[64,768]{1,0:T(8,128)(2,1)} %concatenate.79), channel_id=1, source_target_pairs={{0,3},{1,2},{2,1},{3,0},{4,7},{5,6},{6,5},{7,4},{8,11},{9,10},{10,... | collective-permute-start | bytes 294920 | tf_op jit(solution)/shard_map/ppermute | solution.py:84
  120.7 1.3 concatenate.78
  122.0 1.3 concatenate.77
  124.3 0.9 constant_dynamic-slice_fusion.4
  125.4 1.5 collective-permute-start.31
  126.9 1.1 constant_dynamic-update-slice_fusion.13
  129.6 5.0 %collective-permute-done.23 = bf16[56,768]{1,0:T(8,128)(2,1)S(1)} collective-permute-done((bf16[56,768]{1,0:T(8,128)(2,1)S(1)}, bf16[56,768]{1,0:T(8,128)(2,1)S(1)}, u32[]{:S(2)}, u32[]{:S(2)}) %collective-permute-start.23) | collective-permute-done | bytes 86048 | tf_op jit(solution)/shard_map/ppermute | solution.py:84
  135.1 6.1 %collective-permute-done.24 = bf16[56,768]{1,0:T(8,128)(2,1)S(1)} collective-permute-done((bf16[56,768]{1,0:T(8,128)(2,1)S(1)}, bf16[56,768]{1,0:T(8,128)(2,1)S(1)}, u32[]{:S(2)}, u32[]{:S(2)}) %collective-permute-start.24) | collective-permute-done | bytes 86048 | tf_op jit(solution)/shard_map/ppermute | solution.py:84
  141.2 1.7 collective-permute-start.25
  144.2 2.5 %collective-permute-start.40 = (bf16[1,1440]{1,0:T(2,128)(2,1)S(1)}, bf16[1,1440]{1,0:T(2,128)(2,1)S(1)}, u32[]{:S(2)}, u32[]{:S(2)}) collective-permute-start(bf16[1,1440]{1,0:T(2,128)(2,1)S(1)} %get-tuple-element.153), channel_id=1, source_target_pairs={{0,24},{8,16},{16,8},{24,0},{1,25},{9,17},{17,9},{25,1},{2,26},{10... | collective-permute-start | bytes 8648 | tf_op jit(solution)/shard_map/ppermute | solution.py:87
  148.0 1.5 collective-permute-start.38
  150.3 1.3 collective-permute-done.38
  151.9 1.0 collective-permute-done.41
  152.9 1.2 collective-permute-start.35
  156.2 1.2 collective-permute-done.34
  157.4 1.8 collective-permute-start.36
  159.2 1.6 collective-permute-done.35
  160.8 3.0 %collective-permute-done.36 = bf16[56,768]{1,0:T(8,128)(2,1)S(1)} collective-permute-done((bf16[56,768]{1,0:T(8,128)(2,1)S(1)}, bf16[56,768]{1,0:T(8,128)(2,1)S(1)}, u32[]{:S(2)}, u32[]{:S(2)}) %collective-permute-start.36) | collective-permute-done | bytes 86048 | tf_op jit(solution)/shard_map/ppermute | solution.py:84
  164.0 0.9 copy.138
  165.3 2.9 %bitcast_add_fusion = f32[4,96,2304]{2,1,0:T(8,128)S(1)} fusion(bf16[4,96,2304]{2,1,0:T(8,128)(2,1)} %collective-permute-done.47, f32[4,2,96,2304]{3,2,1,0:T(8,128)} %bitcast.145, s32[]{:T(128)S(6)} %select_n.194), kind=kLoop, calls=%fused_computation.1 | loop fusion | flops 1769472 | bytes 8847364 | tf_op jit(solution)/shard_map/add | solution.py:221
  168.3 2.5 %collective-permute-start.50 = (bf16[96,2304]{1,0:T(8,128)(2,1)S(1)}, bf16[96,2304]{1,0:T(8,128)(2,1)S(1)}, u32[]{:S(2)}, u32[]{:S(2)}) collective-permute-start(bf16[96,2304]{1,0:T(8,128)(2,1)S(1)} %get-tuple-element.117), channel_id=1, source_target_pairs={{0,24},{8,16},{16,8},{24,0},{1,25},{9,17},{17,9},{25,1},{2,26},{10... | collective-permute-start | bytes 1327112 | tf_op jit(solution)/shard_map/ppermute | solution.py:87
  171.9 1.1 copy.139
  173.1 1.1 bitcast_add_fusion.1
  174.3 2.5 %collective-permute-start.45 = (bf16[96,576]{1,0:T(8,128)(2,1)S(1)}, bf16[96,576]{1,0:T(8,128)(2,1)S(1)}, u32[]{:S(2)}, u32[]{:S(2)}) collective-permute-start(bf16[96,576]{1,0:T(8,128)(2,1)S(1)} %get-tuple-element.124), channel_id=1, source_target_pairs={{0,24},{8,16},{16,8},{24,0},{1,25},{9,17},{17,9},{25,1},{2,26},{10... | collective-permute-start | bytes 331784 | tf_op jit(solution)/shard_map/ppermute | solution.py:87
  177.3 5.1 %collective-permute-done.50 = bf16[96,2304]{1,0:T(8,128)(2,1)S(1)} collective-permute-done((bf16[96,2304]{1,0:T(8,128)(2,1)S(1)}, bf16[96,2304]{1,0:T(8,128)(2,1)S(1)}, u32[]{:S(2)}, u32[]{:S(2)}) %collective-permute-start.50) | collective-permute-done | bytes 442400 | tf_op jit(solution)/shard_map/ppermute | solution.py:87
  182.4 1.5 collective-permute-start.43
  183.9 8.0 %collective-permute-done.49 = bf16[96,2304]{1,0:T(8,128)(2,1)S(1)} collective-permute-done((bf16[96,2304]{1,0:T(8,128)(2,1)S(1)}, bf16[96,2304]{1,0:T(8,128)(2,1)S(1)}, u32[]{:S(2)}, u32[]{:S(2)}) %collective-permute-start.49) | collective-permute-done | bytes 442400 | tf_op jit(solution)/shard_map/ppermute | solution.py:87
  192.2 1.9 collective-permute-start.53
  194.5 2.2 %collective-permute-start.51 = (bf16[96,192]{1,0:T(8,128)(2,1)S(1)}, bf16[96,192]{1,0:T(8,128)(2,1)S(1)}, u32[]{:S(2)}, u32[]{:S(2)}) collective-permute-start(bf16[96,192]{1,0:T(8,128)(2,1)S(1)} %get-tuple-element.138), channel_id=1, source_target_pairs={{0,1},{1,0},{2,3},{3,2},{4,5},{5,4},{6,7},{7,6},{8,9},{9,8},{10,11... | collective-permute-start | bytes 110600 | tf_op jit(solution)/shard_map/ppermute | solution.py:84
  196.9 1.3 collective-permute-done.53
  198.2 1.6 collective-permute-done.52
  200.2 1.1 copy.140
  201.7 1.1 fusion.50
  (317 shorter events, 49.6 us)
Async XLA Ops:
  0.6 19.2 %copy-start = (bf16[192,768]{1,0:T(8,128)(2,1)S(1)}, bf16[192,768]{1,0:T(8,128)(2,1)}, u32[]{:S(2)}) copy-start(bf16[192,768]{1,0:T(8,128)(2,1)} %param.24) | copy-start | bytes 884740
  0.7 21.3 %copy-start.5 = (bf16[2,98,768]{2,0,1:T(2,128)(2,1)S(1)}, bf16[2,98,768]{2,0,1:T(2,128)(2,1)}, u32[]{:S(2)}) copy-start(bf16[2,98,768]{2,0,1:T(2,128)(2,1)} %param.28) | copy-start | bytes 903172
  0.7 21.3 %copy-start.6 = (bf16[2,98,768]{2,0,1:T(2,128)(2,1)S(1)}, bf16[2,98,768]{2,0,1:T(2,128)(2,1)}, u32[]{:S(2)}) copy-start(bf16[2,98,768]{2,0,1:T(2,128)(2,1)} %param.15) | copy-start | bytes 903172
  6.8 16.4 %copy-start.14 = (bf16[768,192]{0,1:T(8,128)(2,1)S(1)}, bf16[768,192]{0,1:T(8,128)(2,1)}, u32[]{:S(2)}) copy-start(bf16[768,192]{0,1:T(8,128)(2,1)} %param.26) | copy-start | bytes 884740
  8.0 15.4 %copy-start.25 = (s32[4]{0:T(128)S(1)}, s32[4]{0:T(128)}, u32[]{:S(2)}) copy-start(s32[4]{0:T(128)} %constant.226.clone) | copy-start | bytes 52
  8.3 25.0 %collective-permute-start.3 = (bf16[112,576]{1,0:T(8,128)(2,1)S(1)}, bf16[112,576]{1,0:T(8,128)(2,1)S(1)}, u32[]{:S(2)}, u32[]{:S(2)}) collective-permute-start(bf16[112,576]{1,0:T(8,128)(2,1)S(1)} %pad_maximum_fusion.10), channel_id=1, source_target_pairs={{0,24},{8,16},{16,8},{24,0},{1,25},{9,17},{17,9},{25,1},{2,26},{10... | collective-permute-start | bytes 387080 | tf_op jit(solution)/shard_map/ppermute | solution.py:87
  12.3 22.7 %collective-permute-start.2 = (bf16[112,576]{1,0:T(8,128)(2,1)S(1)}, bf16[112,576]{1,0:T(8,128)(2,1)S(1)}, u32[]{:S(2)}, u32[]{:S(2)}) collective-permute-start(bf16[112,576]{1,0:T(8,128)(2,1)S(1)} %pad_maximum_fusion.10), channel_id=1, source_target_pairs={{0,16},{8,24},{16,0},{24,8},{1,17},{9,25},{17,1},{25,9},{2,18},{10... | collective-permute-start | bytes 387080 | tf_op jit(solution)/shard_map/ppermute | solution.py:87
  12.8 23.7 %collective-permute-start.1 = (bf16[112,576]{1,0:T(8,128)(2,1)S(1)}, bf16[112,576]{1,0:T(8,128)(2,1)S(1)}, u32[]{:S(2)}, u32[]{:S(2)}) collective-permute-start(bf16[112,576]{1,0:T(8,128)(2,1)S(1)} %pad_maximum_fusion.10), channel_id=1, source_target_pairs={{0,8},{8,0},{16,24},{24,16},{1,9},{9,1},{17,25},{25,17},{2,10},{10... | collective-permute-start | bytes 387080 | tf_op jit(solution)/shard_map/ppermute | solution.py:87
  14.0 9.2 %collective-permute-start.7 = (bf16[96,192]{1,0:T(8,128)(2,1)S(1)}, bf16[96,192]{1,0:T(8,128)(2,1)S(1)}, u32[]{:S(2)}, u32[]{:S(2)}) collective-permute-start(bf16[96,192]{1,0:T(8,128)(2,1)S(1)} %bitcast.170), channel_id=1, source_target_pairs={{0,1},{1,0},{2,3},{3,2},{4,5},{5,4},{6,7},{7,6},{8,9},{9,8},{10,11... | collective-permute-start | bytes 110600 | tf_op jit(solution)/shard_map/ppermute | solution.py:84
  16.1 16.5 %collective-permute-start.8 = (bf16[96,192]{1,0:T(8,128)(2,1)S(1)}, bf16[96,192]{1,0:T(8,128)(2,1)S(1)}, u32[]{:S(2)}, u32[]{:S(2)}) collective-permute-start(bf16[96,192]{1,0:T(8,128)(2,1)S(1)} %bitcast.171), channel_id=1, source_target_pairs={{0,2},{1,3},{2,0},{3,1},{4,6},{5,7},{6,4},{7,5},{8,10},{9,11},{10,... | collective-permute-start | bytes 110600 | tf_op jit(solution)/shard_map/ppermute | solution.py:84
  23.2 9.4 %collective-permute-start.9 = (bf16[96,192]{1,0:T(8,128)(2,1)S(1)}, bf16[96,192]{1,0:T(8,128)(2,1)S(1)}, u32[]{:S(2)}, u32[]{:S(2)}) collective-permute-start(bf16[96,192]{1,0:T(8,128)(2,1)S(1)} %bitcast.172), channel_id=1, source_target_pairs={{0,3},{1,2},{2,1},{3,0},{4,7},{5,6},{6,5},{7,4},{8,11},{9,10},{10,... | collective-permute-start | bytes 110600 | tf_op jit(solution)/shard_map/ppermute | solution.py:84
  32.6 5.1 %collective-permute-start = (bf16[98,768]{1,0:T(8,128)(2,1)S(1)}, bf16[98,768]{1,0:T(8,128)(2,1)S(1)}, u32[]{:S(2)}, u32[]{:S(2)}) collective-permute-start(bf16[98,768]{1,0:T(8,128)(2,1)S(1)} %bitcast.174), channel_id=1, source_target_pairs={{0,4},{4,0},{1,5},{5,1},{2,6},{6,2},{3,7},{7,3},{8,12},{12,8},{9,1... | collective-permute-start | bytes 451592 | tf_op jit(solution)/shard_map/ppermute | solution.py:81
  32.8 33.4 %collective-permute-start.10 = (bf16[96,2304]{1,0:T(8,128)(2,1)S(1)}, bf16[96,2304]{1,0:T(8,128)(2,1)S(1)}, u32[]{:S(2)}, u32[]{:S(2)}) collective-permute-start(bf16[96,2304]{1,0:T(8,128)(2,1)S(1)} %concatenate.73), channel_id=1, source_target_pairs={{0,4},{4,0},{1,5},{5,1},{2,6},{6,2},{3,7},{7,3},{8,12},{12,8},{9,1... | collective-permute-start | bytes 1327112 | tf_op jit(solution)/shard_map/ppermute | solution.py:81
  33.3 31.8 %collective-permute-start.11 = (bf16[96,2304]{1,0:T(8,128)(2,1)S(1)}, bf16[96,2304]{1,0:T(8,128)(2,1)S(1)}, u32[]{:S(2)}, u32[]{:S(2)}) collective-permute-start(bf16[96,2304]{1,0:T(8,128)(2,1)S(1)} %concatenate.73), channel_id=1, source_target_pairs={{0,8},{8,0},{16,24},{24,16},{1,9},{9,1},{17,25},{25,17},{2,10},{10... | collective-permute-start | bytes 1327112 | tf_op jit(solution)/shard_map/ppermute | solution.py:87
  35.0 30.7 %collective-permute-start.13 = (bf16[96,2304]{1,0:T(8,128)(2,1)S(1)}, bf16[96,2304]{1,0:T(8,128)(2,1)S(1)}, u32[]{:S(2)}, u32[]{:S(2)}) collective-permute-start(bf16[96,2304]{1,0:T(8,128)(2,1)S(1)} %concatenate.73), channel_id=1, source_target_pairs={{0,16},{8,24},{16,0},{24,8},{1,17},{9,25},{17,1},{25,9},{2,18},{10... | collective-permute-start | bytes 1327112 | tf_op jit(solution)/shard_map/ppermute | solution.py:87
  36.5 29.3 %collective-permute-start.15 = (bf16[96,2304]{1,0:T(8,128)(2,1)S(1)}, bf16[96,2304]{1,0:T(8,128)(2,1)S(1)}, u32[]{:S(2)}, u32[]{:S(2)}) collective-permute-start(bf16[96,2304]{1,0:T(8,128)(2,1)S(1)} %concatenate.73), channel_id=1, source_target_pairs={{0,24},{8,16},{16,8},{24,0},{1,25},{9,17},{17,9},{25,1},{2,26},{10... | collective-permute-start | bytes 1327112 | tf_op jit(solution)/shard_map/ppermute | solution.py:87
  37.7 1.4 collective-permute-start.4
  39.1 1.5 collective-permute-start.5
  40.6 1.7 collective-permute-start.6
  45.8 16.3 %copy-start.28 = (f32[208]{0:T(256)}, f32[208]{0:T(256)S(1)}, u32[]{:S(2)}) copy-start(f32[208]{0:T(256)S(1)} %fusion.75) | copy-start | bytes 2500
  46.1 20.2 %copy-start.30 = (f32[208]{0:T(256)}, f32[208]{0:T(256)S(1)}, u32[]{:S(2)}) copy-start(f32[208]{0:T(256)S(1)} %fusion.77) | copy-start | bytes 2500
  46.4 4.9 %collective-permute-start.17 = (bf16[208,192]{0,1:T(8,128)(2,1)S(1)}, bf16[208,192]{0,1:T(8,128)(2,1)S(1)}, u32[]{:S(2)}, u32[]{:S(2)}) collective-permute-start(bf16[208,192]{0,1:T(8,128)(2,1)S(1)} %pad_maximum_fusion.11), channel_id=1, source_target_pairs={{0,1},{1,0},{2,3},{3,2},{4,5},{5,4},{6,7},{7,6},{8,9},{9,8},{10,11... | collective-permute-start | bytes 239624 | tf_op jit(solution)/shard_map/ppermute | solution.py:84
  51.3 7.3 %collective-permute-start.18 = (bf16[208,192]{0,1:T(8,128)(2,1)S(1)}, bf16[208,192]{0,1:T(8,128)(2,1)S(1)}, u32[]{:S(2)}, u32[]{:S(2)}) collective-permute-start(bf16[208,192]{0,1:T(8,128)(2,1)S(1)} %pad_maximum_fusion.11), channel_id=1, source_target_pairs={{0,2},{1,3},{2,0},{3,1},{4,6},{5,7},{6,4},{7,5},{8,10},{9,11},{10,... | collective-permute-start | bytes 239624 | tf_op jit(solution)/shard_map/ppermute | solution.py:84
  58.6 6.5 %collective-permute-start.19 = (bf16[208,192]{0,1:T(8,128)(2,1)S(1)}, bf16[208,192]{0,1:T(8,128)(2,1)S(1)}, u32[]{:S(2)}, u32[]{:S(2)}) collective-permute-start(bf16[208,192]{0,1:T(8,128)(2,1)S(1)} %pad_maximum_fusion.11), channel_id=1, source_target_pairs={{0,3},{1,2},{2,1},{3,0},{4,7},{5,6},{6,5},{7,4},{8,11},{9,10},{10,... | collective-permute-start | bytes 239624 | tf_op jit(solution)/shard_map/ppermute | solution.py:84
  65.1 6.9 %collective-permute-start.27 = (bf16[98,768]{1,0:T(8,128)(2,1)}, bf16[98,768]{1,0:T(8,128)(2,1)S(1)}, u32[]{:S(2)}, u32[]{:S(2)}) collective-permute-start(bf16[98,768]{1,0:T(8,128)(2,1)} %bitcast.139), channel_id=1, source_target_pairs={{0,4},{4,0},{1,5},{5,1},{2,6},{6,2},{3,7},{7,3},{8,12},{12,8},{9,1... | collective-permute-start | bytes 451592 | tf_op jit(solution)/shard_map/ppermute | solution.py:81
  65.1 2.0 collective-permute-start.12
  65.7 2.0 %collective-permute-start.14 = (bf16[96,2304]{1,0:T(8,128)(2,1)S(1)}, bf16[96,2304]{1,0:T(8,128)(2,1)S(1)}, u32[]{:S(2)}, u32[]{:S(2)}) collective-permute-start(bf16[96,2304]{1,0:T(8,128)(2,1)S(1)} %collective-permute-done.13), channel_id=1, source_target_pairs={{0,4},{4,0},{1,5},{5,1},{2,6},{6,2},{3,7},{7,3},{8,12},{12,8},{9,1... | collective-permute-start | bytes 1327112 | tf_op jit(solution)/shard_map/ppermute | solution.py:81
  65.8 2.6 %collective-permute-start.16 = (bf16[96,2304]{1,0:T(8,128)(2,1)S(1)}, bf16[96,2304]{1,0:T(8,128)(2,1)S(1)}, u32[]{:S(2)}, u32[]{:S(2)}) collective-permute-start(bf16[96,2304]{1,0:T(8,128)(2,1)S(1)} %collective-permute-done.15), channel_id=1, source_target_pairs={{0,4},{4,0},{1,5},{5,1},{2,6},{6,2},{3,7},{7,3},{8,12},{12,8},{9,1... | collective-permute-start | bytes 1327112 | tf_op jit(solution)/shard_map/ppermute | solution.py:81
  77.6 19.7 %copy-start.4 = (f32[208,768]{1,0:T(8,128)}, f32[208,768]{1,0:T(8,128)S(1)}, u32[]{:S(2)}) copy-start(f32[208,768]{1,0:T(8,128)S(1)} %fusion.20) | copy-start | bytes 1916932
  78.4 46.9 %collective-permute-start.22 = (bf16[56,768]{1,0:T(8,128)(2,1)}, bf16[56,768]{1,0:T(8,128)(2,1)}, u32[]{:S(2)}, u32[]{:S(2)}) collective-permute-start(bf16[56,768]{1,0:T(8,128)(2,1)} %get-tuple-element.130), channel_id=1, source_target_pairs={{0,3},{1,2},{2,1},{3,0},{4,7},{5,6},{6,5},{7,4},{8,11},{9,10},{10,... | collective-permute-start | bytes 258056 | tf_op jit(solution)/shard_map/ppermute | solution.py:84
  81.9 43.5 %collective-permute-start.21 = (bf16[56,768]{1,0:T(8,128)(2,1)}, bf16[56,768]{1,0:T(8,128)(2,1)}, u32[]{:S(2)}, u32[]{:S(2)}) collective-permute-start(bf16[56,768]{1,0:T(8,128)(2,1)} %get-tuple-element.131), channel_id=1, source_target_pairs={{0,2},{1,3},{2,0},{3,1},{4,6},{5,7},{6,4},{7,5},{8,10},{9,11},{10,... | collective-permute-start | bytes 258056 | tf_op jit(solution)/shard_map/ppermute | solution.py:84
  84.0 25.0 %collective-permute-start.30 = (bf16[208,192]{1,0:T(8,128)(2,1)}, bf16[208,192]{1,0:T(8,128)(2,1)}, u32[]{:S(2)}, u32[]{:S(2)}) collective-permute-start(bf16[208,192]{1,0:T(8,128)(2,1)} %get-tuple-element.144), channel_id=1, source_target_pairs={{0,3},{1,2},{2,1},{3,0},{4,7},{5,6},{6,5},{7,4},{8,11},{9,10},{10,... | collective-permute-start | bytes 239624 | tf_op jit(solution)/shard_map/ppermute | solution.py:84
  84.4 25.2 %collective-permute-start.29 = (bf16[208,192]{1,0:T(8,128)(2,1)}, bf16[208,192]{1,0:T(8,128)(2,1)}, u32[]{:S(2)}, u32[]{:S(2)}) collective-permute-start(bf16[208,192]{1,0:T(8,128)(2,1)} %get-tuple-element.145), channel_id=1, source_target_pairs={{0,2},{1,3},{2,0},{3,1},{4,6},{5,7},{6,4},{7,5},{8,10},{9,11},{10,... | collective-permute-start | bytes 239624 | tf_op jit(solution)/shard_map/ppermute | solution.py:84
  86.9 22.7 %collective-permute-start.28 = (bf16[208,192]{1,0:T(8,128)(2,1)}, bf16[208,192]{1,0:T(8,128)(2,1)}, u32[]{:S(2)}, u32[]{:S(2)}) collective-permute-start(bf16[208,192]{1,0:T(8,128)(2,1)} %get-tuple-element.143), channel_id=1, source_target_pairs={{0,1},{1,0},{2,3},{3,2},{4,5},{5,4},{6,7},{7,6},{8,9},{9,8},{10,11... | collective-permute-start | bytes 239624 | tf_op jit(solution)/shard_map/ppermute | solution.py:84
  109.0 17.9 %collective-permute-start.20 = (bf16[56,768]{1,0:T(8,128)(2,1)}, bf16[56,768]{1,0:T(8,128)(2,1)}, u32[]{:S(2)}, u32[]{:S(2)}) collective-permute-start(bf16[56,768]{1,0:T(8,128)(2,1)} %get-tuple-element.129), channel_id=1, source_target_pairs={{0,1},{1,0},{2,3},{3,2},{4,5},{5,4},{6,7},{7,6},{8,9},{9,8},{10,11... | collective-permute-start | bytes 258056 | tf_op jit(solution)/shard_map/ppermute | solution.py:84
  109.6 55.7 %collective-permute-start.47 = (bf16[4,96,2304]{2,1,0:T(8,128)(2,1)}, bf16[4,96,2304]{2,1,0:T(8,128)(2,1)}, u32[]{:S(2)}, u32[]{:S(2)}) collective-permute-start(bf16[4,96,2304]{2,1,0:T(8,128)(2,1)} %fusion), channel_id=1, source_target_pairs={{0,4},{4,0},{1,5},{5,1},{2,6},{6,2},{3,7},{7,3},{8,12},{12,8},{9,1... | collective-permute-start | bytes 5308424 | tf_op jit(solution)/shard_map/ppermute | solution.py:81
  117.8 23.4 %collective-permute-start.33 = (bf16[64,768]{1,0:T(8,128)(2,1)}, bf16[64,768]{1,0:T(8,128)(2,1)}, u32[]{:S(2)}, u32[]{:S(2)}) collective-permute-start(bf16[64,768]{1,0:T(8,128)(2,1)} %concatenate.79), channel_id=1, source_target_pairs={{0,3},{1,2},{2,1},{3,0},{4,7},{5,6},{6,5},{7,4},{8,11},{9,10},{10,... | collective-permute-start | bytes 294920 | tf_op jit(solution)/shard_map/ppermute | solution.py:84
  123.3 20.8 %copy-start.15 = (f32[4,192]{1,0:T(4,128)S(1)}, f32[4,192]{1,0:T(4,128)}, u32[]{:S(2)}) copy-start(f32[4,192]{1,0:T(4,128)} %reshape.260) | copy-start | bytes 9220
  125.3 17.6 %collective-permute-start.32 = (bf16[64,768]{1,0:T(8,128)(2,1)}, bf16[64,768]{1,0:T(8,128)(2,1)S(1)}, u32[]{:S(2)}, u32[]{:S(2)}) collective-permute-start(bf16[64,768]{1,0:T(8,128)(2,1)} %concatenate.78), channel_id=1, source_target_pairs={{0,2},{1,3},{2,0},{3,1},{4,6},{5,7},{6,4},{7,5},{8,10},{9,11},{10,... | collective-permute-start | bytes 294920 | tf_op jit(solution)/shard_map/ppermute | solution.py:84
  125.4 17.5 %collective-permute-start.31 = (bf16[64,768]{1,0:T(8,128)(2,1)}, bf16[64,768]{1,0:T(8,128)(2,1)S(1)}, u32[]{:S(2)}, u32[]{:S(2)}) collective-permute-start(bf16[64,768]{1,0:T(8,128)(2,1)} %concatenate.77), channel_id=1, source_target_pairs={{0,1},{1,0},{2,3},{3,2},{4,5},{5,4},{6,7},{7,6},{8,9},{9,8},{10,11... | collective-permute-start | bytes 294920 | tf_op jit(solution)/shard_map/ppermute | solution.py:84
  128.0 6.6 %collective-permute-start.23 = (bf16[56,768]{1,0:T(8,128)(2,1)S(1)}, bf16[56,768]{1,0:T(8,128)(2,1)S(1)}, u32[]{:S(2)}, u32[]{:S(2)}) collective-permute-start(bf16[56,768]{1,0:T(8,128)(2,1)S(1)} %get-tuple-element.113), channel_id=1, source_target_pairs={{0,1},{1,0},{2,3},{3,2},{4,5},{5,4},{6,7},{7,6},{8,9},{9,8},{10,11... | collective-permute-start | bytes 258056 | tf_op jit(solution)/shard_map/ppermute | solution.py:84
  134.6 6.6 %collective-permute-start.24 = (bf16[56,768]{1,0:T(8,128)(2,1)S(1)}, bf16[56,768]{1,0:T(8,128)(2,1)S(1)}, u32[]{:S(2)}, u32[]{:S(2)}) collective-permute-start(bf16[56,768]{1,0:T(8,128)(2,1)S(1)} %get-tuple-element.113), channel_id=1, source_target_pairs={{0,2},{1,3},{2,0},{3,1},{4,6},{5,7},{6,4},{7,5},{8,10},{9,11},{10,... | collective-permute-start | bytes 258056 | tf_op jit(solution)/shard_map/ppermute | solution.py:84
  141.2 31.9 %collective-permute-start.42 = (bf16[4,96,576]{2,1,0:T(8,128)(2,1)}, bf16[4,96,576]{2,1,0:T(8,128)(2,1)}, u32[]{:S(2)}, u32[]{:S(2)}) collective-permute-start(bf16[4,96,576]{2,1,0:T(8,128)(2,1)} %fusion.51), channel_id=1, source_target_pairs={{0,4},{4,0},{1,5},{5,1},{2,6},{6,2},{3,7},{7,3},{8,12},{12,8},{9,1... | collective-permute-start | bytes 1327112 | tf_op jit(solution)/shard_map/ppermute | solution.py:81
  141.2 6.8 %collective-permute-start.25 = (bf16[56,768]{1,0:T(8,128)(2,1)S(1)}, bf16[56,768]{1,0:T(8,128)(2,1)S(1)}, u32[]{:S(2)}, u32[]{:S(2)}) collective-permute-start(bf16[56,768]{1,0:T(8,128)(2,1)S(1)} %get-tuple-element.113), channel_id=1, source_target_pairs={{0,3},{1,2},{2,1},{3,0},{4,7},{5,6},{6,5},{7,4},{8,11},{9,10},{10,... | collective-permute-start | bytes 258056 | tf_op jit(solution)/shard_map/ppermute | solution.py:84
  144.2 5.4 %collective-permute-start.40 = (bf16[1,1440]{1,0:T(2,128)(2,1)S(1)}, bf16[1,1440]{1,0:T(2,128)(2,1)S(1)}, u32[]{:S(2)}, u32[]{:S(2)}) collective-permute-start(bf16[1,1440]{1,0:T(2,128)(2,1)S(1)} %get-tuple-element.153), channel_id=1, source_target_pairs={{0,24},{8,16},{16,8},{24,0},{1,25},{9,17},{17,9},{25,1},{2,26},{10... | collective-permute-start | bytes 8648 | tf_op jit(solution)/shard_map/ppermute | solution.py:87
  146.7 3.6 %collective-permute-start.39 = (bf16[1,1440]{1,0:T(2,128)(2,1)S(1)}, bf16[1,1440]{1,0:T(2,128)(2,1)S(1)}, u32[]{:S(2)}, u32[]{:S(2)}) collective-permute-start(bf16[1,1440]{1,0:T(2,128)(2,1)S(1)} %get-tuple-element.154), channel_id=1, source_target_pairs={{0,16},{8,24},{16,0},{24,8},{1,17},{9,25},{17,1},{25,9},{2,18},{10... | collective-permute-start | bytes 8648 | tf_op jit(solution)/shard_map/ppermute | solution.py:87
  148.0 3.6 %collective-permute-start.38 = (bf16[1,1440]{1,0:T(2,128)(2,1)S(1)}, bf16[1,1440]{1,0:T(2,128)(2,1)S(1)}, u32[]{:S(2)}, u32[]{:S(2)}) collective-permute-start(bf16[1,1440]{1,0:T(2,128)(2,1)S(1)} %get-tuple-element.152), channel_id=1, source_target_pairs={{0,8},{8,0},{16,24},{24,16},{1,9},{9,1},{17,25},{25,17},{2,10},{10... | collective-permute-start | bytes 8648 | tf_op jit(solution)/shard_map/ppermute | solution.py:87
  149.6 14.3 %collective-permute-start.26 = (bf16[98,768]{1,0:T(8,128)(2,1)S(1)}, bf16[98,768]{1,0:T(8,128)(2,1)S(1)}, u32[]{:S(2)}, u32[]{:S(2)}) collective-permute-start(bf16[98,768]{1,0:T(8,128)(2,1)S(1)} %slice.370), channel_id=1, source_target_pairs={{0,4},{4,0},{1,5},{5,1},{2,6},{6,2},{3,7},{7,3},{8,12},{12,8},{9,1... | collective-permute-start | bytes 451592 | tf_op jit(solution)/shard_map/ppermute | solution.py:81
  151.7 1.2 collective-permute-start.41
  151.8 5.6 %collective-permute-start.34 = (bf16[56,768]{1,0:T(8,128)(2,1)S(1)}, bf16[56,768]{1,0:T(8,128)(2,1)S(1)}, u32[]{:S(2)}, u32[]{:S(2)}) collective-permute-start(bf16[56,768]{1,0:T(8,128)(2,1)S(1)} %get-tuple-element.109), channel_id=1, source_target_pairs={{0,1},{1,0},{2,3},{3,2},{4,5},{5,4},{6,7},{7,6},{8,9},{9,8},{10,11... | collective-permute-start | bytes 258056 | tf_op jit(solution)/shard_map/ppermute | solution.py:84
  152.9 7.9 %collective-permute-start.35 = (bf16[56,768]{1,0:T(8,128)(2,1)S(1)}, bf16[56,768]{1,0:T(8,128)(2,1)S(1)}, u32[]{:S(2)}, u32[]{:S(2)}) collective-permute-start(bf16[56,768]{1,0:T(8,128)(2,1)S(1)} %get-tuple-element.109), channel_id=1, source_target_pairs={{0,2},{1,3},{2,0},{3,1},{4,6},{5,7},{6,4},{7,5},{8,10},{9,11},{10,... | collective-permute-start | bytes 258056 | tf_op jit(solution)/shard_map/ppermute | solution.py:84
  157.4 6.4 %collective-permute-start.36 = (bf16[56,768]{1,0:T(8,128)(2,1)S(1)}, bf16[56,768]{1,0:T(8,128)(2,1)S(1)}, u32[]{:S(2)}, u32[]{:S(2)}) collective-permute-start(bf16[56,768]{1,0:T(8,128)(2,1)S(1)} %get-tuple-element.109), channel_id=1, source_target_pairs={{0,3},{1,2},{2,1},{3,0},{4,7},{5,6},{6,5},{7,4},{8,11},{9,10},{10,... | collective-permute-start | bytes 258056 | tf_op jit(solution)/shard_map/ppermute | solution.py:84
  163.8 1.5 collective-permute-start.37
  168.3 14.0 %collective-permute-start.50 = (bf16[96,2304]{1,0:T(8,128)(2,1)S(1)}, bf16[96,2304]{1,0:T(8,128)(2,1)S(1)}, u32[]{:S(2)}, u32[]{:S(2)}) collective-permute-start(bf16[96,2304]{1,0:T(8,128)(2,1)S(1)} %get-tuple-element.117), channel_id=1, source_target_pairs={{0,24},{8,16},{16,8},{24,0},{1,25},{9,17},{17,9},{25,1},{2,26},{10... | collective-permute-start | bytes 1327112 | tf_op jit(solution)/shard_map/ppermute | solution.py:87
  170.8 21.1 %collective-permute-start.49 = (bf16[96,2304]{1,0:T(8,128)(2,1)S(1)}, bf16[96,2304]{1,0:T(8,128)(2,1)S(1)}, u32[]{:S(2)}, u32[]{:S(2)}) collective-permute-start(bf16[96,2304]{1,0:T(8,128)(2,1)S(1)} %get-tuple-element.118), channel_id=1, source_target_pairs={{0,16},{8,24},{16,0},{24,8},{1,17},{9,25},{17,1},{25,9},{2,18},{10... | collective-permute-start | bytes 1327112 | tf_op jit(solution)/shard_map/ppermute | solution.py:87
  171.4 20.5 %collective-permute-start.48 = (bf16[96,2304]{1,0:T(8,128)(2,1)S(1)}, bf16[96,2304]{1,0:T(8,128)(2,1)S(1)}, u32[]{:S(2)}, u32[]{:S(2)}) collective-permute-start(bf16[96,2304]{1,0:T(8,128)(2,1)S(1)} %get-tuple-element.116), channel_id=1, source_target_pairs={{0,8},{8,0},{16,24},{24,16},{1,9},{9,1},{17,25},{25,17},{2,10},{10... | collective-permute-start | bytes 1327112 | tf_op jit(solution)/shard_map/ppermute | solution.py:87
  174.3 20.3 %collective-permute-start.45 = (bf16[96,576]{1,0:T(8,128)(2,1)S(1)}, bf16[96,576]{1,0:T(8,128)(2,1)S(1)}, u32[]{:S(2)}, u32[]{:S(2)}) collective-permute-start(bf16[96,576]{1,0:T(8,128)(2,1)S(1)} %get-tuple-element.124), channel_id=1, source_target_pairs={{0,24},{8,16},{16,8},{24,0},{1,25},{9,17},{17,9},{25,1},{2,26},{10... | collective-permute-start | bytes 331784 | tf_op jit(solution)/shard_map/ppermute | solution.py:87
  176.7 20.0 %collective-permute-start.44 = (bf16[96,576]{1,0:T(8,128)(2,1)S(1)}, bf16[96,576]{1,0:T(8,128)(2,1)S(1)}, u32[]{:S(2)}, u32[]{:S(2)}) collective-permute-start(bf16[96,576]{1,0:T(8,128)(2,1)S(1)} %get-tuple-element.125), channel_id=1, source_target_pairs={{0,16},{8,24},{16,0},{24,8},{1,17},{9,25},{17,1},{25,9},{2,18},{10... | collective-permute-start | bytes 331784 | tf_op jit(solution)/shard_map/ppermute | solution.py:87
  182.4 14.3 %collective-permute-start.43 = (bf16[96,576]{1,0:T(8,128)(2,1)S(1)}, bf16[96,576]{1,0:T(8,128)(2,1)S(1)}, u32[]{:S(2)}, u32[]{:S(2)}) collective-permute-start(bf16[96,576]{1,0:T(8,128)(2,1)S(1)} %get-tuple-element.123), channel_id=1, source_target_pairs={{0,8},{8,0},{16,24},{24,16},{1,9},{9,1},{17,25},{25,17},{2,10},{10... | collective-permute-start | bytes 331784 | tf_op jit(solution)/shard_map/ppermute | solution.py:87
  192.2 6.0 %collective-permute-start.53 = (bf16[96,192]{1,0:T(8,128)(2,1)S(1)}, bf16[96,192]{1,0:T(8,128)(2,1)S(1)}, u32[]{:S(2)}, u32[]{:S(2)}) collective-permute-start(bf16[96,192]{1,0:T(8,128)(2,1)S(1)} %get-tuple-element.139), channel_id=1, source_target_pairs={{0,3},{1,2},{2,1},{3,0},{4,7},{5,6},{6,5},{7,4},{8,11},{9,10},{10,... | collective-permute-start | bytes 110600 | tf_op jit(solution)/shard_map/ppermute | solution.py:84
  194.1 5.6 %collective-permute-start.52 = (bf16[96,192]{1,0:T(8,128)(2,1)S(1)}, bf16[96,192]{1,0:T(8,128)(2,1)S(1)}, u32[]{:S(2)}, u32[]{:S(2)}) collective-permute-start(bf16[96,192]{1,0:T(8,128)(2,1)S(1)} %get-tuple-element.140), channel_id=1, source_target_pairs={{0,2},{1,3},{2,0},{3,1},{4,6},{5,7},{6,4},{7,5},{8,10},{9,11},{10,... | collective-permute-start | bytes 110600 | tf_op jit(solution)/shard_map/ppermute | solution.py:84
  194.5 5.2 %collective-permute-start.51 = (bf16[96,192]{1,0:T(8,128)(2,1)S(1)}, bf16[96,192]{1,0:T(8,128)(2,1)S(1)}, u32[]{:S(2)}, u32[]{:S(2)}) collective-permute-start(bf16[96,192]{1,0:T(8,128)(2,1)S(1)} %get-tuple-element.138), channel_id=1, source_target_pairs={{0,1},{1,0},{2,3},{3,2},{4,5},{5,4},{6,7},{7,6},{8,9},{9,8},{10,11... | collective-permute-start | bytes 110600 | tf_op jit(solution)/shard_map/ppermute | solution.py:84
  196.7 3.2 %collective-permute-start.46 = (bf16[96,576]{1,0:T(8,128)(2,1)S(1)}, bf16[96,576]{1,0:T(8,128)(2,1)S(1)}, u32[]{:S(2)}, u32[]{:S(2)}) collective-permute-start(bf16[96,576]{1,0:T(8,128)(2,1)S(1)} %get-tuple-element.104), channel_id=1, source_target_pairs={{0,4},{4,0},{1,5},{5,1},{2,6},{6,2},{3,7},{7,3},{8,12},{12,8},{9,1... | collective-permute-start | bytes 331784 | tf_op jit(solution)/shard_map/ppermute | solution.py:81
  199.8 1.7 collective-permute-start.54
  (23 other events, 109.3 us)

commit v2 on v1

v2 whole, which is shorter than its diff:
```python
import functools

import jax
import jax.numpy as jnp
from jax import lax
from jax.experimental import pallas as pl
from jax.experimental.pallas import tpu as pltpu
from jax.sharding import PartitionSpec as P

HD = 64
EPSILON = 1e-06
QUERY_SCALE = 0.125
F32 = jnp.float32
LOW = jnp.bfloat16
NN = ((1,), (0,))
NT = ((1,), (1,))
TN = ((0,), (0,))
VMEM = pl.BlockSpec(memory_space=pltpu.VMEM)


def dot(left, right, dims):
    return lax.dot_general(left, right, (dims, ((), ())), preferred_element_type=F32)


def shape(dims, kind):
    return jax.ShapeDtypeStruct(tuple(dims), kind)


def call(kernel, outs, args, scratch=(), name=None, mib=24, out_specs=None):
    return pl.pallas_call(
        kernel,
        out_shape=tuple(outs),
        in_specs=[VMEM] * len(args),
        out_specs=out_specs or tuple([VMEM] * len(outs)),
        scratch_shapes=list(scratch),
        name=name,
        compiler_params=pltpu.CompilerParams(vmem_limit_bytes=mib << 20),
    )(*args)


def gelu_and_slope(v):
    cdf = 0.5 * (1.0 + lax.erf(v * 0.7071067811865476))
    density = jnp.exp(-0.5 * v * v) * 0.3989422804014327
    return v * cdf, cdf + v * density


def mean(v):
    return jnp.mean(v, axis=-1, keepdims=True)


def total_rows(v):
    return jnp.sum(v, axis=0, keepdims=True)


def normalise(v):
    centred = v - mean(v)
    inverse = lax.rsqrt(mean(centred * centred) + EPSILON)
    return centred * inverse, inverse


def norm_backward(grad_normed, normal, inverse, gain):
    scaled = grad_normed * gain
    return inverse * (scaled - mean(scaled) - normal * mean(scaled * normal))


def xor_pairs(size, step):
    return [(i, i ^ step) for i in range(size)]


def lanes(parts):
    return jnp.concatenate(parts, axis=1)


def rows_of(parts):
    return jnp.concatenate(parts, axis=0)


class Sizes:
    def __init__(self, nf, nt, inputs, qv_bias, fc1_weight):
        self.nf, self.nt = nf, nt
        _, self.half, self.width = inputs.shape
        self.shard = self.width // nf
        self.heads = qv_bias.shape[1]
        self.inner = self.heads * HD
        self.ff = fc1_weight.shape[1]
        self.pad = -self.half % 8
        self.padded = self.half + self.pad
        self.rows = 2 * self.padded
        self.block = -(-(self.rows // nt) // 8) * 8
        self.chunk = self.width // 8
        self.direct = nf == 4
        self.cols = 2 * self.ff + nt * self.inner

    def start(self, j):
        return pl.multiple_of(j * (self.rows // self.nt) // 8 * 8, 8)

    def base(self):
        return lax.axis_index("fsdp") if self.direct else 0

    def core(self):
        return lax.axis_index("ctx") if self.direct else 0


EXTRA = 16
UP_AT, QV_AT = 256, 384


def pack_kernel(z, qkv, proj, vec, up_b, qv_b, sent, proj_half):
    c = lax.axis_index("ctx")
    cut = pl.ds(pl.multiple_of(c * z.chunk, 16), z.chunk)
    for i in range(3):
        sent[: z.chunk, i * z.inner : (i + 1) * z.inner] = qkv[i, cut, :]
    tail = jnp.zeros((EXTRA, 3 * z.inner), LOW)
    sent[z.chunk :, :] = tail
    sent[z.chunk : z.chunk + 8, : z.shard] = vec[...]
    sent[z.chunk : z.chunk + up_b.shape[0], UP_AT : UP_AT + up_b.shape[1]] = up_b[...]
    sent[z.chunk : z.chunk + qv_b.shape[0], QV_AT : QV_AT + qv_b.shape[1]] = qv_b[...]
    whole = proj[...].astype(F32).T.astype(LOW)
    proj_half[...] = jnp.where(c == 0, whole[: z.chunk], whole[z.chunk :])


def frame_kernel(z, keep, received, stream, normal, inverse):
    zero = jnp.zeros((z.pad, z.width), F32)
    values = rows_of([keep[...].astype(F32), zero, received[...].astype(F32), zero])
    stream[...] = values.astype(LOW)
    if normal is not None:
        n, i = normalise(values)
        normal[...] = n
        inverse[...] = jnp.broadcast_to(i, inverse.shape)


def cot_kernel(z, keep, received, stream):
    frame_kernel(z, keep, received, stream, None, None)


def attend_kernel(z, *refs):
    refs = list(refs)
    if z.direct:
        qkv, sent = refs[:2]
        got, shared = refs[2:5], refs[5:8]
        refs = refs[8:]
    else:
        qkv, vec_in, up_in, qv_in = refs[:4]
        refs = refs[4:]
    normal, small, w_out, normed_out, act, attended, soft_out = refs[:7]
    c, b = z.core(), z.base()
    if z.direct:
        gather = refs[7]
        own = lanes([qkv[i] for i in range(3)])
        w_out[b, 0] = own[: z.chunk]
        w_out[b, 1] = own[z.chunk :]
        gather[b] = sent[z.chunk :, :].astype(F32)
        for k in (1, 2, 3):
            w_out[b ^ k, c] = got[k - 1][: z.chunk, :]
            w_out[b ^ k, 1 - c] = shared[k - 1][: z.chunk, :]
            gather[b ^ k] = got[k - 1][z.chunk :, :].astype(F32)
        blocks = [gather[i] for i in range(4)]
        wide = blocks[0].shape[1]
        up_w, qv_w = HD // 4, HD // 4
        vec = lanes([g[:8, : z.shard] for g in blocks])
        up = lanes([g[: z.ff // HD, UP_AT : UP_AT + up_w] for g in blocks])
        qv = lanes([g[: 2 * z.heads, QV_AT : QV_AT + qv_w] for g in blocks])
    else:
        w_out[...] = qkv[...]
        vec, up, qv = vec_in[...], up_in[...], qv_in[...]
    up_row = lanes([up[i : i + 1] for i in range(z.ff // HD)])
    query_b = lanes([qv[2 * h : 2 * h + 1] for h in range(z.heads)])
    value_b = lanes([qv[2 * h + 1 : 2 * h + 2] for h in range(z.heads)])
    small[...] = vec
    small[6:7, : z.ff] = up_row
    normed = (normal[...] * vec[0:1] + vec[1:2]).astype(LOW)
    normed_out[...] = normed
    projected = dot(normed, w_out[...].reshape(z.width, 3 * z.inner), NN)
    n = z.inner
    query = ((projected[:, :n] + query_b) * QUERY_SCALE).astype(LOW)
    key = projected[:, n : 2 * n].astype(LOW)
    value = (projected[:, 2 * n :] + value_b).astype(LOW)
    act[0] = query
    act[1] = key
    act[2] = value
    place = lax.broadcasted_iota(jnp.int32, (z.rows, z.rows), 1)
    valid = (place < z.half) | ((place >= z.padded) & (place < z.padded + z.half))
    done = []
    for h in range(z.heads):
        cut = slice(h * HD, (h + 1) * HD)
        scores = jnp.where(valid, dot(query[:, cut], key[:, cut], NT), -1e30)
        exponent = jnp.exp(scores - jnp.max(scores, axis=-1, keepdims=True))
        soft = exponent * (1.0 / jnp.sum(exponent, axis=-1, keepdims=True))
        soft_out[h] = soft
        done.append(dot(soft.astype(LOW), value[:, cut], NN).astype(LOW))
    attended[...] = lanes(done)


def feed_kernel(z, *refs):
    refs = list(refs)
    if z.direct:
        got, shared = refs[:4], refs[4:8]
        refs = refs[8:]
    else:
        whole = refs[0]
        refs = refs[1:]
    att = refs[: z.nt]
    stream, cot, small = refs[z.nt : z.nt + 3]
    (w_out, middle_out, hidden_out, normed_out, pre_out, part_out, low_out, own_att, small_out) = refs[
        z.nt + 3 : z.nt + 12
    ]
    sends = refs[z.nt + 12 :]
    c, b = z.core(), z.base()
    if z.direct:
        for k in range(4):
            w_out[b ^ k, c] = got[k][...]
            w_out[b ^ k, 1 - c] = shared[k][...]
    else:
        w_out[...] = whole[...]
    n = z.inner
    w_up = w_out[:, :, :, : z.ff].reshape(z.width, z.ff)
    w_down_t = w_out[:, :, :, z.ff : 2 * z.ff].reshape(z.width, z.ff)
    w_proj_t = w_out[:, :, :, 2 * z.ff :].reshape(z.width, z.nt * n)
    grad_out_low = cot[...]
    grad_out = grad_out_low.astype(F32)
    branch = dot(lanes([a[...] for a in att]), w_proj_t, NT)
    middle = stream[...].astype(F32) + branch + small[2:3]
    middle_out[...] = middle
    normal, inverse = normalise(middle)
    gain = small[3:4]
    normed = (normal * gain + small[4:5]).astype(LOW)
    normed_out[...] = normed
    hidden, slope = gelu_and_slope(dot(normed, w_up, NN) + small[6:7, : z.ff])
    hidden_out[...] = hidden.astype(LOW)
    grad_pre = (dot(grad_out_low, w_down_t, NN) * slope).astype(LOW)
    pre_out[...] = grad_pre
    grad_normed = dot(grad_pre, w_up, NT)
    part = grad_out * (1.0 / z.nt) + norm_backward(grad_normed, normal, inverse, gain)
    part_out[...] = part
    low = part.astype(LOW)
    low_out[...] = low
    grad_att = dot(low, w_proj_t, NN)
    own_att[...] = grad_att[:, :n]
    for k in range(1, z.nt):
        sends[k - 1][...] = grad_att[:, k * n : (k + 1) * n].astype(LOW)
    small_out[...] = jnp.zeros(small_out.shape, F32)
    small_out[2:3] = total_rows(part)
    small_out[3:4] = total_rows(grad_normed * normal)
    small_out[4:5] = total_rows(grad_normed)
    small_out[5:6] = total_rows(grad_out) * (1.0 / z.nt)
    small_out[6:7, : z.ff] = total_rows(grad_pre.astype(F32))


def down_kernel(z, hidden, w, middle, small, own, *rest):
    sends, scratch = rest[:-1], rest[-1]
    t = lax.axis_index("tp")
    w_down_t = w[:, :, :, z.ff : 2 * z.ff].reshape(z.width, z.ff)
    scratch[...] = dot(hidden[...], w_down_t, NT)
    mine = pl.ds(z.start(t), z.block)
    own[...] = scratch[mine, :] + middle[mine, :] + small[5:6]
    for k in range(1, z.nt):
        sends[k - 1][...] = scratch[pl.ds(z.start(t ^ k), z.block), :].astype(LOW)


def store_halves(z, value, at, keep, sent):
    c, b = z.core(), z.base()
    cols = pl.ds(at, value.shape[1])
    for j in range(4):
        first = value[j * 2 * z.chunk : j * 2 * z.chunk + z.chunk]
        second = value[j * 2 * z.chunk + z.chunk : (j + 1) * 2 * z.chunk]
        if z.direct:
            keep[j ^ b, :, cols] = jnp.where(c == 0, first, second)
            sent[j ^ b, :, cols] = jnp.where(c == 0, second, first).astype(LOW)
        else:
            keep[j, :, cols] = first
            sent[j, :, cols] = second.astype(LOW)


def rest_grad_kernel(z, normed, pre, cot, hidden, low, *refs):
    att, (keep, sent) = refs[:-2], refs[-2:]
    store_halves(z, dot(normed[...], pre[...], TN), 0, keep, sent)
    store_halves(z, dot(cot[...], hidden[...], TN), z.ff, keep, sent)
    store_halves(z, dot(low[...], lanes([a[...] for a in att]), TN), 2 * z.ff, keep, sent)


def sum_cores_kernel(keep, received, own, *sends):
    own[...] = keep[0] + received[0].astype(F32)
    for k in range(1, 4):
        sends[k - 1][...] = (keep[k] + received[k].astype(F32)).astype(LOW)


def sum_fsdp_kernel(z, own, *refs):
    got, (feed, proj_own), sends = refs[:3], refs[3:5], refs[5:]
    total = own[...] + sum(g[...].astype(F32) for g in got)
    feed[...] = total[:, : 2 * z.ff]
    n = z.inner
    proj_own[...] = total[:, 2 * z.ff : 2 * z.ff + n]
    for k in range(1, z.nt):
        sends[k - 1][...] = total[:, 2 * z.ff + k * n : 2 * z.ff + (k + 1) * n].astype(LOW)


def sum_tp_kernel(z, feed, proj_own, *refs):
    got, (sent, own) = refs[:-2], refs[-2:]
    total = proj_own[...] + sum(g[...].astype(F32) for g in got)
    own[:, : 2 * z.ff] = feed[...]
    own[:, 2 * z.ff :] = total
    sent[:, : 2 * z.ff] = feed[...].astype(LOW)
    sent[:, 2 * z.ff :] = total.astype(LOW)


def rest_final_kernel(z, own, theirs, up, down, proj):
    c = lax.axis_index("ctx")
    mine, other = own[...], theirs[...].astype(F32)
    both = rows_of([jnp.where(c == 0, mine, other), jnp.where(c == 0, other, mine)])
    up[...] = both[:, : z.ff]
    down[...] = both[:, z.ff : 2 * z.ff]
    proj[...] = both[:, 2 * z.ff :].T


def back_kernel(z, *refs):
    own_att, got = refs[0], refs[1 : z.nt]
    act, soft, w, normal, inverse, part, small, small_in = refs[z.nt : z.nt + 8]
    grads_out, qv_out, own = refs[z.nt + 8 : z.nt + 11]
    sends, scratch = refs[z.nt + 11 : -1], refs[-1]
    t = lax.axis_index("tp")
    grad_att = (own_att[...] + sum(g[...].astype(F32) for g in got)).astype(LOW)
    parts = [[], [], []]
    query, key, value = act[0], act[1], act[2]
    for h in range(z.heads):
        cut = slice(h * HD, (h + 1) * HD)
        ga = grad_att[:, cut]
        p = soft[h]
        grad_soft = dot(ga, value[:, cut], NT)
        delta = jnp.sum(p * grad_soft, axis=-1, keepdims=True)
        grad_scores = (p * (grad_soft - delta)).astype(LOW)
        parts[0].append((dot(grad_scores, key[:, cut], NN).astype(LOW).astype(F32) * QUERY_SCALE).astype(LOW))
        parts[1].append(dot(grad_scores, query[:, cut], TN).astype(LOW))
        parts[2].append(dot(p.astype(LOW), ga, TN).astype(LOW))
    grads = lanes(parts[0] + parts[1] + parts[2])
    grads_out[...] = grads
    n = z.inner
    qv_out[...] = total_rows(grads.astype(F32))
    grad_normed = dot(grads, w[...].reshape(z.width, 3 * n), NT)
    scratch[...] = part[...] + norm_backward(grad_normed, normal[...], inverse[:, :1], small[0:1])
    row = lax.broadcasted_iota(jnp.int32, (8, z.width), 0)
    vec = small_in[...]
    vec = jnp.where(row == 0, total_rows(grad_normed * normal[...]), vec)
    vec = jnp.where(row == 1, total_rows(grad_normed), vec)
    own[: z.block, :] = scratch[pl.ds(z.start(t), z.block), :]
    own[z.block :, :] = vec
    for k in range(1, z.nt):
        piece = rows_of([scratch[pl.ds(z.start(t ^ k), z.block), :], vec])
        sends[k - 1][...] = piece.astype(LOW)


def qkv_grad_kernel(z, normed, grads, keep, sent):
    store_halves(z, dot(normed[...], grads[...], TN), 0, keep, sent)


def sum_rows_kernel(z, own, *refs):
    got, (block, vec) = refs[:-2], refs[-2:]
    total = own[...] + sum(g[...].astype(F32) for g in got)
    block[...] = total[: z.block].astype(LOW)
    vec[...] = total[z.block :]


def sum_qkv_kernel(z, keep, received, vec, small, qv, own, *rest):
    sends, scratch = rest[:3], rest[3]
    b = z.base()
    vectors = vec[...]
    up = rows_of([small[6:7, i * HD : (i + 1) * HD] for i in range(z.ff // HD)])
    pieces = []
    for h in range(z.heads):
        pieces.append(qv[0:1, h * HD : (h + 1) * HD])
        pieces.append(qv[0:1, 2 * z.inner + h * HD : 2 * z.inner + (h + 1) * HD])
    qv_rows = rows_of(pieces)
    scratch[...] = jnp.zeros(scratch.shape, F32)
    w = HD // 4
    for i in range(4):
        scratch[i, :8, : z.shard] = vectors[:, i * z.shard : (i + 1) * z.shard]
        scratch[i, : z.ff // HD, UP_AT : UP_AT + w] = up[:, i * w : (i + 1) * w]
        scratch[i, : 2 * z.heads, QV_AT : QV_AT + w] = qv_rows[:, i * w : (i + 1) * w]
    own[: z.chunk, :] = keep[0] + received[0].astype(F32)
    own[z.chunk :, :] = scratch[b]
    for k in range(1, 4):
        sends[k - 1][: z.chunk, :] = (keep[k] + received[k].astype(F32)).astype(LOW)
        sends[k - 1][z.chunk :, :] = scratch[b ^ k].astype(LOW)


def sum_last_kernel(own, *refs):
    got, (total, sent) = refs[:3], refs[3:]
    value = own[...] + sum(g[...].astype(F32) for g in got)
    total[...] = value
    sent[...] = value.astype(LOW)


def qkv_final_kernel(z, own, theirs, qkv, vec, up, qv):
    c = lax.axis_index("ctx")
    mine, other = own[: z.chunk, :], theirs[: z.chunk, :].astype(F32)
    both = rows_of([jnp.where(c == 0, mine, other), jnp.where(c == 0, other, mine)])
    for i in range(3):
        qkv[i] = both[:, i * z.inner : (i + 1) * z.inner]
    tail = own[z.chunk :, :] + theirs[z.chunk :, :].astype(F32)
    w = HD // 4
    vec[...] = tail[:8, : z.shard]
    up[...] = tail[: z.ff // HD, UP_AT : UP_AT + w]
    qv[...] = tail[: 2 * z.heads, QV_AT : QV_AT + w]


def rows_kernel(z, own, *refs):
    got, (mine, theirs, scratch) = refs[:-3], refs[-3:]
    t = lax.axis_index("tp")
    for k in range(z.nt):
        piece = own if k == 0 else got[k - 1]
        scratch[pl.ds(z.start(t ^ k), z.block), :] = piece[...].astype(F32)
    mine[...] = scratch[: z.half, :].astype(mine.dtype)
    theirs[...] = scratch[z.padded : z.padded + z.half, :].astype(LOW)


def build(nf, nc, nt):
    def local(
        inputs,
        norm1_gain,
        norm1_bias,
        qkv_weight,
        qv_bias,
        proj_weight,
        proj_bias,
        norm2_gain,
        norm2_bias,
        fc1_weight,
        fc1_bias,
        fc2_weight,
        fc2_bias,
        cotangent,
    ):
        z = Sizes(nf, nt, inputs, qv_bias, fc1_weight)
        part = functools.partial
        rows, width, inner, ff, chunk, block = z.rows, z.width, z.inner, z.ff, z.chunk, z.block
        c = lax.axis_index("ctx")
        f = lax.axis_index("fsdp")

        def other_core(value):
            return lax.ppermute(value, "ctx", [(0, 1), (1, 0)])

        def to_tp(value, k):
            return lax.ppermute(value, "tp", xor_pairs(nt, k))

        def to_fsdp(value, k):
            return lax.ppermute(value, "fsdp", xor_pairs(nf, k))

        def pick(value, index):
            return lax.dynamic_index_in_dim(value, index, 0, False)

        qkv3 = qkv_weight.transpose(1, 0, 2)
        down_t = fc2_weight.T
        row = lax.broadcasted_iota(jnp.int32, (8, z.shard), 0)
        vec = jnp.zeros((8, z.shard), LOW)
        for i, v in enumerate((norm1_gain, norm1_bias, proj_bias, norm2_gain, norm2_bias, fc2_bias)):
            vec = jnp.where(row == i, v[None], vec)
        qv_rows = qv_bias.transpose(1, 0, 2).reshape(2 * z.heads, -1)

        x_recv = other_core(pick(inputs, 1 - c))
        if z.direct:
            sent, proj_half = call(
                part(pack_kernel, z),
                [shape((chunk + EXTRA, 3 * inner), LOW), shape((chunk, inner), LOW)],
                [qkv3, proj_weight, vec, fc1_bias, qv_rows],
                name="pack",
            )
            got = [to_fsdp(sent, k) for k in (1, 2, 3)]
            proj_parts = [proj_half] + [to_tp(proj_half, k) for k in range(1, nt)]
            shared = [other_core(g) for g in got]
            rest = jnp.concatenate(
                [lax.dynamic_slice_in_dim(w, c * chunk, chunk, 0) for w in (fc1_weight, down_t)] + proj_parts, 1
            )
            rest_got = [rest] + [to_fsdp(rest, k) for k in (1, 2, 3)]
            rest_in = rest_got + [other_core(g) for g in rest_got]
            qkv_in = [qkv3, sent] + got + shared
        else:
            whole = lax.all_gather(qkv3, "fsdp", axis=1, tiled=True)
            whole = whole.transpose(1, 0, 2).reshape(4, 2, chunk, 3 * inner)
            vec_all = lax.all_gather(vec.astype(F32), "fsdp", axis=1, tiled=True)
            up_all = lax.all_gather(fc1_bias.astype(F32), "fsdp", axis=1, tiled=True)
            qv_all = lax.all_gather(qv_rows.astype(F32), "fsdp", axis=1, tiled=True)
            qkv_in = [whole, vec_all, up_all, qv_all]
            proj_t = proj_weight.T
            rest = jnp.concatenate([fc1_weight, down_t, proj_t] + [to_tp(proj_t, k) for k in range(1, nt)], 1)
            rest_in = [lax.all_gather(rest, "fsdp", axis=0, tiled=True).reshape(4, 2, chunk, z.cols)]

        stream, normal_one, inverse_one = call(
            part(frame_kernel, z),
            [shape((rows, width), LOW), shape((rows, width), F32), shape((rows, 128), F32)],
            [pick(inputs, c), x_recv],
            name="frame",
        )
        cot_recv = other_core(pick(cotangent, 1 - c))
        (cot,) = call(
            part(cot_kernel, z), [shape((rows, width), LOW)], [pick(cotangent, c), cot_recv], name="cotangent"
        )

        small, w_qkv, normed_one, act, attended, soft = call(
            part(attend_kernel, z),
            [
                shape((8, width), F32),
                shape((4, 2, chunk, 3 * inner), LOW),
                shape((rows, width), LOW),
                shape((3, rows, inner), LOW),
                shape((rows, inner), LOW),
                shape((z.heads, rows, rows), F32),
            ],
            qkv_in + [normal_one],
            [pltpu.VMEM((4, EXTRA, 3 * inner), F32)] if z.direct else [],
            name="attend",
        )
        att = [attended] + [to_tp(attended, k) for k in range(1, nt)]

        (w_rest, middle, hidden, normed_two, grad_pre, part_middle, part_low, own_att, small_two, *att_sends) = call(
            part(feed_kernel, z),
            [
                shape((4, 2, chunk, z.cols), LOW),
                shape((rows, width), F32),
                shape((rows, ff), LOW),
                shape((rows, width), LOW),
                shape((rows, ff), LOW),
                shape((rows, width), F32),
                shape((rows, width), LOW),
                shape((rows, inner), F32),
                shape((8, width), F32),
            ]
            + [shape((rows, inner), LOW)] * (nt - 1),
            rest_in + att + [stream, cot, small],
            name="feed",
        )
        att_got = [to_tp(att_sends[k - 1], k) for k in range(1, nt)]

        out_own, *out_sends = call(
            part(down_kernel, z),
            [shape((block, width), F32)] + [shape((block, width), LOW)] * (nt - 1),
            [hidden, w_rest, middle, small],
            [pltpu.VMEM((rows, width), F32)],
            name="down",
        )
        out_got = [to_tp(out_sends[k - 1], k) for k in range(1, nt)]

        grad_shape = (4, chunk, z.cols)
        keep, sent = call(
            part(rest_grad_kernel, z),
            [shape(grad_shape, F32), shape(grad_shape, LOW)],
            [normed_two, grad_pre, cot, hidden, part_low] + att,
            name="rest_grad",
        )

        grads, qv_sum, in_own, *in_sends = call(
            part(back_kernel, z),
            [shape((rows, 3 * inner), LOW), shape((1, 3 * inner), F32), shape((block + 8, width), F32)]
            + [shape((block + 8, width), LOW)] * (nt - 1),
            [own_att] + att_got + [act, soft, w_qkv, normal_one, inverse_one, part_middle, small, small_two],
            [pltpu.VMEM((rows, width), F32)],
            name="back",
        )
        in_got = [to_tp(in_sends[k - 1], k) for k in range(1, nt)]
        keep_qkv, sent_qkv = call(
            part(qkv_grad_kernel, z),
            [shape((4, chunk, 3 * inner), F32), shape((4, chunk, 3 * inner), LOW)],
            [normed_one, grads],
            name="qkv_grad",
        )
        in_block, vec_sum = call(
            part(sum_rows_kernel, z),
            [shape((block, width), LOW), shape((8, width), F32)],
            [in_own] + in_got,
            name="sum_rows",
        )

        def whole_rows(own, kind):
            mine, theirs = call(
                part(rows_kernel, z),
                [shape((z.half, width), kind), shape((z.half, width), LOW)],
                [own] + [to_tp(own, k) for k in range(1, nt)],
                [pltpu.VMEM((rows, width), F32)],
                name="rows",
            )
            theirs = other_core(theirs).astype(kind)
            return jnp.stack([jnp.where(c == 0, mine, theirs), jnp.where(c == 0, theirs, mine)])

        input_grad = whole_rows(in_block, F32)
        (out_low,) = call(
            lambda own, *refs: refs[-1].__setitem__(
                Ellipsis, (own[...] + sum(g[...].astype(F32) for g in refs[:-1])).astype(LOW)
            ),
            [shape((block, width), LOW)],
            [out_own] + out_got,
            name="out_sum",
        )
        output = whole_rows(out_low, LOW)

        if z.direct:
            own, *sends = call(
                sum_cores_kernel,
                [shape((chunk, z.cols), F32)] + [shape((chunk, z.cols), LOW)] * 3,
                [keep, other_core(sent)],
                name="sum_cores",
            )
            feed_own, proj_own, *sends = call(
                part(sum_fsdp_kernel, z),
                [shape((chunk, 2 * ff), F32), shape((chunk, inner), F32)] + [shape((chunk, inner), LOW)] * (nt - 1),
                [own] + [to_fsdp(sends[k - 1], k) for k in (1, 2, 3)],
                name="sum_fsdp",
            )
            to_other, own = call(
                part(sum_tp_kernel, z),
                [shape((chunk, 2 * ff + inner), LOW), shape((chunk, 2 * ff + inner), F32)],
                [feed_own, proj_own] + [to_tp(sends[k - 1], k) for k in range(1, nt)],
                name="sum_tp",
            )
            fc1_grad, fc2_grad, proj_grad = call(
                part(rest_final_kernel, z),
                [shape((z.shard, ff), F32), shape((z.shard, ff), F32), shape((inner, z.shard), F32)],
                [own, other_core(to_other)],
                name="rest_final",
            )
            own, *sends = call(
                part(sum_qkv_kernel, z),
                [shape((chunk + EXTRA, 3 * inner), F32)] + [shape((chunk + EXTRA, 3 * inner), LOW)] * 3,
                [keep_qkv, other_core(sent_qkv), vec_sum, small_two, qv_sum],
                [pltpu.VMEM((4, EXTRA, 3 * inner), F32)],
                name="sum_qkv",
            )
            own, to_other = call(
                sum_last_kernel,
                [shape((chunk + EXTRA, 3 * inner), F32), shape((chunk + EXTRA, 3 * inner), LOW)],
                [own] + [to_fsdp(sends[k - 1], k) for k in (1, 2, 3)],
                name="sum_last",
            )
            qkv_grad, vec_grad, up_grad, qv_grad = call(
                part(qkv_final_kernel, z),
                [
                    shape((3, z.shard, inner), F32),
                    shape((8, z.shard), F32),
                    shape(fc1_bias.shape, F32),
                    shape(qv_rows.shape, F32),
                ],
                [own, other_core(to_other)],
                name="qkv_final",
            )
        else:

            def scatter(keep, sent):
                whole = jnp.stack([keep.astype(LOW), sent], 1).reshape(width, -1)
                whole = lax.psum(whole, "ctx")
                return lax.psum_scatter(whole, "fsdp", scatter_dimension=0, tiled=True).astype(F32)

            rest_own = scatter(keep, sent)
            fc1_grad, fc2_grad = rest_own[:, :ff], rest_own[:, ff : 2 * ff]
            proj_grad = rest_own[:, 2 * ff : 2 * ff + inner]
            for k in range(1, nt):
                cut = rest_own[:, 2 * ff + k * inner : 2 * ff + (k + 1) * inner]
                proj_grad = proj_grad + to_tp(cut.astype(LOW), k).astype(F32)
            proj_grad = proj_grad.T
            qkv_grad = scatter(keep_qkv, sent_qkv).reshape(z.shard, 3, inner).transpose(1, 0, 2)

            def own_columns(value):
                value = lax.psum(value, ("fsdp", "ctx"))
                return lax.dynamic_slice_in_dim(value, f * (value.shape[1] // nf), value.shape[1] // nf, 1)

            vec_grad = own_columns(vec_sum)
            up_grad = own_columns(small_two[6, :ff].reshape(-1, HD))
            qv_grad = own_columns(
                qv_sum.reshape(3, z.heads, HD)[0::2].transpose(1, 0, 2).reshape(2 * z.heads, HD)
            )
        return (
            output,
            input_grad,
            vec_grad[0],
            vec_grad[1],
            qkv_grad.transpose(1, 0, 2),
            qv_grad.reshape(z.heads, 2, -1).transpose(1, 0, 2),
            proj_grad,
            vec_grad[2],
            vec_grad[3],
            vec_grad[4],
            fc1_grad,
            up_grad,
            fc2_grad.T,
            vec_grad[5],
        )

    return local


def solution(mesh):
    sizes = mesh.shape
    return jax.shard_map(
        build(sizes["fsdp"], sizes["ctx"], sizes["tp"]),
        mesh=mesh,
        in_specs=(
            P("fsdp", "ctx", None),
            P("fsdp"),
            P("fsdp"),
            P("fsdp", None, "tp"),
            P(None, "tp", "fsdp"),
            P("tp", "fsdp"),
            P("fsdp"),
            P("fsdp"),
            P("fsdp"),
            P("fsdp", "tp"),
            P("tp", "fsdp"),
            P("tp", "fsdp"),
            P("fsdp"),
            P("fsdp", "ctx", None),
        ),
        out_specs=(
            P("fsdp", "ctx", None),
            P("fsdp", "ctx", None),
            P("fsdp"),
            P("fsdp"),
            P("fsdp", None, "tp"),
            P(None, "tp", "fsdp"),
            P("tp", "fsdp"),
            P("fsdp"),
            P("fsdp"),
            P("fsdp"),
            P("fsdp", "tp"),
            P("tp", "fsdp"),
            P("tp", "fsdp"),
            P("fsdp"),
        ),
        check_vma=False,
    )
```

time: 204 us -> 168 us (0.82)
  local copies, waits for them, and re-layouts: 48.6 us -> 13 us
  waiting for transfers between devices: 51.4 us -> 84.7 us
  matrix products: 20.2 us -> 0 us
  Pallas kernels: 0 us -> 14.1 us
  other arithmetic: 15 us -> 1.93 us
  between operations: 9.86 us -> 1 us
  starting transfers between devices: 58.4 us -> 52.9 us
    dot_general x33 -> x0, matrix products: 20.2 us -> none  [dot(): lax.dot_general(left, right, (dims, ((), ())), preferred_element_type=F32)]
    ppermute x15 -> x12, waiting for transfers between devices: 15.1 us -> 33 us  [to_fsdp(): return lax.ppermute(value, 'fsdp', xor_pairs(nf, k))]
    ppermute x24, waiting for transfers between devices: 31.9 us -> 48.9 us  [to_tp(): return lax.ppermute(value, 'tp', xor_pairs(nt, k))]
    pallas_call x0 -> x20, Pallas kernels: none -> 14.1 us  [call(): pl.pallas_call(kernel, out_shape=tuple(outs), in_specs=[VMEM] * len(args)...]
    concatenate x9 -> x1, local copies, waits for them, and re-layouts: 12.5 us -> 0.11 us  [local(): jnp.concatenate([lax.dynamic_slice_in_dim(w, c * chunk, chunk, 0) for w i...]
    another operation x14 -> x0, local copies, waits for them, and re-layouts: 6.56 us -> none  [the longest x7 3.98 us: local(): jnp.stack([norm1_gain, norm1_bias, proj_bias, norm2_gain, norm2_bias, fc2...]
    ppermute x15 -> x12, starting transfers between devices: 20.8 us -> 15.2 us  [to_fsdp(): return lax.ppermute(value, 'fsdp', xor_pairs(nf, k))]
    convert_element_type x6 -> x0, local copies, waits for them, and re-layouts: 5.41 us -> none  [the longest x2 4.4 us: scatter(): total = keep + other_core(sent.astype(LOW)).astype(F32)]
  transfers between devices with their start and end apart: 55 -> 51, of which waited for: 22 -> 23; matrix products, arithmetic and copies ran while one was open for 33% -> 5% of each run, Pallas kernels for 0% -> 5%
where the time goes in v2:
time: 168 us
  waiting for transfers between devices  84.7 us (50%)
  starting transfers between devices  52.9 us (31%)
  Pallas kernels  14.1 us (8%)
  local copies, waits for them, and re-layouts  13 us (8%)
  other arithmetic  1.93 us (1%)
    ppermute x24, waiting for transfers between devices, to_tp(): return lax.ppermute(value, 'tp', xor_pairs(nt, k))  48.9 us
    ppermute x24, starting transfers between devices, to_tp(): return lax.ppermute(value, 'tp', xor_pairs(nt, k))  35.2 us
    ppermute x12, waiting for transfers between devices, to_fsdp(): return lax.ppermute(value, 'fsdp', xor_pairs(nf, k))  33 us
    ppermute x12, starting transfers between devices, to_fsdp(): return lax.ppermute(value, 'fsdp', xor_pairs(nf, k))  15.2 us
    pallas_call x20, Pallas kernels, call(): pl.pallas_call(kernel, out_shape=tuple(outs), in_specs=[VMEM] * len(args)...  14.1 us
    unnamed x24, local copies, waits for them, and re-layouts  7.55 us
  transfers between devices with their start and end apart: 51, of which 23 were waited for; matrix products, arithmetic and copies ran while one was open for 5% of the time, Pallas kernels for 5%

profile of v2, /device:TPU:0, one launch (start us, length us, event | category | flops | bytes accessed | tf_op | source)
XLA Modules:
  0.0 167.7 jit_solution(6136370276333394292)
XLA Ops:
  0.7 0.7 reshape.40.qv_b
  1.4 0.8 select_select_fusion.vec
  2.3 1.0 copy-done.1
  3.2 0.9 copy-done.3
  4.1 0.7 copy-done.6
  5.0 5.1 %collective-permute-start.2 = (bf16[96,192]{1,0:T(8,128)(2,1)S(1)}, bf16[96,192]{1,0:T(8,128)(2,1)S(1)}, u32[]{:S(2)}, u32[]{:S(2)}) collective-permute-start(bf16[96,192]{1,0:T(8,128)(2,1)S(1)} %get-tuple-element.81), channel_id=1, source_target_pairs={{0,3},{1,2},{2,1},{3,0},{4,7},{5,6},{6,5},{7,4},{8,11},{9,10},{10,... | collective-permute-start | bytes 110600 | tf_op jit(solution)/shard_map/ppermute | solution.py:442
  10.7 2.6 %collective-permute-start.12 = (bf16[112,576]{1,0:T(8,128)(2,1)S(1)}, bf16[112,576]{1,0:T(8,128)(2,1)S(1)}, u32[]{:S(2)}, u32[]{:S(2)}) collective-permute-start(bf16[112,576]{1,0:T(8,128)(2,1)S(1)} %get-tuple-element.82.refs_1_), channel_id=1, source_target_pairs={{0,24},{8,16},{16,8},{24,0},{1,25},{9,17},{17,9},{25,1},{2,26},{10... | collective-permute-start | bytes 387080 | tf_op jit(solution)/shard_map/ppermute | solution.py:445
  13.3 0.9 dynamic-slice_bitcast_fusion
  14.3 0.8 collective-permute-done.1
  15.2 2.5 %collective-permute-start.5 = (bf16[96,2304]{1,0:T(8,128)(2,1)S(1)}, bf16[96,2304]{1,0:T(8,128)(2,1)S(1)}, u32[]{:S(2)}, u32[]{:S(2)}) collective-permute-start(bf16[96,2304]{1,0:T(8,128)(2,1)S(1)} %concatenate.3.refs_0_), channel_id=1, source_target_pairs={{0,24},{8,16},{16,8},{24,0},{1,25},{9,17},{17,9},{25,1},{2,26},{10... | collective-permute-start | bytes 1327112 | tf_op jit(solution)/shard_map/ppermute | solution.py:445
  18.7 1.5 collective-permute-start.11
  20.3 1.5 collective-permute-start.10
  21.8 2.5 %constant_dynamic-slice_fusion = (bf16[1,98,768]{2,0,1:T(2,128)(2,1)S(1)}, bf16[1,98,768]{2,0,1:T(2,128)(2,1)S(1)}, bf16[1,98,768]{2,0,1:T(2,128)(2,1)S(1)}, bf16[1,98,768]{2,0,1:T(2,128)(2,1)S(1)}) fusion(bf16[2,98,768]{2,0,1:T(2,128)(2,1)} %param.27, s32[]{:T(128)S(6)} %select_n.63, s32[]{:T(128)S(6)} %select_n.62, bf16[2,98,768]{2,0,1:T(2,128)(2,1)} %param.14), kind=kLoop, calls=%fused_computation.14 | loop fusion | bytes 1204232 | tf_op jit(solution)/shard_map/jit(dynamic_index_in_dim)/dynamic_slice | solution.py:448
  24.3 15.5 %collective-permute-done.11.refs_3_ = bf16[112,576]{1,0:T(8,128)(2,1)S(1)} collective-permute-done((bf16[112,576]{1,0:T(8,128)(2,1)S(1)}, bf16[112,576]{1,0:T(8,128)(2,1)S(1)}, u32[]{:S(2)}, u32[]{:S(2)}) %collective-permute-start.11) | collective-permute-done | bytes 129056 | tf_op jit(solution)/shard_map/ppermute | solution.py:445
  40.2 0.9 collective-permute-done.16.received
  41.6 0.9 collective-permute-done.14.refs_6_
  44.1 1.3 attend.1
  45.4 1.0 collective-permute-done.20.received
  46.4 2.8 %collective-permute-start.19 = (bf16[208,192]{1,0:T(8,128)(2,1)S(1)}, bf16[208,192]{1,0:T(8,128)(2,1)S(1)}, u32[]{:S(2)}, u32[]{:S(2)}) collective-permute-start(bf16[208,192]{1,0:T(8,128)(2,1)S(1)} %get-tuple-element.84.refs_8_.refs_0_), channel_id=1, source_target_pairs={{0,3},{1,2},{2,1},{3,0},{4,7},{5,6},{6,5},{7,4},{8,11},{9,10},{10,... | collective-permute-start | bytes 239624 | tf_op jit(solution)/shard_map/ppermute | solution.py:442
  49.2 4.2 %collective-permute-done.19.refs_11_.refs_3_ = bf16[208,192]{1,0:T(8,128)(2,1)S(1)} collective-permute-done((bf16[208,192]{1,0:T(8,128)(2,1)S(1)}, bf16[208,192]{1,0:T(8,128)(2,1)S(1)}, u32[]{:S(2)}, u32[]{:S(2)}) %collective-permute-start.19) | collective-permute-done | bytes 79904 | tf_op jit(solution)/shard_map/ppermute | solution.py:442
  53.4 7.2 %collective-permute-done.18.refs_10_.refs_2_ = bf16[208,192]{1,0:T(8,128)(2,1)S(1)} collective-permute-done((bf16[208,192]{1,0:T(8,128)(2,1)S(1)}, bf16[208,192]{1,0:T(8,128)(2,1)S(1)}, u32[]{:S(2)}, u32[]{:S(2)}) %collective-permute-start.18) | collective-permute-done | bytes 79904 | tf_op jit(solution)/shard_map/ppermute | solution.py:442
  60.7 4.6 %collective-permute-done.17.refs_9_.refs_1_ = bf16[208,192]{1,0:T(8,128)(2,1)S(1)} collective-permute-done((bf16[208,192]{1,0:T(8,128)(2,1)S(1)}, bf16[208,192]{1,0:T(8,128)(2,1)S(1)}, u32[]{:S(2)}, u32[]{:S(2)}) %collective-permute-start.17) | collective-permute-done | bytes 79904 | tf_op jit(solution)/shard_map/ppermute | solution.py:442
  65.4 2.9 %feed.1 = (bf16[4,2,96,2304]{3,2,1,0:T(8,128)(2,1)S(1)}, f32[208,768]{1,0:T(8,128)S(1)}, bf16[208,768]{1,0:T(8,128)(2,1)S(1)}, bf16[208,768]{1,0:T(8,128)(2,1)S(...) custom-call(bf16[96,2304]{1,0:T(8,128)(2,1)S(1)} %concatenate.3.refs, ...), custom_call_target="tpu_custom_call" | custom-call | tf_op jit(solution)/shard_map/feed/pallas_call | solution.py:30
  68.3 1.3 rest_grad.1
  69.8 2.1 %collective-permute-start.29 = (bf16[208,192]{1,0:T(8,128)(2,1)S(1)}, bf16[208,192]{1,0:T(8,128)(2,1)S(1)}, u32[]{:S(2)}, u32[]{:S(2)}) collective-permute-start(bf16[208,192]{1,0:T(8,128)(2,1)S(1)} %get-tuple-element.98), channel_id=1, source_target_pairs={{0,2},{1,3},{2,0},{3,1},{4,6},{5,7},{6,4},{7,5},{8,10},{9,11},{10,... | collective-permute-start | bytes 239624 | tf_op jit(solution)/shard_map/ppermute | solution.py:442
  71.9 2.3 %collective-permute-start.30 = (bf16[208,192]{1,0:T(8,128)(2,1)S(1)}, bf16[208,192]{1,0:T(8,128)(2,1)S(1)}, u32[]{:S(2)}, u32[]{:S(2)}) collective-permute-start(bf16[208,192]{1,0:T(8,128)(2,1)S(1)} %get-tuple-element.99), channel_id=1, source_target_pairs={{0,3},{1,2},{2,1},{3,0},{4,7},{5,6},{6,5},{7,4},{8,11},{9,10},{10,... | collective-permute-start | bytes 239624 | tf_op jit(solution)/shard_map/ppermute | solution.py:442
  74.2 2.2 %collective-permute-done.28.refs_1_ = bf16[208,192]{1,0:T(8,128)(2,1)S(1)} collective-permute-done((bf16[208,192]{1,0:T(8,128)(2,1)S(1)}, bf16[208,192]{1,0:T(8,128)(2,1)S(1)}, u32[]{:S(2)}, u32[]{:S(2)}) %collective-permute-start.28) | collective-permute-done | bytes 79904 | tf_op jit(solution)/shard_map/ppermute | solution.py:442
  76.4 4.8 %collective-permute-done.29.refs_2_ = bf16[208,192]{1,0:T(8,128)(2,1)S(1)} collective-permute-done((bf16[208,192]{1,0:T(8,128)(2,1)S(1)}, bf16[208,192]{1,0:T(8,128)(2,1)S(1)}, u32[]{:S(2)}, u32[]{:S(2)}) %collective-permute-start.29) | collective-permute-done | bytes 79904 | tf_op jit(solution)/shard_map/ppermute | solution.py:442
  81.2 2.0 %back.1 = (bf16[208,576]{1,0:T(8,128)(2,1)S(1)}, f32[1,576]{1,0:T(1,128)S(1)}, f32[64,768]{1,0:T(8,128)S(1)}, bf16[64,768]{1,0:T(8,128)(2,1)S(1)}, bf16[64,768]{...) custom-call(f32[208,192]{1,0:T(8,128)S(1)} %get-tuple-element.96.refs_0_, ...), custom_call_target="tpu_custom_call" | custom-call | tf_op jit(solution)/shard_map/back/pallas_call | solution.py:30
  84.4 2.4 %collective-permute-start.21 = (bf16[56,768]{1,0:T(8,128)(2,1)S(1)}, bf16[56,768]{1,0:T(8,128)(2,1)S(1)}, u32[]{:S(2)}, u32[]{:S(2)}) collective-permute-start(bf16[56,768]{1,0:T(8,128)(2,1)S(1)} %get-tuple-element.91), channel_id=1, source_target_pairs={{0,1},{1,0},{2,3},{3,2},{4,5},{5,4},{6,7},{7,6},{8,9},{9,8},{10,11... | collective-permute-start | bytes 258056 | tf_op jit(solution)/shard_map/ppermute | solution.py:442
  86.9 2.2 %collective-permute-start.23 = (bf16[56,768]{1,0:T(8,128)(2,1)S(1)}, bf16[56,768]{1,0:T(8,128)(2,1)S(1)}, u32[]{:S(2)}, u32[]{:S(2)}) collective-permute-start(bf16[56,768]{1,0:T(8,128)(2,1)S(1)} %get-tuple-element.93), channel_id=1, source_target_pairs={{0,3},{1,2},{2,1},{3,0},{4,7},{5,6},{6,5},{7,4},{8,11},{9,10},{10,... | collective-permute-start | bytes 258056 | tf_op jit(solution)/shard_map/ppermute | solution.py:442
  89.2 0.7 collective-permute-done.21.refs_0_
  89.9 6.6 %collective-permute-done.22.refs_1_ = bf16[56,768]{1,0:T(8,128)(2,1)S(1)} collective-permute-done((bf16[56,768]{1,0:T(8,128)(2,1)S(1)}, bf16[56,768]{1,0:T(8,128)(2,1)S(1)}, u32[]{:S(2)}, u32[]{:S(2)}) %collective-permute-start.22) | collective-permute-done | bytes 86048 | tf_op jit(solution)/shard_map/ppermute | solution.py:442
  96.5 1.8 %collective-permute-start.26 = (bf16[56,768]{1,0:T(8,128)(2,1)S(1)}, bf16[56,768]{1,0:T(8,128)(2,1)S(1)}, u32[]{:S(2)}, u32[]{:S(2)}) collective-permute-start(bf16[56,768]{1,0:T(8,128)(2,1)S(1)} %out_sum.1.own), channel_id=1, source_target_pairs={{0,3},{1,2},{2,1},{3,0},{4,7},{5,6},{6,5},{7,4},{8,11},{9,10},{10,... | collective-permute-start | bytes 258056 | tf_op jit(solution)/shard_map/ppermute | solution.py:442
  98.4 1.6 collective-permute-start.25
  99.9 1.0 collective-permute-start.24
  101.0 2.8 %collective-permute-done.26.refs_2_ = bf16[56,768]{1,0:T(8,128)(2,1)S(1)} collective-permute-done((bf16[56,768]{1,0:T(8,128)(2,1)S(1)}, bf16[56,768]{1,0:T(8,128)(2,1)S(1)}, u32[]{:S(2)}, u32[]{:S(2)}) %collective-permute-start.26) | collective-permute-done | bytes 86048 | tf_op jit(solution)/shard_map/ppermute | solution.py:442
  103.8 2.6 %collective-permute-start.31 = (bf16[64,768]{1,0:T(8,128)(2,1)S(1)}, bf16[64,768]{1,0:T(8,128)(2,1)S(1)}, u32[]{:S(2)}, u32[]{:S(2)}) collective-permute-start(bf16[64,768]{1,0:T(8,128)(2,1)S(1)} %get-tuple-element.107), channel_id=1, source_target_pairs={{0,1},{1,0},{2,3},{3,2},{4,5},{5,4},{6,7},{7,6},{8,9},{9,8},{10,11... | collective-permute-start | bytes 294920 | tf_op jit(solution)/shard_map/ppermute | solution.py:442
  106.4 1.1 collective-permute-done.25.refs_1_
  107.5 1.4 collective-permute-start.33
  109.5 6.9 %collective-permute-done.32.refs_1_ = bf16[64,768]{1,0:T(8,128)(2,1)S(1)} collective-permute-done((bf16[64,768]{1,0:T(8,128)(2,1)S(1)}, bf16[64,768]{1,0:T(8,128)(2,1)S(1)}, u32[]{:S(2)}, u32[]{:S(2)}) %collective-permute-start.32) | collective-permute-done | bytes 98336 | tf_op jit(solution)/shard_map/ppermute | solution.py:442
  116.5 2.5 %collective-permute-start.36 = (bf16[56,768]{1,0:T(8,128)(2,1)S(1)}, bf16[56,768]{1,0:T(8,128)(2,1)S(1)}, u32[]{:S(2)}, u32[]{:S(2)}) collective-permute-start(bf16[56,768]{1,0:T(8,128)(2,1)S(1)} %get-tuple-element.110.own), channel_id=1, source_target_pairs={{0,3},{1,2},{2,1},{3,0},{4,7},{5,6},{6,5},{7,4},{8,11},{9,10},{10,... | collective-permute-start | bytes 258056 | tf_op jit(solution)/shard_map/ppermute | solution.py:442
  119.0 1.3 collective-permute-start.35
  120.3 0.6 collective-permute-start.34
  120.9 0.9 sum_qkv.1
  121.8 0.7 copy-done.7
  122.5 1.2 collective-permute-done.36.refs_2_
  123.7 1.5 collective-permute-start.39
  125.2 1.2 sum_cores.1
  126.4 1.2 collective-permute-done.35.refs_1_
  127.6 1.5 collective-permute-start.44
  129.8 0.7 copy-done.8
  130.5 1.9 %collective-permute-start.46 = (bf16[96,2304]{1,0:T(8,128)(2,1)}, bf16[96,2304]{1,0:T(8,128)(2,1)S(1)}, u32[]{:S(2)}, u32[]{:S(2)}) collective-permute-start(bf16[96,2304]{1,0:T(8,128)(2,1)} %get-tuple-element.136), channel_id=1, source_target_pairs={{0,24},{8,16},{16,8},{24,0},{1,25},{9,17},{17,9},{25,1},{2,26},{10... | collective-permute-start | bytes 1327112 | tf_op jit(solution)/shard_map/ppermute | solution.py:445
  132.4 0.9 copy-done.5
  133.5 1.1 collective-permute-start.41
  134.6 0.9 select_bitcast_fusion.1
  135.5 0.9 copy.34
  136.5 16.8 %collective-permute-done.41.refs_2_ = bf16[112,576]{1,0:T(8,128)(2,1)S(1)} collective-permute-done((bf16[112,576]{1,0:T(8,128)(2,1)}, bf16[112,576]{1,0:T(8,128)(2,1)S(1)}, u32[]{:S(2)}, u32[]{:S(2)}) %collective-permute-start.41) | collective-permute-done | bytes 129056 | tf_op jit(solution)/shard_map/ppermute | solution.py:445
  154.4 1.7 collective-permute-start.47
  156.1 2.8 %collective-permute-start.49 = (bf16[96,192]{1,0:T(8,128)(2,1)S(1)}, bf16[96,192]{1,0:T(8,128)(2,1)S(1)}, u32[]{:S(2)}, u32[]{:S(2)}) collective-permute-start(bf16[96,192]{1,0:T(8,128)(2,1)S(1)} %get-tuple-element.141), channel_id=1, source_target_pairs={{0,3},{1,2},{2,1},{3,0},{4,7},{5,6},{6,5},{7,4},{8,11},{9,10},{10,... | collective-permute-start | bytes 110600 | tf_op jit(solution)/shard_map/ppermute | solution.py:442
  158.9 4.1 %collective-permute-done.48.refs_1_ = bf16[96,192]{1,0:T(8,128)(2,1)S(1)} collective-permute-done((bf16[96,192]{1,0:T(8,128)(2,1)S(1)}, bf16[96,192]{1,0:T(8,128)(2,1)S(1)}, u32[]{:S(2)}, u32[]{:S(2)}) %collective-permute-start.48) | collective-permute-done | bytes 36896 | tf_op jit(solution)/shard_map/ppermute | solution.py:442
  163.2 1.1 copy.35
  164.4 0.9 qkv_final.1
  166.5 1.2 rest_final.1
  (97 shorter events, 10.5 us)
Async XLA Ops:
  0.6 12.7 %copy-start = (bf16[192,768]{1,0:T(8,128)(2,1)S(1)}, bf16[192,768]{1,0:T(8,128)(2,1)}, u32[]{:S(2)}) copy-start(bf16[192,768]{1,0:T(8,128)(2,1)} %param.23) | copy-start | bytes 884740
  2.2 1.0 copy-start.1
  3.2 0.9 copy-start.3
  4.1 0.7 copy-start.6
  4.8 39.3 %copy-start.2 = (bf16[192,3,192]{2,0,1:T(8,128)(2,1)S(1)}, bf16[192,3,192]{2,0,1:T(8,128)(2,1)}, u32[]{:S(2)}) copy-start(bf16[192,3,192]{2,0,1:T(8,128)(2,1)} %param.17) | copy-start | bytes 663556
  5.0 9.3 %collective-permute-start.2 = (bf16[96,192]{1,0:T(8,128)(2,1)S(1)}, bf16[96,192]{1,0:T(8,128)(2,1)S(1)}, u32[]{:S(2)}, u32[]{:S(2)}) collective-permute-start(bf16[96,192]{1,0:T(8,128)(2,1)S(1)} %get-tuple-element.81), channel_id=1, source_target_pairs={{0,3},{1,2},{2,1},{3,0},{4,7},{5,6},{6,5},{7,4},{8,11},{9,10},{10,... | collective-permute-start | bytes 110600 | tf_op jit(solution)/shard_map/ppermute | solution.py:442
  10.1 5.0 %collective-permute-start.1 = (bf16[96,192]{1,0:T(8,128)(2,1)S(1)}, bf16[96,192]{1,0:T(8,128)(2,1)S(1)}, u32[]{:S(2)}, u32[]{:S(2)}) collective-permute-start(bf16[96,192]{1,0:T(8,128)(2,1)S(1)} %get-tuple-element.81), channel_id=1, source_target_pairs={{0,2},{1,3},{2,0},{3,1},{4,6},{5,7},{6,4},{7,5},{8,10},{9,11},{10,... | collective-permute-start | bytes 110600 | tf_op jit(solution)/shard_map/ppermute | solution.py:442
  10.1 5.0 %collective-permute-start = (bf16[96,192]{1,0:T(8,128)(2,1)S(1)}, bf16[96,192]{1,0:T(8,128)(2,1)S(1)}, u32[]{:S(2)}, u32[]{:S(2)}) collective-permute-start(bf16[96,192]{1,0:T(8,128)(2,1)S(1)} %get-tuple-element.81), channel_id=1, source_target_pairs={{0,1},{1,0},{2,3},{3,2},{4,5},{5,4},{6,7},{7,6},{8,9},{9,8},{10,11... | collective-permute-start | bytes 110600 | tf_op jit(solution)/shard_map/ppermute | solution.py:442
  10.7 9.5 %collective-permute-start.12 = (bf16[112,576]{1,0:T(8,128)(2,1)S(1)}, bf16[112,576]{1,0:T(8,128)(2,1)S(1)}, u32[]{:S(2)}, u32[]{:S(2)}) collective-permute-start(bf16[112,576]{1,0:T(8,128)(2,1)S(1)} %get-tuple-element.82.refs_1_), channel_id=1, source_target_pairs={{0,24},{8,16},{16,8},{24,0},{1,25},{9,17},{17,9},{25,1},{2,26},{10... | collective-permute-start | bytes 387080 | tf_op jit(solution)/shard_map/ppermute | solution.py:445
  15.2 27.4 %collective-permute-start.5 = (bf16[96,2304]{1,0:T(8,128)(2,1)S(1)}, bf16[96,2304]{1,0:T(8,128)(2,1)S(1)}, u32[]{:S(2)}, u32[]{:S(2)}) collective-permute-start(bf16[96,2304]{1,0:T(8,128)(2,1)S(1)} %concatenate.3.refs_0_), channel_id=1, source_target_pairs={{0,24},{8,16},{16,8},{24,0},{1,25},{9,17},{17,9},{25,1},{2,26},{10... | collective-permute-start | bytes 1327112 | tf_op jit(solution)/shard_map/ppermute | solution.py:445
  17.7 25.3 %collective-permute-start.4 = (bf16[96,2304]{1,0:T(8,128)(2,1)S(1)}, bf16[96,2304]{1,0:T(8,128)(2,1)S(1)}, u32[]{:S(2)}, u32[]{:S(2)}) collective-permute-start(bf16[96,2304]{1,0:T(8,128)(2,1)S(1)} %concatenate.3.refs_0_), channel_id=1, source_target_pairs={{0,16},{8,24},{16,0},{24,8},{1,17},{9,25},{17,1},{25,9},{2,18},{10... | collective-permute-start | bytes 1327112 | tf_op jit(solution)/shard_map/ppermute | solution.py:445
  18.2 24.9 %collective-permute-start.3 = (bf16[96,2304]{1,0:T(8,128)(2,1)S(1)}, bf16[96,2304]{1,0:T(8,128)(2,1)S(1)}, u32[]{:S(2)}, u32[]{:S(2)}) collective-permute-start(bf16[96,2304]{1,0:T(8,128)(2,1)S(1)} %concatenate.3.refs_0_), channel_id=1, source_target_pairs={{0,8},{8,0},{16,24},{24,16},{1,9},{9,1},{17,25},{25,17},{2,10},{10... | collective-permute-start | bytes 1327112 | tf_op jit(solution)/shard_map/ppermute | solution.py:445
  18.7 21.0 %collective-permute-start.11 = (bf16[112,576]{1,0:T(8,128)(2,1)S(1)}, bf16[112,576]{1,0:T(8,128)(2,1)S(1)}, u32[]{:S(2)}, u32[]{:S(2)}) collective-permute-start(bf16[112,576]{1,0:T(8,128)(2,1)S(1)} %get-tuple-element.82.refs_1_), channel_id=1, source_target_pairs={{0,16},{8,24},{16,0},{24,8},{1,17},{9,25},{17,1},{25,9},{2,18},{10... | collective-permute-start | bytes 387080 | tf_op jit(solution)/shard_map/ppermute | solution.py:445
  20.3 19.6 %collective-permute-start.10 = (bf16[112,576]{1,0:T(8,128)(2,1)S(1)}, bf16[112,576]{1,0:T(8,128)(2,1)S(1)}, u32[]{:S(2)}, u32[]{:S(2)}) collective-permute-start(bf16[112,576]{1,0:T(8,128)(2,1)S(1)} %get-tuple-element.82.refs_1_), channel_id=1, source_target_pairs={{0,8},{8,0},{16,24},{24,16},{1,9},{9,1},{17,25},{25,17},{2,10},{10... | collective-permute-start | bytes 387080 | tf_op jit(solution)/shard_map/ppermute | solution.py:445
  39.7 1.4 collective-permute-start.16
  39.8 1.5 collective-permute-start.15
  41.1 1.4 collective-permute-start.14
  41.3 2.2 %collective-permute-start.13 = (bf16[112,576]{1,0:T(8,128)(2,1)S(1)}, bf16[112,576]{1,0:T(8,128)(2,1)S(1)}, u32[]{:S(2)}, u32[]{:S(2)}) collective-permute-start(bf16[112,576]{1,0:T(8,128)(2,1)S(1)} %collective-permute-done.10.refs_2_), channel_id=1, source_target_pairs={{0,4},{4,0},{1,5},{5,1},{2,6},{6,2},{3,7},{7,3},{8,12},{12,8},{9,1... | collective-permute-start | bytes 387080 | tf_op jit(solution)/shard_map/ppermute | solution.py:439
  42.5 22.9 %collective-permute-start.6 = (bf16[96,2304]{1,0:T(8,128)(2,1)S(1)}, bf16[96,2304]{1,0:T(8,128)(2,1)S(1)}, u32[]{:S(2)}, u32[]{:S(2)}) collective-permute-start(bf16[96,2304]{1,0:T(8,128)(2,1)S(1)} %concatenate.3.refs_0_), channel_id=1, source_target_pairs={{0,4},{4,0},{1,5},{5,1},{2,6},{6,2},{3,7},{7,3},{8,12},{12,8},{9,1... | collective-permute-start | bytes 1327112 | tf_op jit(solution)/shard_map/ppermute | solution.py:439
  42.6 22.7 %collective-permute-start.9 = (bf16[96,2304]{1,0:T(8,128)(2,1)S(1)}, bf16[96,2304]{1,0:T(8,128)(2,1)S(1)}, u32[]{:S(2)}, u32[]{:S(2)}) collective-permute-start(bf16[96,2304]{1,0:T(8,128)(2,1)S(1)} %collective-permute-done.5.refs_3_), channel_id=1, source_target_pairs={{0,4},{4,0},{1,5},{5,1},{2,6},{6,2},{3,7},{7,3},{8,12},{12,8},{9,1... | collective-permute-start | bytes 1327112 | tf_op jit(solution)/shard_map/ppermute | solution.py:439
  43.0 22.4 %collective-permute-start.8 = (bf16[96,2304]{1,0:T(8,128)(2,1)S(1)}, bf16[96,2304]{1,0:T(8,128)(2,1)S(1)}, u32[]{:S(2)}, u32[]{:S(2)}) collective-permute-start(bf16[96,2304]{1,0:T(8,128)(2,1)S(1)} %collective-permute-done.4.refs_2_), channel_id=1, source_target_pairs={{0,4},{4,0},{1,5},{5,1},{2,6},{6,2},{3,7},{7,3},{8,12},{12,8},{9,1... | collective-permute-start | bytes 1327112 | tf_op jit(solution)/shard_map/ppermute | solution.py:439
  43.2 22.2 %collective-permute-start.7 = (bf16[96,2304]{1,0:T(8,128)(2,1)S(1)}, bf16[96,2304]{1,0:T(8,128)(2,1)S(1)}, u32[]{:S(2)}, u32[]{:S(2)}) collective-permute-start(bf16[96,2304]{1,0:T(8,128)(2,1)S(1)} %collective-permute-done.3.refs_1_), channel_id=1, source_target_pairs={{0,4},{4,0},{1,5},{5,1},{2,6},{6,2},{3,7},{7,3},{8,12},{12,8},{9,1... | collective-permute-start | bytes 1327112 | tf_op jit(solution)/shard_map/ppermute | solution.py:439
  43.6 2.9 %collective-permute-start.20 = (bf16[98,768]{1,0:T(8,128)(2,1)S(1)}, bf16[98,768]{1,0:T(8,128)(2,1)S(1)}, u32[]{:S(2)}, u32[]{:S(2)}) collective-permute-start(bf16[98,768]{1,0:T(8,128)(2,1)S(1)} %bitcast.37), channel_id=1, source_target_pairs={{0,4},{4,0},{1,5},{5,1},{2,6},{6,2},{3,7},{7,3},{8,12},{12,8},{9,1... | collective-permute-start | bytes 451592 | tf_op jit(solution)/shard_map/ppermute | solution.py:439
  46.4 6.9 %collective-permute-start.19 = (bf16[208,192]{1,0:T(8,128)(2,1)S(1)}, bf16[208,192]{1,0:T(8,128)(2,1)S(1)}, u32[]{:S(2)}, u32[]{:S(2)}) collective-permute-start(bf16[208,192]{1,0:T(8,128)(2,1)S(1)} %get-tuple-element.84.refs_8_.refs_0_), channel_id=1, source_target_pairs={{0,3},{1,2},{2,1},{3,0},{4,7},{5,6},{6,5},{7,4},{8,11},{9,10},{10,... | collective-permute-start | bytes 239624 | tf_op jit(solution)/shard_map/ppermute | solution.py:442
  53.3 7.3 %collective-permute-start.18 = (bf16[208,192]{1,0:T(8,128)(2,1)S(1)}, bf16[208,192]{1,0:T(8,128)(2,1)S(1)}, u32[]{:S(2)}, u32[]{:S(2)}) collective-permute-start(bf16[208,192]{1,0:T(8,128)(2,1)S(1)} %get-tuple-element.84.refs_8_.refs_0_), channel_id=1, source_target_pairs={{0,2},{1,3},{2,0},{3,1},{4,6},{5,7},{6,4},{7,5},{8,10},{9,11},{10,... | collective-permute-start | bytes 239624 | tf_op jit(solution)/shard_map/ppermute | solution.py:442
  60.6 4.7 %collective-permute-start.17 = (bf16[208,192]{1,0:T(8,128)(2,1)S(1)}, bf16[208,192]{1,0:T(8,128)(2,1)S(1)}, u32[]{:S(2)}, u32[]{:S(2)}) collective-permute-start(bf16[208,192]{1,0:T(8,128)(2,1)S(1)} %get-tuple-element.84.refs_8_.refs_0_), channel_id=1, source_target_pairs={{0,1},{1,0},{2,3},{3,2},{4,5},{5,4},{6,7},{7,6},{8,9},{9,8},{10,11... | collective-permute-start | bytes 239624 | tf_op jit(solution)/shard_map/ppermute | solution.py:442
  69.7 55.5 %collective-permute-start.43 = (bf16[4,96,2304]{2,1,0:T(8,128)(2,1)S(1)}, bf16[4,96,2304]{2,1,0:T(8,128)(2,1)S(1)}, u32[]{:S(2)}, u32[]{:S(2)}) collective-permute-start(bf16[4,96,2304]{2,1,0:T(8,128)(2,1)S(1)} %get-tuple-element.132), channel_id=1, source_target_pairs={{0,4},{4,0},{1,5},{5,1},{2,6},{6,2},{3,7},{7,3},{8,12},{12,8},{9,1... | collective-permute-start | bytes 5308424 | tf_op jit(solution)/shard_map/ppermute | solution.py:439
  69.7 6.7 %collective-permute-start.28 = (bf16[208,192]{1,0:T(8,128)(2,1)S(1)}, bf16[208,192]{1,0:T(8,128)(2,1)S(1)}, u32[]{:S(2)}, u32[]{:S(2)}) collective-permute-start(bf16[208,192]{1,0:T(8,128)(2,1)S(1)} %get-tuple-element.97), channel_id=1, source_target_pairs={{0,1},{1,0},{2,3},{3,2},{4,5},{5,4},{6,7},{7,6},{8,9},{9,8},{10,11... | collective-permute-start | bytes 239624 | tf_op jit(solution)/shard_map/ppermute | solution.py:442
  69.8 11.4 %collective-permute-start.29 = (bf16[208,192]{1,0:T(8,128)(2,1)S(1)}, bf16[208,192]{1,0:T(8,128)(2,1)S(1)}, u32[]{:S(2)}, u32[]{:S(2)}) collective-permute-start(bf16[208,192]{1,0:T(8,128)(2,1)S(1)} %get-tuple-element.98), channel_id=1, source_target_pairs={{0,2},{1,3},{2,0},{3,1},{4,6},{5,7},{6,4},{7,5},{8,10},{9,11},{10,... | collective-permute-start | bytes 239624 | tf_op jit(solution)/shard_map/ppermute | solution.py:442
  71.9 9.2 %collective-permute-start.30 = (bf16[208,192]{1,0:T(8,128)(2,1)S(1)}, bf16[208,192]{1,0:T(8,128)(2,1)S(1)}, u32[]{:S(2)}, u32[]{:S(2)}) collective-permute-start(bf16[208,192]{1,0:T(8,128)(2,1)S(1)} %get-tuple-element.99), channel_id=1, source_target_pairs={{0,3},{1,2},{2,1},{3,0},{4,7},{5,6},{6,5},{7,4},{8,11},{9,10},{10,... | collective-permute-start | bytes 239624 | tf_op jit(solution)/shard_map/ppermute | solution.py:442
  83.7 36.6 %collective-permute-start.38 = (bf16[4,96,576]{2,1,0:T(8,128)(2,1)S(1)}, bf16[4,96,576]{2,1,0:T(8,128)(2,1)S(1)}, u32[]{:S(2)}, u32[]{:S(2)}) collective-permute-start(bf16[4,96,576]{2,1,0:T(8,128)(2,1)S(1)} %get-tuple-element.116), channel_id=1, source_target_pairs={{0,4},{4,0},{1,5},{5,1},{2,6},{6,2},{3,7},{7,3},{8,12},{12,8},{9,1... | collective-permute-start | bytes 1327112 | tf_op jit(solution)/shard_map/ppermute | solution.py:439
  84.4 5.5 %collective-permute-start.21 = (bf16[56,768]{1,0:T(8,128)(2,1)S(1)}, bf16[56,768]{1,0:T(8,128)(2,1)S(1)}, u32[]{:S(2)}, u32[]{:S(2)}) collective-permute-start(bf16[56,768]{1,0:T(8,128)(2,1)S(1)} %get-tuple-element.91), channel_id=1, source_target_pairs={{0,1},{1,0},{2,3},{3,2},{4,5},{5,4},{6,7},{7,6},{8,9},{9,8},{10,11... | collective-permute-start | bytes 258056 | tf_op jit(solution)/shard_map/ppermute | solution.py:442
  86.7 9.8 %collective-permute-start.22 = (bf16[56,768]{1,0:T(8,128)(2,1)S(1)}, bf16[56,768]{1,0:T(8,128)(2,1)S(1)}, u32[]{:S(2)}, u32[]{:S(2)}) collective-permute-start(bf16[56,768]{1,0:T(8,128)(2,1)S(1)} %get-tuple-element.92), channel_id=1, source_target_pairs={{0,2},{1,3},{2,0},{3,1},{4,6},{5,7},{6,4},{7,5},{8,10},{9,11},{10,... | collective-permute-start | bytes 258056 | tf_op jit(solution)/shard_map/ppermute | solution.py:442
  86.9 9.6 %collective-permute-start.23 = (bf16[56,768]{1,0:T(8,128)(2,1)S(1)}, bf16[56,768]{1,0:T(8,128)(2,1)S(1)}, u32[]{:S(2)}, u32[]{:S(2)}) collective-permute-start(bf16[56,768]{1,0:T(8,128)(2,1)S(1)} %get-tuple-element.93), channel_id=1, source_target_pairs={{0,3},{1,2},{2,1},{3,0},{4,7},{5,6},{6,5},{7,4},{8,11},{9,10},{10,... | collective-permute-start | bytes 258056 | tf_op jit(solution)/shard_map/ppermute | solution.py:442
  96.5 7.2 %collective-permute-start.26 = (bf16[56,768]{1,0:T(8,128)(2,1)S(1)}, bf16[56,768]{1,0:T(8,128)(2,1)S(1)}, u32[]{:S(2)}, u32[]{:S(2)}) collective-permute-start(bf16[56,768]{1,0:T(8,128)(2,1)S(1)} %out_sum.1.own), channel_id=1, source_target_pairs={{0,3},{1,2},{2,1},{3,0},{4,7},{5,6},{6,5},{7,4},{8,11},{9,10},{10,... | collective-permute-start | bytes 258056 | tf_op jit(solution)/shard_map/ppermute | solution.py:442
  98.4 9.1 %collective-permute-start.25 = (bf16[56,768]{1,0:T(8,128)(2,1)S(1)}, bf16[56,768]{1,0:T(8,128)(2,1)S(1)}, u32[]{:S(2)}, u32[]{:S(2)}) collective-permute-start(bf16[56,768]{1,0:T(8,128)(2,1)S(1)} %out_sum.1.own), channel_id=1, source_target_pairs={{0,2},{1,3},{2,0},{3,1},{4,6},{5,7},{6,4},{7,5},{8,10},{9,11},{10,... | collective-permute-start | bytes 258056 | tf_op jit(solution)/shard_map/ppermute | solution.py:442
  99.9 7.5 %collective-permute-start.24 = (bf16[56,768]{1,0:T(8,128)(2,1)S(1)}, bf16[56,768]{1,0:T(8,128)(2,1)S(1)}, u32[]{:S(2)}, u32[]{:S(2)}) collective-permute-start(bf16[56,768]{1,0:T(8,128)(2,1)S(1)} %out_sum.1.own), channel_id=1, source_target_pairs={{0,1},{1,0},{2,3},{3,2},{4,5},{5,4},{6,7},{7,6},{8,9},{9,8},{10,11... | collective-permute-start | bytes 258056 | tf_op jit(solution)/shard_map/ppermute | solution.py:442
  103.8 5.8 %collective-permute-start.31 = (bf16[64,768]{1,0:T(8,128)(2,1)S(1)}, bf16[64,768]{1,0:T(8,128)(2,1)S(1)}, u32[]{:S(2)}, u32[]{:S(2)}) collective-permute-start(bf16[64,768]{1,0:T(8,128)(2,1)S(1)} %get-tuple-element.107), channel_id=1, source_target_pairs={{0,1},{1,0},{2,3},{3,2},{4,5},{5,4},{6,7},{7,6},{8,9},{9,8},{10,11... | collective-permute-start | bytes 294920 | tf_op jit(solution)/shard_map/ppermute | solution.py:442
  107.5 8.9 %collective-permute-start.32 = (bf16[64,768]{1,0:T(8,128)(2,1)S(1)}, bf16[64,768]{1,0:T(8,128)(2,1)S(1)}, u32[]{:S(2)}, u32[]{:S(2)}) collective-permute-start(bf16[64,768]{1,0:T(8,128)(2,1)S(1)} %get-tuple-element.108), channel_id=1, source_target_pairs={{0,2},{1,3},{2,0},{3,1},{4,6},{5,7},{6,4},{7,5},{8,10},{9,11},{10,... | collective-permute-start | bytes 294920 | tf_op jit(solution)/shard_map/ppermute | solution.py:442
  107.5 8.9 %collective-permute-start.33 = (bf16[64,768]{1,0:T(8,128)(2,1)S(1)}, bf16[64,768]{1,0:T(8,128)(2,1)S(1)}, u32[]{:S(2)}, u32[]{:S(2)}) collective-permute-start(bf16[64,768]{1,0:T(8,128)(2,1)S(1)} %get-tuple-element.109), channel_id=1, source_target_pairs={{0,3},{1,2},{2,1},{3,0},{4,7},{5,6},{6,5},{7,4},{8,11},{9,10},{10,... | collective-permute-start | bytes 294920 | tf_op jit(solution)/shard_map/ppermute | solution.py:442
  109.5 20.3 %collective-permute-start.27 = (bf16[98,768]{1,0:T(8,128)(2,1)S(1)}, bf16[98,768]{1,0:T(8,128)(2,1)S(1)}, u32[]{:S(2)}, u32[]{:S(2)}) collective-permute-start(bf16[98,768]{1,0:T(8,128)(2,1)S(1)} %get-tuple-element.95), channel_id=1, source_target_pairs={{0,4},{4,0},{1,5},{5,1},{2,6},{6,2},{3,7},{7,3},{8,12},{12,8},{9,1... | collective-permute-start | bytes 451592 | tf_op jit(solution)/shard_map/ppermute | solution.py:439
  116.5 7.2 %collective-permute-start.36 = (bf16[56,768]{1,0:T(8,128)(2,1)S(1)}, bf16[56,768]{1,0:T(8,128)(2,1)S(1)}, u32[]{:S(2)}, u32[]{:S(2)}) collective-permute-start(bf16[56,768]{1,0:T(8,128)(2,1)S(1)} %get-tuple-element.110.own), channel_id=1, source_target_pairs={{0,3},{1,2},{2,1},{3,0},{4,7},{5,6},{6,5},{7,4},{8,11},{9,10},{10,... | collective-permute-start | bytes 258056 | tf_op jit(solution)/shard_map/ppermute | solution.py:442
  119.0 8.6 %collective-permute-start.35 = (bf16[56,768]{1,0:T(8,128)(2,1)S(1)}, bf16[56,768]{1,0:T(8,128)(2,1)S(1)}, u32[]{:S(2)}, u32[]{:S(2)}) collective-permute-start(bf16[56,768]{1,0:T(8,128)(2,1)S(1)} %get-tuple-element.110.own), channel_id=1, source_target_pairs={{0,2},{1,3},{2,0},{3,1},{4,6},{5,7},{6,4},{7,5},{8,10},{9,11},{10,... | collective-permute-start | bytes 258056 | tf_op jit(solution)/shard_map/ppermute | solution.py:442
  120.3 8.9 %collective-permute-start.34 = (bf16[56,768]{1,0:T(8,128)(2,1)S(1)}, bf16[56,768]{1,0:T(8,128)(2,1)S(1)}, u32[]{:S(2)}, u32[]{:S(2)}) collective-permute-start(bf16[56,768]{1,0:T(8,128)(2,1)S(1)} %get-tuple-element.110.own), channel_id=1, source_target_pairs={{0,1},{1,0},{2,3},{3,2},{4,5},{5,4},{6,7},{7,6},{8,9},{9,8},{10,11... | collective-permute-start | bytes 258056 | tf_op jit(solution)/shard_map/ppermute | solution.py:442
  121.8 0.7 copy-start.7
  123.7 9.8 %collective-permute-start.39 = (bf16[112,576]{1,0:T(8,128)(2,1)}, bf16[112,576]{1,0:T(8,128)(2,1)S(1)}, u32[]{:S(2)}, u32[]{:S(2)}) collective-permute-start(bf16[112,576]{1,0:T(8,128)(2,1)} %get-tuple-element.120), channel_id=1, source_target_pairs={{0,8},{8,0},{16,24},{24,16},{1,9},{9,1},{17,25},{25,17},{2,10},{10... | collective-permute-start | bytes 387080 | tf_op jit(solution)/shard_map/ppermute | solution.py:445
  125.2 8.3 %collective-permute-start.40 = (bf16[112,576]{1,0:T(8,128)(2,1)}, bf16[112,576]{1,0:T(8,128)(2,1)S(1)}, u32[]{:S(2)}, u32[]{:S(2)}) collective-permute-start(bf16[112,576]{1,0:T(8,128)(2,1)} %get-tuple-element.121), channel_id=1, source_target_pairs={{0,16},{8,24},{16,0},{24,8},{1,17},{9,25},{17,1},{25,9},{2,18},{10... | collective-permute-start | bytes 387080 | tf_op jit(solution)/shard_map/ppermute | solution.py:445
  127.6 25.8 %collective-permute-start.44 = (bf16[96,2304]{1,0:T(8,128)(2,1)}, bf16[96,2304]{1,0:T(8,128)(2,1)S(1)}, u32[]{:S(2)}, u32[]{:S(2)}) collective-permute-start(bf16[96,2304]{1,0:T(8,128)(2,1)} %get-tuple-element.134), channel_id=1, source_target_pairs={{0,8},{8,0},{16,24},{24,16},{1,9},{9,1},{17,25},{25,17},{2,10},{10... | collective-permute-start | bytes 1327112 | tf_op jit(solution)/shard_map/ppermute | solution.py:445
  129.2 0.6 copy-start.4
  129.8 24.3 %collective-permute-start.45 = (bf16[96,2304]{1,0:T(8,128)(2,1)}, bf16[96,2304]{1,0:T(8,128)(2,1)S(1)}, u32[]{:S(2)}, u32[]{:S(2)}) collective-permute-start(bf16[96,2304]{1,0:T(8,128)(2,1)} %get-tuple-element.135), channel_id=1, source_target_pairs={{0,16},{8,24},{16,0},{24,8},{1,17},{9,25},{17,1},{25,9},{2,18},{10... | collective-permute-start | bytes 1327112 | tf_op jit(solution)/shard_map/ppermute | solution.py:445
  129.8 0.7 copy-start.8
  130.5 23.6 %collective-permute-start.46 = (bf16[96,2304]{1,0:T(8,128)(2,1)}, bf16[96,2304]{1,0:T(8,128)(2,1)S(1)}, u32[]{:S(2)}, u32[]{:S(2)}) collective-permute-start(bf16[96,2304]{1,0:T(8,128)(2,1)} %get-tuple-element.136), channel_id=1, source_target_pairs={{0,24},{8,16},{16,8},{24,0},{1,25},{9,17},{17,9},{25,1},{2,26},{10... | collective-permute-start | bytes 1327112 | tf_op jit(solution)/shard_map/ppermute | solution.py:445
  132.4 0.9 copy-start.5
  133.4 25.5 %collective-permute-start.37 = (bf16[98,768]{1,0:T(8,128)(2,1)S(1)}, bf16[98,768]{1,0:T(8,128)(2,1)S(1)}, u32[]{:S(2)}, u32[]{:S(2)}) collective-permute-start(bf16[98,768]{1,0:T(8,128)(2,1)S(1)} %get-tuple-element.112), channel_id=1, source_target_pairs={{0,4},{4,0},{1,5},{5,1},{2,6},{6,2},{3,7},{7,3},{8,12},{12,8},{9,1... | collective-permute-start | bytes 451592 | tf_op jit(solution)/shard_map/ppermute | solution.py:439
  133.5 19.8 %collective-permute-start.41 = (bf16[112,576]{1,0:T(8,128)(2,1)}, bf16[112,576]{1,0:T(8,128)(2,1)S(1)}, u32[]{:S(2)}, u32[]{:S(2)}) collective-permute-start(bf16[112,576]{1,0:T(8,128)(2,1)} %copy-done.7), channel_id=1, source_target_pairs={{0,24},{8,16},{16,8},{24,0},{1,25},{9,17},{17,9},{25,1},{2,26},{10... | collective-permute-start | bytes 387080 | tf_op jit(solution)/shard_map/ppermute | solution.py:445
  153.3 11.0 %collective-permute-start.42 = (bf16[112,576]{1,0:T(8,128)(2,1)S(1)}, bf16[112,576]{1,0:T(8,128)(2,1)S(1)}, u32[]{:S(2)}, u32[]{:S(2)}) collective-permute-start(bf16[112,576]{1,0:T(8,128)(2,1)S(1)} %get-tuple-element.124), channel_id=1, source_target_pairs={{0,4},{4,0},{1,5},{5,1},{2,6},{6,2},{3,7},{7,3},{8,12},{12,8},{9,1... | collective-permute-start | bytes 387080 | tf_op jit(solution)/shard_map/ppermute | solution.py:439
  154.4 4.5 %collective-permute-start.47 = (bf16[96,192]{1,0:T(8,128)(2,1)S(1)}, bf16[96,192]{1,0:T(8,128)(2,1)S(1)}, u32[]{:S(2)}, u32[]{:S(2)}) collective-permute-start(bf16[96,192]{1,0:T(8,128)(2,1)S(1)} %get-tuple-element.139), channel_id=1, source_target_pairs={{0,1},{1,0},{2,3},{3,2},{4,5},{5,4},{6,7},{7,6},{8,9},{9,8},{10,11... | collective-permute-start | bytes 110600 | tf_op jit(solution)/shard_map/ppermute | solution.py:442
  156.1 6.9 %collective-permute-start.48 = (bf16[96,192]{1,0:T(8,128)(2,1)S(1)}, bf16[96,192]{1,0:T(8,128)(2,1)S(1)}, u32[]{:S(2)}, u32[]{:S(2)}) collective-permute-start(bf16[96,192]{1,0:T(8,128)(2,1)S(1)} %get-tuple-element.140), channel_id=1, source_target_pairs={{0,2},{1,3},{2,0},{3,1},{4,6},{5,7},{6,4},{7,5},{8,10},{9,11},{10,... | collective-permute-start | bytes 110600 | tf_op jit(solution)/shard_map/ppermute | solution.py:442
  156.1 6.9 %collective-permute-start.49 = (bf16[96,192]{1,0:T(8,128)(2,1)S(1)}, bf16[96,192]{1,0:T(8,128)(2,1)S(1)}, u32[]{:S(2)}, u32[]{:S(2)}) collective-permute-start(bf16[96,192]{1,0:T(8,128)(2,1)S(1)} %get-tuple-element.141), channel_id=1, source_target_pairs={{0,3},{1,2},{2,1},{3,0},{4,7},{5,6},{6,5},{7,4},{8,11},{9,10},{10,... | collective-permute-start | bytes 110600 | tf_op jit(solution)/shard_map/ppermute | solution.py:442
  163.1 3.4 %collective-permute-start.50 = (bf16[96,1728]{1,0:T(8,128)(2,1)S(1)}, bf16[96,1728]{1,0:T(8,128)(2,1)S(1)}, u32[]{:S(2)}, u32[]{:S(2)}) collective-permute-start(bf16[96,1728]{1,0:T(8,128)(2,1)S(1)} %get-tuple-element.143), channel_id=1, source_target_pairs={{0,4},{4,0},{1,5},{5,1},{2,6},{6,2},{3,7},{7,3},{8,12},{12,8},{9,1... | collective-permute-start | bytes 995336 | tf_op jit(solution)/shard_map/ppermute | solution.py:439

commit v3 on v2

v3 whole, which is shorter than its diff:
```python
import functools

import jax
import jax.numpy as jnp
from jax import lax
from jax.experimental import pallas as pl
from jax.experimental.pallas import tpu as pltpu
from jax.sharding import PartitionSpec as P

HD = 64
EPSILON = 1e-06
QUERY_SCALE = 0.125
F32 = jnp.float32
LOW = jnp.bfloat16
NN = ((1,), (0,))
NT = ((1,), (1,))
TN = ((0,), (0,))
VMEM = pl.BlockSpec(memory_space=pltpu.VMEM)
ANY = pl.BlockSpec(memory_space=pl.ANY)
EXTRA = 16
UP_AT, QV_AT = 256, 384


def dot(left, right, dims):
    return lax.dot_general(left, right, (dims, ((), ())), preferred_element_type=F32)


def shape(dims, kind):
    return jax.ShapeDtypeStruct(tuple(dims), kind)


def call(kernel, outs, args, scratch=(), name=None, mib=20, in_specs=None, alias=None):
    return pl.pallas_call(
        kernel,
        out_shape=tuple(outs),
        in_specs=in_specs or [VMEM] * len(args),
        out_specs=tuple([VMEM] * len(outs)),
        scratch_shapes=list(scratch),
        input_output_aliases=alias or {},
        name=name,
        compiler_params=pltpu.CompilerParams(vmem_limit_bytes=mib << 20),
    )(*args)


def gelu_and_slope(v):
    cdf = 0.5 * (1.0 + lax.erf(v * 0.7071067811865476))
    density = jnp.exp(-0.5 * v * v) * 0.3989422804014327
    return v * cdf, cdf + v * density


def mean(v):
    return jnp.mean(v, axis=-1, keepdims=True)


def total_rows(v):
    return jnp.sum(v, axis=0, keepdims=True)


def normalise(v):
    centred = v - mean(v)
    inverse = lax.rsqrt(mean(centred * centred) + EPSILON)
    return centred * inverse, inverse


def norm_backward(grad_normed, normal, inverse, gain):
    scaled = grad_normed * gain
    return inverse * (scaled - mean(scaled) - normal * mean(scaled * normal))


def lanes(parts):
    return jnp.concatenate(parts, axis=1)


def rows_of(parts):
    return jnp.concatenate(parts, axis=0)


def read(ref):
    return ref[...].astype(F32)


class Sizes:
    def __init__(self, nf, nt, inputs, qv_bias, fc1_weight):
        self.nf, self.nt = nf, nt
        _, self.half, self.width = inputs.shape
        self.shard = self.width // nf
        self.heads = qv_bias.shape[1]
        self.inner = self.heads * HD
        self.ff = fc1_weight.shape[1]
        self.pad = -self.half % 8
        self.padded = self.half + self.pad
        self.rows = 2 * self.padded
        self.block = -(-(self.rows // nt) // 8) * 8
        self.part = self.width // 4
        self.chunk = self.part // 2
        self.direct = nf == 4
        self.cols = 2 * self.ff + nt * self.inner
        self.dense = self.rows * self.inner // 128

    def start(self, j):
        return pl.multiple_of(j * (self.rows // self.nt) // 8 * 8, 8)

    def base(self):
        return lax.axis_index("fsdp") if self.direct else 0

    def half_of(self, c):
        return pl.ds(pl.multiple_of(c * self.chunk, 16), self.chunk)

    def squeeze(self, v):
        return rows_of([v[:, :128], lanes([v[: self.padded, 128:], v[self.padded :, 128:]])])

    def spread(self, v):
        tail = v[self.rows :]
        return lanes([v[: self.rows], rows_of([tail[:, :HD], tail[:, HD:]])])


def pack_kernel(z, *refs):
    sources, (near, far, proj_half, feed, feed_half), copies, sem = refs[:12], refs[12:17], refs[17:29], refs[29]
    moves = [pltpu.make_async_copy(s, d, sem.at[i]) for i, (s, d) in enumerate(zip(sources, copies))]
    for m in moves:
        m.start()
    for m in moves:
        m.wait()
    qkv, proj, up_b, qv_b = copies[:4]
    vectors = copies[4:10]
    c = lax.axis_index("ctx")
    whole = lanes([read(qkv.at[i]) for i in range(3)])
    near[: z.part, :] = whole.astype(LOW)
    far[: z.chunk, :] = jnp.where(c == 0, whole[: z.chunk], whole[z.chunk :]).astype(LOW)
    row = lax.broadcasted_iota(jnp.int32, (EXTRA, z.shard), 0)
    vec = jnp.zeros((EXTRA, z.shard), F32)
    for i, v in enumerate(vectors):
        vec = jnp.where(row == i, read(v).reshape(1, z.shard), vec)
    biases = read(qv_b)
    biases = rows_of([biases[h, i : i + 1] for h in range(z.heads) for i in range(2)])
    for out, at in ((near, z.part), (far, z.chunk)):
        out[at:, :] = jnp.zeros((EXTRA, 3 * z.inner), LOW)
        out[at:, : z.shard] = vec.astype(LOW)
        out[at : at + up_b.shape[0], UP_AT : UP_AT + up_b.shape[1]] = up_b[...]
        out[at : at + 2 * z.heads, QV_AT : QV_AT + biases.shape[1]] = biases.astype(LOW)
    feed[:, : z.ff] = copies[10][...]
    feed[:, z.ff :] = copies[11][...]
    feed_half[...] = feed[z.half_of(c), :]
    turned = read(proj).T
    proj_half[...] = jnp.where(c == 0, turned[: z.chunk], turned[z.chunk :]).astype(LOW)


def pair_kernel(first, second, out):
    out[0] = first[...]
    out[1] = second[...]


def pack_proj_kernel(own, two, pair, out):
    out[...] = lanes([read(own), pair[0].astype(F32), read(two), pair[1].astype(F32)]).astype(LOW)


def pack_near_kernel(z, mine, theirs, out):
    c = lax.axis_index("ctx")
    out[z.half_of(c), :] = mine[...]
    out[z.half_of(1 - c), :] = theirs[...]


def own_frame(z, keep, received):
    c = lax.axis_index("ctx")
    zero = jnp.zeros((z.pad, z.width), F32)
    pieces = []
    for ref in (keep, received):
        pieces.append(jnp.where(c == 0, ref[:, 0, :].astype(F32), ref[:, 1, :].astype(F32)))
        pieces.append(zero)
    return rows_of(pieces)


def frame_kernel(z, keep, received, stream, normal, inverse):
    values = own_frame(z, keep, received)
    stream[...] = values.astype(LOW)
    n, i = normalise(values)
    normal[...] = n
    inverse[...] = jnp.broadcast_to(i, inverse.shape)


def cot_kernel(z, keep, received, stream):
    stream[...] = own_frame(z, keep, received).astype(LOW)


def attend_kernel(z, *refs):
    refs = list(refs)
    if z.direct:
        own, near, near_their, far, far_their = refs[:5]
        refs = refs[5:]
    else:
        whole, vec_in, up_in, qv_in = refs[:4]
        refs = refs[4:]
    normal, small, w_out, normed_out, act, attended, soft_out = refs[:7]
    if z.direct:
        c, b = lax.axis_index("ctx"), lax.axis_index("fsdp")
        gather = refs[7]
        for ref, at in ((own, b), (near, b ^ (1 + c)), (near_their, b ^ (2 - c))):
            w_out[at] = ref[: z.part, :]
            gather[at] = ref[z.part :, :].astype(F32)
        w_out[b ^ 3, z.half_of(c), :] = far[: z.chunk, :]
        w_out[b ^ 3, z.half_of(1 - c), :] = far_their[: z.chunk, :]
        gather[b ^ 3] = far[z.chunk :, :].astype(F32)
        blocks = [gather[i] for i in range(4)]
        w = HD // 4
        vec = lanes([g[:8, : z.shard] for g in blocks])
        up = lanes([g[: z.ff // HD, UP_AT : UP_AT + w] for g in blocks])
        qv = lanes([g[: 2 * z.heads, QV_AT : QV_AT + w] for g in blocks])
    else:
        w_out[...] = whole[...]
        vec, up, qv = vec_in[...], up_in[...], qv_in[...]
    up_row = lanes([up[i : i + 1] for i in range(z.ff // HD)])
    query_b = lanes([qv[2 * h : 2 * h + 1] for h in range(z.heads)])
    value_b = lanes([qv[2 * h + 1 : 2 * h + 2] for h in range(z.heads)])
    small[...] = vec
    small[6:7, : z.ff] = up_row
    normed = (normal[...] * vec[0:1] + vec[1:2]).astype(LOW)
    normed_out[...] = normed
    projected = dot(normed, w_out[...].reshape(z.width, 3 * z.inner), NN)
    n = z.inner
    query = ((projected[:, :n] + query_b) * QUERY_SCALE).astype(LOW)
    key = projected[:, n : 2 * n].astype(LOW)
    value = (projected[:, 2 * n :] + value_b).astype(LOW)
    act[0] = query
    act[1] = key
    act[2] = value
    place = lax.broadcasted_iota(jnp.int32, (z.rows, z.rows), 1)
    valid = (place < z.half) | ((place >= z.padded) & (place < z.padded + z.half))
    done = []
    for h in range(z.heads):
        cut = slice(h * HD, (h + 1) * HD)
        scores = jnp.where(valid, dot(query[:, cut], key[:, cut], NT), -1e30)
        exponent = jnp.exp(scores - jnp.max(scores, axis=-1, keepdims=True))
        soft = exponent * (1.0 / jnp.sum(exponent, axis=-1, keepdims=True))
        soft_out[h] = soft
        done.append(dot(soft.astype(LOW), value[:, cut], NN))
    attended[...] = z.squeeze(lanes(done)).astype(LOW)


def feed_kernel(z, *refs):
    refs = list(refs)
    if z.direct:
        own, one, one_their, two, two_their, near, near_in, near_their, far, far_their = refs[:10]
        refs = refs[10:]
    else:
        whole = refs[0]
        refs = refs[1:]
    att = refs[:3]
    stream, cot, small = refs[3:6]
    (w_out, att_out, middle_out, hidden_out, normed_out, pre_out, part_out, low_out, own_att, small_out) = refs[6:16]
    sends = refs[16:]
    if z.direct:
        c, b = lax.axis_index("ctx"), lax.axis_index("fsdp")
        mine, other = z.half_of(c), z.half_of(1 - c)
        first, last = pl.ds(0, 2 * z.ff), pl.ds(2 * z.ff, z.nt * z.inner)
        w_out[b, :, first] = own[...]
        w_out[b ^ (1 + c), mine, first] = one[...]
        w_out[b ^ (2 - c), other, first] = one_their[...]
        w_out[b ^ (2 - c), mine, first] = two[0]
        w_out[b ^ (1 + c), other, first] = two_their[0]
        w_out[b ^ 3, mine, first] = two[1]
        w_out[b ^ 3, other, first] = two_their[1]
        w_out[b, :, last] = near[...]
        w_out[b ^ (1 + c), :, last] = near_in[...]
        w_out[b ^ (2 - c), :, last] = near_their[...]
        w_out[b ^ 3, mine, last] = far[...]
        w_out[b ^ 3, other, last] = far_their[...]
    else:
        w_out[...] = whole[...]
    n = z.inner
    w_up = w_out[:, :, : z.ff].reshape(z.width, z.ff)
    w_down_t = w_out[:, :, z.ff : 2 * z.ff].reshape(z.width, z.ff)
    w_proj_t = w_out[:, :, 2 * z.ff :].reshape(z.width, z.nt * n)
    grad_out_low = cot[...]
    grad_out = grad_out_low.astype(F32)
    pieces = [read(att[0]), att[2][0].astype(F32), read(att[1]), att[2][1].astype(F32)]
    attended = lanes([z.spread(p) for p in pieces]).astype(LOW)
    att_out[...] = attended
    branch = dot(attended, w_proj_t, NT)
    middle = stream[...].astype(F32) + branch + small[2:3]
    middle_out[...] = middle
    normal, inverse = normalise(middle)
    gain = small[3:4]
    normed = (normal * gain + small[4:5]).astype(LOW)
    normed_out[...] = normed
    hidden, slope = gelu_and_slope(dot(normed, w_up, NN) + small[6:7, : z.ff])
    hidden_out[...] = hidden.astype(LOW)
    grad_pre = (dot(grad_out_low, w_down_t, NN) * slope).astype(LOW)
    pre_out[...] = grad_pre
    grad_normed = dot(grad_pre, w_up, NT)
    part = grad_out * (1.0 / z.nt) + norm_backward(grad_normed, normal, inverse, gain)
    part_out[...] = part
    low = part.astype(LOW)
    low_out[...] = low
    grad_att = dot(low, w_proj_t, NN)
    own_att[...] = grad_att[:, :n]
    for k in range(1, z.nt):
        sends[k - 1][...] = z.squeeze(grad_att[:, k * n : (k + 1) * n]).astype(LOW)
    small_out[...] = jnp.zeros(small_out.shape, F32)
    small_out[2:3] = total_rows(part)
    small_out[3:4] = total_rows(grad_normed * normal)
    small_out[4:5] = total_rows(grad_normed)
    small_out[5:6] = total_rows(grad_out) * (1.0 / z.nt)
    small_out[6:7, : z.ff] = total_rows(grad_pre.astype(F32))


def down_kernel(z, hidden, w, middle, small, own, sent, scratch):
    t = lax.axis_index("tp")
    w_down_t = w[:, :, z.ff : 2 * z.ff].reshape(z.width, z.ff)
    scratch[...] = dot(hidden[...], w_down_t, NT)
    mine = pl.ds(z.start(t), z.block)
    own[0] = scratch[mine, :] + middle[mine, :] + small[5:6]
    own[1] = scratch[pl.ds(z.start(t ^ 2), z.block), :]
    sent[0] = scratch[pl.ds(z.start(t ^ 1), z.block), :].astype(LOW)
    sent[1] = scratch[pl.ds(z.start(t ^ 3), z.block), :].astype(LOW)


def down_pair_kernel(own, received, kept, sent):
    kept[...] = own[0] + received[0].astype(F32)
    sent[...] = (own[1] + received[1].astype(F32)).astype(LOW)


def down_last_kernel(kept, received, out):
    out[...] = (kept[...] + read(received)).astype(LOW)


def store_halves(z, value, at, keep, sent):
    cols = pl.ds(at, value.shape[1])
    c = lax.axis_index("ctx") if z.direct else 0
    b = lax.axis_index("fsdp") if z.direct else 0
    for j in range(4):
        first = value[j * z.part : j * z.part + z.chunk]
        second = value[j * z.part + z.chunk : (j + 1) * z.part]
        if z.direct:
            keep[j ^ b, :, cols] = jnp.where(c == 0, first, second)
            sent[j ^ b, :, cols] = jnp.where(c == 0, second, first).astype(LOW)
        else:
            keep[j, :, cols] = first
            sent[j, :, cols] = second.astype(LOW)


def rest_grad_kernel(z, normed, pre, cot, hidden, low, att, keep, sent):
    store_halves(z, dot(normed[...], pre[...], TN), 0, keep, sent)
    store_halves(z, dot(cot[...], hidden[...], TN), z.ff, keep, sent)
    store_halves(z, dot(low[...], att[...], TN), 2 * z.ff, keep, sent)


def split_sum(z, keep, received, out, kept, cols):
    c = lax.axis_index("ctx")
    rows = pl.ds(0, z.chunk)
    for target, at, kind in ((out, (1 + c, 3), LOW), (kept, (0, 2 - c), F32)):
        for i in range(2):
            total = keep[at[i], :, cols] + received[at[i], :, cols].astype(F32)
            target[i, rows, :] = total.astype(kind)


def rest_one_kernel(z, keep, received, proj, proj_kept, feed, feed_kept):
    split_sum(z, keep, received, proj, proj_kept, pl.ds(2 * z.ff, z.nt * z.inner))
    split_sum(z, keep, received, feed, feed_kept, pl.ds(0, 2 * z.ff))


def second_kernel(kept, received, own, sent):
    own[...] = kept[0] + received[0].astype(F32)
    sent[...] = (kept[1] + received[1].astype(F32)).astype(LOW)


def third_kernel(own, received, total, sent):
    value = own[...] + read(received)
    total[...] = value
    sent[...] = value.astype(LOW)


def by_half(mine, other):
    c = lax.axis_index("ctx")
    return rows_of([jnp.where(c == 0, mine, other), jnp.where(c == 0, other, mine)])


def feed_final_kernel(z, own, theirs, up, down):
    total = by_half(own[...], read(theirs))
    up[...] = total[:, : z.ff]
    down[...] = total[:, z.ff :]


def unfold(z, v):
    return rows_of([v[:, i * z.inner : (i + 1) * z.inner] for i in range(4)])


def fold(v):
    n = v.shape[0] // 4
    return lanes([v[i * n : (i + 1) * n] for i in range(4)])


def proj_final_kernel(z, own, theirs, proj):
    other = theirs[z.padded :, :].astype(F32)
    proj[...] = by_half(unfold(z, own[...]), unfold(z, other)).T


def back_kernel(z, *refs):
    own_att, got = refs[0], refs[1 : z.nt]
    act, soft, w, normal, inverse, part, small, small_in = refs[z.nt : z.nt + 8]
    grads_out, qv_out, own, sent, scratch = refs[z.nt + 8 :]
    t = lax.axis_index("tp")
    grad_att = (own_att[...] + z.spread(sum(read(g) for g in got))).astype(LOW)
    parts = [[], [], []]
    query, key, value = act[0], act[1], act[2]
    for h in range(z.heads):
        cut = slice(h * HD, (h + 1) * HD)
        ga = grad_att[:, cut]
        p = soft[h]
        grad_soft = dot(ga, value[:, cut], NT)
        delta = jnp.sum(p * grad_soft, axis=-1, keepdims=True)
        grad_scores = (p * (grad_soft - delta)).astype(LOW)
        parts[0].append((dot(grad_scores, key[:, cut], NN).astype(LOW).astype(F32) * QUERY_SCALE).astype(LOW))
        parts[1].append(dot(grad_scores, query[:, cut], TN).astype(LOW))
        parts[2].append(dot(p.astype(LOW), ga, TN).astype(LOW))
    grads = lanes(parts[0] + parts[1] + parts[2])
    grads_out[...] = grads
    n = z.inner
    qv_out[...] = total_rows(grads.astype(F32))
    grad_normed = dot(grads, w[...].reshape(z.width, 3 * n), NT)
    scratch[...] = part[...] + norm_backward(grad_normed, normal[...], inverse[:, :1], small[0:1])
    row = lax.broadcasted_iota(jnp.int32, (8, z.width), 0)
    vec = small_in[...]
    vec = jnp.where(row == 0, total_rows(grad_normed * normal[...]), vec)
    vec = jnp.where(row == 1, total_rows(grad_normed), vec)
    for i, k in enumerate((0, 2)):
        own[i] = rows_of([scratch[pl.ds(z.start(t ^ k), z.block), :], vec])
        sent[i] = rows_of([scratch[pl.ds(z.start(t ^ k ^ 1), z.block), :], vec]).astype(LOW)


def qkv_grad_kernel(z, normed, grads, keep, sent):
    store_halves(z, dot(normed[...], grads[...], TN), 0, keep, sent)


def sum_rows_kernel(z, kept, received, small, qv, *refs):
    if z.direct:
        proj, proj_in, out, vec, proj_keep = refs
    else:
        out, vec = refs
    total = kept[...] + read(received)
    out[: z.block, :] = total[: z.block].astype(LOW)
    vec[:8, :] = total[z.block :]
    vec[8:, :] = jnp.zeros((8, z.width), F32)
    vec[8:9, : z.ff] = small[6:7, : z.ff]
    vec[9:10, : 3 * z.inner] = qv[...]
    if z.direct:
        value = proj[...] + read(proj_in)
        parts = [fold(value[:, k * z.inner : (k + 1) * z.inner]) for k in range(4)]
        proj_keep[0] = parts[0]
        proj_keep[1] = parts[1]
        out[z.block :, :] = rows_of(parts[2:]).astype(LOW)


def rows_pair_kernel(z, own, received, *refs):
    if z.direct:
        proj_keep, out, proj_kept = refs
        n = z.chunk // 4
        arrived = received[z.block :, :].astype(F32)
        proj_kept[...] = proj_keep[0] + arrived[:n]
        tail = [(proj_keep[1] + arrived[n:])]
    else:
        (out,) = refs
        tail = []
    blocks = [own[: z.block, :].astype(F32), received[: z.block, :].astype(F32)]
    out[...] = rows_of(blocks + tail).astype(LOW)


def rows_kernel(z, pair, received, *refs):
    if len(refs) > 3:
        proj_kept, mine, theirs, proj_own, scratch = refs
        value = proj_kept[...] + received[2 * z.block :, :].astype(F32)
        proj_own[...] = value
        theirs[z.half : z.padded, :] = jnp.zeros((z.pad, z.width), LOW)
        theirs[z.padded :, :] = value.astype(LOW)
    else:
        mine, theirs, scratch = refs
    t = lax.axis_index("tp")
    for ref, flip in ((pair, 0), (received, 1)):
        for i, k in enumerate((0, 2)):
            piece = ref[i * z.block : (i + 1) * z.block, :].astype(F32)
            scratch[pl.ds(z.start(t ^ k ^ flip), z.block), :] = piece
    mine[...] = scratch[: z.half, :]
    theirs[: z.half, :] = scratch[z.padded : z.padded + z.half, :].astype(LOW)


def qkv_one_kernel(z, keep, received, vec, out, kept, scratch):
    b, c = lax.axis_index("fsdp"), lax.axis_index("ctx")
    vectors = vec[...]
    up = rows_of([vectors[8:9, i * HD : (i + 1) * HD] for i in range(z.ff // HD)])
    pieces = []
    for h in range(z.heads):
        pieces.append(vectors[9:10, h * HD : (h + 1) * HD])
        pieces.append(vectors[9:10, 2 * z.inner + h * HD : 2 * z.inner + (h + 1) * HD])
    qv_rows = rows_of(pieces)
    scratch[...] = jnp.zeros(scratch.shape, F32)
    w = HD // 4
    for i in range(4):
        scratch[i, :8, : z.shard] = vectors[:8, i * z.shard : (i + 1) * z.shard]
        scratch[i, : z.ff // HD, UP_AT : UP_AT + w] = up[:, i * w : (i + 1) * w]
        scratch[i, : 2 * z.heads, QV_AT : QV_AT + w] = qv_rows[:, i * w : (i + 1) * w]
    split_sum(z, keep, received, out, kept, pl.ds(0, 3 * z.inner))
    for i, at in enumerate((1 + c, 3)):
        out[i, z.chunk :, :] = scratch[b ^ at].astype(LOW)
    for i, at in enumerate((0, 2 - c)):
        kept[i, z.chunk :, :] = scratch[b ^ at]


def qkv_final_kernel(z, own, theirs, qkv, up, qv, *vectors):
    both = by_half(own[: z.chunk, :], theirs[: z.chunk, :].astype(F32))
    for i in range(3):
        qkv[i] = both[:, i * z.inner : (i + 1) * z.inner]
    tail = own[z.chunk :, :] + theirs[z.chunk :, :].astype(F32)
    w = HD // 4
    up[...] = tail[: z.ff // HD, UP_AT : UP_AT + w]
    for h in range(z.heads):
        qv[h] = tail[2 * h : 2 * h + 2, QV_AT : QV_AT + w]
    for i, v in enumerate(vectors):
        v[...] = tail[i : i + 1, : z.shard].reshape(z.shard)


def place_kernel(mine, theirs, out, *scratch):
    c = lax.axis_index("ctx")
    target = scratch[0] if scratch else out
    other = theirs[: out.shape[0], :].astype(F32)
    target[:, 0, :] = jnp.where(c == 0, mine[...], other)
    target[:, 1, :] = jnp.where(c == 0, other, mine[...])
    if scratch:
        out[...] = target[...].astype(out.dtype)


def build(nf, nc, nt):
    def local(
        inputs,
        norm1_gain,
        norm1_bias,
        qkv_weight,
        qv_bias,
        proj_weight,
        proj_bias,
        norm2_gain,
        norm2_bias,
        fc1_weight,
        fc1_bias,
        fc2_weight,
        fc2_bias,
        cotangent,
    ):
        z = Sizes(nf, nt, inputs, qv_bias, fc1_weight)
        part = functools.partial
        rows, width, inner, ff, chunk, block = z.rows, z.width, z.inner, z.ff, z.chunk, z.block
        f = lax.axis_index("fsdp")
        tie = lax.optimization_barrier

        def other_core(value):
            return lax.ppermute(value, "ctx", [(0, 1), (1, 0)])

        def to_tp(value, k):
            return lax.ppermute(value, "tp", [(i, i ^ k) for i in range(nt)])

        def to_far(value):
            return lax.ppermute(value, "fsdp", [(i, i ^ 3) for i in range(nf)])

        def neighbours(value, order):
            pairs = [(2 * i + c, 2 * (i ^ order[c]) + c) for i in range(nf) for c in range(2)]
            return lax.ppermute(value, ("fsdp", "ctx"), pairs)

        def to_near(value):
            return neighbours(value, (1, 2))

        def to_cross(value):
            return neighbours(value, (2, 1))

        def pair_of(first, second):
            return call(pair_kernel, [shape((2,) + first.shape, LOW)], [first, second], name="pair")[0]

        qkv3 = qkv_weight.transpose(1, 0, 2)
        down_t = fc2_weight.T
        qv3 = qv_bias.transpose(1, 0, 2)
        x_raw, cot_raw = inputs.transpose(1, 0, 2), cotangent.transpose(1, 0, 2)
        vectors = [norm1_gain, norm1_bias, proj_bias, norm2_gain, norm2_bias, fc2_bias]

        x_recv = other_core(x_raw)
        cot_recv = other_core(cot_raw)
        stream, normal_one, inverse_one = call(
            part(frame_kernel, z),
            [shape((rows, width), LOW), shape((rows, width), F32), shape((rows, 128), F32)],
            [x_raw, x_recv],
            name="frame",
        )
        (cot,) = call(part(cot_kernel, z), [shape((rows, width), LOW)], [cot_raw, cot_recv], name="cotangent")

        if z.direct:
            sources = [qkv3, proj_weight, fc1_bias, qv3] + vectors + [fc1_weight, down_t]
            near, far, proj_half, feed_own, feed_half = call(
                part(pack_kernel, z),
                [
                    shape((z.part + EXTRA, 3 * inner), LOW),
                    shape((chunk + EXTRA, 3 * inner), LOW),
                    shape((chunk, inner), LOW),
                    shape((z.part, 2 * ff), LOW),
                    shape((chunk, 2 * ff), LOW),
                ],
                sources,
                [pltpu.VMEM(s.shape, s.dtype) for s in sources] + [pltpu.SemaphoreType.DMA((len(sources),))],
                name="pack",
                mib=56,
                in_specs=[ANY] * len(sources),
            )
            got = [to_near(near), to_far(far)]
            proj_two = to_tp(proj_half, 2)
            feed_one = to_near(feed_half)
            got, stream, normal_one, inverse_one, cot = tie((got, stream, normal_one, inverse_one, cot))
            shared = [other_core(g) for g in got]
            qkv_in = [near, got[0], shared[0], got[1], shared[1]]
            proj_pair = to_tp(pair_of(proj_half, proj_two), 1)
            feed_two = to_cross(pair_of(feed_half, feed_one))
            (proj_far,) = call(
                pack_proj_kernel, [shape((chunk, nt * inner), LOW)], [proj_half, proj_two, proj_pair], name="pack_proj"
            )
            (proj_near,) = call(
                part(pack_near_kernel, z),
                [shape((z.part, nt * inner), LOW)],
                [proj_far, other_core(proj_far)],
                name="pack_near",
            )
            proj_got = [to_near(proj_near), to_far(proj_far)]
        else:
            whole = lax.all_gather(qkv3, "fsdp", axis=1, tiled=True)
            whole = whole.transpose(1, 0, 2).reshape(4, z.part, 3 * inner)
            vec = jnp.stack(vectors + [vectors[0]] * 2).astype(F32)
            qv_rows = qv3.reshape(2 * z.heads, -1).astype(F32)
            gathered = [lax.all_gather(v, "fsdp", axis=1, tiled=True) for v in (vec, fc1_bias.astype(F32), qv_rows)]
            qkv_in = [whole] + gathered
            proj_t = proj_weight.T
            rest = jnp.concatenate([fc1_weight, down_t, proj_t] + [to_tp(proj_t, k) for k in range(1, nt)], 1)
            rest_in = [lax.all_gather(rest, "fsdp", axis=0, tiled=True).reshape(4, z.part, z.cols)]

        small, w_qkv, normed_one, act, attended, soft = call(
            part(attend_kernel, z),
            [
                shape((8, width), F32),
                shape((4, z.part, 3 * inner), LOW),
                shape((rows, width), LOW),
                shape((3, rows, inner), LOW),
                shape((z.dense, 128), LOW),
                shape((z.heads, rows, rows), F32),
            ],
            qkv_in + [normal_one],
            [pltpu.VMEM((4, EXTRA, 3 * inner), F32)] if z.direct else [],
            name="attend",
        )
        att_two = to_tp(attended, 2)
        att_pair = to_tp(pair_of(attended, att_two), 1)
        if z.direct:
            att_pair, feed_two, proj_got = tie((att_pair, feed_two, proj_got))
            rest_in = [feed_own, feed_one, other_core(feed_one), feed_two, other_core(feed_two)]
            rest_in += [proj_near, proj_got[0], other_core(proj_got[0]), proj_got[1], other_core(proj_got[1])]

        (w_rest, att_all, middle, hidden, normed_two, grad_pre, part_middle, part_low, own_att, small_two, *att_sends) = (
            call(
                part(feed_kernel, z),
                [
                    shape((4, z.part, z.cols), LOW),
                    shape((rows, nt * inner), LOW),
                    shape((rows, width), F32),
                    shape((rows, ff), LOW),
                    shape((rows, width), LOW),
                    shape((rows, ff), LOW),
                    shape((rows, width), F32),
                    shape((rows, width), LOW),
                    shape((rows, inner), F32),
                    shape((8, width), F32),
                ]
                + [shape((z.dense, 128), LOW)] * (nt - 1),
                rest_in + [attended, att_two, att_pair, stream, cot, small],
                name="feed",
            )
        )
        att_got = [to_tp(att_sends[k - 1], k) for k in range(1, nt)]
        keep, sent = call(
            part(rest_grad_kernel, z),
            [shape((4, chunk, z.cols), F32), shape((4, chunk, z.cols), LOW)],
            [normed_two, grad_pre, cot, hidden, part_low, att_all],
            name="rest_grad",
        )
        out_pair, out_sent = call(
            part(down_kernel, z),
            [shape((2, block, width), F32), shape((2, block, width), LOW)],
            [hidden, w_rest, middle, small],
            [pltpu.VMEM((rows, width), F32)],
            name="down",
        )
        out_sent = to_tp(out_sent, 1)
        if z.direct:
            rest_sent = other_core(sent)
            att_got, rest_sent, out_sent = tie((att_got, rest_sent, out_sent))
            proj_sent, proj_kept, feed_sent, feed_kept = call(
                part(rest_one_kernel, z),
                [
                    shape((2, chunk, nt * inner), LOW),
                    shape((2, chunk, nt * inner), F32),
                    shape((2, chunk, 2 * ff), LOW),
                    shape((2, chunk, 2 * ff), F32),
                ],
                [keep, rest_sent],
                name="rest_one",
            )
            proj_in, feed_in = to_near(proj_sent), to_near(feed_sent)
        out_kept, out_sent = call(
            second_kernel,
            [shape((block, width), F32), shape((block, width), LOW)],
            [out_pair, out_sent],
            name="down_pair",
        )
        out_two = to_tp(out_sent, 2)

        grads, qv_sum, in_pair, in_sent = call(
            part(back_kernel, z),
            [
                shape((rows, 3 * inner), LOW),
                shape((1, 3 * inner), F32),
                shape((2, block + 8, width), F32),
                shape((2, block + 8, width), LOW),
            ],
            [own_att] + att_got + [act, soft, w_qkv, normal_one, inverse_one, part_middle, small, small_two],
            [pltpu.VMEM((rows, width), F32)],
            name="back",
        )
        in_one = to_tp(in_sent, 1)
        keep_qkv, sent_qkv = call(
            part(qkv_grad_kernel, z),
            [shape((4, chunk, 3 * inner), F32), shape((4, chunk, 3 * inner), LOW)],
            [normed_one, grads],
            name="qkv_grad",
        )
        in_kept, in_sent = call(
            second_kernel,
            [shape((block + 8, width), F32), shape((block + 8, width), LOW)],
            [in_pair, in_one],
            name="in_pair",
        )
        in_two = to_tp(in_sent, 2)
        if z.direct:
            proj_own, proj_sent = call(
                second_kernel,
                [shape((chunk, nt * inner), F32), shape((chunk, nt * inner), LOW)],
                [proj_kept, proj_in],
                name="proj_second",
            )
            proj_in = to_cross(proj_sent)
            qkv_in = other_core(sent_qkv)

        (out_own,) = call(down_last_kernel, [shape((block, width), LOW)], [out_kept, out_two], name="down_last")
        extra = chunk // 4 if z.direct else 0
        in_block, vec_sum, *proj_keep = call(
            part(sum_rows_kernel, z),
            [shape((block + 2 * extra, width), LOW), shape((16, width), F32)]
            + ([shape((2, extra, width), F32)] if extra else []),
            [in_kept, in_two, small_two, qv_sum] + ([proj_own, proj_in] if extra else []),
            name="sum_rows",
        )
        block_two = to_tp(in_block, 2)
        out_block = to_tp(out_own, 2)
        if z.direct:
            feed_own, feed_sent = call(
                second_kernel,
                [shape((chunk, 2 * ff), F32), shape((chunk, 2 * ff), LOW)],
                [feed_kept, feed_in],
                name="feed_second",
            )
            feed_in = to_cross(feed_sent)
            qkv_sent, qkv_kept = call(
                part(qkv_one_kernel, z),
                [shape((2, chunk + EXTRA, 3 * inner), LOW), shape((2, chunk + EXTRA, 3 * inner), F32)],
                [keep_qkv, qkv_in, vec_sum],
                [pltpu.VMEM((4, EXTRA, 3 * inner), F32)],
                name="qkv_one",
            )
            qkv_in = to_near(qkv_sent)
        in_pair, *proj_kept = call(
            part(rows_pair_kernel, z),
            [shape((2 * block + extra, width), LOW)] + ([shape((extra, width), F32)] if extra else []),
            [in_block, block_two] + proj_keep,
            name="rows_pair",
        )
        block_pair = to_tp(in_pair, 1)
        out_pair = pair_of(out_own, out_block).reshape(2 * block, width)
        out_far = to_tp(out_pair, 1)
        if z.direct:
            feed_own, feed_sent = call(
                third_kernel,
                [shape((chunk, 2 * ff), F32), shape((chunk, 2 * ff), LOW)],
                [feed_own, feed_in],
                name="feed_third",
            )
            feed_in = other_core(feed_sent)
            qkv_own, qkv_sent = call(
                second_kernel,
                [shape((chunk + EXTRA, 3 * inner), F32), shape((chunk + EXTRA, 3 * inner), LOW)],
                [qkv_kept, qkv_in],
                name="qkv_second",
            )
            qkv_in = to_cross(qkv_sent)
        out_mine, out_theirs = call(
            part(rows_kernel, z),
            [shape((z.half, width), F32), shape((z.half, width), LOW)],
            [out_pair, out_far],
            [pltpu.VMEM((rows, width), F32)],
            name="out_rows",
        )
        out_in = other_core(out_theirs)
        in_mine, in_theirs, *proj_own = call(
            part(rows_kernel, z),
            [shape((z.half, width), F32), shape((z.padded + extra if extra else z.half, width), LOW)]
            + ([shape((extra, width), F32)] if extra else []),
            [in_pair, block_pair] + proj_kept,
            [pltpu.VMEM((rows, width), F32)],
            name="in_rows",
        )
        in_in = other_core(in_theirs)
        (output,) = call(
            place_kernel,
            [shape((z.half, 2, width), LOW)],
            [out_mine, out_in],
            [pltpu.VMEM((z.half, 2, width), F32)],
            name="place_out",
        )
        output = output.transpose(1, 0, 2)
        if z.direct:
            fc1_grad, fc2_grad = call(
                part(feed_final_kernel, z), [shape((z.shard, ff), F32)] * 2, [feed_own, feed_in], name="feed_final"
            )
            qkv_own, qkv_sent = call(
                third_kernel,
                [shape((chunk + EXTRA, 3 * inner), F32), shape((chunk + EXTRA, 3 * inner), LOW)],
                [qkv_own, qkv_in],
                name="qkv_third",
            )
            qkv_in = other_core(qkv_sent)
        (input_grad,) = call(place_kernel, [shape((z.half, 2, width), F32)], [in_mine, in_in], name="place_in")
        input_grad = input_grad.transpose(1, 0, 2)
        if z.direct:
            (proj_grad,) = call(
                part(proj_final_kernel, z), [shape((inner, z.shard), F32)], [proj_own[0], in_in], name="proj_final"
            )
            qkv_grad, up_grad, qv_grad, *vec_grads = call(
                part(qkv_final_kernel, z),
                [shape((3, z.shard, inner), F32), shape(fc1_bias.shape, F32), shape(qv3.shape, F32)]
                + [shape((z.shard,), F32)] * 6,
                [qkv_own, qkv_in],
                name="qkv_final",
            )
        else:

            def scatter(keep, sent):
                whole = jnp.stack([keep.astype(LOW), sent], 1).reshape(width, -1)
                whole = lax.psum(whole, "ctx")
                return lax.psum_scatter(whole, "fsdp", scatter_dimension=0, tiled=True).astype(F32)

            rest_own = scatter(keep, sent)
            fc1_grad, fc2_grad = rest_own[:, :ff], rest_own[:, ff : 2 * ff]
            proj_grad = rest_own[:, 2 * ff : 2 * ff + inner]
            for k in range(1, nt):
                cut = rest_own[:, 2 * ff + k * inner : 2 * ff + (k + 1) * inner]
                proj_grad = proj_grad + to_tp(cut.astype(LOW), k).astype(F32)
            proj_grad = proj_grad.T
            qkv_grad = scatter(keep_qkv, sent_qkv).reshape(z.shard, 3, inner).transpose(1, 0, 2)

            def own_columns(value):
                value = lax.psum(value, ("fsdp", "ctx"))
                return lax.dynamic_slice_in_dim(value, f * (value.shape[1] // nf), value.shape[1] // nf, 1)

            vec_grads = own_columns(vec_sum[:6])
            up_grad = own_columns(vec_sum[8, :ff].reshape(-1, HD))
            qv_grad = vec_sum[9, : 3 * inner].reshape(3, z.heads, HD)[0::2].transpose(1, 0, 2)
            qv_grad = own_columns(qv_grad.reshape(2 * z.heads, HD)).reshape(qv3.shape)
        return (
            output,
            input_grad,
            vec_grads[0],
            vec_grads[1],
            qkv_grad.transpose(1, 0, 2),
            qv_grad.transpose(1, 0, 2),
            proj_grad,
            vec_grads[2],
            vec_grads[3],
            vec_grads[4],
            fc1_grad,
            up_grad,
            fc2_grad.T,
            vec_grads[5],
        )

    return local


def solution(mesh):
    sizes = mesh.shape
    return jax.shard_map(
        build(sizes["fsdp"], sizes["ctx"], sizes["tp"]),
        mesh=mesh,
        in_specs=(
            P("fsdp", "ctx", None),
            P("fsdp"),
            P("fsdp"),
            P("fsdp", None, "tp"),
            P(None, "tp", "fsdp"),
            P("tp", "fsdp"),
            P("fsdp"),
            P("fsdp"),
            P("fsdp"),
            P("fsdp", "tp"),
            P("tp", "fsdp"),
            P("tp", "fsdp"),
            P("fsdp"),
            P("fsdp", "ctx", None),
        ),
        out_specs=(
            P("fsdp", "ctx", None),
            P("fsdp", "ctx", None),
            P("fsdp"),
            P("fsdp"),
            P("fsdp", None, "tp"),
            P(None, "tp", "fsdp"),
            P("tp", "fsdp"),
            P("fsdp"),
            P("fsdp"),
            P("fsdp"),
            P("fsdp", "tp"),
            P("tp", "fsdp"),
            P("tp", "fsdp"),
            P("fsdp"),
        ),
        check_vma=False,
    )
```

time: 168 us -> 114 us (0.68)
  waiting for transfers between devices: 84.7 us -> 51.3 us
  starting transfers between devices: 52.9 us -> 40.9 us
  local copies, waits for them, and re-layouts: 13 us -> 1.78 us
  Pallas kernels: 14.1 us -> 18.9 us
  other arithmetic: 1.93 us -> 0 us
    ppermute x36 -> x27, waiting for transfers between devices: 81.9 us -> 47.6 us  [the longest x15 31.8 us: to_tp(): return lax.ppermute(value, 'tp', [(i, i ^ k) for i in range(nt)])]
    ppermute x36 -> x27, starting transfers between devices: 50.4 us -> 37.7 us  [the longest x15 19.7 us: to_tp(): return lax.ppermute(value, 'tp', [(i, i ^ k) for i in range(nt)])]
    unnamed x24 -> x12, local copies, waits for them, and re-layouts: 7.55 us -> 1.78 us
    pallas_call x20 -> x34, Pallas kernels: 14.1 us -> 18.9 us  [call(): pl.pallas_call(kernel, out_shape=tuple(outs), in_specs=in_specs or [VMEM]...]
    dynamic_slice x3 -> x0, local copies, waits for them, and re-layouts: 3.42 us -> none  [the longest x1 2.48 us: pick(): return lax.dynamic_index_in_dim(value, index, 0, False)]
  transfers between devices with their start and end apart: 51 -> 42, of which waited for: 23 -> 17; matrix products, arithmetic and copies ran while one was open for 5% -> 0% of each run, Pallas kernels for 5% -> 9%
where the time goes in v3:
time: 114 us
  waiting for transfers between devices  51.3 us (45%)
  starting transfers between devices  40.9 us (36%)
  Pallas kernels  18.9 us (17%)
  local copies, waits for them, and re-layouts  1.78 us (2%)
    ppermute x15, waiting for transfers between devices, to_tp(): return lax.ppermute(value, 'tp', [(i, i ^ k) for i in range(nt)])  31.8 us
    ppermute x15, starting transfers between devices, to_tp(): return lax.ppermute(value, 'tp', [(i, i ^ k) for i in range(nt)])  19.7 us
    pallas_call x34, Pallas kernels, call(): pl.pallas_call(kernel, out_shape=tuple(outs), in_specs=in_specs or [VMEM]...  18.9 us
    ppermute x10, starting transfers between devices, neighbours(): return lax.ppermute(value, ('fsdp', 'ctx'), pairs)  14.2 us
    ppermute x10, waiting for transfers between devices, neighbours(): return lax.ppermute(value, ('fsdp', 'ctx'), pairs)  9.61 us
    ppermute x2, waiting for transfers between devices, to_far(): return lax.ppermute(value, 'fsdp', [(i, i ^ 3) for i in range(nf)])  6.25 us
    ppermute x2, starting transfers between devices, to_far(): return lax.ppermute(value, 'fsdp', [(i, i ^ 3) for i in range(nf)])  3.88 us
    ppermute x15, waiting for transfers between devices, other_core(): return lax.ppermute(value, 'ctx', [(0, 1), (1, 0)])  3.68 us
  transfers between devices with their start and end apart: 42, of which 17 were waited for; matrix products, arithmetic and copies ran while one was open for 0% of the time, Pallas kernels for 9%

profile of v3, /device:TPU:0, one launch (start us, length us, event | category | flops | bytes accessed | tf_op | source)
XLA Modules:
  0.0 113.9 jit_solution(13275448048590933486)
XLA Ops:
  0.7 2.6 %pack.1 = (bf16[208,576]{1,0:T(8,128)(2,1)}, bf16[112,576]{1,0:T(8,128)(2,1)}, bf16[96,192]{1,0:T(8,128)(2,1)}, bf16[192,1536]{1,0:T(8,128)(2,1)}, bf16[96,1536]{1,0:T(8,128)(2,1)}) custom-call(bf16[3,192,192]{2,1,0:T(8,128)(2,1)} %bitcast.19, bf16[192,192]{1,0:T(8,128)(2,1)} %refs_1_.1, bf16[12,16]{1,0:T(8,128)(2,1)} %refs_2_.1, ...), custom_call_target="tpu_custom_call" | custom-call | tf_op jit(solution)/shard_map/pack/pallas_call | solution.py:33
  3.3 3.0 %collective-permute-start = (bf16[96,1536]{1,0:T(8,128)(2,1)}, bf16[96,1536]{1,0:T(8,128)(2,1)S(1)}, u32[]{:S(2)}, u32[]{:S(2)}) collective-permute-start(bf16[96,1536]{1,0:T(8,128)(2,1)} %get-tuple-element.108.first), channel_id=1, source_target_pairs={{0,8},{4,20},{8,0},{12,28},{16,24},{20,4},{24,16},{28,12},{1,9},{5... | collective-permute-start | bytes 884744 | tf_op jit(solution)/shard_map/ppermute | solution.py:564
  6.3 0.5 collective-permute-start.4
  6.8 0.6 collective-permute-start.2
  7.4 2.6 %collective-permute-start.11 = (bf16[96,192]{1,0:T(8,128)(2,1)}, bf16[96,192]{1,0:T(8,128)(2,1)S(1)}, u32[]{:S(2)}, u32[]{:S(2)}) collective-permute-start(bf16[96,192]{1,0:T(8,128)(2,1)} %get-tuple-element.118.first.own), channel_id=1, source_target_pairs={{0,2},{1,3},{2,0},{3,1},{4,6},{5,7},{6,4},{7,5},{8,10},{9,11},{10,... | collective-permute-start | bytes 110600 | tf_op jit(solution)/shard_map/ppermute | solution.py:557
  10.0 1.2 %collective-permute-done.second.refs_1_ = bf16[96,1536]{1,0:T(8,128)(2,1)S(1)} collective-permute-done((bf16[96,1536]{1,0:T(8,128)(2,1)}, bf16[96,1536]{1,0:T(8,128)(2,1)S(1)}, u32[]{:S(2)}, u32[]{:S(2)}) %collective-permute-start) | collective-permute-done | bytes 294944 | tf_op jit(solution)/shard_map/ppermute | solution.py:564
  11.2 3.0 %collective-permute-start.3 = (bf16[112,576]{1,0:T(8,128)(2,1)}, bf16[112,576]{1,0:T(8,128)(2,1)S(1)}, u32[]{:S(2)}, u32[]{:S(2)}) collective-permute-start(bf16[112,576]{1,0:T(8,128)(2,1)} %get-tuple-element.110), channel_id=1, source_target_pairs={{0,24},{8,16},{16,8},{24,0},{1,25},{9,17},{17,9},{25,1},{2,26},{10... | collective-permute-start | bytes 387080 | tf_op jit(solution)/shard_map/ppermute | solution.py:560
  14.2 1.0 copy-done.3
  15.2 0.6 collective-permute-start.10
  15.8 0.8 copy-done.5
  16.6 1.6 %collective-permute-start.12 = (bf16[2,96,192]{2,1,0:T(8,128)(2,1)S(1)}, bf16[2,96,192]{2,1,0:T(8,128)(2,1)S(1)}, u32[]{:S(2)}, u32[]{:S(2)}) collective-permute-start(bf16[2,96,192]{2,1,0:T(8,128)(2,1)S(1)} %pair.6), channel_id=1, source_target_pairs={{0,1},{1,0},{2,3},{3,2},{4,5},{5,4},{6,7},{7,6},{8,9},{9,8},{10,11... | collective-permute-start | bytes 221192 | tf_op jit(solution)/shard_map/ppermute | solution.py:557
  18.2 0.4 cotangent.1.refs_14_.cot
  18.6 0.6 frame.1
  19.2 0.7 collective-permute-done.3.refs_3_
  19.9 1.4 %collective-permute-done.12.pair = bf16[2,96,192]{2,1,0:T(8,128)(2,1)S(1)} collective-permute-done((bf16[2,96,192]{2,1,0:T(8,128)(2,1)S(1)}, bf16[2,96,192]{2,1,0:T(8,128)(2,1)S(1)}, u32[]{:S(2)}, u32[]{:S(2)}) %collective-permute-start.12) | collective-permute-done | bytes 73760 | tf_op jit(solution)/shard_map/ppermute | solution.py:557
  21.5 0.5 collective-permute-start.7
  21.9 0.9 collective-permute-done.13.theirs
  22.8 0.2 collective-permute-start.14
  23.0 1.3 %attend.1 = (f32[8,768]{1,0:T(8,128)S(1)}, bf16[4,192,576]{2,1,0:T(8,128)(2,1)S(1)}, bf16[208,768]{1,0:T(8,128)(2,1)S(1)}, bf16[3,208,192]{2,1,0:T(8,128)(2,1)S(...) custom-call(bf16[208,576]{1,0:T(8,128)(2,1)S(1)} %copy-done.4, ...), custom_call_target="tpu_custom_call" | custom-call | tf_op jit(solution)/shard_map/attend/pallas_call | solution.py:33
  24.3 3.1 %collective-permute-start.8 = (bf16[312,128]{1,0:T(8,128)(2,1)S(1)}, bf16[312,128]{1,0:T(8,128)(2,1)S(1)}, u32[]{:S(2)}, u32[]{:S(2)}) collective-permute-start(bf16[312,128]{1,0:T(8,128)(2,1)S(1)} %get-tuple-element.117.first.refs_10_), channel_id=1, source_target_pairs={{0,2},{1,3},{2,0},{3,1},{4,6},{5,7},{6,4},{7,5},{8,10},{9,11},{10,... | collective-permute-start | bytes 239624 | tf_op jit(solution)/shard_map/ppermute | solution.py:557
  27.4 4.8 %collective-permute-done.8.second.refs_11_ = bf16[312,128]{1,0:T(8,128)(2,1)S(1)} collective-permute-done((bf16[312,128]{1,0:T(8,128)(2,1)S(1)}, bf16[312,128]{1,0:T(8,128)(2,1)S(1)}, u32[]{:S(2)}, u32[]{:S(2)}) %collective-permute-start.8) | collective-permute-done | bytes 79904 | tf_op jit(solution)/shard_map/ppermute | solution.py:557
  32.2 1.2 %collective-permute-start.9 = (bf16[2,312,128]{2,1,0:T(8,128)(2,1)S(1)}, bf16[2,312,128]{2,1,0:T(8,128)(2,1)S(1)}, u32[]{:S(2)}, u32[]{:S(2)}) collective-permute-start(bf16[2,312,128]{2,1,0:T(8,128)(2,1)S(1)} %pair.4), channel_id=1, source_target_pairs={{0,1},{1,0},{2,3},{3,2},{4,5},{5,4},{6,7},{7,6},{8,9},{9,8},{10,11... | collective-permute-start | bytes 479240 | tf_op jit(solution)/shard_map/ppermute | solution.py:557
  33.3 0.9 collective-permute-start.15
  34.2 5.6 %collective-permute-done.15.refs_8_ = bf16[96,768]{1,0:T(8,128)(2,1)S(1)} collective-permute-done((bf16[96,768]{1,0:T(8,128)(2,1)S(1)}, bf16[96,768]{1,0:T(8,128)(2,1)S(1)}, u32[]{:S(2)}, u32[]{:S(2)}) %collective-permute-start.15) | collective-permute-done | bytes 147488 | tf_op jit(solution)/shard_map/ppermute | solution.py:560
  39.9 0.5 collective-permute-start.1
  40.5 0.4 collective-permute-start.18
  40.9 1.4 %collective-permute-done.1.refs_2_ = bf16[96,1536]{1,0:T(8,128)(2,1)S(1)} collective-permute-done((bf16[96,1536]{1,0:T(8,128)(2,1)S(1)}, bf16[96,1536]{1,0:T(8,128)(2,1)S(1)}, u32[]{:S(2)}, u32[]{:S(2)}) %collective-permute-start.1) | collective-permute-done | bytes 294944 | tf_op jit(solution)/shard_map/ppermute | solution.py:554
  42.3 0.6 collective-permute-done.18.refs_9_
  43.0 3.1 %feed.1 = (bf16[4,192,2304]{2,1,0:T(8,128)(2,1)S(1)}, bf16[208,768]{1,0:T(8,128)(2,1)S(1)}, f32[208,768]{1,0:T(8,128)S(1)}, bf16[208,768]{1,0:T(8,128)(2,1)S(1)}...) custom-call(bf16[192,1536]{1,0:T(8,128)(2,1)S(1)} %copy-done, ...), custom_call_target="tpu_custom_call" | custom-call | tf_op jit(solution)/shard_map/feed/pallas_call | solution.py:33
  46.0 1.3 %rest_grad.1 = (f32[4,96,2304]{2,1,0:T(8,128)S(1)}, bf16[4,96,2304]{2,1,0:T(8,128)(2,1)S(1)}) custom-call(bf16[208,768]{1,0:T(8,128)(2,1)S(1)} %get-tuple-element.133.normed, bf16[208,768]{1,0:T(8,128)(2,1)S(1)} %get-tuple-element.134.pre, bf16[208,768]{1,0:T(8,128)(2,1)S(1)} %cotangent.1.refs_14_.cot, bf16[208,768]{1,0:T(8,128)(2,1)S(1)} %get-tuple-element.126.hidden, ...), custom_call_target="tpu_custom_call" | custom-call | tf_op jit(solution)/shard_map/rest_grad/pallas_call | solution.py:33
  47.3 0.2 collective-permute-start.22
  47.5 0.6 down.1
  48.1 1.0 collective-permute-start.23
  49.2 1.1 collective-permute-start.19
  50.2 3.4 %collective-permute-start.20 = (bf16[312,128]{1,0:T(8,128)(2,1)S(1)}, bf16[312,128]{1,0:T(8,128)(2,1)S(1)}, u32[]{:S(2)}, u32[]{:S(2)}) collective-permute-start(bf16[312,128]{1,0:T(8,128)(2,1)S(1)} %get-tuple-element.131), channel_id=1, source_target_pairs={{0,2},{1,3},{2,0},{3,1},{4,6},{5,7},{6,4},{7,5},{8,10},{9,11},{10,... | collective-permute-start | bytes 239624 | tf_op jit(solution)/shard_map/ppermute | solution.py:557
  53.6 4.6 %collective-permute-done.19.refs_1_ = bf16[312,128]{1,0:T(8,128)(2,1)S(1)} collective-permute-done((bf16[312,128]{1,0:T(8,128)(2,1)S(1)}, bf16[312,128]{1,0:T(8,128)(2,1)S(1)}, u32[]{:S(2)}, u32[]{:S(2)}) %collective-permute-start.19) | collective-permute-done | bytes 79904 | tf_op jit(solution)/shard_map/ppermute | solution.py:557
  58.3 4.5 %collective-permute-done.21.refs_3_ = bf16[312,128]{1,0:T(8,128)(2,1)S(1)} collective-permute-done((bf16[312,128]{1,0:T(8,128)(2,1)S(1)}, bf16[312,128]{1,0:T(8,128)(2,1)S(1)}, u32[]{:S(2)}, u32[]{:S(2)}) %collective-permute-start.21) | collective-permute-done | bytes 79904 | tf_op jit(solution)/shard_map/ppermute | solution.py:557
  62.8 0.4 rest_one.1
  63.2 0.4 collective-permute-start.39
  63.6 1.7 %collective-permute-start.30 = (bf16[2,96,768]{2,1,0:T(8,128)(2,1)S(1)}, bf16[2,96,768]{2,1,0:T(8,128)(2,1)S(1)}, u32[]{:S(2)}, u32[]{:S(2)}) collective-permute-start(bf16[2,96,768]{2,1,0:T(8,128)(2,1)S(1)} %get-tuple-element.162), channel_id=1, source_target_pairs={{0,8},{4,20},{8,0},{12,28},{16,24},{20,4},{24,16},{28,12},{1,9},{5... | collective-permute-start | bytes 884744 | tf_op jit(solution)/shard_map/ppermute | solution.py:564
  65.3 2.0 %back.1 = (bf16[208,576]{1,0:T(8,128)(2,1)S(1)}, f32[1,576]{1,0:T(1,128)S(1)}, f32[2,64,768]{2,1,0:T(8,128)S(1)}, bf16[2,64,768]{2,1,0:T(8,128)(2,1)S(1)}) custom-call(f32[208,192]{1,0:T(8,128)S(1)} %get-tuple-element.144.refs_0_, bf16[312,128]{1,0:T(8,128)(2,1)S(1)} %collective-permute-done.19.refs_1_, ...), custom_call_target="tpu_custom_call" | custom-call | tf_op jit(solution)/shard_map/back/pallas_call | solution.py:33
  67.3 0.5 qkv_grad.1
  68.0 8.3 %collective-permute-done.30.received = bf16[2,96,768]{2,1,0:T(8,128)(2,1)S(1)} collective-permute-done((bf16[2,96,768]{2,1,0:T(8,128)(2,1)S(1)}, bf16[2,96,768]{2,1,0:T(8,128)(2,1)S(1)}, u32[]{:S(2)}, u32[]{:S(2)}) %collective-permute-start.30) | collective-permute-done | bytes 294944 | tf_op jit(solution)/shard_map/ppermute | solution.py:564
  76.4 0.3 collective-permute-start.31
  76.8 0.7 collective-permute-start.29
  77.6 2.1 %collective-permute-start.40 = (bf16[96,1536]{1,0:T(8,128)(2,1)S(1)}, bf16[96,1536]{1,0:T(8,128)(2,1)S(1)}, u32[]{:S(2)}, u32[]{:S(2)}) collective-permute-start(bf16[96,1536]{1,0:T(8,128)(2,1)S(1)} %get-tuple-element.193), channel_id=1, source_target_pairs={{0,16},{4,12},{8,24},{12,4},{16,0},{20,28},{24,8},{28,20},{1,17},{... | collective-permute-start | bytes 884744 | tf_op jit(solution)/shard_map/ppermute | solution.py:564
  79.7 2.9 %collective-permute-done.29.received = bf16[64,768]{1,0:T(8,128)(2,1)S(1)} collective-permute-done((bf16[64,768]{1,0:T(8,128)(2,1)S(1)}, bf16[64,768]{1,0:T(8,128)(2,1)S(1)}, u32[]{:S(2)}, u32[]{:S(2)}) %collective-permute-start.29) | collective-permute-done | bytes 98336 | tf_op jit(solution)/shard_map/ppermute | solution.py:557
  82.7 0.5 collective-permute-start.32
  83.2 0.2 qkv_one.1
  83.4 2.5 %collective-permute-start.36 = (bf16[2,112,576]{2,1,0:T(8,128)(2,1)S(1)}, bf16[2,112,576]{2,1,0:T(8,128)(2,1)S(1)}, u32[]{:S(2)}, u32[]{:S(2)}) collective-permute-start(bf16[2,112,576]{2,1,0:T(8,128)(2,1)S(1)} %get-tuple-element.177), channel_id=1, source_target_pairs={{0,8},{4,20},{8,0},{12,28},{16,24},{20,4},{24,16},{28,12},{1,9},{5... | collective-permute-start | bytes 774152 | tf_op jit(solution)/shard_map/ppermute | solution.py:564
  85.9 3.0 %collective-permute-start.24 = (bf16[56,768]{1,0:T(8,128)(2,1)S(1)}, bf16[56,768]{1,0:T(8,128)(2,1)S(1)}, u32[]{:S(2)}, u32[]{:S(2)}) collective-permute-start(bf16[56,768]{1,0:T(8,128)(2,1)S(1)} %get-tuple-element.141), channel_id=1, source_target_pairs={{0,2},{1,3},{2,0},{3,1},{4,6},{5,7},{6,4},{7,5},{8,10},{9,11},{10,... | collective-permute-start | bytes 258056 | tf_op jit(solution)/shard_map/ppermute | solution.py:557
  88.9 5.7 %collective-permute-done.24.received = bf16[56,768]{1,0:T(8,128)(2,1)S(1)} collective-permute-done((bf16[56,768]{1,0:T(8,128)(2,1)S(1)}, bf16[56,768]{1,0:T(8,128)(2,1)S(1)}, u32[]{:S(2)}, u32[]{:S(2)}) %collective-permute-start.24) | collective-permute-done | bytes 86048 | tf_op jit(solution)/shard_map/ppermute | solution.py:557
  94.7 1.3 %collective-permute-start.33 = (bf16[136,768]{1,0:T(8,128)(2,1)S(1)}, bf16[136,768]{1,0:T(8,128)(2,1)S(1)}, u32[]{:S(2)}, u32[]{:S(2)}) collective-permute-start(bf16[136,768]{1,0:T(8,128)(2,1)S(1)} %get-tuple-element.167.pair), channel_id=1, source_target_pairs={{0,1},{1,0},{2,3},{3,2},{4,5},{5,4},{6,7},{7,6},{8,9},{9,8},{10,11... | collective-permute-start | bytes 626696 | tf_op jit(solution)/shard_map/ppermute | solution.py:557
  96.0 4.1 %collective-permute-done.25.second = bf16[56,768]{1,0:T(8,128)(2,1)S(1)} collective-permute-done((bf16[56,768]{1,0:T(8,128)(2,1)S(1)}, bf16[56,768]{1,0:T(8,128)(2,1)S(1)}, u32[]{:S(2)}, u32[]{:S(2)}) %collective-permute-start.25) | collective-permute-done | bytes 86048 | tf_op jit(solution)/shard_map/ppermute | solution.py:557
  100.5 2.9 %collective-permute-start.37 = (bf16[112,576]{1,0:T(8,128)(2,1)S(1)}, bf16[112,576]{1,0:T(8,128)(2,1)S(1)}, u32[]{:S(2)}, u32[]{:S(2)}) collective-permute-start(bf16[112,576]{1,0:T(8,128)(2,1)S(1)} %get-tuple-element.179), channel_id=1, source_target_pairs={{0,16},{4,12},{8,24},{12,4},{16,0},{20,28},{24,8},{28,20},{1,17},{... | collective-permute-start | bytes 387080 | tf_op jit(solution)/shard_map/ppermute | solution.py:564
  103.4 1.1 collective-permute-done.33.received
  104.7 2.6 %collective-permute-done.26.received = bf16[112,768]{1,0:T(8,128)(2,1)S(1)} collective-permute-done((bf16[112,768]{1,0:T(8,128)(2,1)S(1)}, bf16[112,768]{1,0:T(8,128)(2,1)S(1)}, u32[]{:S(2)}, u32[]{:S(2)}) %collective-permute-start.26) | collective-permute-done | bytes 172064 | tf_op jit(solution)/shard_map/ppermute | solution.py:557
  107.5 0.6 collective-permute-start.38
  108.1 0.8 collective-permute-done.27.theirs
  108.8 1.2 %place_out.1 = bf16[98,2,768]{2,1,0:T(2,128)(2,1)} custom-call(f32[98,768]{1,0:T(8,128)S(1)} %get-tuple-element.142.mine, bf16[98,768]{1,0:T(8,128)(2,1)S(1)} %collective-permute-done.27.theirs), custom_call_target="tpu_custom_call" | custom-call | tf_op jit(solution)/shard_map/place_out/pallas_call | solution.py:33
  110.0 1.0 qkv_final.1
  111.0 0.9 proj_final.1
  111.8 1.0 place_in.1
  112.8 1.1 feed_final.1
  (66 shorter events, 1.8 us)
Async XLA Ops:
  0.6 17.6 %copy-start.1 = (bf16[2,98,768]{2,0,1:T(2,128)(2,1)S(1)}, bf16[2,98,768]{2,0,1:T(2,128)(2,1)}, u32[]{:S(2)}) copy-start(bf16[2,98,768]{2,0,1:T(2,128)(2,1)} %param.27) | copy-start | bytes 903172
  0.7 18.0 %copy-start.2 = (bf16[2,98,768]{2,0,1:T(2,128)(2,1)S(1)}, bf16[2,98,768]{2,0,1:T(2,128)(2,1)}, u32[]{:S(2)}) copy-start(bf16[2,98,768]{2,0,1:T(2,128)(2,1)} %param.14) | copy-start | bytes 903172
  3.3 7.9 %collective-permute-start = (bf16[96,1536]{1,0:T(8,128)(2,1)}, bf16[96,1536]{1,0:T(8,128)(2,1)S(1)}, u32[]{:S(2)}, u32[]{:S(2)}) collective-permute-start(bf16[96,1536]{1,0:T(8,128)(2,1)} %get-tuple-element.108.first), channel_id=1, source_target_pairs={{0,8},{4,20},{8,0},{12,28},{16,24},{20,4},{24,16},{28,12},{1,9},{5... | collective-permute-start | bytes 884744 | tf_op jit(solution)/shard_map/ppermute | solution.py:564
  6.3 10.3 %collective-permute-start.5 = (bf16[98,2,768]{2,1,0:T(2,128)(2,1)}, bf16[98,2,768]{2,1,0:T(2,128)(2,1)S(1)}, u32[]{:S(2)}, u32[]{:S(2)}) collective-permute-start(bf16[98,2,768]{2,1,0:T(2,128)(2,1)} %bitcast.13), channel_id=1, source_target_pairs={{0,4},{4,0},{1,5},{5,1},{2,6},{6,2},{3,7},{7,3},{8,12},{12,8},{9,1... | collective-permute-start | bytes 903176 | tf_op jit(solution)/shard_map/ppermute | solution.py:554
  6.3 12.3 %collective-permute-start.4 = (bf16[98,2,768]{2,1,0:T(2,128)(2,1)}, bf16[98,2,768]{2,1,0:T(2,128)(2,1)S(1)}, u32[]{:S(2)}, u32[]{:S(2)}) collective-permute-start(bf16[98,2,768]{2,1,0:T(2,128)(2,1)} %bitcast.15), channel_id=1, source_target_pairs={{0,4},{4,0},{1,5},{5,1},{2,6},{6,2},{3,7},{7,3},{8,12},{12,8},{9,1... | collective-permute-start | bytes 903176 | tf_op jit(solution)/shard_map/ppermute | solution.py:554
  6.8 13.1 %collective-permute-start.2 = (bf16[208,576]{1,0:T(8,128)(2,1)}, bf16[208,576]{1,0:T(8,128)(2,1)S(1)}, u32[]{:S(2)}, u32[]{:S(2)}) collective-permute-start(bf16[208,576]{1,0:T(8,128)(2,1)} %get-tuple-element.109.refs_0_), channel_id=1, source_target_pairs={{0,8},{4,20},{8,0},{12,28},{16,24},{20,4},{24,16},{28,12},{1,9},{5... | collective-permute-start | bytes 718856 | tf_op jit(solution)/shard_map/ppermute | solution.py:564
  7.4 7.8 %collective-permute-start.11 = (bf16[96,192]{1,0:T(8,128)(2,1)}, bf16[96,192]{1,0:T(8,128)(2,1)S(1)}, u32[]{:S(2)}, u32[]{:S(2)}) collective-permute-start(bf16[96,192]{1,0:T(8,128)(2,1)} %get-tuple-element.118.first.own), channel_id=1, source_target_pairs={{0,2},{1,3},{2,0},{3,1},{4,6},{5,7},{6,4},{7,5},{8,10},{9,11},{10,... | collective-permute-start | bytes 110600 | tf_op jit(solution)/shard_map/ppermute | solution.py:557
  11.2 8.7 %collective-permute-start.3 = (bf16[112,576]{1,0:T(8,128)(2,1)}, bf16[112,576]{1,0:T(8,128)(2,1)S(1)}, u32[]{:S(2)}, u32[]{:S(2)}) collective-permute-start(bf16[112,576]{1,0:T(8,128)(2,1)} %get-tuple-element.110), channel_id=1, source_target_pairs={{0,24},{8,16},{16,8},{24,0},{1,25},{9,17},{17,9},{25,1},{2,26},{10... | collective-permute-start | bytes 387080 | tf_op jit(solution)/shard_map/ppermute | solution.py:560
  14.2 1.0 copy-start.3
  15.1 7.9 %copy-start.4 = (bf16[208,576]{1,0:T(8,128)(2,1)S(1)}, bf16[208,576]{1,0:T(8,128)(2,1)}, u32[]{:S(2)}) copy-start(bf16[208,576]{1,0:T(8,128)(2,1)} %get-tuple-element.109.refs_0_) | copy-start | bytes 718852
  15.2 24.6 %collective-permute-start.10 = (bf16[2,96,1536]{2,1,0:T(8,128)(2,1)S(1)}, bf16[2,96,1536]{2,1,0:T(8,128)(2,1)S(1)}, u32[]{:S(2)}, u32[]{:S(2)}) collective-permute-start(bf16[2,96,1536]{2,1,0:T(8,128)(2,1)S(1)} %pair.5), channel_id=1, source_target_pairs={{0,16},{4,12},{8,24},{12,4},{16,0},{20,28},{24,8},{28,20},{1,17},{... | collective-permute-start | bytes 1769480 | tf_op jit(solution)/shard_map/ppermute | solution.py:564
  15.8 0.8 copy-start.5
  16.6 4.7 %collective-permute-start.12 = (bf16[2,96,192]{2,1,0:T(8,128)(2,1)S(1)}, bf16[2,96,192]{2,1,0:T(8,128)(2,1)S(1)}, u32[]{:S(2)}, u32[]{:S(2)}) collective-permute-start(bf16[2,96,192]{2,1,0:T(8,128)(2,1)S(1)} %pair.6), channel_id=1, source_target_pairs={{0,1},{1,0},{2,3},{3,2},{4,5},{5,4},{6,7},{7,6},{8,9},{9,8},{10,11... | collective-permute-start | bytes 221192 | tf_op jit(solution)/shard_map/ppermute | solution.py:557
  18.6 24.3 %copy-start = (bf16[192,1536]{1,0:T(8,128)(2,1)S(1)}, bf16[192,1536]{1,0:T(8,128)(2,1)}, u32[]{:S(2)}) copy-start(bf16[192,1536]{1,0:T(8,128)(2,1)} %get-tuple-element.107.refs_0_) | copy-start | bytes 1769476
  19.9 3.2 %collective-permute-start.6 = (bf16[208,576]{1,0:T(8,128)(2,1)S(1)}, bf16[208,576]{1,0:T(8,128)(2,1)S(1)}, u32[]{:S(2)}, u32[]{:S(2)}) collective-permute-start(bf16[208,576]{1,0:T(8,128)(2,1)S(1)} %collective-permute-done.2.refs_1_), channel_id=1, source_target_pairs={{0,4},{4,0},{1,5},{5,1},{2,6},{6,2},{3,7},{7,3},{8,12},{12,8},{9,1... | collective-permute-start | bytes 718856 | tf_op jit(solution)/shard_map/ppermute | solution.py:554
  21.4 1.4 %collective-permute-start.13 = (bf16[96,768]{1,0:T(8,128)(2,1)S(1)}, bf16[96,768]{1,0:T(8,128)(2,1)S(1)}, u32[]{:S(2)}, u32[]{:S(2)}) collective-permute-start(bf16[96,768]{1,0:T(8,128)(2,1)S(1)} %pack_proj.1.mine), channel_id=1, source_target_pairs={{0,4},{4,0},{1,5},{5,1},{2,6},{6,2},{3,7},{7,3},{8,12},{12,8},{9,1... | collective-permute-start | bytes 442376 | tf_op jit(solution)/shard_map/ppermute | solution.py:554
  21.5 1.6 %collective-permute-start.7 = (bf16[112,576]{1,0:T(8,128)(2,1)S(1)}, bf16[112,576]{1,0:T(8,128)(2,1)S(1)}, u32[]{:S(2)}, u32[]{:S(2)}) collective-permute-start(bf16[112,576]{1,0:T(8,128)(2,1)S(1)} %collective-permute-done.3.refs_3_), channel_id=1, source_target_pairs={{0,4},{4,0},{1,5},{5,1},{2,6},{6,2},{3,7},{7,3},{8,12},{12,8},{9,1... | collective-permute-start | bytes 387080 | tf_op jit(solution)/shard_map/ppermute | solution.py:554
  22.8 17.0 %collective-permute-start.14 = (bf16[192,768]{1,0:T(8,128)(2,1)S(1)}, bf16[192,768]{1,0:T(8,128)(2,1)S(1)}, u32[]{:S(2)}, u32[]{:S(2)}) collective-permute-start(bf16[192,768]{1,0:T(8,128)(2,1)S(1)} %pack_near.1.refs_5_), channel_id=1, source_target_pairs={{0,8},{4,20},{8,0},{12,28},{16,24},{20,4},{24,16},{28,12},{1,9},{5... | collective-permute-start | bytes 884744 | tf_op jit(solution)/shard_map/ppermute | solution.py:564
  24.3 7.8 %collective-permute-start.8 = (bf16[312,128]{1,0:T(8,128)(2,1)S(1)}, bf16[312,128]{1,0:T(8,128)(2,1)S(1)}, u32[]{:S(2)}, u32[]{:S(2)}) collective-permute-start(bf16[312,128]{1,0:T(8,128)(2,1)S(1)} %get-tuple-element.117.first.refs_10_), channel_id=1, source_target_pairs={{0,2},{1,3},{2,0},{3,1},{4,6},{5,7},{6,4},{7,5},{8,10},{9,11},{10,... | collective-permute-start | bytes 239624 | tf_op jit(solution)/shard_map/ppermute | solution.py:557
  32.2 7.6 %collective-permute-start.9 = (bf16[2,312,128]{2,1,0:T(8,128)(2,1)S(1)}, bf16[2,312,128]{2,1,0:T(8,128)(2,1)S(1)}, u32[]{:S(2)}, u32[]{:S(2)}) collective-permute-start(bf16[2,312,128]{2,1,0:T(8,128)(2,1)S(1)} %pair.4), channel_id=1, source_target_pairs={{0,1},{1,0},{2,3},{3,2},{4,5},{5,4},{6,7},{7,6},{8,9},{9,8},{10,11... | collective-permute-start | bytes 479240 | tf_op jit(solution)/shard_map/ppermute | solution.py:557
  33.3 6.5 %collective-permute-start.15 = (bf16[96,768]{1,0:T(8,128)(2,1)S(1)}, bf16[96,768]{1,0:T(8,128)(2,1)S(1)}, u32[]{:S(2)}, u32[]{:S(2)}) collective-permute-start(bf16[96,768]{1,0:T(8,128)(2,1)S(1)} %pack_proj.1.mine), channel_id=1, source_target_pairs={{0,24},{8,16},{16,8},{24,0},{1,25},{9,17},{17,9},{25,1},{2,26},{10... | collective-permute-start | bytes 442376 | tf_op jit(solution)/shard_map/ppermute | solution.py:560
  39.8 3.1 %collective-permute-start.16 = (bf16[2,96,1536]{2,1,0:T(8,128)(2,1)S(1)}, bf16[2,96,1536]{2,1,0:T(8,128)(2,1)S(1)}, u32[]{:S(2)}, u32[]{:S(2)}) collective-permute-start(bf16[2,96,1536]{2,1,0:T(8,128)(2,1)S(1)} %collective-permute-done.10.refs_3_), channel_id=1, source_target_pairs={{0,4},{4,0},{1,5},{5,1},{2,6},{6,2},{3,7},{7,3},{8,12},{12,8},{9,1... | collective-permute-start | bytes 1769480 | tf_op jit(solution)/shard_map/ppermute | solution.py:554
  39.9 2.4 %collective-permute-start.1 = (bf16[96,1536]{1,0:T(8,128)(2,1)S(1)}, bf16[96,1536]{1,0:T(8,128)(2,1)S(1)}, u32[]{:S(2)}, u32[]{:S(2)}) collective-permute-start(bf16[96,1536]{1,0:T(8,128)(2,1)S(1)} %collective-permute-done.second.refs_1_), channel_id=1, source_target_pairs={{0,4},{4,0},{1,5},{5,1},{2,6},{6,2},{3,7},{7,3},{8,12},{12,8},{9,1... | collective-permute-start | bytes 884744 | tf_op jit(solution)/shard_map/ppermute | solution.py:554
  40.4 2.6 %collective-permute-start.17 = (bf16[192,768]{1,0:T(8,128)(2,1)S(1)}, bf16[192,768]{1,0:T(8,128)(2,1)S(1)}, u32[]{:S(2)}, u32[]{:S(2)}) collective-permute-start(bf16[192,768]{1,0:T(8,128)(2,1)S(1)} %collective-permute-done.14.refs_6_), channel_id=1, source_target_pairs={{0,4},{4,0},{1,5},{5,1},{2,6},{6,2},{3,7},{7,3},{8,12},{12,8},{9,1... | collective-permute-start | bytes 884744 | tf_op jit(solution)/shard_map/ppermute | solution.py:554
  40.5 2.5 %collective-permute-start.18 = (bf16[96,768]{1,0:T(8,128)(2,1)S(1)}, bf16[96,768]{1,0:T(8,128)(2,1)S(1)}, u32[]{:S(2)}, u32[]{:S(2)}) collective-permute-start(bf16[96,768]{1,0:T(8,128)(2,1)S(1)} %collective-permute-done.15.refs_8_), channel_id=1, source_target_pairs={{0,4},{4,0},{1,5},{5,1},{2,6},{6,2},{3,7},{7,3},{8,12},{12,8},{9,1... | collective-permute-start | bytes 442376 | tf_op jit(solution)/shard_map/ppermute | solution.py:554
  47.3 15.5 %collective-permute-start.22 = (bf16[4,96,2304]{2,1,0:T(8,128)(2,1)S(1)}, bf16[4,96,2304]{2,1,0:T(8,128)(2,1)S(1)}, u32[]{:S(2)}, u32[]{:S(2)}) collective-permute-start(bf16[4,96,2304]{2,1,0:T(8,128)(2,1)S(1)} %get-tuple-element.137), channel_id=1, source_target_pairs={{0,4},{4,0},{1,5},{5,1},{2,6},{6,2},{3,7},{7,3},{8,12},{12,8},{9,1... | collective-permute-start | bytes 5308424 | tf_op jit(solution)/shard_map/ppermute | solution.py:554
  48.1 14.7 %collective-permute-start.23 = (bf16[2,56,768]{2,1,0:T(8,128)(2,1)S(1)}, bf16[2,56,768]{2,1,0:T(8,128)(2,1)S(1)}, u32[]{:S(2)}, u32[]{:S(2)}) collective-permute-start(bf16[2,56,768]{2,1,0:T(8,128)(2,1)S(1)} %get-tuple-element.138), channel_id=1, source_target_pairs={{0,1},{1,0},{2,3},{3,2},{4,5},{5,4},{6,7},{7,6},{8,9},{9,8},{10,11... | collective-permute-start | bytes 516104 | tf_op jit(solution)/shard_map/ppermute | solution.py:557
  49.2 9.1 %collective-permute-start.19 = (bf16[312,128]{1,0:T(8,128)(2,1)S(1)}, bf16[312,128]{1,0:T(8,128)(2,1)S(1)}, u32[]{:S(2)}, u32[]{:S(2)}) collective-permute-start(bf16[312,128]{1,0:T(8,128)(2,1)S(1)} %get-tuple-element.130), channel_id=1, source_target_pairs={{0,1},{1,0},{2,3},{3,2},{4,5},{5,4},{6,7},{7,6},{8,9},{9,8},{10,11... | collective-permute-start | bytes 239624 | tf_op jit(solution)/shard_map/ppermute | solution.py:557
  50.2 8.0 %collective-permute-start.20 = (bf16[312,128]{1,0:T(8,128)(2,1)S(1)}, bf16[312,128]{1,0:T(8,128)(2,1)S(1)}, u32[]{:S(2)}, u32[]{:S(2)}) collective-permute-start(bf16[312,128]{1,0:T(8,128)(2,1)S(1)} %get-tuple-element.131), channel_id=1, source_target_pairs={{0,2},{1,3},{2,0},{3,1},{4,6},{5,7},{6,4},{7,5},{8,10},{9,11},{10,... | collective-permute-start | bytes 239624 | tf_op jit(solution)/shard_map/ppermute | solution.py:557
  53.6 9.2 %collective-permute-start.21 = (bf16[312,128]{1,0:T(8,128)(2,1)S(1)}, bf16[312,128]{1,0:T(8,128)(2,1)S(1)}, u32[]{:S(2)}, u32[]{:S(2)}) collective-permute-start(bf16[312,128]{1,0:T(8,128)(2,1)S(1)} %get-tuple-element.132), channel_id=1, source_target_pairs={{0,3},{1,2},{2,1},{3,0},{4,7},{5,6},{6,5},{7,4},{8,11},{9,10},{10,... | collective-permute-start | bytes 239624 | tf_op jit(solution)/shard_map/ppermute | solution.py:557
  63.2 14.3 %collective-permute-start.39 = (bf16[2,96,1536]{2,1,0:T(8,128)(2,1)S(1)}, bf16[2,96,1536]{2,1,0:T(8,128)(2,1)S(1)}, u32[]{:S(2)}, u32[]{:S(2)}) collective-permute-start(bf16[2,96,1536]{2,1,0:T(8,128)(2,1)S(1)} %get-tuple-element.191), channel_id=1, source_target_pairs={{0,8},{4,20},{8,0},{12,28},{16,24},{20,4},{24,16},{28,12},{1,9},{5... | collective-permute-start | bytes 1769480 | tf_op jit(solution)/shard_map/ppermute | solution.py:564
  63.6 12.7 %collective-permute-start.30 = (bf16[2,96,768]{2,1,0:T(8,128)(2,1)S(1)}, bf16[2,96,768]{2,1,0:T(8,128)(2,1)S(1)}, u32[]{:S(2)}, u32[]{:S(2)}) collective-permute-start(bf16[2,96,768]{2,1,0:T(8,128)(2,1)S(1)} %get-tuple-element.162), channel_id=1, source_target_pairs={{0,8},{4,20},{8,0},{12,28},{16,24},{20,4},{24,16},{28,12},{1,9},{5... | collective-permute-start | bytes 884744 | tf_op jit(solution)/shard_map/ppermute | solution.py:564
  67.8 15.4 %collective-permute-start.35 = (bf16[4,96,576]{2,1,0:T(8,128)(2,1)S(1)}, bf16[4,96,576]{2,1,0:T(8,128)(2,1)S(1)}, u32[]{:S(2)}, u32[]{:S(2)}) collective-permute-start(bf16[4,96,576]{2,1,0:T(8,128)(2,1)S(1)} %get-tuple-element.174), channel_id=1, source_target_pairs={{0,4},{4,0},{1,5},{5,1},{2,6},{6,2},{3,7},{7,3},{8,12},{12,8},{9,1... | collective-permute-start | bytes 1327112 | tf_op jit(solution)/shard_map/ppermute | solution.py:554
  67.9 8.8 %collective-permute-start.28 = (bf16[2,64,768]{2,1,0:T(8,128)(2,1)S(1)}, bf16[2,64,768]{2,1,0:T(8,128)(2,1)S(1)}, u32[]{:S(2)}, u32[]{:S(2)}) collective-permute-start(bf16[2,64,768]{2,1,0:T(8,128)(2,1)S(1)} %get-tuple-element.155), channel_id=1, source_target_pairs={{0,1},{1,0},{2,3},{3,2},{4,5},{5,4},{6,7},{7,6},{8,9},{9,8},{10,11... | collective-permute-start | bytes 589832 | tf_op jit(solution)/shard_map/ppermute | solution.py:557
  76.4 6.2 %collective-permute-start.31 = (bf16[96,768]{1,0:T(8,128)(2,1)S(1)}, bf16[96,768]{1,0:T(8,128)(2,1)S(1)}, u32[]{:S(2)}, u32[]{:S(2)}) collective-permute-start(bf16[96,768]{1,0:T(8,128)(2,1)S(1)} %get-tuple-element.164), channel_id=1, source_target_pairs={{0,16},{4,12},{8,24},{12,4},{16,0},{20,28},{24,8},{28,20},{1,17},{... | collective-permute-start | bytes 442376 | tf_op jit(solution)/shard_map/ppermute | solution.py:564
  76.8 5.8 %collective-permute-start.29 = (bf16[64,768]{1,0:T(8,128)(2,1)S(1)}, bf16[64,768]{1,0:T(8,128)(2,1)S(1)}, u32[]{:S(2)}, u32[]{:S(2)}) collective-permute-start(bf16[64,768]{1,0:T(8,128)(2,1)S(1)} %get-tuple-element.157), channel_id=1, source_target_pairs={{0,2},{1,3},{2,0},{3,1},{4,6},{5,7},{6,4},{7,5},{8,10},{9,11},{10,... | collective-permute-start | bytes 294920 | tf_op jit(solution)/shard_map/ppermute | solution.py:557
  77.6 22.6 %collective-permute-start.40 = (bf16[96,1536]{1,0:T(8,128)(2,1)S(1)}, bf16[96,1536]{1,0:T(8,128)(2,1)S(1)}, u32[]{:S(2)}, u32[]{:S(2)}) collective-permute-start(bf16[96,1536]{1,0:T(8,128)(2,1)S(1)} %get-tuple-element.193), channel_id=1, source_target_pairs={{0,16},{4,12},{8,24},{12,4},{16,0},{20,28},{24,8},{28,20},{1,17},{... | collective-permute-start | bytes 884744 | tf_op jit(solution)/shard_map/ppermute | solution.py:564
  82.7 11.9 %collective-permute-start.32 = (bf16[104,768]{1,0:T(8,128)(2,1)S(1)}, bf16[104,768]{1,0:T(8,128)(2,1)S(1)}, u32[]{:S(2)}, u32[]{:S(2)}) collective-permute-start(bf16[104,768]{1,0:T(8,128)(2,1)S(1)} %get-tuple-element.165.own), channel_id=1, source_target_pairs={{0,2},{1,3},{2,0},{3,1},{4,6},{5,7},{6,4},{7,5},{8,10},{9,11},{10,... | collective-permute-start | bytes 479240 | tf_op jit(solution)/shard_map/ppermute | solution.py:557
  83.4 17.0 %collective-permute-start.36 = (bf16[2,112,576]{2,1,0:T(8,128)(2,1)S(1)}, bf16[2,112,576]{2,1,0:T(8,128)(2,1)S(1)}, u32[]{:S(2)}, u32[]{:S(2)}) collective-permute-start(bf16[2,112,576]{2,1,0:T(8,128)(2,1)S(1)} %get-tuple-element.177), channel_id=1, source_target_pairs={{0,8},{4,20},{8,0},{12,28},{16,24},{20,4},{24,16},{28,12},{1,9},{5... | collective-permute-start | bytes 774152 | tf_op jit(solution)/shard_map/ppermute | solution.py:564
  85.9 8.7 %collective-permute-start.24 = (bf16[56,768]{1,0:T(8,128)(2,1)S(1)}, bf16[56,768]{1,0:T(8,128)(2,1)S(1)}, u32[]{:S(2)}, u32[]{:S(2)}) collective-permute-start(bf16[56,768]{1,0:T(8,128)(2,1)S(1)} %get-tuple-element.141), channel_id=1, source_target_pairs={{0,2},{1,3},{2,0},{3,1},{4,6},{5,7},{6,4},{7,5},{8,10},{9,11},{10,... | collective-permute-start | bytes 258056 | tf_op jit(solution)/shard_map/ppermute | solution.py:557
  94.6 5.5 %collective-permute-start.25 = (bf16[56,768]{1,0:T(8,128)(2,1)S(1)}, bf16[56,768]{1,0:T(8,128)(2,1)S(1)}, u32[]{:S(2)}, u32[]{:S(2)}) collective-permute-start(bf16[56,768]{1,0:T(8,128)(2,1)S(1)} %down_last.1.first), channel_id=1, source_target_pairs={{0,2},{1,3},{2,0},{3,1},{4,6},{5,7},{6,4},{7,5},{8,10},{9,11},{10,... | collective-permute-start | bytes 258056 | tf_op jit(solution)/shard_map/ppermute | solution.py:557
  94.7 9.7 %collective-permute-start.33 = (bf16[136,768]{1,0:T(8,128)(2,1)S(1)}, bf16[136,768]{1,0:T(8,128)(2,1)S(1)}, u32[]{:S(2)}, u32[]{:S(2)}) collective-permute-start(bf16[136,768]{1,0:T(8,128)(2,1)S(1)} %get-tuple-element.167.pair), channel_id=1, source_target_pairs={{0,1},{1,0},{2,3},{3,2},{4,5},{5,4},{6,7},{7,6},{8,9},{9,8},{10,11... | collective-permute-start | bytes 626696 | tf_op jit(solution)/shard_map/ppermute | solution.py:557
  100.1 7.2 %collective-permute-start.26 = (bf16[112,768]{1,0:T(8,128)(2,1)S(1)}, bf16[112,768]{1,0:T(8,128)(2,1)S(1)}, u32[]{:S(2)}, u32[]{:S(2)}) collective-permute-start(bf16[112,768]{1,0:T(8,128)(2,1)S(1)} %bitcast.11), channel_id=1, source_target_pairs={{0,1},{1,0},{2,3},{3,2},{4,5},{5,4},{6,7},{7,6},{8,9},{9,8},{10,11... | collective-permute-start | bytes 516104 | tf_op jit(solution)/shard_map/ppermute | solution.py:557
  100.3 12.5 %collective-permute-start.41 = (bf16[96,1536]{1,0:T(8,128)(2,1)S(1)}, bf16[96,1536]{1,0:T(8,128)(2,1)S(1)}, u32[]{:S(2)}, u32[]{:S(2)}) collective-permute-start(bf16[96,1536]{1,0:T(8,128)(2,1)S(1)} %get-tuple-element.195), channel_id=1, source_target_pairs={{0,4},{4,0},{1,5},{5,1},{2,6},{6,2},{3,7},{7,3},{8,12},{12,8},{9,1... | collective-permute-start | bytes 884744 | tf_op jit(solution)/shard_map/ppermute | solution.py:554
  100.5 7.0 %collective-permute-start.37 = (bf16[112,576]{1,0:T(8,128)(2,1)S(1)}, bf16[112,576]{1,0:T(8,128)(2,1)S(1)}, u32[]{:S(2)}, u32[]{:S(2)}) collective-permute-start(bf16[112,576]{1,0:T(8,128)(2,1)S(1)} %get-tuple-element.179), channel_id=1, source_target_pairs={{0,16},{4,12},{8,24},{12,4},{16,0},{20,28},{24,8},{28,20},{1,17},{... | collective-permute-start | bytes 387080 | tf_op jit(solution)/shard_map/ppermute | solution.py:564
  104.6 6.4 %collective-permute-start.34 = (bf16[128,768]{1,0:T(8,128)(2,1)S(1)}, bf16[128,768]{1,0:T(8,128)(2,1)S(1)}, u32[]{:S(2)}, u32[]{:S(2)}) collective-permute-start(bf16[128,768]{1,0:T(8,128)(2,1)S(1)} %get-tuple-element.170), channel_id=1, source_target_pairs={{0,4},{4,0},{1,5},{5,1},{2,6},{6,2},{3,7},{7,3},{8,12},{12,8},{9,1... | collective-permute-start | bytes 589832 | tf_op jit(solution)/shard_map/ppermute | solution.py:554
  107.4 1.5 %collective-permute-start.27 = (bf16[98,768]{1,0:T(8,128)(2,1)S(1)}, bf16[98,768]{1,0:T(8,128)(2,1)S(1)}, u32[]{:S(2)}, u32[]{:S(2)}) collective-permute-start(bf16[98,768]{1,0:T(8,128)(2,1)S(1)} %get-tuple-element.143), channel_id=1, source_target_pairs={{0,4},{4,0},{1,5},{5,1},{2,6},{6,2},{3,7},{7,3},{8,12},{12,8},{9,1... | collective-permute-start | bytes 451592 | tf_op jit(solution)/shard_map/ppermute | solution.py:554
  107.5 2.5 %collective-permute-start.38 = (bf16[112,576]{1,0:T(8,128)(2,1)S(1)}, bf16[112,576]{1,0:T(8,128)(2,1)S(1)}, u32[]{:S(2)}, u32[]{:S(2)}) collective-permute-start(bf16[112,576]{1,0:T(8,128)(2,1)S(1)} %get-tuple-element.181), channel_id=1, source_target_pairs={{0,4},{4,0},{1,5},{5,1},{2,6},{6,2},{3,7},{7,3},{8,12},{12,8},{9,1... | collective-permute-start | bytes 387080 | tf_op jit(solution)/shard_map/ppermute | solution.py:554

commit v4 on v3

v4 whole, which is shorter than its diff:
```python
import functools

import jax
import jax.numpy as jnp
from jax import lax
from jax.experimental import pallas as pl
from jax.experimental.pallas import tpu as pltpu
from jax.sharding import PartitionSpec as P

HD = 64
EPSILON = 1e-06
QUERY_SCALE = 0.125
F32 = jnp.float32
LOW = jnp.bfloat16
NN = ((1,), (0,))
NT = ((1,), (1,))
TN = ((0,), (0,))
VMEM = pl.BlockSpec(memory_space=pltpu.VMEM)
ANY = pl.BlockSpec(memory_space=pl.ANY)
EXTRA = 16
UP_AT, QV_AT = 256, 384


def dot(left, right, dims):
    return lax.dot_general(left, right, (dims, ((), ())), preferred_element_type=F32)


def shape(dims, kind):
    return jax.ShapeDtypeStruct(tuple(dims), kind)


def call(kernel, outs, args, scratch=(), name=None, mib=20, in_specs=None, alias=None):
    return pl.pallas_call(
        kernel,
        out_shape=tuple(outs),
        in_specs=in_specs or [VMEM] * len(args),
        out_specs=tuple([VMEM] * len(outs)),
        scratch_shapes=list(scratch),
        input_output_aliases=alias or {},
        name=name,
        compiler_params=pltpu.CompilerParams(vmem_limit_bytes=mib << 20),
    )(*args)


def gelu_and_slope(v):
    cdf = 0.5 * (1.0 + lax.erf(v * 0.7071067811865476))
    density = jnp.exp(-0.5 * v * v) * 0.3989422804014327
    return v * cdf, cdf + v * density


def mean(v):
    return jnp.mean(v, axis=-1, keepdims=True)


def total_rows(v):
    return jnp.sum(v, axis=0, keepdims=True)


def normalise(v):
    centred = v - mean(v)
    inverse = lax.rsqrt(mean(centred * centred) + EPSILON)
    return centred * inverse, inverse


def norm_backward(grad_normed, normal, inverse, gain):
    scaled = grad_normed * gain
    return inverse * (scaled - mean(scaled) - normal * mean(scaled * normal))


def lanes(parts):
    return jnp.concatenate(parts, axis=1)


def rows_of(parts):
    return jnp.concatenate(parts, axis=0)


def read(ref):
    return ref[...].astype(F32)


class Sizes:
    def __init__(self, nf, nt, inputs, qv_bias, fc1_weight):
        self.nf, self.nt = nf, nt
        _, self.half, self.width = inputs.shape
        self.shard = self.width // nf
        self.heads = qv_bias.shape[1]
        self.inner = self.heads * HD
        self.ff = fc1_weight.shape[1]
        self.pad = -self.half % 8
        self.padded = self.half + self.pad
        self.rows = 2 * self.padded
        self.part = self.width // 4
        self.chunk = self.part // 2
        self.tail = self.part // 4
        self.direct = nf == 4
        self.cols = 2 * self.ff + nt * self.inner
        self.all_cols = 2 * self.ff + -(-3 * self.inner // 128) * 128
        self.dense = self.rows * self.inner // 128

    def half_rows(self, h):
        return pl.ds(pl.multiple_of(h * self.padded, 8), self.padded)

    def half_of(self, c):
        return pl.ds(pl.multiple_of(c * self.chunk, 16), self.chunk)

    def squeeze(self, v):
        return rows_of([v[:, :128], lanes([v[: self.padded, 128:], v[self.padded :, 128:]])])

    def spread(self, v):
        tail = v[self.rows :]
        return lanes([v[: self.rows], rows_of([tail[:, :HD], tail[:, HD:]])])


def fetch(sources, copies, sem):
    moves = [pltpu.make_async_copy(s, d, sem.at[i]) for i, (s, d) in enumerate(zip(sources, copies))]
    for m in moves:
        m.start()
    for m in moves:
        m.wait()


def stage_kernel(z, up, down_t, out, one, two, sem):
    fetch((up, down_t), (one, two), sem)
    out[:, : z.ff] = one[...]
    out[:, z.ff :] = two[...]


def pack_kernel(z, *refs):
    sources, (near, far, proj_t, proj_half) = refs[:10], refs[10:14]
    copies, sem = refs[14:24], refs[24]
    fetch(sources, copies, sem)
    qkv, proj, up_b, qv_b = copies[:4]
    vectors = copies[4:]
    c = lax.axis_index("ctx")
    whole = lanes([read(qkv.at[i]) for i in range(3)])
    near[: z.part, :] = whole.astype(LOW)
    far[: z.chunk, :] = jnp.where(c == 0, whole[: z.chunk], whole[z.chunk :]).astype(LOW)
    row = lax.broadcasted_iota(jnp.int32, (EXTRA, z.shard), 0)
    vec = jnp.zeros((EXTRA, z.shard), F32)
    for i, v in enumerate(vectors):
        vec = jnp.where(row == i, read(v).reshape(1, z.shard), vec)
    biases = read(qv_b)
    biases = rows_of([biases[h, i : i + 1] for h in range(z.heads) for i in range(2)])
    for out, at in ((near, z.part), (far, z.chunk)):
        out[at:, :] = jnp.zeros((EXTRA, 3 * z.inner), LOW)
        out[at:, : z.shard] = vec.astype(LOW)
        out[at : at + up_b.shape[0], UP_AT : UP_AT + up_b.shape[1]] = up_b[...]
        out[at : at + 2 * z.heads, QV_AT : QV_AT + biases.shape[1]] = biases.astype(LOW)
    turned = read(proj).T
    proj_t[...] = turned.astype(LOW)
    proj_half[...] = jnp.where(c == 0, turned[: z.chunk], turned[z.chunk :]).astype(LOW)


def pair_kernel(first, second, out):
    out[0] = first[...]
    out[1] = second[...]


def pack_rest_kernel(z, feed, proj_t, near_in, near_their, far_in, far_their, near, far, scratch):
    c, t = lax.axis_index("ctx"), lax.axis_index("tp")
    scratch[t] = read(proj_t)
    scratch[t ^ (1 + c)] = read(near_in)
    scratch[t ^ (2 - c)] = read(near_their)
    scratch[t ^ 3, z.half_of(c), :] = read(far_in)
    scratch[t ^ 3, z.half_of(1 - c), :] = read(far_their)
    near[...] = lanes([scratch[i] for i in range(4)]).astype(LOW)
    far[:, : 2 * z.ff] = feed[z.half_of(c), :]
    far[:, 2 * z.ff :] = near[z.half_of(c), :]


def own_frame(z, keep, received):
    c = lax.axis_index("ctx")
    zero = jnp.zeros((z.pad, z.width), F32)
    pieces = []
    for ref in (keep, received):
        pieces.append(jnp.where(c == 0, ref[:, 0, :].astype(F32), ref[:, 1, :].astype(F32)))
        pieces.append(zero)
    return rows_of(pieces)


def frame_kernel(z, keep, received, stream, normal, inverse):
    values = own_frame(z, keep, received)
    stream[...] = values.astype(LOW)
    n, i = normalise(values)
    normal[...] = n
    inverse[...] = jnp.broadcast_to(i, inverse.shape)


def cot_kernel(z, keep, received, stream):
    stream[...] = own_frame(z, keep, received).astype(LOW)


def attend_kernel(z, *refs):
    refs = list(refs)
    if z.direct:
        own, near, near_their, far, far_their = refs[:5]
        refs = refs[5:]
    else:
        whole, vec_in, up_in, qv_in = refs[:4]
        refs = refs[4:]
    normal, small, w_out, normed_out, act, attended, soft_out = refs[:7]
    if z.direct:
        c, b = lax.axis_index("ctx"), lax.axis_index("fsdp")
        gather = refs[7]
        for ref, at in ((own, b), (near, b ^ (1 + c)), (near_their, b ^ (2 - c))):
            w_out[at] = ref[: z.part, :]
            gather[at] = ref[z.part :, :].astype(F32)
        w_out[b ^ 3, z.half_of(c), :] = far[: z.chunk, :]
        w_out[b ^ 3, z.half_of(1 - c), :] = far_their[: z.chunk, :]
        gather[b ^ 3] = far[z.chunk :, :].astype(F32)
        blocks = [gather[i] for i in range(4)]
        w = HD // 4
        vec = lanes([g[:8, : z.shard] for g in blocks])
        up = lanes([g[: z.ff // HD, UP_AT : UP_AT + w] for g in blocks])
        qv = lanes([g[: 2 * z.heads, QV_AT : QV_AT + w] for g in blocks])
    else:
        w_out[...] = whole[...]
        vec, up, qv = vec_in[...], up_in[...], qv_in[...]
    up_row = lanes([up[i : i + 1] for i in range(z.ff // HD)])
    query_b = lanes([qv[2 * h : 2 * h + 1] for h in range(z.heads)])
    value_b = lanes([qv[2 * h + 1 : 2 * h + 2] for h in range(z.heads)])
    small[...] = vec
    small[6:7, : z.ff] = up_row
    normed = (normal[...] * vec[0:1] + vec[1:2]).astype(LOW)
    normed_out[...] = normed
    projected = dot(normed, w_out[...].reshape(z.width, 3 * z.inner), NN)
    n = z.inner
    query = ((projected[:, :n] + query_b) * QUERY_SCALE).astype(LOW)
    key = projected[:, n : 2 * n].astype(LOW)
    value = (projected[:, 2 * n :] + value_b).astype(LOW)
    act[0] = query
    act[1] = key
    act[2] = value
    place = lax.broadcasted_iota(jnp.int32, (z.rows, z.rows), 1)
    valid = (place < z.half) | ((place >= z.padded) & (place < z.padded + z.half))
    done = []
    for h in range(z.heads):
        cut = slice(h * HD, (h + 1) * HD)
        scores = jnp.where(valid, dot(query[:, cut], key[:, cut], NT), -1e30)
        exponent = jnp.exp(scores - jnp.max(scores, axis=-1, keepdims=True))
        soft = exponent * (1.0 / jnp.sum(exponent, axis=-1, keepdims=True))
        soft_out[h] = soft
        done.append(dot(soft.astype(LOW), value[:, cut], NN))
    attended[...] = z.squeeze(lanes(done)).astype(LOW)


def feed_kernel(z, *refs):
    refs = list(refs)
    if z.direct:
        feed, feed_in, feed_their, near, near_in, near_their, far, far_their = refs[:8]
        refs = refs[8:]
    else:
        whole = refs[0]
        refs = refs[1:]
    att = refs[: z.nt]
    stream, cot, small = refs[z.nt : z.nt + 3]
    (w_out, att_out, middle_out, hidden_out, normed_out, pre_out, part_out, low_out, own_att, small_out) = refs[
        z.nt + 3 : z.nt + 13
    ]
    sends, heads = refs[z.nt + 13 : -1], refs[-1]
    t = lax.axis_index("tp")
    if z.direct:
        c, b = lax.axis_index("ctx"), lax.axis_index("fsdp")
        mine, other = z.half_of(c), z.half_of(1 - c)
        first, last = pl.ds(0, 2 * z.ff), pl.ds(2 * z.ff, z.nt * z.inner)
        for at, rest, proj in ((b, feed, near), (b ^ (1 + c), feed_in, near_in), (b ^ (2 - c), feed_their, near_their)):
            w_out[at, :, first] = rest[...]
            w_out[at, :, last] = proj[...]
        w_out[b ^ 3, mine, :] = far[...]
        w_out[b ^ 3, other, :] = far_their[...]
    else:
        w_out[...] = whole[...]
    n = z.inner
    w_up = w_out[:, :, : z.ff].reshape(z.width, z.ff)
    w_down_t = w_out[:, :, z.ff : 2 * z.ff].reshape(z.width, z.ff)
    w_proj_t = w_out[:, :, 2 * z.ff :].reshape(z.width, z.nt * n)
    grad_out_low = cot[...]
    grad_out = grad_out_low.astype(F32)
    for k in range(z.nt):
        heads[t ^ k] = z.spread(read(att[k]))
    attended = lanes([heads[i] for i in range(z.nt)]).astype(LOW)
    att_out[...] = attended
    branch = dot(attended, w_proj_t, NT)
    middle = stream[...].astype(F32) + branch + small[2:3]
    middle_out[...] = middle
    normal, inverse = normalise(middle)
    gain = small[3:4]
    normed = (normal * gain + small[4:5]).astype(LOW)
    normed_out[...] = normed
    hidden, slope = gelu_and_slope(dot(normed, w_up, NN) + small[6:7, : z.ff])
    hidden_out[...] = hidden.astype(LOW)
    grad_pre = (dot(grad_out_low, w_down_t, NN) * slope).astype(LOW)
    pre_out[...] = grad_pre
    grad_normed = dot(grad_pre, w_up, NT)
    part = grad_out * (1.0 / z.nt) + norm_backward(grad_normed, normal, inverse, gain)
    part_out[...] = part
    low = part.astype(LOW)
    low_out[...] = low
    grad_att = dot(low, w_proj_t, NN)
    for i in range(z.nt):
        heads[i] = grad_att[:, i * n : (i + 1) * n]
    own_att[...] = heads[t]
    for k in range(1, z.nt):
        sends[k - 1][...] = z.squeeze(heads[t ^ k]).astype(LOW)
    small_out[...] = jnp.zeros(small_out.shape, F32)
    small_out[2:3] = total_rows(part)
    small_out[3:4] = total_rows(grad_normed * normal)
    small_out[4:5] = total_rows(grad_normed)
    small_out[5:6] = total_rows(grad_out) * (1.0 / z.nt)
    small_out[6:7, : z.ff] = total_rows(grad_pre.astype(F32))


def down_kernel(z, hidden, w, kept, sent, scratch):
    h = lax.axis_index("tp") & 1
    w_down_t = w[:, :, z.ff : 2 * z.ff].reshape(z.width, z.ff)
    scratch[...] = dot(hidden[...], w_down_t, NT)
    kept[...] = scratch[z.half_rows(h), :]
    sent[...] = scratch[z.half_rows(1 - h), :].astype(LOW)


def add_low_kernel(kept, received, out):
    rows = kept.shape[0]
    out[:rows, :] = (kept[...] + read(received)).astype(LOW)
    if out.shape[0] > rows:
        out[rows:, :] = jnp.zeros((out.shape[0] - rows, out.shape[1]), LOW)


def store_halves(z, value, at, keep, sent, sent_at=None):
    cols = pl.ds(at, value.shape[1])
    sent_cols = pl.ds(at if sent_at is None else sent_at, value.shape[1])
    c = lax.axis_index("ctx") if z.direct else 0
    b = lax.axis_index("fsdp") if z.direct else 0
    for j in range(4):
        first = value[j * z.part : j * z.part + z.chunk]
        second = value[j * z.part + z.chunk : (j + 1) * z.part]
        if z.direct:
            keep[j ^ b, :, cols] = jnp.where(c == 0, first, second)
            rows = pl.ds(pl.multiple_of((j ^ b) * z.chunk, 16), z.chunk)
            sent[rows, sent_cols] = jnp.where(c == 0, second, first).astype(LOW)
        else:
            keep[j, :, cols] = first
            sent[pl.ds(j * z.chunk, z.chunk), sent_cols] = second.astype(LOW)


def feed_grad_kernel(z, normed, pre, cot, hidden, keep, sent):
    store_halves(z, dot(normed[...], pre[...], TN), 0, keep, sent)
    store_halves(z, dot(cot[...], hidden[...], TN), z.ff, keep, sent)


def qkv_grad_kernel(z, feed_sent, normed, grads, keep, sent):
    sent[:, : 2 * z.ff] = feed_sent[...]
    sent[:, 2 * z.ff + 3 * z.inner :] = jnp.zeros((sent.shape[0], z.all_cols - 2 * z.ff - 3 * z.inner), LOW)
    store_halves(z, dot(normed[...], grads[...], TN), 0, keep, sent, 2 * z.ff)


def proj_grad_kernel(z, low, att, keep, sent=None):
    value = dot(low[...], att[...], TN)
    b = lax.axis_index("fsdp") if z.direct else 0
    for j in range(4):
        keep[j ^ b] = value[j * z.part : (j + 1) * z.part]
    if z.direct:
        c = lax.axis_index("ctx")
        sent[: z.part, :] = keep[2 - c].astype(LOW)
        sent[z.part :, :] = keep[3, z.half_of(1 - c), :].astype(LOW)


def split_kernel(z, keep, keep_qkv, received, out, kept):
    c = lax.axis_index("ctx")
    for target, at, kind in ((out, (1 + c, 3), LOW), (kept, (0, 2 - c), F32)):
        for i in range(2):
            rows = pl.ds(pl.multiple_of(at[i] * z.chunk, 16), z.chunk)
            total = keep[at[i]] + received[rows, : 2 * z.ff].astype(F32)
            target[i, :, : 2 * z.ff] = total.astype(kind)
            last = pl.ds(2 * z.ff, 3 * z.inner)
            total = keep_qkv[at[i]] + received[rows, last].astype(F32)
            target[i, :, last] = total.astype(kind)
            target[i, :, 2 * z.ff + 3 * z.inner :] = jnp.zeros((z.chunk, z.all_cols - 2 * z.ff - 3 * z.inner), kind)


def proj_one_kernel(z, keep, received, near, far):
    c = lax.axis_index("ctx")
    near[...] = (keep[1 + c] + received[: z.part, :].astype(F32)).astype(LOW)
    far[...] = (keep[3, z.half_of(c), :] + received[z.part :, :].astype(F32)).astype(LOW)


def by_half(mine, other):
    c = lax.axis_index("ctx")
    return rows_of([jnp.where(c == 0, mine, other), jnp.where(c == 0, other, mine)])


def feed_final_kernel(z, own, theirs, up, down):
    total = by_half(own[...], read(theirs))
    up[...] = total[:, : z.ff]
    down[...] = total[:, z.ff :]


def unfold(z, v):
    return rows_of([v[:, i * z.inner : (i + 1) * z.inner] for i in range(4)])


def fold(v):
    n = v.shape[0] // 4
    return lanes([v[i * n : (i + 1) * n] for i in range(4)])


def back_kernel(z, *refs):
    own_att, got = refs[0], refs[1 : z.nt]
    act, soft, w, normal, inverse, part, small, small_in = refs[z.nt : z.nt + 8]
    grads_out, qv_out, kept, sent, scratch = refs[z.nt + 8 :]
    t = lax.axis_index("tp")
    grad_att = (own_att[...] + z.spread(sum(read(g) for g in got))).astype(LOW)
    parts = [[], [], []]
    query, key, value = act[0], act[1], act[2]
    for h in range(z.heads):
        cut = slice(h * HD, (h + 1) * HD)
        ga = grad_att[:, cut]
        p = soft[h]
        grad_soft = dot(ga, value[:, cut], NT)
        delta = jnp.sum(p * grad_soft, axis=-1, keepdims=True)
        grad_scores = (p * (grad_soft - delta)).astype(LOW)
        parts[0].append((dot(grad_scores, key[:, cut], NN).astype(LOW).astype(F32) * QUERY_SCALE).astype(LOW))
        parts[1].append(dot(grad_scores, query[:, cut], TN).astype(LOW))
        parts[2].append(dot(p.astype(LOW), ga, TN).astype(LOW))
    grads = lanes(parts[0] + parts[1] + parts[2])
    grads_out[...] = grads
    n = z.inner
    qv_out[...] = total_rows(grads.astype(F32))
    grad_normed = dot(grads, w[...].reshape(z.width, 3 * n), NT)
    scratch[...] = part[...] + norm_backward(grad_normed, normal[...], inverse[:, :1], small[0:1])
    row = lax.broadcasted_iota(jnp.int32, (8, z.width), 0)
    vec = small_in[...]
    vec = jnp.where(row == 0, total_rows(grad_normed * normal[...]), vec)
    vec = jnp.where(row == 1, total_rows(grad_normed), vec)
    h = t & 1
    kept[: z.padded, :] = scratch[z.half_rows(h), :]
    kept[z.padded :, :] = vec
    sent[: z.padded, :] = scratch[z.half_rows(1 - h), :].astype(LOW)
    sent[z.padded :, :] = vec.astype(LOW)


def out_total_kernel(z, own, received, middle, small, out):
    rows = z.half_rows(lax.axis_index("tp") & 1)
    total = (read(own) + read(received))[: z.padded]
    out[...] = (middle[rows, :] + total + small[5:6]).astype(LOW)


def proj_two_kernel(z, keep, near, far, out, kept, scratch):
    c, t = lax.axis_index("ctx"), lax.axis_index("tp")
    other = read(far)
    zero = jnp.zeros(other.shape, F32)
    proj = keep[0] + read(near) + rows_of([jnp.where(c == 0, other, zero), jnp.where(c == 0, zero, other)])
    for i in range(z.nt):
        scratch[i] = fold(proj[:, i * z.inner : (i + 1) * z.inner])
    kept[0] = scratch[t]
    kept[1] = scratch[t ^ 2]
    out[...] = rows_of([scratch[t ^ 1], scratch[t ^ 3]]).astype(LOW)


def sum_rows_kernel(z, own, received, small, qv, out, vec):
    total = read(own) + read(received)
    out[...] = total[: z.padded].astype(LOW)
    vec[:8, :] = total[z.padded :]
    vec[8:, :] = jnp.zeros((8, z.width), F32)
    vec[8:9, : z.ff] = small[6:7, : z.ff]
    vec[9:10, : 3 * z.inner] = qv[...]


def proj_pair_kernel(z, kept, received, own, sent):
    arrived = read(received)
    own[...] = kept[0] + arrived[: z.tail]
    sent[...] = (kept[1] + arrived[z.tail :]).astype(LOW)


def cross_kernel(kept, received, own, out):
    own[...] = kept[0] + received[0].astype(F32)
    out[...] = (kept[1] + received[1].astype(F32)).astype(LOW)


def small_kernel(z, vec, their, near, far, own, scratch):
    c, b = lax.axis_index("ctx"), lax.axis_index("fsdp")
    vectors = vec[...] + their[...]
    up = rows_of([vectors[8:9, i * HD : (i + 1) * HD] for i in range(z.ff // HD)])
    pieces = []
    for h in range(z.heads):
        pieces.append(vectors[9:10, h * HD : (h + 1) * HD])
        pieces.append(vectors[9:10, 2 * z.inner + h * HD : 2 * z.inner + (h + 1) * HD])
    qv_rows = rows_of(pieces)
    scratch[...] = jnp.zeros(scratch.shape, F32)
    w = HD // 4
    for i in range(4):
        scratch[i, :8, : z.shard] = vectors[:8, i * z.shard : (i + 1) * z.shard]
        scratch[i, : z.ff // HD, UP_AT : UP_AT + w] = up[:, i * w : (i + 1) * w]
        scratch[i, : 2 * z.heads, QV_AT : QV_AT + w] = qv_rows[:, i * w : (i + 1) * w]
    once = jnp.where(c == 0, 1.0, 0.0)
    near[...] = scratch[b ^ (1 + c)].astype(LOW)
    far[...] = (scratch[b ^ 3] * once).astype(LOW)
    own[...] = scratch[b] * once


def halves_of(z, own, received):
    h = lax.axis_index("tp") & 1
    return jnp.where(h == 0, own, received), jnp.where(h == 0, received, own)


def swap_kernel(z, out_own, out_in, in_own, in_in, *refs):
    out_mine, out_theirs = halves_of(z, read(out_own), read(out_in))
    in_mine, in_theirs = halves_of(z, read(in_own), read(in_in))
    theirs = [out_theirs, in_theirs]
    if z.direct:
        proj_own, proj_in, mine, sent, proj = refs
        total = proj_own[...] + read(proj_in)
        proj[...] = total
        theirs.append(total)
    else:
        mine, sent = refs
    mine[0] = out_mine
    mine[1] = in_mine
    sent[...] = rows_of(theirs).astype(LOW)


def last_kernel(z, own, cross, small, near, far, feed_total, feed_sent, qkv_total, qkv_sent):
    value = own[...] + read(cross)
    feed_total[...] = value[:, : 2 * z.ff]
    feed_sent[...] = value[:, : 2 * z.ff].astype(LOW)
    tail = small[...] + read(near) + read(far)
    for out, kind in ((qkv_total, F32), (qkv_sent, LOW)):
        out[: z.chunk, :] = value[:, 2 * z.ff : 2 * z.ff + 3 * z.inner].astype(kind)
        out[z.chunk :, :] = tail.astype(kind)


def qkv_final_kernel(z, own, theirs, qkv, up, qv, *vectors):
    both = by_half(own[: z.chunk, :], theirs[: z.chunk, :].astype(F32))
    for i in range(3):
        qkv[i] = both[:, i * z.inner : (i + 1) * z.inner]
    tail = own[z.chunk :, :] + theirs[z.chunk :, :].astype(F32)
    w = HD // 4
    up[...] = tail[: z.ff // HD, UP_AT : UP_AT + w]
    for h in range(z.heads):
        qv[h] = tail[2 * h : 2 * h + 2, QV_AT : QV_AT + w]
    for i, v in enumerate(vectors):
        v[...] = tail[i : i + 1, : z.shard].reshape(z.shard)


def place_kernel(z, mine, theirs, out, *scratch):
    c = lax.axis_index("ctx")
    target = scratch[0] if scratch else out
    mine, theirs = mine[: z.half], theirs[: z.half]
    target[:, 0, :] = jnp.where(c == 0, mine, theirs)
    target[:, 1, :] = jnp.where(c == 0, theirs, mine)
    if scratch:
        out[...] = target[...].astype(out.dtype)


def final_kernel(z, mine, theirs, *refs):
    if z.direct:
        proj_own, feed_own, feed_in, qkv_own, qkv_in, output, input_grad, proj, up, down, *rest = refs
        total = proj_own[...] + theirs[2 * z.padded :, :].astype(F32)
        proj[...] = unfold(z, total).T
        feed_final_kernel(z, feed_own, feed_in, up, down)
        qkv_final_kernel(z, qkv_own, qkv_in, *rest[:-1])
        scratch = rest[-1]
    else:
        output, input_grad, scratch = refs
    place_kernel(z, mine[1], theirs[z.padded : 2 * z.padded, :].astype(F32), input_grad)
    place_kernel(z, mine[0], theirs[: z.padded, :].astype(F32), output, scratch)


def build(nf, nc, nt):
    def local(
        inputs,
        norm1_gain,
        norm1_bias,
        qkv_weight,
        qv_bias,
        proj_weight,
        proj_bias,
        norm2_gain,
        norm2_bias,
        fc1_weight,
        fc1_bias,
        fc2_weight,
        fc2_bias,
        cotangent,
    ):
        z = Sizes(nf, nt, inputs, qv_bias, fc1_weight)
        part = functools.partial
        rows, width, inner, ff, chunk = z.rows, z.width, z.inner, z.ff, z.chunk
        f = lax.axis_index("fsdp")
        tie = lax.optimization_barrier

        def other_core(value):
            return lax.ppermute(value, "ctx", [(0, 1), (1, 0)])

        def to_tp(value, k):
            return lax.ppermute(value, "tp", [(i, i ^ k) for i in range(nt)])

        def to_far(value):
            return lax.ppermute(value, "fsdp", [(i, i ^ 3) for i in range(nf)])

        def neighbours(value, order):
            pairs = [(2 * i + c, 2 * (i ^ order[c]) + c) for i in range(nf) for c in range(2)]
            return lax.ppermute(value, ("fsdp", "ctx"), pairs)

        def to_near(value):
            return neighbours(value, (1, 2))

        def to_cross(value):
            return neighbours(value, (2, 1))

        def proj_near(value):
            pairs = [(c * nt + i, c * nt + (i ^ (1 + c))) for i in range(nt) for c in range(2)]
            return lax.ppermute(value, ("ctx", "tp"), pairs)

        def pair_of(first, second):
            return call(pair_kernel, [shape((2,) + first.shape, LOW)], [first, second], name="pair")[0]

        qkv3 = qkv_weight.transpose(1, 0, 2)
        down_t = fc2_weight.T
        qv3 = qv_bias.transpose(1, 0, 2)
        x_raw, cot_raw = inputs.transpose(1, 0, 2), cotangent.transpose(1, 0, 2)
        vectors = [norm1_gain, norm1_bias, proj_bias, norm2_gain, norm2_bias, fc2_bias]

        x_recv = other_core(x_raw)
        cot_recv = other_core(cot_raw)
        def frames(x_recv, cot_recv):
            stream, normal_one, inverse_one = call(
                part(frame_kernel, z),
                [shape((rows, width), LOW), shape((rows, width), F32), shape((rows, 128), F32)],
                [x_raw, x_recv],
                name="frame",
            )
            (cot,) = call(part(cot_kernel, z), [shape((rows, width), LOW)], [cot_raw, cot_recv], name="cotangent")
            return stream, normal_one, inverse_one, cot

        if z.direct:
            sources = [qkv3, proj_weight, fc1_bias, qv3] + vectors
            near, far, proj_t, proj_half = call(
                part(pack_kernel, z),
                [
                    shape((z.part + EXTRA, 3 * inner), LOW),
                    shape((chunk + EXTRA, 3 * inner), LOW),
                    shape((z.part, inner), LOW),
                    shape((chunk, inner), LOW),
                ],
                sources,
                [pltpu.VMEM(s.shape, s.dtype) for s in sources] + [pltpu.SemaphoreType.DMA((len(sources),))],
                name="pack",
                mib=56,
                in_specs=[ANY] * len(sources),
            )
            near, far, proj_t, proj_half, x_recv, cot_recv = tie((near, far, proj_t, proj_half, x_recv, cot_recv))
            got = [to_near(near), to_far(far)]
            proj_got = [proj_near(proj_t), to_tp(proj_half, 3)]
            (feed_own,) = call(
                part(stage_kernel, z),
                [shape((z.part, 2 * ff), LOW)],
                [fc1_weight, down_t],
                [pltpu.VMEM((z.part, ff), LOW)] * 2 + [pltpu.SemaphoreType.DMA((2,))],
                name="stage",
                mib=56,
                in_specs=[ANY] * 2,
            )
            stream, normal_one, inverse_one, cot = frames(x_recv, cot_recv)
            got, proj_got, feed_own, stream, normal_one, inverse_one, cot = tie(
                (got, proj_got, feed_own, stream, normal_one, inverse_one, cot)
            )
            feed_in = to_near(feed_own)
            shared = [other_core(g) for g in got]
            qkv_in = [near, got[0], shared[0], got[1], shared[1]]
            rest_near, rest_far = call(
                part(pack_rest_kernel, z),
                [shape((z.part, nt * inner), LOW), shape((chunk, z.cols), LOW)],
                [feed_own, proj_t, proj_got[0], other_core(proj_got[0]), proj_got[1], other_core(proj_got[1])],
                [pltpu.VMEM((nt, z.part, inner), F32)],
                name="pack_rest",
            )
            near_in, far_in = to_near(rest_near), to_far(rest_far)
        else:
            stream, normal_one, inverse_one, cot = frames(x_recv, cot_recv)
            whole = lax.all_gather(qkv3, "fsdp", axis=1, tiled=True)
            whole = whole.transpose(1, 0, 2).reshape(4, z.part, 3 * inner)
            vec = jnp.stack(vectors + [vectors[0]] * 2).astype(F32)
            qv_rows = qv3.reshape(2 * z.heads, -1).astype(F32)
            gathered = [lax.all_gather(v, "fsdp", axis=1, tiled=True) for v in (vec, fc1_bias.astype(F32), qv_rows)]
            qkv_in = [whole] + gathered
            proj_t = proj_weight.T
            rest = jnp.concatenate([fc1_weight, down_t, lax.all_gather(proj_t, "tp", axis=1, tiled=True)], 1)
            rest_in = [lax.all_gather(rest, "fsdp", axis=0, tiled=True).reshape(4, z.part, z.cols)]

        small, w_qkv, normed_one, act, attended, soft = call(
            part(attend_kernel, z),
            [
                shape((8, width), F32),
                shape((4, z.part, 3 * inner), LOW),
                shape((rows, width), LOW),
                shape((3, rows, inner), LOW),
                shape((z.dense, 128), LOW),
                shape((z.heads, rows, rows), F32),
            ],
            qkv_in + [normal_one],
            [pltpu.VMEM((4, EXTRA, 3 * inner), F32)] if z.direct else [],
            name="attend",
        )
        att = [to_tp(attended, k) for k in range(1, nt)]
        if z.direct:
            att, near_in, far_in = tie((att, near_in, far_in))
            rest_in = [feed_own, feed_in, other_core(feed_in), rest_near, near_in, other_core(near_in)]
            rest_in += [far_in, other_core(far_in)]

        (w_rest, att_all, middle, hidden, normed_two, grad_pre, part_middle, part_low, own_att, small_two, *att_sends) = (
            call(
                part(feed_kernel, z),
                [
                    shape((4, z.part, z.cols), LOW),
                    shape((rows, nt * inner), LOW),
                    shape((rows, width), F32),
                    shape((rows, ff), LOW),
                    shape((rows, width), LOW),
                    shape((rows, ff), LOW),
                    shape((rows, width), F32),
                    shape((rows, width), LOW),
                    shape((rows, inner), F32),
                    shape((8, width), F32),
                ]
                + [shape((z.dense, 128), LOW)] * (nt - 1),
                rest_in + [attended] + att + [stream, cot, small],
                [pltpu.VMEM((nt, rows, inner), F32)],
                name="feed",
            )
        )
        att_got = [to_tp(att_sends[k - 1], k) for k in range(1, nt)]
        all_cols = z.all_cols
        keep, sent = call(
            part(feed_grad_kernel, z),
            [shape((4, chunk, 2 * ff), F32), shape((4 * chunk, 2 * ff), LOW)],
            [normed_two, grad_pre, cot, hidden],
            name="feed_grad",
        )
        keep_proj, *sent_proj = call(
            part(proj_grad_kernel, z),
            [shape((4, z.part, nt * inner), F32)]
            + ([shape((z.part + chunk, nt * inner), LOW)] if z.direct else []),
            [part_low, att_all],
            name="proj_grad",
        )
        out_kept, out_sent = call(
            part(down_kernel, z),
            [shape((z.padded, width), F32), shape((z.padded, width), LOW)],
            [hidden, w_rest],
            [pltpu.VMEM((rows, width), F32)],
            name="down",
        )
        out_one = to_tp(out_sent, 1)
        if z.direct:
            proj_in = other_core(sent_proj[0])
            att_got, out_one, keep, sent, proj_in = tie((att_got, out_one, keep, sent, proj_in))
            near, far = call(
                part(proj_one_kernel, z),
                [shape((z.part, nt * inner), LOW), shape((chunk, nt * inner), LOW)],
                [keep_proj, proj_in],
                name="proj_one",
            )
            proj_in = [to_near(near), to_far(far)]
        (out_low,) = call(add_low_kernel, [shape((z.padded + 16, width), LOW)], [out_kept, out_one], name="out_pair")
        out_two = to_tp(out_low, 2)

        grads, qv_sum, in_kept, in_sent = call(
            part(back_kernel, z),
            [
                shape((rows, 3 * inner), LOW),
                shape((1, 3 * inner), F32),
                shape((z.padded + 8, width), F32),
                shape((z.padded + 8, width), LOW),
            ],
            [own_att] + att_got + [act, soft, w_qkv, normal_one, inverse_one, part_middle, small, small_two],
            [pltpu.VMEM((rows, width), F32)],
            name="back",
        )
        in_one = to_tp(in_sent, 1)
        keep_qkv, sent = call(
            part(qkv_grad_kernel, z),
            [shape((4, chunk, 3 * inner), F32), shape((4 * chunk, all_cols), LOW)],
            [sent, normed_one, grads],
            name="qkv_grad",
        )
        if z.direct:
            sent = other_core(sent)
            in_one, out_two, proj_in, sent = tie((in_one, out_two, proj_in, sent))
            grad_sent, grad_kept = call(
                part(split_kernel, z),
                [shape((2, chunk, all_cols), LOW), shape((2, chunk, all_cols), F32)],
                [keep, keep_qkv, sent],
                name="split",
            )
            grad_in = to_near(grad_sent)
        (in_low,) = call(add_low_kernel, [shape((z.padded + 8, width), LOW)], [in_kept, in_one], name="in_pair")
        in_two = to_tp(in_low, 2)
        (out_low,) = call(
            part(out_total_kernel, z),
            [shape((z.padded, width), LOW)],
            [out_low, out_two, middle, small],
            name="out_total",
        )
        out_in = to_tp(out_low, 1)
        if z.direct:
            proj_sent, proj_kept = call(
                part(proj_two_kernel, z),
                [shape((2 * z.tail, width), LOW), shape((2, z.tail, width), F32)],
                [keep_proj] + proj_in,
                [pltpu.VMEM((nt, z.tail, width), F32)],
                name="proj_two",
            )
            proj_in = to_tp(proj_sent, 1)
        if z.direct:
            in_two, out_in, grad_in, proj_in = tie((in_two, out_in, grad_in, proj_in))
        in_low, vec = call(
            part(sum_rows_kernel, z),
            [shape((z.padded, width), LOW), shape((16, width), F32)],
            [in_low, in_two, small_two, qv_sum],
            name="sum_rows",
        )
        in_in = to_tp(in_low, 1)
        proj_all = []
        if z.direct:
            grad_own, cross = call(
                cross_kernel,
                [shape((chunk, all_cols), F32), shape((chunk, all_cols), LOW)],
                [grad_kept, grad_in],
                name="cross",
            )
            cross = to_cross(cross)
            proj_own, proj_sent = call(
                part(proj_pair_kernel, z),
                [shape((z.tail, width), F32), shape((z.tail, width), LOW)],
                [proj_kept, proj_in],
                name="proj_pair",
            )
            proj_two = to_tp(proj_sent, 2)
            near, far, small_own = call(
                part(small_kernel, z),
                [shape((EXTRA, 3 * inner), LOW)] * 2 + [shape((EXTRA, 3 * inner), F32)],
                [vec, other_core(vec)],
                [pltpu.VMEM((4, EXTRA, 3 * inner), F32)],
                name="small",
            )
            near, far = to_near(near), to_far(far)
            in_in, proj_two, cross, near, far = tie((in_in, proj_two, cross, near, far))
            proj_all = [proj_own, proj_two]
            feed_own, feed_sent, qkv_own, qkv_sent = call(
                part(last_kernel, z),
                [
                    shape((chunk, 2 * ff), F32),
                    shape((chunk, 2 * ff), LOW),
                    shape((chunk + EXTRA, 3 * inner), F32),
                    shape((chunk + EXTRA, 3 * inner), LOW),
                ],
                [grad_own, cross, small_own, near, far],
                name="last",
            )
            feed_in, qkv_in = other_core(feed_sent), other_core(qkv_sent)
        mine, theirs, *proj_own = call(
            part(swap_kernel, z),
            [shape((2, z.padded, width), F32), shape((rows + (z.tail if proj_all else 0), width), LOW)]
            + ([shape((z.tail, width), F32)] if proj_all else []),
            [out_low, out_in, in_low, in_in] + proj_all,
            name="swap",
        )
        theirs = other_core(theirs)
        results = [shape((z.half, 2, width), LOW), shape((z.half, 2, width), F32)]
        scratch = [pltpu.VMEM((z.half, 2, width), F32)]
        if z.direct:
            output, input_grad, proj_grad, fc1_grad, fc2_grad, qkv_grad, up_grad, qv_grad, *vec_grads = call(
                part(final_kernel, z),
                results
                + [
                    shape((inner, z.shard), F32),
                    shape((z.shard, ff), F32),
                    shape((z.shard, ff), F32),
                    shape((3, z.shard, inner), F32),
                    shape(fc1_bias.shape, F32),
                    shape(qv3.shape, F32),
                ]
                + [shape((z.shard,), F32)] * 6,
                [mine, theirs, proj_own[0], feed_own, feed_in, qkv_own, qkv_in],
                scratch,
                name="final",
            )
        else:
            output, input_grad = call(part(final_kernel, z), results, [mine, theirs], scratch, name="final")

            def joined(keep, sent):
                return jnp.stack([keep.astype(LOW), sent.reshape(keep.shape)], 1).reshape(width, -1)

            def scatter(whole):
                whole = lax.psum(whole, "ctx")
                return lax.psum_scatter(whole, "fsdp", scatter_dimension=0, tiled=True).astype(F32)

            extra = all_cols - 2 * ff - 3 * inner
            total = scatter(joined(jnp.concatenate([keep, jnp.pad(keep_qkv, ((0, 0), (0, 0), (0, extra)))], 2), sent))
            fc1_grad, fc2_grad = total[:, :ff], total[:, ff : 2 * ff]
            qkv_grad = total[:, 2 * ff : 2 * ff + 3 * inner].reshape(z.shard, 3, inner).transpose(1, 0, 2)
            proj_grad = scatter(keep_proj.reshape(width, -1).astype(LOW)).astype(LOW)
            proj_grad = lax.psum_scatter(proj_grad, "tp", scatter_dimension=1, tiled=True).astype(F32).T

            def own_columns(value):
                value = lax.psum(value, ("fsdp", "ctx"))
                return lax.dynamic_slice_in_dim(value, f * (value.shape[1] // nf), value.shape[1] // nf, 1)

            vec_grads = own_columns(vec[:6])
            up_grad = own_columns(vec[8, :ff].reshape(-1, HD))
            qv_grad = vec[9, : 3 * inner].reshape(3, z.heads, HD)[0::2].transpose(1, 0, 2)
            qv_grad = own_columns(qv_grad.reshape(2 * z.heads, HD)).reshape(qv3.shape)
        return (
            output.transpose(1, 0, 2),
            input_grad.transpose(1, 0, 2),
            vec_grads[0],
            vec_grads[1],
            qkv_grad.transpose(1, 0, 2),
            qv_grad.transpose(1, 0, 2),
            proj_grad,
            vec_grads[2],
            vec_grads[3],
            vec_grads[4],
            fc1_grad,
            up_grad,
            fc2_grad.T,
            vec_grads[5],
        )

    return local


def solution(mesh):
    sizes = mesh.shape
    return jax.shard_map(
        build(sizes["fsdp"], sizes["ctx"], sizes["tp"]),
        mesh=mesh,
        in_specs=(
            P("fsdp", "ctx", None),
            P("fsdp"),
            P("fsdp"),
            P("fsdp", None, "tp"),
            P(None, "tp", "fsdp"),
            P("tp", "fsdp"),
            P("fsdp"),
            P("fsdp"),
            P("fsdp"),
            P("fsdp", "tp"),
            P("tp", "fsdp"),
            P("tp", "fsdp"),
            P("fsdp"),
            P("fsdp", "ctx", None),
        ),
        out_specs=(
            P("fsdp", "ctx", None),
            P("fsdp", "ctx", None),
            P("fsdp"),
            P("fsdp"),
            P("fsdp", None, "tp"),
            P(None, "tp", "fsdp"),
            P("tp", "fsdp"),
            P("fsdp"),
            P("fsdp"),
            P("fsdp"),
            P("fsdp", "tp"),
            P("tp", "fsdp"),
            P("tp", "fsdp"),
            P("fsdp"),
        ),
        check_vma=False,
    )
```

time: 114 us -> 105 us (0.921)
  waiting for transfers between devices: 51.3 us -> 42.4 us
  starting transfers between devices: 40.9 us -> 43.1 us
  local copies, waits for them, and re-layouts: 1.78 us -> 0.02 us
    ppermute x15, waiting for transfers between devices: 31.8 us -> 23 us  [to_tp(): return lax.ppermute(value, 'tp', [(i, i ^ k) for i in range(nt)])]
    ppermute x10 -> x7, waiting for transfers between devices: 9.61 us -> 4.49 us  [neighbours(): return lax.ppermute(value, ('fsdp', 'ctx'), pairs)]
    ppermute x10 -> x7, starting transfers between devices: 14.2 us -> 10.8 us  [neighbours(): return lax.ppermute(value, ('fsdp', 'ctx'), pairs)]
    ppermute x15, starting transfers between devices: 19.7 us -> 23.1 us  [to_tp(): return lax.ppermute(value, 'tp', [(i, i ^ k) for i in range(nt)])]
    ppermute x15, waiting for transfers between devices: 3.68 us -> 6.22 us  [other_core(): return lax.ppermute(value, 'ctx', [(0, 1), (1, 0)])]
    ppermute x2 -> x4, waiting for transfers between devices: 6.25 us -> 8.66 us  [to_far(): return lax.ppermute(value, 'fsdp', [(i, i ^ 3) for i in range(nf)])]
    unnamed x12 -> x10, local copies, waits for them, and re-layouts: 1.78 us -> 0.02 us
    ppermute x0 -> x1, starting transfers between devices: none -> 1.58 us  [proj_near(): return lax.ppermute(value, ('ctx', 'tp'), pairs)]
  transfers between devices with their start and end apart: 42 -> 42, of which waited for: 17 -> 17; matrix products, arithmetic and copies ran while one was open for 0% -> 0% of each run, Pallas kernels for 9% -> 8%
where the time goes in v4:
time: 105 us
  starting transfers between devices  43.1 us (41%)
  waiting for transfers between devices  42.4 us (40%)
  Pallas kernels  17.9 us (17%)
  between operations  1.07 us (1%)
    ppermute x15, starting transfers between devices, to_tp(): return lax.ppermute(value, 'tp', [(i, i ^ k) for i in range(nt)])  23.1 us
    ppermute x15, waiting for transfers between devices, to_tp(): return lax.ppermute(value, 'tp', [(i, i ^ k) for i in range(nt)])  23 us
    pallas_call x25, Pallas kernels, call(): pl.pallas_call(kernel, out_shape=tuple(outs), in_specs=in_specs or [VMEM]...  17.9 us
    ppermute x7, starting transfers between devices, neighbours(): return lax.ppermute(value, ('fsdp', 'ctx'), pairs)  10.8 us
    ppermute x4, waiting for transfers between devices, to_far(): return lax.ppermute(value, 'fsdp', [(i, i ^ 3) for i in range(nf)])  8.66 us
    ppermute x15, waiting for transfers between devices, other_core(): return lax.ppermute(value, 'ctx', [(0, 1), (1, 0)])  6.22 us
    ppermute x7, waiting for transfers between devices, neighbours(): return lax.ppermute(value, ('fsdp', 'ctx'), pairs)  4.49 us
    ppermute x4, starting transfers between devices, to_far(): return lax.ppermute(value, 'fsdp', [(i, i ^ 3) for i in range(nf)])  4.46 us
  transfers between devices with their start and end apart: 42, of which 17 were waited for; matrix products, arithmetic and copies ran while one was open for 0% of the time, Pallas kernels for 8%

profile of v4, /device:TPU:0, one launch (start us, length us, event | category | flops | bytes accessed | tf_op | source)
XLA Modules:
  0.0 104.6 jit_solution(7693283016492181996)
XLA Ops:
  0.7 0.5 collective-permute-start
  1.3 2.0 %pack.1 = (bf16[208,576]{1,0:T(8,128)(2,1)}, bf16[112,576]{1,0:T(8,128)(2,1)}, bf16[192,192]{1,0:T(8,128)(2,1)}, bf16[96,192]{1,0:T(8,128)(2,1)}) custom-call(bf16[3,192,192]{2,1,0:T(8,128)(2,1)} %bitcast.14, bf16[192,192]{1,0:T(8,128)(2,1)} %refs_1_.1, bf16[12,16]{1,0:T(8,128)(2,1)} %refs_2_.1, bf16[3,2,16]{2,1,0:T(2,128)(2,1)} %bitcast.16, ...), custom_call_target="tpu_custom_call" | custom-call | tf_op jit(solution)/shard_map/pack/pallas_call | solution.py:33
  3.3 3.0 %collective-permute-start.2 = (bf16[208,576]{1,0:T(8,128)(2,1)}, bf16[208,576]{1,0:T(8,128)(2,1)S(1)}, u32[]{:S(2)}, u32[]{:S(2)}) collective-permute-start(bf16[208,576]{1,0:T(8,128)(2,1)} %get-tuple-element.135.refs_0_), channel_id=1, source_target_pairs={{0,8},{4,20},{8,0},{12,28},{16,24},{20,4},{24,16},{28,12},{1,9},{5... | collective-permute-start | bytes 718856 | tf_op jit(solution)/shard_map/ppermute | solution.py:603
  6.3 1.5 %collective-permute-start.3 = (bf16[112,576]{1,0:T(8,128)(2,1)}, bf16[112,576]{1,0:T(8,128)(2,1)S(1)}, u32[]{:S(2)}, u32[]{:S(2)}) collective-permute-start(bf16[112,576]{1,0:T(8,128)(2,1)} %get-tuple-element.136), channel_id=1, source_target_pairs={{0,24},{8,16},{16,8},{24,0},{1,25},{9,17},{17,9},{25,1},{2,26},{10... | collective-permute-start | bytes 387080 | tf_op jit(solution)/shard_map/ppermute | solution.py:599
  7.8 1.6 %collective-permute-start.4 = (bf16[192,192]{1,0:T(8,128)(2,1)}, bf16[192,192]{1,0:T(8,128)(2,1)S(1)}, u32[]{:S(2)}, u32[]{:S(2)}) collective-permute-start(bf16[192,192]{1,0:T(8,128)(2,1)} %get-tuple-element.137.proj_t), channel_id=1, source_target_pairs={{0,1},{4,6},{1,0},{5,7},{2,3},{6,4},{3,2},{7,5},{8,9},{12,14},{9,8... | collective-permute-start | bytes 221192 | tf_op jit(solution)/shard_map/ppermute | solution.py:613
  9.3 2.5 %collective-permute-start.5 = (bf16[96,192]{1,0:T(8,128)(2,1)}, bf16[96,192]{1,0:T(8,128)(2,1)S(1)}, u32[]{:S(2)}, u32[]{:S(2)}) collective-permute-start(bf16[96,192]{1,0:T(8,128)(2,1)} %get-tuple-element.138), channel_id=1, source_target_pairs={{0,3},{1,2},{2,1},{3,0},{4,7},{5,6},{6,5},{7,4},{8,11},{9,10},{10,... | collective-permute-start | bytes 110600 | tf_op jit(solution)/shard_map/ppermute | solution.py:596
  11.8 2.0 %stage.1.feed.refs_0_ = bf16[192,1536]{1,0:T(8,128)(2,1)} custom-call(bf16[192,768]{1,0:T(8,128)(2,1)} %up.1, bf16[192,768]{1,0:T(8,128)(2,1)} %bitcast.15), custom_call_target="tpu_custom_call" | custom-call | tf_op jit(solution)/shard_map/stage/pallas_call | solution.py:33
  13.8 0.4 cotangent.1.refs_13_.cot
  14.2 0.6 frame.1
  14.8 0.9 collective-permute-done.5.far_in
  15.7 1.3 %collective-permute-start.6 = (bf16[192,1536]{1,0:T(8,128)(2,1)}, bf16[192,1536]{1,0:T(8,128)(2,1)S(1)}, u32[]{:S(2)}, u32[]{:S(2)}) collective-permute-start(bf16[192,1536]{1,0:T(8,128)(2,1)} %stage.1.feed.refs_0_), channel_id=1, source_target_pairs={{0,8},{4,20},{8,0},{12,28},{16,24},{20,4},{24,16},{28,12},{1,9},{5... | collective-permute-start | bytes 1769480 | tf_op jit(solution)/shard_map/ppermute | solution.py:603
  17.0 0.5 collective-permute-start.9
  17.5 0.9 collective-permute-done.9.far_their
  18.4 0.2 pack_rest.1
  18.6 1.2 %collective-permute-start.16 = (bf16[96,2304]{1,0:T(8,128)(2,1)S(1)}, bf16[96,2304]{1,0:T(8,128)(2,1)S(1)}, u32[]{:S(2)}, u32[]{:S(2)}) collective-permute-start(bf16[96,2304]{1,0:T(8,128)(2,1)S(1)} %get-tuple-element.152), channel_id=1, source_target_pairs={{0,24},{8,16},{16,8},{24,0},{1,25},{9,17},{17,9},{25,1},{2,26},{10... | collective-permute-start | bytes 1327112 | tf_op jit(solution)/shard_map/ppermute | solution.py:599
  19.9 1.1 %collective-permute-start.15 = (bf16[192,768]{1,0:T(8,128)(2,1)S(1)}, bf16[192,768]{1,0:T(8,128)(2,1)S(1)}, u32[]{:S(2)}, u32[]{:S(2)}) collective-permute-start(bf16[192,768]{1,0:T(8,128)(2,1)S(1)} %get-tuple-element.147.refs_3_), channel_id=1, source_target_pairs={{0,8},{4,20},{8,0},{12,28},{16,24},{20,4},{24,16},{28,12},{1,9},{5... | collective-permute-start | bytes 884744 | tf_op jit(solution)/shard_map/ppermute | solution.py:603
  21.2 1.2 %collective-permute-done.11.refs_4_ = bf16[112,576]{1,0:T(8,128)(2,1)S(1)} collective-permute-done((bf16[112,576]{1,0:T(8,128)(2,1)S(1)}, bf16[112,576]{1,0:T(8,128)(2,1)S(1)}, u32[]{:S(2)}, u32[]{:S(2)}) %collective-permute-start.11) | collective-permute-done | bytes 129056 | tf_op jit(solution)/shard_map/ppermute | solution.py:593
  22.3 1.3 %attend.1 = (f32[8,768]{1,0:T(8,128)S(1)}, bf16[4,192,576]{2,1,0:T(8,128)(2,1)S(1)}, bf16[208,768]{1,0:T(8,128)(2,1)S(1)}, bf16[3,208,192]{2,1,0:T(8,128)(2,1)S(...) custom-call(bf16[208,576]{1,0:T(8,128)(2,1)S(1)} %copy-done.3, ...), custom_call_target="tpu_custom_call" | custom-call | tf_op jit(solution)/shard_map/attend/pallas_call | solution.py:33
  23.6 3.4 %collective-permute-start.14 = (bf16[312,128]{1,0:T(8,128)(2,1)S(1)}, bf16[312,128]{1,0:T(8,128)(2,1)S(1)}, u32[]{:S(2)}, u32[]{:S(2)}) collective-permute-start(bf16[312,128]{1,0:T(8,128)(2,1)S(1)} %get-tuple-element.151.refs_8_), channel_id=1, source_target_pairs={{0,3},{1,2},{2,1},{3,0},{4,7},{5,6},{6,5},{7,4},{8,11},{9,10},{10,... | collective-permute-start | bytes 239624 | tf_op jit(solution)/shard_map/ppermute | solution.py:596
  27.0 2.8 %collective-permute-done.6.refs_1_ = bf16[192,1536]{1,0:T(8,128)(2,1)S(1)} collective-permute-done((bf16[192,1536]{1,0:T(8,128)(2,1)}, bf16[192,1536]{1,0:T(8,128)(2,1)S(1)}, u32[]{:S(2)}, u32[]{:S(2)}) %collective-permute-start.6) | collective-permute-done | bytes 589856 | tf_op jit(solution)/shard_map/ppermute | solution.py:603
  29.8 2.3 %collective-permute-start.13 = (bf16[312,128]{1,0:T(8,128)(2,1)S(1)}, bf16[312,128]{1,0:T(8,128)(2,1)S(1)}, u32[]{:S(2)}, u32[]{:S(2)}) collective-permute-start(bf16[312,128]{1,0:T(8,128)(2,1)S(1)} %get-tuple-element.151.refs_8_), channel_id=1, source_target_pairs={{0,2},{1,3},{2,0},{3,1},{4,6},{5,7},{6,4},{7,5},{8,10},{9,11},{10,... | collective-permute-start | bytes 239624 | tf_op jit(solution)/shard_map/ppermute | solution.py:596
  32.1 1.6 %collective-permute-start.12 = (bf16[312,128]{1,0:T(8,128)(2,1)S(1)}, bf16[312,128]{1,0:T(8,128)(2,1)S(1)}, u32[]{:S(2)}, u32[]{:S(2)}) collective-permute-start(bf16[312,128]{1,0:T(8,128)(2,1)S(1)} %get-tuple-element.151.refs_8_), channel_id=1, source_target_pairs={{0,1},{1,0},{2,3},{3,2},{4,5},{5,4},{6,7},{7,6},{8,9},{9,8},{10,11... | collective-permute-start | bytes 239624 | tf_op jit(solution)/shard_map/ppermute | solution.py:596
  33.7 3.7 %collective-permute-done.13.refs_10_ = bf16[312,128]{1,0:T(8,128)(2,1)S(1)} collective-permute-done((bf16[312,128]{1,0:T(8,128)(2,1)S(1)}, bf16[312,128]{1,0:T(8,128)(2,1)S(1)}, u32[]{:S(2)}, u32[]{:S(2)}) %collective-permute-start.13) | collective-permute-done | bytes 79904 | tf_op jit(solution)/shard_map/ppermute | solution.py:596
  37.5 1.0 collective-permute-done.15.refs_4_
  38.5 0.5 collective-permute-start.17
  39.0 1.7 %collective-permute-done.17.refs_5_ = bf16[192,768]{1,0:T(8,128)(2,1)S(1)} collective-permute-done((bf16[192,768]{1,0:T(8,128)(2,1)S(1)}, bf16[192,768]{1,0:T(8,128)(2,1)S(1)}, u32[]{:S(2)}, u32[]{:S(2)}) %collective-permute-start.17) | collective-permute-done | bytes 294944 | tf_op jit(solution)/shard_map/ppermute | solution.py:593
  40.8 3.1 %feed.1 = (bf16[4,192,2304]{2,1,0:T(8,128)(2,1)S(1)}, bf16[208,768]{1,0:T(8,128)(2,1)S(1)}, f32[208,768]{1,0:T(8,128)S(1)}, bf16[208,768]{1,0:T(8,128)(2,1)S(1)}...) custom-call(bf16[192,1536]{1,0:T(8,128)(2,1)S(1)} %copy-done, ...), custom_call_target="tpu_custom_call" | custom-call | tf_op jit(solution)/shard_map/feed/pallas_call | solution.py:33
  43.9 0.6 proj_grad.1
  44.5 0.2 collective-permute-start.23
  44.7 0.6 down.1
  45.3 1.3 %collective-permute-start.22 = (bf16[104,768]{1,0:T(8,128)(2,1)S(1)}, bf16[104,768]{1,0:T(8,128)(2,1)S(1)}, u32[]{:S(2)}, u32[]{:S(2)}) collective-permute-start(bf16[104,768]{1,0:T(8,128)(2,1)S(1)} %get-tuple-element.167), channel_id=1, source_target_pairs={{0,1},{1,0},{2,3},{3,2},{4,5},{5,4},{6,7},{7,6},{8,9},{9,8},{10,11... | collective-permute-start | bytes 479240 | tf_op jit(solution)/shard_map/ppermute | solution.py:596
  46.6 0.8 collective-permute-start.19
  47.4 2.3 %collective-permute-start.20 = (bf16[312,128]{1,0:T(8,128)(2,1)S(1)}, bf16[312,128]{1,0:T(8,128)(2,1)S(1)}, u32[]{:S(2)}, u32[]{:S(2)}) collective-permute-start(bf16[312,128]{1,0:T(8,128)(2,1)S(1)} %get-tuple-element.165), channel_id=1, source_target_pairs={{0,2},{1,3},{2,0},{3,1},{4,6},{5,7},{6,4},{7,5},{8,10},{9,11},{10,... | collective-permute-start | bytes 239624 | tf_op jit(solution)/shard_map/ppermute | solution.py:596
  49.7 1.4 %collective-permute-start.21 = (bf16[312,128]{1,0:T(8,128)(2,1)S(1)}, bf16[312,128]{1,0:T(8,128)(2,1)S(1)}, u32[]{:S(2)}, u32[]{:S(2)}) collective-permute-start(bf16[312,128]{1,0:T(8,128)(2,1)S(1)} %get-tuple-element.166), channel_id=1, source_target_pairs={{0,3},{1,2},{2,1},{3,0},{4,7},{5,6},{6,5},{7,4},{8,11},{9,10},{10,... | collective-permute-start | bytes 239624 | tf_op jit(solution)/shard_map/ppermute | solution.py:596
  51.0 0.9 feed_grad.1
  52.0 3.2 %collective-permute-done.19.refs_1_ = bf16[312,128]{1,0:T(8,128)(2,1)S(1)} collective-permute-done((bf16[312,128]{1,0:T(8,128)(2,1)S(1)}, bf16[312,128]{1,0:T(8,128)(2,1)S(1)}, u32[]{:S(2)}, u32[]{:S(2)}) %collective-permute-start.19) | collective-permute-done | bytes 79904 | tf_op jit(solution)/shard_map/ppermute | solution.py:596
  55.2 3.4 %collective-permute-done.21.refs_3_ = bf16[312,128]{1,0:T(8,128)(2,1)S(1)} collective-permute-done((bf16[312,128]{1,0:T(8,128)(2,1)S(1)}, bf16[312,128]{1,0:T(8,128)(2,1)S(1)}, u32[]{:S(2)}, u32[]{:S(2)}) %collective-permute-start.21) | collective-permute-done | bytes 79904 | tf_op jit(solution)/shard_map/ppermute | solution.py:596
  58.6 2.0 %back.1 = (bf16[208,576]{1,0:T(8,128)(2,1)S(1)}, f32[1,576]{1,0:T(1,128)S(1)}, f32[112,768]{1,0:T(8,128)S(1)}, bf16[112,768]{1,0:T(8,128)(2,1)S(1)}) custom-call(f32[208,192]{1,0:T(8,128)S(1)} %get-tuple-element.176.refs_0_, bf16[312,128]{1,0:T(8,128)(2,1)S(1)} %collective-permute-done.19.refs_1_, bf16[312,128]{1,0:T(8,128)(2,1)S(1)} %collective-permute-done.20.refs_2_, ...), custom_call_target="tpu_custom_call" | custom-call | tf_op jit(solution)/shard_map/back/pallas_call | solution.py:33
  60.6 0.6 qkv_grad.1
  61.4 1.6 %collective-permute-start.26 = (bf16[192,768]{1,0:T(8,128)(2,1)S(1)}, bf16[192,768]{1,0:T(8,128)(2,1)S(1)}, u32[]{:S(2)}, u32[]{:S(2)}) collective-permute-start(bf16[192,768]{1,0:T(8,128)(2,1)S(1)} %get-tuple-element.189), channel_id=1, source_target_pairs={{0,8},{4,20},{8,0},{12,28},{16,24},{20,4},{24,16},{28,12},{1,9},{5... | collective-permute-start | bytes 884744 | tf_op jit(solution)/shard_map/ppermute | solution.py:603
  63.1 1.4 %collective-permute-start.25 = (bf16[120,768]{1,0:T(8,128)(2,1)S(1)}, bf16[120,768]{1,0:T(8,128)(2,1)S(1)}, u32[]{:S(2)}, u32[]{:S(2)}) collective-permute-start(bf16[120,768]{1,0:T(8,128)(2,1)S(1)} %out_pair.1.own), channel_id=1, source_target_pairs={{0,2},{1,3},{2,0},{3,1},{4,6},{5,7},{6,4},{7,5},{8,10},{9,11},{10,... | collective-permute-start | bytes 552968 | tf_op jit(solution)/shard_map/ppermute | solution.py:596
  64.4 0.8 collective-permute-start.24
  65.2 0.5 collective-permute-start.27
  65.8 5.9 %collective-permute-done.27.far = bf16[96,768]{1,0:T(8,128)(2,1)S(1)} collective-permute-done((bf16[96,768]{1,0:T(8,128)(2,1)S(1)}, bf16[96,768]{1,0:T(8,128)(2,1)S(1)}, u32[]{:S(2)}, u32[]{:S(2)}) %collective-permute-start.27) | collective-permute-done | bytes 147488 | tf_op jit(solution)/shard_map/ppermute | solution.py:599
  71.7 2.0 %collective-permute-done.24.received = bf16[112,768]{1,0:T(8,128)(2,1)S(1)} collective-permute-done((bf16[112,768]{1,0:T(8,128)(2,1)S(1)}, bf16[112,768]{1,0:T(8,128)(2,1)S(1)}, u32[]{:S(2)}, u32[]{:S(2)}) %collective-permute-start.24) | collective-permute-done | bytes 172064 | tf_op jit(solution)/shard_map/ppermute | solution.py:596
  73.6 0.4 split.1
  74.0 1.5 %collective-permute-start.31 = (bf16[2,96,2176]{2,1,0:T(8,128)(2,1)S(1)}, bf16[2,96,2176]{2,1,0:T(8,128)(2,1)S(1)}, u32[]{:S(2)}, u32[]{:S(2)}) collective-permute-start(bf16[2,96,2176]{2,1,0:T(8,128)(2,1)S(1)} %get-tuple-element.202), channel_id=1, source_target_pairs={{0,8},{4,20},{8,0},{12,28},{16,24},{20,4},{24,16},{28,12},{1,9},{5... | collective-permute-start | bytes 2506760 | tf_op jit(solution)/shard_map/ppermute | solution.py:603
  75.7 2.3 %collective-permute-start.30 = (bf16[104,768]{1,0:T(8,128)(2,1)S(1)}, bf16[104,768]{1,0:T(8,128)(2,1)S(1)}, u32[]{:S(2)}, u32[]{:S(2)}) collective-permute-start(bf16[104,768]{1,0:T(8,128)(2,1)S(1)} %out_total.1.out_own), channel_id=1, source_target_pairs={{0,1},{1,0},{2,3},{3,2},{4,5},{5,4},{6,7},{7,6},{8,9},{9,8},{10,11... | collective-permute-start | bytes 479240 | tf_op jit(solution)/shard_map/ppermute | solution.py:596
  78.0 0.2 proj_two.1
  78.3 0.3 collective-permute-start.32
  78.5 9.7 %collective-permute-done.32.received = bf16[96,768]{1,0:T(8,128)(2,1)S(1)} collective-permute-done((bf16[96,768]{1,0:T(8,128)(2,1)S(1)}, bf16[96,768]{1,0:T(8,128)(2,1)S(1)}, u32[]{:S(2)}, u32[]{:S(2)}) %collective-permute-start.32) | collective-permute-done | bytes 147488 | tf_op jit(solution)/shard_map/ppermute | solution.py:596
  88.2 0.2 cross.1
  88.4 0.4 collective-permute-start.35
  89.0 2.8 %collective-permute-start.34 = (bf16[48,768]{1,0:T(8,128)(2,1)S(1)}, bf16[48,768]{1,0:T(8,128)(2,1)S(1)}, u32[]{:S(2)}, u32[]{:S(2)}) collective-permute-start(bf16[48,768]{1,0:T(8,128)(2,1)S(1)} %get-tuple-element.212), channel_id=1, source_target_pairs={{0,2},{1,3},{2,0},{3,1},{4,6},{5,7},{6,4},{7,5},{8,10},{9,11},{10,... | collective-permute-start | bytes 221192 | tf_op jit(solution)/shard_map/ppermute | solution.py:596
  91.7 0.4 collective-permute-start.36
  92.1 0.9 collective-permute-done.36.their
  93.2 1.9 %collective-permute-start.37 = (bf16[16,576]{1,0:T(8,128)(2,1)S(1)}, bf16[16,576]{1,0:T(8,128)(2,1)S(1)}, u32[]{:S(2)}, u32[]{:S(2)}) collective-permute-start(bf16[16,576]{1,0:T(8,128)(2,1)S(1)} %get-tuple-element.217), channel_id=1, source_target_pairs={{0,8},{4,20},{8,0},{12,28},{16,24},{20,4},{24,16},{28,12},{1,9},{5... | collective-permute-start | bytes 55304 | tf_op jit(solution)/shard_map/ppermute | solution.py:603
  95.1 1.3 %collective-permute-start.38 = (bf16[16,576]{1,0:T(8,128)(2,1)S(1)}, bf16[16,576]{1,0:T(8,128)(2,1)S(1)}, u32[]{:S(2)}, u32[]{:S(2)}) collective-permute-start(bf16[16,576]{1,0:T(8,128)(2,1)S(1)} %get-tuple-element.218), channel_id=1, source_target_pairs={{0,24},{8,16},{16,8},{24,0},{1,25},{9,17},{17,9},{25,1},{2,26},{10... | collective-permute-start | bytes 55304 | tf_op jit(solution)/shard_map/ppermute | solution.py:599
  96.4 0.7 collective-permute-done.37.near
  97.0 2.8 %collective-permute-done.38.far = bf16[16,576]{1,0:T(8,128)(2,1)S(1)} collective-permute-done((bf16[16,576]{1,0:T(8,128)(2,1)S(1)}, bf16[16,576]{1,0:T(8,128)(2,1)S(1)}, u32[]{:S(2)}, u32[]{:S(2)}) %collective-permute-start.38) | collective-permute-done | bytes 18464 | tf_op jit(solution)/shard_map/ppermute | solution.py:599
  99.8 0.2 swap.1
  100.2 0.6 collective-permute-start.40
  100.9 1.6 %collective-permute-done.41.refs_4_ = bf16[112,576]{1,0:T(8,128)(2,1)S(1)} collective-permute-done((bf16[112,576]{1,0:T(8,128)(2,1)S(1)}, bf16[112,576]{1,0:T(8,128)(2,1)S(1)}, u32[]{:S(2)}, u32[]{:S(2)}) %collective-permute-start.41) | collective-permute-done | bytes 129056 | tf_op jit(solution)/shard_map/ppermute | solution.py:593
  102.4 2.0 %final.1 = (bf16[98,2,768]{2,1,0:T(2,128)(2,1)}, f32[98,2,768]{2,1,0:T(2,128)}, f32[192,192]{1,0:T(8,128)}, f32[192,768]{1,0:T(8,128)}, f32[192,768]{1,0:T(8,128...) custom-call(f32[2,104,768]{2,1,0:T(8,128)S(1)} %get-tuple-element.22, ...), custom_call_target="tpu_custom_call" | custom-call | tf_op jit(solution)/shard_map/final/pallas_call | solution.py:33
  (55 shorter events, 1.6 us)
Async XLA Ops:
  0.6 13.5 %copy-start.2 = (bf16[2,98,768]{2,0,1:T(2,128)(2,1)S(1)}, bf16[2,98,768]{2,0,1:T(2,128)(2,1)}, u32[]{:S(2)}) copy-start(bf16[2,98,768]{2,0,1:T(2,128)(2,1)} %param.14) | copy-start | bytes 903172
  0.7 13.1 %copy-start.1 = (bf16[2,98,768]{2,0,1:T(2,128)(2,1)S(1)}, bf16[2,98,768]{2,0,1:T(2,128)(2,1)}, u32[]{:S(2)}) copy-start(bf16[2,98,768]{2,0,1:T(2,128)(2,1)} %param.27) | copy-start | bytes 903172
  0.7 2.6 %collective-permute-start = (bf16[98,2,768]{2,1,0:T(2,128)(2,1)}, bf16[98,2,768]{2,1,0:T(2,128)(2,1)S(1)}, u32[]{:S(2)}, u32[]{:S(2)}) collective-permute-start(bf16[98,2,768]{2,1,0:T(2,128)(2,1)} %bitcast.12), channel_id=1, source_target_pairs={{0,4},{4,0},{1,5},{5,1},{2,6},{6,2},{3,7},{7,3},{8,12},{12,8},{9,1... | collective-permute-start | bytes 903176 | tf_op jit(solution)/shard_map/ppermute | solution.py:593
  1.2 2.1 %collective-permute-start.1 = (bf16[98,2,768]{2,1,0:T(2,128)(2,1)}, bf16[98,2,768]{2,1,0:T(2,128)(2,1)S(1)}, u32[]{:S(2)}, u32[]{:S(2)}) collective-permute-start(bf16[98,2,768]{2,1,0:T(2,128)(2,1)} %bitcast.10), channel_id=1, source_target_pairs={{0,4},{4,0},{1,5},{5,1},{2,6},{6,2},{3,7},{7,3},{8,12},{12,8},{9,1... | collective-permute-start | bytes 903176 | tf_op jit(solution)/shard_map/ppermute | solution.py:593
  3.3 15.2 %copy-start.4 = (bf16[192,192]{1,0:T(8,128)(2,1)S(1)}, bf16[192,192]{1,0:T(8,128)(2,1)}, u32[]{:S(2)}) copy-start(bf16[192,192]{1,0:T(8,128)(2,1)} %get-tuple-element.137.proj_t) | copy-start | bytes 221188
  3.3 12.4 %collective-permute-start.2 = (bf16[208,576]{1,0:T(8,128)(2,1)}, bf16[208,576]{1,0:T(8,128)(2,1)S(1)}, u32[]{:S(2)}, u32[]{:S(2)}) collective-permute-start(bf16[208,576]{1,0:T(8,128)(2,1)} %get-tuple-element.135.refs_0_), channel_id=1, source_target_pairs={{0,8},{4,20},{8,0},{12,28},{16,24},{20,4},{24,16},{28,12},{1,9},{5... | collective-permute-start | bytes 718856 | tf_op jit(solution)/shard_map/ppermute | solution.py:603
  6.3 9.4 %collective-permute-start.3 = (bf16[112,576]{1,0:T(8,128)(2,1)}, bf16[112,576]{1,0:T(8,128)(2,1)S(1)}, u32[]{:S(2)}, u32[]{:S(2)}) collective-permute-start(bf16[112,576]{1,0:T(8,128)(2,1)} %get-tuple-element.136), channel_id=1, source_target_pairs={{0,24},{8,16},{16,8},{24,0},{1,25},{9,17},{17,9},{25,1},{2,26},{10... | collective-permute-start | bytes 387080 | tf_op jit(solution)/shard_map/ppermute | solution.py:599
  7.8 7.9 %collective-permute-start.4 = (bf16[192,192]{1,0:T(8,128)(2,1)}, bf16[192,192]{1,0:T(8,128)(2,1)S(1)}, u32[]{:S(2)}, u32[]{:S(2)}) collective-permute-start(bf16[192,192]{1,0:T(8,128)(2,1)} %get-tuple-element.137.proj_t), channel_id=1, source_target_pairs={{0,1},{4,6},{1,0},{5,7},{2,3},{6,4},{3,2},{7,5},{8,9},{12,14},{9,8... | collective-permute-start | bytes 221192 | tf_op jit(solution)/shard_map/ppermute | solution.py:613
  9.3 6.3 %collective-permute-start.5 = (bf16[96,192]{1,0:T(8,128)(2,1)}, bf16[96,192]{1,0:T(8,128)(2,1)S(1)}, u32[]{:S(2)}, u32[]{:S(2)}) collective-permute-start(bf16[96,192]{1,0:T(8,128)(2,1)} %get-tuple-element.138), channel_id=1, source_target_pairs={{0,3},{1,2},{2,1},{3,0},{4,7},{5,6},{6,5},{7,4},{8,11},{9,10},{10,... | collective-permute-start | bytes 110600 | tf_op jit(solution)/shard_map/ppermute | solution.py:596
  11.8 10.5 %copy-start.3 = (bf16[208,576]{1,0:T(8,128)(2,1)S(1)}, bf16[208,576]{1,0:T(8,128)(2,1)}, u32[]{:S(2)}) copy-start(bf16[208,576]{1,0:T(8,128)(2,1)} %get-tuple-element.135.refs_0_) | copy-start | bytes 718852
  13.8 4.6 %copy-start = (bf16[192,1536]{1,0:T(8,128)(2,1)S(1)}, bf16[192,1536]{1,0:T(8,128)(2,1)}, u32[]{:S(2)}) copy-start(bf16[192,1536]{1,0:T(8,128)(2,1)} %stage.1.feed.refs_0_) | copy-start | bytes 1769476
  15.7 14.1 %collective-permute-start.6 = (bf16[192,1536]{1,0:T(8,128)(2,1)}, bf16[192,1536]{1,0:T(8,128)(2,1)S(1)}, u32[]{:S(2)}, u32[]{:S(2)}) collective-permute-start(bf16[192,1536]{1,0:T(8,128)(2,1)} %stage.1.feed.refs_0_), channel_id=1, source_target_pairs={{0,8},{4,20},{8,0},{12,28},{16,24},{20,4},{24,16},{28,12},{1,9},{5... | collective-permute-start | bytes 1769480 | tf_op jit(solution)/shard_map/ppermute | solution.py:603
  17.0 1.4 %collective-permute-start.8 = (bf16[192,192]{1,0:T(8,128)(2,1)S(1)}, bf16[192,192]{1,0:T(8,128)(2,1)S(1)}, u32[]{:S(2)}, u32[]{:S(2)}) collective-permute-start(bf16[192,192]{1,0:T(8,128)(2,1)S(1)} %collective-permute-done.4.near_in), channel_id=1, source_target_pairs={{0,4},{4,0},{1,5},{5,1},{2,6},{6,2},{3,7},{7,3},{8,12},{12,8},{9,1... | collective-permute-start | bytes 221192 | tf_op jit(solution)/shard_map/ppermute | solution.py:593
  17.0 1.4 %collective-permute-start.9 = (bf16[96,192]{1,0:T(8,128)(2,1)S(1)}, bf16[96,192]{1,0:T(8,128)(2,1)S(1)}, u32[]{:S(2)}, u32[]{:S(2)}) collective-permute-start(bf16[96,192]{1,0:T(8,128)(2,1)S(1)} %collective-permute-done.5.far_in), channel_id=1, source_target_pairs={{0,4},{4,0},{1,5},{5,1},{2,6},{6,2},{3,7},{7,3},{8,12},{12,8},{9,1... | collective-permute-start | bytes 110600 | tf_op jit(solution)/shard_map/ppermute | solution.py:593
  18.6 19.9 %collective-permute-start.16 = (bf16[96,2304]{1,0:T(8,128)(2,1)S(1)}, bf16[96,2304]{1,0:T(8,128)(2,1)S(1)}, u32[]{:S(2)}, u32[]{:S(2)}) collective-permute-start(bf16[96,2304]{1,0:T(8,128)(2,1)S(1)} %get-tuple-element.152), channel_id=1, source_target_pairs={{0,24},{8,16},{16,8},{24,0},{1,25},{9,17},{17,9},{25,1},{2,26},{10... | collective-permute-start | bytes 1327112 | tf_op jit(solution)/shard_map/ppermute | solution.py:599
  19.8 2.5 %collective-permute-start.10 = (bf16[208,576]{1,0:T(8,128)(2,1)S(1)}, bf16[208,576]{1,0:T(8,128)(2,1)S(1)}, u32[]{:S(2)}, u32[]{:S(2)}) collective-permute-start(bf16[208,576]{1,0:T(8,128)(2,1)S(1)} %collective-permute-done.2.refs_1_), channel_id=1, source_target_pairs={{0,4},{4,0},{1,5},{5,1},{2,6},{6,2},{3,7},{7,3},{8,12},{12,8},{9,1... | collective-permute-start | bytes 718856 | tf_op jit(solution)/shard_map/ppermute | solution.py:593
  19.9 18.6 %collective-permute-start.15 = (bf16[192,768]{1,0:T(8,128)(2,1)S(1)}, bf16[192,768]{1,0:T(8,128)(2,1)S(1)}, u32[]{:S(2)}, u32[]{:S(2)}) collective-permute-start(bf16[192,768]{1,0:T(8,128)(2,1)S(1)} %get-tuple-element.147.refs_3_), channel_id=1, source_target_pairs={{0,8},{4,20},{8,0},{12,28},{16,24},{20,4},{24,16},{28,12},{1,9},{5... | collective-permute-start | bytes 884744 | tf_op jit(solution)/shard_map/ppermute | solution.py:603
  21.0 1.4 %collective-permute-start.11 = (bf16[112,576]{1,0:T(8,128)(2,1)S(1)}, bf16[112,576]{1,0:T(8,128)(2,1)S(1)}, u32[]{:S(2)}, u32[]{:S(2)}) collective-permute-start(bf16[112,576]{1,0:T(8,128)(2,1)S(1)} %collective-permute-done.3.refs_3_), channel_id=1, source_target_pairs={{0,4},{4,0},{1,5},{5,1},{2,6},{6,2},{3,7},{7,3},{8,12},{12,8},{9,1... | collective-permute-start | bytes 387080 | tf_op jit(solution)/shard_map/ppermute | solution.py:593
  23.6 8.5 %collective-permute-start.14 = (bf16[312,128]{1,0:T(8,128)(2,1)S(1)}, bf16[312,128]{1,0:T(8,128)(2,1)S(1)}, u32[]{:S(2)}, u32[]{:S(2)}) collective-permute-start(bf16[312,128]{1,0:T(8,128)(2,1)S(1)} %get-tuple-element.151.refs_8_), channel_id=1, source_target_pairs={{0,3},{1,2},{2,1},{3,0},{4,7},{5,6},{6,5},{7,4},{8,11},{9,10},{10,... | collective-permute-start | bytes 239624 | tf_op jit(solution)/shard_map/ppermute | solution.py:596
  29.8 10.9 %collective-permute-start.7 = (bf16[192,1536]{1,0:T(8,128)(2,1)S(1)}, bf16[192,1536]{1,0:T(8,128)(2,1)S(1)}, u32[]{:S(2)}, u32[]{:S(2)}) collective-permute-start(bf16[192,1536]{1,0:T(8,128)(2,1)S(1)} %collective-permute-done.6.refs_1_), channel_id=1, source_target_pairs={{0,4},{4,0},{1,5},{5,1},{2,6},{6,2},{3,7},{7,3},{8,12},{12,8},{9,1... | collective-permute-start | bytes 1769480 | tf_op jit(solution)/shard_map/ppermute | solution.py:593
  29.8 7.5 %collective-permute-start.13 = (bf16[312,128]{1,0:T(8,128)(2,1)S(1)}, bf16[312,128]{1,0:T(8,128)(2,1)S(1)}, u32[]{:S(2)}, u32[]{:S(2)}) collective-permute-start(bf16[312,128]{1,0:T(8,128)(2,1)S(1)} %get-tuple-element.151.refs_8_), channel_id=1, source_target_pairs={{0,2},{1,3},{2,0},{3,1},{4,6},{5,7},{6,4},{7,5},{8,10},{9,11},{10,... | collective-permute-start | bytes 239624 | tf_op jit(solution)/shard_map/ppermute | solution.py:596
  32.1 5.4 %collective-permute-start.12 = (bf16[312,128]{1,0:T(8,128)(2,1)S(1)}, bf16[312,128]{1,0:T(8,128)(2,1)S(1)}, u32[]{:S(2)}, u32[]{:S(2)}) collective-permute-start(bf16[312,128]{1,0:T(8,128)(2,1)S(1)} %get-tuple-element.151.refs_8_), channel_id=1, source_target_pairs={{0,1},{1,0},{2,3},{3,2},{4,5},{5,4},{6,7},{7,6},{8,9},{9,8},{10,11... | collective-permute-start | bytes 239624 | tf_op jit(solution)/shard_map/ppermute | solution.py:596
  38.5 2.2 %collective-permute-start.18 = (bf16[96,2304]{1,0:T(8,128)(2,1)S(1)}, bf16[96,2304]{1,0:T(8,128)(2,1)S(1)}, u32[]{:S(2)}, u32[]{:S(2)}) collective-permute-start(bf16[96,2304]{1,0:T(8,128)(2,1)S(1)} %collective-permute-done.16.refs_6_), channel_id=1, source_target_pairs={{0,4},{4,0},{1,5},{5,1},{2,6},{6,2},{3,7},{7,3},{8,12},{12,8},{9,1... | collective-permute-start | bytes 1327112 | tf_op jit(solution)/shard_map/ppermute | solution.py:593
  38.5 2.2 %collective-permute-start.17 = (bf16[192,768]{1,0:T(8,128)(2,1)S(1)}, bf16[192,768]{1,0:T(8,128)(2,1)S(1)}, u32[]{:S(2)}, u32[]{:S(2)}) collective-permute-start(bf16[192,768]{1,0:T(8,128)(2,1)S(1)} %collective-permute-done.15.refs_4_), channel_id=1, source_target_pairs={{0,4},{4,0},{1,5},{5,1},{2,6},{6,2},{3,7},{7,3},{8,12},{12,8},{9,1... | collective-permute-start | bytes 884744 | tf_op jit(solution)/shard_map/ppermute | solution.py:593
  44.5 14.1 %collective-permute-start.23 = (bf16[288,768]{1,0:T(8,128)(2,1)S(1)}, bf16[288,768]{1,0:T(8,128)(2,1)S(1)}, u32[]{:S(2)}, u32[]{:S(2)}) collective-permute-start(bf16[288,768]{1,0:T(8,128)(2,1)S(1)} %get-tuple-element.174), channel_id=1, source_target_pairs={{0,4},{4,0},{1,5},{5,1},{2,6},{6,2},{3,7},{7,3},{8,12},{12,8},{9,1... | collective-permute-start | bytes 1327112 | tf_op jit(solution)/shard_map/ppermute | solution.py:593
  45.3 13.3 %collective-permute-start.22 = (bf16[104,768]{1,0:T(8,128)(2,1)S(1)}, bf16[104,768]{1,0:T(8,128)(2,1)S(1)}, u32[]{:S(2)}, u32[]{:S(2)}) collective-permute-start(bf16[104,768]{1,0:T(8,128)(2,1)S(1)} %get-tuple-element.167), channel_id=1, source_target_pairs={{0,1},{1,0},{2,3},{3,2},{4,5},{5,4},{6,7},{7,6},{8,9},{9,8},{10,11... | collective-permute-start | bytes 479240 | tf_op jit(solution)/shard_map/ppermute | solution.py:596
  46.6 8.5 %collective-permute-start.19 = (bf16[312,128]{1,0:T(8,128)(2,1)S(1)}, bf16[312,128]{1,0:T(8,128)(2,1)S(1)}, u32[]{:S(2)}, u32[]{:S(2)}) collective-permute-start(bf16[312,128]{1,0:T(8,128)(2,1)S(1)} %get-tuple-element.164), channel_id=1, source_target_pairs={{0,1},{1,0},{2,3},{3,2},{4,5},{5,4},{6,7},{7,6},{8,9},{9,8},{10,11... | collective-permute-start | bytes 239624 | tf_op jit(solution)/shard_map/ppermute | solution.py:596
  47.4 7.8 %collective-permute-start.20 = (bf16[312,128]{1,0:T(8,128)(2,1)S(1)}, bf16[312,128]{1,0:T(8,128)(2,1)S(1)}, u32[]{:S(2)}, u32[]{:S(2)}) collective-permute-start(bf16[312,128]{1,0:T(8,128)(2,1)S(1)} %get-tuple-element.165), channel_id=1, source_target_pairs={{0,2},{1,3},{2,0},{3,1},{4,6},{5,7},{6,4},{7,5},{8,10},{9,11},{10,... | collective-permute-start | bytes 239624 | tf_op jit(solution)/shard_map/ppermute | solution.py:596
  49.7 8.9 %collective-permute-start.21 = (bf16[312,128]{1,0:T(8,128)(2,1)S(1)}, bf16[312,128]{1,0:T(8,128)(2,1)S(1)}, u32[]{:S(2)}, u32[]{:S(2)}) collective-permute-start(bf16[312,128]{1,0:T(8,128)(2,1)S(1)} %get-tuple-element.166), channel_id=1, source_target_pairs={{0,3},{1,2},{2,1},{3,0},{4,7},{5,6},{6,5},{7,4},{8,11},{9,10},{10,... | collective-permute-start | bytes 239624 | tf_op jit(solution)/shard_map/ppermute | solution.py:596
  61.3 12.4 %collective-permute-start.28 = (bf16[384,2176]{1,0:T(8,128)(2,1)S(1)}, bf16[384,2176]{1,0:T(8,128)(2,1)S(1)}, u32[]{:S(2)}, u32[]{:S(2)}) collective-permute-start(bf16[384,2176]{1,0:T(8,128)(2,1)S(1)} %get-tuple-element.194), channel_id=1, source_target_pairs={{0,4},{4,0},{1,5},{5,1},{2,6},{6,2},{3,7},{7,3},{8,12},{12,8},{9,1... | collective-permute-start | bytes 5013512 | tf_op jit(solution)/shard_map/ppermute | solution.py:593
  61.4 12.2 %collective-permute-start.26 = (bf16[192,768]{1,0:T(8,128)(2,1)S(1)}, bf16[192,768]{1,0:T(8,128)(2,1)S(1)}, u32[]{:S(2)}, u32[]{:S(2)}) collective-permute-start(bf16[192,768]{1,0:T(8,128)(2,1)S(1)} %get-tuple-element.189), channel_id=1, source_target_pairs={{0,8},{4,20},{8,0},{12,28},{16,24},{20,4},{24,16},{28,12},{1,9},{5... | collective-permute-start | bytes 884744 | tf_op jit(solution)/shard_map/ppermute | solution.py:603
  63.1 10.6 %collective-permute-start.25 = (bf16[120,768]{1,0:T(8,128)(2,1)S(1)}, bf16[120,768]{1,0:T(8,128)(2,1)S(1)}, u32[]{:S(2)}, u32[]{:S(2)}) collective-permute-start(bf16[120,768]{1,0:T(8,128)(2,1)S(1)} %out_pair.1.own), channel_id=1, source_target_pairs={{0,2},{1,3},{2,0},{3,1},{4,6},{5,7},{6,4},{7,5},{8,10},{9,11},{10,... | collective-permute-start | bytes 552968 | tf_op jit(solution)/shard_map/ppermute | solution.py:596
  64.4 9.2 %collective-permute-start.24 = (bf16[112,768]{1,0:T(8,128)(2,1)S(1)}, bf16[112,768]{1,0:T(8,128)(2,1)S(1)}, u32[]{:S(2)}, u32[]{:S(2)}) collective-permute-start(bf16[112,768]{1,0:T(8,128)(2,1)S(1)} %get-tuple-element.186), channel_id=1, source_target_pairs={{0,1},{1,0},{2,3},{3,2},{4,5},{5,4},{6,7},{7,6},{8,9},{9,8},{10,11... | collective-permute-start | bytes 516104 | tf_op jit(solution)/shard_map/ppermute | solution.py:596
  65.2 6.4 %collective-permute-start.27 = (bf16[96,768]{1,0:T(8,128)(2,1)S(1)}, bf16[96,768]{1,0:T(8,128)(2,1)S(1)}, u32[]{:S(2)}, u32[]{:S(2)}) collective-permute-start(bf16[96,768]{1,0:T(8,128)(2,1)S(1)} %get-tuple-element.190), channel_id=1, source_target_pairs={{0,24},{8,16},{16,8},{24,0},{1,25},{9,17},{17,9},{25,1},{2,26},{10... | collective-permute-start | bytes 442376 | tf_op jit(solution)/shard_map/ppermute | solution.py:599
  74.0 14.2 %collective-permute-start.31 = (bf16[2,96,2176]{2,1,0:T(8,128)(2,1)S(1)}, bf16[2,96,2176]{2,1,0:T(8,128)(2,1)S(1)}, u32[]{:S(2)}, u32[]{:S(2)}) collective-permute-start(bf16[2,96,2176]{2,1,0:T(8,128)(2,1)S(1)} %get-tuple-element.202), channel_id=1, source_target_pairs={{0,8},{4,20},{8,0},{12,28},{16,24},{20,4},{24,16},{28,12},{1,9},{5... | collective-permute-start | bytes 2506760 | tf_op jit(solution)/shard_map/ppermute | solution.py:603
  75.6 12.6 %collective-permute-start.29 = (bf16[112,768]{1,0:T(8,128)(2,1)S(1)}, bf16[112,768]{1,0:T(8,128)(2,1)S(1)}, u32[]{:S(2)}, u32[]{:S(2)}) collective-permute-start(bf16[112,768]{1,0:T(8,128)(2,1)S(1)} %in_pair.1.own), channel_id=1, source_target_pairs={{0,2},{1,3},{2,0},{3,1},{4,6},{5,7},{6,4},{7,5},{8,10},{9,11},{10,... | collective-permute-start | bytes 516104 | tf_op jit(solution)/shard_map/ppermute | solution.py:596
  75.7 12.5 %collective-permute-start.30 = (bf16[104,768]{1,0:T(8,128)(2,1)S(1)}, bf16[104,768]{1,0:T(8,128)(2,1)S(1)}, u32[]{:S(2)}, u32[]{:S(2)}) collective-permute-start(bf16[104,768]{1,0:T(8,128)(2,1)S(1)} %out_total.1.out_own), channel_id=1, source_target_pairs={{0,1},{1,0},{2,3},{3,2},{4,5},{5,4},{6,7},{7,6},{8,9},{9,8},{10,11... | collective-permute-start | bytes 479240 | tf_op jit(solution)/shard_map/ppermute | solution.py:596
  78.3 9.9 %collective-permute-start.32 = (bf16[96,768]{1,0:T(8,128)(2,1)S(1)}, bf16[96,768]{1,0:T(8,128)(2,1)S(1)}, u32[]{:S(2)}, u32[]{:S(2)}) collective-permute-start(bf16[96,768]{1,0:T(8,128)(2,1)S(1)} %get-tuple-element.205), channel_id=1, source_target_pairs={{0,1},{1,0},{2,3},{3,2},{4,5},{5,4},{6,7},{7,6},{8,9},{9,8},{10,11... | collective-permute-start | bytes 442376 | tf_op jit(solution)/shard_map/ppermute | solution.py:596
  88.4 11.4 %collective-permute-start.35 = (bf16[96,2176]{1,0:T(8,128)(2,1)S(1)}, bf16[96,2176]{1,0:T(8,128)(2,1)S(1)}, u32[]{:S(2)}, u32[]{:S(2)}) collective-permute-start(bf16[96,2176]{1,0:T(8,128)(2,1)S(1)} %get-tuple-element.215), channel_id=1, source_target_pairs={{0,16},{4,12},{8,24},{12,4},{16,0},{20,28},{24,8},{28,20},{1,17},{... | collective-permute-start | bytes 1253384 | tf_op jit(solution)/shard_map/ppermute | solution.py:603
  88.8 10.9 %collective-permute-start.33 = (bf16[104,768]{1,0:T(8,128)(2,1)S(1)}, bf16[104,768]{1,0:T(8,128)(2,1)S(1)}, u32[]{:S(2)}, u32[]{:S(2)}) collective-permute-start(bf16[104,768]{1,0:T(8,128)(2,1)S(1)} %get-tuple-element.209.in_own), channel_id=1, source_target_pairs={{0,1},{1,0},{2,3},{3,2},{4,5},{5,4},{6,7},{7,6},{8,9},{9,8},{10,11... | collective-permute-start | bytes 479240 | tf_op jit(solution)/shard_map/ppermute | solution.py:596
  89.0 10.8 %collective-permute-start.34 = (bf16[48,768]{1,0:T(8,128)(2,1)S(1)}, bf16[48,768]{1,0:T(8,128)(2,1)S(1)}, u32[]{:S(2)}, u32[]{:S(2)}) collective-permute-start(bf16[48,768]{1,0:T(8,128)(2,1)S(1)} %get-tuple-element.212), channel_id=1, source_target_pairs={{0,2},{1,3},{2,0},{3,1},{4,6},{5,7},{6,4},{7,5},{8,10},{9,11},{10,... | collective-permute-start | bytes 221192 | tf_op jit(solution)/shard_map/ppermute | solution.py:596
  91.7 1.3 %collective-permute-start.36 = (f32[16,768]{1,0:T(8,128)S(1)}, f32[16,768]{1,0:T(8,128)S(1)}, u32[]{:S(2)}, u32[]{:S(2)}) collective-permute-start(f32[16,768]{1,0:T(8,128)S(1)} %get-tuple-element.216.vec), channel_id=1, source_target_pairs={{0,4},{4,0},{1,5},{5,1},{2,6},{6,2},{3,7},{7,3},{8,12},{12,8},{9,1... | collective-permute-start | bytes 147464 | tf_op jit(solution)/shard_map/ppermute | solution.py:593
  93.2 3.8 %collective-permute-start.37 = (bf16[16,576]{1,0:T(8,128)(2,1)S(1)}, bf16[16,576]{1,0:T(8,128)(2,1)S(1)}, u32[]{:S(2)}, u32[]{:S(2)}) collective-permute-start(bf16[16,576]{1,0:T(8,128)(2,1)S(1)} %get-tuple-element.217), channel_id=1, source_target_pairs={{0,8},{4,20},{8,0},{12,28},{16,24},{20,4},{24,16},{28,12},{1,9},{5... | collective-permute-start | bytes 55304 | tf_op jit(solution)/shard_map/ppermute | solution.py:603
  95.1 4.7 %collective-permute-start.38 = (bf16[16,576]{1,0:T(8,128)(2,1)S(1)}, bf16[16,576]{1,0:T(8,128)(2,1)S(1)}, u32[]{:S(2)}, u32[]{:S(2)}) collective-permute-start(bf16[16,576]{1,0:T(8,128)(2,1)S(1)} %get-tuple-element.218), channel_id=1, source_target_pairs={{0,24},{8,16},{16,8},{24,0},{1,25},{9,17},{17,9},{25,1},{2,26},{10... | collective-permute-start | bytes 55304 | tf_op jit(solution)/shard_map/ppermute | solution.py:599
  100.0 2.4 %collective-permute-start.39 = (bf16[256,768]{1,0:T(8,128)(2,1)S(1)}, bf16[256,768]{1,0:T(8,128)(2,1)S(1)}, u32[]{:S(2)}, u32[]{:S(2)}) collective-permute-start(bf16[256,768]{1,0:T(8,128)(2,1)S(1)} %get-tuple-element.223), channel_id=1, source_target_pairs={{0,4},{4,0},{1,5},{5,1},{2,6},{6,2},{3,7},{7,3},{8,12},{12,8},{9,1... | collective-permute-start | bytes 1179656 | tf_op jit(solution)/shard_map/ppermute | solution.py:593
  100.2 2.2 %collective-permute-start.40 = (bf16[96,1536]{1,0:T(8,128)(2,1)S(1)}, bf16[96,1536]{1,0:T(8,128)(2,1)S(1)}, u32[]{:S(2)}, u32[]{:S(2)}) collective-permute-start(bf16[96,1536]{1,0:T(8,128)(2,1)S(1)} %get-tuple-element.231), channel_id=1, source_target_pairs={{0,4},{4,0},{1,5},{5,1},{2,6},{6,2},{3,7},{7,3},{8,12},{12,8},{9,1... | collective-permute-start | bytes 884744 | tf_op jit(solution)/shard_map/ppermute | solution.py:593
  100.8 1.6 %collective-permute-start.41 = (bf16[112,576]{1,0:T(8,128)(2,1)S(1)}, bf16[112,576]{1,0:T(8,128)(2,1)S(1)}, u32[]{:S(2)}, u32[]{:S(2)}) collective-permute-start(bf16[112,576]{1,0:T(8,128)(2,1)S(1)} %get-tuple-element.233), channel_id=1, source_target_pairs={{0,4},{4,0},{1,5},{5,1},{2,6},{6,2},{3,7},{7,3},{8,12},{12,8},{9,1... | collective-permute-start | bytes 387080 | tf_op jit(solution)/shard_map/ppermute | solution.py:593

commit v5 on v4

--- a/solution.py
+++ b/solution.py
@@ -18,6 +18,7 @@
 VMEM = pl.BlockSpec(memory_space=pltpu.VMEM)
 ANY = pl.BlockSpec(memory_space=pl.ANY)
 EXTRA = 16
+VEC_ROWS = 144
 UP_AT, QV_AT = 256, 384
 
 
@@ -65,6 +66,10 @@
 def norm_backward(grad_normed, normal, inverse, gain):
     scaled = grad_normed * gain
     return inverse * (scaled - mean(scaled) - normal * mean(scaled * normal))
+
+
+def row_half(t):
+    return (t ^ (t >> 1)) & 1
 
 
 def lanes(parts):
@@ -95,6 +100,7 @@
         self.tail = self.part // 4
         self.direct = nf == 4
         self.cols = 2 * self.ff + nt * self.inner
+        self.early = 1152 if self.ff == 768 else self.ff
         self.all_cols = 2 * self.ff + -(-3 * self.inner // 128) * 128
         self.dense = self.rows * self.inner // 128
 
@@ -120,10 +126,12 @@
         m.wait()
 
 
-def stage_kernel(z, up, down_t, out, one, two, sem):
+def stage_kernel(z, up, down_t, out, rest, one, two, sem):
     fetch((up, down_t), (one, two), sem)
+    first = z.early - z.ff
     out[:, : z.ff] = one[...]
-    out[:, z.ff :] = two[...]
+    out[:, z.ff :] = two[:, :first]
+    rest[...] = two[:, first:]
 
 
 def pack_kernel(z, *refs):
@@ -157,16 +165,17 @@
     out[1] = second[...]
 
 
-def pack_rest_kernel(z, feed, proj_t, near_in, near_their, far_in, far_their, near, far, scratch):
+def pack_rest_kernel(z, feed, rest, proj_t, near_in, near_their, far_in, far_their, near, far, scratch):
     c, t = lax.axis_index("ctx"), lax.axis_index("tp")
     scratch[t] = read(proj_t)
-    scratch[t ^ (1 + c)] = read(near_in)
-    scratch[t ^ (2 - c)] = read(near_their)
-    scratch[t ^ 3, z.half_of(c), :] = read(far_in)
-    scratch[t ^ 3, z.half_of(1 - c), :] = read(far_their)
-    near[...] = lanes([scratch[i] for i in range(4)]).astype(LOW)
-    far[:, : 2 * z.ff] = feed[z.half_of(c), :]
-    far[:, 2 * z.ff :] = near[z.half_of(c), :]
+    scratch[t ^ (1 + 2 * c)] = read(near_in)
+    scratch[t ^ (3 - 2 * c)] = read(near_their)
+    scratch[t ^ 2, z.half_of(c), :] = read(far_in)
+    scratch[t ^ 2, z.half_of(1 - c), :] = read(far_their)
+    near[:, : 2 * z.ff - z.early] = rest[...]
+    near[:, 2 * z.ff - z.early :] = lanes([scratch[i] for i in range(4)]).astype(LOW)
+    far[:, : z.early] = feed[z.half_of(c), :]
+    far[:, z.early :] = near[z.half_of(c), :]
 
 
 def own_frame(z, keep, received):
@@ -263,10 +272,10 @@
     if z.direct:
         c, b = lax.axis_index("ctx"), lax.axis_index("fsdp")
         mine, other = z.half_of(c), z.half_of(1 - c)
-        first, last = pl.ds(0, 2 * z.ff), pl.ds(2 * z.ff, z.nt * z.inner)
-        for at, rest, proj in ((b, feed, near), (b ^ (1 + c), feed_in, near_in), (b ^ (2 - c), feed_their, near_their)):
-            w_out[at, :, first] = rest[...]
-            w_out[at, :, last] = proj[...]
+        first, last = pl.ds(0, z.early), pl.ds(z.early, z.cols - z.early)
+        for at, one, two in ((b, feed, near), (b ^ (1 + c), feed_in, near_in), (b ^ (2 - c), feed_their, near_their)):
+            w_out[at, :, first] = one[...]
+            w_out[at, :, last] = two[...]
         w_out[b ^ 3, mine, :] = far[...]
         w_out[b ^ 3, other, :] = far_their[...]
     else:
@@ -312,7 +321,7 @@
 
 
 def down_kernel(z, hidden, w, kept, sent, scratch):
-    h = lax.axis_index("tp") & 1
+    h = row_half(lax.axis_index("tp"))
     w_down_t = w[:, :, z.ff : 2 * z.ff].reshape(z.width, z.ff)
     scratch[...] = dot(hidden[...], w_down_t, NT)
     kept[...] = scratch[z.half_rows(h), :]
@@ -432,17 +441,22 @@
     vec = small_in[...]
     vec = jnp.where(row == 0, total_rows(grad_normed * normal[...]), vec)
     vec = jnp.where(row == 1, total_rows(grad_normed), vec)
-    h = t & 1
+    h = row_half(t)
     kept[: z.padded, :] = scratch[z.half_rows(h), :]
     kept[z.padded :, :] = vec
     sent[: z.padded, :] = scratch[z.half_rows(1 - h), :].astype(LOW)
     sent[z.padded :, :] = vec.astype(LOW)
 
 
-def out_total_kernel(z, own, received, middle, small, out):
-    rows = z.half_rows(lax.axis_index("tp") & 1)
+def out_total_kernel(z, own, received, middle, small, *refs):
+    if z.direct:
+        keep, near, far, kept, out, scratch = refs
+        proj_two_kernel(z, keep, near, far, out, kept, scratch)
+    else:
+        (out,) = refs
+    rows = z.half_rows(row_half(lax.axis_index("tp")))
     total = (read(own) + read(received))[: z.padded]
-    out[...] = (middle[rows, :] + total + small[5:6]).astype(LOW)
+    out[: z.padded, :] = (middle[rows, :] + total + small[5:6]).astype(LOW)
 
 
 def proj_two_kernel(z, keep, near, far, out, kept, scratch):
@@ -453,21 +467,21 @@
     for i in range(z.nt):
         scratch[i] = fold(proj[:, i * z.inner : (i + 1) * z.inner])
     kept[0] = scratch[t]
-    kept[1] = scratch[t ^ 2]
-    out[...] = rows_of([scratch[t ^ 1], scratch[t ^ 3]]).astype(LOW)
+    kept[1] = scratch[t ^ 3]
+    out[z.padded :, :] = rows_of([scratch[t ^ 1], scratch[t ^ 2]]).astype(LOW)
 
 
 def sum_rows_kernel(z, own, received, small, qv, out, vec):
     total = read(own) + read(received)
     out[...] = total[: z.padded].astype(LOW)
     vec[:8, :] = total[z.padded :]
-    vec[8:, :] = jnp.zeros((8, z.width), F32)
+    vec[8:, :] = jnp.zeros((vec.shape[0] - 8, z.width), F32)
     vec[8:9, : z.ff] = small[6:7, : z.ff]
     vec[9:10, : 3 * z.inner] = qv[...]
 
 
 def proj_pair_kernel(z, kept, received, own, sent):
-    arrived = read(received)
+    arrived = received[z.padded :, :].astype(F32)
     own[...] = kept[0] + arrived[: z.tail]
     sent[...] = (kept[1] + arrived[z.tail :]).astype(LOW)
 
@@ -479,7 +493,7 @@
 
 def small_kernel(z, vec, their, near, far, own, scratch):
     c, b = lax.axis_index("ctx"), lax.axis_index("fsdp")
-    vectors = vec[...] + their[...]
+    vectors = vec[:16, :] + their[:16, :]
     up = rows_of([vectors[8:9, i * HD : (i + 1) * HD] for i in range(z.ff // HD)])
     pieces = []
     for h in range(z.heads):
@@ -499,12 +513,12 @@
 
 
 def halves_of(z, own, received):
-    h = lax.axis_index("tp") & 1
+    h = row_half(lax.axis_index("tp"))
     return jnp.where(h == 0, own, received), jnp.where(h == 0, received, own)
 
 
 def swap_kernel(z, out_own, out_in, in_own, in_in, *refs):
-    out_mine, out_theirs = halves_of(z, read(out_own), read(out_in))
+    out_mine, out_theirs = halves_of(z, out_own[: z.padded, :].astype(F32), out_in[: z.padded, :].astype(F32))
     in_mine, in_theirs = halves_of(z, read(in_own), read(in_in))
     theirs = [out_theirs, in_theirs]
     if z.direct:
@@ -609,7 +623,7 @@
             return neighbours(value, (2, 1))
 
         def proj_near(value):
-            pairs = [(c * nt + i, c * nt + (i ^ (1 + c))) for i in range(nt) for c in range(2)]
+            pairs = [(c * nt + i, c * nt + (i ^ (1 + 2 * c))) for i in range(nt) for c in range(2)]
             return lax.ppermute(value, ("ctx", "tp"), pairs)
 
         def pair_of(first, second):
@@ -651,27 +665,27 @@
             )
             near, far, proj_t, proj_half, x_recv, cot_recv = tie((near, far, proj_t, proj_half, x_recv, cot_recv))
             got = [to_near(near), to_far(far)]
-            proj_got = [proj_near(proj_t), to_tp(proj_half, 3)]
-            (feed_own,) = call(
+            proj_got = [proj_near(proj_t), to_tp(proj_half, 2)]
+            feed_own, feed_rest = call(
                 part(stage_kernel, z),
-                [shape((z.part, 2 * ff), LOW)],
+                [shape((z.part, z.early), LOW), shape((z.part, 2 * ff - z.early), LOW)],
                 [fc1_weight, down_t],
                 [pltpu.VMEM((z.part, ff), LOW)] * 2 + [pltpu.SemaphoreType.DMA((2,))],
                 name="stage",
-                mib=56,
+                mib=20,
                 in_specs=[ANY] * 2,
             )
             stream, normal_one, inverse_one, cot = frames(x_recv, cot_recv)
-            got, proj_got, feed_own, stream, normal_one, inverse_one, cot = tie(
-                (got, proj_got, feed_own, stream, normal_one, inverse_one, cot)
-            )
             feed_in = to_near(feed_own)
+            got, proj_got, feed_rest, stream, normal_one, inverse_one, cot = tie(
+                (got, proj_got, feed_rest, stream, normal_one, inverse_one, cot)
+            )
             shared = [other_core(g) for g in got]
             qkv_in = [near, got[0], shared[0], got[1], shared[1]]
             rest_near, rest_far = call(
                 part(pack_rest_kernel, z),
-                [shape((z.part, nt * inner), LOW), shape((chunk, z.cols), LOW)],
-                [feed_own, proj_t, proj_got[0], other_core(proj_got[0]), proj_got[1], other_core(proj_got[1])],
+                [shape((z.part, z.cols - z.early), LOW), shape((chunk, z.cols), LOW)],
+                [feed_own, feed_rest, proj_t, proj_got[0], other_core(proj_got[0]), proj_got[1], other_core(proj_got[1])],
                 [pltpu.VMEM((nt, z.part, inner), F32)],
                 name="pack_rest",
             )
@@ -704,8 +718,8 @@
         )
         att = [to_tp(attended, k) for k in range(1, nt)]
         if z.direct:
-            att, near_in, far_in = tie((att, near_in, far_in))
-            rest_in = [feed_own, feed_in, other_core(feed_in), rest_near, near_in, other_core(near_in)]
+            att, feed_in, near_in, far_in = tie((att, feed_in, near_in, far_in))
+            rest_in = [feed_own, feed_in, other_core(feed_in)] + [rest_near, near_in, other_core(near_in)]
             rest_in += [far_in, other_core(far_in)]
 
         (w_rest, att_all, middle, hidden, normed_two, grad_pre, part_middle, part_low, own_att, small_two, *att_sends) = (
@@ -762,8 +776,8 @@
                 name="proj_one",
             )
             proj_in = [to_near(near), to_far(far)]
-        (out_low,) = call(add_low_kernel, [shape((z.padded + 16, width), LOW)], [out_kept, out_one], name="out_pair")
-        out_two = to_tp(out_low, 2)
+        (out_low,) = call(add_low_kernel, [shape((z.padded, width), LOW)], [out_kept, out_one], name="out_pair")
+        out_two = to_tp(out_low, 3)
 
         grads, qv_sum, in_kept, in_sent = call(
             part(back_kernel, z),
@@ -795,28 +809,21 @@
             )
             grad_in = to_near(grad_sent)
         (in_low,) = call(add_low_kernel, [shape((z.padded + 8, width), LOW)], [in_kept, in_one], name="in_pair")
-        in_two = to_tp(in_low, 2)
-        (out_low,) = call(
+        in_two = to_tp(in_low, 3)
+        *proj_kept, out_low = call(
             part(out_total_kernel, z),
-            [shape((z.padded, width), LOW)],
-            [out_low, out_two, middle, small],
+            ([shape((2, z.tail, width), F32)] if z.direct else [])
+            + [shape((z.padded + (2 * z.tail if z.direct else 0), width), LOW)],
+            [out_low, out_two, middle, small] + ([keep_proj] + proj_in if z.direct else []),
+            [pltpu.VMEM((nt, z.tail, width), F32)] if z.direct else [],
             name="out_total",
         )
         out_in = to_tp(out_low, 1)
         if z.direct:
-            proj_sent, proj_kept = call(
-                part(proj_two_kernel, z),
-                [shape((2 * z.tail, width), LOW), shape((2, z.tail, width), F32)],
-                [keep_proj] + proj_in,
-                [pltpu.VMEM((nt, z.tail, width), F32)],
-                name="proj_two",
-            )
-            proj_in = to_tp(proj_sent, 1)
-        if z.direct:
-            in_two, out_in, grad_in, proj_in = tie((in_two, out_in, grad_in, proj_in))
+            in_two, out_in, grad_in = tie((in_two, out_in, grad_in))
         in_low, vec = call(
             part(sum_rows_kernel, z),
-            [shape((z.padded, width), LOW), shape((16, width), F32)],
+            [shape((z.padded, width), LOW), shape((VEC_ROWS, width), F32)],
             [in_low, in_two, small_two, qv_sum],
             name="sum_rows",
         )
@@ -833,10 +840,10 @@
             proj_own, proj_sent = call(
                 part(proj_pair_kernel, z),
                 [shape((z.tail, width), F32), shape((z.tail, width), LOW)],
-                [proj_kept, proj_in],
+                [proj_kept[0], out_in],
                 name="proj_pair",
             )
-            proj_two = to_tp(proj_sent, 2)
+            proj_two = to_tp(proj_sent, 3)
             near, far, small_own = call(
                 part(small_kernel, z),
                 [shape((EXTRA, 3 * inner), LOW)] * 2 + [shape((EXTRA, 3 * inner), F32)],

time: 105 us -> 99.9 us (0.951)
  starting transfers between devices: 43.1 us -> 39.7 us
  local copies, waits for them, and re-layouts: 0.02 us -> 2.9 us
  waiting for transfers between devices: 42.4 us -> 40.1 us
  Pallas kernels: 17.9 us -> 16 us
    ppermute x15 -> x14, starting transfers between devices: 23.1 us -> 18.4 us  [to_tp(): return lax.ppermute(value, 'tp', [(i, i ^ k) for i in range(nt)])]
    ppermute x4, waiting for transfers between devices: 8.66 us -> 5.21 us  [to_far(): return lax.ppermute(value, 'fsdp', [(i, i ^ 3) for i in range(nf)])]
    ppermute x15 -> x14, waiting for transfers between devices: 23 us -> 26.1 us  [to_tp(): return lax.ppermute(value, 'tp', [(i, i ^ k) for i in range(nt)])]
    unnamed x10 -> x12, local copies, waits for them, and re-layouts: 0.02 us -> 2.9 us
    pallas_call x25 -> x24, Pallas kernels: 17.9 us -> 16 us  [call(): pl.pallas_call(kernel, out_shape=tuple(outs), in_specs=in_specs or [VMEM]...]
    ppermute x7, waiting for transfers between devices: 4.49 us -> 2.65 us  [neighbours(): return lax.ppermute(value, ('fsdp', 'ctx'), pairs)]
  transfers between devices with their start and end apart: 42 -> 41, of which waited for: 17 -> 16; matrix products, arithmetic and copies ran while one was open for 0% -> 0% of each run, Pallas kernels for 8% -> 7%
where the time goes in v5:
time: 99.9 us; the launch traced here: 99.6 us
  waiting for transfers between devices  40.1 us (40%)
  starting transfers between devices  39.7 us (40%)
  Pallas kernels  16 us (16%)
  local copies, waits for them, and re-layouts  2.9 us (3%)
    ppermute x14, waiting for transfers between devices, to_tp(): return lax.ppermute(value, 'tp', [(i, i ^ k) for i in range(nt)])  26.1 us
    ppermute x14, starting transfers between devices, to_tp(): return lax.ppermute(value, 'tp', [(i, i ^ k) for i in range(nt)])  18.4 us
    pallas_call x24, Pallas kernels, call(): pl.pallas_call(kernel, out_shape=tuple(outs), in_specs=in_specs or [VMEM]...  16 us
    ppermute x7, starting transfers between devices, neighbours(): return lax.ppermute(value, ('fsdp', 'ctx'), pairs)  11.7 us
    ppermute x15, waiting for transfers between devices, other_core(): return lax.ppermute(value, 'ctx', [(0, 1), (1, 0)])  6.13 us
    ppermute x4, waiting for transfers between devices, to_far(): return lax.ppermute(value, 'fsdp', [(i, i ^ 3) for i in range(nf)])  5.21 us
    ppermute x4, starting transfers between devices, to_far(): return lax.ppermute(value, 'fsdp', [(i, i ^ 3) for i in range(nf)])  4.76 us
    ppermute x15, starting transfers between devices, other_core(): return lax.ppermute(value, 'ctx', [(0, 1), (1, 0)])  3.34 us
  transfers between devices with their start and end apart: 41, of which 16 were waited for; matrix products, arithmetic and copies ran while one was open for 0% of the time, Pallas kernels for 7%

profile of v5, /device:TPU:0, one launch (start us, length us, event | category | flops | bytes accessed | tf_op | source)
XLA Modules:
  0.0 99.6 jit_solution(3338243436404708179)
XLA Ops:
  0.7 0.5 collective-permute-start
  1.3 2.0 %pack.1 = (bf16[208,576]{1,0:T(8,128)(2,1)}, bf16[112,576]{1,0:T(8,128)(2,1)}, bf16[192,192]{1,0:T(8,128)(2,1)}, bf16[96,192]{1,0:T(8,128)(2,1)}) custom-call(bf16[3,192,192]{2,1,0:T(8,128)(2,1)} %bitcast.15, bf16[192,192]{1,0:T(8,128)(2,1)} %refs_1_.1, bf16[12,16]{1,0:T(8,128)(2,1)} %refs_2_.1, bf16[3,2,16]{2,1,0:T(2,128)(2,1)} %bitcast.16, ...), custom_call_target="tpu_custom_call" | custom-call | tf_op jit(solution)/shard_map/pack/pallas_call | solution.py:34
  3.3 3.0 %collective-permute-start.2 = (bf16[208,576]{1,0:T(8,128)(2,1)}, bf16[208,576]{1,0:T(8,128)(2,1)S(1)}, u32[]{:S(2)}, u32[]{:S(2)}) collective-permute-start(bf16[208,576]{1,0:T(8,128)(2,1)} %get-tuple-element.138.refs_0_), channel_id=1, source_target_pairs={{0,8},{4,20},{8,0},{12,28},{16,24},{20,4},{24,16},{28,12},{1,9},{5... | collective-permute-start | bytes 718856 | tf_op jit(solution)/shard_map/ppermute | solution.py:617
  6.3 1.5 %collective-permute-start.3 = (bf16[112,576]{1,0:T(8,128)(2,1)}, bf16[112,576]{1,0:T(8,128)(2,1)S(1)}, u32[]{:S(2)}, u32[]{:S(2)}) collective-permute-start(bf16[112,576]{1,0:T(8,128)(2,1)} %get-tuple-element.139), channel_id=1, source_target_pairs={{0,24},{8,16},{16,8},{24,0},{1,25},{9,17},{17,9},{25,1},{2,26},{10... | collective-permute-start | bytes 387080 | tf_op jit(solution)/shard_map/ppermute | solution.py:613
  7.7 1.6 %collective-permute-start.4 = (bf16[192,192]{1,0:T(8,128)(2,1)}, bf16[192,192]{1,0:T(8,128)(2,1)S(1)}, u32[]{:S(2)}, u32[]{:S(2)}) collective-permute-start(bf16[192,192]{1,0:T(8,128)(2,1)} %get-tuple-element.140.proj_t), channel_id=1, source_target_pairs={{0,1},{4,7},{1,0},{5,6},{2,3},{6,5},{3,2},{7,4},{8,9},{12,15},{9,8... | collective-permute-start | bytes 221192 | tf_op jit(solution)/shard_map/ppermute | solution.py:627
  9.3 2.6 %collective-permute-start.5 = (bf16[96,192]{1,0:T(8,128)(2,1)}, bf16[96,192]{1,0:T(8,128)(2,1)S(1)}, u32[]{:S(2)}, u32[]{:S(2)}) collective-permute-start(bf16[96,192]{1,0:T(8,128)(2,1)} %get-tuple-element.141), channel_id=1, source_target_pairs={{0,2},{1,3},{2,0},{3,1},{4,6},{5,7},{6,4},{7,5},{8,10},{9,11},{10,... | collective-permute-start | bytes 110600 | tf_op jit(solution)/shard_map/ppermute | solution.py:610
  11.9 1.0 copy-done.2
  12.9 1.0 copy-done.3
  14.0 1.6 %collective-permute-start.11 = (bf16[192,1152]{1,0:T(8,128)(2,1)S(1)}, bf16[192,1152]{1,0:T(8,128)(2,1)S(1)}, u32[]{:S(2)}, u32[]{:S(2)}) collective-permute-start(bf16[192,1152]{1,0:T(8,128)(2,1)S(1)} %get-tuple-element.133.feed.refs_0_), channel_id=1, source_target_pairs={{0,8},{4,20},{8,0},{12,28},{16,24},{20,4},{24,16},{28,12},{1,9},{5... | collective-permute-start | bytes 1327112 | tf_op jit(solution)/shard_map/ppermute | solution.py:617
  15.6 1.0 copy-done
  16.6 0.4 cotangent.1.refs_13_.cot
  16.9 0.6 frame.1
  17.6 0.5 collective-permute-start.13
  18.1 0.9 collective-permute-done.13.far_their
  19.0 0.2 pack_rest.1
  19.2 0.5 collective-permute-start.15
  19.8 1.5 %collective-permute-start.14 = (bf16[192,1152]{1,0:T(8,128)(2,1)S(1)}, bf16[192,1152]{1,0:T(8,128)(2,1)S(1)}, u32[]{:S(2)}, u32[]{:S(2)}) collective-permute-start(bf16[192,1152]{1,0:T(8,128)(2,1)S(1)} %get-tuple-element.155.refs_3_), channel_id=1, source_target_pairs={{0,8},{4,20},{8,0},{12,28},{16,24},{20,4},{24,16},{28,12},{1,9},{5... | collective-permute-start | bytes 1327112 | tf_op jit(solution)/shard_map/ppermute | solution.py:617
  21.3 0.5 collective-permute-start.7
  21.8 1.2 %collective-permute-done.7.refs_4_ = bf16[112,576]{1,0:T(8,128)(2,1)S(1)} collective-permute-done((bf16[112,576]{1,0:T(8,128)(2,1)S(1)}, bf16[112,576]{1,0:T(8,128)(2,1)S(1)}, u32[]{:S(2)}, u32[]{:S(2)}) %collective-permute-start.7) | collective-permute-done | bytes 129056 | tf_op jit(solution)/shard_map/ppermute | solution.py:607
  23.0 1.3 %attend.1 = (f32[8,768]{1,0:T(8,128)S(1)}, bf16[4,192,576]{2,1,0:T(8,128)(2,1)S(1)}, bf16[208,768]{1,0:T(8,128)(2,1)S(1)}, bf16[3,208,192]{2,1,0:T(8,128)(2,1)S(...) custom-call(bf16[208,576]{1,0:T(8,128)(2,1)S(1)} %copy-done.4, ...), custom_call_target="tpu_custom_call" | custom-call | tf_op jit(solution)/shard_map/attend/pallas_call | solution.py:34
  24.3 2.0 %collective-permute-start.10 = (bf16[312,128]{1,0:T(8,128)(2,1)S(1)}, bf16[312,128]{1,0:T(8,128)(2,1)S(1)}, u32[]{:S(2)}, u32[]{:S(2)}) collective-permute-start(bf16[312,128]{1,0:T(8,128)(2,1)S(1)} %get-tuple-element.151.refs_8_), channel_id=1, source_target_pairs={{0,3},{1,2},{2,1},{3,0},{4,7},{5,6},{6,5},{7,4},{8,11},{9,10},{10,... | collective-permute-start | bytes 239624 | tf_op jit(solution)/shard_map/ppermute | solution.py:610
  26.3 2.4 %collective-permute-start.8 = (bf16[312,128]{1,0:T(8,128)(2,1)S(1)}, bf16[312,128]{1,0:T(8,128)(2,1)S(1)}, u32[]{:S(2)}, u32[]{:S(2)}) collective-permute-start(bf16[312,128]{1,0:T(8,128)(2,1)S(1)} %get-tuple-element.151.refs_8_), channel_id=1, source_target_pairs={{0,1},{1,0},{2,3},{3,2},{4,5},{5,4},{6,7},{7,6},{8,9},{9,8},{10,11... | collective-permute-start | bytes 239624 | tf_op jit(solution)/shard_map/ppermute | solution.py:610
  28.7 2.8 %collective-permute-done.10.refs_11_ = bf16[312,128]{1,0:T(8,128)(2,1)S(1)} collective-permute-done((bf16[312,128]{1,0:T(8,128)(2,1)S(1)}, bf16[312,128]{1,0:T(8,128)(2,1)S(1)}, u32[]{:S(2)}, u32[]{:S(2)}) %collective-permute-start.10) | collective-permute-done | bytes 79904 | tf_op jit(solution)/shard_map/ppermute | solution.py:610
  31.5 2.5 %collective-permute-done.9.refs_10_ = bf16[312,128]{1,0:T(8,128)(2,1)S(1)} collective-permute-done((bf16[312,128]{1,0:T(8,128)(2,1)S(1)}, bf16[312,128]{1,0:T(8,128)(2,1)S(1)}, u32[]{:S(2)}, u32[]{:S(2)}) %collective-permute-start.9) | collective-permute-done | bytes 79904 | tf_op jit(solution)/shard_map/ppermute | solution.py:610
  34.0 2.6 %collective-permute-done.14.refs_4_ = bf16[192,1152]{1,0:T(8,128)(2,1)S(1)} collective-permute-done((bf16[192,1152]{1,0:T(8,128)(2,1)S(1)}, bf16[192,1152]{1,0:T(8,128)(2,1)S(1)}, u32[]{:S(2)}, u32[]{:S(2)}) %collective-permute-start.14) | collective-permute-done | bytes 442400 | tf_op jit(solution)/shard_map/ppermute | solution.py:617
  36.8 0.4 collective-permute-start.17
  37.3 1.2 %collective-permute-done.16.refs_2_ = bf16[192,1152]{1,0:T(8,128)(2,1)S(1)} collective-permute-done((bf16[192,1152]{1,0:T(8,128)(2,1)S(1)}, bf16[192,1152]{1,0:T(8,128)(2,1)S(1)}, u32[]{:S(2)}, u32[]{:S(2)}) %collective-permute-start.16) | collective-permute-done | bytes 442400 | tf_op jit(solution)/shard_map/ppermute | solution.py:607
  38.5 0.6 collective-permute-done.17.refs_5_
  39.1 0.6 collective-permute-done.18.refs_7_
  39.7 3.1 %feed.1 = (bf16[4,192,2304]{2,1,0:T(8,128)(2,1)S(1)}, bf16[208,768]{1,0:T(8,128)(2,1)S(1)}, f32[208,768]{1,0:T(8,128)S(1)}, bf16[208,768]{1,0:T(8,128)(2,1)S(1)}...) custom-call(bf16[192,1152]{1,0:T(8,128)(2,1)S(1)} %get-tuple-element, ...), custom_call_target="tpu_custom_call" | custom-call | tf_op jit(solution)/shard_map/feed/pallas_call | solution.py:34
  42.9 0.6 proj_grad.1
  43.5 0.2 collective-permute-start.23
  43.7 0.6 down.1
  44.3 0.5 collective-permute-start.22
  44.8 1.6 %collective-permute-start.19 = (bf16[312,128]{1,0:T(8,128)(2,1)S(1)}, bf16[312,128]{1,0:T(8,128)(2,1)S(1)}, u32[]{:S(2)}, u32[]{:S(2)}) collective-permute-start(bf16[312,128]{1,0:T(8,128)(2,1)S(1)} %get-tuple-element.169), channel_id=1, source_target_pairs={{0,1},{1,0},{2,3},{3,2},{4,5},{5,4},{6,7},{7,6},{8,9},{9,8},{10,11... | collective-permute-start | bytes 239624 | tf_op jit(solution)/shard_map/ppermute | solution.py:610
  46.4 1.0 %collective-permute-start.20 = (bf16[312,128]{1,0:T(8,128)(2,1)S(1)}, bf16[312,128]{1,0:T(8,128)(2,1)S(1)}, u32[]{:S(2)}, u32[]{:S(2)}) collective-permute-start(bf16[312,128]{1,0:T(8,128)(2,1)S(1)} %get-tuple-element.170), channel_id=1, source_target_pairs={{0,2},{1,3},{2,0},{3,1},{4,6},{5,7},{6,4},{7,5},{8,10},{9,11},{10,... | collective-permute-start | bytes 239624 | tf_op jit(solution)/shard_map/ppermute | solution.py:610
  47.4 1.8 %collective-permute-start.21 = (bf16[312,128]{1,0:T(8,128)(2,1)S(1)}, bf16[312,128]{1,0:T(8,128)(2,1)S(1)}, u32[]{:S(2)}, u32[]{:S(2)}) collective-permute-start(bf16[312,128]{1,0:T(8,128)(2,1)S(1)} %get-tuple-element.171), channel_id=1, source_target_pairs={{0,3},{1,2},{2,1},{3,0},{4,7},{5,6},{6,5},{7,4},{8,11},{9,10},{10,... | collective-permute-start | bytes 239624 | tf_op jit(solution)/shard_map/ppermute | solution.py:610
  49.2 0.9 feed_grad.1
  50.1 4.4 %collective-permute-done.19.refs_1_ = bf16[312,128]{1,0:T(8,128)(2,1)S(1)} collective-permute-done((bf16[312,128]{1,0:T(8,128)(2,1)S(1)}, bf16[312,128]{1,0:T(8,128)(2,1)S(1)}, u32[]{:S(2)}, u32[]{:S(2)}) %collective-permute-start.19) | collective-permute-done | bytes 79904 | tf_op jit(solution)/shard_map/ppermute | solution.py:610
  54.6 1.6 %collective-permute-done.21.refs_3_ = bf16[312,128]{1,0:T(8,128)(2,1)S(1)} collective-permute-done((bf16[312,128]{1,0:T(8,128)(2,1)S(1)}, bf16[312,128]{1,0:T(8,128)(2,1)S(1)}, u32[]{:S(2)}, u32[]{:S(2)}) %collective-permute-start.21) | collective-permute-done | bytes 79904 | tf_op jit(solution)/shard_map/ppermute | solution.py:610
  56.2 2.0 %back.1 = (bf16[208,576]{1,0:T(8,128)(2,1)S(1)}, f32[1,576]{1,0:T(1,128)S(1)}, f32[112,768]{1,0:T(8,128)S(1)}, bf16[112,768]{1,0:T(8,128)(2,1)S(1)}) custom-call(f32[208,192]{1,0:T(8,128)S(1)} %get-tuple-element.181.refs_0_, bf16[312,128]{1,0:T(8,128)(2,1)S(1)} %collective-permute-done.19.refs_1_, bf16[312,128]{1,0:T(8,128)(2,1)S(1)} %collective-permute-done.20.refs_2_, ...), custom_call_target="tpu_custom_call" | custom-call | tf_op jit(solution)/shard_map/back/pallas_call | solution.py:34
  58.2 0.6 qkv_grad.1
  59.1 1.2 %collective-permute-start.26 = (bf16[192,768]{1,0:T(8,128)(2,1)S(1)}, bf16[192,768]{1,0:T(8,128)(2,1)S(1)}, u32[]{:S(2)}, u32[]{:S(2)}) collective-permute-start(bf16[192,768]{1,0:T(8,128)(2,1)S(1)} %get-tuple-element.194), channel_id=1, source_target_pairs={{0,8},{4,20},{8,0},{12,28},{16,24},{20,4},{24,16},{28,12},{1,9},{5... | collective-permute-start | bytes 884744 | tf_op jit(solution)/shard_map/ppermute | solution.py:617
  60.3 1.2 %collective-permute-start.24 = (bf16[112,768]{1,0:T(8,128)(2,1)S(1)}, bf16[112,768]{1,0:T(8,128)(2,1)S(1)}, u32[]{:S(2)}, u32[]{:S(2)}) collective-permute-start(bf16[112,768]{1,0:T(8,128)(2,1)S(1)} %get-tuple-element.191), channel_id=1, source_target_pairs={{0,1},{1,0},{2,3},{3,2},{4,5},{5,4},{6,7},{7,6},{8,9},{9,8},{10,11... | collective-permute-start | bytes 516104 | tf_op jit(solution)/shard_map/ppermute | solution.py:610
  61.5 1.1 %collective-permute-start.25 = (bf16[104,768]{1,0:T(8,128)(2,1)S(1)}, bf16[104,768]{1,0:T(8,128)(2,1)S(1)}, u32[]{:S(2)}, u32[]{:S(2)}) collective-permute-start(bf16[104,768]{1,0:T(8,128)(2,1)S(1)} %out_pair.1.own), channel_id=1, source_target_pairs={{0,3},{1,2},{2,1},{3,0},{4,7},{5,6},{6,5},{7,4},{8,11},{9,10},{10,... | collective-permute-start | bytes 479240 | tf_op jit(solution)/shard_map/ppermute | solution.py:610
  62.7 2.0 %collective-permute-start.27 = (bf16[96,768]{1,0:T(8,128)(2,1)S(1)}, bf16[96,768]{1,0:T(8,128)(2,1)S(1)}, u32[]{:S(2)}, u32[]{:S(2)}) collective-permute-start(bf16[96,768]{1,0:T(8,128)(2,1)S(1)} %get-tuple-element.195), channel_id=1, source_target_pairs={{0,24},{8,16},{16,8},{24,0},{1,25},{9,17},{17,9},{25,1},{2,26},{10... | collective-permute-start | bytes 442376 | tf_op jit(solution)/shard_map/ppermute | solution.py:613
  64.7 5.0 %collective-permute-done.27.refs_2_ = bf16[96,768]{1,0:T(8,128)(2,1)S(1)} collective-permute-done((bf16[96,768]{1,0:T(8,128)(2,1)S(1)}, bf16[96,768]{1,0:T(8,128)(2,1)S(1)}, u32[]{:S(2)}, u32[]{:S(2)}) %collective-permute-start.27) | collective-permute-done | bytes 147488 | tf_op jit(solution)/shard_map/ppermute | solution.py:613
  69.6 1.4 %collective-permute-done.25.received = bf16[104,768]{1,0:T(8,128)(2,1)S(1)} collective-permute-done((bf16[104,768]{1,0:T(8,128)(2,1)S(1)}, bf16[104,768]{1,0:T(8,128)(2,1)S(1)}, u32[]{:S(2)}, u32[]{:S(2)}) %collective-permute-start.25) | collective-permute-done | bytes 159776 | tf_op jit(solution)/shard_map/ppermute | solution.py:610
  71.1 0.3 split.1
  71.4 1.3 %collective-permute-start.31 = (bf16[2,96,2176]{2,1,0:T(8,128)(2,1)S(1)}, bf16[2,96,2176]{2,1,0:T(8,128)(2,1)S(1)}, u32[]{:S(2)}, u32[]{:S(2)}) collective-permute-start(bf16[2,96,2176]{2,1,0:T(8,128)(2,1)S(1)} %get-tuple-element.210), channel_id=1, source_target_pairs={{0,8},{4,20},{8,0},{12,28},{16,24},{20,4},{24,16},{28,12},{1,9},{5... | collective-permute-start | bytes 2506760 | tf_op jit(solution)/shard_map/ppermute | solution.py:617
  72.7 0.3 out_total.1
  73.0 0.9 collective-permute-start.30
  73.9 1.0 %collective-permute-start.29 = (bf16[112,768]{1,0:T(8,128)(2,1)S(1)}, bf16[112,768]{1,0:T(8,128)(2,1)S(1)}, u32[]{:S(2)}, u32[]{:S(2)}) collective-permute-start(bf16[112,768]{1,0:T(8,128)(2,1)S(1)} %in_pair.1.own), channel_id=1, source_target_pairs={{0,3},{1,2},{2,1},{3,0},{4,7},{5,6},{6,5},{7,4},{8,11},{9,10},{10,... | collective-permute-start | bytes 516104 | tf_op jit(solution)/shard_map/ppermute | solution.py:610
  75.0 9.6 %collective-permute-done.29.received = bf16[112,768]{1,0:T(8,128)(2,1)S(1)} collective-permute-done((bf16[112,768]{1,0:T(8,128)(2,1)S(1)}, bf16[112,768]{1,0:T(8,128)(2,1)S(1)}, u32[]{:S(2)}, u32[]{:S(2)}) %collective-permute-start.29) | collective-permute-done | bytes 172064 | tf_op jit(solution)/shard_map/ppermute | solution.py:610
  84.9 1.8 %collective-permute-start.34 = (bf16[96,2176]{1,0:T(8,128)(2,1)S(1)}, bf16[96,2176]{1,0:T(8,128)(2,1)S(1)}, u32[]{:S(2)}, u32[]{:S(2)}) collective-permute-start(bf16[96,2176]{1,0:T(8,128)(2,1)S(1)} %get-tuple-element.219), channel_id=1, source_target_pairs={{0,16},{4,12},{8,24},{12,4},{16,0},{20,28},{24,8},{28,20},{1,17},{... | collective-permute-start | bytes 1253384 | tf_op jit(solution)/shard_map/ppermute | solution.py:617
  86.7 2.2 %collective-permute-start.33 = (bf16[48,768]{1,0:T(8,128)(2,1)S(1)}, bf16[48,768]{1,0:T(8,128)(2,1)S(1)}, u32[]{:S(2)}, u32[]{:S(2)}) collective-permute-start(bf16[48,768]{1,0:T(8,128)(2,1)S(1)} %get-tuple-element.216), channel_id=1, source_target_pairs={{0,3},{1,2},{2,1},{3,0},{4,7},{5,6},{6,5},{7,4},{8,11},{9,10},{10,... | collective-permute-start | bytes 221192 | tf_op jit(solution)/shard_map/ppermute | solution.py:610
  89.0 1.3 %collective-permute-start.36 = (bf16[16,576]{1,0:T(8,128)(2,1)S(1)}, bf16[16,576]{1,0:T(8,128)(2,1)S(1)}, u32[]{:S(2)}, u32[]{:S(2)}) collective-permute-start(bf16[16,576]{1,0:T(8,128)(2,1)S(1)} %get-tuple-element.221), channel_id=1, source_target_pairs={{0,8},{4,20},{8,0},{12,28},{16,24},{20,4},{24,16},{28,12},{1,9},{5... | collective-permute-start | bytes 55304 | tf_op jit(solution)/shard_map/ppermute | solution.py:617
  90.3 0.7 collective-permute-start.37
  91.1 3.7 %collective-permute-done.33.refs_1_ = bf16[48,768]{1,0:T(8,128)(2,1)S(1)} collective-permute-done((bf16[48,768]{1,0:T(8,128)(2,1)S(1)}, bf16[48,768]{1,0:T(8,128)(2,1)S(1)}, u32[]{:S(2)}, u32[]{:S(2)}) %collective-permute-start.33) | collective-permute-done | bytes 73760 | tf_op jit(solution)/shard_map/ppermute | solution.py:610
  94.8 0.2 collective-permute-done.37.far
  95.0 0.2 swap.1
  95.4 0.6 collective-permute-start.39
  96.1 1.5 %collective-permute-done.40.refs_4_ = bf16[112,576]{1,0:T(8,128)(2,1)S(1)} collective-permute-done((bf16[112,576]{1,0:T(8,128)(2,1)S(1)}, bf16[112,576]{1,0:T(8,128)(2,1)S(1)}, u32[]{:S(2)}, u32[]{:S(2)}) %collective-permute-start.40) | collective-permute-done | bytes 129056 | tf_op jit(solution)/shard_map/ppermute | solution.py:607
  97.6 2.0 %final.1 = (bf16[98,2,768]{2,1,0:T(2,128)(2,1)}, f32[98,2,768]{2,1,0:T(2,128)}, f32[192,192]{1,0:T(8,128)}, f32[192,768]{1,0:T(8,128)}, f32[192,768]{1,0:T(8,128...) custom-call(f32[2,104,768]{2,1,0:T(8,128)S(1)} %get-tuple-element.22, ...), custom_call_target="tpu_custom_call" | custom-call | tf_op jit(solution)/shard_map/final/pallas_call | solution.py:34
  (54 shorter events, 1.7 us)
Async XLA Ops:
  0.6 16.3 %copy-start.1 = (bf16[2,98,768]{2,0,1:T(2,128)(2,1)S(1)}, bf16[2,98,768]{2,0,1:T(2,128)(2,1)}, u32[]{:S(2)}) copy-start(bf16[2,98,768]{2,0,1:T(2,128)(2,1)} %param.14) | copy-start | bytes 903172
  0.7 2.6 %collective-permute-start = (bf16[98,2,768]{2,1,0:T(2,128)(2,1)}, bf16[98,2,768]{2,1,0:T(2,128)(2,1)S(1)}, u32[]{:S(2)}, u32[]{:S(2)}) collective-permute-start(bf16[98,2,768]{2,1,0:T(2,128)(2,1)} %bitcast.12), channel_id=1, source_target_pairs={{0,4},{4,0},{1,5},{5,1},{2,6},{6,2},{3,7},{7,3},{8,12},{12,8},{9,1... | collective-permute-start | bytes 903176 | tf_op jit(solution)/shard_map/ppermute | solution.py:607
  1.2 2.1 %collective-permute-start.1 = (bf16[98,2,768]{2,1,0:T(2,128)(2,1)}, bf16[98,2,768]{2,1,0:T(2,128)(2,1)S(1)}, u32[]{:S(2)}, u32[]{:S(2)}) collective-permute-start(bf16[98,2,768]{2,1,0:T(2,128)(2,1)} %bitcast.10), channel_id=1, source_target_pairs={{0,4},{4,0},{1,5},{5,1},{2,6},{6,2},{3,7},{7,3},{8,12},{12,8},{9,1... | collective-permute-start | bytes 903176 | tf_op jit(solution)/shard_map/ppermute | solution.py:607
  3.3 14.3 %collective-permute-start.2 = (bf16[208,576]{1,0:T(8,128)(2,1)}, bf16[208,576]{1,0:T(8,128)(2,1)S(1)}, u32[]{:S(2)}, u32[]{:S(2)}) collective-permute-start(bf16[208,576]{1,0:T(8,128)(2,1)} %get-tuple-element.138.refs_0_), channel_id=1, source_target_pairs={{0,8},{4,20},{8,0},{12,28},{16,24},{20,4},{24,16},{28,12},{1,9},{5... | collective-permute-start | bytes 718856 | tf_op jit(solution)/shard_map/ppermute | solution.py:617
  6.3 11.3 %collective-permute-start.3 = (bf16[112,576]{1,0:T(8,128)(2,1)}, bf16[112,576]{1,0:T(8,128)(2,1)S(1)}, u32[]{:S(2)}, u32[]{:S(2)}) collective-permute-start(bf16[112,576]{1,0:T(8,128)(2,1)} %get-tuple-element.139), channel_id=1, source_target_pairs={{0,24},{8,16},{16,8},{24,0},{1,25},{9,17},{17,9},{25,1},{2,26},{10... | collective-permute-start | bytes 387080 | tf_op jit(solution)/shard_map/ppermute | solution.py:613
  7.7 9.8 %collective-permute-start.4 = (bf16[192,192]{1,0:T(8,128)(2,1)}, bf16[192,192]{1,0:T(8,128)(2,1)S(1)}, u32[]{:S(2)}, u32[]{:S(2)}) collective-permute-start(bf16[192,192]{1,0:T(8,128)(2,1)} %get-tuple-element.140.proj_t), channel_id=1, source_target_pairs={{0,1},{4,7},{1,0},{5,6},{2,3},{6,5},{3,2},{7,4},{8,9},{12,15},{9,8... | collective-permute-start | bytes 221192 | tf_op jit(solution)/shard_map/ppermute | solution.py:627
  9.3 8.2 %collective-permute-start.5 = (bf16[96,192]{1,0:T(8,128)(2,1)}, bf16[96,192]{1,0:T(8,128)(2,1)S(1)}, u32[]{:S(2)}, u32[]{:S(2)}) collective-permute-start(bf16[96,192]{1,0:T(8,128)(2,1)} %get-tuple-element.141), channel_id=1, source_target_pairs={{0,2},{1,3},{2,0},{3,1},{4,6},{5,7},{6,4},{7,5},{8,10},{9,11},{10,... | collective-permute-start | bytes 110600 | tf_op jit(solution)/shard_map/ppermute | solution.py:610
  11.9 1.0 copy-start.2
  12.9 1.0 copy-start.3
  13.8 5.2 %copy-start.5 = (bf16[192,192]{1,0:T(8,128)(2,1)S(1)}, bf16[192,192]{1,0:T(8,128)(2,1)}, u32[]{:S(2)}) copy-start(bf16[192,192]{1,0:T(8,128)(2,1)} %get-tuple-element.140.proj_t) | copy-start | bytes 221188
  13.8 9.2 %copy-start.4 = (bf16[208,576]{1,0:T(8,128)(2,1)S(1)}, bf16[208,576]{1,0:T(8,128)(2,1)}, u32[]{:S(2)}) copy-start(bf16[208,576]{1,0:T(8,128)(2,1)} %get-tuple-element.138.refs_0_) | copy-start | bytes 718852
  14.0 12.3 %collective-permute-start.11 = (bf16[192,1152]{1,0:T(8,128)(2,1)S(1)}, bf16[192,1152]{1,0:T(8,128)(2,1)S(1)}, u32[]{:S(2)}, u32[]{:S(2)}) collective-permute-start(bf16[192,1152]{1,0:T(8,128)(2,1)S(1)} %get-tuple-element.133.feed.refs_0_), channel_id=1, source_target_pairs={{0,8},{4,20},{8,0},{12,28},{16,24},{20,4},{24,16},{28,12},{1,9},{5... | collective-permute-start | bytes 1327112 | tf_op jit(solution)/shard_map/ppermute | solution.py:617
  15.6 1.0 copy-start
  17.5 1.5 %collective-permute-start.12 = (bf16[192,192]{1,0:T(8,128)(2,1)S(1)}, bf16[192,192]{1,0:T(8,128)(2,1)S(1)}, u32[]{:S(2)}, u32[]{:S(2)}) collective-permute-start(bf16[192,192]{1,0:T(8,128)(2,1)S(1)} %collective-permute-done.4.near_in), channel_id=1, source_target_pairs={{0,4},{4,0},{1,5},{5,1},{2,6},{6,2},{3,7},{7,3},{8,12},{12,8},{9,1... | collective-permute-start | bytes 221192 | tf_op jit(solution)/shard_map/ppermute | solution.py:607
  17.6 1.4 %collective-permute-start.13 = (bf16[96,192]{1,0:T(8,128)(2,1)S(1)}, bf16[96,192]{1,0:T(8,128)(2,1)S(1)}, u32[]{:S(2)}, u32[]{:S(2)}) collective-permute-start(bf16[96,192]{1,0:T(8,128)(2,1)S(1)} %collective-permute-done.5.far_in), channel_id=1, source_target_pairs={{0,4},{4,0},{1,5},{5,1},{2,6},{6,2},{3,7},{7,3},{8,12},{12,8},{9,1... | collective-permute-start | bytes 110600 | tf_op jit(solution)/shard_map/ppermute | solution.py:607
  19.2 14.8 %collective-permute-start.15 = (bf16[96,2304]{1,0:T(8,128)(2,1)S(1)}, bf16[96,2304]{1,0:T(8,128)(2,1)S(1)}, u32[]{:S(2)}, u32[]{:S(2)}) collective-permute-start(bf16[96,2304]{1,0:T(8,128)(2,1)S(1)} %get-tuple-element.156), channel_id=1, source_target_pairs={{0,24},{8,16},{16,8},{24,0},{1,25},{9,17},{17,9},{25,1},{2,26},{10... | collective-permute-start | bytes 1327112 | tf_op jit(solution)/shard_map/ppermute | solution.py:613
  19.8 16.9 %collective-permute-start.14 = (bf16[192,1152]{1,0:T(8,128)(2,1)S(1)}, bf16[192,1152]{1,0:T(8,128)(2,1)S(1)}, u32[]{:S(2)}, u32[]{:S(2)}) collective-permute-start(bf16[192,1152]{1,0:T(8,128)(2,1)S(1)} %get-tuple-element.155.refs_3_), channel_id=1, source_target_pairs={{0,8},{4,20},{8,0},{12,28},{16,24},{20,4},{24,16},{28,12},{1,9},{5... | collective-permute-start | bytes 1327112 | tf_op jit(solution)/shard_map/ppermute | solution.py:617
  21.3 1.8 %collective-permute-start.6 = (bf16[208,576]{1,0:T(8,128)(2,1)S(1)}, bf16[208,576]{1,0:T(8,128)(2,1)S(1)}, u32[]{:S(2)}, u32[]{:S(2)}) collective-permute-start(bf16[208,576]{1,0:T(8,128)(2,1)S(1)} %collective-permute-done.2.refs_1_), channel_id=1, source_target_pairs={{0,4},{4,0},{1,5},{5,1},{2,6},{6,2},{3,7},{7,3},{8,12},{12,8},{9,1... | collective-permute-start | bytes 718856 | tf_op jit(solution)/shard_map/ppermute | solution.py:607
  21.3 1.7 %collective-permute-start.7 = (bf16[112,576]{1,0:T(8,128)(2,1)S(1)}, bf16[112,576]{1,0:T(8,128)(2,1)S(1)}, u32[]{:S(2)}, u32[]{:S(2)}) collective-permute-start(bf16[112,576]{1,0:T(8,128)(2,1)S(1)} %collective-permute-done.3.refs_3_), channel_id=1, source_target_pairs={{0,4},{4,0},{1,5},{5,1},{2,6},{6,2},{3,7},{7,3},{8,12},{12,8},{9,1... | collective-permute-start | bytes 387080 | tf_op jit(solution)/shard_map/ppermute | solution.py:607
  24.3 7.2 %collective-permute-start.10 = (bf16[312,128]{1,0:T(8,128)(2,1)S(1)}, bf16[312,128]{1,0:T(8,128)(2,1)S(1)}, u32[]{:S(2)}, u32[]{:S(2)}) collective-permute-start(bf16[312,128]{1,0:T(8,128)(2,1)S(1)} %get-tuple-element.151.refs_8_), channel_id=1, source_target_pairs={{0,3},{1,2},{2,1},{3,0},{4,7},{5,6},{6,5},{7,4},{8,11},{9,10},{10,... | collective-permute-start | bytes 239624 | tf_op jit(solution)/shard_map/ppermute | solution.py:610
  26.3 7.7 %collective-permute-start.9 = (bf16[312,128]{1,0:T(8,128)(2,1)S(1)}, bf16[312,128]{1,0:T(8,128)(2,1)S(1)}, u32[]{:S(2)}, u32[]{:S(2)}) collective-permute-start(bf16[312,128]{1,0:T(8,128)(2,1)S(1)} %get-tuple-element.151.refs_8_), channel_id=1, source_target_pairs={{0,2},{1,3},{2,0},{3,1},{4,6},{5,7},{6,4},{7,5},{8,10},{9,11},{10,... | collective-permute-start | bytes 239624 | tf_op jit(solution)/shard_map/ppermute | solution.py:610
  26.3 7.7 %collective-permute-start.8 = (bf16[312,128]{1,0:T(8,128)(2,1)S(1)}, bf16[312,128]{1,0:T(8,128)(2,1)S(1)}, u32[]{:S(2)}, u32[]{:S(2)}) collective-permute-start(bf16[312,128]{1,0:T(8,128)(2,1)S(1)} %get-tuple-element.151.refs_8_), channel_id=1, source_target_pairs={{0,1},{1,0},{2,3},{3,2},{4,5},{5,4},{6,7},{7,6},{8,9},{9,8},{10,11... | collective-permute-start | bytes 239624 | tf_op jit(solution)/shard_map/ppermute | solution.py:610
  36.7 1.8 %collective-permute-start.16 = (bf16[192,1152]{1,0:T(8,128)(2,1)S(1)}, bf16[192,1152]{1,0:T(8,128)(2,1)S(1)}, u32[]{:S(2)}, u32[]{:S(2)}) collective-permute-start(bf16[192,1152]{1,0:T(8,128)(2,1)S(1)} %collective-permute-done.11.refs_1_), channel_id=1, source_target_pairs={{0,4},{4,0},{1,5},{5,1},{2,6},{6,2},{3,7},{7,3},{8,12},{12,8},{9,1... | collective-permute-start | bytes 1327112 | tf_op jit(solution)/shard_map/ppermute | solution.py:607
  36.8 2.3 %collective-permute-start.17 = (bf16[192,1152]{1,0:T(8,128)(2,1)S(1)}, bf16[192,1152]{1,0:T(8,128)(2,1)S(1)}, u32[]{:S(2)}, u32[]{:S(2)}) collective-permute-start(bf16[192,1152]{1,0:T(8,128)(2,1)S(1)} %collective-permute-done.14.refs_4_), channel_id=1, source_target_pairs={{0,4},{4,0},{1,5},{5,1},{2,6},{6,2},{3,7},{7,3},{8,12},{12,8},{9,1... | collective-permute-start | bytes 1327112 | tf_op jit(solution)/shard_map/ppermute | solution.py:607
  37.2 2.5 %collective-permute-start.18 = (bf16[96,2304]{1,0:T(8,128)(2,1)S(1)}, bf16[96,2304]{1,0:T(8,128)(2,1)S(1)}, u32[]{:S(2)}, u32[]{:S(2)}) collective-permute-start(bf16[96,2304]{1,0:T(8,128)(2,1)S(1)} %collective-permute-done.15.refs_6_), channel_id=1, source_target_pairs={{0,4},{4,0},{1,5},{5,1},{2,6},{6,2},{3,7},{7,3},{8,12},{12,8},{9,1... | collective-permute-start | bytes 1327112 | tf_op jit(solution)/shard_map/ppermute | solution.py:607
  43.5 12.8 %collective-permute-start.23 = (bf16[288,768]{1,0:T(8,128)(2,1)S(1)}, bf16[288,768]{1,0:T(8,128)(2,1)S(1)}, u32[]{:S(2)}, u32[]{:S(2)}) collective-permute-start(bf16[288,768]{1,0:T(8,128)(2,1)S(1)} %get-tuple-element.179), channel_id=1, source_target_pairs={{0,4},{4,0},{1,5},{5,1},{2,6},{6,2},{3,7},{7,3},{8,12},{12,8},{9,1... | collective-permute-start | bytes 1327112 | tf_op jit(solution)/shard_map/ppermute | solution.py:607
  44.3 11.9 %collective-permute-start.22 = (bf16[104,768]{1,0:T(8,128)(2,1)S(1)}, bf16[104,768]{1,0:T(8,128)(2,1)S(1)}, u32[]{:S(2)}, u32[]{:S(2)}) collective-permute-start(bf16[104,768]{1,0:T(8,128)(2,1)S(1)} %get-tuple-element.172), channel_id=1, source_target_pairs={{0,1},{1,0},{2,3},{3,2},{4,5},{5,4},{6,7},{7,6},{8,9},{9,8},{10,11... | collective-permute-start | bytes 479240 | tf_op jit(solution)/shard_map/ppermute | solution.py:610
  44.8 9.8 %collective-permute-start.19 = (bf16[312,128]{1,0:T(8,128)(2,1)S(1)}, bf16[312,128]{1,0:T(8,128)(2,1)S(1)}, u32[]{:S(2)}, u32[]{:S(2)}) collective-permute-start(bf16[312,128]{1,0:T(8,128)(2,1)S(1)} %get-tuple-element.169), channel_id=1, source_target_pairs={{0,1},{1,0},{2,3},{3,2},{4,5},{5,4},{6,7},{7,6},{8,9},{9,8},{10,11... | collective-permute-start | bytes 239624 | tf_op jit(solution)/shard_map/ppermute | solution.py:610
  46.4 8.2 %collective-permute-start.20 = (bf16[312,128]{1,0:T(8,128)(2,1)S(1)}, bf16[312,128]{1,0:T(8,128)(2,1)S(1)}, u32[]{:S(2)}, u32[]{:S(2)}) collective-permute-start(bf16[312,128]{1,0:T(8,128)(2,1)S(1)} %get-tuple-element.170), channel_id=1, source_target_pairs={{0,2},{1,3},{2,0},{3,1},{4,6},{5,7},{6,4},{7,5},{8,10},{9,11},{10,... | collective-permute-start | bytes 239624 | tf_op jit(solution)/shard_map/ppermute | solution.py:610
  47.4 8.8 %collective-permute-start.21 = (bf16[312,128]{1,0:T(8,128)(2,1)S(1)}, bf16[312,128]{1,0:T(8,128)(2,1)S(1)}, u32[]{:S(2)}, u32[]{:S(2)}) collective-permute-start(bf16[312,128]{1,0:T(8,128)(2,1)S(1)} %get-tuple-element.171), channel_id=1, source_target_pairs={{0,3},{1,2},{2,1},{3,0},{4,7},{5,6},{6,5},{7,4},{8,11},{9,10},{10,... | collective-permute-start | bytes 239624 | tf_op jit(solution)/shard_map/ppermute | solution.py:610
  58.9 12.2 %collective-permute-start.28 = (bf16[384,2176]{1,0:T(8,128)(2,1)S(1)}, bf16[384,2176]{1,0:T(8,128)(2,1)S(1)}, u32[]{:S(2)}, u32[]{:S(2)}) collective-permute-start(bf16[384,2176]{1,0:T(8,128)(2,1)S(1)} %get-tuple-element.199), channel_id=1, source_target_pairs={{0,4},{4,0},{1,5},{5,1},{2,6},{6,2},{3,7},{7,3},{8,12},{12,8},{9,1... | collective-permute-start | bytes 5013512 | tf_op jit(solution)/shard_map/ppermute | solution.py:607
  59.1 12.0 %collective-permute-start.26 = (bf16[192,768]{1,0:T(8,128)(2,1)S(1)}, bf16[192,768]{1,0:T(8,128)(2,1)S(1)}, u32[]{:S(2)}, u32[]{:S(2)}) collective-permute-start(bf16[192,768]{1,0:T(8,128)(2,1)S(1)} %get-tuple-element.194), channel_id=1, source_target_pairs={{0,8},{4,20},{8,0},{12,28},{16,24},{20,4},{24,16},{28,12},{1,9},{5... | collective-permute-start | bytes 884744 | tf_op jit(solution)/shard_map/ppermute | solution.py:617
  60.3 10.8 %collective-permute-start.24 = (bf16[112,768]{1,0:T(8,128)(2,1)S(1)}, bf16[112,768]{1,0:T(8,128)(2,1)S(1)}, u32[]{:S(2)}, u32[]{:S(2)}) collective-permute-start(bf16[112,768]{1,0:T(8,128)(2,1)S(1)} %get-tuple-element.191), channel_id=1, source_target_pairs={{0,1},{1,0},{2,3},{3,2},{4,5},{5,4},{6,7},{7,6},{8,9},{9,8},{10,11... | collective-permute-start | bytes 516104 | tf_op jit(solution)/shard_map/ppermute | solution.py:610
  61.5 9.5 %collective-permute-start.25 = (bf16[104,768]{1,0:T(8,128)(2,1)S(1)}, bf16[104,768]{1,0:T(8,128)(2,1)S(1)}, u32[]{:S(2)}, u32[]{:S(2)}) collective-permute-start(bf16[104,768]{1,0:T(8,128)(2,1)S(1)} %out_pair.1.own), channel_id=1, source_target_pairs={{0,3},{1,2},{2,1},{3,0},{4,7},{5,6},{6,5},{7,4},{8,11},{9,10},{10,... | collective-permute-start | bytes 479240 | tf_op jit(solution)/shard_map/ppermute | solution.py:610
  62.7 7.0 %collective-permute-start.27 = (bf16[96,768]{1,0:T(8,128)(2,1)S(1)}, bf16[96,768]{1,0:T(8,128)(2,1)S(1)}, u32[]{:S(2)}, u32[]{:S(2)}) collective-permute-start(bf16[96,768]{1,0:T(8,128)(2,1)S(1)} %get-tuple-element.195), channel_id=1, source_target_pairs={{0,24},{8,16},{16,8},{24,0},{1,25},{9,17},{17,9},{25,1},{2,26},{10... | collective-permute-start | bytes 442376 | tf_op jit(solution)/shard_map/ppermute | solution.py:613
  71.4 13.1 %collective-permute-start.31 = (bf16[2,96,2176]{2,1,0:T(8,128)(2,1)S(1)}, bf16[2,96,2176]{2,1,0:T(8,128)(2,1)S(1)}, u32[]{:S(2)}, u32[]{:S(2)}) collective-permute-start(bf16[2,96,2176]{2,1,0:T(8,128)(2,1)S(1)} %get-tuple-element.210), channel_id=1, source_target_pairs={{0,8},{4,20},{8,0},{12,28},{16,24},{20,4},{24,16},{28,12},{1,9},{5... | collective-permute-start | bytes 2506760 | tf_op jit(solution)/shard_map/ppermute | solution.py:617
  73.0 11.5 %collective-permute-start.30 = (bf16[200,768]{1,0:T(8,128)(2,1)S(1)}, bf16[200,768]{1,0:T(8,128)(2,1)S(1)}, u32[]{:S(2)}, u32[]{:S(2)}) collective-permute-start(bf16[200,768]{1,0:T(8,128)(2,1)S(1)} %get-tuple-element.204.out_own), channel_id=1, source_target_pairs={{0,1},{1,0},{2,3},{3,2},{4,5},{5,4},{6,7},{7,6},{8,9},{9,8},{10,11... | collective-permute-start | bytes 921608 | tf_op jit(solution)/shard_map/ppermute | solution.py:610
  73.9 10.6 %collective-permute-start.29 = (bf16[112,768]{1,0:T(8,128)(2,1)S(1)}, bf16[112,768]{1,0:T(8,128)(2,1)S(1)}, u32[]{:S(2)}, u32[]{:S(2)}) collective-permute-start(bf16[112,768]{1,0:T(8,128)(2,1)S(1)} %in_pair.1.own), channel_id=1, source_target_pairs={{0,3},{1,2},{2,1},{3,0},{4,7},{5,6},{6,5},{7,4},{8,11},{9,10},{10,... | collective-permute-start | bytes 516104 | tf_op jit(solution)/shard_map/ppermute | solution.py:610
  84.6 4.3 %collective-permute-start.35 = (f32[144,768]{1,0:T(8,128)S(1)}, f32[144,768]{1,0:T(8,128)S(1)}, u32[]{:S(2)}, u32[]{:S(2)}) collective-permute-start(f32[144,768]{1,0:T(8,128)S(1)} %get-tuple-element.220.vec), channel_id=1, source_target_pairs={{0,4},{4,0},{1,5},{5,1},{2,6},{6,2},{3,7},{7,3},{8,12},{12,8},{9,1... | collective-permute-start | bytes 1327112 | tf_op jit(solution)/shard_map/ppermute | solution.py:607
  84.9 9.9 %collective-permute-start.34 = (bf16[96,2176]{1,0:T(8,128)(2,1)S(1)}, bf16[96,2176]{1,0:T(8,128)(2,1)S(1)}, u32[]{:S(2)}, u32[]{:S(2)}) collective-permute-start(bf16[96,2176]{1,0:T(8,128)(2,1)S(1)} %get-tuple-element.219), channel_id=1, source_target_pairs={{0,16},{4,12},{8,24},{12,4},{16,0},{20,28},{24,8},{28,20},{1,17},{... | collective-permute-start | bytes 1253384 | tf_op jit(solution)/shard_map/ppermute | solution.py:617
  86.7 8.1 %collective-permute-start.32 = (bf16[104,768]{1,0:T(8,128)(2,1)S(1)}, bf16[104,768]{1,0:T(8,128)(2,1)S(1)}, u32[]{:S(2)}, u32[]{:S(2)}) collective-permute-start(bf16[104,768]{1,0:T(8,128)(2,1)S(1)} %get-tuple-element.214.in_own), channel_id=1, source_target_pairs={{0,1},{1,0},{2,3},{3,2},{4,5},{5,4},{6,7},{7,6},{8,9},{9,8},{10,11... | collective-permute-start | bytes 479240 | tf_op jit(solution)/shard_map/ppermute | solution.py:610
  86.7 8.1 %collective-permute-start.33 = (bf16[48,768]{1,0:T(8,128)(2,1)S(1)}, bf16[48,768]{1,0:T(8,128)(2,1)S(1)}, u32[]{:S(2)}, u32[]{:S(2)}) collective-permute-start(bf16[48,768]{1,0:T(8,128)(2,1)S(1)} %get-tuple-element.216), channel_id=1, source_target_pairs={{0,3},{1,2},{2,1},{3,0},{4,7},{5,6},{6,5},{7,4},{8,11},{9,10},{10,... | collective-permute-start | bytes 221192 | tf_op jit(solution)/shard_map/ppermute | solution.py:610
  89.0 5.8 %collective-permute-start.36 = (bf16[16,576]{1,0:T(8,128)(2,1)S(1)}, bf16[16,576]{1,0:T(8,128)(2,1)S(1)}, u32[]{:S(2)}, u32[]{:S(2)}) collective-permute-start(bf16[16,576]{1,0:T(8,128)(2,1)S(1)} %get-tuple-element.221), channel_id=1, source_target_pairs={{0,8},{4,20},{8,0},{12,28},{16,24},{20,4},{24,16},{28,12},{1,9},{5... | collective-permute-start | bytes 55304 | tf_op jit(solution)/shard_map/ppermute | solution.py:617
  90.3 4.7 %collective-permute-start.37 = (bf16[16,576]{1,0:T(8,128)(2,1)S(1)}, bf16[16,576]{1,0:T(8,128)(2,1)S(1)}, u32[]{:S(2)}, u32[]{:S(2)}) collective-permute-start(bf16[16,576]{1,0:T(8,128)(2,1)S(1)} %get-tuple-element.222), channel_id=1, source_target_pairs={{0,24},{8,16},{16,8},{24,0},{1,25},{9,17},{17,9},{25,1},{2,26},{10... | collective-permute-start | bytes 55304 | tf_op jit(solution)/shard_map/ppermute | solution.py:613
  95.2 2.4 %collective-permute-start.38 = (bf16[256,768]{1,0:T(8,128)(2,1)S(1)}, bf16[256,768]{1,0:T(8,128)(2,1)S(1)}, u32[]{:S(2)}, u32[]{:S(2)}) collective-permute-start(bf16[256,768]{1,0:T(8,128)(2,1)S(1)} %get-tuple-element.227), channel_id=1, source_target_pairs={{0,4},{4,0},{1,5},{5,1},{2,6},{6,2},{3,7},{7,3},{8,12},{12,8},{9,1... | collective-permute-start | bytes 1179656 | tf_op jit(solution)/shard_map/ppermute | solution.py:607
  95.4 2.2 %collective-permute-start.39 = (bf16[96,1536]{1,0:T(8,128)(2,1)S(1)}, bf16[96,1536]{1,0:T(8,128)(2,1)S(1)}, u32[]{:S(2)}, u32[]{:S(2)}) collective-permute-start(bf16[96,1536]{1,0:T(8,128)(2,1)S(1)} %get-tuple-element.235), channel_id=1, source_target_pairs={{0,4},{4,0},{1,5},{5,1},{2,6},{6,2},{3,7},{7,3},{8,12},{12,8},{9,1... | collective-permute-start | bytes 884744 | tf_op jit(solution)/shard_map/ppermute | solution.py:607
  96.0 1.6 %collective-permute-start.40 = (bf16[112,576]{1,0:T(8,128)(2,1)S(1)}, bf16[112,576]{1,0:T(8,128)(2,1)S(1)}, u32[]{:S(2)}, u32[]{:S(2)}) collective-permute-start(bf16[112,576]{1,0:T(8,128)(2,1)S(1)} %get-tuple-element.237), channel_id=1, source_target_pairs={{0,4},{4,0},{1,5},{5,1},{2,6},{6,2},{3,7},{7,3},{8,12},{12,8},{9,1... | collective-permute-start | bytes 387080 | tf_op jit(solution)/shard_map/ppermute | solution.py:607

commit v6 on v5

--- a/solution.py
+++ b/solution.py
@@ -100,7 +100,7 @@
         self.tail = self.part // 4
         self.direct = nf == 4
         self.cols = 2 * self.ff + nt * self.inner
-        self.early = 1152 if self.ff == 768 else self.ff
+        self.early = 1280 if self.ff == 768 else self.ff
         self.all_cols = 2 * self.ff + -(-3 * self.inner // 128) * 128
         self.dense = self.rows * self.inner // 128
 
@@ -156,26 +156,30 @@
         out[at : at + up_b.shape[0], UP_AT : UP_AT + up_b.shape[1]] = up_b[...]
         out[at : at + 2 * z.heads, QV_AT : QV_AT + biases.shape[1]] = biases.astype(LOW)
     turned = read(proj).T
-    proj_t[...] = turned.astype(LOW)
+    proj_t[...] = rows_of([turned, jnp.zeros((proj_t.shape[0] - z.part, z.inner), F32)]).astype(LOW)
     proj_half[...] = jnp.where(c == 0, turned[: z.chunk], turned[z.chunk :]).astype(LOW)
 
 
+def cut_kernel(z, value, out):
+    out[...] = value[z.half_of(lax.axis_index("ctx")), :]
+
+
 def pair_kernel(first, second, out):
-    out[0] = first[...]
-    out[1] = second[...]
-
-
-def pack_rest_kernel(z, feed, rest, proj_t, near_in, near_their, far_in, far_their, near, far, scratch):
+    rows = first.shape[0]
+    out[0, :rows, :] = first[...]
+    out[1, :rows, :] = second[...]
+    out[:, rows:, :] = jnp.zeros((2, out.shape[1] - rows, out.shape[2]), LOW)
+
+
+def pack_rest_kernel(z, rest, proj_t, near_in, near_their, far_in, far_their, near, scratch):
     c, t = lax.axis_index("ctx"), lax.axis_index("tp")
-    scratch[t] = read(proj_t)
-    scratch[t ^ (1 + 2 * c)] = read(near_in)
-    scratch[t ^ (3 - 2 * c)] = read(near_their)
-    scratch[t ^ 2, z.half_of(c), :] = read(far_in)
-    scratch[t ^ 2, z.half_of(1 - c), :] = read(far_their)
+    scratch[t] = proj_t[: z.part, :].astype(F32)
+    scratch[t ^ (1 + 2 * c)] = near_in[: z.part, :].astype(F32)
+    scratch[t ^ (3 - 2 * c)] = near_their[: z.part, :].astype(F32)
+    scratch[t ^ 2, z.half_of(c), :] = far_in[: z.chunk, :].astype(F32)
+    scratch[t ^ 2, z.half_of(1 - c), :] = far_their[: z.chunk, :].astype(F32)
     near[:, : 2 * z.ff - z.early] = rest[...]
     near[:, 2 * z.ff - z.early :] = lanes([scratch[i] for i in range(4)]).astype(LOW)
-    far[:, : z.early] = feed[z.half_of(c), :]
-    far[:, z.early :] = near[z.half_of(c), :]
 
 
 def own_frame(z, keep, received):
@@ -257,17 +261,15 @@
 def feed_kernel(z, *refs):
     refs = list(refs)
     if z.direct:
-        feed, feed_in, feed_their, near, near_in, near_their, far, far_their = refs[:8]
-        refs = refs[8:]
+        feed, feed_in, feed_their, near, near_in, near_their, far, far_their, last_far, last_far_their = refs[:10]
+        refs = refs[10:]
     else:
         whole = refs[0]
         refs = refs[1:]
-    att = refs[: z.nt]
-    stream, cot, small = refs[z.nt : z.nt + 3]
-    (w_out, att_out, middle_out, hidden_out, normed_out, pre_out, part_out, low_out, own_att, small_out) = refs[
-        z.nt + 3 : z.nt + 13
-    ]
-    sends, heads = refs[z.nt + 13 : -1], refs[-1]
+    att = refs[:3]
+    stream, cot, small = refs[3:6]
+    (w_out, att_out, middle_out, hidden_out, normed_out, pre_out, part_out, low_out, own_att, small_out) = refs[6:16]
+    sends, heads = refs[16:-1], refs[-1]
     t = lax.axis_index("tp")
     if z.direct:
         c, b = lax.axis_index("ctx"), lax.axis_index("fsdp")
@@ -276,8 +278,10 @@
         for at, one, two in ((b, feed, near), (b ^ (1 + c), feed_in, near_in), (b ^ (2 - c), feed_their, near_their)):
             w_out[at, :, first] = one[...]
             w_out[at, :, last] = two[...]
-        w_out[b ^ 3, mine, :] = far[...]
-        w_out[b ^ 3, other, :] = far_their[...]
+        w_out[b ^ 3, mine, first] = far[...]
+        w_out[b ^ 3, other, first] = far_their[...]
+        w_out[b ^ 3, mine, last] = last_far[...]
+        w_out[b ^ 3, other, last] = last_far_their[...]
     else:
         w_out[...] = whole[...]
     n = z.inner
@@ -286,8 +290,10 @@
     w_proj_t = w_out[:, :, 2 * z.ff :].reshape(z.width, z.nt * n)
     grad_out_low = cot[...]
     grad_out = grad_out_low.astype(F32)
-    for k in range(z.nt):
-        heads[t ^ k] = z.spread(read(att[k]))
+    heads[t] = z.spread(read(att[0]))
+    heads[t ^ 2] = z.spread(read(att[1]))
+    heads[t ^ 1] = z.spread(att[2][0, : z.dense, :].astype(F32))
+    heads[t ^ 3] = z.spread(att[2][1, : z.dense, :].astype(F32))
     attended = lanes([heads[i] for i in range(z.nt)]).astype(LOW)
     att_out[...] = attended
     branch = dot(attended, w_proj_t, NT)
@@ -654,7 +660,7 @@
                 [
                     shape((z.part + EXTRA, 3 * inner), LOW),
                     shape((chunk + EXTRA, 3 * inner), LOW),
-                    shape((z.part, inner), LOW),
+                    shape((z.part + 104, inner), LOW),
                     shape((chunk, inner), LOW),
                 ],
                 sources,
@@ -682,14 +688,18 @@
             )
             shared = [other_core(g) for g in got]
             qkv_in = [near, got[0], shared[0], got[1], shared[1]]
-            rest_near, rest_far = call(
+            (rest_near,) = call(
                 part(pack_rest_kernel, z),
-                [shape((z.part, z.cols - z.early), LOW), shape((chunk, z.cols), LOW)],
-                [feed_own, feed_rest, proj_t, proj_got[0], other_core(proj_got[0]), proj_got[1], other_core(proj_got[1])],
+                [shape((z.part, z.cols - z.early), LOW)],
+                [feed_rest, proj_t, proj_got[0], other_core(proj_got[0]), proj_got[1], other_core(proj_got[1])],
                 [pltpu.VMEM((nt, z.part, inner), F32)],
                 name="pack_rest",
             )
-            near_in, far_in = to_near(rest_near), to_far(rest_far)
+            near_in = to_near(rest_near)
+            far_in = []
+            for value in (feed_in, near_in):
+                (half,) = call(part(cut_kernel, z), [shape((chunk, value.shape[1]), LOW)], [value], name="cut")
+                far_in.append(to_cross(half))
         else:
             stream, normal_one, inverse_one, cot = frames(x_recv, cot_recv)
             whole = lax.all_gather(qkv3, "fsdp", axis=1, tiled=True)
@@ -716,11 +726,13 @@
             [pltpu.VMEM((4, EXTRA, 3 * inner), F32)] if z.direct else [],
             name="attend",
         )
-        att = [to_tp(attended, k) for k in range(1, nt)]
+        att_one = to_tp(attended, 2)
+        (att_two,) = call(pair_kernel, [shape((2, z.dense + 16, 128), LOW)], [attended, att_one], name="pair")
+        att_two = to_tp(att_two, 1)
         if z.direct:
-            att, feed_in, near_in, far_in = tie((att, feed_in, near_in, far_in))
-            rest_in = [feed_own, feed_in, other_core(feed_in)] + [rest_near, near_in, other_core(near_in)]
-            rest_in += [far_in, other_core(far_in)]
+            att_two, far_in = tie((att_two, far_in))
+            rest_in = [feed_own, feed_in, other_core(feed_in), rest_near, near_in, other_core(near_in)]
+            rest_in += [far_in[0], other_core(far_in[0]), far_in[1], other_core(far_in[1])]
 
         (w_rest, att_all, middle, hidden, normed_two, grad_pre, part_middle, part_low, own_att, small_two, *att_sends) = (
             call(
@@ -738,7 +750,7 @@
                     shape((8, width), F32),
                 ]
                 + [shape((z.dense, 128), LOW)] * (nt - 1),
-                rest_in + [attended] + att + [stream, cot, small],
+                rest_in + [attended, att_one, att_two, stream, cot, small],
                 [pltpu.VMEM((nt, rows, inner), F32)],
                 name="feed",
             )

time: 99.9 us -> 97.8 us (0.979)
  starting transfers between devices: 39.7 us -> 35.6 us
  waiting for transfers between devices: 40.1 us -> 42.2 us
    ppermute x14 -> x13, waiting for transfers between devices: 26.1 us -> 29.4 us  [to_tp(): return lax.ppermute(value, 'tp', [(i, i ^ k) for i in range(nt)])]
    ppermute x14 -> x13, starting transfers between devices: 18.4 us -> 15.5 us  [to_tp(): return lax.ppermute(value, 'tp', [(i, i ^ k) for i in range(nt)])]
    ppermute x7 -> x9, starting transfers between devices: 11.7 us -> 10.4 us  [neighbours(): return lax.ppermute(value, ('fsdp', 'ctx'), pairs)]
    ppermute x15 -> x16, waiting for transfers between devices: 6.13 us -> 5.02 us  [other_core(): return lax.ppermute(value, 'ctx', [(0, 1), (1, 0)])]
    ppermute x4 -> x3, waiting for transfers between devices: 5.21 us -> 4.86 us  [to_far(): return lax.ppermute(value, 'fsdp', [(i, i ^ 3) for i in range(nf)])]
    ppermute x7 -> x9, waiting for transfers between devices: 2.65 us -> 2.95 us  [neighbours(): return lax.ppermute(value, ('fsdp', 'ctx'), pairs)]
    ppermute x4 -> x3, starting transfers between devices: 4.76 us -> 4.68 us  [to_far(): return lax.ppermute(value, 'fsdp', [(i, i ^ 3) for i in range(nf)])]
    ppermute x15 -> x16, starting transfers between devices: 3.34 us -> 3.38 us  [other_core(): return lax.ppermute(value, 'ctx', [(0, 1), (1, 0)])]
  transfers between devices with their start and end apart: 41 -> 42, of which waited for: 16 -> 15; matrix products, arithmetic and copies ran while one was open for 0% -> 0% of each run, Pallas kernels for 7% -> 7%
where the time goes in v6:
time: 97.8 us; the launch traced here: 97.6 us
  waiting for transfers between devices  42.2 us (43%)
  starting transfers between devices  35.6 us (36%)
  Pallas kernels  16 us (16%)
  local copies, waits for them, and re-layouts  2.9 us (3%)
    ppermute x13, waiting for transfers between devices, to_tp(): return lax.ppermute(value, 'tp', [(i, i ^ k) for i in range(nt)])  29.4 us
    pallas_call x27, Pallas kernels, call(): pl.pallas_call(kernel, out_shape=tuple(outs), in_specs=in_specs or [VMEM]...  16 us
    ppermute x13, starting transfers between devices, to_tp(): return lax.ppermute(value, 'tp', [(i, i ^ k) for i in range(nt)])  15.5 us
    ppermute x9, starting transfers between devices, neighbours(): return lax.ppermute(value, ('fsdp', 'ctx'), pairs)  10.4 us
    ppermute x16, waiting for transfers between devices, other_core(): return lax.ppermute(value, 'ctx', [(0, 1), (1, 0)])  5.02 us
    ppermute x3, waiting for transfers between devices, to_far(): return lax.ppermute(value, 'fsdp', [(i, i ^ 3) for i in range(nf)])  4.86 us
    ppermute x3, starting transfers between devices, to_far(): return lax.ppermute(value, 'fsdp', [(i, i ^ 3) for i in range(nf)])  4.68 us
    ppermute x16, starting transfers between devices, other_core(): return lax.ppermute(value, 'ctx', [(0, 1), (1, 0)])  3.38 us
  transfers between devices with their start and end apart: 42, of which 15 were waited for; matrix products, arithmetic and copies ran while one was open for 0% of the time, Pallas kernels for 7%

profile of v6, /device:TPU:0, one launch (start us, length us, event | category | flops | bytes accessed | tf_op | source)
XLA Modules:
  0.0 97.6 jit_solution(6689969363757491209)
XLA Ops:
  0.7 0.5 collective-permute-start.2
  1.3 2.0 %pack.1 = (bf16[208,576]{1,0:T(8,128)(2,1)}, bf16[112,576]{1,0:T(8,128)(2,1)}, bf16[296,192]{1,0:T(8,128)(2,1)}, bf16[96,192]{1,0:T(8,128)(2,1)}) custom-call(bf16[3,192,192]{2,1,0:T(8,128)(2,1)} %bitcast.15, bf16[192,192]{1,0:T(8,128)(2,1)} %refs_1_.1, bf16[12,16]{1,0:T(8,128)(2,1)} %refs_2_.1, bf16[3,2,16]{2,1,0:T(2,128)(2,1)} %bitcast.16, ...), custom_call_target="tpu_custom_call" | custom-call | tf_op jit(solution)/shard_map/pack/pallas_call | solution.py:34
  3.3 3.0 %collective-permute-start.4 = (bf16[208,576]{1,0:T(8,128)(2,1)}, bf16[208,576]{1,0:T(8,128)(2,1)S(1)}, u32[]{:S(2)}, u32[]{:S(2)}) collective-permute-start(bf16[208,576]{1,0:T(8,128)(2,1)} %get-tuple-element.133.refs_0_), channel_id=1, source_target_pairs={{0,8},{4,20},{8,0},{12,28},{16,24},{20,4},{24,16},{28,12},{1,9},{5... | collective-permute-start | bytes 718856 | tf_op jit(solution)/shard_map/ppermute | solution.py:623
  6.3 1.5 %collective-permute-start.5 = (bf16[112,576]{1,0:T(8,128)(2,1)}, bf16[112,576]{1,0:T(8,128)(2,1)S(1)}, u32[]{:S(2)}, u32[]{:S(2)}) collective-permute-start(bf16[112,576]{1,0:T(8,128)(2,1)} %get-tuple-element.134), channel_id=1, source_target_pairs={{0,24},{8,16},{16,8},{24,0},{1,25},{9,17},{17,9},{25,1},{2,26},{10... | collective-permute-start | bytes 387080 | tf_op jit(solution)/shard_map/ppermute | solution.py:619
  7.8 1.6 %collective-permute-start.6 = (bf16[296,192]{1,0:T(8,128)(2,1)}, bf16[296,192]{1,0:T(8,128)(2,1)S(1)}, u32[]{:S(2)}, u32[]{:S(2)}) collective-permute-start(bf16[296,192]{1,0:T(8,128)(2,1)} %get-tuple-element.135.proj_t), channel_id=1, source_target_pairs={{0,1},{4,7},{1,0},{5,6},{2,3},{6,5},{3,2},{7,4},{8,9},{12,15},{9,8... | collective-permute-start | bytes 341000 | tf_op jit(solution)/shard_map/ppermute | solution.py:633
  9.3 2.6 %collective-permute-start.7 = (bf16[96,192]{1,0:T(8,128)(2,1)}, bf16[96,192]{1,0:T(8,128)(2,1)S(1)}, u32[]{:S(2)}, u32[]{:S(2)}) collective-permute-start(bf16[96,192]{1,0:T(8,128)(2,1)} %get-tuple-element.136), channel_id=1, source_target_pairs={{0,2},{1,3},{2,0},{3,1},{4,6},{5,7},{6,4},{7,5},{8,10},{9,11},{10,... | collective-permute-start | bytes 110600 | tf_op jit(solution)/shard_map/ppermute | solution.py:616
  11.9 1.0 copy-done.2
  12.9 1.0 copy-done.3
  13.9 0.2 stage.1
  14.0 1.6 %collective-permute-start = (bf16[192,1280]{1,0:T(8,128)(2,1)S(1)}, bf16[192,1280]{1,0:T(8,128)(2,1)S(1)}, u32[]{:S(2)}, u32[]{:S(2)}) collective-permute-start(bf16[192,1280]{1,0:T(8,128)(2,1)S(1)} %get-tuple-element.128.refs_0_), channel_id=1, source_target_pairs={{0,8},{4,20},{8,0},{12,28},{16,24},{20,4},{24,16},{28,12},{1,9},{5... | collective-permute-start | bytes 1474568 | tf_op jit(solution)/shard_map/ppermute | solution.py:623
  15.6 1.0 copy-done
  16.6 0.4 cotangent.1.refs_14_.cot
  16.9 0.6 frame.1
  17.6 0.5 collective-permute-start.9
  18.1 0.9 collective-permute-done.9.far_their
  19.1 0.2 pack_rest.1.refs_3_
  19.3 0.6 collective-permute-start.10
  19.9 0.5 collective-permute-start.13
  20.4 1.2 %collective-permute-done.13.refs_4_ = bf16[112,576]{1,0:T(8,128)(2,1)S(1)} collective-permute-done((bf16[112,576]{1,0:T(8,128)(2,1)S(1)}, bf16[112,576]{1,0:T(8,128)(2,1)S(1)}, u32[]{:S(2)}, u32[]{:S(2)}) %collective-permute-start.13) | collective-permute-done | bytes 129056 | tf_op jit(solution)/shard_map/ppermute | solution.py:613
  21.6 1.3 %attend.1 = (f32[8,768]{1,0:T(8,128)S(1)}, bf16[4,192,576]{2,1,0:T(8,128)(2,1)S(1)}, bf16[208,768]{1,0:T(8,128)(2,1)S(1)}, bf16[3,208,192]{2,1,0:T(8,128)(2,1)S(...) custom-call(bf16[208,576]{1,0:T(8,128)(2,1)S(1)} %copy-done.4, ...), custom_call_target="tpu_custom_call" | custom-call | tf_op jit(solution)/shard_map/attend/pallas_call | solution.py:34
  22.9 1.6 %collective-permute-start.14 = (bf16[312,128]{1,0:T(8,128)(2,1)S(1)}, bf16[312,128]{1,0:T(8,128)(2,1)S(1)}, u32[]{:S(2)}, u32[]{:S(2)}) collective-permute-start(bf16[312,128]{1,0:T(8,128)(2,1)S(1)} %get-tuple-element.149.first.refs_10_), channel_id=1, source_target_pairs={{0,2},{1,3},{2,0},{3,1},{4,6},{5,7},{6,4},{7,5},{8,10},{9,11},{10,... | collective-permute-start | bytes 239624 | tf_op jit(solution)/shard_map/ppermute | solution.py:616
  24.5 0.5 collective-permute-start.16
  24.9 2.3 %collective-permute-done.10.value.refs_4_ = bf16[192,1024]{1,0:T(8,128)(2,1)S(1)} collective-permute-done((bf16[192,1024]{1,0:T(8,128)(2,1)S(1)}, bf16[192,1024]{1,0:T(8,128)(2,1)S(1)}, u32[]{:S(2)}, u32[]{:S(2)}) %collective-permute-start.10) | collective-permute-done | bytes 393248 | tf_op jit(solution)/shard_map/ppermute | solution.py:623
  27.3 0.5 collective-permute-start.17
  27.7 2.2 %collective-permute-done.14.second.refs_11_ = bf16[312,128]{1,0:T(8,128)(2,1)S(1)} collective-permute-done((bf16[312,128]{1,0:T(8,128)(2,1)S(1)}, bf16[312,128]{1,0:T(8,128)(2,1)S(1)}, u32[]{:S(2)}, u32[]{:S(2)}) %collective-permute-start.14) | collective-permute-done | bytes 79904 | tf_op jit(solution)/shard_map/ppermute | solution.py:616
  30.1 0.6 collective-permute-done.16.refs_6_
  30.7 5.5 %collective-permute-done.15.refs_12_ = bf16[2,328,128]{2,1,0:T(8,128)(2,1)S(1)} collective-permute-done((bf16[2,328,128]{2,1,0:T(8,128)(2,1)S(1)}, bf16[2,328,128]{2,1,0:T(8,128)(2,1)S(1)}, u32[]{:S(2)}, u32[]{:S(2)}) %collective-permute-start.15) | collective-permute-done | bytes 167968 | tf_op jit(solution)/shard_map/ppermute | solution.py:616
  36.2 0.5 collective-permute-start.19
  36.7 1.3 %collective-permute-done.19.refs_9_ = bf16[96,1024]{1,0:T(8,128)(2,1)S(1)} collective-permute-done((bf16[96,1024]{1,0:T(8,128)(2,1)S(1)}, bf16[96,1024]{1,0:T(8,128)(2,1)S(1)}, u32[]{:S(2)}, u32[]{:S(2)}) %collective-permute-start.19) | collective-permute-done | bytes 196640 | tf_op jit(solution)/shard_map/ppermute | solution.py:613
  38.0 3.1 %feed.1 = (bf16[4,192,2304]{2,1,0:T(8,128)(2,1)S(1)}, bf16[208,768]{1,0:T(8,128)(2,1)S(1)}, f32[208,768]{1,0:T(8,128)S(1)}, bf16[208,768]{1,0:T(8,128)(2,1)S(1)}...) custom-call(bf16[192,1280]{1,0:T(8,128)(2,1)S(1)} %get-tuple-element, ...), custom_call_target="tpu_custom_call" | custom-call | tf_op jit(solution)/shard_map/feed/pallas_call | solution.py:34
  41.1 0.6 proj_grad.1
  41.7 0.2 collective-permute-start.24
  41.9 0.6 down.1
  42.6 0.3 collective-permute-start.23
  42.9 1.7 %collective-permute-start.20 = (bf16[312,128]{1,0:T(8,128)(2,1)S(1)}, bf16[312,128]{1,0:T(8,128)(2,1)S(1)}, u32[]{:S(2)}, u32[]{:S(2)}) collective-permute-start(bf16[312,128]{1,0:T(8,128)(2,1)S(1)} %get-tuple-element.159), channel_id=1, source_target_pairs={{0,1},{1,0},{2,3},{3,2},{4,5},{5,4},{6,7},{7,6},{8,9},{9,8},{10,11... | collective-permute-start | bytes 239624 | tf_op jit(solution)/shard_map/ppermute | solution.py:616
  44.6 1.3 %collective-permute-start.21 = (bf16[312,128]{1,0:T(8,128)(2,1)S(1)}, bf16[312,128]{1,0:T(8,128)(2,1)S(1)}, u32[]{:S(2)}, u32[]{:S(2)}) collective-permute-start(bf16[312,128]{1,0:T(8,128)(2,1)S(1)} %get-tuple-element.160), channel_id=1, source_target_pairs={{0,2},{1,3},{2,0},{3,1},{4,6},{5,7},{6,4},{7,5},{8,10},{9,11},{10,... | collective-permute-start | bytes 239624 | tf_op jit(solution)/shard_map/ppermute | solution.py:616
  45.9 1.3 %collective-permute-start.22 = (bf16[312,128]{1,0:T(8,128)(2,1)S(1)}, bf16[312,128]{1,0:T(8,128)(2,1)S(1)}, u32[]{:S(2)}, u32[]{:S(2)}) collective-permute-start(bf16[312,128]{1,0:T(8,128)(2,1)S(1)} %get-tuple-element.161), channel_id=1, source_target_pairs={{0,3},{1,2},{2,1},{3,0},{4,7},{5,6},{6,5},{7,4},{8,11},{9,10},{10,... | collective-permute-start | bytes 239624 | tf_op jit(solution)/shard_map/ppermute | solution.py:616
  47.3 0.9 feed_grad.1
  48.2 4.2 %collective-permute-done.20.refs_1_ = bf16[312,128]{1,0:T(8,128)(2,1)S(1)} collective-permute-done((bf16[312,128]{1,0:T(8,128)(2,1)S(1)}, bf16[312,128]{1,0:T(8,128)(2,1)S(1)}, u32[]{:S(2)}, u32[]{:S(2)}) %collective-permute-start.20) | collective-permute-done | bytes 79904 | tf_op jit(solution)/shard_map/ppermute | solution.py:616
  52.4 2.5 %collective-permute-done.22.refs_3_ = bf16[312,128]{1,0:T(8,128)(2,1)S(1)} collective-permute-done((bf16[312,128]{1,0:T(8,128)(2,1)S(1)}, bf16[312,128]{1,0:T(8,128)(2,1)S(1)}, u32[]{:S(2)}, u32[]{:S(2)}) %collective-permute-start.22) | collective-permute-done | bytes 79904 | tf_op jit(solution)/shard_map/ppermute | solution.py:616
  55.0 2.0 %back.1 = (bf16[208,576]{1,0:T(8,128)(2,1)S(1)}, f32[1,576]{1,0:T(1,128)S(1)}, f32[112,768]{1,0:T(8,128)S(1)}, bf16[112,768]{1,0:T(8,128)(2,1)S(1)}) custom-call(f32[208,192]{1,0:T(8,128)S(1)} %get-tuple-element.171.refs_0_, bf16[312,128]{1,0:T(8,128)(2,1)S(1)} %collective-permute-done.20.refs_1_, bf16[312,128]{1,0:T(8,128)(2,1)S(1)} %collective-permute-done.21.refs_2_, ...), custom_call_target="tpu_custom_call" | custom-call | tf_op jit(solution)/shard_map/back/pallas_call | solution.py:34
  57.0 0.6 qkv_grad.1
  57.8 0.9 collective-permute-start.27
  58.7 1.0 %collective-permute-start.25 = (bf16[112,768]{1,0:T(8,128)(2,1)S(1)}, bf16[112,768]{1,0:T(8,128)(2,1)S(1)}, u32[]{:S(2)}, u32[]{:S(2)}) collective-permute-start(bf16[112,768]{1,0:T(8,128)(2,1)S(1)} %get-tuple-element.181), channel_id=1, source_target_pairs={{0,1},{1,0},{2,3},{3,2},{4,5},{5,4},{6,7},{7,6},{8,9},{9,8},{10,11... | collective-permute-start | bytes 516104 | tf_op jit(solution)/shard_map/ppermute | solution.py:616
  59.8 1.9 %collective-permute-start.26 = (bf16[104,768]{1,0:T(8,128)(2,1)S(1)}, bf16[104,768]{1,0:T(8,128)(2,1)S(1)}, u32[]{:S(2)}, u32[]{:S(2)}) collective-permute-start(bf16[104,768]{1,0:T(8,128)(2,1)S(1)} %out_pair.1.own), channel_id=1, source_target_pairs={{0,3},{1,2},{2,1},{3,0},{4,7},{5,6},{6,5},{7,4},{8,11},{9,10},{10,... | collective-permute-start | bytes 479240 | tf_op jit(solution)/shard_map/ppermute | solution.py:616
  61.7 1.3 %collective-permute-start.28 = (bf16[96,768]{1,0:T(8,128)(2,1)S(1)}, bf16[96,768]{1,0:T(8,128)(2,1)S(1)}, u32[]{:S(2)}, u32[]{:S(2)}) collective-permute-start(bf16[96,768]{1,0:T(8,128)(2,1)S(1)} %get-tuple-element.185), channel_id=1, source_target_pairs={{0,24},{8,16},{16,8},{24,0},{1,25},{9,17},{17,9},{25,1},{2,26},{10... | collective-permute-start | bytes 442376 | tf_op jit(solution)/shard_map/ppermute | solution.py:619
  63.0 4.9 %collective-permute-done.28.refs_2_ = bf16[96,768]{1,0:T(8,128)(2,1)S(1)} collective-permute-done((bf16[96,768]{1,0:T(8,128)(2,1)S(1)}, bf16[96,768]{1,0:T(8,128)(2,1)S(1)}, u32[]{:S(2)}, u32[]{:S(2)}) %collective-permute-start.28) | collective-permute-done | bytes 147488 | tf_op jit(solution)/shard_map/ppermute | solution.py:619
  67.8 1.6 %collective-permute-done.26.received = bf16[104,768]{1,0:T(8,128)(2,1)S(1)} collective-permute-done((bf16[104,768]{1,0:T(8,128)(2,1)S(1)}, bf16[104,768]{1,0:T(8,128)(2,1)S(1)}, u32[]{:S(2)}, u32[]{:S(2)}) %collective-permute-start.26) | collective-permute-done | bytes 159776 | tf_op jit(solution)/shard_map/ppermute | solution.py:616
  69.4 0.3 split.1
  69.8 1.3 %collective-permute-start.32 = (bf16[2,96,2176]{2,1,0:T(8,128)(2,1)S(1)}, bf16[2,96,2176]{2,1,0:T(8,128)(2,1)S(1)}, u32[]{:S(2)}, u32[]{:S(2)}) collective-permute-start(bf16[2,96,2176]{2,1,0:T(8,128)(2,1)S(1)} %get-tuple-element.200), channel_id=1, source_target_pairs={{0,8},{4,20},{8,0},{12,28},{16,24},{20,4},{24,16},{28,12},{1,9},{5... | collective-permute-start | bytes 2506760 | tf_op jit(solution)/shard_map/ppermute | solution.py:623
  71.1 0.3 out_total.1
  71.4 0.7 collective-permute-start.31
  72.1 1.2 %collective-permute-start.30 = (bf16[112,768]{1,0:T(8,128)(2,1)S(1)}, bf16[112,768]{1,0:T(8,128)(2,1)S(1)}, u32[]{:S(2)}, u32[]{:S(2)}) collective-permute-start(bf16[112,768]{1,0:T(8,128)(2,1)S(1)} %in_pair.1.own), channel_id=1, source_target_pairs={{0,3},{1,2},{2,1},{3,0},{4,7},{5,6},{6,5},{7,4},{8,11},{9,10},{10,... | collective-permute-start | bytes 516104 | tf_op jit(solution)/shard_map/ppermute | solution.py:616
  73.3 10.3 %collective-permute-done.30.received = bf16[112,768]{1,0:T(8,128)(2,1)S(1)} collective-permute-done((bf16[112,768]{1,0:T(8,128)(2,1)S(1)}, bf16[112,768]{1,0:T(8,128)(2,1)S(1)}, u32[]{:S(2)}, u32[]{:S(2)}) %collective-permute-start.30) | collective-permute-done | bytes 172064 | tf_op jit(solution)/shard_map/ppermute | solution.py:616
  83.8 0.2 cross.1
  84.0 0.8 collective-permute-start.35
  84.8 1.8 %collective-permute-start.34 = (bf16[48,768]{1,0:T(8,128)(2,1)S(1)}, bf16[48,768]{1,0:T(8,128)(2,1)S(1)}, u32[]{:S(2)}, u32[]{:S(2)}) collective-permute-start(bf16[48,768]{1,0:T(8,128)(2,1)S(1)} %get-tuple-element.206), channel_id=1, source_target_pairs={{0,3},{1,2},{2,1},{3,0},{4,7},{5,6},{6,5},{7,4},{8,11},{9,10},{10,... | collective-permute-start | bytes 221192 | tf_op jit(solution)/shard_map/ppermute | solution.py:616
  86.7 1.3 %collective-permute-start.37 = (bf16[16,576]{1,0:T(8,128)(2,1)S(1)}, bf16[16,576]{1,0:T(8,128)(2,1)S(1)}, u32[]{:S(2)}, u32[]{:S(2)}) collective-permute-start(bf16[16,576]{1,0:T(8,128)(2,1)S(1)} %get-tuple-element.211), channel_id=1, source_target_pairs={{0,8},{4,20},{8,0},{12,28},{16,24},{20,4},{24,16},{28,12},{1,9},{5... | collective-permute-start | bytes 55304 | tf_op jit(solution)/shard_map/ppermute | solution.py:623
  88.1 1.9 %collective-permute-start.38 = (bf16[16,576]{1,0:T(8,128)(2,1)S(1)}, bf16[16,576]{1,0:T(8,128)(2,1)S(1)}, u32[]{:S(2)}, u32[]{:S(2)}) collective-permute-start(bf16[16,576]{1,0:T(8,128)(2,1)S(1)} %get-tuple-element.212), channel_id=1, source_target_pairs={{0,24},{8,16},{16,8},{24,0},{1,25},{9,17},{17,9},{25,1},{2,26},{10... | collective-permute-start | bytes 55304 | tf_op jit(solution)/shard_map/ppermute | solution.py:619
  89.9 3.0 %collective-permute-done.34.refs_1_ = bf16[48,768]{1,0:T(8,128)(2,1)S(1)} collective-permute-done((bf16[48,768]{1,0:T(8,128)(2,1)S(1)}, bf16[48,768]{1,0:T(8,128)(2,1)S(1)}, u32[]{:S(2)}, u32[]{:S(2)}) %collective-permute-start.34) | collective-permute-done | bytes 73760 | tf_op jit(solution)/shard_map/ppermute | solution.py:616
  93.0 0.2 swap.1
  93.5 0.5 collective-permute-start.40
  94.1 1.5 %collective-permute-done.41.refs_4_ = bf16[112,576]{1,0:T(8,128)(2,1)S(1)} collective-permute-done((bf16[112,576]{1,0:T(8,128)(2,1)S(1)}, bf16[112,576]{1,0:T(8,128)(2,1)S(1)}, u32[]{:S(2)}, u32[]{:S(2)}) %collective-permute-start.41) | collective-permute-done | bytes 129056 | tf_op jit(solution)/shard_map/ppermute | solution.py:613
  95.6 2.0 %final.1 = (bf16[98,2,768]{2,1,0:T(2,128)(2,1)}, f32[98,2,768]{2,1,0:T(2,128)}, f32[192,192]{1,0:T(8,128)}, f32[192,768]{1,0:T(8,128)}, f32[192,768]{1,0:T(8,128...) custom-call(f32[2,104,768]{2,1,0:T(8,128)S(1)} %get-tuple-element.21, ...), custom_call_target="tpu_custom_call" | custom-call | tf_op jit(solution)/shard_map/final/pallas_call | solution.py:34
  (59 shorter events, 1.5 us)
Async XLA Ops:
  0.6 16.3 %copy-start.1 = (bf16[2,98,768]{2,0,1:T(2,128)(2,1)S(1)}, bf16[2,98,768]{2,0,1:T(2,128)(2,1)}, u32[]{:S(2)}) copy-start(bf16[2,98,768]{2,0,1:T(2,128)(2,1)} %param.14) | copy-start | bytes 903172
  0.7 2.6 %collective-permute-start.2 = (bf16[98,2,768]{2,1,0:T(2,128)(2,1)}, bf16[98,2,768]{2,1,0:T(2,128)(2,1)S(1)}, u32[]{:S(2)}, u32[]{:S(2)}) collective-permute-start(bf16[98,2,768]{2,1,0:T(2,128)(2,1)} %bitcast.12), channel_id=1, source_target_pairs={{0,4},{4,0},{1,5},{5,1},{2,6},{6,2},{3,7},{7,3},{8,12},{12,8},{9,1... | collective-permute-start | bytes 903176 | tf_op jit(solution)/shard_map/ppermute | solution.py:613
  1.2 2.1 %collective-permute-start.3 = (bf16[98,2,768]{2,1,0:T(2,128)(2,1)}, bf16[98,2,768]{2,1,0:T(2,128)(2,1)S(1)}, u32[]{:S(2)}, u32[]{:S(2)}) collective-permute-start(bf16[98,2,768]{2,1,0:T(2,128)(2,1)} %bitcast.10), channel_id=1, source_target_pairs={{0,4},{4,0},{1,5},{5,1},{2,6},{6,2},{3,7},{7,3},{8,12},{12,8},{9,1... | collective-permute-start | bytes 903176 | tf_op jit(solution)/shard_map/ppermute | solution.py:613
  3.3 14.2 %collective-permute-start.4 = (bf16[208,576]{1,0:T(8,128)(2,1)}, bf16[208,576]{1,0:T(8,128)(2,1)S(1)}, u32[]{:S(2)}, u32[]{:S(2)}) collective-permute-start(bf16[208,576]{1,0:T(8,128)(2,1)} %get-tuple-element.133.refs_0_), channel_id=1, source_target_pairs={{0,8},{4,20},{8,0},{12,28},{16,24},{20,4},{24,16},{28,12},{1,9},{5... | collective-permute-start | bytes 718856 | tf_op jit(solution)/shard_map/ppermute | solution.py:623
  6.3 11.2 %collective-permute-start.5 = (bf16[112,576]{1,0:T(8,128)(2,1)}, bf16[112,576]{1,0:T(8,128)(2,1)S(1)}, u32[]{:S(2)}, u32[]{:S(2)}) collective-permute-start(bf16[112,576]{1,0:T(8,128)(2,1)} %get-tuple-element.134), channel_id=1, source_target_pairs={{0,24},{8,16},{16,8},{24,0},{1,25},{9,17},{17,9},{25,1},{2,26},{10... | collective-permute-start | bytes 387080 | tf_op jit(solution)/shard_map/ppermute | solution.py:619
  7.8 9.7 %collective-permute-start.6 = (bf16[296,192]{1,0:T(8,128)(2,1)}, bf16[296,192]{1,0:T(8,128)(2,1)S(1)}, u32[]{:S(2)}, u32[]{:S(2)}) collective-permute-start(bf16[296,192]{1,0:T(8,128)(2,1)} %get-tuple-element.135.proj_t), channel_id=1, source_target_pairs={{0,1},{4,7},{1,0},{5,6},{2,3},{6,5},{3,2},{7,4},{8,9},{12,15},{9,8... | collective-permute-start | bytes 341000 | tf_op jit(solution)/shard_map/ppermute | solution.py:633
  9.3 8.2 %collective-permute-start.7 = (bf16[96,192]{1,0:T(8,128)(2,1)}, bf16[96,192]{1,0:T(8,128)(2,1)S(1)}, u32[]{:S(2)}, u32[]{:S(2)}) collective-permute-start(bf16[96,192]{1,0:T(8,128)(2,1)} %get-tuple-element.136), channel_id=1, source_target_pairs={{0,2},{1,3},{2,0},{3,1},{4,6},{5,7},{6,4},{7,5},{8,10},{9,11},{10,... | collective-permute-start | bytes 110600 | tf_op jit(solution)/shard_map/ppermute | solution.py:616
  11.9 1.0 copy-start.2
  12.9 1.0 copy-start.3
  13.9 5.2 %copy-start.5 = (bf16[296,192]{1,0:T(8,128)(2,1)S(1)}, bf16[296,192]{1,0:T(8,128)(2,1)}, u32[]{:S(2)}) copy-start(bf16[296,192]{1,0:T(8,128)(2,1)} %get-tuple-element.135.proj_t) | copy-start | bytes 340996
  13.9 7.7 %copy-start.4 = (bf16[208,576]{1,0:T(8,128)(2,1)S(1)}, bf16[208,576]{1,0:T(8,128)(2,1)}, u32[]{:S(2)}) copy-start(bf16[208,576]{1,0:T(8,128)(2,1)} %get-tuple-element.133.refs_0_) | copy-start | bytes 718852
  14.0 10.4 %collective-permute-start = (bf16[192,1280]{1,0:T(8,128)(2,1)S(1)}, bf16[192,1280]{1,0:T(8,128)(2,1)S(1)}, u32[]{:S(2)}, u32[]{:S(2)}) collective-permute-start(bf16[192,1280]{1,0:T(8,128)(2,1)S(1)} %get-tuple-element.128.refs_0_), channel_id=1, source_target_pairs={{0,8},{4,20},{8,0},{12,28},{16,24},{20,4},{24,16},{28,12},{1,9},{5... | collective-permute-start | bytes 1474568 | tf_op jit(solution)/shard_map/ppermute | solution.py:623
  15.6 1.0 copy-start
  17.5 1.5 %collective-permute-start.8 = (bf16[296,192]{1,0:T(8,128)(2,1)S(1)}, bf16[296,192]{1,0:T(8,128)(2,1)S(1)}, u32[]{:S(2)}, u32[]{:S(2)}) collective-permute-start(bf16[296,192]{1,0:T(8,128)(2,1)S(1)} %collective-permute-done.6.near_in), channel_id=1, source_target_pairs={{0,4},{4,0},{1,5},{5,1},{2,6},{6,2},{3,7},{7,3},{8,12},{12,8},{9,1... | collective-permute-start | bytes 341000 | tf_op jit(solution)/shard_map/ppermute | solution.py:613
  17.6 1.4 %collective-permute-start.9 = (bf16[96,192]{1,0:T(8,128)(2,1)S(1)}, bf16[96,192]{1,0:T(8,128)(2,1)S(1)}, u32[]{:S(2)}, u32[]{:S(2)}) collective-permute-start(bf16[96,192]{1,0:T(8,128)(2,1)S(1)} %collective-permute-done.7.far_in), channel_id=1, source_target_pairs={{0,4},{4,0},{1,5},{5,1},{2,6},{6,2},{3,7},{7,3},{8,12},{12,8},{9,1... | collective-permute-start | bytes 110600 | tf_op jit(solution)/shard_map/ppermute | solution.py:613
  19.3 8.0 %collective-permute-start.10 = (bf16[192,1024]{1,0:T(8,128)(2,1)S(1)}, bf16[192,1024]{1,0:T(8,128)(2,1)S(1)}, u32[]{:S(2)}, u32[]{:S(2)}) collective-permute-start(bf16[192,1024]{1,0:T(8,128)(2,1)S(1)} %pack_rest.1.refs_3_), channel_id=1, source_target_pairs={{0,8},{4,20},{8,0},{12,28},{16,24},{20,4},{24,16},{28,12},{1,9},{5... | collective-permute-start | bytes 1179656 | tf_op jit(solution)/shard_map/ppermute | solution.py:623
  19.9 1.8 %collective-permute-start.12 = (bf16[208,576]{1,0:T(8,128)(2,1)S(1)}, bf16[208,576]{1,0:T(8,128)(2,1)S(1)}, u32[]{:S(2)}, u32[]{:S(2)}) collective-permute-start(bf16[208,576]{1,0:T(8,128)(2,1)S(1)} %collective-permute-done.4.refs_1_), channel_id=1, source_target_pairs={{0,4},{4,0},{1,5},{5,1},{2,6},{6,2},{3,7},{7,3},{8,12},{12,8},{9,1... | collective-permute-start | bytes 718856 | tf_op jit(solution)/shard_map/ppermute | solution.py:613
  19.9 1.7 %collective-permute-start.13 = (bf16[112,576]{1,0:T(8,128)(2,1)S(1)}, bf16[112,576]{1,0:T(8,128)(2,1)S(1)}, u32[]{:S(2)}, u32[]{:S(2)}) collective-permute-start(bf16[112,576]{1,0:T(8,128)(2,1)S(1)} %collective-permute-done.5.refs_3_), channel_id=1, source_target_pairs={{0,4},{4,0},{1,5},{5,1},{2,6},{6,2},{3,7},{7,3},{8,12},{12,8},{9,1... | collective-permute-start | bytes 387080 | tf_op jit(solution)/shard_map/ppermute | solution.py:613
  22.9 7.0 %collective-permute-start.14 = (bf16[312,128]{1,0:T(8,128)(2,1)S(1)}, bf16[312,128]{1,0:T(8,128)(2,1)S(1)}, u32[]{:S(2)}, u32[]{:S(2)}) collective-permute-start(bf16[312,128]{1,0:T(8,128)(2,1)S(1)} %get-tuple-element.149.first.refs_10_), channel_id=1, source_target_pairs={{0,2},{1,3},{2,0},{3,1},{4,6},{5,7},{6,4},{7,5},{8,10},{9,11},{10,... | collective-permute-start | bytes 239624 | tf_op jit(solution)/shard_map/ppermute | solution.py:616
  24.5 6.3 %collective-permute-start.16 = (bf16[96,1280]{1,0:T(8,128)(2,1)S(1)}, bf16[96,1280]{1,0:T(8,128)(2,1)S(1)}, u32[]{:S(2)}, u32[]{:S(2)}) collective-permute-start(bf16[96,1280]{1,0:T(8,128)(2,1)S(1)} %cut.2), channel_id=1, source_target_pairs={{0,16},{4,12},{8,24},{12,4},{16,0},{20,28},{24,8},{28,20},{1,17},{... | collective-permute-start | bytes 737288 | tf_op jit(solution)/shard_map/ppermute | solution.py:623
  24.9 11.8 %collective-permute-start.1 = (bf16[192,1280]{1,0:T(8,128)(2,1)S(1)}, bf16[192,1280]{1,0:T(8,128)(2,1)S(1)}, u32[]{:S(2)}, u32[]{:S(2)}) collective-permute-start(bf16[192,1280]{1,0:T(8,128)(2,1)S(1)} %collective-permute-done.value.refs_1_), channel_id=1, source_target_pairs={{0,4},{4,0},{1,5},{5,1},{2,6},{6,2},{3,7},{7,3},{8,12},{12,8},{9,1... | collective-permute-start | bytes 1474568 | tf_op jit(solution)/shard_map/ppermute | solution.py:613
  27.3 9.0 %collective-permute-start.17 = (bf16[96,1024]{1,0:T(8,128)(2,1)S(1)}, bf16[96,1024]{1,0:T(8,128)(2,1)S(1)}, u32[]{:S(2)}, u32[]{:S(2)}) collective-permute-start(bf16[96,1024]{1,0:T(8,128)(2,1)S(1)} %cut.3), channel_id=1, source_target_pairs={{0,16},{4,12},{8,24},{12,4},{16,0},{20,28},{24,8},{28,20},{1,17},{... | collective-permute-start | bytes 589832 | tf_op jit(solution)/shard_map/ppermute | solution.py:623
  29.9 6.3 %collective-permute-start.15 = (bf16[2,328,128]{2,1,0:T(8,128)(2,1)S(1)}, bf16[2,328,128]{2,1,0:T(8,128)(2,1)S(1)}, u32[]{:S(2)}, u32[]{:S(2)}) collective-permute-start(bf16[2,328,128]{2,1,0:T(8,128)(2,1)S(1)} %pair.1), channel_id=1, source_target_pairs={{0,1},{1,0},{2,3},{3,2},{4,5},{5,4},{6,7},{7,6},{8,9},{9,8},{10,11... | collective-permute-start | bytes 503816 | tf_op jit(solution)/shard_map/ppermute | solution.py:616
  30.0 6.7 %collective-permute-start.11 = (bf16[192,1024]{1,0:T(8,128)(2,1)S(1)}, bf16[192,1024]{1,0:T(8,128)(2,1)S(1)}, u32[]{:S(2)}, u32[]{:S(2)}) collective-permute-start(bf16[192,1024]{1,0:T(8,128)(2,1)S(1)} %collective-permute-done.10.value.refs_4_), channel_id=1, source_target_pairs={{0,4},{4,0},{1,5},{5,1},{2,6},{6,2},{3,7},{7,3},{8,12},{12,8},{9,1... | collective-permute-start | bytes 1179656 | tf_op jit(solution)/shard_map/ppermute | solution.py:613
  36.2 1.8 %collective-permute-start.18 = (bf16[96,1280]{1,0:T(8,128)(2,1)S(1)}, bf16[96,1280]{1,0:T(8,128)(2,1)S(1)}, u32[]{:S(2)}, u32[]{:S(2)}) collective-permute-start(bf16[96,1280]{1,0:T(8,128)(2,1)S(1)} %collective-permute-done.16.refs_6_), channel_id=1, source_target_pairs={{0,4},{4,0},{1,5},{5,1},{2,6},{6,2},{3,7},{7,3},{8,12},{12,8},{9,1... | collective-permute-start | bytes 737288 | tf_op jit(solution)/shard_map/ppermute | solution.py:613
  36.2 1.8 %collective-permute-start.19 = (bf16[96,1024]{1,0:T(8,128)(2,1)S(1)}, bf16[96,1024]{1,0:T(8,128)(2,1)S(1)}, u32[]{:S(2)}, u32[]{:S(2)}) collective-permute-start(bf16[96,1024]{1,0:T(8,128)(2,1)S(1)} %collective-permute-done.17.refs_8_), channel_id=1, source_target_pairs={{0,4},{4,0},{1,5},{5,1},{2,6},{6,2},{3,7},{7,3},{8,12},{12,8},{9,1... | collective-permute-start | bytes 589832 | tf_op jit(solution)/shard_map/ppermute | solution.py:613
  41.7 13.3 %collective-permute-start.24 = (bf16[288,768]{1,0:T(8,128)(2,1)S(1)}, bf16[288,768]{1,0:T(8,128)(2,1)S(1)}, u32[]{:S(2)}, u32[]{:S(2)}) collective-permute-start(bf16[288,768]{1,0:T(8,128)(2,1)S(1)} %get-tuple-element.169), channel_id=1, source_target_pairs={{0,4},{4,0},{1,5},{5,1},{2,6},{6,2},{3,7},{7,3},{8,12},{12,8},{9,1... | collective-permute-start | bytes 1327112 | tf_op jit(solution)/shard_map/ppermute | solution.py:613
  42.6 12.4 %collective-permute-start.23 = (bf16[104,768]{1,0:T(8,128)(2,1)S(1)}, bf16[104,768]{1,0:T(8,128)(2,1)S(1)}, u32[]{:S(2)}, u32[]{:S(2)}) collective-permute-start(bf16[104,768]{1,0:T(8,128)(2,1)S(1)} %get-tuple-element.162), channel_id=1, source_target_pairs={{0,1},{1,0},{2,3},{3,2},{4,5},{5,4},{6,7},{7,6},{8,9},{9,8},{10,11... | collective-permute-start | bytes 479240 | tf_op jit(solution)/shard_map/ppermute | solution.py:616
  42.9 9.5 %collective-permute-start.20 = (bf16[312,128]{1,0:T(8,128)(2,1)S(1)}, bf16[312,128]{1,0:T(8,128)(2,1)S(1)}, u32[]{:S(2)}, u32[]{:S(2)}) collective-permute-start(bf16[312,128]{1,0:T(8,128)(2,1)S(1)} %get-tuple-element.159), channel_id=1, source_target_pairs={{0,1},{1,0},{2,3},{3,2},{4,5},{5,4},{6,7},{7,6},{8,9},{9,8},{10,11... | collective-permute-start | bytes 239624 | tf_op jit(solution)/shard_map/ppermute | solution.py:616
  44.6 7.8 %collective-permute-start.21 = (bf16[312,128]{1,0:T(8,128)(2,1)S(1)}, bf16[312,128]{1,0:T(8,128)(2,1)S(1)}, u32[]{:S(2)}, u32[]{:S(2)}) collective-permute-start(bf16[312,128]{1,0:T(8,128)(2,1)S(1)} %get-tuple-element.160), channel_id=1, source_target_pairs={{0,2},{1,3},{2,0},{3,1},{4,6},{5,7},{6,4},{7,5},{8,10},{9,11},{10,... | collective-permute-start | bytes 239624 | tf_op jit(solution)/shard_map/ppermute | solution.py:616
  45.9 9.0 %collective-permute-start.22 = (bf16[312,128]{1,0:T(8,128)(2,1)S(1)}, bf16[312,128]{1,0:T(8,128)(2,1)S(1)}, u32[]{:S(2)}, u32[]{:S(2)}) collective-permute-start(bf16[312,128]{1,0:T(8,128)(2,1)S(1)} %get-tuple-element.161), channel_id=1, source_target_pairs={{0,3},{1,2},{2,1},{3,0},{4,7},{5,6},{6,5},{7,4},{8,11},{9,10},{10,... | collective-permute-start | bytes 239624 | tf_op jit(solution)/shard_map/ppermute | solution.py:616
  57.6 11.8 %collective-permute-start.29 = (bf16[384,2176]{1,0:T(8,128)(2,1)S(1)}, bf16[384,2176]{1,0:T(8,128)(2,1)S(1)}, u32[]{:S(2)}, u32[]{:S(2)}) collective-permute-start(bf16[384,2176]{1,0:T(8,128)(2,1)S(1)} %get-tuple-element.189), channel_id=1, source_target_pairs={{0,4},{4,0},{1,5},{5,1},{2,6},{6,2},{3,7},{7,3},{8,12},{12,8},{9,1... | collective-permute-start | bytes 5013512 | tf_op jit(solution)/shard_map/ppermute | solution.py:613
  57.8 11.6 %collective-permute-start.27 = (bf16[192,768]{1,0:T(8,128)(2,1)S(1)}, bf16[192,768]{1,0:T(8,128)(2,1)S(1)}, u32[]{:S(2)}, u32[]{:S(2)}) collective-permute-start(bf16[192,768]{1,0:T(8,128)(2,1)S(1)} %get-tuple-element.184), channel_id=1, source_target_pairs={{0,8},{4,20},{8,0},{12,28},{16,24},{20,4},{24,16},{28,12},{1,9},{5... | collective-permute-start | bytes 884744 | tf_op jit(solution)/shard_map/ppermute | solution.py:623
  58.7 10.7 %collective-permute-start.25 = (bf16[112,768]{1,0:T(8,128)(2,1)S(1)}, bf16[112,768]{1,0:T(8,128)(2,1)S(1)}, u32[]{:S(2)}, u32[]{:S(2)}) collective-permute-start(bf16[112,768]{1,0:T(8,128)(2,1)S(1)} %get-tuple-element.181), channel_id=1, source_target_pairs={{0,1},{1,0},{2,3},{3,2},{4,5},{5,4},{6,7},{7,6},{8,9},{9,8},{10,11... | collective-permute-start | bytes 516104 | tf_op jit(solution)/shard_map/ppermute | solution.py:616
  59.8 9.7 %collective-permute-start.26 = (bf16[104,768]{1,0:T(8,128)(2,1)S(1)}, bf16[104,768]{1,0:T(8,128)(2,1)S(1)}, u32[]{:S(2)}, u32[]{:S(2)}) collective-permute-start(bf16[104,768]{1,0:T(8,128)(2,1)S(1)} %out_pair.1.own), channel_id=1, source_target_pairs={{0,3},{1,2},{2,1},{3,0},{4,7},{5,6},{6,5},{7,4},{8,11},{9,10},{10,... | collective-permute-start | bytes 479240 | tf_op jit(solution)/shard_map/ppermute | solution.py:616
  61.7 6.2 %collective-permute-start.28 = (bf16[96,768]{1,0:T(8,128)(2,1)S(1)}, bf16[96,768]{1,0:T(8,128)(2,1)S(1)}, u32[]{:S(2)}, u32[]{:S(2)}) collective-permute-start(bf16[96,768]{1,0:T(8,128)(2,1)S(1)} %get-tuple-element.185), channel_id=1, source_target_pairs={{0,24},{8,16},{16,8},{24,0},{1,25},{9,17},{17,9},{25,1},{2,26},{10... | collective-permute-start | bytes 442376 | tf_op jit(solution)/shard_map/ppermute | solution.py:619
  69.8 13.9 %collective-permute-start.32 = (bf16[2,96,2176]{2,1,0:T(8,128)(2,1)S(1)}, bf16[2,96,2176]{2,1,0:T(8,128)(2,1)S(1)}, u32[]{:S(2)}, u32[]{:S(2)}) collective-permute-start(bf16[2,96,2176]{2,1,0:T(8,128)(2,1)S(1)} %get-tuple-element.200), channel_id=1, source_target_pairs={{0,8},{4,20},{8,0},{12,28},{16,24},{20,4},{24,16},{28,12},{1,9},{5... | collective-permute-start | bytes 2506760 | tf_op jit(solution)/shard_map/ppermute | solution.py:623
  71.4 12.2 %collective-permute-start.31 = (bf16[200,768]{1,0:T(8,128)(2,1)S(1)}, bf16[200,768]{1,0:T(8,128)(2,1)S(1)}, u32[]{:S(2)}, u32[]{:S(2)}) collective-permute-start(bf16[200,768]{1,0:T(8,128)(2,1)S(1)} %get-tuple-element.194.out_own), channel_id=1, source_target_pairs={{0,1},{1,0},{2,3},{3,2},{4,5},{5,4},{6,7},{7,6},{8,9},{9,8},{10,11... | collective-permute-start | bytes 921608 | tf_op jit(solution)/shard_map/ppermute | solution.py:616
  72.1 11.5 %collective-permute-start.30 = (bf16[112,768]{1,0:T(8,128)(2,1)S(1)}, bf16[112,768]{1,0:T(8,128)(2,1)S(1)}, u32[]{:S(2)}, u32[]{:S(2)}) collective-permute-start(bf16[112,768]{1,0:T(8,128)(2,1)S(1)} %in_pair.1.own), channel_id=1, source_target_pairs={{0,3},{1,2},{2,1},{3,0},{4,7},{5,6},{6,5},{7,4},{8,11},{9,10},{10,... | collective-permute-start | bytes 516104 | tf_op jit(solution)/shard_map/ppermute | solution.py:616
  83.7 2.9 %collective-permute-start.36 = (f32[144,768]{1,0:T(8,128)S(1)}, f32[144,768]{1,0:T(8,128)S(1)}, u32[]{:S(2)}, u32[]{:S(2)}) collective-permute-start(f32[144,768]{1,0:T(8,128)S(1)} %get-tuple-element.210.vec), channel_id=1, source_target_pairs={{0,4},{4,0},{1,5},{5,1},{2,6},{6,2},{3,7},{7,3},{8,12},{12,8},{9,1... | collective-permute-start | bytes 1327112 | tf_op jit(solution)/shard_map/ppermute | solution.py:613
  84.0 9.0 %collective-permute-start.35 = (bf16[96,2176]{1,0:T(8,128)(2,1)S(1)}, bf16[96,2176]{1,0:T(8,128)(2,1)S(1)}, u32[]{:S(2)}, u32[]{:S(2)}) collective-permute-start(bf16[96,2176]{1,0:T(8,128)(2,1)S(1)} %get-tuple-element.209), channel_id=1, source_target_pairs={{0,16},{4,12},{8,24},{12,4},{16,0},{20,28},{24,8},{28,20},{1,17},{... | collective-permute-start | bytes 1253384 | tf_op jit(solution)/shard_map/ppermute | solution.py:623
  84.7 8.3 %collective-permute-start.33 = (bf16[104,768]{1,0:T(8,128)(2,1)S(1)}, bf16[104,768]{1,0:T(8,128)(2,1)S(1)}, u32[]{:S(2)}, u32[]{:S(2)}) collective-permute-start(bf16[104,768]{1,0:T(8,128)(2,1)S(1)} %get-tuple-element.204.in_own), channel_id=1, source_target_pairs={{0,1},{1,0},{2,3},{3,2},{4,5},{5,4},{6,7},{7,6},{8,9},{9,8},{10,11... | collective-permute-start | bytes 479240 | tf_op jit(solution)/shard_map/ppermute | solution.py:616
  84.8 8.2 %collective-permute-start.34 = (bf16[48,768]{1,0:T(8,128)(2,1)S(1)}, bf16[48,768]{1,0:T(8,128)(2,1)S(1)}, u32[]{:S(2)}, u32[]{:S(2)}) collective-permute-start(bf16[48,768]{1,0:T(8,128)(2,1)S(1)} %get-tuple-element.206), channel_id=1, source_target_pairs={{0,3},{1,2},{2,1},{3,0},{4,7},{5,6},{6,5},{7,4},{8,11},{9,10},{10,... | collective-permute-start | bytes 221192 | tf_op jit(solution)/shard_map/ppermute | solution.py:616
  86.7 6.2 %collective-permute-start.37 = (bf16[16,576]{1,0:T(8,128)(2,1)S(1)}, bf16[16,576]{1,0:T(8,128)(2,1)S(1)}, u32[]{:S(2)}, u32[]{:S(2)}) collective-permute-start(bf16[16,576]{1,0:T(8,128)(2,1)S(1)} %get-tuple-element.211), channel_id=1, source_target_pairs={{0,8},{4,20},{8,0},{12,28},{16,24},{20,4},{24,16},{28,12},{1,9},{5... | collective-permute-start | bytes 55304 | tf_op jit(solution)/shard_map/ppermute | solution.py:623
  88.1 4.9 %collective-permute-start.38 = (bf16[16,576]{1,0:T(8,128)(2,1)S(1)}, bf16[16,576]{1,0:T(8,128)(2,1)S(1)}, u32[]{:S(2)}, u32[]{:S(2)}) collective-permute-start(bf16[16,576]{1,0:T(8,128)(2,1)S(1)} %get-tuple-element.212), channel_id=1, source_target_pairs={{0,24},{8,16},{16,8},{24,0},{1,25},{9,17},{17,9},{25,1},{2,26},{10... | collective-permute-start | bytes 55304 | tf_op jit(solution)/shard_map/ppermute | solution.py:619
  93.2 2.4 %collective-permute-start.39 = (bf16[256,768]{1,0:T(8,128)(2,1)S(1)}, bf16[256,768]{1,0:T(8,128)(2,1)S(1)}, u32[]{:S(2)}, u32[]{:S(2)}) collective-permute-start(bf16[256,768]{1,0:T(8,128)(2,1)S(1)} %get-tuple-element.217), channel_id=1, source_target_pairs={{0,4},{4,0},{1,5},{5,1},{2,6},{6,2},{3,7},{7,3},{8,12},{12,8},{9,1... | collective-permute-start | bytes 1179656 | tf_op jit(solution)/shard_map/ppermute | solution.py:613
  93.5 2.1 %collective-permute-start.40 = (bf16[96,1536]{1,0:T(8,128)(2,1)S(1)}, bf16[96,1536]{1,0:T(8,128)(2,1)S(1)}, u32[]{:S(2)}, u32[]{:S(2)}) collective-permute-start(bf16[96,1536]{1,0:T(8,128)(2,1)S(1)} %get-tuple-element.225), channel_id=1, source_target_pairs={{0,4},{4,0},{1,5},{5,1},{2,6},{6,2},{3,7},{7,3},{8,12},{12,8},{9,1... | collective-permute-start | bytes 884744 | tf_op jit(solution)/shard_map/ppermute | solution.py:613
  94.0 1.6 %collective-permute-start.41 = (bf16[112,576]{1,0:T(8,128)(2,1)S(1)}, bf16[112,576]{1,0:T(8,128)(2,1)S(1)}, u32[]{:S(2)}, u32[]{:S(2)}) collective-permute-start(bf16[112,576]{1,0:T(8,128)(2,1)S(1)} %get-tuple-element.227), channel_id=1, source_target_pairs={{0,4},{4,0},{1,5},{5,1},{2,6},{6,2},{3,7},{7,3},{8,12},{12,8},{9,1... | collective-permute-start | bytes 387080 | tf_op jit(solution)/shard_map/ppermute | solution.py:613

commit v7 on v6

--- a/solution.py
+++ b/solution.py
@@ -69,7 +69,7 @@
 
 
 def row_half(t):
-    return (t ^ (t >> 1)) & 1
+    return t & 1
 
 
 def lanes(parts):
@@ -97,10 +97,11 @@
         self.rows = 2 * self.padded
         self.part = self.width // 4
         self.chunk = self.part // 2
-        self.tail = self.part // 4
+        self.tail = self.chunk // 4
         self.direct = nf == 4
         self.cols = 2 * self.ff + nt * self.inner
         self.early = 1280 if self.ff == 768 else self.ff
+        self.first = 3 * self.ff // 2
         self.all_cols = 2 * self.ff + -(-3 * self.inner // 128) * 128
         self.dense = self.rows * self.inner // 128
 
@@ -369,34 +370,39 @@
     store_halves(z, dot(normed[...], grads[...], TN), 0, keep, sent, 2 * z.ff)
 
 
-def proj_grad_kernel(z, low, att, keep, sent=None):
-    value = dot(low[...], att[...], TN)
-    b = lax.axis_index("fsdp") if z.direct else 0
-    for j in range(4):
-        keep[j ^ b] = value[j * z.part : (j + 1) * z.part]
-    if z.direct:
-        c = lax.axis_index("ctx")
-        sent[: z.part, :] = keep[2 - c].astype(LOW)
-        sent[z.part :, :] = keep[3, z.half_of(1 - c), :].astype(LOW)
-
-
-def split_kernel(z, keep, keep_qkv, received, out, kept):
+def proj_grad_kernel(z, low, att, keep, sent):
+    store_halves(z, dot(low[...], att[...], TN), 0, keep, sent)
+
+
+def split_kernel(z, keep, received, out, kept):
+    c = lax.axis_index("ctx")
+    cols = pl.ds(0, z.first)
+    for target, at, kind in ((out, (1 + c, 3), LOW), (kept, (0, 2 - c), F32)):
+        for i in range(2):
+            rows = pl.ds(pl.multiple_of(at[i] * z.chunk, 16), z.chunk)
+            target[i] = (keep[at[i], :, cols] + received[rows, cols].astype(F32)).astype(kind)
+
+
+def split_rest_kernel(z, keep, keep_qkv, received, out, kept):
     c = lax.axis_index("ctx")
     for target, at, kind in ((out, (1 + c, 3), LOW), (kept, (0, 2 - c), F32)):
         for i in range(2):
             rows = pl.ds(pl.multiple_of(at[i] * z.chunk, 16), z.chunk)
-            total = keep[at[i]] + received[rows, : 2 * z.ff].astype(F32)
-            target[i, :, : 2 * z.ff] = total.astype(kind)
-            last = pl.ds(2 * z.ff, 3 * z.inner)
-            total = keep_qkv[at[i]] + received[rows, last].astype(F32)
-            target[i, :, last] = total.astype(kind)
-            target[i, :, 2 * z.ff + 3 * z.inner :] = jnp.zeros((z.chunk, z.all_cols - 2 * z.ff - 3 * z.inner), kind)
-
-
-def proj_one_kernel(z, keep, received, near, far):
-    c = lax.axis_index("ctx")
-    near[...] = (keep[1 + c] + received[: z.part, :].astype(F32)).astype(LOW)
-    far[...] = (keep[3, z.half_of(c), :] + received[z.part :, :].astype(F32)).astype(LOW)
+            n, m = 2 * z.ff - z.first, 3 * z.inner
+            total = keep[at[i], :, z.first :] + received[rows, z.first : 2 * z.ff].astype(F32)
+            target[i, :, :n] = total.astype(kind)
+            total = keep_qkv[at[i]] + received[rows, 2 * z.ff : 2 * z.ff + m].astype(F32)
+            target[i, :, n : n + m] = total.astype(kind)
+            target[i, :, n + m :] = jnp.zeros((z.chunk, target.shape[2] - n - m), kind)
+
+
+def proj_one_kernel(z, keep, received, own, *sends):
+    for k in range(4):
+        total = keep[k] + received[k * z.chunk : (k + 1) * z.chunk, :].astype(F32)
+        if k == 0:
+            own[...] = total
+        else:
+            sends[k - 1][...] = total.astype(LOW)
 
 
 def by_half(mine, other):
@@ -456,8 +462,8 @@
 
 def out_total_kernel(z, own, received, middle, small, *refs):
     if z.direct:
-        keep, near, far, kept, out, scratch = refs
-        proj_two_kernel(z, keep, near, far, out, kept, scratch)
+        keep, *parts, kept, out, scratch = refs
+        proj_two_kernel(z, keep, parts, out, kept, scratch)
     else:
         (out,) = refs
     rows = z.half_rows(row_half(lax.axis_index("tp")))
@@ -465,16 +471,14 @@
     out[: z.padded, :] = (middle[rows, :] + total + small[5:6]).astype(LOW)
 
 
-def proj_two_kernel(z, keep, near, far, out, kept, scratch):
-    c, t = lax.axis_index("ctx"), lax.axis_index("tp")
-    other = read(far)
-    zero = jnp.zeros(other.shape, F32)
-    proj = keep[0] + read(near) + rows_of([jnp.where(c == 0, other, zero), jnp.where(c == 0, zero, other)])
+def proj_two_kernel(z, own, parts, out, kept, scratch):
+    t = lax.axis_index("tp")
+    proj = own[...] + sum(read(p) for p in parts)
     for i in range(z.nt):
         scratch[i] = fold(proj[:, i * z.inner : (i + 1) * z.inner])
     kept[0] = scratch[t]
-    kept[1] = scratch[t ^ 3]
-    out[z.padded :, :] = rows_of([scratch[t ^ 1], scratch[t ^ 2]]).astype(LOW)
+    kept[1] = scratch[t ^ 2]
+    out[z.padded :, :] = rows_of([scratch[t ^ 1], scratch[t ^ 3]]).astype(LOW)
 
 
 def sum_rows_kernel(z, own, received, small, qv, out, vec):
@@ -492,9 +496,11 @@
     sent[...] = (kept[1] + arrived[z.tail :]).astype(LOW)
 
 
-def cross_kernel(kept, received, own, out):
-    own[...] = kept[0] + received[0].astype(F32)
-    out[...] = (kept[1] + received[1].astype(F32)).astype(LOW)
+def cross_kernel(z, kept, rest_kept, received, rest_received, own, out):
+    own[:, : z.first] = kept[0] + received[0].astype(F32)
+    own[:, z.first :] = rest_kept[0] + rest_received[0].astype(F32)
+    out[:, : z.first] = (kept[1] + received[1].astype(F32)).astype(LOW)
+    out[:, z.first :] = (rest_kept[1] + rest_received[1].astype(F32)).astype(LOW)
 
 
 def small_kernel(z, vec, their, near, far, own, scratch):
@@ -575,8 +581,8 @@
 def final_kernel(z, mine, theirs, *refs):
     if z.direct:
         proj_own, feed_own, feed_in, qkv_own, qkv_in, output, input_grad, proj, up, down, *rest = refs
-        total = proj_own[...] + theirs[2 * z.padded :, :].astype(F32)
-        proj[...] = unfold(z, total).T
+        other = theirs[2 * z.padded :, :].astype(F32)
+        proj[...] = by_half(unfold(z, proj_own[...]), unfold(z, other)).T
         feed_final_kernel(z, feed_own, feed_in, up, down)
         qkv_final_kernel(z, qkv_own, qkv_in, *rest[:-1])
         scratch = rest[-1]
@@ -763,10 +769,9 @@
             [normed_two, grad_pre, cot, hidden],
             name="feed_grad",
         )
-        keep_proj, *sent_proj = call(
+        keep_proj, sent_proj = call(
             part(proj_grad_kernel, z),
-            [shape((4, z.part, nt * inner), F32)]
-            + ([shape((z.part + chunk, nt * inner), LOW)] if z.direct else []),
+            [shape((4, chunk, nt * inner), F32), shape((4 * chunk, nt * inner), LOW)],
             [part_low, att_all],
             name="proj_grad",
         )
@@ -779,17 +784,17 @@
         )
         out_one = to_tp(out_sent, 1)
         if z.direct:
-            proj_in = other_core(sent_proj[0])
+            proj_in = other_core(sent_proj)
             att_got, out_one, keep, sent, proj_in = tie((att_got, out_one, keep, sent, proj_in))
-            near, far = call(
+            proj_own, *sends = call(
                 part(proj_one_kernel, z),
-                [shape((z.part, nt * inner), LOW), shape((chunk, nt * inner), LOW)],
+                [shape((chunk, nt * inner), F32)] + [shape((chunk, nt * inner), LOW)] * 3,
                 [keep_proj, proj_in],
                 name="proj_one",
             )
-            proj_in = [to_near(near), to_far(far)]
+            proj_in = [lax.ppermute(sends[k - 1], "fsdp", [(i, i ^ k) for i in range(nf)]) for k in (3, 1)]
         (out_low,) = call(add_low_kernel, [shape((z.padded, width), LOW)], [out_kept, out_one], name="out_pair")
-        out_two = to_tp(out_low, 3)
+        out_two = to_tp(out_low, 2)
 
         grads, qv_sum, in_kept, in_sent = call(
             part(back_kernel, z),
@@ -812,27 +817,36 @@
         )
         if z.direct:
             sent = other_core(sent)
-            in_one, out_two, proj_in, sent = tie((in_one, out_two, proj_in, sent))
+            sent, last_send = tie((sent, sends[1]))
+            proj_in.append(lax.ppermute(last_send, "fsdp", [(i, i ^ 2) for i in range(nf)]))
             grad_sent, grad_kept = call(
                 part(split_kernel, z),
-                [shape((2, chunk, all_cols), LOW), shape((2, chunk, all_cols), F32)],
+                [shape((2, chunk, z.first), LOW), shape((2, chunk, z.first), F32)],
+                [keep, sent],
+                name="split",
+            )
+            grad_in = to_near(grad_sent)
+            in_one, out_two, proj_in, sent = tie((in_one, out_two, proj_in, sent))
+            rest_sent, rest_kept = call(
+                part(split_rest_kernel, z),
+                [shape((2, chunk, all_cols - z.first), LOW), shape((2, chunk, all_cols - z.first), F32)],
                 [keep, keep_qkv, sent],
-                name="split",
-            )
-            grad_in = to_near(grad_sent)
+                name="split_rest",
+            )
+            rest_in = to_near(rest_sent)
         (in_low,) = call(add_low_kernel, [shape((z.padded + 8, width), LOW)], [in_kept, in_one], name="in_pair")
-        in_two = to_tp(in_low, 3)
+        in_two = to_tp(in_low, 2)
         *proj_kept, out_low = call(
             part(out_total_kernel, z),
             ([shape((2, z.tail, width), F32)] if z.direct else [])
             + [shape((z.padded + (2 * z.tail if z.direct else 0), width), LOW)],
-            [out_low, out_two, middle, small] + ([keep_proj] + proj_in if z.direct else []),
+            [out_low, out_two, middle, small] + ([proj_own] + proj_in if z.direct else []),
             [pltpu.VMEM((nt, z.tail, width), F32)] if z.direct else [],
             name="out_total",
         )
         out_in = to_tp(out_low, 1)
         if z.direct:
-            in_two, out_in, grad_in = tie((in_two, out_in, grad_in))
+            in_two, out_in, grad_in, rest_in = tie((in_two, out_in, grad_in, rest_in))
         in_low, vec = call(
             part(sum_rows_kernel, z),
             [shape((z.padded, width), LOW), shape((VEC_ROWS, width), F32)],
@@ -843,9 +857,9 @@
         proj_all = []
         if z.direct:
             grad_own, cross = call(
-                cross_kernel,
+                part(cross_kernel, z),
                 [shape((chunk, all_cols), F32), shape((chunk, all_cols), LOW)],
-                [grad_kept, grad_in],
+                [grad_kept, rest_kept, grad_in, rest_in],
                 name="cross",
             )
             cross = to_cross(cross)
@@ -855,7 +869,7 @@
                 [proj_kept[0], out_in],
                 name="proj_pair",
             )
-            proj_two = to_tp(proj_sent, 3)
+            proj_two = to_tp(proj_sent, 2)
             near, far, small_own = call(
                 part(small_kernel, z),
                 [shape((EXTRA, 3 * inner), LOW)] * 2 + [shape((EXTRA, 3 * inner), F32)],
@@ -919,7 +933,7 @@
             total = scatter(joined(jnp.concatenate([keep, jnp.pad(keep_qkv, ((0, 0), (0, 0), (0, extra)))], 2), sent))
             fc1_grad, fc2_grad = total[:, :ff], total[:, ff : 2 * ff]
             qkv_grad = total[:, 2 * ff : 2 * ff + 3 * inner].reshape(z.shard, 3, inner).transpose(1, 0, 2)
-            proj_grad = scatter(keep_proj.reshape(width, -1).astype(LOW)).astype(LOW)
+            proj_grad = scatter(joined(keep_proj, sent_proj)).astype(LOW)
             proj_grad = lax.psum_scatter(proj_grad, "tp", scatter_dimension=1, tiled=True).astype(F32).T
 
             def own_columns(value):

time: 97.8 us -> 95.4 us (0.975)
  waiting for transfers between devices: 42.2 us -> 37.4 us
  starting transfers between devices: 35.6 us -> 38.1 us
    ppermute x3 -> x2, waiting for transfers between devices: 4.86 us -> 1.09 us  [to_far(): return lax.ppermute(value, 'fsdp', [(i, i ^ 3) for i in range(nf)])]
    ppermute x13, waiting for transfers between devices: 29.4 us -> 25.7 us  [to_tp(): return lax.ppermute(value, 'tp', [(i, i ^ k) for i in range(nt)])]
    ppermute x0 -> x3, starting transfers between devices: none -> 3.55 us  [the longest x2 2.57 us: local(): lax.ppermute(sends[k - 1], 'fsdp', [(i, i ^ k) for i in range(nf)])]
    ppermute x0 -> x3, waiting for transfers between devices: none -> 2.68 us  [the longest x2 2.67 us: local(): lax.ppermute(sends[k - 1], 'fsdp', [(i, i ^ k) for i in range(nf)])]
    ppermute x3 -> x2, starting transfers between devices: 4.68 us -> 3.1 us  [to_far(): return lax.ppermute(value, 'fsdp', [(i, i ^ 3) for i in range(nf)])]
    pallas_call x27 -> x28, Pallas kernels: 16 us -> 15.9 us  [call(): pl.pallas_call(kernel, out_shape=tuple(outs), in_specs=in_specs or [VMEM]...]
  transfers between devices with their start and end apart: 42 -> 44, of which waited for: 15 -> 18; matrix products, arithmetic and copies ran while one was open for 0% -> 0% of each run, Pallas kernels for 7% -> 8%
where the time goes in v7:
time: 95.4 us; the launch traced here: 95.1 us
  starting transfers between devices  38.1 us (40%)
  waiting for transfers between devices  37.4 us (39%)
  Pallas kernels  15.9 us (17%)
  local copies, waits for them, and re-layouts  2.9 us (3%)
    ppermute x13, waiting for transfers between devices, to_tp(): return lax.ppermute(value, 'tp', [(i, i ^ k) for i in range(nt)])  25.7 us
    ppermute x13, starting transfers between devices, to_tp(): return lax.ppermute(value, 'tp', [(i, i ^ k) for i in range(nt)])  16.4 us
    pallas_call x28, Pallas kernels, call(): pl.pallas_call(kernel, out_shape=tuple(outs), in_specs=in_specs or [VMEM]...  15.9 us
    ppermute x9, starting transfers between devices, neighbours(): return lax.ppermute(value, ('fsdp', 'ctx'), pairs)  10.1 us
    ppermute x16, waiting for transfers between devices, other_core(): return lax.ppermute(value, 'ctx', [(0, 1), (1, 0)])  4.99 us
    ppermute x16, starting transfers between devices, other_core(): return lax.ppermute(value, 'ctx', [(0, 1), (1, 0)])  3.36 us
    ppermute x2, starting transfers between devices, to_far(): return lax.ppermute(value, 'fsdp', [(i, i ^ 3) for i in range(nf)])  3.1 us
    ppermute x9, waiting for transfers between devices, neighbours(): return lax.ppermute(value, ('fsdp', 'ctx'), pairs)  2.93 us
  transfers between devices with their start and end apart: 44, of which 18 were waited for; matrix products, arithmetic and copies ran while one was open for 0% of the time, Pallas kernels for 8%

profile of v7, /device:TPU:0, one launch (start us, length us, event | category | flops | bytes accessed | tf_op | source)
XLA Modules:
  0.0 95.1 jit_solution(15928816064274313120)
XLA Ops:
  0.7 0.5 collective-permute-start.2
  1.3 2.0 %pack.1 = (bf16[208,576]{1,0:T(8,128)(2,1)}, bf16[112,576]{1,0:T(8,128)(2,1)}, bf16[296,192]{1,0:T(8,128)(2,1)}, bf16[96,192]{1,0:T(8,128)(2,1)}) custom-call(bf16[3,192,192]{2,1,0:T(8,128)(2,1)} %bitcast.15, bf16[192,192]{1,0:T(8,128)(2,1)} %refs_1_.1, bf16[12,16]{1,0:T(8,128)(2,1)} %refs_2_.1, bf16[3,2,16]{2,1,0:T(2,128)(2,1)} %bitcast.16, ...), custom_call_target="tpu_custom_call" | custom-call | tf_op jit(solution)/shard_map/pack/pallas_call | solution.py:34
  3.3 3.0 %collective-permute-start.4 = (bf16[208,576]{1,0:T(8,128)(2,1)}, bf16[208,576]{1,0:T(8,128)(2,1)S(1)}, u32[]{:S(2)}, u32[]{:S(2)}) collective-permute-start(bf16[208,576]{1,0:T(8,128)(2,1)} %get-tuple-element.141.refs_0_), channel_id=1, source_target_pairs={{0,8},{4,20},{8,0},{12,28},{16,24},{20,4},{24,16},{28,12},{1,9},{5... | collective-permute-start | bytes 718856 | tf_op jit(solution)/shard_map/ppermute | solution.py:629
  6.3 1.5 %collective-permute-start.5 = (bf16[112,576]{1,0:T(8,128)(2,1)}, bf16[112,576]{1,0:T(8,128)(2,1)S(1)}, u32[]{:S(2)}, u32[]{:S(2)}) collective-permute-start(bf16[112,576]{1,0:T(8,128)(2,1)} %get-tuple-element.142), channel_id=1, source_target_pairs={{0,24},{8,16},{16,8},{24,0},{1,25},{9,17},{17,9},{25,1},{2,26},{10... | collective-permute-start | bytes 387080 | tf_op jit(solution)/shard_map/ppermute | solution.py:625
  7.8 1.6 %collective-permute-start.6 = (bf16[296,192]{1,0:T(8,128)(2,1)}, bf16[296,192]{1,0:T(8,128)(2,1)S(1)}, u32[]{:S(2)}, u32[]{:S(2)}) collective-permute-start(bf16[296,192]{1,0:T(8,128)(2,1)} %get-tuple-element.143.proj_t), channel_id=1, source_target_pairs={{0,1},{4,7},{1,0},{5,6},{2,3},{6,5},{3,2},{7,4},{8,9},{12,15},{9,8... | collective-permute-start | bytes 341000 | tf_op jit(solution)/shard_map/ppermute | solution.py:639
  9.3 2.6 %collective-permute-start.7 = (bf16[96,192]{1,0:T(8,128)(2,1)}, bf16[96,192]{1,0:T(8,128)(2,1)S(1)}, u32[]{:S(2)}, u32[]{:S(2)}) collective-permute-start(bf16[96,192]{1,0:T(8,128)(2,1)} %get-tuple-element.144), channel_id=1, source_target_pairs={{0,2},{1,3},{2,0},{3,1},{4,6},{5,7},{6,4},{7,5},{8,10},{9,11},{10,... | collective-permute-start | bytes 110600 | tf_op jit(solution)/shard_map/ppermute | solution.py:622
  11.9 1.0 %copy-done.2 = bf16[192,768]{1,0:T(8,128)(2,1)S(1)} copy-done((bf16[192,768]{1,0:T(8,128)(2,1)S(1)}, bf16[192,768]{1,0:T(8,128)(2,1)}, u32[]{:S(2)}) %copy-start.2) | copy-done | bytes 294936
  12.9 1.0 %copy-done.3 = bf16[768,192]{0,1:T(8,128)(2,1)S(1)} copy-done((bf16[768,192]{0,1:T(8,128)(2,1)S(1)}, bf16[768,192]{0,1:T(8,128)(2,1)}, u32[]{:S(2)}) %copy-start.3) | copy-done | bytes 294936
  14.0 1.6 %collective-permute-start = (bf16[192,1280]{1,0:T(8,128)(2,1)S(1)}, bf16[192,1280]{1,0:T(8,128)(2,1)S(1)}, u32[]{:S(2)}, u32[]{:S(2)}) collective-permute-start(bf16[192,1280]{1,0:T(8,128)(2,1)S(1)} %get-tuple-element.136.refs_0_), channel_id=1, source_target_pairs={{0,8},{4,20},{8,0},{12,28},{16,24},{20,4},{24,16},{28,12},{1,9},{5... | collective-permute-start | bytes 1474568 | tf_op jit(solution)/shard_map/ppermute | solution.py:629
  15.6 1.0 %copy-done = bf16[2,98,768]{2,0,1:T(2,128)(2,1)S(1)} copy-done((bf16[2,98,768]{2,0,1:T(2,128)(2,1)S(1)}, bf16[2,98,768]{2,0,1:T(2,128)(2,1)}, u32[]{:S(2)}) %copy-start) | copy-done | bytes 301080
  16.6 0.4 cotangent.1.refs_14_.cot
  16.9 0.6 frame.1
  17.6 0.5 collective-permute-start.9
  18.1 0.9 collective-permute-done.9.far_their
  19.3 0.6 collective-permute-start.10
  19.9 0.5 collective-permute-start.13
  20.4 1.2 %collective-permute-done.13.refs_4_ = bf16[112,576]{1,0:T(8,128)(2,1)S(1)} collective-permute-done((bf16[112,576]{1,0:T(8,128)(2,1)S(1)}, bf16[112,576]{1,0:T(8,128)(2,1)S(1)}, u32[]{:S(2)}, u32[]{:S(2)}) %collective-permute-start.13) | collective-permute-done | bytes 129056 | tf_op jit(solution)/shard_map/ppermute | solution.py:619
  21.6 1.3 %attend.1 = (f32[8,768]{1,0:T(8,128)S(1)}, bf16[4,192,576]{2,1,0:T(8,128)(2,1)S(1)}, bf16[208,768]{1,0:T(8,128)(2,1)S(1)}, bf16[3,208,192]{2,1,0:T(8,128)(2,1)S(...) custom-call(bf16[208,576]{1,0:T(8,128)(2,1)S(1)} %copy-done.4, ...), custom_call_target="tpu_custom_call" | custom-call | tf_op jit(solution)/shard_map/attend/pallas_call | solution.py:34
  22.9 1.5 %collective-permute-start.14 = (bf16[312,128]{1,0:T(8,128)(2,1)S(1)}, bf16[312,128]{1,0:T(8,128)(2,1)S(1)}, u32[]{:S(2)}, u32[]{:S(2)}) collective-permute-start(bf16[312,128]{1,0:T(8,128)(2,1)S(1)} %get-tuple-element.157.first.refs_10_), channel_id=1, source_target_pairs={{0,2},{1,3},{2,0},{3,1},{4,6},{5,7},{6,4},{7,5},{8,10},{9,11},{10,... | collective-permute-start | bytes 239624 | tf_op jit(solution)/shard_map/ppermute | solution.py:622
  24.5 0.5 collective-permute-start.16
  24.9 2.3 %collective-permute-done.10.value.refs_4_ = bf16[192,1024]{1,0:T(8,128)(2,1)S(1)} collective-permute-done((bf16[192,1024]{1,0:T(8,128)(2,1)S(1)}, bf16[192,1024]{1,0:T(8,128)(2,1)S(1)}, u32[]{:S(2)}, u32[]{:S(2)}) %collective-permute-start.10) | collective-permute-done | bytes 393248 | tf_op jit(solution)/shard_map/ppermute | solution.py:629
  27.3 0.5 collective-permute-start.17
  27.7 2.2 %collective-permute-done.14.second.refs_11_ = bf16[312,128]{1,0:T(8,128)(2,1)S(1)} collective-permute-done((bf16[312,128]{1,0:T(8,128)(2,1)S(1)}, bf16[312,128]{1,0:T(8,128)(2,1)S(1)}, u32[]{:S(2)}, u32[]{:S(2)}) %collective-permute-start.14) | collective-permute-done | bytes 79904 | tf_op jit(solution)/shard_map/ppermute | solution.py:622
  30.1 0.6 collective-permute-done.16.refs_6_
  30.7 5.5 %collective-permute-done.15.refs_12_ = bf16[2,328,128]{2,1,0:T(8,128)(2,1)S(1)} collective-permute-done((bf16[2,328,128]{2,1,0:T(8,128)(2,1)S(1)}, bf16[2,328,128]{2,1,0:T(8,128)(2,1)S(1)}, u32[]{:S(2)}, u32[]{:S(2)}) %collective-permute-start.15) | collective-permute-done | bytes 167968 | tf_op jit(solution)/shard_map/ppermute | solution.py:622
  36.2 0.5 collective-permute-start.19
  36.8 1.3 %collective-permute-done.19.refs_9_ = bf16[96,1024]{1,0:T(8,128)(2,1)S(1)} collective-permute-done((bf16[96,1024]{1,0:T(8,128)(2,1)S(1)}, bf16[96,1024]{1,0:T(8,128)(2,1)S(1)}, u32[]{:S(2)}, u32[]{:S(2)}) %collective-permute-start.19) | collective-permute-done | bytes 196640 | tf_op jit(solution)/shard_map/ppermute | solution.py:619
  38.0 3.1 %feed.1 = (bf16[4,192,2304]{2,1,0:T(8,128)(2,1)S(1)}, bf16[208,768]{1,0:T(8,128)(2,1)S(1)}, f32[208,768]{1,0:T(8,128)S(1)}, bf16[208,768]{1,0:T(8,128)(2,1)S(1)}...) custom-call(bf16[192,1280]{1,0:T(8,128)(2,1)S(1)} %get-tuple-element, ...), custom_call_target="tpu_custom_call" | custom-call | tf_op jit(solution)/shard_map/feed/pallas_call | solution.py:34
  41.1 0.5 proj_grad.1
  41.7 0.2 collective-permute-start.24
  41.9 0.6 down.1
  42.5 0.3 collective-permute-start.23
  42.9 1.7 %collective-permute-start.20 = (bf16[312,128]{1,0:T(8,128)(2,1)S(1)}, bf16[312,128]{1,0:T(8,128)(2,1)S(1)}, u32[]{:S(2)}, u32[]{:S(2)}) collective-permute-start(bf16[312,128]{1,0:T(8,128)(2,1)S(1)} %get-tuple-element.167), channel_id=1, source_target_pairs={{0,1},{1,0},{2,3},{3,2},{4,5},{5,4},{6,7},{7,6},{8,9},{9,8},{10,11... | collective-permute-start | bytes 239624 | tf_op jit(solution)/shard_map/ppermute | solution.py:622
  44.6 1.3 %collective-permute-start.21 = (bf16[312,128]{1,0:T(8,128)(2,1)S(1)}, bf16[312,128]{1,0:T(8,128)(2,1)S(1)}, u32[]{:S(2)}, u32[]{:S(2)}) collective-permute-start(bf16[312,128]{1,0:T(8,128)(2,1)S(1)} %get-tuple-element.168), channel_id=1, source_target_pairs={{0,2},{1,3},{2,0},{3,1},{4,6},{5,7},{6,4},{7,5},{8,10},{9,11},{10,... | collective-permute-start | bytes 239624 | tf_op jit(solution)/shard_map/ppermute | solution.py:622
  45.9 1.4 %collective-permute-start.22 = (bf16[312,128]{1,0:T(8,128)(2,1)S(1)}, bf16[312,128]{1,0:T(8,128)(2,1)S(1)}, u32[]{:S(2)}, u32[]{:S(2)}) collective-permute-start(bf16[312,128]{1,0:T(8,128)(2,1)S(1)} %get-tuple-element.169), channel_id=1, source_target_pairs={{0,3},{1,2},{2,1},{3,0},{4,7},{5,6},{6,5},{7,4},{8,11},{9,10},{10,... | collective-permute-start | bytes 239624 | tf_op jit(solution)/shard_map/ppermute | solution.py:622
  47.2 0.9 feed_grad.1
  48.2 4.2 %collective-permute-done.20.refs_1_ = bf16[312,128]{1,0:T(8,128)(2,1)S(1)} collective-permute-done((bf16[312,128]{1,0:T(8,128)(2,1)S(1)}, bf16[312,128]{1,0:T(8,128)(2,1)S(1)}, u32[]{:S(2)}, u32[]{:S(2)}) %collective-permute-start.20) | collective-permute-done | bytes 79904 | tf_op jit(solution)/shard_map/ppermute | solution.py:622
  52.4 2.6 %collective-permute-done.22.refs_3_ = bf16[312,128]{1,0:T(8,128)(2,1)S(1)} collective-permute-done((bf16[312,128]{1,0:T(8,128)(2,1)S(1)}, bf16[312,128]{1,0:T(8,128)(2,1)S(1)}, u32[]{:S(2)}, u32[]{:S(2)}) %collective-permute-start.22) | collective-permute-done | bytes 79904 | tf_op jit(solution)/shard_map/ppermute | solution.py:622
  54.9 2.0 %back.1 = (bf16[208,576]{1,0:T(8,128)(2,1)S(1)}, f32[1,576]{1,0:T(1,128)S(1)}, f32[112,768]{1,0:T(8,128)S(1)}, bf16[112,768]{1,0:T(8,128)(2,1)S(1)}) custom-call(f32[208,192]{1,0:T(8,128)S(1)} %get-tuple-element.179.refs_0_, bf16[312,128]{1,0:T(8,128)(2,1)S(1)} %collective-permute-done.20.refs_1_, bf16[312,128]{1,0:T(8,128)(2,1)S(1)} %collective-permute-done.21.refs_2_, ...), custom_call_target="tpu_custom_call" | custom-call | tf_op jit(solution)/shard_map/back/pallas_call | solution.py:34
  56.9 0.6 qkv_grad.1
  57.8 1.4 %collective-permute-start.27 = (bf16[96,768]{1,0:T(8,128)(2,1)S(1)}, bf16[96,768]{1,0:T(8,128)(2,1)S(1)}, u32[]{:S(2)}, u32[]{:S(2)}) collective-permute-start(bf16[96,768]{1,0:T(8,128)(2,1)S(1)} %get-tuple-element.192), channel_id=1, source_target_pairs={{0,24},{8,16},{16,8},{24,0},{1,25},{9,17},{17,9},{25,1},{2,26},{10... | collective-permute-start | bytes 442376 | tf_op jit(solution)/shard_map/ppermute | solution.py:795
  59.2 0.8 collective-permute-start.25
  60.0 1.5 %collective-permute-start.26 = (bf16[104,768]{1,0:T(8,128)(2,1)S(1)}, bf16[104,768]{1,0:T(8,128)(2,1)S(1)}, u32[]{:S(2)}, u32[]{:S(2)}) collective-permute-start(bf16[104,768]{1,0:T(8,128)(2,1)S(1)} %out_pair.1.own), channel_id=1, source_target_pairs={{0,2},{1,3},{2,0},{3,1},{4,6},{5,7},{6,4},{7,5},{8,10},{9,11},{10,... | collective-permute-start | bytes 479240 | tf_op jit(solution)/shard_map/ppermute | solution.py:622
  61.5 1.2 %collective-permute-start.28 = (bf16[96,768]{1,0:T(8,128)(2,1)S(1)}, bf16[96,768]{1,0:T(8,128)(2,1)S(1)}, u32[]{:S(2)}, u32[]{:S(2)}) collective-permute-start(bf16[96,768]{1,0:T(8,128)(2,1)S(1)} %get-tuple-element.193), channel_id=1, source_target_pairs={{0,8},{8,0},{16,24},{24,16},{1,9},{9,1},{17,25},{25,17},{2,10},{10... | collective-permute-start | bytes 442376 | tf_op jit(solution)/shard_map/ppermute | solution.py:795
  62.7 1.0 %collective-permute-start.30 = (bf16[96,768]{1,0:T(8,128)(2,1)S(1)}, bf16[96,768]{1,0:T(8,128)(2,1)S(1)}, u32[]{:S(2)}, u32[]{:S(2)}) collective-permute-start(bf16[96,768]{1,0:T(8,128)(2,1)S(1)} %get-tuple-element.199), channel_id=1, source_target_pairs={{0,16},{8,24},{16,0},{24,8},{1,17},{9,25},{17,1},{25,9},{2,18},{10... | collective-permute-start | bytes 442376 | tf_op jit(solution)/shard_map/ppermute | solution.py:821
  63.8 1.6 %collective-permute-done.27.refs_1_ = bf16[96,768]{1,0:T(8,128)(2,1)S(1)} collective-permute-done((bf16[96,768]{1,0:T(8,128)(2,1)S(1)}, bf16[96,768]{1,0:T(8,128)(2,1)S(1)}, u32[]{:S(2)}, u32[]{:S(2)}) %collective-permute-start.27) | collective-permute-done | bytes 147488 | tf_op jit(solution)/shard_map/ppermute | solution.py:795
  65.4 0.8 collective-permute-start.33
  66.3 1.1 %collective-permute-done.28.refs_2_ = bf16[96,768]{1,0:T(8,128)(2,1)S(1)} collective-permute-done((bf16[96,768]{1,0:T(8,128)(2,1)S(1)}, bf16[96,768]{1,0:T(8,128)(2,1)S(1)}, u32[]{:S(2)}, u32[]{:S(2)}) %collective-permute-start.28) | collective-permute-done | bytes 147488 | tf_op jit(solution)/shard_map/ppermute | solution.py:795
  67.3 3.1 %collective-permute-done.26.received = bf16[104,768]{1,0:T(8,128)(2,1)S(1)} collective-permute-done((bf16[104,768]{1,0:T(8,128)(2,1)S(1)}, bf16[104,768]{1,0:T(8,128)(2,1)S(1)}, u32[]{:S(2)}, u32[]{:S(2)}) %collective-permute-start.26) | collective-permute-done | bytes 159776 | tf_op jit(solution)/shard_map/ppermute | solution.py:622
  70.6 1.1 %collective-permute-start.34 = (bf16[2,96,1024]{2,1,0:T(8,128)(2,1)S(1)}, bf16[2,96,1024]{2,1,0:T(8,128)(2,1)S(1)}, u32[]{:S(2)}, u32[]{:S(2)}) collective-permute-start(bf16[2,96,1024]{2,1,0:T(8,128)(2,1)S(1)} %get-tuple-element.214), channel_id=1, source_target_pairs={{0,8},{4,20},{8,0},{12,28},{16,24},{20,4},{24,16},{28,12},{1,9},{5... | collective-permute-start | bytes 1179656 | tf_op jit(solution)/shard_map/ppermute | solution.py:629
  72.1 2.4 %collective-permute-start.31 = (bf16[112,768]{1,0:T(8,128)(2,1)S(1)}, bf16[112,768]{1,0:T(8,128)(2,1)S(1)}, u32[]{:S(2)}, u32[]{:S(2)}) collective-permute-start(bf16[112,768]{1,0:T(8,128)(2,1)S(1)} %in_pair.1.own), channel_id=1, source_target_pairs={{0,2},{1,3},{2,0},{3,1},{4,6},{5,7},{6,4},{7,5},{8,10},{9,11},{10,... | collective-permute-start | bytes 516104 | tf_op jit(solution)/shard_map/ppermute | solution.py:622
  74.5 5.6 %collective-permute-done.31.received = bf16[112,768]{1,0:T(8,128)(2,1)S(1)} collective-permute-done((bf16[112,768]{1,0:T(8,128)(2,1)S(1)}, bf16[112,768]{1,0:T(8,128)(2,1)S(1)}, u32[]{:S(2)}, u32[]{:S(2)}) %collective-permute-start.31) | collective-permute-done | bytes 172064 | tf_op jit(solution)/shard_map/ppermute | solution.py:622
  80.0 0.6 collective-permute-done.32.received.out_in
  81.0 1.2 %collective-permute-start.37 = (bf16[96,2176]{1,0:T(8,128)(2,1)S(1)}, bf16[96,2176]{1,0:T(8,128)(2,1)S(1)}, u32[]{:S(2)}, u32[]{:S(2)}) collective-permute-start(bf16[96,2176]{1,0:T(8,128)(2,1)S(1)} %get-tuple-element.225), channel_id=1, source_target_pairs={{0,16},{4,12},{8,24},{12,4},{16,0},{20,28},{24,8},{28,20},{1,17},{... | collective-permute-start | bytes 1253384 | tf_op jit(solution)/shard_map/ppermute | solution.py:629
  82.2 2.0 %collective-permute-start.35 = (bf16[104,768]{1,0:T(8,128)(2,1)S(1)}, bf16[104,768]{1,0:T(8,128)(2,1)S(1)}, u32[]{:S(2)}, u32[]{:S(2)}) collective-permute-start(bf16[104,768]{1,0:T(8,128)(2,1)S(1)} %get-tuple-element.218.in_own), channel_id=1, source_target_pairs={{0,1},{1,0},{2,3},{3,2},{4,5},{5,4},{6,7},{7,6},{8,9},{9,8},{10,11... | collective-permute-start | bytes 479240 | tf_op jit(solution)/shard_map/ppermute | solution.py:622
  84.2 0.7 collective-permute-start.36
  85.1 0.8 collective-permute-start.39
  85.9 1.6 %collective-permute-start.40 = (bf16[16,576]{1,0:T(8,128)(2,1)S(1)}, bf16[16,576]{1,0:T(8,128)(2,1)S(1)}, u32[]{:S(2)}, u32[]{:S(2)}) collective-permute-start(bf16[16,576]{1,0:T(8,128)(2,1)S(1)} %get-tuple-element.228), channel_id=1, source_target_pairs={{0,24},{8,16},{16,8},{24,0},{1,25},{9,17},{17,9},{25,1},{2,26},{10... | collective-permute-start | bytes 55304 | tf_op jit(solution)/shard_map/ppermute | solution.py:625
  87.5 1.7 %collective-permute-done.36.refs_1_ = bf16[24,768]{1,0:T(8,128)(2,1)S(1)} collective-permute-done((bf16[24,768]{1,0:T(8,128)(2,1)S(1)}, bf16[24,768]{1,0:T(8,128)(2,1)S(1)}, u32[]{:S(2)}, u32[]{:S(2)}) %collective-permute-start.36) | collective-permute-done | bytes 36896 | tf_op jit(solution)/shard_map/ppermute | solution.py:622
  89.2 0.3 collective-permute-done.35.in_in
  89.5 1.1 %collective-permute-done.40.far = bf16[16,576]{1,0:T(8,128)(2,1)S(1)} collective-permute-done((bf16[16,576]{1,0:T(8,128)(2,1)S(1)}, bf16[16,576]{1,0:T(8,128)(2,1)S(1)}, u32[]{:S(2)}, u32[]{:S(2)}) %collective-permute-start.40) | collective-permute-done | bytes 18464 | tf_op jit(solution)/shard_map/ppermute | solution.py:625
  91.0 0.6 collective-permute-start.42
  91.6 1.5 %collective-permute-done.43.refs_4_ = bf16[112,576]{1,0:T(8,128)(2,1)S(1)} collective-permute-done((bf16[112,576]{1,0:T(8,128)(2,1)S(1)}, bf16[112,576]{1,0:T(8,128)(2,1)S(1)}, u32[]{:S(2)}, u32[]{:S(2)}) %collective-permute-start.43) | collective-permute-done | bytes 129056 | tf_op jit(solution)/shard_map/ppermute | solution.py:619
  93.1 2.0 %final.1 = (bf16[98,2,768]{2,1,0:T(2,128)(2,1)}, f32[98,2,768]{2,1,0:T(2,128)}, f32[192,192]{1,0:T(8,128)}, f32[192,768]{1,0:T(8,128)}, f32[192,768]{1,0:T(8,128...) custom-call(f32[2,104,768]{2,1,0:T(8,128)S(1)} %get-tuple-element.23, ...), custom_call_target="tpu_custom_call" | custom-call | tf_op jit(solution)/shard_map/final/pallas_call | solution.py:34
  (64 shorter events, 2.6 us)
Async XLA Ops:
  0.6 16.3 %copy-start.1 = (bf16[2,98,768]{2,0,1:T(2,128)(2,1)S(1)}, bf16[2,98,768]{2,0,1:T(2,128)(2,1)}, u32[]{:S(2)}) copy-start(bf16[2,98,768]{2,0,1:T(2,128)(2,1)} %param.14) | copy-start | bytes 903172
  0.7 2.6 %collective-permute-start.2 = (bf16[98,2,768]{2,1,0:T(2,128)(2,1)}, bf16[98,2,768]{2,1,0:T(2,128)(2,1)S(1)}, u32[]{:S(2)}, u32[]{:S(2)}) collective-permute-start(bf16[98,2,768]{2,1,0:T(2,128)(2,1)} %bitcast.12), channel_id=1, source_target_pairs={{0,4},{4,0},{1,5},{5,1},{2,6},{6,2},{3,7},{7,3},{8,12},{12,8},{9,1... | collective-permute-start | bytes 903176 | tf_op jit(solution)/shard_map/ppermute | solution.py:619
  1.2 2.1 %collective-permute-start.3 = (bf16[98,2,768]{2,1,0:T(2,128)(2,1)}, bf16[98,2,768]{2,1,0:T(2,128)(2,1)S(1)}, u32[]{:S(2)}, u32[]{:S(2)}) collective-permute-start(bf16[98,2,768]{2,1,0:T(2,128)(2,1)} %bitcast.10), channel_id=1, source_target_pairs={{0,4},{4,0},{1,5},{5,1},{2,6},{6,2},{3,7},{7,3},{8,12},{12,8},{9,1... | collective-permute-start | bytes 903176 | tf_op jit(solution)/shard_map/ppermute | solution.py:619
  3.3 14.2 %collective-permute-start.4 = (bf16[208,576]{1,0:T(8,128)(2,1)}, bf16[208,576]{1,0:T(8,128)(2,1)S(1)}, u32[]{:S(2)}, u32[]{:S(2)}) collective-permute-start(bf16[208,576]{1,0:T(8,128)(2,1)} %get-tuple-element.141.refs_0_), channel_id=1, source_target_pairs={{0,8},{4,20},{8,0},{12,28},{16,24},{20,4},{24,16},{28,12},{1,9},{5... | collective-permute-start | bytes 718856 | tf_op jit(solution)/shard_map/ppermute | solution.py:629
  6.3 11.2 %collective-permute-start.5 = (bf16[112,576]{1,0:T(8,128)(2,1)}, bf16[112,576]{1,0:T(8,128)(2,1)S(1)}, u32[]{:S(2)}, u32[]{:S(2)}) collective-permute-start(bf16[112,576]{1,0:T(8,128)(2,1)} %get-tuple-element.142), channel_id=1, source_target_pairs={{0,24},{8,16},{16,8},{24,0},{1,25},{9,17},{17,9},{25,1},{2,26},{10... | collective-permute-start | bytes 387080 | tf_op jit(solution)/shard_map/ppermute | solution.py:625
  7.8 9.7 %collective-permute-start.6 = (bf16[296,192]{1,0:T(8,128)(2,1)}, bf16[296,192]{1,0:T(8,128)(2,1)S(1)}, u32[]{:S(2)}, u32[]{:S(2)}) collective-permute-start(bf16[296,192]{1,0:T(8,128)(2,1)} %get-tuple-element.143.proj_t), channel_id=1, source_target_pairs={{0,1},{4,7},{1,0},{5,6},{2,3},{6,5},{3,2},{7,4},{8,9},{12,15},{9,8... | collective-permute-start | bytes 341000 | tf_op jit(solution)/shard_map/ppermute | solution.py:639
  9.3 8.2 %collective-permute-start.7 = (bf16[96,192]{1,0:T(8,128)(2,1)}, bf16[96,192]{1,0:T(8,128)(2,1)S(1)}, u32[]{:S(2)}, u32[]{:S(2)}) collective-permute-start(bf16[96,192]{1,0:T(8,128)(2,1)} %get-tuple-element.144), channel_id=1, source_target_pairs={{0,2},{1,3},{2,0},{3,1},{4,6},{5,7},{6,4},{7,5},{8,10},{9,11},{10,... | collective-permute-start | bytes 110600 | tf_op jit(solution)/shard_map/ppermute | solution.py:622
  11.9 1.0 %copy-start.2 = (bf16[192,768]{1,0:T(8,128)(2,1)S(1)}, bf16[192,768]{1,0:T(8,128)(2,1)}, u32[]{:S(2)}) copy-start(bf16[192,768]{1,0:T(8,128)(2,1)} %up.1) | copy-start | bytes 884740
  12.9 1.0 %copy-start.3 = (bf16[768,192]{0,1:T(8,128)(2,1)S(1)}, bf16[768,192]{0,1:T(8,128)(2,1)}, u32[]{:S(2)}) copy-start(bf16[768,192]{0,1:T(8,128)(2,1)} %param.25) | copy-start | bytes 884740
  13.9 5.2 %copy-start.5 = (bf16[296,192]{1,0:T(8,128)(2,1)S(1)}, bf16[296,192]{1,0:T(8,128)(2,1)}, u32[]{:S(2)}) copy-start(bf16[296,192]{1,0:T(8,128)(2,1)} %get-tuple-element.143.proj_t) | copy-start | bytes 340996
  13.9 7.7 %copy-start.4 = (bf16[208,576]{1,0:T(8,128)(2,1)S(1)}, bf16[208,576]{1,0:T(8,128)(2,1)}, u32[]{:S(2)}) copy-start(bf16[208,576]{1,0:T(8,128)(2,1)} %get-tuple-element.141.refs_0_) | copy-start | bytes 718852
  14.0 10.4 %collective-permute-start = (bf16[192,1280]{1,0:T(8,128)(2,1)S(1)}, bf16[192,1280]{1,0:T(8,128)(2,1)S(1)}, u32[]{:S(2)}, u32[]{:S(2)}) collective-permute-start(bf16[192,1280]{1,0:T(8,128)(2,1)S(1)} %get-tuple-element.136.refs_0_), channel_id=1, source_target_pairs={{0,8},{4,20},{8,0},{12,28},{16,24},{20,4},{24,16},{28,12},{1,9},{5... | collective-permute-start | bytes 1474568 | tf_op jit(solution)/shard_map/ppermute | solution.py:629
  15.6 1.0 %copy-start = (bf16[2,98,768]{2,0,1:T(2,128)(2,1)S(1)}, bf16[2,98,768]{2,0,1:T(2,128)(2,1)}, u32[]{:S(2)}) copy-start(bf16[2,98,768]{2,0,1:T(2,128)(2,1)} %param.27) | copy-start | bytes 903172
  17.5 1.5 %collective-permute-start.8 = (bf16[296,192]{1,0:T(8,128)(2,1)S(1)}, bf16[296,192]{1,0:T(8,128)(2,1)S(1)}, u32[]{:S(2)}, u32[]{:S(2)}) collective-permute-start(bf16[296,192]{1,0:T(8,128)(2,1)S(1)} %collective-permute-done.6.near_in), channel_id=1, source_target_pairs={{0,4},{4,0},{1,5},{5,1},{2,6},{6,2},{3,7},{7,3},{8,12},{12,8},{9,1... | collective-permute-start | bytes 341000 | tf_op jit(solution)/shard_map/ppermute | solution.py:619
  17.6 1.4 %collective-permute-start.9 = (bf16[96,192]{1,0:T(8,128)(2,1)S(1)}, bf16[96,192]{1,0:T(8,128)(2,1)S(1)}, u32[]{:S(2)}, u32[]{:S(2)}) collective-permute-start(bf16[96,192]{1,0:T(8,128)(2,1)S(1)} %collective-permute-done.7.far_in), channel_id=1, source_target_pairs={{0,4},{4,0},{1,5},{5,1},{2,6},{6,2},{3,7},{7,3},{8,12},{12,8},{9,1... | collective-permute-start | bytes 110600 | tf_op jit(solution)/shard_map/ppermute | solution.py:619
  19.3 8.0 %collective-permute-start.10 = (bf16[192,1024]{1,0:T(8,128)(2,1)S(1)}, bf16[192,1024]{1,0:T(8,128)(2,1)S(1)}, u32[]{:S(2)}, u32[]{:S(2)}) collective-permute-start(bf16[192,1024]{1,0:T(8,128)(2,1)S(1)} %pack_rest.1.refs_3_), channel_id=1, source_target_pairs={{0,8},{4,20},{8,0},{12,28},{16,24},{20,4},{24,16},{28,12},{1,9},{5... | collective-permute-start | bytes 1179656 | tf_op jit(solution)/shard_map/ppermute | solution.py:629
  19.9 1.8 %collective-permute-start.12 = (bf16[208,576]{1,0:T(8,128)(2,1)S(1)}, bf16[208,576]{1,0:T(8,128)(2,1)S(1)}, u32[]{:S(2)}, u32[]{:S(2)}) collective-permute-start(bf16[208,576]{1,0:T(8,128)(2,1)S(1)} %collective-permute-done.4.refs_1_), channel_id=1, source_target_pairs={{0,4},{4,0},{1,5},{5,1},{2,6},{6,2},{3,7},{7,3},{8,12},{12,8},{9,1... | collective-permute-start | bytes 718856 | tf_op jit(solution)/shard_map/ppermute | solution.py:619
  19.9 1.7 %collective-permute-start.13 = (bf16[112,576]{1,0:T(8,128)(2,1)S(1)}, bf16[112,576]{1,0:T(8,128)(2,1)S(1)}, u32[]{:S(2)}, u32[]{:S(2)}) collective-permute-start(bf16[112,576]{1,0:T(8,128)(2,1)S(1)} %collective-permute-done.5.refs_3_), channel_id=1, source_target_pairs={{0,4},{4,0},{1,5},{5,1},{2,6},{6,2},{3,7},{7,3},{8,12},{12,8},{9,1... | collective-permute-start | bytes 387080 | tf_op jit(solution)/shard_map/ppermute | solution.py:619
  22.9 7.0 %collective-permute-start.14 = (bf16[312,128]{1,0:T(8,128)(2,1)S(1)}, bf16[312,128]{1,0:T(8,128)(2,1)S(1)}, u32[]{:S(2)}, u32[]{:S(2)}) collective-permute-start(bf16[312,128]{1,0:T(8,128)(2,1)S(1)} %get-tuple-element.157.first.refs_10_), channel_id=1, source_target_pairs={{0,2},{1,3},{2,0},{3,1},{4,6},{5,7},{6,4},{7,5},{8,10},{9,11},{10,... | collective-permute-start | bytes 239624 | tf_op jit(solution)/shard_map/ppermute | solution.py:622
  24.5 6.3 %collective-permute-start.16 = (bf16[96,1280]{1,0:T(8,128)(2,1)S(1)}, bf16[96,1280]{1,0:T(8,128)(2,1)S(1)}, u32[]{:S(2)}, u32[]{:S(2)}) collective-permute-start(bf16[96,1280]{1,0:T(8,128)(2,1)S(1)} %cut.2), channel_id=1, source_target_pairs={{0,16},{4,12},{8,24},{12,4},{16,0},{20,28},{24,8},{28,20},{1,17},{... | collective-permute-start | bytes 737288 | tf_op jit(solution)/shard_map/ppermute | solution.py:629
  24.9 11.8 %collective-permute-start.1 = (bf16[192,1280]{1,0:T(8,128)(2,1)S(1)}, bf16[192,1280]{1,0:T(8,128)(2,1)S(1)}, u32[]{:S(2)}, u32[]{:S(2)}) collective-permute-start(bf16[192,1280]{1,0:T(8,128)(2,1)S(1)} %collective-permute-done.value.refs_1_), channel_id=1, source_target_pairs={{0,4},{4,0},{1,5},{5,1},{2,6},{6,2},{3,7},{7,3},{8,12},{12,8},{9,1... | collective-permute-start | bytes 1474568 | tf_op jit(solution)/shard_map/ppermute | solution.py:619
  27.3 9.0 %collective-permute-start.17 = (bf16[96,1024]{1,0:T(8,128)(2,1)S(1)}, bf16[96,1024]{1,0:T(8,128)(2,1)S(1)}, u32[]{:S(2)}, u32[]{:S(2)}) collective-permute-start(bf16[96,1024]{1,0:T(8,128)(2,1)S(1)} %cut.3), channel_id=1, source_target_pairs={{0,16},{4,12},{8,24},{12,4},{16,0},{20,28},{24,8},{28,20},{1,17},{... | collective-permute-start | bytes 589832 | tf_op jit(solution)/shard_map/ppermute | solution.py:629
  29.9 6.3 %collective-permute-start.15 = (bf16[2,328,128]{2,1,0:T(8,128)(2,1)S(1)}, bf16[2,328,128]{2,1,0:T(8,128)(2,1)S(1)}, u32[]{:S(2)}, u32[]{:S(2)}) collective-permute-start(bf16[2,328,128]{2,1,0:T(8,128)(2,1)S(1)} %pair.1), channel_id=1, source_target_pairs={{0,1},{1,0},{2,3},{3,2},{4,5},{5,4},{6,7},{7,6},{8,9},{9,8},{10,11... | collective-permute-start | bytes 503816 | tf_op jit(solution)/shard_map/ppermute | solution.py:622
  30.0 6.7 %collective-permute-start.11 = (bf16[192,1024]{1,0:T(8,128)(2,1)S(1)}, bf16[192,1024]{1,0:T(8,128)(2,1)S(1)}, u32[]{:S(2)}, u32[]{:S(2)}) collective-permute-start(bf16[192,1024]{1,0:T(8,128)(2,1)S(1)} %collective-permute-done.10.value.refs_4_), channel_id=1, source_target_pairs={{0,4},{4,0},{1,5},{5,1},{2,6},{6,2},{3,7},{7,3},{8,12},{12,8},{9,1... | collective-permute-start | bytes 1179656 | tf_op jit(solution)/shard_map/ppermute | solution.py:619
  36.2 1.8 %collective-permute-start.18 = (bf16[96,1280]{1,0:T(8,128)(2,1)S(1)}, bf16[96,1280]{1,0:T(8,128)(2,1)S(1)}, u32[]{:S(2)}, u32[]{:S(2)}) collective-permute-start(bf16[96,1280]{1,0:T(8,128)(2,1)S(1)} %collective-permute-done.16.refs_6_), channel_id=1, source_target_pairs={{0,4},{4,0},{1,5},{5,1},{2,6},{6,2},{3,7},{7,3},{8,12},{12,8},{9,1... | collective-permute-start | bytes 737288 | tf_op jit(solution)/shard_map/ppermute | solution.py:619
  36.2 1.8 %collective-permute-start.19 = (bf16[96,1024]{1,0:T(8,128)(2,1)S(1)}, bf16[96,1024]{1,0:T(8,128)(2,1)S(1)}, u32[]{:S(2)}, u32[]{:S(2)}) collective-permute-start(bf16[96,1024]{1,0:T(8,128)(2,1)S(1)} %collective-permute-done.17.refs_8_), channel_id=1, source_target_pairs={{0,4},{4,0},{1,5},{5,1},{2,6},{6,2},{3,7},{7,3},{8,12},{12,8},{9,1... | collective-permute-start | bytes 589832 | tf_op jit(solution)/shard_map/ppermute | solution.py:619
  41.7 13.3 %collective-permute-start.24 = (bf16[384,768]{1,0:T(8,128)(2,1)S(1)}, bf16[384,768]{1,0:T(8,128)(2,1)S(1)}, u32[]{:S(2)}, u32[]{:S(2)}) collective-permute-start(bf16[384,768]{1,0:T(8,128)(2,1)S(1)} %get-tuple-element.177), channel_id=1, source_target_pairs={{0,4},{4,0},{1,5},{5,1},{2,6},{6,2},{3,7},{7,3},{8,12},{12,8},{9,1... | collective-permute-start | bytes 1769480 | tf_op jit(solution)/shard_map/ppermute | solution.py:619
  42.5 12.4 %collective-permute-start.23 = (bf16[104,768]{1,0:T(8,128)(2,1)S(1)}, bf16[104,768]{1,0:T(8,128)(2,1)S(1)}, u32[]{:S(2)}, u32[]{:S(2)}) collective-permute-start(bf16[104,768]{1,0:T(8,128)(2,1)S(1)} %get-tuple-element.170), channel_id=1, source_target_pairs={{0,1},{1,0},{2,3},{3,2},{4,5},{5,4},{6,7},{7,6},{8,9},{9,8},{10,11... | collective-permute-start | bytes 479240 | tf_op jit(solution)/shard_map/ppermute | solution.py:622
  42.9 9.5 %collective-permute-start.20 = (bf16[312,128]{1,0:T(8,128)(2,1)S(1)}, bf16[312,128]{1,0:T(8,128)(2,1)S(1)}, u32[]{:S(2)}, u32[]{:S(2)}) collective-permute-start(bf16[312,128]{1,0:T(8,128)(2,1)S(1)} %get-tuple-element.167), channel_id=1, source_target_pairs={{0,1},{1,0},{2,3},{3,2},{4,5},{5,4},{6,7},{7,6},{8,9},{9,8},{10,11... | collective-permute-start | bytes 239624 | tf_op jit(solution)/shard_map/ppermute | solution.py:622
  44.6 7.8 %collective-permute-start.21 = (bf16[312,128]{1,0:T(8,128)(2,1)S(1)}, bf16[312,128]{1,0:T(8,128)(2,1)S(1)}, u32[]{:S(2)}, u32[]{:S(2)}) collective-permute-start(bf16[312,128]{1,0:T(8,128)(2,1)S(1)} %get-tuple-element.168), channel_id=1, source_target_pairs={{0,2},{1,3},{2,0},{3,1},{4,6},{5,7},{6,4},{7,5},{8,10},{9,11},{10,... | collective-permute-start | bytes 239624 | tf_op jit(solution)/shard_map/ppermute | solution.py:622
  45.9 9.0 %collective-permute-start.22 = (bf16[312,128]{1,0:T(8,128)(2,1)S(1)}, bf16[312,128]{1,0:T(8,128)(2,1)S(1)}, u32[]{:S(2)}, u32[]{:S(2)}) collective-permute-start(bf16[312,128]{1,0:T(8,128)(2,1)S(1)} %get-tuple-element.169), channel_id=1, source_target_pairs={{0,3},{1,2},{2,1},{3,0},{4,7},{5,6},{6,5},{7,4},{8,11},{9,10},{10,... | collective-permute-start | bytes 239624 | tf_op jit(solution)/shard_map/ppermute | solution.py:622
  57.6 5.1 %collective-permute-start.29 = (bf16[384,2176]{1,0:T(8,128)(2,1)S(1)}, bf16[384,2176]{1,0:T(8,128)(2,1)S(1)}, u32[]{:S(2)}, u32[]{:S(2)}) collective-permute-start(bf16[384,2176]{1,0:T(8,128)(2,1)S(1)} %get-tuple-element.197), channel_id=1, source_target_pairs={{0,4},{4,0},{1,5},{5,1},{2,6},{6,2},{3,7},{7,3},{8,12},{12,8},{9,1... | collective-permute-start | bytes 5013512 | tf_op jit(solution)/shard_map/ppermute | solution.py:619
  57.8 7.6 %collective-permute-start.27 = (bf16[96,768]{1,0:T(8,128)(2,1)S(1)}, bf16[96,768]{1,0:T(8,128)(2,1)S(1)}, u32[]{:S(2)}, u32[]{:S(2)}) collective-permute-start(bf16[96,768]{1,0:T(8,128)(2,1)S(1)} %get-tuple-element.192), channel_id=1, source_target_pairs={{0,24},{8,16},{16,8},{24,0},{1,25},{9,17},{17,9},{25,1},{2,26},{10... | collective-permute-start | bytes 442376 | tf_op jit(solution)/shard_map/ppermute | solution.py:795
  59.2 11.2 %collective-permute-start.25 = (bf16[112,768]{1,0:T(8,128)(2,1)S(1)}, bf16[112,768]{1,0:T(8,128)(2,1)S(1)}, u32[]{:S(2)}, u32[]{:S(2)}) collective-permute-start(bf16[112,768]{1,0:T(8,128)(2,1)S(1)} %get-tuple-element.189), channel_id=1, source_target_pairs={{0,1},{1,0},{2,3},{3,2},{4,5},{5,4},{6,7},{7,6},{8,9},{9,8},{10,11... | collective-permute-start | bytes 516104 | tf_op jit(solution)/shard_map/ppermute | solution.py:622
  60.0 10.4 %collective-permute-start.26 = (bf16[104,768]{1,0:T(8,128)(2,1)S(1)}, bf16[104,768]{1,0:T(8,128)(2,1)S(1)}, u32[]{:S(2)}, u32[]{:S(2)}) collective-permute-start(bf16[104,768]{1,0:T(8,128)(2,1)S(1)} %out_pair.1.own), channel_id=1, source_target_pairs={{0,2},{1,3},{2,0},{3,1},{4,6},{5,7},{6,4},{7,5},{8,10},{9,11},{10,... | collective-permute-start | bytes 479240 | tf_op jit(solution)/shard_map/ppermute | solution.py:622
  61.5 5.8 %collective-permute-start.28 = (bf16[96,768]{1,0:T(8,128)(2,1)S(1)}, bf16[96,768]{1,0:T(8,128)(2,1)S(1)}, u32[]{:S(2)}, u32[]{:S(2)}) collective-permute-start(bf16[96,768]{1,0:T(8,128)(2,1)S(1)} %get-tuple-element.193), channel_id=1, source_target_pairs={{0,8},{8,0},{16,24},{24,16},{1,9},{9,1},{17,25},{25,17},{2,10},{10... | collective-permute-start | bytes 442376 | tf_op jit(solution)/shard_map/ppermute | solution.py:795
  62.7 7.7 %collective-permute-start.30 = (bf16[96,768]{1,0:T(8,128)(2,1)S(1)}, bf16[96,768]{1,0:T(8,128)(2,1)S(1)}, u32[]{:S(2)}, u32[]{:S(2)}) collective-permute-start(bf16[96,768]{1,0:T(8,128)(2,1)S(1)} %get-tuple-element.199), channel_id=1, source_target_pairs={{0,16},{8,24},{16,0},{24,8},{1,17},{9,25},{17,1},{25,9},{2,18},{10... | collective-permute-start | bytes 442376 | tf_op jit(solution)/shard_map/ppermute | solution.py:821
  65.4 15.3 %collective-permute-start.33 = (bf16[2,96,1152]{2,1,0:T(8,128)(2,1)S(1)}, bf16[2,96,1152]{2,1,0:T(8,128)(2,1)S(1)}, u32[]{:S(2)}, u32[]{:S(2)}) collective-permute-start(bf16[2,96,1152]{2,1,0:T(8,128)(2,1)S(1)} %get-tuple-element.211), channel_id=1, source_target_pairs={{0,8},{4,20},{8,0},{12,28},{16,24},{20,4},{24,16},{28,12},{1,9},{5... | collective-permute-start | bytes 1327112 | tf_op jit(solution)/shard_map/ppermute | solution.py:629
  70.6 10.1 %collective-permute-start.34 = (bf16[2,96,1024]{2,1,0:T(8,128)(2,1)S(1)}, bf16[2,96,1024]{2,1,0:T(8,128)(2,1)S(1)}, u32[]{:S(2)}, u32[]{:S(2)}) collective-permute-start(bf16[2,96,1024]{2,1,0:T(8,128)(2,1)S(1)} %get-tuple-element.214), channel_id=1, source_target_pairs={{0,8},{4,20},{8,0},{12,28},{16,24},{20,4},{24,16},{28,12},{1,9},{5... | collective-permute-start | bytes 1179656 | tf_op jit(solution)/shard_map/ppermute | solution.py:629
  71.9 8.8 %collective-permute-start.32 = (bf16[152,768]{1,0:T(8,128)(2,1)S(1)}, bf16[152,768]{1,0:T(8,128)(2,1)S(1)}, u32[]{:S(2)}, u32[]{:S(2)}) collective-permute-start(bf16[152,768]{1,0:T(8,128)(2,1)S(1)} %get-tuple-element.207.out_own), channel_id=1, source_target_pairs={{0,1},{1,0},{2,3},{3,2},{4,5},{5,4},{6,7},{7,6},{8,9},{9,8},{10,11... | collective-permute-start | bytes 700424 | tf_op jit(solution)/shard_map/ppermute | solution.py:622
  72.1 8.0 %collective-permute-start.31 = (bf16[112,768]{1,0:T(8,128)(2,1)S(1)}, bf16[112,768]{1,0:T(8,128)(2,1)S(1)}, u32[]{:S(2)}, u32[]{:S(2)}) collective-permute-start(bf16[112,768]{1,0:T(8,128)(2,1)S(1)} %in_pair.1.own), channel_id=1, source_target_pairs={{0,2},{1,3},{2,0},{3,1},{4,6},{5,7},{6,4},{7,5},{8,10},{9,11},{10,... | collective-permute-start | bytes 516104 | tf_op jit(solution)/shard_map/ppermute | solution.py:622
  80.8 4.2 %collective-permute-start.38 = (f32[144,768]{1,0:T(8,128)S(1)}, f32[144,768]{1,0:T(8,128)S(1)}, u32[]{:S(2)}, u32[]{:S(2)}) collective-permute-start(f32[144,768]{1,0:T(8,128)S(1)} %get-tuple-element.226.vec), channel_id=1, source_target_pairs={{0,4},{4,0},{1,5},{5,1},{2,6},{6,2},{3,7},{7,3},{8,12},{12,8},{9,1... | collective-permute-start | bytes 1327112 | tf_op jit(solution)/shard_map/ppermute | solution.py:619
  81.0 8.5 %collective-permute-start.37 = (bf16[96,2176]{1,0:T(8,128)(2,1)S(1)}, bf16[96,2176]{1,0:T(8,128)(2,1)S(1)}, u32[]{:S(2)}, u32[]{:S(2)}) collective-permute-start(bf16[96,2176]{1,0:T(8,128)(2,1)S(1)} %get-tuple-element.225), channel_id=1, source_target_pairs={{0,16},{4,12},{8,24},{12,4},{16,0},{20,28},{24,8},{28,20},{1,17},{... | collective-permute-start | bytes 1253384 | tf_op jit(solution)/shard_map/ppermute | solution.py:629
  82.2 7.3 %collective-permute-start.35 = (bf16[104,768]{1,0:T(8,128)(2,1)S(1)}, bf16[104,768]{1,0:T(8,128)(2,1)S(1)}, u32[]{:S(2)}, u32[]{:S(2)}) collective-permute-start(bf16[104,768]{1,0:T(8,128)(2,1)S(1)} %get-tuple-element.218.in_own), channel_id=1, source_target_pairs={{0,1},{1,0},{2,3},{3,2},{4,5},{5,4},{6,7},{7,6},{8,9},{9,8},{10,11... | collective-permute-start | bytes 479240 | tf_op jit(solution)/shard_map/ppermute | solution.py:622
  84.2 5.0 %collective-permute-start.36 = (bf16[24,768]{1,0:T(8,128)(2,1)S(1)}, bf16[24,768]{1,0:T(8,128)(2,1)S(1)}, u32[]{:S(2)}, u32[]{:S(2)}) collective-permute-start(bf16[24,768]{1,0:T(8,128)(2,1)S(1)} %get-tuple-element.220), channel_id=1, source_target_pairs={{0,2},{1,3},{2,0},{3,1},{4,6},{5,7},{6,4},{7,5},{8,10},{9,11},{10,... | collective-permute-start | bytes 110600 | tf_op jit(solution)/shard_map/ppermute | solution.py:622
  85.1 4.4 %collective-permute-start.39 = (bf16[16,576]{1,0:T(8,128)(2,1)S(1)}, bf16[16,576]{1,0:T(8,128)(2,1)S(1)}, u32[]{:S(2)}, u32[]{:S(2)}) collective-permute-start(bf16[16,576]{1,0:T(8,128)(2,1)S(1)} %get-tuple-element.227), channel_id=1, source_target_pairs={{0,8},{4,20},{8,0},{12,28},{16,24},{20,4},{24,16},{28,12},{1,9},{5... | collective-permute-start | bytes 55304 | tf_op jit(solution)/shard_map/ppermute | solution.py:629
  85.9 4.7 %collective-permute-start.40 = (bf16[16,576]{1,0:T(8,128)(2,1)S(1)}, bf16[16,576]{1,0:T(8,128)(2,1)S(1)}, u32[]{:S(2)}, u32[]{:S(2)}) collective-permute-start(bf16[16,576]{1,0:T(8,128)(2,1)S(1)} %get-tuple-element.228), channel_id=1, source_target_pairs={{0,24},{8,16},{16,8},{24,0},{1,25},{9,17},{17,9},{25,1},{2,26},{10... | collective-permute-start | bytes 55304 | tf_op jit(solution)/shard_map/ppermute | solution.py:625
  90.8 2.4 %collective-permute-start.41 = (bf16[232,768]{1,0:T(8,128)(2,1)S(1)}, bf16[232,768]{1,0:T(8,128)(2,1)S(1)}, u32[]{:S(2)}, u32[]{:S(2)}) collective-permute-start(bf16[232,768]{1,0:T(8,128)(2,1)S(1)} %get-tuple-element.233), channel_id=1, source_target_pairs={{0,4},{4,0},{1,5},{5,1},{2,6},{6,2},{3,7},{7,3},{8,12},{12,8},{9,1... | collective-permute-start | bytes 1069064 | tf_op jit(solution)/shard_map/ppermute | solution.py:619
  91.0 2.2 %collective-permute-start.42 = (bf16[96,1536]{1,0:T(8,128)(2,1)S(1)}, bf16[96,1536]{1,0:T(8,128)(2,1)S(1)}, u32[]{:S(2)}, u32[]{:S(2)}) collective-permute-start(bf16[96,1536]{1,0:T(8,128)(2,1)S(1)} %get-tuple-element.241), channel_id=1, source_target_pairs={{0,4},{4,0},{1,5},{5,1},{2,6},{6,2},{3,7},{7,3},{8,12},{12,8},{9,1... | collective-permute-start | bytes 884744 | tf_op jit(solution)/shard_map/ppermute | solution.py:619
  91.5 1.6 %collective-permute-start.43 = (bf16[112,576]{1,0:T(8,128)(2,1)S(1)}, bf16[112,576]{1,0:T(8,128)(2,1)S(1)}, u32[]{:S(2)}, u32[]{:S(2)}) collective-permute-start(bf16[112,576]{1,0:T(8,128)(2,1)S(1)} %get-tuple-element.243), channel_id=1, source_target_pairs={{0,4},{4,0},{1,5},{5,1},{2,6},{6,2},{3,7},{7,3},{8,12},{12,8},{9,1... | collective-permute-start | bytes 387080 | tf_op jit(solution)/shard_map/ppermute | solution.py:619

commit v8 on v7

--- a/solution.py
+++ b/solution.py
@@ -18,7 +18,7 @@
 VMEM = pl.BlockSpec(memory_space=pltpu.VMEM)
 ANY = pl.BlockSpec(memory_space=pl.ANY)
 EXTRA = 16
-VEC_ROWS = 144
+VEC_ROWS = 16
 UP_AT, QV_AT = 256, 384
 
 
@@ -101,9 +101,11 @@
         self.direct = nf == 4
         self.cols = 2 * self.ff + nt * self.inner
         self.early = 1280 if self.ff == 768 else self.ff
-        self.first = 3 * self.ff // 2
-        self.all_cols = 2 * self.ff + -(-3 * self.inner // 128) * 128
+        self.wide = 2 * self.ff
         self.dense = self.rows * self.inner // 128
+
+    def live_rows(self, h):
+        return pl.ds(pl.multiple_of(h * self.padded, 8), self.half)
 
     def half_rows(self, h):
         return pl.ds(pl.multiple_of(h * self.padded, 8), self.padded)
@@ -183,26 +185,29 @@
     near[:, 2 * z.ff - z.early :] = lanes([scratch[i] for i in range(4)]).astype(LOW)
 
 
-def own_frame(z, keep, received):
-    c = lax.axis_index("ctx")
+def frame_of(z, keep, received, frame):
     zero = jnp.zeros((z.pad, z.width), F32)
     pieces = []
     for ref in (keep, received):
-        pieces.append(jnp.where(c == 0, ref[:, 0, :].astype(F32), ref[:, 1, :].astype(F32)))
+        pieces.append(jnp.where(frame == 0, ref[:, 0, :].astype(F32), ref[:, 1, :].astype(F32)))
         pieces.append(zero)
     return rows_of(pieces)
 
 
-def frame_kernel(z, keep, received, stream, normal, inverse):
-    values = own_frame(z, keep, received)
+def frame_kernel(z, keep, received, stream, normal, inverse, normal_their):
+    c = lax.axis_index("ctx")
+    values = frame_of(z, keep, received, c)
     stream[...] = values.astype(LOW)
     n, i = normalise(values)
     normal[...] = n
     inverse[...] = jnp.broadcast_to(i, inverse.shape)
-
-
-def cot_kernel(z, keep, received, stream):
-    stream[...] = own_frame(z, keep, received).astype(LOW)
+    normal_their[...] = normalise(frame_of(z, received, keep, 1 - c))[0]
+
+
+def cot_kernel(z, keep, received, out):
+    c = lax.axis_index("ctx")
+    out[0] = frame_of(z, keep, received, c).astype(LOW)
+    out[1] = frame_of(z, received, keep, 1 - c).astype(LOW)
 
 
 def attend_kernel(z, *refs):
@@ -269,8 +274,8 @@
         refs = refs[1:]
     att = refs[:3]
     stream, cot, small = refs[3:6]
-    (w_out, att_out, middle_out, hidden_out, normed_out, pre_out, part_out, low_out, own_att, small_out) = refs[6:16]
-    sends, heads = refs[16:-1], refs[-1]
+    w_out, middle_out, acts, part_out, own_att, small_out = refs[6:12]
+    sends, heads = refs[12:-1], refs[-1]
     t = lax.axis_index("tp")
     if z.direct:
         c, b = lax.axis_index("ctx"), lax.axis_index("fsdp")
@@ -289,30 +294,30 @@
     w_up = w_out[:, :, : z.ff].reshape(z.width, z.ff)
     w_down_t = w_out[:, :, z.ff : 2 * z.ff].reshape(z.width, z.ff)
     w_proj_t = w_out[:, :, 2 * z.ff :].reshape(z.width, z.nt * n)
-    grad_out_low = cot[...]
+    grad_out_low = cot[0]
     grad_out = grad_out_low.astype(F32)
     heads[t] = z.spread(read(att[0]))
     heads[t ^ 2] = z.spread(read(att[1]))
     heads[t ^ 1] = z.spread(att[2][0, : z.dense, :].astype(F32))
     heads[t ^ 3] = z.spread(att[2][1, : z.dense, :].astype(F32))
     attended = lanes([heads[i] for i in range(z.nt)]).astype(LOW)
-    att_out[...] = attended
+    acts[4] = attended
     branch = dot(attended, w_proj_t, NT)
     middle = stream[...].astype(F32) + branch + small[2:3]
     middle_out[...] = middle
     normal, inverse = normalise(middle)
     gain = small[3:4]
     normed = (normal * gain + small[4:5]).astype(LOW)
-    normed_out[...] = normed
+    acts[0] = normed
     hidden, slope = gelu_and_slope(dot(normed, w_up, NN) + small[6:7, : z.ff])
-    hidden_out[...] = hidden.astype(LOW)
+    acts[1] = hidden.astype(LOW)
     grad_pre = (dot(grad_out_low, w_down_t, NN) * slope).astype(LOW)
-    pre_out[...] = grad_pre
+    acts[2] = grad_pre
     grad_normed = dot(grad_pre, w_up, NT)
     part = grad_out * (1.0 / z.nt) + norm_backward(grad_normed, normal, inverse, gain)
     part_out[...] = part
     low = part.astype(LOW)
-    low_out[...] = low
+    acts[3] = low
     grad_att = dot(low, w_proj_t, NN)
     for i in range(z.nt):
         heads[i] = grad_att[:, i * n : (i + 1) * n]
@@ -327,12 +332,12 @@
     small_out[6:7, : z.ff] = total_rows(grad_pre.astype(F32))
 
 
-def down_kernel(z, hidden, w, kept, sent, scratch):
+def down_kernel(z, acts, w, kept, sent, scratch):
     h = row_half(lax.axis_index("tp"))
     w_down_t = w[:, :, z.ff : 2 * z.ff].reshape(z.width, z.ff)
-    scratch[...] = dot(hidden[...], w_down_t, NT)
-    kept[...] = scratch[z.half_rows(h), :]
-    sent[...] = scratch[z.half_rows(1 - h), :].astype(LOW)
+    scratch[...] = dot(acts[1], w_down_t, NT)
+    kept[...] = scratch[z.live_rows(h), :]
+    sent[...] = scratch[z.live_rows(1 - h), :].astype(LOW)
 
 
 def add_low_kernel(kept, received, out):
@@ -342,67 +347,51 @@
         out[rows:, :] = jnp.zeros((out.shape[0] - rows, out.shape[1]), LOW)
 
 
-def store_halves(z, value, at, keep, sent, sent_at=None):
+def store_own(z, value, at, keep):
     cols = pl.ds(at, value.shape[1])
-    sent_cols = pl.ds(at if sent_at is None else sent_at, value.shape[1])
-    c = lax.axis_index("ctx") if z.direct else 0
-    b = lax.axis_index("fsdp") if z.direct else 0
+    c, b = (lax.axis_index("ctx"), lax.axis_index("fsdp")) if z.direct else (0, 0)
     for j in range(4):
-        first = value[j * z.part : j * z.part + z.chunk]
-        second = value[j * z.part + z.chunk : (j + 1) * z.part]
+        whole = value[j * z.part : (j + 1) * z.part]
         if z.direct:
-            keep[j ^ b, :, cols] = jnp.where(c == 0, first, second)
-            rows = pl.ds(pl.multiple_of((j ^ b) * z.chunk, 16), z.chunk)
-            sent[rows, sent_cols] = jnp.where(c == 0, second, first).astype(LOW)
+            keep[j ^ b, :, cols] = jnp.where(c == 0, whole[: z.chunk], whole[z.chunk :])
         else:
-            keep[j, :, cols] = first
-            sent[pl.ds(j * z.chunk, z.chunk), sent_cols] = second.astype(LOW)
-
-
-def feed_grad_kernel(z, normed, pre, cot, hidden, keep, sent):
-    store_halves(z, dot(normed[...], pre[...], TN), 0, keep, sent)
-    store_halves(z, dot(cot[...], hidden[...], TN), z.ff, keep, sent)
-
-
-def qkv_grad_kernel(z, feed_sent, normed, grads, keep, sent):
-    sent[:, : 2 * z.ff] = feed_sent[...]
-    sent[:, 2 * z.ff + 3 * z.inner :] = jnp.zeros((sent.shape[0], z.all_cols - 2 * z.ff - 3 * z.inner), LOW)
-    store_halves(z, dot(normed[...], grads[...], TN), 0, keep, sent, 2 * z.ff)
-
-
-def proj_grad_kernel(z, low, att, keep, sent):
-    store_halves(z, dot(low[...], att[...], TN), 0, keep, sent)
-
-
-def split_kernel(z, keep, received, out, kept):
+            keep[j, :, cols] = whole
+
+
+def both_frames(left, right, left_their, right_their):
+    return dot(left, right, TN) + dot(left_their, right_their, TN)
+
+
+def feed_grad_kernel(z, acts, theirs, cot, keep):
+    store_own(z, both_frames(acts[0], acts[2], theirs[0], theirs[2]), 0, keep)
+    store_own(z, both_frames(cot[0], acts[1], cot[1], theirs[1]), z.ff, keep)
+
+
+def proj_grad_kernel(z, acts, theirs, own, *refs):
+    value = both_frames(acts[3], acts[4], theirs[3], theirs[4])
+    if not z.direct:
+        store_own(z, value, 0, own)
+        return
+    sends, keep = refs[:3], refs[3]
+    store_own(z, value, 0, keep)
+    own[...] = keep[0]
+    for k in range(1, 4):
+        sends[k - 1][...] = keep[k].astype(LOW)
+
+
+def qkv_grad_kernel(z, normed, grads, normal_their, grads_their, small, keep):
+    normed_their = (normal_their[...] * small[0:1] + small[1:2]).astype(LOW)
+    store_own(z, both_frames(normed[...], grads[...], normed_their, grads_their[...]), 0, keep)
+
+
+def split_kernel(keep, out, kept):
     c = lax.axis_index("ctx")
-    cols = pl.ds(0, z.first)
+    n = keep.shape[2]
     for target, at, kind in ((out, (1 + c, 3), LOW), (kept, (0, 2 - c), F32)):
         for i in range(2):
-            rows = pl.ds(pl.multiple_of(at[i] * z.chunk, 16), z.chunk)
-            target[i] = (keep[at[i], :, cols] + received[rows, cols].astype(F32)).astype(kind)
-
-
-def split_rest_kernel(z, keep, keep_qkv, received, out, kept):
-    c = lax.axis_index("ctx")
-    for target, at, kind in ((out, (1 + c, 3), LOW), (kept, (0, 2 - c), F32)):
-        for i in range(2):
-            rows = pl.ds(pl.multiple_of(at[i] * z.chunk, 16), z.chunk)
-            n, m = 2 * z.ff - z.first, 3 * z.inner
-            total = keep[at[i], :, z.first :] + received[rows, z.first : 2 * z.ff].astype(F32)
-            target[i, :, :n] = total.astype(kind)
-            total = keep_qkv[at[i]] + received[rows, 2 * z.ff : 2 * z.ff + m].astype(F32)
-            target[i, :, n : n + m] = total.astype(kind)
-            target[i, :, n + m :] = jnp.zeros((z.chunk, target.shape[2] - n - m), kind)
-
-
-def proj_one_kernel(z, keep, received, own, *sends):
-    for k in range(4):
-        total = keep[k] + received[k * z.chunk : (k + 1) * z.chunk, :].astype(F32)
-        if k == 0:
-            own[...] = total
-        else:
-            sends[k - 1][...] = total.astype(LOW)
+            target[i, :, :n] = keep[at[i]].astype(kind)
+            if target.shape[2] > n:
+                target[i, :, n:] = jnp.zeros((target.shape[1], target.shape[2] - n), kind)
 
 
 def by_half(mine, other):
@@ -454,58 +443,60 @@
     vec = jnp.where(row == 0, total_rows(grad_normed * normal[...]), vec)
     vec = jnp.where(row == 1, total_rows(grad_normed), vec)
     h = row_half(t)
-    kept[: z.padded, :] = scratch[z.half_rows(h), :]
-    kept[z.padded :, :] = vec
-    sent[: z.padded, :] = scratch[z.half_rows(1 - h), :].astype(LOW)
-    sent[z.padded :, :] = vec.astype(LOW)
-
-
-def out_total_kernel(z, own, received, middle, small, *refs):
-    if z.direct:
-        keep, *parts, kept, out, scratch = refs
-        proj_two_kernel(z, keep, parts, out, kept, scratch)
-    else:
-        (out,) = refs
-    rows = z.half_rows(row_half(lax.axis_index("tp")))
-    total = (read(own) + read(received))[: z.padded]
-    out[: z.padded, :] = (middle[rows, :] + total + small[5:6]).astype(LOW)
-
-
-def proj_two_kernel(z, own, parts, out, kept, scratch):
+    for at in (z.half, z.padded + z.half):
+        scratch[at : at + 6, :] = vec[:6]
+    kept[...] = scratch[z.half_rows(h), :]
+    sent[...] = scratch[z.half_rows(1 - h), :].astype(LOW)
+
+
+def out_total_kernel(z, own, received, middle, small, out):
+    rows = z.live_rows(row_half(lax.axis_index("tp")))
+    out[...] = (middle[rows, :] + read(own) + read(received) + small[5:6]).astype(LOW)
+
+
+def in_pair_kernel(z, kept, received, own, *refs):
+    parts, (out, proj_kept, scratch) = refs[:3], refs[3:]
+    out[: z.padded, :] = (kept[...] + read(received)).astype(LOW)
     t = lax.axis_index("tp")
     proj = own[...] + sum(read(p) for p in parts)
     for i in range(z.nt):
         scratch[i] = fold(proj[:, i * z.inner : (i + 1) * z.inner])
-    kept[0] = scratch[t]
-    kept[1] = scratch[t ^ 2]
-    out[z.padded :, :] = rows_of([scratch[t ^ 1], scratch[t ^ 3]]).astype(LOW)
-
-
-def sum_rows_kernel(z, own, received, small, qv, out, vec):
-    total = read(own) + read(received)
-    out[...] = total[: z.padded].astype(LOW)
-    vec[:8, :] = total[z.padded :]
-    vec[8:, :] = jnp.zeros((vec.shape[0] - 8, z.width), F32)
+    proj_kept[0] = scratch[t]
+    proj_kept[1] = scratch[t ^ 1]
+    out[z.padded :, :] = rows_of([scratch[t ^ 2], scratch[t ^ 3]]).astype(LOW)
+
+
+def sum_rows_kernel(z, own, received, small, qv, *refs):
+    if z.direct:
+        proj_kept, out, vec, proj_own = refs
+        arrived = received[z.padded :, :].astype(F32)
+        proj_own[...] = proj_kept[0] + arrived[: z.tail]
+        out[z.padded :, :] = (proj_kept[1] + arrived[z.tail :]).astype(LOW)
+    else:
+        out, vec = refs
+    total = own[: z.padded, :].astype(F32) + received[: z.padded, :].astype(F32)
+    out[: z.padded, :] = total.astype(LOW)
+    vec[...] = jnp.zeros(vec.shape, F32)
+    vec[:6, :] = total[z.half : z.half + 6]
     vec[8:9, : z.ff] = small[6:7, : z.ff]
     vec[9:10, : 3 * z.inner] = qv[...]
 
 
-def proj_pair_kernel(z, kept, received, own, sent):
-    arrived = received[z.padded :, :].astype(F32)
-    own[...] = kept[0] + arrived[: z.tail]
-    sent[...] = (kept[1] + arrived[z.tail :]).astype(LOW)
-
-
-def cross_kernel(z, kept, rest_kept, received, rest_received, own, out):
-    own[:, : z.first] = kept[0] + received[0].astype(F32)
-    own[:, z.first :] = rest_kept[0] + rest_received[0].astype(F32)
-    out[:, : z.first] = (kept[1] + received[1].astype(F32)).astype(LOW)
-    out[:, z.first :] = (rest_kept[1] + rest_received[1].astype(F32)).astype(LOW)
-
-
-def small_kernel(z, vec, their, near, far, own, scratch):
+def cross_kernel(kept, received, own, out):
+    n = kept.shape[2]
+    own[...] = kept[0] + received[0, :, :n].astype(F32)
+    out[...] = (kept[1] + received[1, :, :n].astype(F32)).astype(LOW)
+
+
+def cross_qkv_kernel(z, kept, received, small, own, out):
+    own[...] = kept[0] + received[0].astype(F32)
+    out[: z.chunk, :] = (kept[1] + received[1].astype(F32)).astype(LOW)
+    out[z.chunk :, :] = small[...].astype(LOW)
+
+
+def small_kernel(z, vec, near, cross, far, own, scratch):
     c, b = lax.axis_index("ctx"), lax.axis_index("fsdp")
-    vectors = vec[:16, :] + their[:16, :]
+    vectors = vec[...]
     up = rows_of([vectors[8:9, i * HD : (i + 1) * HD] for i in range(z.ff // HD)])
     pieces = []
     for h in range(z.heads):
@@ -518,10 +509,10 @@
         scratch[i, :8, : z.shard] = vectors[:8, i * z.shard : (i + 1) * z.shard]
         scratch[i, : z.ff // HD, UP_AT : UP_AT + w] = up[:, i * w : (i + 1) * w]
         scratch[i, : 2 * z.heads, QV_AT : QV_AT + w] = qv_rows[:, i * w : (i + 1) * w]
-    once = jnp.where(c == 0, 1.0, 0.0)
     near[...] = scratch[b ^ (1 + c)].astype(LOW)
-    far[...] = (scratch[b ^ 3] * once).astype(LOW)
-    own[...] = scratch[b] * once
+    cross[...] = scratch[b ^ (2 - c)]
+    far[...] = scratch[b ^ 3].astype(LOW)
+    own[...] = scratch[b]
 
 
 def halves_of(z, own, received):
@@ -530,28 +521,31 @@
 
 
 def swap_kernel(z, out_own, out_in, in_own, in_in, *refs):
-    out_mine, out_theirs = halves_of(z, out_own[: z.padded, :].astype(F32), out_in[: z.padded, :].astype(F32))
-    in_mine, in_theirs = halves_of(z, read(in_own), read(in_in))
-    theirs = [out_theirs, in_theirs]
+    n = z.padded
+    pad = jnp.zeros((z.pad, z.width), F32)
+    out_mine, out_theirs = halves_of(z, read(out_own), read(out_in))
+    in_mine, in_theirs = halves_of(z, in_own[:n, :].astype(F32), in_in[:n, :].astype(F32))
+    theirs = [out_theirs, pad, in_theirs]
     if z.direct:
-        proj_own, proj_in, mine, sent, proj = refs
-        total = proj_own[...] + read(proj_in)
+        proj_own, mine, sent, proj = refs
+        total = proj_own[...] + in_in[n:, :].astype(F32)
         proj[...] = total
         theirs.append(total)
     else:
         mine, sent = refs
-    mine[0] = out_mine
+    mine[0] = rows_of([out_mine, pad])
     mine[1] = in_mine
     sent[...] = rows_of(theirs).astype(LOW)
 
 
-def last_kernel(z, own, cross, small, near, far, feed_total, feed_sent, qkv_total, qkv_sent):
-    value = own[...] + read(cross)
-    feed_total[...] = value[:, : 2 * z.ff]
-    feed_sent[...] = value[:, : 2 * z.ff].astype(LOW)
-    tail = small[...] + read(near) + read(far)
+def last_kernel(z, feed, feed_in, qkv, qkv_in, small, near, far, feed_total, feed_sent, qkv_total, qkv_sent):
+    value = feed[...] + read(feed_in)
+    feed_total[...] = value
+    feed_sent[...] = value.astype(LOW)
+    value = qkv[...] + qkv_in[: z.chunk, :].astype(F32)
+    tail = small[...] + read(near) + read(far) + qkv_in[z.chunk :, :].astype(F32)
     for out, kind in ((qkv_total, F32), (qkv_sent, LOW)):
-        out[: z.chunk, :] = value[:, 2 * z.ff : 2 * z.ff + 3 * z.inner].astype(kind)
+        out[: z.chunk, :] = value.astype(kind)
         out[z.chunk :, :] = tail.astype(kind)
 
 
@@ -650,14 +644,14 @@
         x_recv = other_core(x_raw)
         cot_recv = other_core(cot_raw)
         def frames(x_recv, cot_recv):
-            stream, normal_one, inverse_one = call(
+            stream, normal_one, inverse_one, normal_their = call(
                 part(frame_kernel, z),
-                [shape((rows, width), LOW), shape((rows, width), F32), shape((rows, 128), F32)],
+                [shape((rows, width), LOW), shape((rows, width), F32), shape((rows, 128), F32), shape((rows, width), F32)],
                 [x_raw, x_recv],
                 name="frame",
             )
-            (cot,) = call(part(cot_kernel, z), [shape((rows, width), LOW)], [cot_raw, cot_recv], name="cotangent")
-            return stream, normal_one, inverse_one, cot
+            (cot,) = call(part(cot_kernel, z), [shape((2, rows, width), LOW)], [cot_raw, cot_recv], name="cotangent")
+            return stream, normal_one, inverse_one, normal_their, cot
 
         if z.direct:
             sources = [qkv3, proj_weight, fc1_bias, qv3] + vectors
@@ -687,10 +681,10 @@
                 mib=20,
                 in_specs=[ANY] * 2,
             )
-            stream, normal_one, inverse_one, cot = frames(x_recv, cot_recv)
+            stream, normal_one, inverse_one, normal_their, cot = frames(x_recv, cot_recv)
             feed_in = to_near(feed_own)
-            got, proj_got, feed_rest, stream, normal_one, inverse_one, cot = tie(
-                (got, proj_got, feed_rest, stream, normal_one, inverse_one, cot)
+            got, proj_got, feed_rest, stream, normal_one, inverse_one, normal_their, cot = tie(
+                (got, proj_got, feed_rest, stream, normal_one, inverse_one, normal_their, cot)
             )
             shared = [other_core(g) for g in got]
             qkv_in = [near, got[0], shared[0], got[1], shared[1]]
@@ -707,7 +701,7 @@
                 (half,) = call(part(cut_kernel, z), [shape((chunk, value.shape[1]), LOW)], [value], name="cut")
                 far_in.append(to_cross(half))
         else:
-            stream, normal_one, inverse_one, cot = frames(x_recv, cot_recv)
+            stream, normal_one, inverse_one, normal_their, cot = frames(x_recv, cot_recv)
             whole = lax.all_gather(qkv3, "fsdp", axis=1, tiled=True)
             whole = whole.transpose(1, 0, 2).reshape(4, z.part, 3 * inner)
             vec = jnp.stack(vectors + [vectors[0]] * 2).astype(F32)
@@ -740,18 +734,14 @@
             rest_in = [feed_own, feed_in, other_core(feed_in), rest_near, near_in, other_core(near_in)]
             rest_in += [far_in[0], other_core(far_in[0]), far_in[1], other_core(far_in[1])]
 
-        (w_rest, att_all, middle, hidden, normed_two, grad_pre, part_middle, part_low, own_att, small_two, *att_sends) = (
+        (w_rest, middle, acts, part_middle, own_att, small_two, *att_sends) = (
             call(
                 part(feed_kernel, z),
                 [
                     shape((4, z.part, z.cols), LOW),
-                    shape((rows, nt * inner), LOW),
                     shape((rows, width), F32),
-                    shape((rows, ff), LOW),
-                    shape((rows, width), LOW),
-                    shape((rows, ff), LOW),
+                    shape((5, rows, width), LOW),
                     shape((rows, width), F32),
-                    shape((rows, width), LOW),
                     shape((rows, inner), F32),
                     shape((8, width), F32),
                 ]
@@ -761,39 +751,44 @@
                 name="feed",
             )
         )
-        att_got = [to_tp(att_sends[k - 1], k) for k in range(1, nt)]
-        all_cols = z.all_cols
-        keep, sent = call(
+        att_got = [to_tp(att_sends[k - 1], k) for k in (2, 3, 1)]
+        acts_their = other_core(acts)
+        kept_rows = chunk if z.direct else z.part
+        (keep,) = call(
             part(feed_grad_kernel, z),
-            [shape((4, chunk, 2 * ff), F32), shape((4 * chunk, 2 * ff), LOW)],
-            [normed_two, grad_pre, cot, hidden],
+            [shape((4, kept_rows, 2 * ff), F32)],
+            [acts, acts_their, cot],
             name="feed_grad",
         )
-        keep_proj, sent_proj = call(
+        proj_own, *sends = call(
             part(proj_grad_kernel, z),
-            [shape((4, chunk, nt * inner), F32), shape((4 * chunk, nt * inner), LOW)],
-            [part_low, att_all],
+            [shape((chunk, nt * inner), F32)] + [shape((chunk, nt * inner), LOW)] * 3
+            if z.direct
+            else [shape((4, z.part, nt * inner), F32)],
+            [acts, acts_their],
+            [pltpu.VMEM((4, chunk, nt * inner), F32)] if z.direct else [],
             name="proj_grad",
         )
+        proj_full = proj_own
         out_kept, out_sent = call(
             part(down_kernel, z),
-            [shape((z.padded, width), F32), shape((z.padded, width), LOW)],
-            [hidden, w_rest],
+            [shape((z.half, width), F32), shape((z.half, width), LOW)],
+            [acts, w_rest],
             [pltpu.VMEM((rows, width), F32)],
             name="down",
         )
         out_one = to_tp(out_sent, 1)
         if z.direct:
-            proj_in = other_core(sent_proj)
-            att_got, out_one, keep, sent, proj_in = tie((att_got, out_one, keep, sent, proj_in))
-            proj_own, *sends = call(
-                part(proj_one_kernel, z),
-                [shape((chunk, nt * inner), F32)] + [shape((chunk, nt * inner), LOW)] * 3,
-                [keep_proj, proj_in],
-                name="proj_one",
-            )
+            grad_sent, grad_kept = call(
+                split_kernel,
+                [shape((2, chunk, z.wide), LOW), shape((2, chunk, 2 * ff), F32)],
+                [keep],
+                name="split",
+            )
+            grad_in = to_near(grad_sent)
+            att_got, out_one, grad_kept, proj_own, sends = tie((att_got, out_one, grad_kept, proj_own, sends))
             proj_in = [lax.ppermute(sends[k - 1], "fsdp", [(i, i ^ k) for i in range(nf)]) for k in (3, 1)]
-        (out_low,) = call(add_low_kernel, [shape((z.padded, width), LOW)], [out_kept, out_one], name="out_pair")
+        (out_low,) = call(add_low_kernel, [shape((z.half, width), LOW)], [out_kept, out_one], name="out_pair")
         out_two = to_tp(out_low, 2)
 
         grads, qv_sum, in_kept, in_sent = call(
@@ -801,85 +796,84 @@
             [
                 shape((rows, 3 * inner), LOW),
                 shape((1, 3 * inner), F32),
-                shape((z.padded + 8, width), F32),
-                shape((z.padded + 8, width), LOW),
+                shape((z.padded, width), F32),
+                shape((z.padded, width), LOW),
             ],
             [own_att] + att_got + [act, soft, w_qkv, normal_one, inverse_one, part_middle, small, small_two],
             [pltpu.VMEM((rows, width), F32)],
             name="back",
         )
         in_one = to_tp(in_sent, 1)
-        keep_qkv, sent = call(
+        grads_their = other_core(grads)
+        if z.direct:
+            grads_their, last_send = tie((grads_their, sends[1]))
+            proj_in.append(lax.ppermute(last_send, "fsdp", [(i, i ^ 2) for i in range(nf)]))
+        (keep_qkv,) = call(
             part(qkv_grad_kernel, z),
-            [shape((4, chunk, 3 * inner), F32), shape((4 * chunk, all_cols), LOW)],
-            [sent, normed_one, grads],
+            [shape((4, kept_rows, 3 * inner), F32)],
+            [normed_one, grads, normal_their, grads_their, small],
             name="qkv_grad",
         )
+        extra = z.tail if z.direct else 0
         if z.direct:
-            sent = other_core(sent)
-            sent, last_send = tie((sent, sends[1]))
-            proj_in.append(lax.ppermute(last_send, "fsdp", [(i, i ^ 2) for i in range(nf)]))
-            grad_sent, grad_kept = call(
-                part(split_kernel, z),
-                [shape((2, chunk, z.first), LOW), shape((2, chunk, z.first), F32)],
-                [keep, sent],
-                name="split",
-            )
-            grad_in = to_near(grad_sent)
-            in_one, out_two, proj_in, sent = tie((in_one, out_two, proj_in, sent))
-            rest_sent, rest_kept = call(
-                part(split_rest_kernel, z),
-                [shape((2, chunk, all_cols - z.first), LOW), shape((2, chunk, all_cols - z.first), F32)],
-                [keep, keep_qkv, sent],
-                name="split_rest",
-            )
-            rest_in = to_near(rest_sent)
-        (in_low,) = call(add_low_kernel, [shape((z.padded + 8, width), LOW)], [in_kept, in_one], name="in_pair")
+            in_one, out_two, proj_in, keep_qkv = tie((in_one, out_two, proj_in, keep_qkv))
+            in_low, proj_kept = call(
+                part(in_pair_kernel, z),
+                [shape((z.padded + 2 * extra, width), LOW), shape((2, extra, width), F32)],
+                [in_kept, in_one, proj_own] + proj_in,
+                [pltpu.VMEM((nt, extra, width), F32)],
+                name="in_pair",
+            )
+            qkv_sent, qkv_kept = call(
+                split_kernel,
+                [shape((2, chunk, 3 * inner), LOW), shape((2, chunk, 3 * inner), F32)],
+                [keep_qkv],
+                name="split_qkv",
+            )
+            qkv_in = to_near(qkv_sent)
+        else:
+            (in_low,) = call(add_low_kernel, [shape((z.padded, width), LOW)], [in_kept, in_one], name="in_pair")
         in_two = to_tp(in_low, 2)
-        *proj_kept, out_low = call(
-            part(out_total_kernel, z),
-            ([shape((2, z.tail, width), F32)] if z.direct else [])
-            + [shape((z.padded + (2 * z.tail if z.direct else 0), width), LOW)],
-            [out_low, out_two, middle, small] + ([proj_own] + proj_in if z.direct else []),
-            [pltpu.VMEM((nt, z.tail, width), F32)] if z.direct else [],
-            name="out_total",
+        (out_low,) = call(
+            part(out_total_kernel, z), [shape((z.half, width), LOW)], [out_low, out_two, middle, small], name="out_total"
         )
         out_in = to_tp(out_low, 1)
         if z.direct:
-            in_two, out_in, grad_in, rest_in = tie((in_two, out_in, grad_in, rest_in))
-        in_low, vec = call(
+            grad_own, cross = call(
+                cross_kernel,
+                [shape((chunk, 2 * ff), F32), shape((chunk, 2 * ff), LOW)],
+                [grad_kept, grad_in],
+                name="cross",
+            )
+            cross = to_cross(cross)
+            in_two, out_in, qkv_in = tie((in_two, out_in, qkv_in))
+        in_low, vec, *proj_own = call(
             part(sum_rows_kernel, z),
-            [shape((z.padded, width), LOW), shape((VEC_ROWS, width), F32)],
-            [in_low, in_two, small_two, qv_sum],
+            [shape((z.padded + extra, width), LOW), shape((VEC_ROWS, width), F32)]
+            + ([shape((extra, width), F32)] if extra else []),
+            [in_low, in_two, small_two, qv_sum] + ([proj_kept] if extra else []),
             name="sum_rows",
         )
         in_in = to_tp(in_low, 1)
         proj_all = []
         if z.direct:
-            grad_own, cross = call(
-                part(cross_kernel, z),
-                [shape((chunk, all_cols), F32), shape((chunk, all_cols), LOW)],
-                [grad_kept, rest_kept, grad_in, rest_in],
-                name="cross",
-            )
-            cross = to_cross(cross)
-            proj_own, proj_sent = call(
-                part(proj_pair_kernel, z),
-                [shape((z.tail, width), F32), shape((z.tail, width), LOW)],
-                [proj_kept[0], out_in],
-                name="proj_pair",
-            )
-            proj_two = to_tp(proj_sent, 2)
-            near, far, small_own = call(
+            near, side, far, small_own = call(
                 part(small_kernel, z),
-                [shape((EXTRA, 3 * inner), LOW)] * 2 + [shape((EXTRA, 3 * inner), F32)],
-                [vec, other_core(vec)],
+                [shape((EXTRA, 3 * inner), LOW), shape((EXTRA, 3 * inner), F32)] * 2,
+                [vec],
                 [pltpu.VMEM((4, EXTRA, 3 * inner), F32)],
                 name="small",
             )
+            qkv_own, qkv_sent = call(
+                part(cross_qkv_kernel, z),
+                [shape((chunk, 3 * inner), F32), shape((chunk + EXTRA, 3 * inner), LOW)],
+                [qkv_kept, qkv_in, side],
+                name="cross_qkv",
+            )
+            qkv_in = to_cross(qkv_sent)
             near, far = to_near(near), to_far(far)
-            in_in, proj_two, cross, near, far = tie((in_in, proj_two, cross, near, far))
-            proj_all = [proj_own, proj_two]
+            in_in, cross, qkv_in, near, far = tie((in_in, cross, qkv_in, near, far))
+            proj_all = proj_own
             feed_own, feed_sent, qkv_own, qkv_sent = call(
                 part(last_kernel, z),
                 [
@@ -888,7 +882,7 @@
                     shape((chunk + EXTRA, 3 * inner), F32),
                     shape((chunk + EXTRA, 3 * inner), LOW),
                 ],
-                [grad_own, cross, small_own, near, far],
+                [grad_own, cross, qkv_own, qkv_in, small_own, near, far],
                 name="last",
             )
             feed_in, qkv_in = other_core(feed_sent), other_core(qkv_sent)
@@ -922,18 +916,14 @@
         else:
             output, input_grad = call(part(final_kernel, z), results, [mine, theirs], scratch, name="final")
 
-            def joined(keep, sent):
-                return jnp.stack([keep.astype(LOW), sent.reshape(keep.shape)], 1).reshape(width, -1)
-
-            def scatter(whole):
-                whole = lax.psum(whole, "ctx")
-                return lax.psum_scatter(whole, "fsdp", scatter_dimension=0, tiled=True).astype(F32)
-
-            extra = all_cols - 2 * ff - 3 * inner
-            total = scatter(joined(jnp.concatenate([keep, jnp.pad(keep_qkv, ((0, 0), (0, 0), (0, extra)))], 2), sent))
-            fc1_grad, fc2_grad = total[:, :ff], total[:, ff : 2 * ff]
-            qkv_grad = total[:, 2 * ff : 2 * ff + 3 * inner].reshape(z.shard, 3, inner).transpose(1, 0, 2)
-            proj_grad = scatter(joined(keep_proj, sent_proj)).astype(LOW)
+            def scatter(value):
+                value = value.reshape(width, -1).astype(LOW)
+                return lax.psum_scatter(value, "fsdp", scatter_dimension=0, tiled=True).astype(F32)
+
+            total = scatter(keep)
+            fc1_grad, fc2_grad = total[:, :ff], total[:, ff:]
+            qkv_grad = scatter(keep_qkv).reshape(z.shard, 3, inner).transpose(1, 0, 2)
+            proj_grad = scatter(proj_full).astype(LOW)
             proj_grad = lax.psum_scatter(proj_grad, "tp", scatter_dimension=1, tiled=True).astype(F32).T
 
             def own_columns(value):

time: 95.4 us -> 93.4 us (0.979)
  starting transfers between devices: 38.1 us -> 36.1 us
  waiting for transfers between devices: 37.4 us -> 35.5 us
  Pallas kernels: 15.9 us -> 17.5 us
    ppermute x13 -> x12, waiting for transfers between devices: 25.7 us -> 19.6 us  [to_tp(): return lax.ppermute(value, 'tp', [(i, i ^ k) for i in range(nt)])]
    ppermute x13 -> x12, starting transfers between devices: 16.4 us -> 11.6 us  [to_tp(): return lax.ppermute(value, 'tp', [(i, i ^ k) for i in range(nt)])]
    ppermute x9 -> x10, starting transfers between devices: 10.1 us -> 12.8 us  [neighbours(): return lax.ppermute(value, ('fsdp', 'ctx'), pairs)]
    ppermute x9 -> x10, waiting for transfers between devices: 2.93 us -> 5.62 us  [neighbours(): return lax.ppermute(value, ('fsdp', 'ctx'), pairs)]
    pallas_call x28 -> x27, Pallas kernels: 15.9 us -> 17.5 us  [call(): pl.pallas_call(kernel, out_shape=tuple(outs), in_specs=in_specs or [VMEM]...]
    ppermute x16 -> x15, starting transfers between devices: 3.36 us -> 3.29 us  [other_core(): return lax.ppermute(value, 'ctx', [(0, 1), (1, 0)])]
    ppermute x16 -> x15, waiting for transfers between devices: 4.99 us -> 4.97 us  [other_core(): return lax.ppermute(value, 'ctx', [(0, 1), (1, 0)])]
  transfers between devices with their start and end apart: 44 -> 43, of which waited for: 18 -> 18; matrix products, arithmetic and copies ran while one was open for 0% -> 0% of each run, Pallas kernels for 8% -> 13%
where the time goes in v8:
time: 93.4 us; the launch traced here: 93.1 us
  starting transfers between devices  36.1 us (39%)
  waiting for transfers between devices  35.5 us (38%)
  Pallas kernels  17.5 us (19%)
  local copies, waits for them, and re-layouts  2.9 us (3%)
  between operations  1.1 us (1%)
    ppermute x12, waiting for transfers between devices, to_tp(): return lax.ppermute(value, 'tp', [(i, i ^ k) for i in range(nt)])  19.6 us
    pallas_call x27, Pallas kernels, call(): pl.pallas_call(kernel, out_shape=tuple(outs), in_specs=in_specs or [VMEM]...  17.5 us
    ppermute x10, starting transfers between devices, neighbours(): return lax.ppermute(value, ('fsdp', 'ctx'), pairs)  12.8 us
    ppermute x12, starting transfers between devices, to_tp(): return lax.ppermute(value, 'tp', [(i, i ^ k) for i in range(nt)])  11.6 us
    ppermute x10, waiting for transfers between devices, neighbours(): return lax.ppermute(value, ('fsdp', 'ctx'), pairs)  5.62 us
    ppermute x15, waiting for transfers between devices, other_core(): return lax.ppermute(value, 'ctx', [(0, 1), (1, 0)])  4.97 us
    ppermute x2, waiting for transfers between devices, local(): lax.ppermute(sends[k - 1], 'fsdp', [(i, i ^ k) for i in range(nf)])  3.45 us
    ppermute x15, starting transfers between devices, other_core(): return lax.ppermute(value, 'ctx', [(0, 1), (1, 0)])  3.29 us
  transfers between devices with their start and end apart: 43, of which 18 were waited for; matrix products, arithmetic and copies ran while one was open for 0% of the time, Pallas kernels for 13%

profile of v8, /device:TPU:0, one launch (start us, length us, event | category | flops | bytes accessed | tf_op | source)
XLA Modules:
  0.0 93.1 jit_solution(17356115517019975276)
XLA Ops:
  0.7 0.5 collective-permute-start.2
  1.3 2.0 %pack.1 = (bf16[208,576]{1,0:T(8,128)(2,1)}, bf16[112,576]{1,0:T(8,128)(2,1)}, bf16[296,192]{1,0:T(8,128)(2,1)}, bf16[96,192]{1,0:T(8,128)(2,1)}) custom-call(bf16[3,192,192]{2,1,0:T(8,128)(2,1)} %bitcast.15, bf16[192,192]{1,0:T(8,128)(2,1)} %refs_1_.1, bf16[12,16]{1,0:T(8,128)(2,1)} %refs_2_.1, bf16[3,2,16]{2,1,0:T(2,128)(2,1)} %bitcast.16, ...), custom_call_target="tpu_custom_call" | custom-call | tf_op jit(solution)/shard_map/pack/pallas_call | solution.py:34
  3.3 3.0 %collective-permute-start.4 = (bf16[208,576]{1,0:T(8,128)(2,1)}, bf16[208,576]{1,0:T(8,128)(2,1)S(1)}, u32[]{:S(2)}, u32[]{:S(2)}) collective-permute-start(bf16[208,576]{1,0:T(8,128)(2,1)} %get-tuple-element.136.refs_0_), channel_id=1, source_target_pairs={{0,8},{4,20},{8,0},{12,28},{16,24},{20,4},{24,16},{28,12},{1,9},{5... | collective-permute-start | bytes 718856 | tf_op jit(solution)/shard_map/ppermute | solution.py:623
  6.3 1.5 %collective-permute-start.5 = (bf16[112,576]{1,0:T(8,128)(2,1)}, bf16[112,576]{1,0:T(8,128)(2,1)S(1)}, u32[]{:S(2)}, u32[]{:S(2)}) collective-permute-start(bf16[112,576]{1,0:T(8,128)(2,1)} %get-tuple-element.137), channel_id=1, source_target_pairs={{0,24},{8,16},{16,8},{24,0},{1,25},{9,17},{17,9},{25,1},{2,26},{10... | collective-permute-start | bytes 387080 | tf_op jit(solution)/shard_map/ppermute | solution.py:619
  7.8 1.6 %collective-permute-start.6 = (bf16[296,192]{1,0:T(8,128)(2,1)}, bf16[296,192]{1,0:T(8,128)(2,1)S(1)}, u32[]{:S(2)}, u32[]{:S(2)}) collective-permute-start(bf16[296,192]{1,0:T(8,128)(2,1)} %get-tuple-element.138.proj_t), channel_id=1, source_target_pairs={{0,1},{4,7},{1,0},{5,6},{2,3},{6,5},{3,2},{7,4},{8,9},{12,15},{9,8... | collective-permute-start | bytes 341000 | tf_op jit(solution)/shard_map/ppermute | solution.py:633
  9.3 2.6 %collective-permute-start.7 = (bf16[96,192]{1,0:T(8,128)(2,1)}, bf16[96,192]{1,0:T(8,128)(2,1)S(1)}, u32[]{:S(2)}, u32[]{:S(2)}) collective-permute-start(bf16[96,192]{1,0:T(8,128)(2,1)} %get-tuple-element.139), channel_id=1, source_target_pairs={{0,2},{1,3},{2,0},{3,1},{4,6},{5,7},{6,4},{7,5},{8,10},{9,11},{10,... | collective-permute-start | bytes 110600 | tf_op jit(solution)/shard_map/ppermute | solution.py:616
  11.9 1.0 %copy-done.2 = bf16[192,768]{1,0:T(8,128)(2,1)S(1)} copy-done((bf16[192,768]{1,0:T(8,128)(2,1)S(1)}, bf16[192,768]{1,0:T(8,128)(2,1)}, u32[]{:S(2)}) %copy-start.2) | copy-done | bytes 294936
  12.9 1.0 %copy-done.3 = bf16[768,192]{0,1:T(8,128)(2,1)S(1)} copy-done((bf16[768,192]{0,1:T(8,128)(2,1)S(1)}, bf16[768,192]{0,1:T(8,128)(2,1)}, u32[]{:S(2)}) %copy-start.3) | copy-done | bytes 294936
  14.0 1.6 %collective-permute-start = (bf16[192,1280]{1,0:T(8,128)(2,1)S(1)}, bf16[192,1280]{1,0:T(8,128)(2,1)S(1)}, u32[]{:S(2)}, u32[]{:S(2)}) collective-permute-start(bf16[192,1280]{1,0:T(8,128)(2,1)S(1)} %get-tuple-element.131.refs_0_), channel_id=1, source_target_pairs={{0,8},{4,20},{8,0},{12,28},{16,24},{20,4},{24,16},{28,12},{1,9},{5... | collective-permute-start | bytes 1474568 | tf_op jit(solution)/shard_map/ppermute | solution.py:623
  15.6 1.0 %copy-done.1 = bf16[2,98,768]{2,0,1:T(2,128)(2,1)S(1)} copy-done((bf16[2,98,768]{2,0,1:T(2,128)(2,1)S(1)}, bf16[2,98,768]{2,0,1:T(2,128)(2,1)}, u32[]{:S(2)}) %copy-start.1) | copy-done | bytes 301080
  16.6 0.7 cotangent.1.refs_14_.cot
  17.3 1.0 %frame.1 = (bf16[208,768]{1,0:T(8,128)(2,1)S(1)}, f32[208,768]{1,0:T(8,128)S(1)}, f32[208,128]{1,0:T(8,128)S(1)}, f32[208,768]{1,0:T(8,128)S(1)}) custom-call(bf16[98,2,768]{2,1,0:T(2,128)(2,1)S(1)} %bitcast.11, bf16[98,2,768]{2,1,0:T(2,128)(2,1)S(1)} %collective-permute-done.2.received), custom_call_target="tpu_custom_call" | custom-call | tf_op jit(solution)/shard_map/frame/pallas_call | solution.py:34
  18.4 0.5 collective-permute-start.9
  18.9 0.9 %collective-permute-done.9.far_their = bf16[96,192]{1,0:T(8,128)(2,1)S(1)} collective-permute-done((bf16[96,192]{1,0:T(8,128)(2,1)S(1)}, bf16[96,192]{1,0:T(8,128)(2,1)S(1)}, u32[]{:S(2)}, u32[]{:S(2)}) %collective-permute-start.9) | collective-permute-done | bytes 36896 | tf_op jit(solution)/shard_map/ppermute | solution.py:613
  19.9 0.2 pack_rest.1.refs_3_
  20.1 0.6 collective-permute-start.10
  20.7 0.5 collective-permute-start.13
  21.2 1.2 %collective-permute-done.13.refs_4_ = bf16[112,576]{1,0:T(8,128)(2,1)S(1)} collective-permute-done((bf16[112,576]{1,0:T(8,128)(2,1)S(1)}, bf16[112,576]{1,0:T(8,128)(2,1)S(1)}, u32[]{:S(2)}, u32[]{:S(2)}) %collective-permute-start.13) | collective-permute-done | bytes 129056 | tf_op jit(solution)/shard_map/ppermute | solution.py:613
  22.4 1.3 %attend.1 = (f32[8,768]{1,0:T(8,128)S(1)}, bf16[4,192,576]{2,1,0:T(8,128)(2,1)S(1)}, bf16[208,768]{1,0:T(8,128)(2,1)S(1)}, bf16[3,208,192]{2,1,0:T(8,128)(2,1)S(...) custom-call(bf16[208,576]{1,0:T(8,128)(2,1)S(1)} %copy-done.4, ...), custom_call_target="tpu_custom_call" | custom-call | tf_op jit(solution)/shard_map/attend/pallas_call | solution.py:34
  23.7 0.9 collective-permute-start.14
  24.6 1.1 %collective-permute-start.16 = (bf16[96,1280]{1,0:T(8,128)(2,1)S(1)}, bf16[96,1280]{1,0:T(8,128)(2,1)S(1)}, u32[]{:S(2)}, u32[]{:S(2)}) collective-permute-start(bf16[96,1280]{1,0:T(8,128)(2,1)S(1)} %cut.2), channel_id=1, source_target_pairs={{0,16},{4,12},{8,24},{12,4},{16,0},{20,28},{24,8},{28,20},{1,17},{... | collective-permute-start | bytes 737288 | tf_op jit(solution)/shard_map/ppermute | solution.py:623
  25.8 2.9 %collective-permute-done.10.value.refs_4_ = bf16[192,1024]{1,0:T(8,128)(2,1)S(1)} collective-permute-done((bf16[192,1024]{1,0:T(8,128)(2,1)S(1)}, bf16[192,1024]{1,0:T(8,128)(2,1)S(1)}, u32[]{:S(2)}, u32[]{:S(2)}) %collective-permute-start.10) | collective-permute-done | bytes 393248 | tf_op jit(solution)/shard_map/ppermute | solution.py:623
  28.7 2.0 %collective-permute-done.14.second.refs_11_ = bf16[312,128]{1,0:T(8,128)(2,1)S(1)} collective-permute-done((bf16[312,128]{1,0:T(8,128)(2,1)S(1)}, bf16[312,128]{1,0:T(8,128)(2,1)S(1)}, u32[]{:S(2)}, u32[]{:S(2)}) %collective-permute-start.14) | collective-permute-done | bytes 79904 | tf_op jit(solution)/shard_map/ppermute | solution.py:616
  30.9 6.1 %collective-permute-done.15.refs_12_ = bf16[2,328,128]{2,1,0:T(8,128)(2,1)S(1)} collective-permute-done((bf16[2,328,128]{2,1,0:T(8,128)(2,1)S(1)}, bf16[2,328,128]{2,1,0:T(8,128)(2,1)S(1)}, u32[]{:S(2)}, u32[]{:S(2)}) %collective-permute-start.15) | collective-permute-done | bytes 167968 | tf_op jit(solution)/shard_map/ppermute | solution.py:616
  37.0 0.5 collective-permute-start.19
  37.5 1.3 %collective-permute-done.19.refs_9_ = bf16[96,1024]{1,0:T(8,128)(2,1)S(1)} collective-permute-done((bf16[96,1024]{1,0:T(8,128)(2,1)S(1)}, bf16[96,1024]{1,0:T(8,128)(2,1)S(1)}, u32[]{:S(2)}, u32[]{:S(2)}) %collective-permute-start.19) | collective-permute-done | bytes 196640 | tf_op jit(solution)/shard_map/ppermute | solution.py:613
  38.8 3.1 %feed.1 = (bf16[4,192,2304]{2,1,0:T(8,128)(2,1)S(1)}, f32[208,768]{1,0:T(8,128)S(1)}, bf16[5,208,768]{2,1,0:T(8,128)(2,1)S(1)}, f32[208,768]{1,0:T(8,128)S(1)}, ...) custom-call(bf16[192,1280]{1,0:T(8,128)(2,1)S(1)} %get-tuple-element, ...), custom_call_target="tpu_custom_call" | custom-call | tf_op jit(solution)/shard_map/feed/pallas_call | solution.py:34
  41.9 0.2 collective-permute-start.24
  42.1 0.6 down.1
  42.7 0.4 collective-permute-start.23
  43.1 2.0 %collective-permute-start.20 = (bf16[312,128]{1,0:T(8,128)(2,1)S(1)}, bf16[312,128]{1,0:T(8,128)(2,1)S(1)}, u32[]{:S(2)}, u32[]{:S(2)}) collective-permute-start(bf16[312,128]{1,0:T(8,128)(2,1)S(1)} %get-tuple-element.163), channel_id=1, source_target_pairs={{0,2},{1,3},{2,0},{3,1},{4,6},{5,7},{6,4},{7,5},{8,10},{9,11},{10,... | collective-permute-start | bytes 239624 | tf_op jit(solution)/shard_map/ppermute | solution.py:616
  45.1 2.1 %collective-permute-start.21 = (bf16[312,128]{1,0:T(8,128)(2,1)S(1)}, bf16[312,128]{1,0:T(8,128)(2,1)S(1)}, u32[]{:S(2)}, u32[]{:S(2)}) collective-permute-start(bf16[312,128]{1,0:T(8,128)(2,1)S(1)} %get-tuple-element.164), channel_id=1, source_target_pairs={{0,3},{1,2},{2,1},{3,0},{4,7},{5,6},{6,5},{7,4},{8,11},{9,10},{10,... | collective-permute-start | bytes 239624 | tf_op jit(solution)/shard_map/ppermute | solution.py:616
  47.2 1.5 %feed_grad.1.keep = f32[4,96,1536]{2,1,0:T(8,128)S(1)} custom-call(bf16[5,208,768]{2,1,0:T(8,128)(2,1)S(1)} %get-tuple-element.160.acts, bf16[5,208,768]{2,1,0:T(8,128)(2,1)S(1)} %collective-permute-done.24.theirs, bf16[2,208,768]{2,1,0:T(8,128)(2,1)S(1)} %cotangent.1.refs_14_.cot), custom_call_target="tpu_custom_call" | custom-call | tf_op jit(solution)/shard_map/feed_grad/pallas_call | solution.py:34
  48.9 1.6 %collective-permute-start.35 = (bf16[2,96,1536]{2,1,0:T(8,128)(2,1)S(1)}, bf16[2,96,1536]{2,1,0:T(8,128)(2,1)S(1)}, u32[]{:S(2)}, u32[]{:S(2)}) collective-permute-start(bf16[2,96,1536]{2,1,0:T(8,128)(2,1)S(1)} %get-tuple-element.209), channel_id=1, source_target_pairs={{0,8},{4,20},{8,0},{12,28},{16,24},{20,4},{24,16},{28,12},{1,9},{5... | collective-permute-start | bytes 1769480 | tf_op jit(solution)/shard_map/ppermute | solution.py:623
  50.4 0.9 proj_grad.1
  51.3 1.9 %collective-permute-done.21.refs_2_ = bf16[312,128]{1,0:T(8,128)(2,1)S(1)} collective-permute-done((bf16[312,128]{1,0:T(8,128)(2,1)S(1)}, bf16[312,128]{1,0:T(8,128)(2,1)S(1)}, u32[]{:S(2)}, u32[]{:S(2)}) %collective-permute-start.21) | collective-permute-done | bytes 79904 | tf_op jit(solution)/shard_map/ppermute | solution.py:616
  53.2 1.1 %collective-permute-done.22.refs_3_ = bf16[312,128]{1,0:T(8,128)(2,1)S(1)} collective-permute-done((bf16[312,128]{1,0:T(8,128)(2,1)S(1)}, bf16[312,128]{1,0:T(8,128)(2,1)S(1)}, u32[]{:S(2)}, u32[]{:S(2)}) %collective-permute-start.22) | collective-permute-done | bytes 79904 | tf_op jit(solution)/shard_map/ppermute | solution.py:616
  54.3 2.0 %back.1 = (bf16[208,576]{1,0:T(8,128)(2,1)S(1)}, f32[1,576]{1,0:T(1,128)S(1)}, f32[104,768]{1,0:T(8,128)S(1)}, bf16[104,768]{1,0:T(8,128)(2,1)S(1)}) custom-call(f32[208,192]{1,0:T(8,128)S(1)} %get-tuple-element.173.refs_0_, bf16[312,128]{1,0:T(8,128)(2,1)S(1)} %collective-permute-done.20.refs_1_, bf16[312,128]{1,0:T(8,128)(2,1)S(1)} %collective-permute-done.21.refs_2_, ...), custom_call_target="tpu_custom_call" | custom-call | tf_op jit(solution)/shard_map/back/pallas_call | solution.py:34
  56.4 1.5 %collective-permute-start.27 = (bf16[96,768]{1,0:T(8,128)(2,1)S(1)}, bf16[96,768]{1,0:T(8,128)(2,1)S(1)}, u32[]{:S(2)}, u32[]{:S(2)}) collective-permute-start(bf16[96,768]{1,0:T(8,128)(2,1)S(1)} %get-tuple-element.184), channel_id=1, source_target_pairs={{0,24},{8,16},{16,8},{24,0},{1,25},{9,17},{17,9},{25,1},{2,26},{10... | collective-permute-start | bytes 442376 | tf_op jit(solution)/shard_map/ppermute | solution.py:790
  57.9 0.3 collective-permute-start.25
  58.3 1.9 %collective-permute-start.26 = (bf16[98,768]{1,0:T(8,128)(2,1)S(1)}, bf16[98,768]{1,0:T(8,128)(2,1)S(1)}, u32[]{:S(2)}, u32[]{:S(2)}) collective-permute-start(bf16[98,768]{1,0:T(8,128)(2,1)S(1)} %out_pair.1.own), channel_id=1, source_target_pairs={{0,2},{1,3},{2,0},{3,1},{4,6},{5,7},{6,4},{7,5},{8,10},{9,11},{10,... | collective-permute-start | bytes 451592 | tf_op jit(solution)/shard_map/ppermute | solution.py:616
  60.2 0.8 collective-permute-start.28
  61.0 3.0 %collective-permute-done.27.refs_0_ = bf16[96,768]{1,0:T(8,128)(2,1)S(1)} collective-permute-done((bf16[96,768]{1,0:T(8,128)(2,1)S(1)}, bf16[96,768]{1,0:T(8,128)(2,1)S(1)}, u32[]{:S(2)}, u32[]{:S(2)}) %collective-permute-start.27) | collective-permute-done | bytes 147488 | tf_op jit(solution)/shard_map/ppermute | solution.py:790
  64.0 1.4 %collective-permute-start.30 = (bf16[96,768]{1,0:T(8,128)(2,1)S(1)}, bf16[96,768]{1,0:T(8,128)(2,1)S(1)}, u32[]{:S(2)}, u32[]{:S(2)}) collective-permute-start(bf16[96,768]{1,0:T(8,128)(2,1)S(1)} %get-tuple-element.188), channel_id=1, source_target_pairs={{0,16},{8,24},{16,0},{24,8},{1,17},{9,25},{17,1},{25,9},{2,18},{10... | collective-permute-start | bytes 442376 | tf_op jit(solution)/shard_map/ppermute | solution.py:810
  65.4 0.8 qkv_grad.1.keep
  66.3 0.4 collective-permute-done.28.refs_1_
  66.7 2.0 %collective-permute-done.26.received = bf16[98,768]{1,0:T(8,128)(2,1)S(1)} collective-permute-done((bf16[98,768]{1,0:T(8,128)(2,1)S(1)}, bf16[98,768]{1,0:T(8,128)(2,1)S(1)}, u32[]{:S(2)}, u32[]{:S(2)}) %collective-permute-start.26) | collective-permute-done | bytes 150560 | tf_op jit(solution)/shard_map/ppermute | solution.py:616
  68.6 0.5 collective-permute-done.30.refs_2_
  69.4 0.5 collective-permute-start.31
  69.9 1.7 %collective-permute-start.33 = (bf16[2,96,576]{2,1,0:T(8,128)(2,1)S(1)}, bf16[2,96,576]{2,1,0:T(8,128)(2,1)S(1)}, u32[]{:S(2)}, u32[]{:S(2)}) collective-permute-start(bf16[2,96,576]{2,1,0:T(8,128)(2,1)S(1)} %get-tuple-element.202), channel_id=1, source_target_pairs={{0,8},{4,20},{8,0},{12,28},{16,24},{20,4},{24,16},{28,12},{1,9},{5... | collective-permute-start | bytes 663560 | tf_op jit(solution)/shard_map/ppermute | solution.py:623
  71.7 0.8 collective-permute-start.32
  72.7 1.2 %collective-permute-start.36 = (bf16[96,1536]{1,0:T(8,128)(2,1)S(1)}, bf16[96,1536]{1,0:T(8,128)(2,1)S(1)}, u32[]{:S(2)}, u32[]{:S(2)}) collective-permute-start(bf16[96,1536]{1,0:T(8,128)(2,1)S(1)} %get-tuple-element.210), channel_id=1, source_target_pairs={{0,16},{4,12},{8,24},{12,4},{16,0},{20,28},{24,8},{28,20},{1,17},{... | collective-permute-start | bytes 884744 | tf_op jit(solution)/shard_map/ppermute | solution.py:623
  73.9 3.9 %collective-permute-done.32.out_in = bf16[98,768]{1,0:T(8,128)(2,1)S(1)} collective-permute-done((bf16[98,768]{1,0:T(8,128)(2,1)S(1)}, bf16[98,768]{1,0:T(8,128)(2,1)S(1)}, u32[]{:S(2)}, u32[]{:S(2)}) %collective-permute-start.32) | collective-permute-done | bytes 150560 | tf_op jit(solution)/shard_map/ppermute | solution.py:616
  77.8 1.0 %collective-permute-done.33.received = bf16[2,96,576]{2,1,0:T(8,128)(2,1)S(1)} collective-permute-done((bf16[2,96,576]{2,1,0:T(8,128)(2,1)S(1)}, bf16[2,96,576]{2,1,0:T(8,128)(2,1)S(1)}, u32[]{:S(2)}, u32[]{:S(2)}) %collective-permute-start.33) | collective-permute-done | bytes 221216 | tf_op jit(solution)/shard_map/ppermute | solution.py:623
  78.7 2.6 %collective-permute-done.31.received = bf16[152,768]{1,0:T(8,128)(2,1)S(1)} collective-permute-done((bf16[152,768]{1,0:T(8,128)(2,1)S(1)}, bf16[152,768]{1,0:T(8,128)(2,1)S(1)}, u32[]{:S(2)}, u32[]{:S(2)}) %collective-permute-start.31) | collective-permute-done | bytes 233504 | tf_op jit(solution)/shard_map/ppermute | solution.py:616
  81.7 1.5 %collective-permute-start.37 = (bf16[112,576]{1,0:T(8,128)(2,1)S(1)}, bf16[112,576]{1,0:T(8,128)(2,1)S(1)}, u32[]{:S(2)}, u32[]{:S(2)}) collective-permute-start(bf16[112,576]{1,0:T(8,128)(2,1)S(1)} %get-tuple-element.215), channel_id=1, source_target_pairs={{0,16},{4,12},{8,24},{12,4},{16,0},{20,28},{24,8},{28,20},{1,17},{... | collective-permute-start | bytes 387080 | tf_op jit(solution)/shard_map/ppermute | solution.py:623
  83.3 0.5 collective-permute-start.38
  83.7 1.6 %collective-permute-start.39 = (bf16[16,576]{1,0:T(8,128)(2,1)S(1)}, bf16[16,576]{1,0:T(8,128)(2,1)S(1)}, u32[]{:S(2)}, u32[]{:S(2)}) collective-permute-start(bf16[16,576]{1,0:T(8,128)(2,1)S(1)} %get-tuple-element.217), channel_id=1, source_target_pairs={{0,24},{8,16},{16,8},{24,0},{1,25},{9,17},{17,9},{25,1},{2,26},{10... | collective-permute-start | bytes 55304 | tf_op jit(solution)/shard_map/ppermute | solution.py:619
  85.3 1.8 %collective-permute-done.38.near = bf16[16,576]{1,0:T(8,128)(2,1)S(1)} collective-permute-done((bf16[16,576]{1,0:T(8,128)(2,1)S(1)}, bf16[16,576]{1,0:T(8,128)(2,1)S(1)}, u32[]{:S(2)}, u32[]{:S(2)}) %collective-permute-start.38) | collective-permute-done | bytes 18464 | tf_op jit(solution)/shard_map/ppermute | solution.py:623
  87.0 1.4 %collective-permute-done.39.far = bf16[16,576]{1,0:T(8,128)(2,1)S(1)} collective-permute-done((bf16[16,576]{1,0:T(8,128)(2,1)S(1)}, bf16[16,576]{1,0:T(8,128)(2,1)S(1)}, u32[]{:S(2)}, u32[]{:S(2)}) %collective-permute-start.39) | collective-permute-done | bytes 18464 | tf_op jit(solution)/shard_map/ppermute | solution.py:619
  88.4 0.2 swap.1
  88.8 0.6 collective-permute-start.41
  89.5 1.5 %collective-permute-done.42.refs_4_ = bf16[112,576]{1,0:T(8,128)(2,1)S(1)} collective-permute-done((bf16[112,576]{1,0:T(8,128)(2,1)S(1)}, bf16[112,576]{1,0:T(8,128)(2,1)S(1)}, u32[]{:S(2)}, u32[]{:S(2)}) %collective-permute-start.42) | collective-permute-done | bytes 129056 | tf_op jit(solution)/shard_map/ppermute | solution.py:613
  91.0 2.0 %final.1 = (bf16[98,2,768]{2,1,0:T(2,128)(2,1)}, f32[98,2,768]{2,1,0:T(2,128)}, f32[192,192]{1,0:T(8,128)}, f32[192,768]{1,0:T(8,128)}, f32[192,768]{1,0:T(8,128...) custom-call(f32[2,104,768]{2,1,0:T(8,128)S(1)} %get-tuple-element.22, ...), custom_call_target="tpu_custom_call" | custom-call | tf_op jit(solution)/shard_map/final/pallas_call | solution.py:34
  (61 shorter events, 2.0 us)
Async XLA Ops:
  0.6 16.6 %copy-start = (bf16[2,98,768]{2,0,1:T(2,128)(2,1)S(1)}, bf16[2,98,768]{2,0,1:T(2,128)(2,1)}, u32[]{:S(2)}) copy-start(bf16[2,98,768]{2,0,1:T(2,128)(2,1)} %param.14) | copy-start | bytes 903172
  0.7 2.6 %collective-permute-start.2 = (bf16[98,2,768]{2,1,0:T(2,128)(2,1)}, bf16[98,2,768]{2,1,0:T(2,128)(2,1)S(1)}, u32[]{:S(2)}, u32[]{:S(2)}) collective-permute-start(bf16[98,2,768]{2,1,0:T(2,128)(2,1)} %bitcast.10), channel_id=1, source_target_pairs={{0,4},{4,0},{1,5},{5,1},{2,6},{6,2},{3,7},{7,3},{8,12},{12,8},{9,1... | collective-permute-start | bytes 903176 | tf_op jit(solution)/shard_map/ppermute | solution.py:613
  1.2 2.1 %collective-permute-start.3 = (bf16[98,2,768]{2,1,0:T(2,128)(2,1)}, bf16[98,2,768]{2,1,0:T(2,128)(2,1)S(1)}, u32[]{:S(2)}, u32[]{:S(2)}) collective-permute-start(bf16[98,2,768]{2,1,0:T(2,128)(2,1)} %bitcast.12), channel_id=1, source_target_pairs={{0,4},{4,0},{1,5},{5,1},{2,6},{6,2},{3,7},{7,3},{8,12},{12,8},{9,1... | collective-permute-start | bytes 903176 | tf_op jit(solution)/shard_map/ppermute | solution.py:613
  3.3 15.1 %collective-permute-start.4 = (bf16[208,576]{1,0:T(8,128)(2,1)}, bf16[208,576]{1,0:T(8,128)(2,1)S(1)}, u32[]{:S(2)}, u32[]{:S(2)}) collective-permute-start(bf16[208,576]{1,0:T(8,128)(2,1)} %get-tuple-element.136.refs_0_), channel_id=1, source_target_pairs={{0,8},{4,20},{8,0},{12,28},{16,24},{20,4},{24,16},{28,12},{1,9},{5... | collective-permute-start | bytes 718856 | tf_op jit(solution)/shard_map/ppermute | solution.py:623
  6.3 12.1 %collective-permute-start.5 = (bf16[112,576]{1,0:T(8,128)(2,1)}, bf16[112,576]{1,0:T(8,128)(2,1)S(1)}, u32[]{:S(2)}, u32[]{:S(2)}) collective-permute-start(bf16[112,576]{1,0:T(8,128)(2,1)} %get-tuple-element.137), channel_id=1, source_target_pairs={{0,24},{8,16},{16,8},{24,0},{1,25},{9,17},{17,9},{25,1},{2,26},{10... | collective-permute-start | bytes 387080 | tf_op jit(solution)/shard_map/ppermute | solution.py:619
  7.8 10.6 %collective-permute-start.6 = (bf16[296,192]{1,0:T(8,128)(2,1)}, bf16[296,192]{1,0:T(8,128)(2,1)S(1)}, u32[]{:S(2)}, u32[]{:S(2)}) collective-permute-start(bf16[296,192]{1,0:T(8,128)(2,1)} %get-tuple-element.138.proj_t), channel_id=1, source_target_pairs={{0,1},{4,7},{1,0},{5,6},{2,3},{6,5},{3,2},{7,4},{8,9},{12,15},{9,8... | collective-permute-start | bytes 341000 | tf_op jit(solution)/shard_map/ppermute | solution.py:633
  9.3 9.0 %collective-permute-start.7 = (bf16[96,192]{1,0:T(8,128)(2,1)}, bf16[96,192]{1,0:T(8,128)(2,1)S(1)}, u32[]{:S(2)}, u32[]{:S(2)}) collective-permute-start(bf16[96,192]{1,0:T(8,128)(2,1)} %get-tuple-element.139), channel_id=1, source_target_pairs={{0,2},{1,3},{2,0},{3,1},{4,6},{5,7},{6,4},{7,5},{8,10},{9,11},{10,... | collective-permute-start | bytes 110600 | tf_op jit(solution)/shard_map/ppermute | solution.py:616
  11.9 1.0 %copy-start.2 = (bf16[192,768]{1,0:T(8,128)(2,1)S(1)}, bf16[192,768]{1,0:T(8,128)(2,1)}, u32[]{:S(2)}) copy-start(bf16[192,768]{1,0:T(8,128)(2,1)} %up.1) | copy-start | bytes 884740
  12.9 1.0 %copy-start.3 = (bf16[768,192]{0,1:T(8,128)(2,1)S(1)}, bf16[768,192]{0,1:T(8,128)(2,1)}, u32[]{:S(2)}) copy-start(bf16[768,192]{0,1:T(8,128)(2,1)} %param.25) | copy-start | bytes 884740
  13.9 6.0 %copy-start.5 = (bf16[296,192]{1,0:T(8,128)(2,1)S(1)}, bf16[296,192]{1,0:T(8,128)(2,1)}, u32[]{:S(2)}) copy-start(bf16[296,192]{1,0:T(8,128)(2,1)} %get-tuple-element.138.proj_t) | copy-start | bytes 340996
  13.9 8.6 %copy-start.4 = (bf16[208,576]{1,0:T(8,128)(2,1)S(1)}, bf16[208,576]{1,0:T(8,128)(2,1)}, u32[]{:S(2)}) copy-start(bf16[208,576]{1,0:T(8,128)(2,1)} %get-tuple-element.136.refs_0_) | copy-start | bytes 718852
  14.0 10.5 %collective-permute-start = (bf16[192,1280]{1,0:T(8,128)(2,1)S(1)}, bf16[192,1280]{1,0:T(8,128)(2,1)S(1)}, u32[]{:S(2)}, u32[]{:S(2)}) collective-permute-start(bf16[192,1280]{1,0:T(8,128)(2,1)S(1)} %get-tuple-element.131.refs_0_), channel_id=1, source_target_pairs={{0,8},{4,20},{8,0},{12,28},{16,24},{20,4},{24,16},{28,12},{1,9},{5... | collective-permute-start | bytes 1474568 | tf_op jit(solution)/shard_map/ppermute | solution.py:623
  15.6 1.0 %copy-start.1 = (bf16[2,98,768]{2,0,1:T(2,128)(2,1)S(1)}, bf16[2,98,768]{2,0,1:T(2,128)(2,1)}, u32[]{:S(2)}) copy-start(bf16[2,98,768]{2,0,1:T(2,128)(2,1)} %param.27) | copy-start | bytes 903172
  18.4 1.5 %collective-permute-start.8 = (bf16[296,192]{1,0:T(8,128)(2,1)S(1)}, bf16[296,192]{1,0:T(8,128)(2,1)S(1)}, u32[]{:S(2)}, u32[]{:S(2)}) collective-permute-start(bf16[296,192]{1,0:T(8,128)(2,1)S(1)} %collective-permute-done.6.near_in), channel_id=1, source_target_pairs={{0,4},{4,0},{1,5},{5,1},{2,6},{6,2},{3,7},{7,3},{8,12},{12,8},{9,1... | collective-permute-start | bytes 341000 | tf_op jit(solution)/shard_map/ppermute | solution.py:613
  18.4 1.4 %collective-permute-start.9 = (bf16[96,192]{1,0:T(8,128)(2,1)S(1)}, bf16[96,192]{1,0:T(8,128)(2,1)S(1)}, u32[]{:S(2)}, u32[]{:S(2)}) collective-permute-start(bf16[96,192]{1,0:T(8,128)(2,1)S(1)} %collective-permute-done.7.far_in), channel_id=1, source_target_pairs={{0,4},{4,0},{1,5},{5,1},{2,6},{6,2},{3,7},{7,3},{8,12},{12,8},{9,1... | collective-permute-start | bytes 110600 | tf_op jit(solution)/shard_map/ppermute | solution.py:613
  20.1 8.5 %collective-permute-start.10 = (bf16[192,1024]{1,0:T(8,128)(2,1)S(1)}, bf16[192,1024]{1,0:T(8,128)(2,1)S(1)}, u32[]{:S(2)}, u32[]{:S(2)}) collective-permute-start(bf16[192,1024]{1,0:T(8,128)(2,1)S(1)} %pack_rest.1.refs_3_), channel_id=1, source_target_pairs={{0,8},{4,20},{8,0},{12,28},{16,24},{20,4},{24,16},{28,12},{1,9},{5... | collective-permute-start | bytes 1179656 | tf_op jit(solution)/shard_map/ppermute | solution.py:623
  20.7 1.8 %collective-permute-start.12 = (bf16[208,576]{1,0:T(8,128)(2,1)S(1)}, bf16[208,576]{1,0:T(8,128)(2,1)S(1)}, u32[]{:S(2)}, u32[]{:S(2)}) collective-permute-start(bf16[208,576]{1,0:T(8,128)(2,1)S(1)} %collective-permute-done.4.refs_1_), channel_id=1, source_target_pairs={{0,4},{4,0},{1,5},{5,1},{2,6},{6,2},{3,7},{7,3},{8,12},{12,8},{9,1... | collective-permute-start | bytes 718856 | tf_op jit(solution)/shard_map/ppermute | solution.py:613
  20.7 1.7 %collective-permute-start.13 = (bf16[112,576]{1,0:T(8,128)(2,1)S(1)}, bf16[112,576]{1,0:T(8,128)(2,1)S(1)}, u32[]{:S(2)}, u32[]{:S(2)}) collective-permute-start(bf16[112,576]{1,0:T(8,128)(2,1)S(1)} %collective-permute-done.5.refs_3_), channel_id=1, source_target_pairs={{0,4},{4,0},{1,5},{5,1},{2,6},{6,2},{3,7},{7,3},{8,12},{12,8},{9,1... | collective-permute-start | bytes 387080 | tf_op jit(solution)/shard_map/ppermute | solution.py:613
  23.7 7.0 %collective-permute-start.14 = (bf16[312,128]{1,0:T(8,128)(2,1)S(1)}, bf16[312,128]{1,0:T(8,128)(2,1)S(1)}, u32[]{:S(2)}, u32[]{:S(2)}) collective-permute-start(bf16[312,128]{1,0:T(8,128)(2,1)S(1)} %get-tuple-element.153.first.refs_10_), channel_id=1, source_target_pairs={{0,2},{1,3},{2,0},{3,1},{4,6},{5,7},{6,4},{7,5},{8,10},{9,11},{10,... | collective-permute-start | bytes 239624 | tf_op jit(solution)/shard_map/ppermute | solution.py:616
  24.6 6.3 %collective-permute-start.16 = (bf16[96,1280]{1,0:T(8,128)(2,1)S(1)}, bf16[96,1280]{1,0:T(8,128)(2,1)S(1)}, u32[]{:S(2)}, u32[]{:S(2)}) collective-permute-start(bf16[96,1280]{1,0:T(8,128)(2,1)S(1)} %cut.2), channel_id=1, source_target_pairs={{0,16},{4,12},{8,24},{12,4},{16,0},{20,28},{24,8},{28,20},{1,17},{... | collective-permute-start | bytes 737288 | tf_op jit(solution)/shard_map/ppermute | solution.py:623
  25.7 11.8 %collective-permute-start.1 = (bf16[192,1280]{1,0:T(8,128)(2,1)S(1)}, bf16[192,1280]{1,0:T(8,128)(2,1)S(1)}, u32[]{:S(2)}, u32[]{:S(2)}) collective-permute-start(bf16[192,1280]{1,0:T(8,128)(2,1)S(1)} %collective-permute-done.value.refs_1_), channel_id=1, source_target_pairs={{0,4},{4,0},{1,5},{5,1},{2,6},{6,2},{3,7},{7,3},{8,12},{12,8},{9,1... | collective-permute-start | bytes 1474568 | tf_op jit(solution)/shard_map/ppermute | solution.py:613
  28.6 8.4 %collective-permute-start.17 = (bf16[96,1024]{1,0:T(8,128)(2,1)S(1)}, bf16[96,1024]{1,0:T(8,128)(2,1)S(1)}, u32[]{:S(2)}, u32[]{:S(2)}) collective-permute-start(bf16[96,1024]{1,0:T(8,128)(2,1)S(1)} %cut.3), channel_id=1, source_target_pairs={{0,16},{4,12},{8,24},{12,4},{16,0},{20,28},{24,8},{28,20},{1,17},{... | collective-permute-start | bytes 589832 | tf_op jit(solution)/shard_map/ppermute | solution.py:623
  30.7 6.3 %collective-permute-start.15 = (bf16[2,328,128]{2,1,0:T(8,128)(2,1)S(1)}, bf16[2,328,128]{2,1,0:T(8,128)(2,1)S(1)}, u32[]{:S(2)}, u32[]{:S(2)}) collective-permute-start(bf16[2,328,128]{2,1,0:T(8,128)(2,1)S(1)} %pair.1), channel_id=1, source_target_pairs={{0,1},{1,0},{2,3},{3,2},{4,5},{5,4},{6,7},{7,6},{8,9},{9,8},{10,11... | collective-permute-start | bytes 503816 | tf_op jit(solution)/shard_map/ppermute | solution.py:616
  30.8 6.7 %collective-permute-start.11 = (bf16[192,1024]{1,0:T(8,128)(2,1)S(1)}, bf16[192,1024]{1,0:T(8,128)(2,1)S(1)}, u32[]{:S(2)}, u32[]{:S(2)}) collective-permute-start(bf16[192,1024]{1,0:T(8,128)(2,1)S(1)} %collective-permute-done.10.value.refs_4_), channel_id=1, source_target_pairs={{0,4},{4,0},{1,5},{5,1},{2,6},{6,2},{3,7},{7,3},{8,12},{12,8},{9,1... | collective-permute-start | bytes 1179656 | tf_op jit(solution)/shard_map/ppermute | solution.py:613
  37.0 1.8 %collective-permute-start.18 = (bf16[96,1280]{1,0:T(8,128)(2,1)S(1)}, bf16[96,1280]{1,0:T(8,128)(2,1)S(1)}, u32[]{:S(2)}, u32[]{:S(2)}) collective-permute-start(bf16[96,1280]{1,0:T(8,128)(2,1)S(1)} %collective-permute-done.16.refs_6_), channel_id=1, source_target_pairs={{0,4},{4,0},{1,5},{5,1},{2,6},{6,2},{3,7},{7,3},{8,12},{12,8},{9,1... | collective-permute-start | bytes 737288 | tf_op jit(solution)/shard_map/ppermute | solution.py:613
  37.0 1.8 %collective-permute-start.19 = (bf16[96,1024]{1,0:T(8,128)(2,1)S(1)}, bf16[96,1024]{1,0:T(8,128)(2,1)S(1)}, u32[]{:S(2)}, u32[]{:S(2)}) collective-permute-start(bf16[96,1024]{1,0:T(8,128)(2,1)S(1)} %collective-permute-done.17.refs_8_), channel_id=1, source_target_pairs={{0,4},{4,0},{1,5},{5,1},{2,6},{6,2},{3,7},{7,3},{8,12},{12,8},{9,1... | collective-permute-start | bytes 589832 | tf_op jit(solution)/shard_map/ppermute | solution.py:613
  41.9 5.3 %collective-permute-start.24 = (bf16[5,208,768]{2,1,0:T(8,128)(2,1)S(1)}, bf16[5,208,768]{2,1,0:T(8,128)(2,1)S(1)}, u32[]{:S(2)}, u32[]{:S(2)}) collective-permute-start(bf16[5,208,768]{2,1,0:T(8,128)(2,1)S(1)} %get-tuple-element.160.acts), channel_id=1, source_target_pairs={{0,4},{4,0},{1,5},{5,1},{2,6},{6,2},{3,7},{7,3},{8,12},{12,8},{9,1... | collective-permute-start | bytes 4792328 | tf_op jit(solution)/shard_map/ppermute | solution.py:613
  42.7 11.6 %collective-permute-start.23 = (bf16[98,768]{1,0:T(8,128)(2,1)S(1)}, bf16[98,768]{1,0:T(8,128)(2,1)S(1)}, u32[]{:S(2)}, u32[]{:S(2)}) collective-permute-start(bf16[98,768]{1,0:T(8,128)(2,1)S(1)} %get-tuple-element.166), channel_id=1, source_target_pairs={{0,1},{1,0},{2,3},{3,2},{4,5},{5,4},{6,7},{7,6},{8,9},{9,8},{10,11... | collective-permute-start | bytes 451592 | tf_op jit(solution)/shard_map/ppermute | solution.py:616
  43.1 8.2 %collective-permute-start.20 = (bf16[312,128]{1,0:T(8,128)(2,1)S(1)}, bf16[312,128]{1,0:T(8,128)(2,1)S(1)}, u32[]{:S(2)}, u32[]{:S(2)}) collective-permute-start(bf16[312,128]{1,0:T(8,128)(2,1)S(1)} %get-tuple-element.163), channel_id=1, source_target_pairs={{0,2},{1,3},{2,0},{3,1},{4,6},{5,7},{6,4},{7,5},{8,10},{9,11},{10,... | collective-permute-start | bytes 239624 | tf_op jit(solution)/shard_map/ppermute | solution.py:616
  45.1 8.1 %collective-permute-start.21 = (bf16[312,128]{1,0:T(8,128)(2,1)S(1)}, bf16[312,128]{1,0:T(8,128)(2,1)S(1)}, u32[]{:S(2)}, u32[]{:S(2)}) collective-permute-start(bf16[312,128]{1,0:T(8,128)(2,1)S(1)} %get-tuple-element.164), channel_id=1, source_target_pairs={{0,3},{1,2},{2,1},{3,0},{4,7},{5,6},{6,5},{7,4},{8,11},{9,10},{10,... | collective-permute-start | bytes 239624 | tf_op jit(solution)/shard_map/ppermute | solution.py:616
  47.2 7.1 %collective-permute-start.22 = (bf16[312,128]{1,0:T(8,128)(2,1)S(1)}, bf16[312,128]{1,0:T(8,128)(2,1)S(1)}, u32[]{:S(2)}, u32[]{:S(2)}) collective-permute-start(bf16[312,128]{1,0:T(8,128)(2,1)S(1)} %get-tuple-element.165), channel_id=1, source_target_pairs={{0,1},{1,0},{2,3},{3,2},{4,5},{5,4},{6,7},{7,6},{8,9},{9,8},{10,11... | collective-permute-start | bytes 239624 | tf_op jit(solution)/shard_map/ppermute | solution.py:616
  48.9 23.7 %collective-permute-start.35 = (bf16[2,96,1536]{2,1,0:T(8,128)(2,1)S(1)}, bf16[2,96,1536]{2,1,0:T(8,128)(2,1)S(1)}, u32[]{:S(2)}, u32[]{:S(2)}) collective-permute-start(bf16[2,96,1536]{2,1,0:T(8,128)(2,1)S(1)} %get-tuple-element.209), channel_id=1, source_target_pairs={{0,8},{4,20},{8,0},{12,28},{16,24},{20,4},{24,16},{28,12},{1,9},{5... | collective-permute-start | bytes 1769480 | tf_op jit(solution)/shard_map/ppermute | solution.py:623
  56.4 3.9 %collective-permute-start.29 = (bf16[208,576]{1,0:T(8,128)(2,1)S(1)}, bf16[208,576]{1,0:T(8,128)(2,1)S(1)}, u32[]{:S(2)}, u32[]{:S(2)}) collective-permute-start(bf16[208,576]{1,0:T(8,128)(2,1)S(1)} %get-tuple-element.186.grads), channel_id=1, source_target_pairs={{0,4},{4,0},{1,5},{5,1},{2,6},{6,2},{3,7},{7,3},{8,12},{12,8},{9,1... | collective-permute-start | bytes 718856 | tf_op jit(solution)/shard_map/ppermute | solution.py:613
  56.4 7.6 %collective-permute-start.27 = (bf16[96,768]{1,0:T(8,128)(2,1)S(1)}, bf16[96,768]{1,0:T(8,128)(2,1)S(1)}, u32[]{:S(2)}, u32[]{:S(2)}) collective-permute-start(bf16[96,768]{1,0:T(8,128)(2,1)S(1)} %get-tuple-element.184), channel_id=1, source_target_pairs={{0,24},{8,16},{16,8},{24,0},{1,25},{9,17},{17,9},{25,1},{2,26},{10... | collective-permute-start | bytes 442376 | tf_op jit(solution)/shard_map/ppermute | solution.py:790
  57.9 10.7 %collective-permute-start.25 = (bf16[104,768]{1,0:T(8,128)(2,1)S(1)}, bf16[104,768]{1,0:T(8,128)(2,1)S(1)}, u32[]{:S(2)}, u32[]{:S(2)}) collective-permute-start(bf16[104,768]{1,0:T(8,128)(2,1)S(1)} %get-tuple-element.183), channel_id=1, source_target_pairs={{0,1},{1,0},{2,3},{3,2},{4,5},{5,4},{6,7},{7,6},{8,9},{9,8},{10,11... | collective-permute-start | bytes 479240 | tf_op jit(solution)/shard_map/ppermute | solution.py:616
  58.3 10.3 %collective-permute-start.26 = (bf16[98,768]{1,0:T(8,128)(2,1)S(1)}, bf16[98,768]{1,0:T(8,128)(2,1)S(1)}, u32[]{:S(2)}, u32[]{:S(2)}) collective-permute-start(bf16[98,768]{1,0:T(8,128)(2,1)S(1)} %out_pair.1.own), channel_id=1, source_target_pairs={{0,2},{1,3},{2,0},{3,1},{4,6},{5,7},{6,4},{7,5},{8,10},{9,11},{10,... | collective-permute-start | bytes 451592 | tf_op jit(solution)/shard_map/ppermute | solution.py:616
  60.2 6.5 %collective-permute-start.28 = (bf16[96,768]{1,0:T(8,128)(2,1)S(1)}, bf16[96,768]{1,0:T(8,128)(2,1)S(1)}, u32[]{:S(2)}, u32[]{:S(2)}) collective-permute-start(bf16[96,768]{1,0:T(8,128)(2,1)S(1)} %get-tuple-element.185), channel_id=1, source_target_pairs={{0,8},{8,0},{16,24},{24,16},{1,9},{9,1},{17,25},{25,17},{2,10},{10... | collective-permute-start | bytes 442376 | tf_op jit(solution)/shard_map/ppermute | solution.py:790
  64.0 5.1 %collective-permute-start.30 = (bf16[96,768]{1,0:T(8,128)(2,1)S(1)}, bf16[96,768]{1,0:T(8,128)(2,1)S(1)}, u32[]{:S(2)}, u32[]{:S(2)}) collective-permute-start(bf16[96,768]{1,0:T(8,128)(2,1)S(1)} %get-tuple-element.188), channel_id=1, source_target_pairs={{0,16},{8,24},{16,0},{24,8},{1,17},{9,25},{17,1},{25,9},{2,18},{10... | collective-permute-start | bytes 442376 | tf_op jit(solution)/shard_map/ppermute | solution.py:810
  69.4 12.0 %collective-permute-start.31 = (bf16[152,768]{1,0:T(8,128)(2,1)S(1)}, bf16[152,768]{1,0:T(8,128)(2,1)S(1)}, u32[]{:S(2)}, u32[]{:S(2)}) collective-permute-start(bf16[152,768]{1,0:T(8,128)(2,1)S(1)} %get-tuple-element.200.own), channel_id=1, source_target_pairs={{0,2},{1,3},{2,0},{3,1},{4,6},{5,7},{6,4},{7,5},{8,10},{9,11},{10,... | collective-permute-start | bytes 700424 | tf_op jit(solution)/shard_map/ppermute | solution.py:616
  69.9 8.8 %collective-permute-start.33 = (bf16[2,96,576]{2,1,0:T(8,128)(2,1)S(1)}, bf16[2,96,576]{2,1,0:T(8,128)(2,1)S(1)}, u32[]{:S(2)}, u32[]{:S(2)}) collective-permute-start(bf16[2,96,576]{2,1,0:T(8,128)(2,1)S(1)} %get-tuple-element.202), channel_id=1, source_target_pairs={{0,8},{4,20},{8,0},{12,28},{16,24},{20,4},{24,16},{28,12},{1,9},{5... | collective-permute-start | bytes 663560 | tf_op jit(solution)/shard_map/ppermute | solution.py:623
  71.7 6.0 %collective-permute-start.32 = (bf16[98,768]{1,0:T(8,128)(2,1)S(1)}, bf16[98,768]{1,0:T(8,128)(2,1)S(1)}, u32[]{:S(2)}, u32[]{:S(2)}) collective-permute-start(bf16[98,768]{1,0:T(8,128)(2,1)S(1)} %out_total.1.out_own), channel_id=1, source_target_pairs={{0,1},{1,0},{2,3},{3,2},{4,5},{5,4},{6,7},{7,6},{8,9},{9,8},{10,11... | collective-permute-start | bytes 451592 | tf_op jit(solution)/shard_map/ppermute | solution.py:616
  72.7 15.7 %collective-permute-start.36 = (bf16[96,1536]{1,0:T(8,128)(2,1)S(1)}, bf16[96,1536]{1,0:T(8,128)(2,1)S(1)}, u32[]{:S(2)}, u32[]{:S(2)}) collective-permute-start(bf16[96,1536]{1,0:T(8,128)(2,1)S(1)} %get-tuple-element.210), channel_id=1, source_target_pairs={{0,16},{4,12},{8,24},{12,4},{16,0},{20,28},{24,8},{28,20},{1,17},{... | collective-permute-start | bytes 884744 | tf_op jit(solution)/shard_map/ppermute | solution.py:623
  81.4 7.0 %collective-permute-start.34 = (bf16[128,768]{1,0:T(8,128)(2,1)S(1)}, bf16[128,768]{1,0:T(8,128)(2,1)S(1)}, u32[]{:S(2)}, u32[]{:S(2)}) collective-permute-start(bf16[128,768]{1,0:T(8,128)(2,1)S(1)} %get-tuple-element.207.in_own), channel_id=1, source_target_pairs={{0,1},{1,0},{2,3},{3,2},{4,5},{5,4},{6,7},{7,6},{8,9},{9,8},{10,11... | collective-permute-start | bytes 589832 | tf_op jit(solution)/shard_map/ppermute | solution.py:616
  81.7 6.7 %collective-permute-start.37 = (bf16[112,576]{1,0:T(8,128)(2,1)S(1)}, bf16[112,576]{1,0:T(8,128)(2,1)S(1)}, u32[]{:S(2)}, u32[]{:S(2)}) collective-permute-start(bf16[112,576]{1,0:T(8,128)(2,1)S(1)} %get-tuple-element.215), channel_id=1, source_target_pairs={{0,16},{4,12},{8,24},{12,4},{16,0},{20,28},{24,8},{28,20},{1,17},{... | collective-permute-start | bytes 387080 | tf_op jit(solution)/shard_map/ppermute | solution.py:623
  83.3 3.8 %collective-permute-start.38 = (bf16[16,576]{1,0:T(8,128)(2,1)S(1)}, bf16[16,576]{1,0:T(8,128)(2,1)S(1)}, u32[]{:S(2)}, u32[]{:S(2)}) collective-permute-start(bf16[16,576]{1,0:T(8,128)(2,1)S(1)} %get-tuple-element.216), channel_id=1, source_target_pairs={{0,8},{4,20},{8,0},{12,28},{16,24},{20,4},{24,16},{28,12},{1,9},{5... | collective-permute-start | bytes 55304 | tf_op jit(solution)/shard_map/ppermute | solution.py:623
  83.7 4.7 %collective-permute-start.39 = (bf16[16,576]{1,0:T(8,128)(2,1)S(1)}, bf16[16,576]{1,0:T(8,128)(2,1)S(1)}, u32[]{:S(2)}, u32[]{:S(2)}) collective-permute-start(bf16[16,576]{1,0:T(8,128)(2,1)S(1)} %get-tuple-element.217), channel_id=1, source_target_pairs={{0,24},{8,16},{16,8},{24,0},{1,25},{9,17},{17,9},{25,1},{2,26},{10... | collective-permute-start | bytes 55304 | tf_op jit(solution)/shard_map/ppermute | solution.py:619
  88.6 2.4 %collective-permute-start.40 = (bf16[232,768]{1,0:T(8,128)(2,1)S(1)}, bf16[232,768]{1,0:T(8,128)(2,1)S(1)}, u32[]{:S(2)}, u32[]{:S(2)}) collective-permute-start(bf16[232,768]{1,0:T(8,128)(2,1)S(1)} %get-tuple-element.221), channel_id=1, source_target_pairs={{0,4},{4,0},{1,5},{5,1},{2,6},{6,2},{3,7},{7,3},{8,12},{12,8},{9,1... | collective-permute-start | bytes 1069064 | tf_op jit(solution)/shard_map/ppermute | solution.py:613
  88.8 2.1 %collective-permute-start.41 = (bf16[96,1536]{1,0:T(8,128)(2,1)S(1)}, bf16[96,1536]{1,0:T(8,128)(2,1)S(1)}, u32[]{:S(2)}, u32[]{:S(2)}) collective-permute-start(bf16[96,1536]{1,0:T(8,128)(2,1)S(1)} %get-tuple-element.231), channel_id=1, source_target_pairs={{0,4},{4,0},{1,5},{5,1},{2,6},{6,2},{3,7},{7,3},{8,12},{12,8},{9,1... | collective-permute-start | bytes 884744 | tf_op jit(solution)/shard_map/ppermute | solution.py:613
  89.4 1.6 %collective-permute-start.42 = (bf16[112,576]{1,0:T(8,128)(2,1)S(1)}, bf16[112,576]{1,0:T(8,128)(2,1)S(1)}, u32[]{:S(2)}, u32[]{:S(2)}) collective-permute-start(bf16[112,576]{1,0:T(8,128)(2,1)S(1)} %get-tuple-element.233), channel_id=1, source_target_pairs={{0,4},{4,0},{1,5},{5,1},{2,6},{6,2},{3,7},{7,3},{8,12},{12,8},{9,1... | collective-permute-start | bytes 387080 | tf_op jit(solution)/shard_map/ppermute | solution.py:613

commit v9 on v8

--- a/solution.py
+++ b/solution.py
@@ -297,9 +297,9 @@
     grad_out_low = cot[0]
     grad_out = grad_out_low.astype(F32)
     heads[t] = z.spread(read(att[0]))
-    heads[t ^ 2] = z.spread(read(att[1]))
+    heads[t ^ 3] = z.spread(read(att[1]))
     heads[t ^ 1] = z.spread(att[2][0, : z.dense, :].astype(F32))
-    heads[t ^ 3] = z.spread(att[2][1, : z.dense, :].astype(F32))
+    heads[t ^ 2] = z.spread(att[2][1, : z.dense, :].astype(F32))
     attended = lanes([heads[i] for i in range(z.nt)]).astype(LOW)
     acts[4] = attended
     branch = dot(attended, w_proj_t, NT)
@@ -726,7 +726,7 @@
             [pltpu.VMEM((4, EXTRA, 3 * inner), F32)] if z.direct else [],
             name="attend",
         )
-        att_one = to_tp(attended, 2)
+        att_one = to_tp(attended, 3)
         (att_two,) = call(pair_kernel, [shape((2, z.dense + 16, 128), LOW)], [attended, att_one], name="pair")
         att_two = to_tp(att_two, 1)
         if z.direct:
@@ -751,7 +751,7 @@
                 name="feed",
             )
         )
-        att_got = [to_tp(att_sends[k - 1], k) for k in (2, 3, 1)]
+        att_got = [to_tp(att_sends[k - 1], k) for k in (3, 2, 1)]
         acts_their = other_core(acts)
         kept_rows = chunk if z.direct else z.part
         (keep,) = call(
@@ -871,7 +871,8 @@
                 name="cross_qkv",
             )
             qkv_in = to_cross(qkv_sent)
-            near, far = to_near(near), to_far(far)
+            far = to_far(far)
+            near = to_near(near)
             in_in, cross, qkv_in, near, far = tie((in_in, cross, qkv_in, near, far))
             proj_all = proj_own
             feed_own, feed_sent, qkv_own, qkv_sent = call(

time: 93.4 us -> 92 us (0.985)
  waiting for transfers between devices: 35.5 us -> 32.2 us
  starting transfers between devices: 36.1 us -> 38 us
    ppermute x12, waiting for transfers between devices: 19.6 us -> 16.7 us  [to_tp(): return lax.ppermute(value, 'tp', [(i, i ^ k) for i in range(nt)])]
    ppermute x12, starting transfers between devices: 11.6 us -> 13 us  [to_tp(): return lax.ppermute(value, 'tp', [(i, i ^ k) for i in range(nt)])]
  transfers between devices with their start and end apart: 43 -> 43, of which waited for: 18 -> 19; matrix products, arithmetic and copies ran while one was open for 0% -> 0% of each run, Pallas kernels for 13% -> 13%
where the time goes in v9:
time: 92 us; the launch traced here: 91.7 us
  starting transfers between devices  38 us (41%)
  waiting for transfers between devices  32.2 us (35%)
  Pallas kernels  17.5 us (19%)
  local copies, waits for them, and re-layouts  2.9 us (3%)
  between operations  1.1 us (1%)
    pallas_call x27, Pallas kernels, call(): pl.pallas_call(kernel, out_shape=tuple(outs), in_specs=in_specs or [VMEM]...  17.5 us
    ppermute x12, waiting for transfers between devices, to_tp(): return lax.ppermute(value, 'tp', [(i, i ^ k) for i in range(nt)])  16.7 us
    ppermute x12, starting transfers between devices, to_tp(): return lax.ppermute(value, 'tp', [(i, i ^ k) for i in range(nt)])  13 us
    ppermute x10, starting transfers between devices, neighbours(): return lax.ppermute(value, ('fsdp', 'ctx'), pairs)  13 us
    ppermute x10, waiting for transfers between devices, neighbours(): return lax.ppermute(value, ('fsdp', 'ctx'), pairs)  5.3 us
    ppermute x15, waiting for transfers between devices, other_core(): return lax.ppermute(value, 'ctx', [(0, 1), (1, 0)])  4.97 us
    ppermute x15, starting transfers between devices, other_core(): return lax.ppermute(value, 'ctx', [(0, 1), (1, 0)])  3.26 us
    ppermute x2, waiting for transfers between devices, local(): lax.ppermute(sends[k - 1], 'fsdp', [(i, i ^ k) for i in range(nf)])  3.07 us
  transfers between devices with their start and end apart: 43, of which 19 were waited for; matrix products, arithmetic and copies ran while one was open for 0% of the time, Pallas kernels for 13%

profile of v9, /device:TPU:0, one launch (start us, length us, event | category | flops | bytes accessed | tf_op | source)
XLA Modules:
  0.0 91.7 jit_solution(4957300479293149220)
XLA Ops:
  0.7 0.5 collective-permute-start.2
  1.3 2.0 %pack.1 = (bf16[208,576]{1,0:T(8,128)(2,1)}, bf16[112,576]{1,0:T(8,128)(2,1)}, bf16[296,192]{1,0:T(8,128)(2,1)}, bf16[96,192]{1,0:T(8,128)(2,1)}) custom-call(bf16[3,192,192]{2,1,0:T(8,128)(2,1)} %bitcast.15, bf16[192,192]{1,0:T(8,128)(2,1)} %refs_1_.1, bf16[12,16]{1,0:T(8,128)(2,1)} %refs_2_.1, bf16[3,2,16]{2,1,0:T(2,128)(2,1)} %bitcast.16, ...), custom_call_target="tpu_custom_call" | custom-call | tf_op jit(solution)/shard_map/pack/pallas_call | solution.py:34
  3.3 3.0 %collective-permute-start.4 = (bf16[208,576]{1,0:T(8,128)(2,1)}, bf16[208,576]{1,0:T(8,128)(2,1)S(1)}, u32[]{:S(2)}, u32[]{:S(2)}) collective-permute-start(bf16[208,576]{1,0:T(8,128)(2,1)} %get-tuple-element.136.refs_0_), channel_id=1, source_target_pairs={{0,8},{4,20},{8,0},{12,28},{16,24},{20,4},{24,16},{28,12},{1,9},{5... | collective-permute-start | bytes 718856 | tf_op jit(solution)/shard_map/ppermute | solution.py:623
  6.3 1.5 %collective-permute-start.5 = (bf16[112,576]{1,0:T(8,128)(2,1)}, bf16[112,576]{1,0:T(8,128)(2,1)S(1)}, u32[]{:S(2)}, u32[]{:S(2)}) collective-permute-start(bf16[112,576]{1,0:T(8,128)(2,1)} %get-tuple-element.137), channel_id=1, source_target_pairs={{0,24},{8,16},{16,8},{24,0},{1,25},{9,17},{17,9},{25,1},{2,26},{10... | collective-permute-start | bytes 387080 | tf_op jit(solution)/shard_map/ppermute | solution.py:619
  7.8 1.6 %collective-permute-start.6 = (bf16[296,192]{1,0:T(8,128)(2,1)}, bf16[296,192]{1,0:T(8,128)(2,1)S(1)}, u32[]{:S(2)}, u32[]{:S(2)}) collective-permute-start(bf16[296,192]{1,0:T(8,128)(2,1)} %get-tuple-element.138.proj_t), channel_id=1, source_target_pairs={{0,1},{4,7},{1,0},{5,6},{2,3},{6,5},{3,2},{7,4},{8,9},{12,15},{9,8... | collective-permute-start | bytes 341000 | tf_op jit(solution)/shard_map/ppermute | solution.py:633
  9.3 2.6 %collective-permute-start.7 = (bf16[96,192]{1,0:T(8,128)(2,1)}, bf16[96,192]{1,0:T(8,128)(2,1)S(1)}, u32[]{:S(2)}, u32[]{:S(2)}) collective-permute-start(bf16[96,192]{1,0:T(8,128)(2,1)} %get-tuple-element.139), channel_id=1, source_target_pairs={{0,2},{1,3},{2,0},{3,1},{4,6},{5,7},{6,4},{7,5},{8,10},{9,11},{10,... | collective-permute-start | bytes 110600 | tf_op jit(solution)/shard_map/ppermute | solution.py:616
  11.9 1.0 %copy-done.2 = bf16[192,768]{1,0:T(8,128)(2,1)S(1)} copy-done((bf16[192,768]{1,0:T(8,128)(2,1)S(1)}, bf16[192,768]{1,0:T(8,128)(2,1)}, u32[]{:S(2)}) %copy-start.2) | copy-done | bytes 294936
  12.9 1.0 %copy-done.3 = bf16[768,192]{0,1:T(8,128)(2,1)S(1)} copy-done((bf16[768,192]{0,1:T(8,128)(2,1)S(1)}, bf16[768,192]{0,1:T(8,128)(2,1)}, u32[]{:S(2)}) %copy-start.3) | copy-done | bytes 294936
  14.0 1.6 %collective-permute-start = (bf16[192,1280]{1,0:T(8,128)(2,1)S(1)}, bf16[192,1280]{1,0:T(8,128)(2,1)S(1)}, u32[]{:S(2)}, u32[]{:S(2)}) collective-permute-start(bf16[192,1280]{1,0:T(8,128)(2,1)S(1)} %get-tuple-element.131.refs_0_), channel_id=1, source_target_pairs={{0,8},{4,20},{8,0},{12,28},{16,24},{20,4},{24,16},{28,12},{1,9},{5... | collective-permute-start | bytes 1474568 | tf_op jit(solution)/shard_map/ppermute | solution.py:623
  15.6 1.0 %copy-done.1 = bf16[2,98,768]{2,0,1:T(2,128)(2,1)S(1)} copy-done((bf16[2,98,768]{2,0,1:T(2,128)(2,1)S(1)}, bf16[2,98,768]{2,0,1:T(2,128)(2,1)}, u32[]{:S(2)}) %copy-start.1) | copy-done | bytes 301080
  16.6 0.7 cotangent.1.refs_14_.cot
  17.3 1.0 %frame.1 = (bf16[208,768]{1,0:T(8,128)(2,1)S(1)}, f32[208,768]{1,0:T(8,128)S(1)}, f32[208,128]{1,0:T(8,128)S(1)}, f32[208,768]{1,0:T(8,128)S(1)}) custom-call(bf16[98,2,768]{2,1,0:T(2,128)(2,1)S(1)} %bitcast.11, bf16[98,2,768]{2,1,0:T(2,128)(2,1)S(1)} %collective-permute-done.2.received), custom_call_target="tpu_custom_call" | custom-call | tf_op jit(solution)/shard_map/frame/pallas_call | solution.py:34
  18.4 0.5 collective-permute-start.9
  18.9 0.9 %collective-permute-done.9.far_their = bf16[96,192]{1,0:T(8,128)(2,1)S(1)} collective-permute-done((bf16[96,192]{1,0:T(8,128)(2,1)S(1)}, bf16[96,192]{1,0:T(8,128)(2,1)S(1)}, u32[]{:S(2)}, u32[]{:S(2)}) %collective-permute-start.9) | collective-permute-done | bytes 36896 | tf_op jit(solution)/shard_map/ppermute | solution.py:613
  20.1 0.6 collective-permute-start.10
  20.7 0.5 collective-permute-start.13
  21.2 1.2 %collective-permute-done.13.refs_4_ = bf16[112,576]{1,0:T(8,128)(2,1)S(1)} collective-permute-done((bf16[112,576]{1,0:T(8,128)(2,1)S(1)}, bf16[112,576]{1,0:T(8,128)(2,1)S(1)}, u32[]{:S(2)}, u32[]{:S(2)}) %collective-permute-start.13) | collective-permute-done | bytes 129056 | tf_op jit(solution)/shard_map/ppermute | solution.py:613
  22.4 1.3 %attend.1 = (f32[8,768]{1,0:T(8,128)S(1)}, bf16[4,192,576]{2,1,0:T(8,128)(2,1)S(1)}, bf16[208,768]{1,0:T(8,128)(2,1)S(1)}, bf16[3,208,192]{2,1,0:T(8,128)(2,1)S(...) custom-call(bf16[208,576]{1,0:T(8,128)(2,1)S(1)} %copy-done.4, ...), custom_call_target="tpu_custom_call" | custom-call | tf_op jit(solution)/shard_map/attend/pallas_call | solution.py:34
  23.7 1.8 %collective-permute-start.14 = (bf16[312,128]{1,0:T(8,128)(2,1)S(1)}, bf16[312,128]{1,0:T(8,128)(2,1)S(1)}, u32[]{:S(2)}, u32[]{:S(2)}) collective-permute-start(bf16[312,128]{1,0:T(8,128)(2,1)S(1)} %get-tuple-element.153.first.refs_10_), channel_id=1, source_target_pairs={{0,3},{1,2},{2,1},{3,0},{4,7},{5,6},{6,5},{7,4},{8,11},{9,10},{10,... | collective-permute-start | bytes 239624 | tf_op jit(solution)/shard_map/ppermute | solution.py:616
  25.5 0.9 collective-permute-start.16
  26.4 1.6 %collective-permute-done.10.value.refs_4_ = bf16[192,1024]{1,0:T(8,128)(2,1)S(1)} collective-permute-done((bf16[192,1024]{1,0:T(8,128)(2,1)S(1)}, bf16[192,1024]{1,0:T(8,128)(2,1)S(1)}, u32[]{:S(2)}, u32[]{:S(2)}) %collective-permute-start.10) | collective-permute-done | bytes 393248 | tf_op jit(solution)/shard_map/ppermute | solution.py:623
  27.9 0.6 collective-permute-start.17
  28.5 1.5 %collective-permute-done.14.second.refs_11_ = bf16[312,128]{1,0:T(8,128)(2,1)S(1)} collective-permute-done((bf16[312,128]{1,0:T(8,128)(2,1)S(1)}, bf16[312,128]{1,0:T(8,128)(2,1)S(1)}, u32[]{:S(2)}, u32[]{:S(2)}) %collective-permute-start.14) | collective-permute-done | bytes 79904 | tf_op jit(solution)/shard_map/ppermute | solution.py:616
  30.2 1.6 %collective-permute-done.16.refs_6_ = bf16[96,1280]{1,0:T(8,128)(2,1)S(1)} collective-permute-done((bf16[96,1280]{1,0:T(8,128)(2,1)S(1)}, bf16[96,1280]{1,0:T(8,128)(2,1)S(1)}, u32[]{:S(2)}, u32[]{:S(2)}) %collective-permute-start.16) | collective-permute-done | bytes 245792 | tf_op jit(solution)/shard_map/ppermute | solution.py:623
  31.7 3.9 %collective-permute-done.15.refs_12_ = bf16[2,328,128]{2,1,0:T(8,128)(2,1)S(1)} collective-permute-done((bf16[2,328,128]{2,1,0:T(8,128)(2,1)S(1)}, bf16[2,328,128]{2,1,0:T(8,128)(2,1)S(1)}, u32[]{:S(2)}, u32[]{:S(2)}) %collective-permute-start.15) | collective-permute-done | bytes 167968 | tf_op jit(solution)/shard_map/ppermute | solution.py:616
  35.6 0.5 collective-permute-start.19
  36.1 1.3 %collective-permute-done.19.refs_9_ = bf16[96,1024]{1,0:T(8,128)(2,1)S(1)} collective-permute-done((bf16[96,1024]{1,0:T(8,128)(2,1)S(1)}, bf16[96,1024]{1,0:T(8,128)(2,1)S(1)}, u32[]{:S(2)}, u32[]{:S(2)}) %collective-permute-start.19) | collective-permute-done | bytes 196640 | tf_op jit(solution)/shard_map/ppermute | solution.py:613
  37.4 3.1 %feed.1 = (bf16[4,192,2304]{2,1,0:T(8,128)(2,1)S(1)}, f32[208,768]{1,0:T(8,128)S(1)}, bf16[5,208,768]{2,1,0:T(8,128)(2,1)S(1)}, f32[208,768]{1,0:T(8,128)S(1)}, ...) custom-call(bf16[192,1280]{1,0:T(8,128)(2,1)S(1)} %get-tuple-element, ...), custom_call_target="tpu_custom_call" | custom-call | tf_op jit(solution)/shard_map/feed/pallas_call | solution.py:34
  40.7 0.6 down.1
  41.3 0.4 collective-permute-start.23
  41.7 1.7 %collective-permute-start.20 = (bf16[312,128]{1,0:T(8,128)(2,1)S(1)}, bf16[312,128]{1,0:T(8,128)(2,1)S(1)}, u32[]{:S(2)}, u32[]{:S(2)}) collective-permute-start(bf16[312,128]{1,0:T(8,128)(2,1)S(1)} %get-tuple-element.163), channel_id=1, source_target_pairs={{0,3},{1,2},{2,1},{3,0},{4,7},{5,6},{6,5},{7,4},{8,11},{9,10},{10,... | collective-permute-start | bytes 239624 | tf_op jit(solution)/shard_map/ppermute | solution.py:616
  43.4 1.5 %collective-permute-start.21 = (bf16[312,128]{1,0:T(8,128)(2,1)S(1)}, bf16[312,128]{1,0:T(8,128)(2,1)S(1)}, u32[]{:S(2)}, u32[]{:S(2)}) collective-permute-start(bf16[312,128]{1,0:T(8,128)(2,1)S(1)} %get-tuple-element.164), channel_id=1, source_target_pairs={{0,2},{1,3},{2,0},{3,1},{4,6},{5,7},{6,4},{7,5},{8,10},{9,11},{10,... | collective-permute-start | bytes 239624 | tf_op jit(solution)/shard_map/ppermute | solution.py:616
  44.9 1.2 %collective-permute-start.22 = (bf16[312,128]{1,0:T(8,128)(2,1)S(1)}, bf16[312,128]{1,0:T(8,128)(2,1)S(1)}, u32[]{:S(2)}, u32[]{:S(2)}) collective-permute-start(bf16[312,128]{1,0:T(8,128)(2,1)S(1)} %get-tuple-element.165), channel_id=1, source_target_pairs={{0,1},{1,0},{2,3},{3,2},{4,5},{5,4},{6,7},{7,6},{8,9},{9,8},{10,11... | collective-permute-start | bytes 239624 | tf_op jit(solution)/shard_map/ppermute | solution.py:616
  46.1 1.5 %feed_grad.1.keep = f32[4,96,1536]{2,1,0:T(8,128)S(1)} custom-call(bf16[5,208,768]{2,1,0:T(8,128)(2,1)S(1)} %get-tuple-element.160.acts, bf16[5,208,768]{2,1,0:T(8,128)(2,1)S(1)} %collective-permute-done.24.theirs, bf16[2,208,768]{2,1,0:T(8,128)(2,1)S(1)} %cotangent.1.refs_14_.cot), custom_call_target="tpu_custom_call" | custom-call | tf_op jit(solution)/shard_map/feed_grad/pallas_call | solution.py:34
  47.8 1.5 %collective-permute-start.35 = (bf16[2,96,1536]{2,1,0:T(8,128)(2,1)S(1)}, bf16[2,96,1536]{2,1,0:T(8,128)(2,1)S(1)}, u32[]{:S(2)}, u32[]{:S(2)}) collective-permute-start(bf16[2,96,1536]{2,1,0:T(8,128)(2,1)S(1)} %get-tuple-element.209), channel_id=1, source_target_pairs={{0,8},{4,20},{8,0},{12,28},{16,24},{20,4},{24,16},{28,12},{1,9},{5... | collective-permute-start | bytes 1769480 | tf_op jit(solution)/shard_map/ppermute | solution.py:623
  49.3 0.9 proj_grad.1
  50.2 2.3 %collective-permute-done.21.refs_2_ = bf16[312,128]{1,0:T(8,128)(2,1)S(1)} collective-permute-done((bf16[312,128]{1,0:T(8,128)(2,1)S(1)}, bf16[312,128]{1,0:T(8,128)(2,1)S(1)}, u32[]{:S(2)}, u32[]{:S(2)}) %collective-permute-start.21) | collective-permute-done | bytes 79904 | tf_op jit(solution)/shard_map/ppermute | solution.py:616
  52.5 0.4 collective-permute-done.22.refs_3_
  52.9 2.0 %back.1 = (bf16[208,576]{1,0:T(8,128)(2,1)S(1)}, f32[1,576]{1,0:T(1,128)S(1)}, f32[104,768]{1,0:T(8,128)S(1)}, bf16[104,768]{1,0:T(8,128)(2,1)S(1)}) custom-call(f32[208,192]{1,0:T(8,128)S(1)} %get-tuple-element.173.refs_0_, bf16[312,128]{1,0:T(8,128)(2,1)S(1)} %collective-permute-done.20.refs_1_, bf16[312,128]{1,0:T(8,128)(2,1)S(1)} %collective-permute-done.21.refs_2_, ...), custom_call_target="tpu_custom_call" | custom-call | tf_op jit(solution)/shard_map/back/pallas_call | solution.py:34
  55.0 1.5 %collective-permute-start.27 = (bf16[96,768]{1,0:T(8,128)(2,1)S(1)}, bf16[96,768]{1,0:T(8,128)(2,1)S(1)}, u32[]{:S(2)}, u32[]{:S(2)}) collective-permute-start(bf16[96,768]{1,0:T(8,128)(2,1)S(1)} %get-tuple-element.184), channel_id=1, source_target_pairs={{0,24},{8,16},{16,8},{24,0},{1,25},{9,17},{17,9},{25,1},{2,26},{10... | collective-permute-start | bytes 442376 | tf_op jit(solution)/shard_map/ppermute | solution.py:790
  56.5 0.3 collective-permute-start.25
  56.8 1.9 %collective-permute-start.26 = (bf16[98,768]{1,0:T(8,128)(2,1)S(1)}, bf16[98,768]{1,0:T(8,128)(2,1)S(1)}, u32[]{:S(2)}, u32[]{:S(2)}) collective-permute-start(bf16[98,768]{1,0:T(8,128)(2,1)S(1)} %out_pair.1.own), channel_id=1, source_target_pairs={{0,2},{1,3},{2,0},{3,1},{4,6},{5,7},{6,4},{7,5},{8,10},{9,11},{10,... | collective-permute-start | bytes 451592 | tf_op jit(solution)/shard_map/ppermute | solution.py:616
  58.8 1.2 %collective-permute-start.28 = (bf16[96,768]{1,0:T(8,128)(2,1)S(1)}, bf16[96,768]{1,0:T(8,128)(2,1)S(1)}, u32[]{:S(2)}, u32[]{:S(2)}) collective-permute-start(bf16[96,768]{1,0:T(8,128)(2,1)S(1)} %get-tuple-element.185), channel_id=1, source_target_pairs={{0,8},{8,0},{16,24},{24,16},{1,9},{9,1},{17,25},{25,17},{2,10},{10... | collective-permute-start | bytes 442376 | tf_op jit(solution)/shard_map/ppermute | solution.py:790
  60.0 2.6 %collective-permute-done.27.refs_0_ = bf16[96,768]{1,0:T(8,128)(2,1)S(1)} collective-permute-done((bf16[96,768]{1,0:T(8,128)(2,1)S(1)}, bf16[96,768]{1,0:T(8,128)(2,1)S(1)}, u32[]{:S(2)}, u32[]{:S(2)}) %collective-permute-start.27) | collective-permute-done | bytes 147488 | tf_op jit(solution)/shard_map/ppermute | solution.py:790
  62.6 1.6 %collective-permute-start.30 = (bf16[96,768]{1,0:T(8,128)(2,1)S(1)}, bf16[96,768]{1,0:T(8,128)(2,1)S(1)}, u32[]{:S(2)}, u32[]{:S(2)}) collective-permute-start(bf16[96,768]{1,0:T(8,128)(2,1)S(1)} %get-tuple-element.188), channel_id=1, source_target_pairs={{0,16},{8,24},{16,0},{24,8},{1,17},{9,25},{17,1},{25,9},{2,18},{10... | collective-permute-start | bytes 442376 | tf_op jit(solution)/shard_map/ppermute | solution.py:810
  64.2 0.8 qkv_grad.1.keep
  65.1 0.4 collective-permute-done.28.refs_1_
  65.5 1.7 %collective-permute-done.26.received = bf16[98,768]{1,0:T(8,128)(2,1)S(1)} collective-permute-done((bf16[98,768]{1,0:T(8,128)(2,1)S(1)}, bf16[98,768]{1,0:T(8,128)(2,1)S(1)}, u32[]{:S(2)}, u32[]{:S(2)}) %collective-permute-start.26) | collective-permute-done | bytes 150560 | tf_op jit(solution)/shard_map/ppermute | solution.py:616
  67.2 0.6 collective-permute-done.30.refs_2_
  68.0 0.4 collective-permute-start.31
  68.5 1.8 %collective-permute-start.33 = (bf16[2,96,576]{2,1,0:T(8,128)(2,1)S(1)}, bf16[2,96,576]{2,1,0:T(8,128)(2,1)S(1)}, u32[]{:S(2)}, u32[]{:S(2)}) collective-permute-start(bf16[2,96,576]{2,1,0:T(8,128)(2,1)S(1)} %get-tuple-element.202), channel_id=1, source_target_pairs={{0,8},{4,20},{8,0},{12,28},{16,24},{20,4},{24,16},{28,12},{1,9},{5... | collective-permute-start | bytes 663560 | tf_op jit(solution)/shard_map/ppermute | solution.py:623
  70.3 1.1 %collective-permute-start.32 = (bf16[98,768]{1,0:T(8,128)(2,1)S(1)}, bf16[98,768]{1,0:T(8,128)(2,1)S(1)}, u32[]{:S(2)}, u32[]{:S(2)}) collective-permute-start(bf16[98,768]{1,0:T(8,128)(2,1)S(1)} %out_total.1.out_own), channel_id=1, source_target_pairs={{0,1},{1,0},{2,3},{3,2},{4,5},{5,4},{6,7},{7,6},{8,9},{9,8},{10,11... | collective-permute-start | bytes 451592 | tf_op jit(solution)/shard_map/ppermute | solution.py:616
  71.5 0.9 %collective-permute-start.36 = (bf16[96,1536]{1,0:T(8,128)(2,1)S(1)}, bf16[96,1536]{1,0:T(8,128)(2,1)S(1)}, u32[]{:S(2)}, u32[]{:S(2)}) collective-permute-start(bf16[96,1536]{1,0:T(8,128)(2,1)S(1)} %get-tuple-element.210), channel_id=1, source_target_pairs={{0,16},{4,12},{8,24},{12,4},{16,0},{20,28},{24,8},{28,20},{1,17},{... | collective-permute-start | bytes 884744 | tf_op jit(solution)/shard_map/ppermute | solution.py:623
  72.4 4.3 %collective-permute-done.32.out_in = bf16[98,768]{1,0:T(8,128)(2,1)S(1)} collective-permute-done((bf16[98,768]{1,0:T(8,128)(2,1)S(1)}, bf16[98,768]{1,0:T(8,128)(2,1)S(1)}, u32[]{:S(2)}, u32[]{:S(2)}) %collective-permute-start.32) | collective-permute-done | bytes 150560 | tf_op jit(solution)/shard_map/ppermute | solution.py:616
  76.8 0.6 collective-permute-done.33.received
  77.3 2.5 %collective-permute-done.31.received = bf16[152,768]{1,0:T(8,128)(2,1)S(1)} collective-permute-done((bf16[152,768]{1,0:T(8,128)(2,1)S(1)}, bf16[152,768]{1,0:T(8,128)(2,1)S(1)}, u32[]{:S(2)}, u32[]{:S(2)}) %collective-permute-start.31) | collective-permute-done | bytes 233504 | tf_op jit(solution)/shard_map/ppermute | solution.py:616
  80.2 1.4 %collective-permute-start.37 = (bf16[112,576]{1,0:T(8,128)(2,1)S(1)}, bf16[112,576]{1,0:T(8,128)(2,1)S(1)}, u32[]{:S(2)}, u32[]{:S(2)}) collective-permute-start(bf16[112,576]{1,0:T(8,128)(2,1)S(1)} %get-tuple-element.215), channel_id=1, source_target_pairs={{0,16},{4,12},{8,24},{12,4},{16,0},{20,28},{24,8},{28,20},{1,17},{... | collective-permute-start | bytes 387080 | tf_op jit(solution)/shard_map/ppermute | solution.py:623
  81.6 0.7 collective-permute-start.38
  82.3 1.5 %collective-permute-start.39 = (bf16[16,576]{1,0:T(8,128)(2,1)S(1)}, bf16[16,576]{1,0:T(8,128)(2,1)S(1)}, u32[]{:S(2)}, u32[]{:S(2)}) collective-permute-start(bf16[16,576]{1,0:T(8,128)(2,1)S(1)} %get-tuple-element.217), channel_id=1, source_target_pairs={{0,24},{8,16},{16,8},{24,0},{1,25},{9,17},{17,9},{25,1},{2,26},{10... | collective-permute-start | bytes 55304 | tf_op jit(solution)/shard_map/ppermute | solution.py:619
  83.8 1.6 %collective-permute-done.38.near = bf16[16,576]{1,0:T(8,128)(2,1)S(1)} collective-permute-done((bf16[16,576]{1,0:T(8,128)(2,1)S(1)}, bf16[16,576]{1,0:T(8,128)(2,1)S(1)}, u32[]{:S(2)}, u32[]{:S(2)}) %collective-permute-start.38) | collective-permute-done | bytes 18464 | tf_op jit(solution)/shard_map/ppermute | solution.py:623
  85.4 1.6 %collective-permute-done.39.far = bf16[16,576]{1,0:T(8,128)(2,1)S(1)} collective-permute-done((bf16[16,576]{1,0:T(8,128)(2,1)S(1)}, bf16[16,576]{1,0:T(8,128)(2,1)S(1)}, u32[]{:S(2)}, u32[]{:S(2)}) %collective-permute-start.39) | collective-permute-done | bytes 18464 | tf_op jit(solution)/shard_map/ppermute | solution.py:619
  87.5 0.6 collective-permute-start.41
  88.1 1.5 %collective-permute-done.42.refs_4_ = bf16[112,576]{1,0:T(8,128)(2,1)S(1)} collective-permute-done((bf16[112,576]{1,0:T(8,128)(2,1)S(1)}, bf16[112,576]{1,0:T(8,128)(2,1)S(1)}, u32[]{:S(2)}, u32[]{:S(2)}) %collective-permute-start.42) | collective-permute-done | bytes 129056 | tf_op jit(solution)/shard_map/ppermute | solution.py:613
  89.6 2.0 %final.1 = (bf16[98,2,768]{2,1,0:T(2,128)(2,1)}, f32[98,2,768]{2,1,0:T(2,128)}, f32[192,192]{1,0:T(8,128)}, f32[192,768]{1,0:T(8,128)}, f32[192,768]{1,0:T(8,128...) custom-call(f32[2,104,768]{2,1,0:T(8,128)S(1)} %get-tuple-element.22, ...), custom_call_target="tpu_custom_call" | custom-call | tf_op jit(solution)/shard_map/final/pallas_call | solution.py:34
  (61 shorter events, 2.5 us)
Async XLA Ops:
  0.6 16.6 %copy-start = (bf16[2,98,768]{2,0,1:T(2,128)(2,1)S(1)}, bf16[2,98,768]{2,0,1:T(2,128)(2,1)}, u32[]{:S(2)}) copy-start(bf16[2,98,768]{2,0,1:T(2,128)(2,1)} %param.14) | copy-start | bytes 903172
  0.7 2.6 %collective-permute-start.2 = (bf16[98,2,768]{2,1,0:T(2,128)(2,1)}, bf16[98,2,768]{2,1,0:T(2,128)(2,1)S(1)}, u32[]{:S(2)}, u32[]{:S(2)}) collective-permute-start(bf16[98,2,768]{2,1,0:T(2,128)(2,1)} %bitcast.10), channel_id=1, source_target_pairs={{0,4},{4,0},{1,5},{5,1},{2,6},{6,2},{3,7},{7,3},{8,12},{12,8},{9,1... | collective-permute-start | bytes 903176 | tf_op jit(solution)/shard_map/ppermute | solution.py:613
  1.2 2.1 %collective-permute-start.3 = (bf16[98,2,768]{2,1,0:T(2,128)(2,1)}, bf16[98,2,768]{2,1,0:T(2,128)(2,1)S(1)}, u32[]{:S(2)}, u32[]{:S(2)}) collective-permute-start(bf16[98,2,768]{2,1,0:T(2,128)(2,1)} %bitcast.12), channel_id=1, source_target_pairs={{0,4},{4,0},{1,5},{5,1},{2,6},{6,2},{3,7},{7,3},{8,12},{12,8},{9,1... | collective-permute-start | bytes 903176 | tf_op jit(solution)/shard_map/ppermute | solution.py:613
  3.3 15.1 %collective-permute-start.4 = (bf16[208,576]{1,0:T(8,128)(2,1)}, bf16[208,576]{1,0:T(8,128)(2,1)S(1)}, u32[]{:S(2)}, u32[]{:S(2)}) collective-permute-start(bf16[208,576]{1,0:T(8,128)(2,1)} %get-tuple-element.136.refs_0_), channel_id=1, source_target_pairs={{0,8},{4,20},{8,0},{12,28},{16,24},{20,4},{24,16},{28,12},{1,9},{5... | collective-permute-start | bytes 718856 | tf_op jit(solution)/shard_map/ppermute | solution.py:623
  6.3 12.1 %collective-permute-start.5 = (bf16[112,576]{1,0:T(8,128)(2,1)}, bf16[112,576]{1,0:T(8,128)(2,1)S(1)}, u32[]{:S(2)}, u32[]{:S(2)}) collective-permute-start(bf16[112,576]{1,0:T(8,128)(2,1)} %get-tuple-element.137), channel_id=1, source_target_pairs={{0,24},{8,16},{16,8},{24,0},{1,25},{9,17},{17,9},{25,1},{2,26},{10... | collective-permute-start | bytes 387080 | tf_op jit(solution)/shard_map/ppermute | solution.py:619
  7.8 10.6 %collective-permute-start.6 = (bf16[296,192]{1,0:T(8,128)(2,1)}, bf16[296,192]{1,0:T(8,128)(2,1)S(1)}, u32[]{:S(2)}, u32[]{:S(2)}) collective-permute-start(bf16[296,192]{1,0:T(8,128)(2,1)} %get-tuple-element.138.proj_t), channel_id=1, source_target_pairs={{0,1},{4,7},{1,0},{5,6},{2,3},{6,5},{3,2},{7,4},{8,9},{12,15},{9,8... | collective-permute-start | bytes 341000 | tf_op jit(solution)/shard_map/ppermute | solution.py:633
  9.3 9.0 %collective-permute-start.7 = (bf16[96,192]{1,0:T(8,128)(2,1)}, bf16[96,192]{1,0:T(8,128)(2,1)S(1)}, u32[]{:S(2)}, u32[]{:S(2)}) collective-permute-start(bf16[96,192]{1,0:T(8,128)(2,1)} %get-tuple-element.139), channel_id=1, source_target_pairs={{0,2},{1,3},{2,0},{3,1},{4,6},{5,7},{6,4},{7,5},{8,10},{9,11},{10,... | collective-permute-start | bytes 110600 | tf_op jit(solution)/shard_map/ppermute | solution.py:616
  11.9 1.0 %copy-start.2 = (bf16[192,768]{1,0:T(8,128)(2,1)S(1)}, bf16[192,768]{1,0:T(8,128)(2,1)}, u32[]{:S(2)}) copy-start(bf16[192,768]{1,0:T(8,128)(2,1)} %up.1) | copy-start | bytes 884740
  12.9 1.0 %copy-start.3 = (bf16[768,192]{0,1:T(8,128)(2,1)S(1)}, bf16[768,192]{0,1:T(8,128)(2,1)}, u32[]{:S(2)}) copy-start(bf16[768,192]{0,1:T(8,128)(2,1)} %param.25) | copy-start | bytes 884740
  13.9 6.0 %copy-start.5 = (bf16[296,192]{1,0:T(8,128)(2,1)S(1)}, bf16[296,192]{1,0:T(8,128)(2,1)}, u32[]{:S(2)}) copy-start(bf16[296,192]{1,0:T(8,128)(2,1)} %get-tuple-element.138.proj_t) | copy-start | bytes 340996
  13.9 8.6 %copy-start.4 = (bf16[208,576]{1,0:T(8,128)(2,1)S(1)}, bf16[208,576]{1,0:T(8,128)(2,1)}, u32[]{:S(2)}) copy-start(bf16[208,576]{1,0:T(8,128)(2,1)} %get-tuple-element.136.refs_0_) | copy-start | bytes 718852
  14.0 11.4 %collective-permute-start = (bf16[192,1280]{1,0:T(8,128)(2,1)S(1)}, bf16[192,1280]{1,0:T(8,128)(2,1)S(1)}, u32[]{:S(2)}, u32[]{:S(2)}) collective-permute-start(bf16[192,1280]{1,0:T(8,128)(2,1)S(1)} %get-tuple-element.131.refs_0_), channel_id=1, source_target_pairs={{0,8},{4,20},{8,0},{12,28},{16,24},{20,4},{24,16},{28,12},{1,9},{5... | collective-permute-start | bytes 1474568 | tf_op jit(solution)/shard_map/ppermute | solution.py:623
  15.6 1.0 %copy-start.1 = (bf16[2,98,768]{2,0,1:T(2,128)(2,1)S(1)}, bf16[2,98,768]{2,0,1:T(2,128)(2,1)}, u32[]{:S(2)}) copy-start(bf16[2,98,768]{2,0,1:T(2,128)(2,1)} %param.27) | copy-start | bytes 903172
  18.4 1.5 %collective-permute-start.8 = (bf16[296,192]{1,0:T(8,128)(2,1)S(1)}, bf16[296,192]{1,0:T(8,128)(2,1)S(1)}, u32[]{:S(2)}, u32[]{:S(2)}) collective-permute-start(bf16[296,192]{1,0:T(8,128)(2,1)S(1)} %collective-permute-done.6.near_in), channel_id=1, source_target_pairs={{0,4},{4,0},{1,5},{5,1},{2,6},{6,2},{3,7},{7,3},{8,12},{12,8},{9,1... | collective-permute-start | bytes 341000 | tf_op jit(solution)/shard_map/ppermute | solution.py:613
  18.4 1.4 %collective-permute-start.9 = (bf16[96,192]{1,0:T(8,128)(2,1)S(1)}, bf16[96,192]{1,0:T(8,128)(2,1)S(1)}, u32[]{:S(2)}, u32[]{:S(2)}) collective-permute-start(bf16[96,192]{1,0:T(8,128)(2,1)S(1)} %collective-permute-done.7.far_in), channel_id=1, source_target_pairs={{0,4},{4,0},{1,5},{5,1},{2,6},{6,2},{3,7},{7,3},{8,12},{12,8},{9,1... | collective-permute-start | bytes 110600 | tf_op jit(solution)/shard_map/ppermute | solution.py:613
  20.1 7.8 %collective-permute-start.10 = (bf16[192,1024]{1,0:T(8,128)(2,1)S(1)}, bf16[192,1024]{1,0:T(8,128)(2,1)S(1)}, u32[]{:S(2)}, u32[]{:S(2)}) collective-permute-start(bf16[192,1024]{1,0:T(8,128)(2,1)S(1)} %pack_rest.1.refs_3_), channel_id=1, source_target_pairs={{0,8},{4,20},{8,0},{12,28},{16,24},{20,4},{24,16},{28,12},{1,9},{5... | collective-permute-start | bytes 1179656 | tf_op jit(solution)/shard_map/ppermute | solution.py:623
  20.7 1.8 %collective-permute-start.12 = (bf16[208,576]{1,0:T(8,128)(2,1)S(1)}, bf16[208,576]{1,0:T(8,128)(2,1)S(1)}, u32[]{:S(2)}, u32[]{:S(2)}) collective-permute-start(bf16[208,576]{1,0:T(8,128)(2,1)S(1)} %collective-permute-done.4.refs_1_), channel_id=1, source_target_pairs={{0,4},{4,0},{1,5},{5,1},{2,6},{6,2},{3,7},{7,3},{8,12},{12,8},{9,1... | collective-permute-start | bytes 718856 | tf_op jit(solution)/shard_map/ppermute | solution.py:613
  20.7 1.7 %collective-permute-start.13 = (bf16[112,576]{1,0:T(8,128)(2,1)S(1)}, bf16[112,576]{1,0:T(8,128)(2,1)S(1)}, u32[]{:S(2)}, u32[]{:S(2)}) collective-permute-start(bf16[112,576]{1,0:T(8,128)(2,1)S(1)} %collective-permute-done.5.refs_3_), channel_id=1, source_target_pairs={{0,4},{4,0},{1,5},{5,1},{2,6},{6,2},{3,7},{7,3},{8,12},{12,8},{9,1... | collective-permute-start | bytes 387080 | tf_op jit(solution)/shard_map/ppermute | solution.py:613
  23.7 6.3 %collective-permute-start.14 = (bf16[312,128]{1,0:T(8,128)(2,1)S(1)}, bf16[312,128]{1,0:T(8,128)(2,1)S(1)}, u32[]{:S(2)}, u32[]{:S(2)}) collective-permute-start(bf16[312,128]{1,0:T(8,128)(2,1)S(1)} %get-tuple-element.153.first.refs_10_), channel_id=1, source_target_pairs={{0,3},{1,2},{2,1},{3,0},{4,7},{5,6},{6,5},{7,4},{8,11},{9,10},{10,... | collective-permute-start | bytes 239624 | tf_op jit(solution)/shard_map/ppermute | solution.py:616
  25.5 6.3 %collective-permute-start.16 = (bf16[96,1280]{1,0:T(8,128)(2,1)S(1)}, bf16[96,1280]{1,0:T(8,128)(2,1)S(1)}, u32[]{:S(2)}, u32[]{:S(2)}) collective-permute-start(bf16[96,1280]{1,0:T(8,128)(2,1)S(1)} %cut.2), channel_id=1, source_target_pairs={{0,16},{4,12},{8,24},{12,4},{16,0},{20,28},{24,8},{28,20},{1,17},{... | collective-permute-start | bytes 737288 | tf_op jit(solution)/shard_map/ppermute | solution.py:623
  26.4 9.8 %collective-permute-start.1 = (bf16[192,1280]{1,0:T(8,128)(2,1)S(1)}, bf16[192,1280]{1,0:T(8,128)(2,1)S(1)}, u32[]{:S(2)}, u32[]{:S(2)}) collective-permute-start(bf16[192,1280]{1,0:T(8,128)(2,1)S(1)} %collective-permute-done.value.refs_1_), channel_id=1, source_target_pairs={{0,4},{4,0},{1,5},{5,1},{2,6},{6,2},{3,7},{7,3},{8,12},{12,8},{9,1... | collective-permute-start | bytes 1474568 | tf_op jit(solution)/shard_map/ppermute | solution.py:613
  27.9 7.7 %collective-permute-start.17 = (bf16[96,1024]{1,0:T(8,128)(2,1)S(1)}, bf16[96,1024]{1,0:T(8,128)(2,1)S(1)}, u32[]{:S(2)}, u32[]{:S(2)}) collective-permute-start(bf16[96,1024]{1,0:T(8,128)(2,1)S(1)} %cut.3), channel_id=1, source_target_pairs={{0,16},{4,12},{8,24},{12,4},{16,0},{20,28},{24,8},{28,20},{1,17},{... | collective-permute-start | bytes 589832 | tf_op jit(solution)/shard_map/ppermute | solution.py:623
  30.0 5.6 %collective-permute-start.15 = (bf16[2,328,128]{2,1,0:T(8,128)(2,1)S(1)}, bf16[2,328,128]{2,1,0:T(8,128)(2,1)S(1)}, u32[]{:S(2)}, u32[]{:S(2)}) collective-permute-start(bf16[2,328,128]{2,1,0:T(8,128)(2,1)S(1)} %pair.1), channel_id=1, source_target_pairs={{0,1},{1,0},{2,3},{3,2},{4,5},{5,4},{6,7},{7,6},{8,9},{9,8},{10,11... | collective-permute-start | bytes 503816 | tf_op jit(solution)/shard_map/ppermute | solution.py:616
  30.1 6.0 %collective-permute-start.11 = (bf16[192,1024]{1,0:T(8,128)(2,1)S(1)}, bf16[192,1024]{1,0:T(8,128)(2,1)S(1)}, u32[]{:S(2)}, u32[]{:S(2)}) collective-permute-start(bf16[192,1024]{1,0:T(8,128)(2,1)S(1)} %collective-permute-done.10.value.refs_4_), channel_id=1, source_target_pairs={{0,4},{4,0},{1,5},{5,1},{2,6},{6,2},{3,7},{7,3},{8,12},{12,8},{9,1... | collective-permute-start | bytes 1179656 | tf_op jit(solution)/shard_map/ppermute | solution.py:613
  35.6 1.8 %collective-permute-start.18 = (bf16[96,1280]{1,0:T(8,128)(2,1)S(1)}, bf16[96,1280]{1,0:T(8,128)(2,1)S(1)}, u32[]{:S(2)}, u32[]{:S(2)}) collective-permute-start(bf16[96,1280]{1,0:T(8,128)(2,1)S(1)} %collective-permute-done.16.refs_6_), channel_id=1, source_target_pairs={{0,4},{4,0},{1,5},{5,1},{2,6},{6,2},{3,7},{7,3},{8,12},{12,8},{9,1... | collective-permute-start | bytes 737288 | tf_op jit(solution)/shard_map/ppermute | solution.py:613
  35.6 1.8 %collective-permute-start.19 = (bf16[96,1024]{1,0:T(8,128)(2,1)S(1)}, bf16[96,1024]{1,0:T(8,128)(2,1)S(1)}, u32[]{:S(2)}, u32[]{:S(2)}) collective-permute-start(bf16[96,1024]{1,0:T(8,128)(2,1)S(1)} %collective-permute-done.17.refs_8_), channel_id=1, source_target_pairs={{0,4},{4,0},{1,5},{5,1},{2,6},{6,2},{3,7},{7,3},{8,12},{12,8},{9,1... | collective-permute-start | bytes 589832 | tf_op jit(solution)/shard_map/ppermute | solution.py:613
  40.5 5.6 %collective-permute-start.24 = (bf16[5,208,768]{2,1,0:T(8,128)(2,1)S(1)}, bf16[5,208,768]{2,1,0:T(8,128)(2,1)S(1)}, u32[]{:S(2)}, u32[]{:S(2)}) collective-permute-start(bf16[5,208,768]{2,1,0:T(8,128)(2,1)S(1)} %get-tuple-element.160.acts), channel_id=1, source_target_pairs={{0,4},{4,0},{1,5},{5,1},{2,6},{6,2},{3,7},{7,3},{8,12},{12,8},{9,1... | collective-permute-start | bytes 4792328 | tf_op jit(solution)/shard_map/ppermute | solution.py:613
  41.3 11.6 %collective-permute-start.23 = (bf16[98,768]{1,0:T(8,128)(2,1)S(1)}, bf16[98,768]{1,0:T(8,128)(2,1)S(1)}, u32[]{:S(2)}, u32[]{:S(2)}) collective-permute-start(bf16[98,768]{1,0:T(8,128)(2,1)S(1)} %get-tuple-element.166), channel_id=1, source_target_pairs={{0,1},{1,0},{2,3},{3,2},{4,5},{5,4},{6,7},{7,6},{8,9},{9,8},{10,11... | collective-permute-start | bytes 451592 | tf_op jit(solution)/shard_map/ppermute | solution.py:616
  41.7 8.5 %collective-permute-start.20 = (bf16[312,128]{1,0:T(8,128)(2,1)S(1)}, bf16[312,128]{1,0:T(8,128)(2,1)S(1)}, u32[]{:S(2)}, u32[]{:S(2)}) collective-permute-start(bf16[312,128]{1,0:T(8,128)(2,1)S(1)} %get-tuple-element.163), channel_id=1, source_target_pairs={{0,3},{1,2},{2,1},{3,0},{4,7},{5,6},{6,5},{7,4},{8,11},{9,10},{10,... | collective-permute-start | bytes 239624 | tf_op jit(solution)/shard_map/ppermute | solution.py:616
  43.4 9.2 %collective-permute-start.21 = (bf16[312,128]{1,0:T(8,128)(2,1)S(1)}, bf16[312,128]{1,0:T(8,128)(2,1)S(1)}, u32[]{:S(2)}, u32[]{:S(2)}) collective-permute-start(bf16[312,128]{1,0:T(8,128)(2,1)S(1)} %get-tuple-element.164), channel_id=1, source_target_pairs={{0,2},{1,3},{2,0},{3,1},{4,6},{5,7},{6,4},{7,5},{8,10},{9,11},{10,... | collective-permute-start | bytes 239624 | tf_op jit(solution)/shard_map/ppermute | solution.py:616
  44.9 8.0 %collective-permute-start.22 = (bf16[312,128]{1,0:T(8,128)(2,1)S(1)}, bf16[312,128]{1,0:T(8,128)(2,1)S(1)}, u32[]{:S(2)}, u32[]{:S(2)}) collective-permute-start(bf16[312,128]{1,0:T(8,128)(2,1)S(1)} %get-tuple-element.165), channel_id=1, source_target_pairs={{0,1},{1,0},{2,3},{3,2},{4,5},{5,4},{6,7},{7,6},{8,9},{9,8},{10,11... | collective-permute-start | bytes 239624 | tf_op jit(solution)/shard_map/ppermute | solution.py:616
  47.8 23.7 %collective-permute-start.35 = (bf16[2,96,1536]{2,1,0:T(8,128)(2,1)S(1)}, bf16[2,96,1536]{2,1,0:T(8,128)(2,1)S(1)}, u32[]{:S(2)}, u32[]{:S(2)}) collective-permute-start(bf16[2,96,1536]{2,1,0:T(8,128)(2,1)S(1)} %get-tuple-element.209), channel_id=1, source_target_pairs={{0,8},{4,20},{8,0},{12,28},{16,24},{20,4},{24,16},{28,12},{1,9},{5... | collective-permute-start | bytes 1769480 | tf_op jit(solution)/shard_map/ppermute | solution.py:623
  54.9 3.9 %collective-permute-start.29 = (bf16[208,576]{1,0:T(8,128)(2,1)S(1)}, bf16[208,576]{1,0:T(8,128)(2,1)S(1)}, u32[]{:S(2)}, u32[]{:S(2)}) collective-permute-start(bf16[208,576]{1,0:T(8,128)(2,1)S(1)} %get-tuple-element.186.grads), channel_id=1, source_target_pairs={{0,4},{4,0},{1,5},{5,1},{2,6},{6,2},{3,7},{7,3},{8,12},{12,8},{9,1... | collective-permute-start | bytes 718856 | tf_op jit(solution)/shard_map/ppermute | solution.py:613
  55.0 7.6 %collective-permute-start.27 = (bf16[96,768]{1,0:T(8,128)(2,1)S(1)}, bf16[96,768]{1,0:T(8,128)(2,1)S(1)}, u32[]{:S(2)}, u32[]{:S(2)}) collective-permute-start(bf16[96,768]{1,0:T(8,128)(2,1)S(1)} %get-tuple-element.184), channel_id=1, source_target_pairs={{0,24},{8,16},{16,8},{24,0},{1,25},{9,17},{17,9},{25,1},{2,26},{10... | collective-permute-start | bytes 442376 | tf_op jit(solution)/shard_map/ppermute | solution.py:790
  56.5 10.7 %collective-permute-start.25 = (bf16[104,768]{1,0:T(8,128)(2,1)S(1)}, bf16[104,768]{1,0:T(8,128)(2,1)S(1)}, u32[]{:S(2)}, u32[]{:S(2)}) collective-permute-start(bf16[104,768]{1,0:T(8,128)(2,1)S(1)} %get-tuple-element.183), channel_id=1, source_target_pairs={{0,1},{1,0},{2,3},{3,2},{4,5},{5,4},{6,7},{7,6},{8,9},{9,8},{10,11... | collective-permute-start | bytes 479240 | tf_op jit(solution)/shard_map/ppermute | solution.py:616
  56.8 10.3 %collective-permute-start.26 = (bf16[98,768]{1,0:T(8,128)(2,1)S(1)}, bf16[98,768]{1,0:T(8,128)(2,1)S(1)}, u32[]{:S(2)}, u32[]{:S(2)}) collective-permute-start(bf16[98,768]{1,0:T(8,128)(2,1)S(1)} %out_pair.1.own), channel_id=1, source_target_pairs={{0,2},{1,3},{2,0},{3,1},{4,6},{5,7},{6,4},{7,5},{8,10},{9,11},{10,... | collective-permute-start | bytes 451592 | tf_op jit(solution)/shard_map/ppermute | solution.py:616
  58.8 6.7 %collective-permute-start.28 = (bf16[96,768]{1,0:T(8,128)(2,1)S(1)}, bf16[96,768]{1,0:T(8,128)(2,1)S(1)}, u32[]{:S(2)}, u32[]{:S(2)}) collective-permute-start(bf16[96,768]{1,0:T(8,128)(2,1)S(1)} %get-tuple-element.185), channel_id=1, source_target_pairs={{0,8},{8,0},{16,24},{24,16},{1,9},{9,1},{17,25},{25,17},{2,10},{10... | collective-permute-start | bytes 442376 | tf_op jit(solution)/shard_map/ppermute | solution.py:790
  62.6 5.1 %collective-permute-start.30 = (bf16[96,768]{1,0:T(8,128)(2,1)S(1)}, bf16[96,768]{1,0:T(8,128)(2,1)S(1)}, u32[]{:S(2)}, u32[]{:S(2)}) collective-permute-start(bf16[96,768]{1,0:T(8,128)(2,1)S(1)} %get-tuple-element.188), channel_id=1, source_target_pairs={{0,16},{8,24},{16,0},{24,8},{1,17},{9,25},{17,1},{25,9},{2,18},{10... | collective-permute-start | bytes 442376 | tf_op jit(solution)/shard_map/ppermute | solution.py:810
  68.0 11.9 %collective-permute-start.31 = (bf16[152,768]{1,0:T(8,128)(2,1)S(1)}, bf16[152,768]{1,0:T(8,128)(2,1)S(1)}, u32[]{:S(2)}, u32[]{:S(2)}) collective-permute-start(bf16[152,768]{1,0:T(8,128)(2,1)S(1)} %get-tuple-element.200.own), channel_id=1, source_target_pairs={{0,2},{1,3},{2,0},{3,1},{4,6},{5,7},{6,4},{7,5},{8,10},{9,11},{10,... | collective-permute-start | bytes 700424 | tf_op jit(solution)/shard_map/ppermute | solution.py:616
  68.5 8.9 %collective-permute-start.33 = (bf16[2,96,576]{2,1,0:T(8,128)(2,1)S(1)}, bf16[2,96,576]{2,1,0:T(8,128)(2,1)S(1)}, u32[]{:S(2)}, u32[]{:S(2)}) collective-permute-start(bf16[2,96,576]{2,1,0:T(8,128)(2,1)S(1)} %get-tuple-element.202), channel_id=1, source_target_pairs={{0,8},{4,20},{8,0},{12,28},{16,24},{20,4},{24,16},{28,12},{1,9},{5... | collective-permute-start | bytes 663560 | tf_op jit(solution)/shard_map/ppermute | solution.py:623
  70.3 6.5 %collective-permute-start.32 = (bf16[98,768]{1,0:T(8,128)(2,1)S(1)}, bf16[98,768]{1,0:T(8,128)(2,1)S(1)}, u32[]{:S(2)}, u32[]{:S(2)}) collective-permute-start(bf16[98,768]{1,0:T(8,128)(2,1)S(1)} %out_total.1.out_own), channel_id=1, source_target_pairs={{0,1},{1,0},{2,3},{3,2},{4,5},{5,4},{6,7},{7,6},{8,9},{9,8},{10,11... | collective-permute-start | bytes 451592 | tf_op jit(solution)/shard_map/ppermute | solution.py:616
  71.5 15.5 %collective-permute-start.36 = (bf16[96,1536]{1,0:T(8,128)(2,1)S(1)}, bf16[96,1536]{1,0:T(8,128)(2,1)S(1)}, u32[]{:S(2)}, u32[]{:S(2)}) collective-permute-start(bf16[96,1536]{1,0:T(8,128)(2,1)S(1)} %get-tuple-element.210), channel_id=1, source_target_pairs={{0,16},{4,12},{8,24},{12,4},{16,0},{20,28},{24,8},{28,20},{1,17},{... | collective-permute-start | bytes 884744 | tf_op jit(solution)/shard_map/ppermute | solution.py:623
  79.9 7.1 %collective-permute-start.34 = (bf16[128,768]{1,0:T(8,128)(2,1)S(1)}, bf16[128,768]{1,0:T(8,128)(2,1)S(1)}, u32[]{:S(2)}, u32[]{:S(2)}) collective-permute-start(bf16[128,768]{1,0:T(8,128)(2,1)S(1)} %get-tuple-element.207.in_own), channel_id=1, source_target_pairs={{0,1},{1,0},{2,3},{3,2},{4,5},{5,4},{6,7},{7,6},{8,9},{9,8},{10,11... | collective-permute-start | bytes 589832 | tf_op jit(solution)/shard_map/ppermute | solution.py:616
  80.2 6.8 %collective-permute-start.37 = (bf16[112,576]{1,0:T(8,128)(2,1)S(1)}, bf16[112,576]{1,0:T(8,128)(2,1)S(1)}, u32[]{:S(2)}, u32[]{:S(2)}) collective-permute-start(bf16[112,576]{1,0:T(8,128)(2,1)S(1)} %get-tuple-element.215), channel_id=1, source_target_pairs={{0,16},{4,12},{8,24},{12,4},{16,0},{20,28},{24,8},{28,20},{1,17},{... | collective-permute-start | bytes 387080 | tf_op jit(solution)/shard_map/ppermute | solution.py:623
  81.6 3.8 %collective-permute-start.38 = (bf16[16,576]{1,0:T(8,128)(2,1)S(1)}, bf16[16,576]{1,0:T(8,128)(2,1)S(1)}, u32[]{:S(2)}, u32[]{:S(2)}) collective-permute-start(bf16[16,576]{1,0:T(8,128)(2,1)S(1)} %get-tuple-element.216), channel_id=1, source_target_pairs={{0,8},{4,20},{8,0},{12,28},{16,24},{20,4},{24,16},{28,12},{1,9},{5... | collective-permute-start | bytes 55304 | tf_op jit(solution)/shard_map/ppermute | solution.py:623
  82.3 4.7 %collective-permute-start.39 = (bf16[16,576]{1,0:T(8,128)(2,1)S(1)}, bf16[16,576]{1,0:T(8,128)(2,1)S(1)}, u32[]{:S(2)}, u32[]{:S(2)}) collective-permute-start(bf16[16,576]{1,0:T(8,128)(2,1)S(1)} %get-tuple-element.217), channel_id=1, source_target_pairs={{0,24},{8,16},{16,8},{24,0},{1,25},{9,17},{17,9},{25,1},{2,26},{10... | collective-permute-start | bytes 55304 | tf_op jit(solution)/shard_map/ppermute | solution.py:619
  87.2 2.4 %collective-permute-start.40 = (bf16[232,768]{1,0:T(8,128)(2,1)S(1)}, bf16[232,768]{1,0:T(8,128)(2,1)S(1)}, u32[]{:S(2)}, u32[]{:S(2)}) collective-permute-start(bf16[232,768]{1,0:T(8,128)(2,1)S(1)} %get-tuple-element.221), channel_id=1, source_target_pairs={{0,4},{4,0},{1,5},{5,1},{2,6},{6,2},{3,7},{7,3},{8,12},{12,8},{9,1... | collective-permute-start | bytes 1069064 | tf_op jit(solution)/shard_map/ppermute | solution.py:613
  87.5 2.1 %collective-permute-start.41 = (bf16[96,1536]{1,0:T(8,128)(2,1)S(1)}, bf16[96,1536]{1,0:T(8,128)(2,1)S(1)}, u32[]{:S(2)}, u32[]{:S(2)}) collective-permute-start(bf16[96,1536]{1,0:T(8,128)(2,1)S(1)} %get-tuple-element.231), channel_id=1, source_target_pairs={{0,4},{4,0},{1,5},{5,1},{2,6},{6,2},{3,7},{7,3},{8,12},{12,8},{9,1... | collective-permute-start | bytes 884744 | tf_op jit(solution)/shard_map/ppermute | solution.py:613
  88.0 1.6 %collective-permute-start.42 = (bf16[112,576]{1,0:T(8,128)(2,1)S(1)}, bf16[112,576]{1,0:T(8,128)(2,1)S(1)}, u32[]{:S(2)}, u32[]{:S(2)}) collective-permute-start(bf16[112,576]{1,0:T(8,128)(2,1)S(1)} %get-tuple-element.233), channel_id=1, source_target_pairs={{0,4},{4,0},{1,5},{5,1},{2,6},{6,2},{3,7},{7,3},{8,12},{12,8},{9,1... | collective-permute-start | bytes 387080 | tf_op jit(solution)/shard_map/ppermute | solution.py:613

commit v10 on v9

--- a/solution.py
+++ b/solution.py
@@ -168,10 +168,9 @@
 
 
 def pair_kernel(first, second, out):
-    rows = first.shape[0]
-    out[0, :rows, :] = first[...]
-    out[1, :rows, :] = second[...]
-    out[:, rows:, :] = jnp.zeros((2, out.shape[1] - rows, out.shape[2]), LOW)
+    pad = jnp.zeros((out.shape[1] - first.shape[0], out.shape[2]), F32)
+    for i, value in enumerate((first, second)):
+        out[i] = rows_of([read(value), pad]).astype(LOW)
 
 
 def pack_rest_kernel(z, rest, proj_t, near_in, near_their, far_in, far_their, near, scratch):
@@ -298,8 +297,8 @@
     grad_out = grad_out_low.astype(F32)
     heads[t] = z.spread(read(att[0]))
     heads[t ^ 3] = z.spread(read(att[1]))
-    heads[t ^ 1] = z.spread(att[2][0, : z.dense, :].astype(F32))
-    heads[t ^ 2] = z.spread(att[2][1, : z.dense, :].astype(F32))
+    heads[t ^ 1] = z.spread(att[2][0].astype(F32)[: z.dense])
+    heads[t ^ 2] = z.spread(att[2][1].astype(F32)[: z.dense])
     attended = lanes([heads[i] for i in range(z.nt)]).astype(LOW)
     acts[4] = attended
     branch = dot(attended, w_proj_t, NT)
@@ -456,26 +455,28 @@
 
 def in_pair_kernel(z, kept, received, own, *refs):
     parts, (out, proj_kept, scratch) = refs[:3], refs[3:]
-    out[: z.padded, :] = (kept[...] + read(received)).astype(LOW)
     t = lax.axis_index("tp")
     proj = own[...] + sum(read(p) for p in parts)
     for i in range(z.nt):
         scratch[i] = fold(proj[:, i * z.inner : (i + 1) * z.inner])
     proj_kept[0] = scratch[t]
     proj_kept[1] = scratch[t ^ 1]
-    out[z.padded :, :] = rows_of([scratch[t ^ 2], scratch[t ^ 3]]).astype(LOW)
+    out[...] = rows_of([kept[...] + read(received), scratch[t ^ 2], scratch[t ^ 3]]).astype(LOW)
 
 
 def sum_rows_kernel(z, own, received, small, qv, *refs):
     if z.direct:
         proj_kept, out, vec, proj_own = refs
-        arrived = received[z.padded :, :].astype(F32)
-        proj_own[...] = proj_kept[0] + arrived[: z.tail]
-        out[z.padded :, :] = (proj_kept[1] + arrived[z.tail :]).astype(LOW)
     else:
         out, vec = refs
-    total = own[: z.padded, :].astype(F32) + received[: z.padded, :].astype(F32)
-    out[: z.padded, :] = total.astype(LOW)
+    arrived = read(received)
+    total = read(own)[: z.padded] + arrived[: z.padded]
+    if z.direct:
+        tail = arrived[z.padded :]
+        proj_own[...] = proj_kept[0] + tail[: z.tail]
+        out[...] = rows_of([total, proj_kept[1] + tail[z.tail :]]).astype(LOW)
+    else:
+        out[...] = total.astype(LOW)
     vec[...] = jnp.zeros(vec.shape, F32)
     vec[:6, :] = total[z.half : z.half + 6]
     vec[8:9, : z.ff] = small[6:7, : z.ff]
@@ -524,11 +525,12 @@
     n = z.padded
     pad = jnp.zeros((z.pad, z.width), F32)
     out_mine, out_theirs = halves_of(z, read(out_own), read(out_in))
-    in_mine, in_theirs = halves_of(z, in_own[:n, :].astype(F32), in_in[:n, :].astype(F32))
+    arrived = read(in_in)
+    in_mine, in_theirs = halves_of(z, read(in_own)[:n], arrived[:n])
     theirs = [out_theirs, pad, in_theirs]
     if z.direct:
         proj_own, mine, sent, proj = refs
-        total = proj_own[...] + in_in[n:, :].astype(F32)
+        total = proj_own[...] + arrived[n:]
         proj[...] = total
         theirs.append(total)
     else:
@@ -573,17 +575,18 @@
 
 
 def final_kernel(z, mine, theirs, *refs):
+    arrived = read(theirs)
     if z.direct:
         proj_own, feed_own, feed_in, qkv_own, qkv_in, output, input_grad, proj, up, down, *rest = refs
-        other = theirs[2 * z.padded :, :].astype(F32)
+        other = arrived[2 * z.padded :]
         proj[...] = by_half(unfold(z, proj_own[...]), unfold(z, other)).T
         feed_final_kernel(z, feed_own, feed_in, up, down)
         qkv_final_kernel(z, qkv_own, qkv_in, *rest[:-1])
         scratch = rest[-1]
     else:
         output, input_grad, scratch = refs
-    place_kernel(z, mine[1], theirs[z.padded : 2 * z.padded, :].astype(F32), input_grad)
-    place_kernel(z, mine[0], theirs[: z.padded, :].astype(F32), output, scratch)
+    place_kernel(z, mine[1], arrived[z.padded : 2 * z.padded], input_grad)
+    place_kernel(z, mine[0], arrived[: z.padded], output, scratch)
 
 
 def build(nf, nc, nt):

time: 92 us -> 92 us (level)
  no operation moved by 1% of the time
where the time goes in v10:
time: 92 us; the launch traced here: 91.8 us
  starting transfers between devices  38 us (41%)
  waiting for transfers between devices  32.2 us (35%)
  Pallas kernels  17.6 us (19%)
  local copies, waits for them, and re-layouts  2.9 us (3%)
  between operations  1.1 us (1%)
    pallas_call x27, Pallas kernels, call(): pl.pallas_call(kernel, out_shape=tuple(outs), in_specs=in_specs or [VMEM]...  17.6 us
    ppermute x12, waiting for transfers between devices, to_tp(): return lax.ppermute(value, 'tp', [(i, i ^ k) for i in range(nt)])  16.7 us
    ppermute x10, starting transfers between devices, neighbours(): return lax.ppermute(value, ('fsdp', 'ctx'), pairs)  13 us
    ppermute x12, starting transfers between devices, to_tp(): return lax.ppermute(value, 'tp', [(i, i ^ k) for i in range(nt)])  13 us
    ppermute x10, waiting for transfers between devices, neighbours(): return lax.ppermute(value, ('fsdp', 'ctx'), pairs)  5.27 us
    ppermute x15, waiting for transfers between devices, other_core(): return lax.ppermute(value, 'ctx', [(0, 1), (1, 0)])  4.97 us
    ppermute x15, starting transfers between devices, other_core(): return lax.ppermute(value, 'ctx', [(0, 1), (1, 0)])  3.26 us
    ppermute x2, waiting for transfers between devices, local(): lax.ppermute(sends[k - 1], 'fsdp', [(i, i ^ k) for i in range(nf)])  3.07 us
  transfers between devices with their start and end apart: 43, of which 19 were waited for; matrix products, arithmetic and copies ran while one was open for 0% of the time, Pallas kernels for 13%

profile of v10, /device:TPU:0, one launch (start us, length us, event | category | flops | bytes accessed | tf_op | source)
XLA Modules:
  0.0 91.8 jit_solution(5702122718361721359)
XLA Ops:
  0.7 0.5 collective-permute-start.2
  1.3 2.0 %pack.1 = (bf16[208,576]{1,0:T(8,128)(2,1)}, bf16[112,576]{1,0:T(8,128)(2,1)}, bf16[296,192]{1,0:T(8,128)(2,1)}, bf16[96,192]{1,0:T(8,128)(2,1)}) custom-call(bf16[3,192,192]{2,1,0:T(8,128)(2,1)} %bitcast.15, bf16[192,192]{1,0:T(8,128)(2,1)} %refs_1_.1, bf16[12,16]{1,0:T(8,128)(2,1)} %refs_2_.1, bf16[3,2,16]{2,1,0:T(2,128)(2,1)} %bitcast.16, ...), custom_call_target="tpu_custom_call" | custom-call | tf_op jit(solution)/shard_map/pack/pallas_call | solution.py:34
  3.3 3.0 %collective-permute-start.4 = (bf16[208,576]{1,0:T(8,128)(2,1)}, bf16[208,576]{1,0:T(8,128)(2,1)S(1)}, u32[]{:S(2)}, u32[]{:S(2)}) collective-permute-start(bf16[208,576]{1,0:T(8,128)(2,1)} %get-tuple-element.136.refs_0_), channel_id=1, source_target_pairs={{0,8},{4,20},{8,0},{12,28},{16,24},{20,4},{24,16},{28,12},{1,9},{5... | collective-permute-start | bytes 718856 | tf_op jit(solution)/shard_map/ppermute | solution.py:626
  6.3 1.5 %collective-permute-start.5 = (bf16[112,576]{1,0:T(8,128)(2,1)}, bf16[112,576]{1,0:T(8,128)(2,1)S(1)}, u32[]{:S(2)}, u32[]{:S(2)}) collective-permute-start(bf16[112,576]{1,0:T(8,128)(2,1)} %get-tuple-element.137), channel_id=1, source_target_pairs={{0,24},{8,16},{16,8},{24,0},{1,25},{9,17},{17,9},{25,1},{2,26},{10... | collective-permute-start | bytes 387080 | tf_op jit(solution)/shard_map/ppermute | solution.py:622
  7.8 1.6 %collective-permute-start.6 = (bf16[296,192]{1,0:T(8,128)(2,1)}, bf16[296,192]{1,0:T(8,128)(2,1)S(1)}, u32[]{:S(2)}, u32[]{:S(2)}) collective-permute-start(bf16[296,192]{1,0:T(8,128)(2,1)} %get-tuple-element.138.proj_t), channel_id=1, source_target_pairs={{0,1},{4,7},{1,0},{5,6},{2,3},{6,5},{3,2},{7,4},{8,9},{12,15},{9,8... | collective-permute-start | bytes 341000 | tf_op jit(solution)/shard_map/ppermute | solution.py:636
  9.3 2.6 %collective-permute-start.7 = (bf16[96,192]{1,0:T(8,128)(2,1)}, bf16[96,192]{1,0:T(8,128)(2,1)S(1)}, u32[]{:S(2)}, u32[]{:S(2)}) collective-permute-start(bf16[96,192]{1,0:T(8,128)(2,1)} %get-tuple-element.139), channel_id=1, source_target_pairs={{0,2},{1,3},{2,0},{3,1},{4,6},{5,7},{6,4},{7,5},{8,10},{9,11},{10,... | collective-permute-start | bytes 110600 | tf_op jit(solution)/shard_map/ppermute | solution.py:619
  11.9 1.0 %copy-done.2 = bf16[192,768]{1,0:T(8,128)(2,1)S(1)} copy-done((bf16[192,768]{1,0:T(8,128)(2,1)S(1)}, bf16[192,768]{1,0:T(8,128)(2,1)}, u32[]{:S(2)}) %copy-start.2) | copy-done | bytes 294936
  12.9 1.0 %copy-done.3 = bf16[768,192]{0,1:T(8,128)(2,1)S(1)} copy-done((bf16[768,192]{0,1:T(8,128)(2,1)S(1)}, bf16[768,192]{0,1:T(8,128)(2,1)}, u32[]{:S(2)}) %copy-start.3) | copy-done | bytes 294936
  14.0 1.6 %collective-permute-start = (bf16[192,1280]{1,0:T(8,128)(2,1)S(1)}, bf16[192,1280]{1,0:T(8,128)(2,1)S(1)}, u32[]{:S(2)}, u32[]{:S(2)}) collective-permute-start(bf16[192,1280]{1,0:T(8,128)(2,1)S(1)} %get-tuple-element.131.refs_0_), channel_id=1, source_target_pairs={{0,8},{4,20},{8,0},{12,28},{16,24},{20,4},{24,16},{28,12},{1,9},{5... | collective-permute-start | bytes 1474568 | tf_op jit(solution)/shard_map/ppermute | solution.py:626
  15.6 1.0 %copy-done.1 = bf16[2,98,768]{2,0,1:T(2,128)(2,1)S(1)} copy-done((bf16[2,98,768]{2,0,1:T(2,128)(2,1)S(1)}, bf16[2,98,768]{2,0,1:T(2,128)(2,1)}, u32[]{:S(2)}) %copy-start.1) | copy-done | bytes 301080
  16.6 0.7 cotangent.1.refs_14_.cot
  17.3 1.0 %frame.1 = (bf16[208,768]{1,0:T(8,128)(2,1)S(1)}, f32[208,768]{1,0:T(8,128)S(1)}, f32[208,128]{1,0:T(8,128)S(1)}, f32[208,768]{1,0:T(8,128)S(1)}) custom-call(bf16[98,2,768]{2,1,0:T(2,128)(2,1)S(1)} %bitcast.11, bf16[98,2,768]{2,1,0:T(2,128)(2,1)S(1)} %collective-permute-done.2.received), custom_call_target="tpu_custom_call" | custom-call | tf_op jit(solution)/shard_map/frame/pallas_call | solution.py:34
  18.4 0.5 collective-permute-start.9
  18.9 0.9 %collective-permute-done.9.far_their = bf16[96,192]{1,0:T(8,128)(2,1)S(1)} collective-permute-done((bf16[96,192]{1,0:T(8,128)(2,1)S(1)}, bf16[96,192]{1,0:T(8,128)(2,1)S(1)}, u32[]{:S(2)}, u32[]{:S(2)}) %collective-permute-start.9) | collective-permute-done | bytes 36896 | tf_op jit(solution)/shard_map/ppermute | solution.py:616
  20.1 0.6 collective-permute-start.10
  20.7 0.5 collective-permute-start.13
  21.2 1.2 %collective-permute-done.13.refs_4_ = bf16[112,576]{1,0:T(8,128)(2,1)S(1)} collective-permute-done((bf16[112,576]{1,0:T(8,128)(2,1)S(1)}, bf16[112,576]{1,0:T(8,128)(2,1)S(1)}, u32[]{:S(2)}, u32[]{:S(2)}) %collective-permute-start.13) | collective-permute-done | bytes 129056 | tf_op jit(solution)/shard_map/ppermute | solution.py:616
  22.4 1.3 %attend.1 = (f32[8,768]{1,0:T(8,128)S(1)}, bf16[4,192,576]{2,1,0:T(8,128)(2,1)S(1)}, bf16[208,768]{1,0:T(8,128)(2,1)S(1)}, bf16[3,208,192]{2,1,0:T(8,128)(2,1)S(...) custom-call(bf16[208,576]{1,0:T(8,128)(2,1)S(1)} %copy-done.4, ...), custom_call_target="tpu_custom_call" | custom-call | tf_op jit(solution)/shard_map/attend/pallas_call | solution.py:34
  23.7 1.8 %collective-permute-start.14 = (bf16[312,128]{1,0:T(8,128)(2,1)S(1)}, bf16[312,128]{1,0:T(8,128)(2,1)S(1)}, u32[]{:S(2)}, u32[]{:S(2)}) collective-permute-start(bf16[312,128]{1,0:T(8,128)(2,1)S(1)} %get-tuple-element.153.first.refs_10_), channel_id=1, source_target_pairs={{0,3},{1,2},{2,1},{3,0},{4,7},{5,6},{6,5},{7,4},{8,11},{9,10},{10,... | collective-permute-start | bytes 239624 | tf_op jit(solution)/shard_map/ppermute | solution.py:619
  25.5 0.9 collective-permute-start.16
  26.4 1.6 %collective-permute-done.10.value.refs_4_ = bf16[192,1024]{1,0:T(8,128)(2,1)S(1)} collective-permute-done((bf16[192,1024]{1,0:T(8,128)(2,1)S(1)}, bf16[192,1024]{1,0:T(8,128)(2,1)S(1)}, u32[]{:S(2)}, u32[]{:S(2)}) %collective-permute-start.10) | collective-permute-done | bytes 393248 | tf_op jit(solution)/shard_map/ppermute | solution.py:626
  27.9 0.6 collective-permute-start.17
  28.5 1.5 %collective-permute-done.14.second.refs_11_ = bf16[312,128]{1,0:T(8,128)(2,1)S(1)} collective-permute-done((bf16[312,128]{1,0:T(8,128)(2,1)S(1)}, bf16[312,128]{1,0:T(8,128)(2,1)S(1)}, u32[]{:S(2)}, u32[]{:S(2)}) %collective-permute-start.14) | collective-permute-done | bytes 79904 | tf_op jit(solution)/shard_map/ppermute | solution.py:619
  30.2 1.5 %collective-permute-done.16.refs_6_ = bf16[96,1280]{1,0:T(8,128)(2,1)S(1)} collective-permute-done((bf16[96,1280]{1,0:T(8,128)(2,1)S(1)}, bf16[96,1280]{1,0:T(8,128)(2,1)S(1)}, u32[]{:S(2)}, u32[]{:S(2)}) %collective-permute-start.16) | collective-permute-done | bytes 245792 | tf_op jit(solution)/shard_map/ppermute | solution.py:626
  31.7 3.9 %collective-permute-done.15.refs_12_ = bf16[2,328,128]{2,1,0:T(8,128)(2,1)S(1)} collective-permute-done((bf16[2,328,128]{2,1,0:T(8,128)(2,1)S(1)}, bf16[2,328,128]{2,1,0:T(8,128)(2,1)S(1)}, u32[]{:S(2)}, u32[]{:S(2)}) %collective-permute-start.15) | collective-permute-done | bytes 167968 | tf_op jit(solution)/shard_map/ppermute | solution.py:619
  35.6 0.5 collective-permute-start.19
  36.1 1.3 %collective-permute-done.19.refs_9_ = bf16[96,1024]{1,0:T(8,128)(2,1)S(1)} collective-permute-done((bf16[96,1024]{1,0:T(8,128)(2,1)S(1)}, bf16[96,1024]{1,0:T(8,128)(2,1)S(1)}, u32[]{:S(2)}, u32[]{:S(2)}) %collective-permute-start.19) | collective-permute-done | bytes 196640 | tf_op jit(solution)/shard_map/ppermute | solution.py:616
  37.4 3.1 %feed.1 = (bf16[4,192,2304]{2,1,0:T(8,128)(2,1)S(1)}, f32[208,768]{1,0:T(8,128)S(1)}, bf16[5,208,768]{2,1,0:T(8,128)(2,1)S(1)}, f32[208,768]{1,0:T(8,128)S(1)}, ...) custom-call(bf16[192,1280]{1,0:T(8,128)(2,1)S(1)} %get-tuple-element, ...), custom_call_target="tpu_custom_call" | custom-call | tf_op jit(solution)/shard_map/feed/pallas_call | solution.py:34
  40.7 0.6 down.1
  41.3 0.4 collective-permute-start.23
  41.7 1.7 %collective-permute-start.20 = (bf16[312,128]{1,0:T(8,128)(2,1)S(1)}, bf16[312,128]{1,0:T(8,128)(2,1)S(1)}, u32[]{:S(2)}, u32[]{:S(2)}) collective-permute-start(bf16[312,128]{1,0:T(8,128)(2,1)S(1)} %get-tuple-element.163), channel_id=1, source_target_pairs={{0,3},{1,2},{2,1},{3,0},{4,7},{5,6},{6,5},{7,4},{8,11},{9,10},{10,... | collective-permute-start | bytes 239624 | tf_op jit(solution)/shard_map/ppermute | solution.py:619
  43.4 1.5 %collective-permute-start.21 = (bf16[312,128]{1,0:T(8,128)(2,1)S(1)}, bf16[312,128]{1,0:T(8,128)(2,1)S(1)}, u32[]{:S(2)}, u32[]{:S(2)}) collective-permute-start(bf16[312,128]{1,0:T(8,128)(2,1)S(1)} %get-tuple-element.164), channel_id=1, source_target_pairs={{0,2},{1,3},{2,0},{3,1},{4,6},{5,7},{6,4},{7,5},{8,10},{9,11},{10,... | collective-permute-start | bytes 239624 | tf_op jit(solution)/shard_map/ppermute | solution.py:619
  44.9 1.2 %collective-permute-start.22 = (bf16[312,128]{1,0:T(8,128)(2,1)S(1)}, bf16[312,128]{1,0:T(8,128)(2,1)S(1)}, u32[]{:S(2)}, u32[]{:S(2)}) collective-permute-start(bf16[312,128]{1,0:T(8,128)(2,1)S(1)} %get-tuple-element.165), channel_id=1, source_target_pairs={{0,1},{1,0},{2,3},{3,2},{4,5},{5,4},{6,7},{7,6},{8,9},{9,8},{10,11... | collective-permute-start | bytes 239624 | tf_op jit(solution)/shard_map/ppermute | solution.py:619
  46.1 1.5 %feed_grad.1.keep = f32[4,96,1536]{2,1,0:T(8,128)S(1)} custom-call(bf16[5,208,768]{2,1,0:T(8,128)(2,1)S(1)} %get-tuple-element.160.acts, bf16[5,208,768]{2,1,0:T(8,128)(2,1)S(1)} %collective-permute-done.24.theirs, bf16[2,208,768]{2,1,0:T(8,128)(2,1)S(1)} %cotangent.1.refs_14_.cot), custom_call_target="tpu_custom_call" | custom-call | tf_op jit(solution)/shard_map/feed_grad/pallas_call | solution.py:34
  47.8 1.5 %collective-permute-start.35 = (bf16[2,96,1536]{2,1,0:T(8,128)(2,1)S(1)}, bf16[2,96,1536]{2,1,0:T(8,128)(2,1)S(1)}, u32[]{:S(2)}, u32[]{:S(2)}) collective-permute-start(bf16[2,96,1536]{2,1,0:T(8,128)(2,1)S(1)} %get-tuple-element.209), channel_id=1, source_target_pairs={{0,8},{4,20},{8,0},{12,28},{16,24},{20,4},{24,16},{28,12},{1,9},{5... | collective-permute-start | bytes 1769480 | tf_op jit(solution)/shard_map/ppermute | solution.py:626
  49.3 0.9 proj_grad.1
  50.2 2.3 %collective-permute-done.21.refs_2_ = bf16[312,128]{1,0:T(8,128)(2,1)S(1)} collective-permute-done((bf16[312,128]{1,0:T(8,128)(2,1)S(1)}, bf16[312,128]{1,0:T(8,128)(2,1)S(1)}, u32[]{:S(2)}, u32[]{:S(2)}) %collective-permute-start.21) | collective-permute-done | bytes 79904 | tf_op jit(solution)/shard_map/ppermute | solution.py:619
  52.5 0.4 collective-permute-done.22.refs_3_
  52.9 2.0 %back.1 = (bf16[208,576]{1,0:T(8,128)(2,1)S(1)}, f32[1,576]{1,0:T(1,128)S(1)}, f32[104,768]{1,0:T(8,128)S(1)}, bf16[104,768]{1,0:T(8,128)(2,1)S(1)}) custom-call(f32[208,192]{1,0:T(8,128)S(1)} %get-tuple-element.173.refs_0_, bf16[312,128]{1,0:T(8,128)(2,1)S(1)} %collective-permute-done.20.refs_1_, bf16[312,128]{1,0:T(8,128)(2,1)S(1)} %collective-permute-done.21.refs_2_, ...), custom_call_target="tpu_custom_call" | custom-call | tf_op jit(solution)/shard_map/back/pallas_call | solution.py:34
  55.0 1.5 %collective-permute-start.27 = (bf16[96,768]{1,0:T(8,128)(2,1)S(1)}, bf16[96,768]{1,0:T(8,128)(2,1)S(1)}, u32[]{:S(2)}, u32[]{:S(2)}) collective-permute-start(bf16[96,768]{1,0:T(8,128)(2,1)S(1)} %get-tuple-element.184), channel_id=1, source_target_pairs={{0,24},{8,16},{16,8},{24,0},{1,25},{9,17},{17,9},{25,1},{2,26},{10... | collective-permute-start | bytes 442376 | tf_op jit(solution)/shard_map/ppermute | solution.py:793
  56.5 0.3 collective-permute-start.25
  56.8 2.0 %collective-permute-start.26 = (bf16[98,768]{1,0:T(8,128)(2,1)S(1)}, bf16[98,768]{1,0:T(8,128)(2,1)S(1)}, u32[]{:S(2)}, u32[]{:S(2)}) collective-permute-start(bf16[98,768]{1,0:T(8,128)(2,1)S(1)} %out_pair.1.own), channel_id=1, source_target_pairs={{0,2},{1,3},{2,0},{3,1},{4,6},{5,7},{6,4},{7,5},{8,10},{9,11},{10,... | collective-permute-start | bytes 451592 | tf_op jit(solution)/shard_map/ppermute | solution.py:619
  58.8 1.2 %collective-permute-start.28 = (bf16[96,768]{1,0:T(8,128)(2,1)S(1)}, bf16[96,768]{1,0:T(8,128)(2,1)S(1)}, u32[]{:S(2)}, u32[]{:S(2)}) collective-permute-start(bf16[96,768]{1,0:T(8,128)(2,1)S(1)} %get-tuple-element.185), channel_id=1, source_target_pairs={{0,8},{8,0},{16,24},{24,16},{1,9},{9,1},{17,25},{25,17},{2,10},{10... | collective-permute-start | bytes 442376 | tf_op jit(solution)/shard_map/ppermute | solution.py:793
  60.0 2.6 %collective-permute-done.27.refs_0_ = bf16[96,768]{1,0:T(8,128)(2,1)S(1)} collective-permute-done((bf16[96,768]{1,0:T(8,128)(2,1)S(1)}, bf16[96,768]{1,0:T(8,128)(2,1)S(1)}, u32[]{:S(2)}, u32[]{:S(2)}) %collective-permute-start.27) | collective-permute-done | bytes 147488 | tf_op jit(solution)/shard_map/ppermute | solution.py:793
  62.6 1.6 %collective-permute-start.30 = (bf16[96,768]{1,0:T(8,128)(2,1)S(1)}, bf16[96,768]{1,0:T(8,128)(2,1)S(1)}, u32[]{:S(2)}, u32[]{:S(2)}) collective-permute-start(bf16[96,768]{1,0:T(8,128)(2,1)S(1)} %get-tuple-element.188), channel_id=1, source_target_pairs={{0,16},{8,24},{16,0},{24,8},{1,17},{9,25},{17,1},{25,9},{2,18},{10... | collective-permute-start | bytes 442376 | tf_op jit(solution)/shard_map/ppermute | solution.py:813
  64.3 0.8 qkv_grad.1.keep
  65.1 0.4 collective-permute-done.28.refs_1_
  65.5 1.7 %collective-permute-done.26.received = bf16[98,768]{1,0:T(8,128)(2,1)S(1)} collective-permute-done((bf16[98,768]{1,0:T(8,128)(2,1)S(1)}, bf16[98,768]{1,0:T(8,128)(2,1)S(1)}, u32[]{:S(2)}, u32[]{:S(2)}) %collective-permute-start.26) | collective-permute-done | bytes 150560 | tf_op jit(solution)/shard_map/ppermute | solution.py:619
  67.2 0.6 collective-permute-done.30.refs_2_
  68.0 0.4 collective-permute-start.31
  68.5 1.8 %collective-permute-start.33 = (bf16[2,96,576]{2,1,0:T(8,128)(2,1)S(1)}, bf16[2,96,576]{2,1,0:T(8,128)(2,1)S(1)}, u32[]{:S(2)}, u32[]{:S(2)}) collective-permute-start(bf16[2,96,576]{2,1,0:T(8,128)(2,1)S(1)} %get-tuple-element.202), channel_id=1, source_target_pairs={{0,8},{4,20},{8,0},{12,28},{16,24},{20,4},{24,16},{28,12},{1,9},{5... | collective-permute-start | bytes 663560 | tf_op jit(solution)/shard_map/ppermute | solution.py:626
  70.4 1.1 %collective-permute-start.32 = (bf16[98,768]{1,0:T(8,128)(2,1)S(1)}, bf16[98,768]{1,0:T(8,128)(2,1)S(1)}, u32[]{:S(2)}, u32[]{:S(2)}) collective-permute-start(bf16[98,768]{1,0:T(8,128)(2,1)S(1)} %out_total.1.out_own), channel_id=1, source_target_pairs={{0,1},{1,0},{2,3},{3,2},{4,5},{5,4},{6,7},{7,6},{8,9},{9,8},{10,11... | collective-permute-start | bytes 451592 | tf_op jit(solution)/shard_map/ppermute | solution.py:619
  71.5 0.9 %collective-permute-start.36 = (bf16[96,1536]{1,0:T(8,128)(2,1)S(1)}, bf16[96,1536]{1,0:T(8,128)(2,1)S(1)}, u32[]{:S(2)}, u32[]{:S(2)}) collective-permute-start(bf16[96,1536]{1,0:T(8,128)(2,1)S(1)} %get-tuple-element.210), channel_id=1, source_target_pairs={{0,16},{4,12},{8,24},{12,4},{16,0},{20,28},{24,8},{28,20},{1,17},{... | collective-permute-start | bytes 884744 | tf_op jit(solution)/shard_map/ppermute | solution.py:626
  72.5 4.4 %collective-permute-done.32.out_in = bf16[98,768]{1,0:T(8,128)(2,1)S(1)} collective-permute-done((bf16[98,768]{1,0:T(8,128)(2,1)S(1)}, bf16[98,768]{1,0:T(8,128)(2,1)S(1)}, u32[]{:S(2)}, u32[]{:S(2)}) %collective-permute-start.32) | collective-permute-done | bytes 150560 | tf_op jit(solution)/shard_map/ppermute | solution.py:619
  76.8 0.5 collective-permute-done.33.received
  77.4 2.5 %collective-permute-done.31.received = bf16[152,768]{1,0:T(8,128)(2,1)S(1)} collective-permute-done((bf16[152,768]{1,0:T(8,128)(2,1)S(1)}, bf16[152,768]{1,0:T(8,128)(2,1)S(1)}, u32[]{:S(2)}, u32[]{:S(2)}) %collective-permute-start.31) | collective-permute-done | bytes 233504 | tf_op jit(solution)/shard_map/ppermute | solution.py:619
  80.3 1.4 %collective-permute-start.37 = (bf16[112,576]{1,0:T(8,128)(2,1)S(1)}, bf16[112,576]{1,0:T(8,128)(2,1)S(1)}, u32[]{:S(2)}, u32[]{:S(2)}) collective-permute-start(bf16[112,576]{1,0:T(8,128)(2,1)S(1)} %get-tuple-element.215), channel_id=1, source_target_pairs={{0,16},{4,12},{8,24},{12,4},{16,0},{20,28},{24,8},{28,20},{1,17},{... | collective-permute-start | bytes 387080 | tf_op jit(solution)/shard_map/ppermute | solution.py:626
  81.7 0.7 collective-permute-start.38
  82.4 1.5 %collective-permute-start.39 = (bf16[16,576]{1,0:T(8,128)(2,1)S(1)}, bf16[16,576]{1,0:T(8,128)(2,1)S(1)}, u32[]{:S(2)}, u32[]{:S(2)}) collective-permute-start(bf16[16,576]{1,0:T(8,128)(2,1)S(1)} %get-tuple-element.217), channel_id=1, source_target_pairs={{0,24},{8,16},{16,8},{24,0},{1,25},{9,17},{17,9},{25,1},{2,26},{10... | collective-permute-start | bytes 55304 | tf_op jit(solution)/shard_map/ppermute | solution.py:622
  83.8 1.6 %collective-permute-done.38.near = bf16[16,576]{1,0:T(8,128)(2,1)S(1)} collective-permute-done((bf16[16,576]{1,0:T(8,128)(2,1)S(1)}, bf16[16,576]{1,0:T(8,128)(2,1)S(1)}, u32[]{:S(2)}, u32[]{:S(2)}) %collective-permute-start.38) | collective-permute-done | bytes 18464 | tf_op jit(solution)/shard_map/ppermute | solution.py:626
  85.5 1.6 %collective-permute-done.39.far = bf16[16,576]{1,0:T(8,128)(2,1)S(1)} collective-permute-done((bf16[16,576]{1,0:T(8,128)(2,1)S(1)}, bf16[16,576]{1,0:T(8,128)(2,1)S(1)}, u32[]{:S(2)}, u32[]{:S(2)}) %collective-permute-start.39) | collective-permute-done | bytes 18464 | tf_op jit(solution)/shard_map/ppermute | solution.py:622
  87.5 0.6 collective-permute-start.41
  88.1 1.5 %collective-permute-done.42.refs_4_ = bf16[112,576]{1,0:T(8,128)(2,1)S(1)} collective-permute-done((bf16[112,576]{1,0:T(8,128)(2,1)S(1)}, bf16[112,576]{1,0:T(8,128)(2,1)S(1)}, u32[]{:S(2)}, u32[]{:S(2)}) %collective-permute-start.42) | collective-permute-done | bytes 129056 | tf_op jit(solution)/shard_map/ppermute | solution.py:616
  89.6 2.0 %final.1 = (bf16[98,2,768]{2,1,0:T(2,128)(2,1)}, f32[98,2,768]{2,1,0:T(2,128)}, f32[192,192]{1,0:T(8,128)}, f32[192,768]{1,0:T(8,128)}, f32[192,768]{1,0:T(8,128...) custom-call(f32[2,104,768]{2,1,0:T(8,128)S(1)} %get-tuple-element.22, ...), custom_call_target="tpu_custom_call" | custom-call | tf_op jit(solution)/shard_map/final/pallas_call | solution.py:34
  (61 shorter events, 2.5 us)
Async XLA Ops:
  0.6 16.6 %copy-start = (bf16[2,98,768]{2,0,1:T(2,128)(2,1)S(1)}, bf16[2,98,768]{2,0,1:T(2,128)(2,1)}, u32[]{:S(2)}) copy-start(bf16[2,98,768]{2,0,1:T(2,128)(2,1)} %param.14) | copy-start | bytes 903172
  0.7 2.6 %collective-permute-start.2 = (bf16[98,2,768]{2,1,0:T(2,128)(2,1)}, bf16[98,2,768]{2,1,0:T(2,128)(2,1)S(1)}, u32[]{:S(2)}, u32[]{:S(2)}) collective-permute-start(bf16[98,2,768]{2,1,0:T(2,128)(2,1)} %bitcast.10), channel_id=1, source_target_pairs={{0,4},{4,0},{1,5},{5,1},{2,6},{6,2},{3,7},{7,3},{8,12},{12,8},{9,1... | collective-permute-start | bytes 903176 | tf_op jit(solution)/shard_map/ppermute | solution.py:616
  1.2 2.1 %collective-permute-start.3 = (bf16[98,2,768]{2,1,0:T(2,128)(2,1)}, bf16[98,2,768]{2,1,0:T(2,128)(2,1)S(1)}, u32[]{:S(2)}, u32[]{:S(2)}) collective-permute-start(bf16[98,2,768]{2,1,0:T(2,128)(2,1)} %bitcast.12), channel_id=1, source_target_pairs={{0,4},{4,0},{1,5},{5,1},{2,6},{6,2},{3,7},{7,3},{8,12},{12,8},{9,1... | collective-permute-start | bytes 903176 | tf_op jit(solution)/shard_map/ppermute | solution.py:616
  3.3 15.1 %collective-permute-start.4 = (bf16[208,576]{1,0:T(8,128)(2,1)}, bf16[208,576]{1,0:T(8,128)(2,1)S(1)}, u32[]{:S(2)}, u32[]{:S(2)}) collective-permute-start(bf16[208,576]{1,0:T(8,128)(2,1)} %get-tuple-element.136.refs_0_), channel_id=1, source_target_pairs={{0,8},{4,20},{8,0},{12,28},{16,24},{20,4},{24,16},{28,12},{1,9},{5... | collective-permute-start | bytes 718856 | tf_op jit(solution)/shard_map/ppermute | solution.py:626
  6.3 12.1 %collective-permute-start.5 = (bf16[112,576]{1,0:T(8,128)(2,1)}, bf16[112,576]{1,0:T(8,128)(2,1)S(1)}, u32[]{:S(2)}, u32[]{:S(2)}) collective-permute-start(bf16[112,576]{1,0:T(8,128)(2,1)} %get-tuple-element.137), channel_id=1, source_target_pairs={{0,24},{8,16},{16,8},{24,0},{1,25},{9,17},{17,9},{25,1},{2,26},{10... | collective-permute-start | bytes 387080 | tf_op jit(solution)/shard_map/ppermute | solution.py:622
  7.8 10.6 %collective-permute-start.6 = (bf16[296,192]{1,0:T(8,128)(2,1)}, bf16[296,192]{1,0:T(8,128)(2,1)S(1)}, u32[]{:S(2)}, u32[]{:S(2)}) collective-permute-start(bf16[296,192]{1,0:T(8,128)(2,1)} %get-tuple-element.138.proj_t), channel_id=1, source_target_pairs={{0,1},{4,7},{1,0},{5,6},{2,3},{6,5},{3,2},{7,4},{8,9},{12,15},{9,8... | collective-permute-start | bytes 341000 | tf_op jit(solution)/shard_map/ppermute | solution.py:636
  9.3 9.0 %collective-permute-start.7 = (bf16[96,192]{1,0:T(8,128)(2,1)}, bf16[96,192]{1,0:T(8,128)(2,1)S(1)}, u32[]{:S(2)}, u32[]{:S(2)}) collective-permute-start(bf16[96,192]{1,0:T(8,128)(2,1)} %get-tuple-element.139), channel_id=1, source_target_pairs={{0,2},{1,3},{2,0},{3,1},{4,6},{5,7},{6,4},{7,5},{8,10},{9,11},{10,... | collective-permute-start | bytes 110600 | tf_op jit(solution)/shard_map/ppermute | solution.py:619
  11.9 1.0 %copy-start.2 = (bf16[192,768]{1,0:T(8,128)(2,1)S(1)}, bf16[192,768]{1,0:T(8,128)(2,1)}, u32[]{:S(2)}) copy-start(bf16[192,768]{1,0:T(8,128)(2,1)} %up.1) | copy-start | bytes 884740
  12.9 1.0 %copy-start.3 = (bf16[768,192]{0,1:T(8,128)(2,1)S(1)}, bf16[768,192]{0,1:T(8,128)(2,1)}, u32[]{:S(2)}) copy-start(bf16[768,192]{0,1:T(8,128)(2,1)} %param.25) | copy-start | bytes 884740
  13.9 6.0 %copy-start.5 = (bf16[296,192]{1,0:T(8,128)(2,1)S(1)}, bf16[296,192]{1,0:T(8,128)(2,1)}, u32[]{:S(2)}) copy-start(bf16[296,192]{1,0:T(8,128)(2,1)} %get-tuple-element.138.proj_t) | copy-start | bytes 340996
  13.9 8.6 %copy-start.4 = (bf16[208,576]{1,0:T(8,128)(2,1)S(1)}, bf16[208,576]{1,0:T(8,128)(2,1)}, u32[]{:S(2)}) copy-start(bf16[208,576]{1,0:T(8,128)(2,1)} %get-tuple-element.136.refs_0_) | copy-start | bytes 718852
  14.0 11.4 %collective-permute-start = (bf16[192,1280]{1,0:T(8,128)(2,1)S(1)}, bf16[192,1280]{1,0:T(8,128)(2,1)S(1)}, u32[]{:S(2)}, u32[]{:S(2)}) collective-permute-start(bf16[192,1280]{1,0:T(8,128)(2,1)S(1)} %get-tuple-element.131.refs_0_), channel_id=1, source_target_pairs={{0,8},{4,20},{8,0},{12,28},{16,24},{20,4},{24,16},{28,12},{1,9},{5... | collective-permute-start | bytes 1474568 | tf_op jit(solution)/shard_map/ppermute | solution.py:626
  15.6 1.0 %copy-start.1 = (bf16[2,98,768]{2,0,1:T(2,128)(2,1)S(1)}, bf16[2,98,768]{2,0,1:T(2,128)(2,1)}, u32[]{:S(2)}) copy-start(bf16[2,98,768]{2,0,1:T(2,128)(2,1)} %param.27) | copy-start | bytes 903172
  18.4 1.5 %collective-permute-start.8 = (bf16[296,192]{1,0:T(8,128)(2,1)S(1)}, bf16[296,192]{1,0:T(8,128)(2,1)S(1)}, u32[]{:S(2)}, u32[]{:S(2)}) collective-permute-start(bf16[296,192]{1,0:T(8,128)(2,1)S(1)} %collective-permute-done.6.near_in), channel_id=1, source_target_pairs={{0,4},{4,0},{1,5},{5,1},{2,6},{6,2},{3,7},{7,3},{8,12},{12,8},{9,1... | collective-permute-start | bytes 341000 | tf_op jit(solution)/shard_map/ppermute | solution.py:616
  18.4 1.4 %collective-permute-start.9 = (bf16[96,192]{1,0:T(8,128)(2,1)S(1)}, bf16[96,192]{1,0:T(8,128)(2,1)S(1)}, u32[]{:S(2)}, u32[]{:S(2)}) collective-permute-start(bf16[96,192]{1,0:T(8,128)(2,1)S(1)} %collective-permute-done.7.far_in), channel_id=1, source_target_pairs={{0,4},{4,0},{1,5},{5,1},{2,6},{6,2},{3,7},{7,3},{8,12},{12,8},{9,1... | collective-permute-start | bytes 110600 | tf_op jit(solution)/shard_map/ppermute | solution.py:616
  20.1 7.8 %collective-permute-start.10 = (bf16[192,1024]{1,0:T(8,128)(2,1)S(1)}, bf16[192,1024]{1,0:T(8,128)(2,1)S(1)}, u32[]{:S(2)}, u32[]{:S(2)}) collective-permute-start(bf16[192,1024]{1,0:T(8,128)(2,1)S(1)} %pack_rest.1.refs_3_), channel_id=1, source_target_pairs={{0,8},{4,20},{8,0},{12,28},{16,24},{20,4},{24,16},{28,12},{1,9},{5... | collective-permute-start | bytes 1179656 | tf_op jit(solution)/shard_map/ppermute | solution.py:626
  20.7 1.8 %collective-permute-start.12 = (bf16[208,576]{1,0:T(8,128)(2,1)S(1)}, bf16[208,576]{1,0:T(8,128)(2,1)S(1)}, u32[]{:S(2)}, u32[]{:S(2)}) collective-permute-start(bf16[208,576]{1,0:T(8,128)(2,1)S(1)} %collective-permute-done.4.refs_1_), channel_id=1, source_target_pairs={{0,4},{4,0},{1,5},{5,1},{2,6},{6,2},{3,7},{7,3},{8,12},{12,8},{9,1... | collective-permute-start | bytes 718856 | tf_op jit(solution)/shard_map/ppermute | solution.py:616
  20.7 1.7 %collective-permute-start.13 = (bf16[112,576]{1,0:T(8,128)(2,1)S(1)}, bf16[112,576]{1,0:T(8,128)(2,1)S(1)}, u32[]{:S(2)}, u32[]{:S(2)}) collective-permute-start(bf16[112,576]{1,0:T(8,128)(2,1)S(1)} %collective-permute-done.5.refs_3_), channel_id=1, source_target_pairs={{0,4},{4,0},{1,5},{5,1},{2,6},{6,2},{3,7},{7,3},{8,12},{12,8},{9,1... | collective-permute-start | bytes 387080 | tf_op jit(solution)/shard_map/ppermute | solution.py:616
  23.7 6.3 %collective-permute-start.14 = (bf16[312,128]{1,0:T(8,128)(2,1)S(1)}, bf16[312,128]{1,0:T(8,128)(2,1)S(1)}, u32[]{:S(2)}, u32[]{:S(2)}) collective-permute-start(bf16[312,128]{1,0:T(8,128)(2,1)S(1)} %get-tuple-element.153.first.refs_10_), channel_id=1, source_target_pairs={{0,3},{1,2},{2,1},{3,0},{4,7},{5,6},{6,5},{7,4},{8,11},{9,10},{10,... | collective-permute-start | bytes 239624 | tf_op jit(solution)/shard_map/ppermute | solution.py:619
  25.5 6.3 %collective-permute-start.16 = (bf16[96,1280]{1,0:T(8,128)(2,1)S(1)}, bf16[96,1280]{1,0:T(8,128)(2,1)S(1)}, u32[]{:S(2)}, u32[]{:S(2)}) collective-permute-start(bf16[96,1280]{1,0:T(8,128)(2,1)S(1)} %cut.2), channel_id=1, source_target_pairs={{0,16},{4,12},{8,24},{12,4},{16,0},{20,28},{24,8},{28,20},{1,17},{... | collective-permute-start | bytes 737288 | tf_op jit(solution)/shard_map/ppermute | solution.py:626
  26.4 9.8 %collective-permute-start.1 = (bf16[192,1280]{1,0:T(8,128)(2,1)S(1)}, bf16[192,1280]{1,0:T(8,128)(2,1)S(1)}, u32[]{:S(2)}, u32[]{:S(2)}) collective-permute-start(bf16[192,1280]{1,0:T(8,128)(2,1)S(1)} %collective-permute-done.value.refs_1_), channel_id=1, source_target_pairs={{0,4},{4,0},{1,5},{5,1},{2,6},{6,2},{3,7},{7,3},{8,12},{12,8},{9,1... | collective-permute-start | bytes 1474568 | tf_op jit(solution)/shard_map/ppermute | solution.py:616
  27.9 7.7 %collective-permute-start.17 = (bf16[96,1024]{1,0:T(8,128)(2,1)S(1)}, bf16[96,1024]{1,0:T(8,128)(2,1)S(1)}, u32[]{:S(2)}, u32[]{:S(2)}) collective-permute-start(bf16[96,1024]{1,0:T(8,128)(2,1)S(1)} %cut.3), channel_id=1, source_target_pairs={{0,16},{4,12},{8,24},{12,4},{16,0},{20,28},{24,8},{28,20},{1,17},{... | collective-permute-start | bytes 589832 | tf_op jit(solution)/shard_map/ppermute | solution.py:626
  30.0 5.6 %collective-permute-start.15 = (bf16[2,328,128]{2,1,0:T(8,128)(2,1)S(1)}, bf16[2,328,128]{2,1,0:T(8,128)(2,1)S(1)}, u32[]{:S(2)}, u32[]{:S(2)}) collective-permute-start(bf16[2,328,128]{2,1,0:T(8,128)(2,1)S(1)} %pair.1), channel_id=1, source_target_pairs={{0,1},{1,0},{2,3},{3,2},{4,5},{5,4},{6,7},{7,6},{8,9},{9,8},{10,11... | collective-permute-start | bytes 503816 | tf_op jit(solution)/shard_map/ppermute | solution.py:619
  30.1 6.0 %collective-permute-start.11 = (bf16[192,1024]{1,0:T(8,128)(2,1)S(1)}, bf16[192,1024]{1,0:T(8,128)(2,1)S(1)}, u32[]{:S(2)}, u32[]{:S(2)}) collective-permute-start(bf16[192,1024]{1,0:T(8,128)(2,1)S(1)} %collective-permute-done.10.value.refs_4_), channel_id=1, source_target_pairs={{0,4},{4,0},{1,5},{5,1},{2,6},{6,2},{3,7},{7,3},{8,12},{12,8},{9,1... | collective-permute-start | bytes 1179656 | tf_op jit(solution)/shard_map/ppermute | solution.py:616
  35.6 1.8 %collective-permute-start.18 = (bf16[96,1280]{1,0:T(8,128)(2,1)S(1)}, bf16[96,1280]{1,0:T(8,128)(2,1)S(1)}, u32[]{:S(2)}, u32[]{:S(2)}) collective-permute-start(bf16[96,1280]{1,0:T(8,128)(2,1)S(1)} %collective-permute-done.16.refs_6_), channel_id=1, source_target_pairs={{0,4},{4,0},{1,5},{5,1},{2,6},{6,2},{3,7},{7,3},{8,12},{12,8},{9,1... | collective-permute-start | bytes 737288 | tf_op jit(solution)/shard_map/ppermute | solution.py:616
  35.6 1.8 %collective-permute-start.19 = (bf16[96,1024]{1,0:T(8,128)(2,1)S(1)}, bf16[96,1024]{1,0:T(8,128)(2,1)S(1)}, u32[]{:S(2)}, u32[]{:S(2)}) collective-permute-start(bf16[96,1024]{1,0:T(8,128)(2,1)S(1)} %collective-permute-done.17.refs_8_), channel_id=1, source_target_pairs={{0,4},{4,0},{1,5},{5,1},{2,6},{6,2},{3,7},{7,3},{8,12},{12,8},{9,1... | collective-permute-start | bytes 589832 | tf_op jit(solution)/shard_map/ppermute | solution.py:616
  40.5 5.6 %collective-permute-start.24 = (bf16[5,208,768]{2,1,0:T(8,128)(2,1)S(1)}, bf16[5,208,768]{2,1,0:T(8,128)(2,1)S(1)}, u32[]{:S(2)}, u32[]{:S(2)}) collective-permute-start(bf16[5,208,768]{2,1,0:T(8,128)(2,1)S(1)} %get-tuple-element.160.acts), channel_id=1, source_target_pairs={{0,4},{4,0},{1,5},{5,1},{2,6},{6,2},{3,7},{7,3},{8,12},{12,8},{9,1... | collective-permute-start | bytes 4792328 | tf_op jit(solution)/shard_map/ppermute | solution.py:616
  41.3 11.6 %collective-permute-start.23 = (bf16[98,768]{1,0:T(8,128)(2,1)S(1)}, bf16[98,768]{1,0:T(8,128)(2,1)S(1)}, u32[]{:S(2)}, u32[]{:S(2)}) collective-permute-start(bf16[98,768]{1,0:T(8,128)(2,1)S(1)} %get-tuple-element.166), channel_id=1, source_target_pairs={{0,1},{1,0},{2,3},{3,2},{4,5},{5,4},{6,7},{7,6},{8,9},{9,8},{10,11... | collective-permute-start | bytes 451592 | tf_op jit(solution)/shard_map/ppermute | solution.py:619
  41.7 8.5 %collective-permute-start.20 = (bf16[312,128]{1,0:T(8,128)(2,1)S(1)}, bf16[312,128]{1,0:T(8,128)(2,1)S(1)}, u32[]{:S(2)}, u32[]{:S(2)}) collective-permute-start(bf16[312,128]{1,0:T(8,128)(2,1)S(1)} %get-tuple-element.163), channel_id=1, source_target_pairs={{0,3},{1,2},{2,1},{3,0},{4,7},{5,6},{6,5},{7,4},{8,11},{9,10},{10,... | collective-permute-start | bytes 239624 | tf_op jit(solution)/shard_map/ppermute | solution.py:619
  43.4 9.2 %collective-permute-start.21 = (bf16[312,128]{1,0:T(8,128)(2,1)S(1)}, bf16[312,128]{1,0:T(8,128)(2,1)S(1)}, u32[]{:S(2)}, u32[]{:S(2)}) collective-permute-start(bf16[312,128]{1,0:T(8,128)(2,1)S(1)} %get-tuple-element.164), channel_id=1, source_target_pairs={{0,2},{1,3},{2,0},{3,1},{4,6},{5,7},{6,4},{7,5},{8,10},{9,11},{10,... | collective-permute-start | bytes 239624 | tf_op jit(solution)/shard_map/ppermute | solution.py:619
  44.9 8.0 %collective-permute-start.22 = (bf16[312,128]{1,0:T(8,128)(2,1)S(1)}, bf16[312,128]{1,0:T(8,128)(2,1)S(1)}, u32[]{:S(2)}, u32[]{:S(2)}) collective-permute-start(bf16[312,128]{1,0:T(8,128)(2,1)S(1)} %get-tuple-element.165), channel_id=1, source_target_pairs={{0,1},{1,0},{2,3},{3,2},{4,5},{5,4},{6,7},{7,6},{8,9},{9,8},{10,11... | collective-permute-start | bytes 239624 | tf_op jit(solution)/shard_map/ppermute | solution.py:619
  47.8 23.7 %collective-permute-start.35 = (bf16[2,96,1536]{2,1,0:T(8,128)(2,1)S(1)}, bf16[2,96,1536]{2,1,0:T(8,128)(2,1)S(1)}, u32[]{:S(2)}, u32[]{:S(2)}) collective-permute-start(bf16[2,96,1536]{2,1,0:T(8,128)(2,1)S(1)} %get-tuple-element.209), channel_id=1, source_target_pairs={{0,8},{4,20},{8,0},{12,28},{16,24},{20,4},{24,16},{28,12},{1,9},{5... | collective-permute-start | bytes 1769480 | tf_op jit(solution)/shard_map/ppermute | solution.py:626
  55.0 3.9 %collective-permute-start.29 = (bf16[208,576]{1,0:T(8,128)(2,1)S(1)}, bf16[208,576]{1,0:T(8,128)(2,1)S(1)}, u32[]{:S(2)}, u32[]{:S(2)}) collective-permute-start(bf16[208,576]{1,0:T(8,128)(2,1)S(1)} %get-tuple-element.186.grads), channel_id=1, source_target_pairs={{0,4},{4,0},{1,5},{5,1},{2,6},{6,2},{3,7},{7,3},{8,12},{12,8},{9,1... | collective-permute-start | bytes 718856 | tf_op jit(solution)/shard_map/ppermute | solution.py:616
  55.0 7.6 %collective-permute-start.27 = (bf16[96,768]{1,0:T(8,128)(2,1)S(1)}, bf16[96,768]{1,0:T(8,128)(2,1)S(1)}, u32[]{:S(2)}, u32[]{:S(2)}) collective-permute-start(bf16[96,768]{1,0:T(8,128)(2,1)S(1)} %get-tuple-element.184), channel_id=1, source_target_pairs={{0,24},{8,16},{16,8},{24,0},{1,25},{9,17},{17,9},{25,1},{2,26},{10... | collective-permute-start | bytes 442376 | tf_op jit(solution)/shard_map/ppermute | solution.py:793
  56.5 10.7 %collective-permute-start.25 = (bf16[104,768]{1,0:T(8,128)(2,1)S(1)}, bf16[104,768]{1,0:T(8,128)(2,1)S(1)}, u32[]{:S(2)}, u32[]{:S(2)}) collective-permute-start(bf16[104,768]{1,0:T(8,128)(2,1)S(1)} %get-tuple-element.183), channel_id=1, source_target_pairs={{0,1},{1,0},{2,3},{3,2},{4,5},{5,4},{6,7},{7,6},{8,9},{9,8},{10,11... | collective-permute-start | bytes 479240 | tf_op jit(solution)/shard_map/ppermute | solution.py:619
  56.8 10.3 %collective-permute-start.26 = (bf16[98,768]{1,0:T(8,128)(2,1)S(1)}, bf16[98,768]{1,0:T(8,128)(2,1)S(1)}, u32[]{:S(2)}, u32[]{:S(2)}) collective-permute-start(bf16[98,768]{1,0:T(8,128)(2,1)S(1)} %out_pair.1.own), channel_id=1, source_target_pairs={{0,2},{1,3},{2,0},{3,1},{4,6},{5,7},{6,4},{7,5},{8,10},{9,11},{10,... | collective-permute-start | bytes 451592 | tf_op jit(solution)/shard_map/ppermute | solution.py:619
  58.8 6.7 %collective-permute-start.28 = (bf16[96,768]{1,0:T(8,128)(2,1)S(1)}, bf16[96,768]{1,0:T(8,128)(2,1)S(1)}, u32[]{:S(2)}, u32[]{:S(2)}) collective-permute-start(bf16[96,768]{1,0:T(8,128)(2,1)S(1)} %get-tuple-element.185), channel_id=1, source_target_pairs={{0,8},{8,0},{16,24},{24,16},{1,9},{9,1},{17,25},{25,17},{2,10},{10... | collective-permute-start | bytes 442376 | tf_op jit(solution)/shard_map/ppermute | solution.py:793
  62.6 5.1 %collective-permute-start.30 = (bf16[96,768]{1,0:T(8,128)(2,1)S(1)}, bf16[96,768]{1,0:T(8,128)(2,1)S(1)}, u32[]{:S(2)}, u32[]{:S(2)}) collective-permute-start(bf16[96,768]{1,0:T(8,128)(2,1)S(1)} %get-tuple-element.188), channel_id=1, source_target_pairs={{0,16},{8,24},{16,0},{24,8},{1,17},{9,25},{17,1},{25,9},{2,18},{10... | collective-permute-start | bytes 442376 | tf_op jit(solution)/shard_map/ppermute | solution.py:813
  68.0 11.9 %collective-permute-start.31 = (bf16[152,768]{1,0:T(8,128)(2,1)S(1)}, bf16[152,768]{1,0:T(8,128)(2,1)S(1)}, u32[]{:S(2)}, u32[]{:S(2)}) collective-permute-start(bf16[152,768]{1,0:T(8,128)(2,1)S(1)} %get-tuple-element.200.own), channel_id=1, source_target_pairs={{0,2},{1,3},{2,0},{3,1},{4,6},{5,7},{6,4},{7,5},{8,10},{9,11},{10,... | collective-permute-start | bytes 700424 | tf_op jit(solution)/shard_map/ppermute | solution.py:619
  68.5 8.9 %collective-permute-start.33 = (bf16[2,96,576]{2,1,0:T(8,128)(2,1)S(1)}, bf16[2,96,576]{2,1,0:T(8,128)(2,1)S(1)}, u32[]{:S(2)}, u32[]{:S(2)}) collective-permute-start(bf16[2,96,576]{2,1,0:T(8,128)(2,1)S(1)} %get-tuple-element.202), channel_id=1, source_target_pairs={{0,8},{4,20},{8,0},{12,28},{16,24},{20,4},{24,16},{28,12},{1,9},{5... | collective-permute-start | bytes 663560 | tf_op jit(solution)/shard_map/ppermute | solution.py:626
  70.4 6.5 %collective-permute-start.32 = (bf16[98,768]{1,0:T(8,128)(2,1)S(1)}, bf16[98,768]{1,0:T(8,128)(2,1)S(1)}, u32[]{:S(2)}, u32[]{:S(2)}) collective-permute-start(bf16[98,768]{1,0:T(8,128)(2,1)S(1)} %out_total.1.out_own), channel_id=1, source_target_pairs={{0,1},{1,0},{2,3},{3,2},{4,5},{5,4},{6,7},{7,6},{8,9},{9,8},{10,11... | collective-permute-start | bytes 451592 | tf_op jit(solution)/shard_map/ppermute | solution.py:619
  71.5 15.5 %collective-permute-start.36 = (bf16[96,1536]{1,0:T(8,128)(2,1)S(1)}, bf16[96,1536]{1,0:T(8,128)(2,1)S(1)}, u32[]{:S(2)}, u32[]{:S(2)}) collective-permute-start(bf16[96,1536]{1,0:T(8,128)(2,1)S(1)} %get-tuple-element.210), channel_id=1, source_target_pairs={{0,16},{4,12},{8,24},{12,4},{16,0},{20,28},{24,8},{28,20},{1,17},{... | collective-permute-start | bytes 884744 | tf_op jit(solution)/shard_map/ppermute | solution.py:626
  80.0 7.1 %collective-permute-start.34 = (bf16[128,768]{1,0:T(8,128)(2,1)S(1)}, bf16[128,768]{1,0:T(8,128)(2,1)S(1)}, u32[]{:S(2)}, u32[]{:S(2)}) collective-permute-start(bf16[128,768]{1,0:T(8,128)(2,1)S(1)} %get-tuple-element.207.in_own), channel_id=1, source_target_pairs={{0,1},{1,0},{2,3},{3,2},{4,5},{5,4},{6,7},{7,6},{8,9},{9,8},{10,11... | collective-permute-start | bytes 589832 | tf_op jit(solution)/shard_map/ppermute | solution.py:619
  80.3 6.8 %collective-permute-start.37 = (bf16[112,576]{1,0:T(8,128)(2,1)S(1)}, bf16[112,576]{1,0:T(8,128)(2,1)S(1)}, u32[]{:S(2)}, u32[]{:S(2)}) collective-permute-start(bf16[112,576]{1,0:T(8,128)(2,1)S(1)} %get-tuple-element.215), channel_id=1, source_target_pairs={{0,16},{4,12},{8,24},{12,4},{16,0},{20,28},{24,8},{28,20},{1,17},{... | collective-permute-start | bytes 387080 | tf_op jit(solution)/shard_map/ppermute | solution.py:626
  81.7 3.8 %collective-permute-start.38 = (bf16[16,576]{1,0:T(8,128)(2,1)S(1)}, bf16[16,576]{1,0:T(8,128)(2,1)S(1)}, u32[]{:S(2)}, u32[]{:S(2)}) collective-permute-start(bf16[16,576]{1,0:T(8,128)(2,1)S(1)} %get-tuple-element.216), channel_id=1, source_target_pairs={{0,8},{4,20},{8,0},{12,28},{16,24},{20,4},{24,16},{28,12},{1,9},{5... | collective-permute-start | bytes 55304 | tf_op jit(solution)/shard_map/ppermute | solution.py:626
  82.4 4.7 %collective-permute-start.39 = (bf16[16,576]{1,0:T(8,128)(2,1)S(1)}, bf16[16,576]{1,0:T(8,128)(2,1)S(1)}, u32[]{:S(2)}, u32[]{:S(2)}) collective-permute-start(bf16[16,576]{1,0:T(8,128)(2,1)S(1)} %get-tuple-element.217), channel_id=1, source_target_pairs={{0,24},{8,16},{16,8},{24,0},{1,25},{9,17},{17,9},{25,1},{2,26},{10... | collective-permute-start | bytes 55304 | tf_op jit(solution)/shard_map/ppermute | solution.py:622
  87.2 2.4 %collective-permute-start.40 = (bf16[232,768]{1,0:T(8,128)(2,1)S(1)}, bf16[232,768]{1,0:T(8,128)(2,1)S(1)}, u32[]{:S(2)}, u32[]{:S(2)}) collective-permute-start(bf16[232,768]{1,0:T(8,128)(2,1)S(1)} %get-tuple-element.221), channel_id=1, source_target_pairs={{0,4},{4,0},{1,5},{5,1},{2,6},{6,2},{3,7},{7,3},{8,12},{12,8},{9,1... | collective-permute-start | bytes 1069064 | tf_op jit(solution)/shard_map/ppermute | solution.py:616
  87.5 2.1 %collective-permute-start.41 = (bf16[96,1536]{1,0:T(8,128)(2,1)S(1)}, bf16[96,1536]{1,0:T(8,128)(2,1)S(1)}, u32[]{:S(2)}, u32[]{:S(2)}) collective-permute-start(bf16[96,1536]{1,0:T(8,128)(2,1)S(1)} %get-tuple-element.231), channel_id=1, source_target_pairs={{0,4},{4,0},{1,5},{5,1},{2,6},{6,2},{3,7},{7,3},{8,12},{12,8},{9,1... | collective-permute-start | bytes 884744 | tf_op jit(solution)/shard_map/ppermute | solution.py:616
  88.0 1.6 %collective-permute-start.42 = (bf16[112,576]{1,0:T(8,128)(2,1)S(1)}, bf16[112,576]{1,0:T(8,128)(2,1)S(1)}, u32[]{:S(2)}, u32[]{:S(2)}) collective-permute-start(bf16[112,576]{1,0:T(8,128)(2,1)S(1)} %get-tuple-element.233), channel_id=1, source_target_pairs={{0,4},{4,0},{1,5},{5,1},{2,6},{6,2},{3,7},{7,3},{8,12},{12,8},{9,1... | collective-permute-start | bytes 387080 | tf_op jit(solution)/shard_map/ppermute | solution.py:616

commit v11 on v10

--- a/solution.py
+++ b/solution.py
@@ -645,15 +645,15 @@
         vectors = [norm1_gain, norm1_bias, proj_bias, norm2_gain, norm2_bias, fc2_bias]
 
         x_recv = other_core(x_raw)
-        cot_recv = other_core(cot_raw)
-        def frames(x_recv, cot_recv):
+        cot_recv = None if z.direct else other_core(cot_raw)
+        def frames(x_recv, cot_mine, cot_recv):
             stream, normal_one, inverse_one, normal_their = call(
                 part(frame_kernel, z),
                 [shape((rows, width), LOW), shape((rows, width), F32), shape((rows, 128), F32), shape((rows, width), F32)],
                 [x_raw, x_recv],
                 name="frame",
             )
-            (cot,) = call(part(cot_kernel, z), [shape((2, rows, width), LOW)], [cot_raw, cot_recv], name="cotangent")
+            (cot,) = call(part(cot_kernel, z), [shape((2, rows, width), LOW)], [cot_mine, cot_recv], name="cotangent")
             return stream, normal_one, inverse_one, normal_their, cot
 
         if z.direct:
@@ -672,7 +672,8 @@
                 mib=56,
                 in_specs=[ANY] * len(sources),
             )
-            near, far, proj_t, proj_half, x_recv, cot_recv = tie((near, far, proj_t, proj_half, x_recv, cot_recv))
+            near, far, proj_t, proj_half, x_recv, cot_raw = tie((near, far, proj_t, proj_half, x_recv, cot_raw))
+            cot_recv = other_core(cot_raw)
             got = [to_near(near), to_far(far)]
             proj_got = [proj_near(proj_t), to_tp(proj_half, 2)]
             feed_own, feed_rest = call(
@@ -684,7 +685,7 @@
                 mib=20,
                 in_specs=[ANY] * 2,
             )
-            stream, normal_one, inverse_one, normal_their, cot = frames(x_recv, cot_recv)
+            stream, normal_one, inverse_one, normal_their, cot = frames(x_recv, cot_raw, cot_recv)
             feed_in = to_near(feed_own)
             got, proj_got, feed_rest, stream, normal_one, inverse_one, normal_their, cot = tie(
                 (got, proj_got, feed_rest, stream, normal_one, inverse_one, normal_their, cot)
@@ -704,7 +705,7 @@
                 (half,) = call(part(cut_kernel, z), [shape((chunk, value.shape[1]), LOW)], [value], name="cut")
                 far_in.append(to_cross(half))
         else:
-            stream, normal_one, inverse_one, normal_their, cot = frames(x_recv, cot_recv)
+            stream, normal_one, inverse_one, normal_their, cot = frames(x_recv, cot_raw, cot_recv)
             whole = lax.all_gather(qkv3, "fsdp", axis=1, tiled=True)
             whole = whole.transpose(1, 0, 2).reshape(4, z.part, 3 * inner)
             vec = jnp.stack(vectors + [vectors[0]] * 2).astype(F32)

time: 92 us -> 92 us (level)
  no operation moved by 1% of the time
where the time goes in v11:
time: 92 us; the launch traced here: 91.8 us
  starting transfers between devices  38 us (41%)
  waiting for transfers between devices  32.2 us (35%)
  Pallas kernels  17.6 us (19%)
  local copies, waits for them, and re-layouts  2.9 us (3%)
  between operations  1.1 us (1%)
    pallas_call x27, Pallas kernels, call(): pl.pallas_call(kernel, out_shape=tuple(outs), in_specs=in_specs or [VMEM]...  17.6 us
    ppermute x12, waiting for transfers between devices, to_tp(): return lax.ppermute(value, 'tp', [(i, i ^ k) for i in range(nt)])  16.9 us
    ppermute x12, starting transfers between devices, to_tp(): return lax.ppermute(value, 'tp', [(i, i ^ k) for i in range(nt)])  12.9 us
    ppermute x10, starting transfers between devices, neighbours(): return lax.ppermute(value, ('fsdp', 'ctx'), pairs)  12.8 us
    ppermute x10, waiting for transfers between devices, neighbours(): return lax.ppermute(value, ('fsdp', 'ctx'), pairs)  5.1 us
    ppermute x15, waiting for transfers between devices, other_core(): return lax.ppermute(value, 'ctx', [(0, 1), (1, 0)])  4.97 us
    ppermute x15, starting transfers between devices, other_core(): return lax.ppermute(value, 'ctx', [(0, 1), (1, 0)])  3.3 us
    ppermute x2, waiting for transfers between devices, local(): lax.ppermute(sends[k - 1], 'fsdp', [(i, i ^ k) for i in range(nf)])  3.07 us
  transfers between devices with their start and end apart: 43, of which 19 were waited for; matrix products, arithmetic and copies ran while one was open for 0% of the time, Pallas kernels for 13%

profile of v11, /device:TPU:0, one launch (start us, length us, event | category | flops | bytes accessed | tf_op | source)
XLA Modules:
  0.0 91.8 jit_solution(5331567922171427712)
XLA Ops:
  0.7 0.5 collective-permute-start.2
  1.2 2.0 %pack.1 = (bf16[208,576]{1,0:T(8,128)(2,1)}, bf16[112,576]{1,0:T(8,128)(2,1)}, bf16[296,192]{1,0:T(8,128)(2,1)}, bf16[96,192]{1,0:T(8,128)(2,1)}) custom-call(bf16[3,192,192]{2,1,0:T(8,128)(2,1)} %bitcast.15, bf16[192,192]{1,0:T(8,128)(2,1)} %refs_1_.1, bf16[12,16]{1,0:T(8,128)(2,1)} %refs_2_.1, bf16[3,2,16]{2,1,0:T(2,128)(2,1)} %bitcast.16, ...), custom_call_target="tpu_custom_call" | custom-call | tf_op jit(solution)/shard_map/pack/pallas_call | solution.py:34
  3.3 2.9 %collective-permute-start.3 = (bf16[208,576]{1,0:T(8,128)(2,1)}, bf16[208,576]{1,0:T(8,128)(2,1)S(1)}, u32[]{:S(2)}, u32[]{:S(2)}) collective-permute-start(bf16[208,576]{1,0:T(8,128)(2,1)} %get-tuple-element.136.refs_0_), channel_id=1, source_target_pairs={{0,8},{4,20},{8,0},{12,28},{16,24},{20,4},{24,16},{28,12},{1,9},{5... | collective-permute-start | bytes 718856 | tf_op jit(solution)/shard_map/ppermute | solution.py:626
  6.3 1.5 %collective-permute-start.4 = (bf16[112,576]{1,0:T(8,128)(2,1)}, bf16[112,576]{1,0:T(8,128)(2,1)S(1)}, u32[]{:S(2)}, u32[]{:S(2)}) collective-permute-start(bf16[112,576]{1,0:T(8,128)(2,1)} %get-tuple-element.137), channel_id=1, source_target_pairs={{0,24},{8,16},{16,8},{24,0},{1,25},{9,17},{17,9},{25,1},{2,26},{10... | collective-permute-start | bytes 387080 | tf_op jit(solution)/shard_map/ppermute | solution.py:622
  7.8 1.6 %collective-permute-start.5 = (bf16[296,192]{1,0:T(8,128)(2,1)}, bf16[296,192]{1,0:T(8,128)(2,1)S(1)}, u32[]{:S(2)}, u32[]{:S(2)}) collective-permute-start(bf16[296,192]{1,0:T(8,128)(2,1)} %get-tuple-element.138.proj_t), channel_id=1, source_target_pairs={{0,1},{4,7},{1,0},{5,6},{2,3},{6,5},{3,2},{7,4},{8,9},{12,15},{9,8... | collective-permute-start | bytes 341000 | tf_op jit(solution)/shard_map/ppermute | solution.py:636
  9.3 2.6 %collective-permute-start.6 = (bf16[96,192]{1,0:T(8,128)(2,1)}, bf16[96,192]{1,0:T(8,128)(2,1)S(1)}, u32[]{:S(2)}, u32[]{:S(2)}) collective-permute-start(bf16[96,192]{1,0:T(8,128)(2,1)} %get-tuple-element.139), channel_id=1, source_target_pairs={{0,2},{1,3},{2,0},{3,1},{4,6},{5,7},{6,4},{7,5},{8,10},{9,11},{10,... | collective-permute-start | bytes 110600 | tf_op jit(solution)/shard_map/ppermute | solution.py:619
  11.9 1.0 %copy-done.2 = bf16[192,768]{1,0:T(8,128)(2,1)S(1)} copy-done((bf16[192,768]{1,0:T(8,128)(2,1)S(1)}, bf16[192,768]{1,0:T(8,128)(2,1)}, u32[]{:S(2)}) %copy-start.2) | copy-done | bytes 294936
  12.9 1.0 %copy-done.3 = bf16[768,192]{0,1:T(8,128)(2,1)S(1)} copy-done((bf16[768,192]{0,1:T(8,128)(2,1)S(1)}, bf16[768,192]{0,1:T(8,128)(2,1)}, u32[]{:S(2)}) %copy-start.3) | copy-done | bytes 294936
  14.0 1.6 %collective-permute-start = (bf16[192,1280]{1,0:T(8,128)(2,1)S(1)}, bf16[192,1280]{1,0:T(8,128)(2,1)S(1)}, u32[]{:S(2)}, u32[]{:S(2)}) collective-permute-start(bf16[192,1280]{1,0:T(8,128)(2,1)S(1)} %get-tuple-element.131.refs_0_), channel_id=1, source_target_pairs={{0,8},{4,20},{8,0},{12,28},{16,24},{20,4},{24,16},{28,12},{1,9},{5... | collective-permute-start | bytes 1474568 | tf_op jit(solution)/shard_map/ppermute | solution.py:626
  15.6 1.0 %copy-done = bf16[2,98,768]{2,0,1:T(2,128)(2,1)S(1)} copy-done((bf16[2,98,768]{2,0,1:T(2,128)(2,1)S(1)}, bf16[2,98,768]{2,0,1:T(2,128)(2,1)}, u32[]{:S(2)}) %copy-start) | copy-done | bytes 301080
  16.6 1.0 %frame.1 = (bf16[208,768]{1,0:T(8,128)(2,1)S(1)}, f32[208,768]{1,0:T(8,128)S(1)}, f32[208,128]{1,0:T(8,128)S(1)}, f32[208,768]{1,0:T(8,128)S(1)}) custom-call(bf16[98,2,768]{2,1,0:T(2,128)(2,1)S(1)} %bitcast.11, bf16[98,2,768]{2,1,0:T(2,128)(2,1)S(1)} %collective-permute-done.2.received), custom_call_target="tpu_custom_call" | custom-call | tf_op jit(solution)/shard_map/frame/pallas_call | solution.py:34
  17.6 0.7 cotangent.1.refs_14_.cot
  18.4 0.5 collective-permute-start.9
  18.9 0.9 %collective-permute-done.9.far_their = bf16[96,192]{1,0:T(8,128)(2,1)S(1)} collective-permute-done((bf16[96,192]{1,0:T(8,128)(2,1)S(1)}, bf16[96,192]{1,0:T(8,128)(2,1)S(1)}, u32[]{:S(2)}, u32[]{:S(2)}) %collective-permute-start.9) | collective-permute-done | bytes 36896 | tf_op jit(solution)/shard_map/ppermute | solution.py:616
  20.1 0.6 collective-permute-start.10
  20.7 0.5 collective-permute-start.13
  21.2 1.2 %collective-permute-done.13.refs_4_ = bf16[112,576]{1,0:T(8,128)(2,1)S(1)} collective-permute-done((bf16[112,576]{1,0:T(8,128)(2,1)S(1)}, bf16[112,576]{1,0:T(8,128)(2,1)S(1)}, u32[]{:S(2)}, u32[]{:S(2)}) %collective-permute-start.13) | collective-permute-done | bytes 129056 | tf_op jit(solution)/shard_map/ppermute | solution.py:616
  22.4 1.3 %attend.1 = (f32[8,768]{1,0:T(8,128)S(1)}, bf16[4,192,576]{2,1,0:T(8,128)(2,1)S(1)}, bf16[208,768]{1,0:T(8,128)(2,1)S(1)}, bf16[3,208,192]{2,1,0:T(8,128)(2,1)S(...) custom-call(bf16[208,576]{1,0:T(8,128)(2,1)S(1)} %copy-done.4, ...), custom_call_target="tpu_custom_call" | custom-call | tf_op jit(solution)/shard_map/attend/pallas_call | solution.py:34
  23.7 1.7 %collective-permute-start.14 = (bf16[312,128]{1,0:T(8,128)(2,1)S(1)}, bf16[312,128]{1,0:T(8,128)(2,1)S(1)}, u32[]{:S(2)}, u32[]{:S(2)}) collective-permute-start(bf16[312,128]{1,0:T(8,128)(2,1)S(1)} %get-tuple-element.153.first.refs_10_), channel_id=1, source_target_pairs={{0,3},{1,2},{2,1},{3,0},{4,7},{5,6},{6,5},{7,4},{8,11},{9,10},{10,... | collective-permute-start | bytes 239624 | tf_op jit(solution)/shard_map/ppermute | solution.py:619
  25.5 0.9 collective-permute-start.16
  26.3 1.6 %collective-permute-done.10.value.refs_4_ = bf16[192,1024]{1,0:T(8,128)(2,1)S(1)} collective-permute-done((bf16[192,1024]{1,0:T(8,128)(2,1)S(1)}, bf16[192,1024]{1,0:T(8,128)(2,1)S(1)}, u32[]{:S(2)}, u32[]{:S(2)}) %collective-permute-start.10) | collective-permute-done | bytes 393248 | tf_op jit(solution)/shard_map/ppermute | solution.py:626
  27.9 0.6 collective-permute-start.17
  28.5 1.5 %collective-permute-done.14.second.refs_11_ = bf16[312,128]{1,0:T(8,128)(2,1)S(1)} collective-permute-done((bf16[312,128]{1,0:T(8,128)(2,1)S(1)}, bf16[312,128]{1,0:T(8,128)(2,1)S(1)}, u32[]{:S(2)}, u32[]{:S(2)}) %collective-permute-start.14) | collective-permute-done | bytes 79904 | tf_op jit(solution)/shard_map/ppermute | solution.py:619
  30.2 1.5 %collective-permute-done.16.refs_6_ = bf16[96,1280]{1,0:T(8,128)(2,1)S(1)} collective-permute-done((bf16[96,1280]{1,0:T(8,128)(2,1)S(1)}, bf16[96,1280]{1,0:T(8,128)(2,1)S(1)}, u32[]{:S(2)}, u32[]{:S(2)}) %collective-permute-start.16) | collective-permute-done | bytes 245792 | tf_op jit(solution)/shard_map/ppermute | solution.py:626
  31.7 3.9 %collective-permute-done.15.refs_12_ = bf16[2,328,128]{2,1,0:T(8,128)(2,1)S(1)} collective-permute-done((bf16[2,328,128]{2,1,0:T(8,128)(2,1)S(1)}, bf16[2,328,128]{2,1,0:T(8,128)(2,1)S(1)}, u32[]{:S(2)}, u32[]{:S(2)}) %collective-permute-start.15) | collective-permute-done | bytes 167968 | tf_op jit(solution)/shard_map/ppermute | solution.py:619
  35.6 0.5 collective-permute-start.19
  36.1 1.3 %collective-permute-done.19.refs_9_ = bf16[96,1024]{1,0:T(8,128)(2,1)S(1)} collective-permute-done((bf16[96,1024]{1,0:T(8,128)(2,1)S(1)}, bf16[96,1024]{1,0:T(8,128)(2,1)S(1)}, u32[]{:S(2)}, u32[]{:S(2)}) %collective-permute-start.19) | collective-permute-done | bytes 196640 | tf_op jit(solution)/shard_map/ppermute | solution.py:616
  37.4 3.1 %feed.1 = (bf16[4,192,2304]{2,1,0:T(8,128)(2,1)S(1)}, f32[208,768]{1,0:T(8,128)S(1)}, bf16[5,208,768]{2,1,0:T(8,128)(2,1)S(1)}, f32[208,768]{1,0:T(8,128)S(1)}, ...) custom-call(bf16[192,1280]{1,0:T(8,128)(2,1)S(1)} %get-tuple-element, ...), custom_call_target="tpu_custom_call" | custom-call | tf_op jit(solution)/shard_map/feed/pallas_call | solution.py:34
  40.7 0.6 down.1
  41.3 0.4 collective-permute-start.23
  41.7 1.7 %collective-permute-start.20 = (bf16[312,128]{1,0:T(8,128)(2,1)S(1)}, bf16[312,128]{1,0:T(8,128)(2,1)S(1)}, u32[]{:S(2)}, u32[]{:S(2)}) collective-permute-start(bf16[312,128]{1,0:T(8,128)(2,1)S(1)} %get-tuple-element.163), channel_id=1, source_target_pairs={{0,3},{1,2},{2,1},{3,0},{4,7},{5,6},{6,5},{7,4},{8,11},{9,10},{10,... | collective-permute-start | bytes 239624 | tf_op jit(solution)/shard_map/ppermute | solution.py:619
  43.4 1.5 %collective-permute-start.21 = (bf16[312,128]{1,0:T(8,128)(2,1)S(1)}, bf16[312,128]{1,0:T(8,128)(2,1)S(1)}, u32[]{:S(2)}, u32[]{:S(2)}) collective-permute-start(bf16[312,128]{1,0:T(8,128)(2,1)S(1)} %get-tuple-element.164), channel_id=1, source_target_pairs={{0,2},{1,3},{2,0},{3,1},{4,6},{5,7},{6,4},{7,5},{8,10},{9,11},{10,... | collective-permute-start | bytes 239624 | tf_op jit(solution)/shard_map/ppermute | solution.py:619
  44.9 1.2 %collective-permute-start.22 = (bf16[312,128]{1,0:T(8,128)(2,1)S(1)}, bf16[312,128]{1,0:T(8,128)(2,1)S(1)}, u32[]{:S(2)}, u32[]{:S(2)}) collective-permute-start(bf16[312,128]{1,0:T(8,128)(2,1)S(1)} %get-tuple-element.165), channel_id=1, source_target_pairs={{0,1},{1,0},{2,3},{3,2},{4,5},{5,4},{6,7},{7,6},{8,9},{9,8},{10,11... | collective-permute-start | bytes 239624 | tf_op jit(solution)/shard_map/ppermute | solution.py:619
  46.1 1.5 %feed_grad.1.keep = f32[4,96,1536]{2,1,0:T(8,128)S(1)} custom-call(bf16[5,208,768]{2,1,0:T(8,128)(2,1)S(1)} %get-tuple-element.160.acts, bf16[5,208,768]{2,1,0:T(8,128)(2,1)S(1)} %collective-permute-done.24.theirs, bf16[2,208,768]{2,1,0:T(8,128)(2,1)S(1)} %cotangent.1.refs_14_.cot), custom_call_target="tpu_custom_call" | custom-call | tf_op jit(solution)/shard_map/feed_grad/pallas_call | solution.py:34
  47.8 1.5 %collective-permute-start.35 = (bf16[2,96,1536]{2,1,0:T(8,128)(2,1)S(1)}, bf16[2,96,1536]{2,1,0:T(8,128)(2,1)S(1)}, u32[]{:S(2)}, u32[]{:S(2)}) collective-permute-start(bf16[2,96,1536]{2,1,0:T(8,128)(2,1)S(1)} %get-tuple-element.209), channel_id=1, source_target_pairs={{0,8},{4,20},{8,0},{12,28},{16,24},{20,4},{24,16},{28,12},{1,9},{5... | collective-permute-start | bytes 1769480 | tf_op jit(solution)/shard_map/ppermute | solution.py:626
  49.3 0.9 proj_grad.1
  50.2 2.3 %collective-permute-done.21.refs_2_ = bf16[312,128]{1,0:T(8,128)(2,1)S(1)} collective-permute-done((bf16[312,128]{1,0:T(8,128)(2,1)S(1)}, bf16[312,128]{1,0:T(8,128)(2,1)S(1)}, u32[]{:S(2)}, u32[]{:S(2)}) %collective-permute-start.21) | collective-permute-done | bytes 79904 | tf_op jit(solution)/shard_map/ppermute | solution.py:619
  52.5 0.4 collective-permute-done.22.refs_3_
  52.9 2.0 %back.1 = (bf16[208,576]{1,0:T(8,128)(2,1)S(1)}, f32[1,576]{1,0:T(1,128)S(1)}, f32[104,768]{1,0:T(8,128)S(1)}, bf16[104,768]{1,0:T(8,128)(2,1)S(1)}) custom-call(f32[208,192]{1,0:T(8,128)S(1)} %get-tuple-element.173.refs_0_, bf16[312,128]{1,0:T(8,128)(2,1)S(1)} %collective-permute-done.20.refs_1_, bf16[312,128]{1,0:T(8,128)(2,1)S(1)} %collective-permute-done.21.refs_2_, ...), custom_call_target="tpu_custom_call" | custom-call | tf_op jit(solution)/shard_map/back/pallas_call | solution.py:34
  55.0 1.5 %collective-permute-start.27 = (bf16[96,768]{1,0:T(8,128)(2,1)S(1)}, bf16[96,768]{1,0:T(8,128)(2,1)S(1)}, u32[]{:S(2)}, u32[]{:S(2)}) collective-permute-start(bf16[96,768]{1,0:T(8,128)(2,1)S(1)} %get-tuple-element.184), channel_id=1, source_target_pairs={{0,24},{8,16},{16,8},{24,0},{1,25},{9,17},{17,9},{25,1},{2,26},{10... | collective-permute-start | bytes 442376 | tf_op jit(solution)/shard_map/ppermute | solution.py:794
  56.5 0.3 collective-permute-start.25
  56.8 1.9 %collective-permute-start.26 = (bf16[98,768]{1,0:T(8,128)(2,1)S(1)}, bf16[98,768]{1,0:T(8,128)(2,1)S(1)}, u32[]{:S(2)}, u32[]{:S(2)}) collective-permute-start(bf16[98,768]{1,0:T(8,128)(2,1)S(1)} %out_pair.1.own), channel_id=1, source_target_pairs={{0,2},{1,3},{2,0},{3,1},{4,6},{5,7},{6,4},{7,5},{8,10},{9,11},{10,... | collective-permute-start | bytes 451592 | tf_op jit(solution)/shard_map/ppermute | solution.py:619
  58.8 1.2 %collective-permute-start.28 = (bf16[96,768]{1,0:T(8,128)(2,1)S(1)}, bf16[96,768]{1,0:T(8,128)(2,1)S(1)}, u32[]{:S(2)}, u32[]{:S(2)}) collective-permute-start(bf16[96,768]{1,0:T(8,128)(2,1)S(1)} %get-tuple-element.185), channel_id=1, source_target_pairs={{0,8},{8,0},{16,24},{24,16},{1,9},{9,1},{17,25},{25,17},{2,10},{10... | collective-permute-start | bytes 442376 | tf_op jit(solution)/shard_map/ppermute | solution.py:794
  60.0 2.6 %collective-permute-done.27.refs_0_ = bf16[96,768]{1,0:T(8,128)(2,1)S(1)} collective-permute-done((bf16[96,768]{1,0:T(8,128)(2,1)S(1)}, bf16[96,768]{1,0:T(8,128)(2,1)S(1)}, u32[]{:S(2)}, u32[]{:S(2)}) %collective-permute-start.27) | collective-permute-done | bytes 147488 | tf_op jit(solution)/shard_map/ppermute | solution.py:794
  62.6 1.6 %collective-permute-start.30 = (bf16[96,768]{1,0:T(8,128)(2,1)S(1)}, bf16[96,768]{1,0:T(8,128)(2,1)S(1)}, u32[]{:S(2)}, u32[]{:S(2)}) collective-permute-start(bf16[96,768]{1,0:T(8,128)(2,1)S(1)} %get-tuple-element.188), channel_id=1, source_target_pairs={{0,16},{8,24},{16,0},{24,8},{1,17},{9,25},{17,1},{25,9},{2,18},{10... | collective-permute-start | bytes 442376 | tf_op jit(solution)/shard_map/ppermute | solution.py:814
  64.2 0.8 qkv_grad.1.keep
  65.1 0.4 collective-permute-done.28.refs_1_
  65.5 1.7 %collective-permute-done.26.received = bf16[98,768]{1,0:T(8,128)(2,1)S(1)} collective-permute-done((bf16[98,768]{1,0:T(8,128)(2,1)S(1)}, bf16[98,768]{1,0:T(8,128)(2,1)S(1)}, u32[]{:S(2)}, u32[]{:S(2)}) %collective-permute-start.26) | collective-permute-done | bytes 150560 | tf_op jit(solution)/shard_map/ppermute | solution.py:619
  67.2 0.6 collective-permute-done.30.refs_2_
  68.0 0.4 collective-permute-start.31
  68.5 1.8 %collective-permute-start.33 = (bf16[2,96,576]{2,1,0:T(8,128)(2,1)S(1)}, bf16[2,96,576]{2,1,0:T(8,128)(2,1)S(1)}, u32[]{:S(2)}, u32[]{:S(2)}) collective-permute-start(bf16[2,96,576]{2,1,0:T(8,128)(2,1)S(1)} %get-tuple-element.202), channel_id=1, source_target_pairs={{0,8},{4,20},{8,0},{12,28},{16,24},{20,4},{24,16},{28,12},{1,9},{5... | collective-permute-start | bytes 663560 | tf_op jit(solution)/shard_map/ppermute | solution.py:626
  70.4 1.0 %collective-permute-start.32 = (bf16[98,768]{1,0:T(8,128)(2,1)S(1)}, bf16[98,768]{1,0:T(8,128)(2,1)S(1)}, u32[]{:S(2)}, u32[]{:S(2)}) collective-permute-start(bf16[98,768]{1,0:T(8,128)(2,1)S(1)} %out_total.1.out_own), channel_id=1, source_target_pairs={{0,1},{1,0},{2,3},{3,2},{4,5},{5,4},{6,7},{7,6},{8,9},{9,8},{10,11... | collective-permute-start | bytes 451592 | tf_op jit(solution)/shard_map/ppermute | solution.py:619
  71.5 0.9 %collective-permute-start.36 = (bf16[96,1536]{1,0:T(8,128)(2,1)S(1)}, bf16[96,1536]{1,0:T(8,128)(2,1)S(1)}, u32[]{:S(2)}, u32[]{:S(2)}) collective-permute-start(bf16[96,1536]{1,0:T(8,128)(2,1)S(1)} %get-tuple-element.210), channel_id=1, source_target_pairs={{0,16},{4,12},{8,24},{12,4},{16,0},{20,28},{24,8},{28,20},{1,17},{... | collective-permute-start | bytes 884744 | tf_op jit(solution)/shard_map/ppermute | solution.py:626
  72.5 4.4 %collective-permute-done.32.out_in = bf16[98,768]{1,0:T(8,128)(2,1)S(1)} collective-permute-done((bf16[98,768]{1,0:T(8,128)(2,1)S(1)}, bf16[98,768]{1,0:T(8,128)(2,1)S(1)}, u32[]{:S(2)}, u32[]{:S(2)}) %collective-permute-start.32) | collective-permute-done | bytes 150560 | tf_op jit(solution)/shard_map/ppermute | solution.py:619
  76.9 0.5 collective-permute-done.33.received
  77.4 2.7 %collective-permute-done.31.received = bf16[152,768]{1,0:T(8,128)(2,1)S(1)} collective-permute-done((bf16[152,768]{1,0:T(8,128)(2,1)S(1)}, bf16[152,768]{1,0:T(8,128)(2,1)S(1)}, u32[]{:S(2)}, u32[]{:S(2)}) %collective-permute-start.31) | collective-permute-done | bytes 233504 | tf_op jit(solution)/shard_map/ppermute | solution.py:619
  80.4 1.3 %collective-permute-start.37 = (bf16[112,576]{1,0:T(8,128)(2,1)S(1)}, bf16[112,576]{1,0:T(8,128)(2,1)S(1)}, u32[]{:S(2)}, u32[]{:S(2)}) collective-permute-start(bf16[112,576]{1,0:T(8,128)(2,1)S(1)} %get-tuple-element.215), channel_id=1, source_target_pairs={{0,16},{4,12},{8,24},{12,4},{16,0},{20,28},{24,8},{28,20},{1,17},{... | collective-permute-start | bytes 387080 | tf_op jit(solution)/shard_map/ppermute | solution.py:626
  81.7 0.7 collective-permute-start.38
  82.4 1.6 %collective-permute-start.39 = (bf16[16,576]{1,0:T(8,128)(2,1)S(1)}, bf16[16,576]{1,0:T(8,128)(2,1)S(1)}, u32[]{:S(2)}, u32[]{:S(2)}) collective-permute-start(bf16[16,576]{1,0:T(8,128)(2,1)S(1)} %get-tuple-element.217), channel_id=1, source_target_pairs={{0,24},{8,16},{16,8},{24,0},{1,25},{9,17},{17,9},{25,1},{2,26},{10... | collective-permute-start | bytes 55304 | tf_op jit(solution)/shard_map/ppermute | solution.py:622
  83.9 1.5 %collective-permute-done.38.near = bf16[16,576]{1,0:T(8,128)(2,1)S(1)} collective-permute-done((bf16[16,576]{1,0:T(8,128)(2,1)S(1)}, bf16[16,576]{1,0:T(8,128)(2,1)S(1)}, u32[]{:S(2)}, u32[]{:S(2)}) %collective-permute-start.38) | collective-permute-done | bytes 18464 | tf_op jit(solution)/shard_map/ppermute | solution.py:626
  85.4 1.6 %collective-permute-done.39.far = bf16[16,576]{1,0:T(8,128)(2,1)S(1)} collective-permute-done((bf16[16,576]{1,0:T(8,128)(2,1)S(1)}, bf16[16,576]{1,0:T(8,128)(2,1)S(1)}, u32[]{:S(2)}, u32[]{:S(2)}) %collective-permute-start.39) | collective-permute-done | bytes 18464 | tf_op jit(solution)/shard_map/ppermute | solution.py:622
  87.5 0.6 collective-permute-start.41
  88.1 1.5 %collective-permute-done.42.refs_4_ = bf16[112,576]{1,0:T(8,128)(2,1)S(1)} collective-permute-done((bf16[112,576]{1,0:T(8,128)(2,1)S(1)}, bf16[112,576]{1,0:T(8,128)(2,1)S(1)}, u32[]{:S(2)}, u32[]{:S(2)}) %collective-permute-start.42) | collective-permute-done | bytes 129056 | tf_op jit(solution)/shard_map/ppermute | solution.py:616
  89.6 2.0 %final.1 = (bf16[98,2,768]{2,1,0:T(2,128)(2,1)}, f32[98,2,768]{2,1,0:T(2,128)}, f32[192,192]{1,0:T(8,128)}, f32[192,768]{1,0:T(8,128)}, f32[192,768]{1,0:T(8,128...) custom-call(f32[2,104,768]{2,1,0:T(8,128)S(1)} %get-tuple-element.22, ...), custom_call_target="tpu_custom_call" | custom-call | tf_op jit(solution)/shard_map/final/pallas_call | solution.py:34
  (61 shorter events, 2.6 us)
Async XLA Ops:
  0.6 16.9 %copy-start.1 = (bf16[2,98,768]{2,0,1:T(2,128)(2,1)S(1)}, bf16[2,98,768]{2,0,1:T(2,128)(2,1)}, u32[]{:S(2)}) copy-start(bf16[2,98,768]{2,0,1:T(2,128)(2,1)} %param.27) | copy-start | bytes 903172
  0.7 2.5 %collective-permute-start.2 = (bf16[98,2,768]{2,1,0:T(2,128)(2,1)}, bf16[98,2,768]{2,1,0:T(2,128)(2,1)S(1)}, u32[]{:S(2)}, u32[]{:S(2)}) collective-permute-start(bf16[98,2,768]{2,1,0:T(2,128)(2,1)} %bitcast.10), channel_id=1, source_target_pairs={{0,4},{4,0},{1,5},{5,1},{2,6},{6,2},{3,7},{7,3},{8,12},{12,8},{9,1... | collective-permute-start | bytes 903176 | tf_op jit(solution)/shard_map/ppermute | solution.py:616
  3.2 10.8 %collective-permute-start.7 = (bf16[98,2,768]{2,1,0:T(2,128)(2,1)}, bf16[98,2,768]{2,1,0:T(2,128)(2,1)S(1)}, u32[]{:S(2)}, u32[]{:S(2)}) collective-permute-start(bf16[98,2,768]{2,1,0:T(2,128)(2,1)} %bitcast.12), channel_id=1, source_target_pairs={{0,4},{4,0},{1,5},{5,1},{2,6},{6,2},{3,7},{7,3},{8,12},{12,8},{9,1... | collective-permute-start | bytes 903176 | tf_op jit(solution)/shard_map/ppermute | solution.py:616
  3.3 15.0 %collective-permute-start.3 = (bf16[208,576]{1,0:T(8,128)(2,1)}, bf16[208,576]{1,0:T(8,128)(2,1)S(1)}, u32[]{:S(2)}, u32[]{:S(2)}) collective-permute-start(bf16[208,576]{1,0:T(8,128)(2,1)} %get-tuple-element.136.refs_0_), channel_id=1, source_target_pairs={{0,8},{4,20},{8,0},{12,28},{16,24},{20,4},{24,16},{28,12},{1,9},{5... | collective-permute-start | bytes 718856 | tf_op jit(solution)/shard_map/ppermute | solution.py:626
  6.3 12.1 %collective-permute-start.4 = (bf16[112,576]{1,0:T(8,128)(2,1)}, bf16[112,576]{1,0:T(8,128)(2,1)S(1)}, u32[]{:S(2)}, u32[]{:S(2)}) collective-permute-start(bf16[112,576]{1,0:T(8,128)(2,1)} %get-tuple-element.137), channel_id=1, source_target_pairs={{0,24},{8,16},{16,8},{24,0},{1,25},{9,17},{17,9},{25,1},{2,26},{10... | collective-permute-start | bytes 387080 | tf_op jit(solution)/shard_map/ppermute | solution.py:622
  7.8 10.6 %collective-permute-start.5 = (bf16[296,192]{1,0:T(8,128)(2,1)}, bf16[296,192]{1,0:T(8,128)(2,1)S(1)}, u32[]{:S(2)}, u32[]{:S(2)}) collective-permute-start(bf16[296,192]{1,0:T(8,128)(2,1)} %get-tuple-element.138.proj_t), channel_id=1, source_target_pairs={{0,1},{4,7},{1,0},{5,6},{2,3},{6,5},{3,2},{7,4},{8,9},{12,15},{9,8... | collective-permute-start | bytes 341000 | tf_op jit(solution)/shard_map/ppermute | solution.py:636
  9.3 9.0 %collective-permute-start.6 = (bf16[96,192]{1,0:T(8,128)(2,1)}, bf16[96,192]{1,0:T(8,128)(2,1)S(1)}, u32[]{:S(2)}, u32[]{:S(2)}) collective-permute-start(bf16[96,192]{1,0:T(8,128)(2,1)} %get-tuple-element.139), channel_id=1, source_target_pairs={{0,2},{1,3},{2,0},{3,1},{4,6},{5,7},{6,4},{7,5},{8,10},{9,11},{10,... | collective-permute-start | bytes 110600 | tf_op jit(solution)/shard_map/ppermute | solution.py:619
  11.9 1.0 %copy-start.2 = (bf16[192,768]{1,0:T(8,128)(2,1)S(1)}, bf16[192,768]{1,0:T(8,128)(2,1)}, u32[]{:S(2)}) copy-start(bf16[192,768]{1,0:T(8,128)(2,1)} %up.1) | copy-start | bytes 884740
  12.9 1.0 %copy-start.3 = (bf16[768,192]{0,1:T(8,128)(2,1)S(1)}, bf16[768,192]{0,1:T(8,128)(2,1)}, u32[]{:S(2)}) copy-start(bf16[768,192]{0,1:T(8,128)(2,1)} %param.25) | copy-start | bytes 884740
  13.8 6.0 %copy-start.5 = (bf16[296,192]{1,0:T(8,128)(2,1)S(1)}, bf16[296,192]{1,0:T(8,128)(2,1)}, u32[]{:S(2)}) copy-start(bf16[296,192]{1,0:T(8,128)(2,1)} %get-tuple-element.138.proj_t) | copy-start | bytes 340996
  13.9 8.6 %copy-start.4 = (bf16[208,576]{1,0:T(8,128)(2,1)S(1)}, bf16[208,576]{1,0:T(8,128)(2,1)}, u32[]{:S(2)}) copy-start(bf16[208,576]{1,0:T(8,128)(2,1)} %get-tuple-element.136.refs_0_) | copy-start | bytes 718852
  14.0 11.4 %collective-permute-start = (bf16[192,1280]{1,0:T(8,128)(2,1)S(1)}, bf16[192,1280]{1,0:T(8,128)(2,1)S(1)}, u32[]{:S(2)}, u32[]{:S(2)}) collective-permute-start(bf16[192,1280]{1,0:T(8,128)(2,1)S(1)} %get-tuple-element.131.refs_0_), channel_id=1, source_target_pairs={{0,8},{4,20},{8,0},{12,28},{16,24},{20,4},{24,16},{28,12},{1,9},{5... | collective-permute-start | bytes 1474568 | tf_op jit(solution)/shard_map/ppermute | solution.py:626
  15.6 1.0 %copy-start = (bf16[2,98,768]{2,0,1:T(2,128)(2,1)S(1)}, bf16[2,98,768]{2,0,1:T(2,128)(2,1)}, u32[]{:S(2)}) copy-start(bf16[2,98,768]{2,0,1:T(2,128)(2,1)} %param.14) | copy-start | bytes 903172
  18.4 1.5 %collective-permute-start.8 = (bf16[296,192]{1,0:T(8,128)(2,1)S(1)}, bf16[296,192]{1,0:T(8,128)(2,1)S(1)}, u32[]{:S(2)}, u32[]{:S(2)}) collective-permute-start(bf16[296,192]{1,0:T(8,128)(2,1)S(1)} %collective-permute-done.5.near_in), channel_id=1, source_target_pairs={{0,4},{4,0},{1,5},{5,1},{2,6},{6,2},{3,7},{7,3},{8,12},{12,8},{9,1... | collective-permute-start | bytes 341000 | tf_op jit(solution)/shard_map/ppermute | solution.py:616
  18.4 1.4 %collective-permute-start.9 = (bf16[96,192]{1,0:T(8,128)(2,1)S(1)}, bf16[96,192]{1,0:T(8,128)(2,1)S(1)}, u32[]{:S(2)}, u32[]{:S(2)}) collective-permute-start(bf16[96,192]{1,0:T(8,128)(2,1)S(1)} %collective-permute-done.6.far_in), channel_id=1, source_target_pairs={{0,4},{4,0},{1,5},{5,1},{2,6},{6,2},{3,7},{7,3},{8,12},{12,8},{9,1... | collective-permute-start | bytes 110600 | tf_op jit(solution)/shard_map/ppermute | solution.py:616
  20.1 7.8 %collective-permute-start.10 = (bf16[192,1024]{1,0:T(8,128)(2,1)S(1)}, bf16[192,1024]{1,0:T(8,128)(2,1)S(1)}, u32[]{:S(2)}, u32[]{:S(2)}) collective-permute-start(bf16[192,1024]{1,0:T(8,128)(2,1)S(1)} %pack_rest.1.refs_3_), channel_id=1, source_target_pairs={{0,8},{4,20},{8,0},{12,28},{16,24},{20,4},{24,16},{28,12},{1,9},{5... | collective-permute-start | bytes 1179656 | tf_op jit(solution)/shard_map/ppermute | solution.py:626
  20.7 1.8 %collective-permute-start.12 = (bf16[208,576]{1,0:T(8,128)(2,1)S(1)}, bf16[208,576]{1,0:T(8,128)(2,1)S(1)}, u32[]{:S(2)}, u32[]{:S(2)}) collective-permute-start(bf16[208,576]{1,0:T(8,128)(2,1)S(1)} %collective-permute-done.3.refs_1_), channel_id=1, source_target_pairs={{0,4},{4,0},{1,5},{5,1},{2,6},{6,2},{3,7},{7,3},{8,12},{12,8},{9,1... | collective-permute-start | bytes 718856 | tf_op jit(solution)/shard_map/ppermute | solution.py:616
  20.7 1.7 %collective-permute-start.13 = (bf16[112,576]{1,0:T(8,128)(2,1)S(1)}, bf16[112,576]{1,0:T(8,128)(2,1)S(1)}, u32[]{:S(2)}, u32[]{:S(2)}) collective-permute-start(bf16[112,576]{1,0:T(8,128)(2,1)S(1)} %collective-permute-done.4.refs_3_), channel_id=1, source_target_pairs={{0,4},{4,0},{1,5},{5,1},{2,6},{6,2},{3,7},{7,3},{8,12},{12,8},{9,1... | collective-permute-start | bytes 387080 | tf_op jit(solution)/shard_map/ppermute | solution.py:616
  23.7 6.3 %collective-permute-start.14 = (bf16[312,128]{1,0:T(8,128)(2,1)S(1)}, bf16[312,128]{1,0:T(8,128)(2,1)S(1)}, u32[]{:S(2)}, u32[]{:S(2)}) collective-permute-start(bf16[312,128]{1,0:T(8,128)(2,1)S(1)} %get-tuple-element.153.first.refs_10_), channel_id=1, source_target_pairs={{0,3},{1,2},{2,1},{3,0},{4,7},{5,6},{6,5},{7,4},{8,11},{9,10},{10,... | collective-permute-start | bytes 239624 | tf_op jit(solution)/shard_map/ppermute | solution.py:619
  25.5 6.3 %collective-permute-start.16 = (bf16[96,1280]{1,0:T(8,128)(2,1)S(1)}, bf16[96,1280]{1,0:T(8,128)(2,1)S(1)}, u32[]{:S(2)}, u32[]{:S(2)}) collective-permute-start(bf16[96,1280]{1,0:T(8,128)(2,1)S(1)} %cut.2), channel_id=1, source_target_pairs={{0,16},{4,12},{8,24},{12,4},{16,0},{20,28},{24,8},{28,20},{1,17},{... | collective-permute-start | bytes 737288 | tf_op jit(solution)/shard_map/ppermute | solution.py:626
  26.3 9.8 %collective-permute-start.1 = (bf16[192,1280]{1,0:T(8,128)(2,1)S(1)}, bf16[192,1280]{1,0:T(8,128)(2,1)S(1)}, u32[]{:S(2)}, u32[]{:S(2)}) collective-permute-start(bf16[192,1280]{1,0:T(8,128)(2,1)S(1)} %collective-permute-done.value.refs_1_), channel_id=1, source_target_pairs={{0,4},{4,0},{1,5},{5,1},{2,6},{6,2},{3,7},{7,3},{8,12},{12,8},{9,1... | collective-permute-start | bytes 1474568 | tf_op jit(solution)/shard_map/ppermute | solution.py:616
  27.9 7.7 %collective-permute-start.17 = (bf16[96,1024]{1,0:T(8,128)(2,1)S(1)}, bf16[96,1024]{1,0:T(8,128)(2,1)S(1)}, u32[]{:S(2)}, u32[]{:S(2)}) collective-permute-start(bf16[96,1024]{1,0:T(8,128)(2,1)S(1)} %cut.3), channel_id=1, source_target_pairs={{0,16},{4,12},{8,24},{12,4},{16,0},{20,28},{24,8},{28,20},{1,17},{... | collective-permute-start | bytes 589832 | tf_op jit(solution)/shard_map/ppermute | solution.py:626
  30.0 5.6 %collective-permute-start.15 = (bf16[2,328,128]{2,1,0:T(8,128)(2,1)S(1)}, bf16[2,328,128]{2,1,0:T(8,128)(2,1)S(1)}, u32[]{:S(2)}, u32[]{:S(2)}) collective-permute-start(bf16[2,328,128]{2,1,0:T(8,128)(2,1)S(1)} %pair.1), channel_id=1, source_target_pairs={{0,1},{1,0},{2,3},{3,2},{4,5},{5,4},{6,7},{7,6},{8,9},{9,8},{10,11... | collective-permute-start | bytes 503816 | tf_op jit(solution)/shard_map/ppermute | solution.py:619
  30.1 6.0 %collective-permute-start.11 = (bf16[192,1024]{1,0:T(8,128)(2,1)S(1)}, bf16[192,1024]{1,0:T(8,128)(2,1)S(1)}, u32[]{:S(2)}, u32[]{:S(2)}) collective-permute-start(bf16[192,1024]{1,0:T(8,128)(2,1)S(1)} %collective-permute-done.10.value.refs_4_), channel_id=1, source_target_pairs={{0,4},{4,0},{1,5},{5,1},{2,6},{6,2},{3,7},{7,3},{8,12},{12,8},{9,1... | collective-permute-start | bytes 1179656 | tf_op jit(solution)/shard_map/ppermute | solution.py:616
  35.6 1.8 %collective-permute-start.18 = (bf16[96,1280]{1,0:T(8,128)(2,1)S(1)}, bf16[96,1280]{1,0:T(8,128)(2,1)S(1)}, u32[]{:S(2)}, u32[]{:S(2)}) collective-permute-start(bf16[96,1280]{1,0:T(8,128)(2,1)S(1)} %collective-permute-done.16.refs_6_), channel_id=1, source_target_pairs={{0,4},{4,0},{1,5},{5,1},{2,6},{6,2},{3,7},{7,3},{8,12},{12,8},{9,1... | collective-permute-start | bytes 737288 | tf_op jit(solution)/shard_map/ppermute | solution.py:616
  35.6 1.8 %collective-permute-start.19 = (bf16[96,1024]{1,0:T(8,128)(2,1)S(1)}, bf16[96,1024]{1,0:T(8,128)(2,1)S(1)}, u32[]{:S(2)}, u32[]{:S(2)}) collective-permute-start(bf16[96,1024]{1,0:T(8,128)(2,1)S(1)} %collective-permute-done.17.refs_8_), channel_id=1, source_target_pairs={{0,4},{4,0},{1,5},{5,1},{2,6},{6,2},{3,7},{7,3},{8,12},{12,8},{9,1... | collective-permute-start | bytes 589832 | tf_op jit(solution)/shard_map/ppermute | solution.py:616
  40.5 5.6 %collective-permute-start.24 = (bf16[5,208,768]{2,1,0:T(8,128)(2,1)S(1)}, bf16[5,208,768]{2,1,0:T(8,128)(2,1)S(1)}, u32[]{:S(2)}, u32[]{:S(2)}) collective-permute-start(bf16[5,208,768]{2,1,0:T(8,128)(2,1)S(1)} %get-tuple-element.160.acts), channel_id=1, source_target_pairs={{0,4},{4,0},{1,5},{5,1},{2,6},{6,2},{3,7},{7,3},{8,12},{12,8},{9,1... | collective-permute-start | bytes 4792328 | tf_op jit(solution)/shard_map/ppermute | solution.py:616
  41.3 11.6 %collective-permute-start.23 = (bf16[98,768]{1,0:T(8,128)(2,1)S(1)}, bf16[98,768]{1,0:T(8,128)(2,1)S(1)}, u32[]{:S(2)}, u32[]{:S(2)}) collective-permute-start(bf16[98,768]{1,0:T(8,128)(2,1)S(1)} %get-tuple-element.166), channel_id=1, source_target_pairs={{0,1},{1,0},{2,3},{3,2},{4,5},{5,4},{6,7},{7,6},{8,9},{9,8},{10,11... | collective-permute-start | bytes 451592 | tf_op jit(solution)/shard_map/ppermute | solution.py:619
  41.7 8.5 %collective-permute-start.20 = (bf16[312,128]{1,0:T(8,128)(2,1)S(1)}, bf16[312,128]{1,0:T(8,128)(2,1)S(1)}, u32[]{:S(2)}, u32[]{:S(2)}) collective-permute-start(bf16[312,128]{1,0:T(8,128)(2,1)S(1)} %get-tuple-element.163), channel_id=1, source_target_pairs={{0,3},{1,2},{2,1},{3,0},{4,7},{5,6},{6,5},{7,4},{8,11},{9,10},{10,... | collective-permute-start | bytes 239624 | tf_op jit(solution)/shard_map/ppermute | solution.py:619
  43.4 9.2 %collective-permute-start.21 = (bf16[312,128]{1,0:T(8,128)(2,1)S(1)}, bf16[312,128]{1,0:T(8,128)(2,1)S(1)}, u32[]{:S(2)}, u32[]{:S(2)}) collective-permute-start(bf16[312,128]{1,0:T(8,128)(2,1)S(1)} %get-tuple-element.164), channel_id=1, source_target_pairs={{0,2},{1,3},{2,0},{3,1},{4,6},{5,7},{6,4},{7,5},{8,10},{9,11},{10,... | collective-permute-start | bytes 239624 | tf_op jit(solution)/shard_map/ppermute | solution.py:619
  44.9 8.0 %collective-permute-start.22 = (bf16[312,128]{1,0:T(8,128)(2,1)S(1)}, bf16[312,128]{1,0:T(8,128)(2,1)S(1)}, u32[]{:S(2)}, u32[]{:S(2)}) collective-permute-start(bf16[312,128]{1,0:T(8,128)(2,1)S(1)} %get-tuple-element.165), channel_id=1, source_target_pairs={{0,1},{1,0},{2,3},{3,2},{4,5},{5,4},{6,7},{7,6},{8,9},{9,8},{10,11... | collective-permute-start | bytes 239624 | tf_op jit(solution)/shard_map/ppermute | solution.py:619
  47.8 23.7 %collective-permute-start.35 = (bf16[2,96,1536]{2,1,0:T(8,128)(2,1)S(1)}, bf16[2,96,1536]{2,1,0:T(8,128)(2,1)S(1)}, u32[]{:S(2)}, u32[]{:S(2)}) collective-permute-start(bf16[2,96,1536]{2,1,0:T(8,128)(2,1)S(1)} %get-tuple-element.209), channel_id=1, source_target_pairs={{0,8},{4,20},{8,0},{12,28},{16,24},{20,4},{24,16},{28,12},{1,9},{5... | collective-permute-start | bytes 1769480 | tf_op jit(solution)/shard_map/ppermute | solution.py:626
  54.9 3.9 %collective-permute-start.29 = (bf16[208,576]{1,0:T(8,128)(2,1)S(1)}, bf16[208,576]{1,0:T(8,128)(2,1)S(1)}, u32[]{:S(2)}, u32[]{:S(2)}) collective-permute-start(bf16[208,576]{1,0:T(8,128)(2,1)S(1)} %get-tuple-element.186.grads), channel_id=1, source_target_pairs={{0,4},{4,0},{1,5},{5,1},{2,6},{6,2},{3,7},{7,3},{8,12},{12,8},{9,1... | collective-permute-start | bytes 718856 | tf_op jit(solution)/shard_map/ppermute | solution.py:616
  55.0 7.6 %collective-permute-start.27 = (bf16[96,768]{1,0:T(8,128)(2,1)S(1)}, bf16[96,768]{1,0:T(8,128)(2,1)S(1)}, u32[]{:S(2)}, u32[]{:S(2)}) collective-permute-start(bf16[96,768]{1,0:T(8,128)(2,1)S(1)} %get-tuple-element.184), channel_id=1, source_target_pairs={{0,24},{8,16},{16,8},{24,0},{1,25},{9,17},{17,9},{25,1},{2,26},{10... | collective-permute-start | bytes 442376 | tf_op jit(solution)/shard_map/ppermute | solution.py:794
  56.5 10.7 %collective-permute-start.25 = (bf16[104,768]{1,0:T(8,128)(2,1)S(1)}, bf16[104,768]{1,0:T(8,128)(2,1)S(1)}, u32[]{:S(2)}, u32[]{:S(2)}) collective-permute-start(bf16[104,768]{1,0:T(8,128)(2,1)S(1)} %get-tuple-element.183), channel_id=1, source_target_pairs={{0,1},{1,0},{2,3},{3,2},{4,5},{5,4},{6,7},{7,6},{8,9},{9,8},{10,11... | collective-permute-start | bytes 479240 | tf_op jit(solution)/shard_map/ppermute | solution.py:619
  56.8 10.3 %collective-permute-start.26 = (bf16[98,768]{1,0:T(8,128)(2,1)S(1)}, bf16[98,768]{1,0:T(8,128)(2,1)S(1)}, u32[]{:S(2)}, u32[]{:S(2)}) collective-permute-start(bf16[98,768]{1,0:T(8,128)(2,1)S(1)} %out_pair.1.own), channel_id=1, source_target_pairs={{0,2},{1,3},{2,0},{3,1},{4,6},{5,7},{6,4},{7,5},{8,10},{9,11},{10,... | collective-permute-start | bytes 451592 | tf_op jit(solution)/shard_map/ppermute | solution.py:619
  58.8 6.7 %collective-permute-start.28 = (bf16[96,768]{1,0:T(8,128)(2,1)S(1)}, bf16[96,768]{1,0:T(8,128)(2,1)S(1)}, u32[]{:S(2)}, u32[]{:S(2)}) collective-permute-start(bf16[96,768]{1,0:T(8,128)(2,1)S(1)} %get-tuple-element.185), channel_id=1, source_target_pairs={{0,8},{8,0},{16,24},{24,16},{1,9},{9,1},{17,25},{25,17},{2,10},{10... | collective-permute-start | bytes 442376 | tf_op jit(solution)/shard_map/ppermute | solution.py:794
  62.6 5.1 %collective-permute-start.30 = (bf16[96,768]{1,0:T(8,128)(2,1)S(1)}, bf16[96,768]{1,0:T(8,128)(2,1)S(1)}, u32[]{:S(2)}, u32[]{:S(2)}) collective-permute-start(bf16[96,768]{1,0:T(8,128)(2,1)S(1)} %get-tuple-element.188), channel_id=1, source_target_pairs={{0,16},{8,24},{16,0},{24,8},{1,17},{9,25},{17,1},{25,9},{2,18},{10... | collective-permute-start | bytes 442376 | tf_op jit(solution)/shard_map/ppermute | solution.py:814
  68.0 12.0 %collective-permute-start.31 = (bf16[152,768]{1,0:T(8,128)(2,1)S(1)}, bf16[152,768]{1,0:T(8,128)(2,1)S(1)}, u32[]{:S(2)}, u32[]{:S(2)}) collective-permute-start(bf16[152,768]{1,0:T(8,128)(2,1)S(1)} %get-tuple-element.200.own), channel_id=1, source_target_pairs={{0,2},{1,3},{2,0},{3,1},{4,6},{5,7},{6,4},{7,5},{8,10},{9,11},{10,... | collective-permute-start | bytes 700424 | tf_op jit(solution)/shard_map/ppermute | solution.py:619
  68.5 8.9 %collective-permute-start.33 = (bf16[2,96,576]{2,1,0:T(8,128)(2,1)S(1)}, bf16[2,96,576]{2,1,0:T(8,128)(2,1)S(1)}, u32[]{:S(2)}, u32[]{:S(2)}) collective-permute-start(bf16[2,96,576]{2,1,0:T(8,128)(2,1)S(1)} %get-tuple-element.202), channel_id=1, source_target_pairs={{0,8},{4,20},{8,0},{12,28},{16,24},{20,4},{24,16},{28,12},{1,9},{5... | collective-permute-start | bytes 663560 | tf_op jit(solution)/shard_map/ppermute | solution.py:626
  70.4 6.5 %collective-permute-start.32 = (bf16[98,768]{1,0:T(8,128)(2,1)S(1)}, bf16[98,768]{1,0:T(8,128)(2,1)S(1)}, u32[]{:S(2)}, u32[]{:S(2)}) collective-permute-start(bf16[98,768]{1,0:T(8,128)(2,1)S(1)} %out_total.1.out_own), channel_id=1, source_target_pairs={{0,1},{1,0},{2,3},{3,2},{4,5},{5,4},{6,7},{7,6},{8,9},{9,8},{10,11... | collective-permute-start | bytes 451592 | tf_op jit(solution)/shard_map/ppermute | solution.py:619
  71.5 15.5 %collective-permute-start.36 = (bf16[96,1536]{1,0:T(8,128)(2,1)S(1)}, bf16[96,1536]{1,0:T(8,128)(2,1)S(1)}, u32[]{:S(2)}, u32[]{:S(2)}) collective-permute-start(bf16[96,1536]{1,0:T(8,128)(2,1)S(1)} %get-tuple-element.210), channel_id=1, source_target_pairs={{0,16},{4,12},{8,24},{12,4},{16,0},{20,28},{24,8},{28,20},{1,17},{... | collective-permute-start | bytes 884744 | tf_op jit(solution)/shard_map/ppermute | solution.py:626
  80.1 7.0 %collective-permute-start.34 = (bf16[128,768]{1,0:T(8,128)(2,1)S(1)}, bf16[128,768]{1,0:T(8,128)(2,1)S(1)}, u32[]{:S(2)}, u32[]{:S(2)}) collective-permute-start(bf16[128,768]{1,0:T(8,128)(2,1)S(1)} %get-tuple-element.207.in_own), channel_id=1, source_target_pairs={{0,1},{1,0},{2,3},{3,2},{4,5},{5,4},{6,7},{7,6},{8,9},{9,8},{10,11... | collective-permute-start | bytes 589832 | tf_op jit(solution)/shard_map/ppermute | solution.py:619
  80.4 6.7 %collective-permute-start.37 = (bf16[112,576]{1,0:T(8,128)(2,1)S(1)}, bf16[112,576]{1,0:T(8,128)(2,1)S(1)}, u32[]{:S(2)}, u32[]{:S(2)}) collective-permute-start(bf16[112,576]{1,0:T(8,128)(2,1)S(1)} %get-tuple-element.215), channel_id=1, source_target_pairs={{0,16},{4,12},{8,24},{12,4},{16,0},{20,28},{24,8},{28,20},{1,17},{... | collective-permute-start | bytes 387080 | tf_op jit(solution)/shard_map/ppermute | solution.py:626
  81.7 3.8 %collective-permute-start.38 = (bf16[16,576]{1,0:T(8,128)(2,1)S(1)}, bf16[16,576]{1,0:T(8,128)(2,1)S(1)}, u32[]{:S(2)}, u32[]{:S(2)}) collective-permute-start(bf16[16,576]{1,0:T(8,128)(2,1)S(1)} %get-tuple-element.216), channel_id=1, source_target_pairs={{0,8},{4,20},{8,0},{12,28},{16,24},{20,4},{24,16},{28,12},{1,9},{5... | collective-permute-start | bytes 55304 | tf_op jit(solution)/shard_map/ppermute | solution.py:626
  82.4 4.7 %collective-permute-start.39 = (bf16[16,576]{1,0:T(8,128)(2,1)S(1)}, bf16[16,576]{1,0:T(8,128)(2,1)S(1)}, u32[]{:S(2)}, u32[]{:S(2)}) collective-permute-start(bf16[16,576]{1,0:T(8,128)(2,1)S(1)} %get-tuple-element.217), channel_id=1, source_target_pairs={{0,24},{8,16},{16,8},{24,0},{1,25},{9,17},{17,9},{25,1},{2,26},{10... | collective-permute-start | bytes 55304 | tf_op jit(solution)/shard_map/ppermute | solution.py:622
  87.3 2.4 %collective-permute-start.40 = (bf16[232,768]{1,0:T(8,128)(2,1)S(1)}, bf16[232,768]{1,0:T(8,128)(2,1)S(1)}, u32[]{:S(2)}, u32[]{:S(2)}) collective-permute-start(bf16[232,768]{1,0:T(8,128)(2,1)S(1)} %get-tuple-element.221), channel_id=1, source_target_pairs={{0,4},{4,0},{1,5},{5,1},{2,6},{6,2},{3,7},{7,3},{8,12},{12,8},{9,1... | collective-permute-start | bytes 1069064 | tf_op jit(solution)/shard_map/ppermute | solution.py:616
  87.5 2.1 %collective-permute-start.41 = (bf16[96,1536]{1,0:T(8,128)(2,1)S(1)}, bf16[96,1536]{1,0:T(8,128)(2,1)S(1)}, u32[]{:S(2)}, u32[]{:S(2)}) collective-permute-start(bf16[96,1536]{1,0:T(8,128)(2,1)S(1)} %get-tuple-element.231), channel_id=1, source_target_pairs={{0,4},{4,0},{1,5},{5,1},{2,6},{6,2},{3,7},{7,3},{8,12},{12,8},{9,1... | collective-permute-start | bytes 884744 | tf_op jit(solution)/shard_map/ppermute | solution.py:616
  88.0 1.6 %collective-permute-start.42 = (bf16[112,576]{1,0:T(8,128)(2,1)S(1)}, bf16[112,576]{1,0:T(8,128)(2,1)S(1)}, u32[]{:S(2)}, u32[]{:S(2)}) collective-permute-start(bf16[112,576]{1,0:T(8,128)(2,1)S(1)} %get-tuple-element.233), channel_id=1, source_target_pairs={{0,4},{4,0},{1,5},{5,1},{2,6},{6,2},{3,7},{7,3},{8,12},{12,8},{9,1... | collective-permute-start | bytes 387080 | tf_op jit(solution)/shard_map/ppermute | solution.py:616
